TPU v7x, 256 devices: a whole 4x4x8 slice. The times are simulated.
256 devices in a mesh: row: 32 (over x_lo, z, core), col: 8 (over y, x_hi).
Axes of the slice: x: 4 (x_hi: 2, x_lo: 2; x = x_hi * 2 + x_lo), y: 4, z: 8, core: 2. Of those that a mesh axis runs over, the one named last changes fastest.
Arguments:
- image_embed: bfloat16 [12288, 1024], P(('row', 'col')), may hold values from -30 to 30
- text_embed: bfloat16 [12288, 1024], P(('col', 'row')), may hold values from -30 to 30
- pair_index: int32 [12288], P('row'), may hold values from 0 to 12287, each once
Outputs:
- loss: float32 [], replicated
- grad_image: float32 [12288, 1024], P(('row', 'col'))
- grad_text: float32 [12288, 1024], P(('col', 'row'))
All inputs are finite; a program needn't handle non-finite values.
Results may differ from a plain program's by a relative error of at most 0.0015.
Values may be sent and summed in bfloat16 or wider, within the bound.
No kernel may reach another device: no remote copies, remote signals or barrier semaphores. Data moves between devices by JAX's collectives and lax.ppermute only.
A program may use at most 128 MiB of HBM per device.

v0:
```python
import jax
import jax.numpy as jnp
from jax import lax
from jax.sharding import PartitionSpec as P


def shards(image_embed, text_embed, pair_index):
    inv_root = image_embed.shape[1] ** (-0.5)
    image_block = lax.all_gather(image_embed, "col", axis=0, tiled=True)
    col_count = text_embed.shape[0] * lax.axis_size("row")
    pair_total = col_count * lax.axis_size("col")
    text_block = lax.all_gather(text_embed, "row", axis=0, tiled=True)
    score_tile = (
        lax.dot_general(
            image_block, text_block, (((1,), (1,)), ((), ())), preferred_element_type=jnp.float32
        )
        * inv_root
    )
    col_start = lax.axis_index("col") * col_count
    positive = pair_index[:, None] == col_start + lax.broadcasted_iota(
        jnp.int32, score_tile.shape, 1
    )
    row_high = lax.pmax(jnp.max(score_tile, axis=1), "col")
    col_high = lax.pmax(jnp.max(score_tile, axis=0), "row")
    row_sum = lax.psum(jnp.sum(jnp.exp(score_tile - row_high[:, None]), axis=1), "col")
    col_sum = lax.psum(jnp.sum(jnp.exp(score_tile - col_high[None, :]), axis=0), "row")
    row_lse = row_high + jnp.log(row_sum)
    col_lse = col_high + jnp.log(col_sum)
    probs = 0.5 * (jnp.exp(score_tile - row_lse[:, None]) + jnp.exp(score_tile - col_lse[None, :]))
    grad_scores = (probs - positive.astype(jnp.float32)).astype(jnp.bfloat16)
    matched = jnp.sum(jnp.where(positive, score_tile, 0.0))
    local_loss = (
        jnp.sum(row_lse) / lax.axis_size("col")
        + jnp.sum(col_lse) / lax.axis_size("row")
        - 2.0 * matched
    ) / (2.0 * pair_total)
    loss = lax.psum(local_loss, ("row", "col"))
    grad_text = lax.psum_scatter(
        lax.dot_general(
            grad_scores, image_block, (((0,), (0,)), ((), ())), preferred_element_type=jnp.float32
        )
        * inv_root,
        "row",
        scatter_dimension=0,
        tiled=True,
    )
    grad_image = lax.psum_scatter(
        jnp.dot(grad_scores, text_block, preferred_element_type=jnp.float32) * inv_root,
        "col",
        scatter_dimension=0,
        tiled=True,
    )
    return (loss, grad_image, grad_text)


def solution(mesh):
    return jax.shard_map(
        shards,
        mesh=mesh,
        in_specs=(P(("row", "col"), None), P(("col", "row"), None), P("row")),
        out_specs=(P(), P(("row", "col"), None), P(("col", "row"), None)),
        check_vma=False,
    )
```

profile of v0, /device:TPU:1, one launch (start us, length us, event | category | flops | bytes accessed | tf_op | source)
XLA Modules:
  0.0 447.2 jit_solution(16075136781742532685)
XLA Ops:
  7.2 0.0 all-gather.2.cloned.1.call-start
  7.2 0.7 all-gather.2.cloned.1.call-update
  7.9 0.0 reduce-scatter.3.cloned.1.call-start
  8.0 33.7 %all_gather.6 = bf16[384,1024]{1,0:T(8,128)(2,1)S(1)} all-gather(bf16[48,1024]{1,0:T(8,128)(2,1)} %param.3), channel_id=1, replica_groups=mesh['row'=32,'col'=8] {'col'}, dimensions={0}, use_global_device_ids=true | all-gather | bytes 884736 | tf_op jit(solution)/shard_map/all_gather | solution.py:9
  41.7 0.0 copy-start
  41.7 38.6 %all-gather.2.cloned.1.call-done = bf16[1536,1024]{1,0:T(8,128)(2,1)} async-done(((bf16[48,1024]{1,0:T(8,128)(2,1)}), bf16[1536,1024]{1,0:T(8,128)(2,1)}) %all-gather.2.cloned.1.call-update) | async-done | bytes 3145744 | tf_op jit(solution)/shard_map/all_gather | solution.py:12
  80.3 3.4 fusion.5
  83.7 53.6 %pmax.15 = f32[1536]{0:T(1024)S(1)} all-reduce(f32[1536]{0:T(1024)S(1)} %get-tuple-element.6), channel_id=1, replica_groups=mesh['row'=32,'col'=8] {'row'}, use_global_device_ids=true, to_apply=%region_6.0 | all-reduce | flops 1536 | bytes 12288 | tf_op jit(solution)/shard_map/pmax | solution.py:24
  137.3 20.1 %pmax.14 = f32[384]{0:T(512)S(1)} all-reduce(f32[384]{0:T(512)S(1)} %get-tuple-element.7), channel_id=1, replica_groups=mesh['row'=32,'col'=8] {'col'}, use_global_device_ids=true, to_apply=%region_1.0 | all-reduce | flops 384 | bytes 3072 | tf_op jit(solution)/shard_map/pmax | solution.py:23
  157.5 0.0 copy-done
  157.5 1.9 fusion
  159.4 59.3 %psum.22 = f32[1536]{0:T(1024)S(1)} all-reduce(f32[1536]{0:T(1024)S(1)} %get-tuple-element.4), channel_id=1, replica_groups=mesh['row'=32,'col'=8] {'row'}, use_global_device_ids=true, to_apply=%region_8.9 | all-reduce | flops 1536 | bytes 12288 | tf_op jit(solution)/shard_map/psum | solution.py:26
  218.7 0.6 fusion.6
  219.3 15.5 %psum.21 = f32[384]{0:T(512)S(1)} all-reduce(f32[384]{0:T(512)S(1)} %get-tuple-element.5), channel_id=1, replica_groups=mesh['row'=32,'col'=8] {'col'}, use_global_device_ids=true, to_apply=%region_3.0 | all-reduce | flops 384 | bytes 3072 | tf_op jit(solution)/shard_map/psum | solution.py:25
  234.8 0.7 fusion.7
  235.5 4.8 %convolution_multiply_fusion.2 = f32[384,1024]{1,0:T(8,128)} fusion(bf16[1536,1024]{1,0:T(8,128)(2,1)} %all-gather.2.cloned.1.call-done, f32[384,1536]{1,0:T(8,128)S(1)} %get-tuple-element.12, f32[1536]{0:T(1024)S(1)} %get-tuple-element.9, f32[384]{0:T(512)S(1)} %get-tuple-element.11, s32[1536]{0:T(1024)S(1)} %iota_add_fusion, s32[384]{0:T(512)S(1)} %copy-done), kind=kOutput, calls=%fused_computation.9 | convolution fusion | flops 1213071360 | bytes 7093248 | tf_op jit(solution)/shard_map/dot_general | solution.py:48
  240.3 0.0 reduce-scatter.3.cloned.1.call-update
  240.4 0.0 reduce-scatter.5.cloned.1.call-start
  240.4 5.0 %convolution_multiply_fusion = f32[1536,1024]{1,0:T(8,128)} fusion(bf16[384,1024]{1,0:T(8,128)(2,1)S(1)} %all_gather.6, f32[384,1536]{1,0:T(8,128)S(1)} %get-tuple-element.12, f32[1536]{0:T(1024)S(1)} %get-tuple-element.9, f32[384]{0:T(512)S(1)} %get-tuple-element.11, s32[1536]{0:T(1024)S(1)} %iota_add_fusion, s32[384]{0:T(512)S(1)} %copy-done), kind=kOutput, calls=%fused_computation | convolution fusion | flops 1214251008 | bytes 9452544 | tf_op jit(solution)/shard_map/dot_general | solution.py:39
  245.4 0.0 reduce-scatter.5.cloned.1.call-update
  247.3 78.5 %psum.23 = f32[]{:T(128)} all-reduce(f32[]{:T(128)S(6)} %div.11), channel_id=1, replica_groups=mesh['row'=32,'col'=8] {'row','col'}, use_global_device_ids=true, to_apply=%region_11.12 | all-reduce | flops 1 | bytes 8 | tf_op jit(solution)/shard_map/psum | solution.py:37
  325.8 0.0 reduce-scatter.3.cloned.1.call-done
  325.8 114.8 %reduce-scatter.5.cloned.1.call-done = f32[48,1024]{1,0:T(8,128)} async-done(((f32[1536,1024]{1,0:T(8,128)}), f32[48,1024]{1,0:T(8,128)}) %reduce-scatter.5.cloned.1.call-update) | async-done | bytes 196624 | tf_op jit(solution)/shard_map/reduce_scatter | solution.py:38
  (1 shorter events, 0.0 us)
Async XLA Ops:
  7.2 73.1 %all-gather.2.cloned.1.call-start = ((), (), s32[]{:S(2)}) async-start(), calls=%async_computation.2 | async-start | bytes 3244032 | tf_op jit(solution)/shard_map/all_gather | solution.py:12
  7.9 317.9 %reduce-scatter.3.cloned.1.call-start = ((), (), s32[]{:S(2)}) async-start(), calls=%async_computation.3 | async-start | bytes 1769472 | tf_op jit(solution)/shard_map/reduce_scatter | solution.py:47
  41.7 115.8 %copy-start = (s32[384]{0:T(512)S(1)}, s32[384]{0:T(512)}, u32[]{:S(2)}) copy-start(s32[384]{0:T(512)} %param.5) | copy-start | bytes 4612
  240.4 200.3 %reduce-scatter.5.cloned.1.call-start = ((), (), s32[]{:S(2)}) async-start(), calls=%async_computation.4 | async-start | bytes 6488064 | tf_op jit(solution)/shard_map/reduce_scatter | solution.py:38
Sparse Core Ops, SparseCore 0:
  9.9 70.3 all-gather.1
  240.5 75.0 reduce-scatter.2
  318.9 121.7 reduce-scatter.4
where the time goes:
time: 450 us; the launch traced here: 447 us
  blocking collectives  261 us (58%)
  waiting for transfers between devices  154 us (34%)
  between operations  15.7 us (3%)
  matrix products  13.2 us (3%)
    reduce_scatter x1, waiting for transfers between devices, shards(): lax.psum_scatter(lax.dot_general(grad_scores, image_block, (((0,), (0,)),...  115 us
    psum x1, blocking collectives, shards(): loss = lax.psum(local_loss, ('row', 'col'))  78.5 us
    psum x1, blocking collectives, shards(): lax.psum(jnp.sum(jnp.exp(score_tile - col_high[None, :]), axis=0), 'row')  59.3 us
    pmax x1, blocking collectives, shards(): col_high = lax.pmax(jnp.max(score_tile, axis=0), 'row')  53.6 us
    all_gather x1, waiting for transfers between devices, shards(): text_block = lax.all_gather(text_embed, 'row', axis=0, tiled=True)  38.6 us
    all_gather x1, blocking collectives, shards(): image_block = lax.all_gather(image_embed, 'col', axis=0, tiled=True)  33.7 us
    pmax x1, blocking collectives, shards(): row_high = lax.pmax(jnp.max(score_tile, axis=1), 'col')  20.1 us
    psum x1, blocking collectives, shards(): lax.psum(jnp.sum(jnp.exp(score_tile - row_high[:, None]), axis=1), 'col')  15.5 us
  transfers between devices with their start and end apart: 3, of which 2 were waited for; matrix products, arithmetic and copies ran while one was open for 1% of the time, Pallas kernels for 0%

commit v1 on v0

v1 whole, which is shorter than its diff:
```python
import jax
import jax.numpy as jnp
from jax import lax
from jax.sharding import Mesh, PartitionSpec as P

PLANE = ("xl", "y", "xh")


def combine(parts):
    high = jnp.max(parts, axis=0)
    return high + jnp.log(jnp.sum(jnp.exp(parts - high[None]), axis=0))


def spread(x, axes, count):
    return lax.all_to_all(jnp.broadcast_to(x[None], (count,) + x.shape), axes, 0, 0)


def shards(image_embed, text_embed, pair_index):
    rows, width = image_embed.shape
    n_xl, n_z, n_c, n_y, n_xh = (lax.axis_size(a) for a in ("xl", "z", "c", "y", "xh"))
    n_plane = n_xl * n_y * n_xh
    pairs = rows * n_plane * n_z * n_c
    inv_root = width ** (-0.5)
    core = lax.axis_index("c")
    swap = [(0, 1), (1, 0)]

    pair_other = lax.ppermute(pair_index, "xl", swap)
    first = lax.axis_index("xl") == 0
    pair_rows = jnp.concatenate(
        [jnp.where(first, pair_index, pair_other), jnp.where(first, pair_other, pair_index)]
    )

    text_own = spread(text_embed, "z", n_z).reshape(n_z * rows, width)
    text_other = lax.ppermute(text_own, "c", swap)
    text = jnp.concatenate([text_own, text_other], axis=0)
    image = spread(image_embed, PLANE, n_plane).reshape(n_plane * rows, width)

    half = n_z * rows
    scores = (
        lax.dot_general(image, text, (((1,), (1,)), ((), ())), preferred_element_type=jnp.float32)
        * inv_root
    )
    block = (lax.axis_index("y") * n_xh + lax.axis_index("xh")) * n_xl + lax.axis_index("xl")
    slot = lax.iota(jnp.int32, 2 * half)
    own = slot < half
    within = jnp.where(own, slot, slot - half)
    column = (
        ((block * n_z + within // rows) * n_c + jnp.where(own, core, 1 - core)) * rows
        + within % rows
    )
    positive = pair_rows[:, None] == column[None, :]
    matched = jnp.sum(jnp.where(positive, scores, 0.0))

    row_high = jnp.max(scores, axis=1)
    row_part = row_high + jnp.log(jnp.sum(jnp.exp(scores - row_high[:, None]), axis=1))
    col_high = jnp.max(scores, axis=0)
    col_part = col_high + jnp.log(jnp.sum(jnp.exp(scores - col_high[None, :]), axis=0))

    row_sent = jnp.concatenate([row_part, jnp.broadcast_to(matched, (128,))])
    row_got = spread(row_sent, PLANE, n_plane)
    row_lse = combine(row_got[:, : 2 * half])
    row_terms = jnp.sum(row_lse) - 2.0 * jnp.sum(row_got[:, 2 * half])

    col_sent = jnp.concatenate([col_part, jnp.broadcast_to(row_terms, (128,))])
    col_seen = lax.ppermute(col_sent, "c", swap)
    col_seen_lse = jnp.concatenate([col_seen[half : 2 * half], col_seen[:half]])
    col_pair = combine(jnp.stack([col_part, col_seen_lse]))
    terms_pair = row_terms + col_seen[2 * half]
    col_got = spread(jnp.concatenate([col_pair, jnp.broadcast_to(terms_pair, (128,))]), "z", n_z)
    col_lse = combine(col_got[:, : 2 * half])
    all_row_terms = jnp.sum(col_got[:, 2 * half])
    col_terms = jnp.sum(col_lse)

    probs = 0.5 * (jnp.exp(scores - row_lse[:, None]) + jnp.exp(scores - col_lse[None, :]))
    grad_scores = (probs - positive.astype(jnp.float32)).astype(jnp.bfloat16)

    image_part = jnp.dot(grad_scores, text, preferred_element_type=jnp.float32) * inv_root
    image_sent = jnp.concatenate(
        [
            image_part.reshape(n_plane, rows, width),
            jnp.broadcast_to(col_terms, (n_plane, 8, width)),
        ],
        axis=1,
    )
    image_got = lax.all_to_all(image_sent, PLANE, 0, 0)
    grad_image = jnp.sum(image_got[:, :rows], axis=0)
    loss = (all_row_terms + jnp.sum(image_got[:, rows, 0])) / (2.0 * pairs)

    text_part = (
        lax.dot_general(
            grad_scores, image, (((0,), (0,)), ((), ())), preferred_element_type=jnp.float32
        )
        * inv_root
    )
    text_sum = text_part[:half] + lax.ppermute(text_part[half:], "c", swap)
    text_got = lax.all_to_all(text_sum.reshape(n_z, rows, width), "z", 0, 0)
    grad_text = jnp.sum(text_got, axis=0)
    return (loss, grad_image, grad_text)


def solution(mesh):
    fine = Mesh(mesh.devices.reshape(2, 8, 2, 4, 2), ("xl", "z", "c", "y", "xh"))
    image_spec = P(("xl", "z", "c", "y", "xh"), None)
    text_spec = P(("y", "xh", "xl", "z", "c"), None)
    return jax.shard_map(
        shards,
        mesh=fine,
        in_specs=(image_spec, text_spec, P(("xl", "z", "c"))),
        out_specs=(P(), image_spec, text_spec),
        check_vma=False,
    )
```

time: 450 us -> 210 us (0.47)
  blocking collectives: 261 us -> 53.3 us
  waiting for transfers between devices: 154 us -> 97.5 us
  starting transfers between devices: 0.12 us -> 24.2 us
  between operations: 15.7 us -> 5.19 us
  local copies, waits for them, and re-layouts: 0.01 us -> 8.72 us
  other arithmetic: 3.23 us -> 10.7 us
    psum x3 -> x0, blocking collectives: 153 us -> none  [the longest x1 78.5 us: shards(): loss = lax.psum(local_loss, ('row', 'col'))]
    reduce_scatter x2 -> x0, waiting for transfers between devices: 115 us -> none  [the longest x1 115 us: shards(): lax.psum_scatter(lax.dot_general(grad_scores, image_block, (((0,), (0,)),...]
    all_to_all x0 -> x3, waiting for transfers between devices: none -> 81.6 us  [the longest x1 44.1 us: shards(): image_got = lax.all_to_all(image_sent, PLANE, 0, 0)]
    pmax x2 -> x0, blocking collectives: 73.7 us -> none  [the longest x1 53.6 us: shards(): col_high = lax.pmax(jnp.max(score_tile, axis=0), 'row')]
    all_to_all x0 -> x3, blocking collectives: none -> 53.3 us  [spread(): lax.all_to_all(jnp.broadcast_to(x[None], (count,) + x.shape), axes, 0, 0)]
    all_gather x1 -> x0, waiting for transfers between devices: 38.6 us -> none  [shards(): text_block = lax.all_gather(text_embed, 'row', axis=0, tiled=True)]
    all_gather x1 -> x0, blocking collectives: 33.7 us -> none  [shards(): image_block = lax.all_gather(image_embed, 'col', axis=0, tiled=True)]
    ppermute x0 -> x4, waiting for transfers between devices: none -> 15.9 us  [the longest x1 12 us: shards(): pair_other = lax.ppermute(pair_index, 'xl', swap)]
  transfers between devices with their start and end apart: 3 -> 7, of which waited for: 2 -> 6; matrix products, arithmetic and copies ran while one was open for 1% -> 5% of each run, Pallas kernels for 0% -> 0%
where the time goes in v1:
time: 210 us; the launch traced here: 209 us
  waiting for transfers between devices  97.5 us (46%)
  blocking collectives  53.3 us (25%)
  starting transfers between devices  24.2 us (12%)
  other arithmetic  10.7 us (5%)
  matrix products  9.36 us (4%)
  local copies, waits for them, and re-layouts  8.72 us (4%)
  between operations  5.19 us (2%)
    all_to_all x3, blocking collectives, spread(): lax.all_to_all(jnp.broadcast_to(x[None], (count,) + x.shape), axes, 0, 0)  53.3 us
    all_to_all x1, waiting for transfers between devices, shards(): image_got = lax.all_to_all(image_sent, PLANE, 0, 0)  44.1 us
    all_to_all x1, waiting for transfers between devices, shards(): text_got = lax.all_to_all(text_sum.reshape(n_z, rows, width), 'z', 0, 0)  34.2 us
    ppermute x1, waiting for transfers between devices, shards(): pair_other = lax.ppermute(pair_index, 'xl', swap)  12 us
    all_to_all x1, starting transfers between devices, spread(): lax.all_to_all(jnp.broadcast_to(x[None], (count,) + x.shape), axes, 0, 0)  6.75 us
    all_to_all x1, starting transfers between devices, shards(): image_got = lax.all_to_all(image_sent, PLANE, 0, 0)  4.49 us
  transfers between devices with their start and end apart: 7, of which 6 were waited for; matrix products, arithmetic and copies ran while one was open for 5% of the time, Pallas kernels for 0%

profile of v1, /device:TPU:1, one launch (start us, length us, event | category | flops | bytes accessed | tf_op | source)
XLA Modules:
  0.0 209.0 jit_solution(14275855560977557135)
XLA Ops:
  0.6 0.0 copy-start.1
  0.6 1.0 broadcast_in_dim.20
  1.7 30.4 %all_to_all.38 = bf16[8,48,1024]{2,1,0:T(8,128)(2,1)S(1)} all-to-all(bf16[8,48,1024]{2,1,0:T(8,128)(2,1)S(1)} %broadcast_in_dim.20), channel_id=1, replica_groups=mesh['xl'=2,'z'=8,'c'=2,'y'=4,'xh'=2] {'z'}, dimensions={0} | all-to-all | bytes 1572864 | tf_op jit(solution)/shard_map/all_to_all | solution.py:15
  32.1 0.0 copy-done.1
  32.1 0.0 copy-start.2
  32.1 1.3 broadcast_in_dim.21
  33.4 6.8 %all-to-all-start.1 = ((bf16[16,48,1024]{2,1,0:T(8,128)(2,1)}), bf16[16,48,1024]{2,1,0:T(8,128)(2,1)S(1)}, u32[]{:S(2)}, u32[]{:S(2)}) async-start(bf16[16,48,1024]{2,1,0:T(8,128)(2,1)} %broadcast_in_dim.21), calls=%async_computation.1 | async-start | bytes 3145728 | tf_op jit(solution)/shard_map/all_to_all | solution.py:15
  40.2 2.8 %collective-permute-start = (bf16[384,1024]{1,0:T(8,128)(2,1)S(1)}, bf16[384,1024]{1,0:T(8,128)(2,1)S(1)}, u32[]{:S(2)}, u32[]{:S(2)}) collective-permute-start(bf16[384,1024]{1,0:T(8,128)(2,1)S(1)} %bitcast.44), channel_id=1, source_target_pairs={{0,8},{8,0},{1,9},{9,1},{2,10},{10,2},{3,11},{11,3},{4,12},{12,4},... | collective-permute-start | bytes 2359304 | tf_op jit(solution)/shard_map/ppermute | solution.py:34
  43.0 0.0 copy-done.2
  43.0 1.6 collective-permute-start.1
  44.6 12.0 %collective-permute-done.1 = s32[384]{0:T(512)S(1)} collective-permute-done((s32[384]{0:T(512)S(1)}, s32[384]{0:T(512)S(1)}, u32[]{:S(2)}, u32[]{:S(2)}) %collective-permute-start.1) | collective-permute-done | bytes 1568 | tf_op jit(solution)/shard_map/ppermute | solution.py:27
  56.7 3.3 %all-to-all-done.1 = bf16[16,48,1024]{2,1,0:T(8,128)(2,1)S(1)} async-done(((bf16[16,48,1024]{2,1,0:T(8,128)(2,1)}), bf16[16,48,1024]{2,1,0:T(8,128)(2,1)S(1)}, u32[]{:S(2)}, u32[]{:S(2)}) %all-to-all-start.1) | async-done | bytes 1572896 | tf_op jit(solution)/shard_map/all_to_all | solution.py:15
  60.0 0.0 copy-start
  60.0 0.0 collective-permute-done
  60.0 1.2 copy-done
  61.2 0.0 copy-start.3
  61.2 0.9 copy-done.3
  62.1 3.2 %fusion.32 = (f32[768]{0:T(1024)S(1)}, f32[768]{0:T(1024)S(1)}, f32[768,768]{1,0:T(8,128)S(1)}) fusion(bf16[768,1024]{1,0:T(8,128)(2,1)} %bitcast.42, bf16[384,1024]{1,0:T(8,128)(2,1)} %copy-done.3, bf16[384,1024]{1,0:T(8,128)(2,1)S(1)} %bitcast.45), kind=kOutput, calls=%fused_computation.66 | convolution fusion | flops 1212873216 | bytes 5511168 | tf_op jit(solution)/shard_map/dot_general | solution.py:40
  65.3 1.7 fusion
  66.9 0.7 concatenate.25
  67.6 12.9 %all_to_all.39 = f32[16,1,896]{2,1,0:T(1,128)S(1)} all-to-all(f32[16,1,896]{2,1,0:T(1,128)S(1)} %broadcast_in_dim.25), channel_id=1, replica_groups=mesh['xl'=2,'z'=8,'c'=2,'y'=4,'xh'=2] {'xl','y','xh'}, dimensions={0} | all-to-all | bytes 114688 | tf_op jit(solution)/shard_map/all_to_all | solution.py:15
  80.6 0.6 slice_reduce_fusion.4
  81.2 0.6 fusion.34
  83.1 3.2 %collective-permute-start.2 = (f32[896]{0:T(1024)S(1)}, f32[896]{0:T(1024)S(1)}, u32[]{:S(2)}, u32[]{:S(2)}) collective-permute-start(f32[896]{0:T(1024)S(1)} %concatenate.26), channel_id=1, source_target_pairs={{0,8},{8,0},{1,9},{9,1},{2,10},{10,2},{3,11},{11,3},{4,12},{12,4},... | collective-permute-start | bytes 10760 | tf_op jit(solution)/shard_map/ppermute | solution.py:65
  86.3 0.8 collective-permute-done.2
  87.1 0.5 slice.37
  88.4 10.0 %all_to_all.40 = f32[8,1,896]{2,1,0:T(1,128)S(1)} all-to-all(f32[8,1,896]{2,1,0:T(1,128)S(1)} %broadcast_in_dim.26), channel_id=1, replica_groups=mesh['xl'=2,'z'=8,'c'=2,'y'=4,'xh'=2] {'z'}, dimensions={0} | all-to-all | bytes 57344 | tf_op jit(solution)/shard_map/all_to_all | solution.py:15
  98.4 0.6 fusion.33
  99.1 3.0 %convolution_multiply_fusion.1 = f32[768,1024]{1,0:T(8,128)S(1)} fusion(bf16[384,1024]{1,0:T(8,128)(2,1)} %copy-done.3, bf16[384,1024]{1,0:T(8,128)(2,1)S(1)} %bitcast.46, f32[768,768]{1,0:T(8,128)S(1)} %get-tuple-element.18, f32[768]{0:T(1024)S(1)} %get-tuple-element.9, f32[768]{0:T(1024)S(1)} %get-tuple-element.11, s32[768]{0:T(1024)S(1)} %pad_add_fusion, ...), kind=kOutput, calls=%fused_computation.19 | convolution fusion | flops 1216610304 | bytes 7090176 | tf_op jit(solution)/shard_map/dot_general | solution.py:77
  102.1 2.8 %concatenate.29 = f32[16,56,1024]{2,1,0:T(8,128)} pad(f32[16,48,1024]{2,1,0:T(8,128)S(1)} %bitcast.41, f32[]{:T(128)} %get-tuple-element.8), padding=0_0x0_8x0_0 | pad | bytes 6815748 | tf_op jit(solution)/shard_map/concatenate | solution.py:78
  104.9 4.5 %all-to-all-start.4 = ((f32[16,56,1024]{2,1,0:T(8,128)}), f32[16,56,1024]{2,1,0:T(8,128)}, u32[]{:S(2)}, u32[]{:S(2)}) async-start(f32[16,56,1024]{2,1,0:T(8,128)} %concatenate.29), calls=%async_computation.4 | async-start | bytes 7340032 | tf_op jit(solution)/shard_map/all_to_all | solution.py:85
  109.4 3.2 %convolution_multiply_fusion = f32[768,1024]{1,0:T(8,128)S(1)} fusion(bf16[768,1024]{1,0:T(8,128)(2,1)} %bitcast.43, f32[768,768]{1,0:T(8,128)S(1)} %get-tuple-element.18, f32[768]{0:T(1024)S(1)} %get-tuple-element.9, f32[768]{0:T(1024)S(1)} %get-tuple-element.11, s32[768]{0:T(1024)S(1)} %pad_add_fusion, s32[768]{0:T(1024)S(1)} %fusion.16), kind=kOutput, calls=%fused_computation.18 | convolution fusion | flops 1213464576 | bytes 7090176 | tf_op jit(solution)/shard_map/dot_general | solution.py:90
  112.6 0.2 slice.51
  112.8 1.8 collective-permute-start.3
  114.6 3.0 %collective-permute-done.3 = f32[384,1024]{1,0:T(8,128)S(1)} collective-permute-done((f32[384,1024]{1,0:T(8,128)S(1)}, f32[384,1024]{1,0:T(8,128)S(1)}, u32[]{:S(2)}, u32[]{:S(2)}) %collective-permute-start.3) | collective-permute-done | bytes 1572896 | tf_op jit(solution)/shard_map/ppermute | solution.py:95
  117.6 1.5 slice_add_fusion
  119.1 44.1 %all-to-all-done.4 = f32[16,56,1024]{2,1,0:T(8,128)} async-done(((f32[16,56,1024]{2,1,0:T(8,128)}), f32[16,56,1024]{2,1,0:T(8,128)}, u32[]{:S(2)}, u32[]{:S(2)}) %all-to-all-start.4) | async-done | bytes 3670048 | tf_op jit(solution)/shard_map/all_to_all | solution.py:85
  163.2 3.6 %all-to-all-start.5 = ((f32[8,48,1024]{2,1,0:T(8,128)}), f32[8,48,1024]{2,1,0:T(8,128)S(1)}, u32[]{:S(2)}, u32[]{:S(2)}) async-start(f32[8,48,1024]{2,1,0:T(8,128)} %bitcast.5), calls=%async_computation.5 | async-start | bytes 3145728 | tf_op jit(solution)/shard_map/all_to_all | solution.py:96
  166.8 0.6 slice_reduce_fusion.5
  167.4 1.5 slice_reduce_fusion.3
  170.2 2.8 %slice_reduce_fusion = f32[48,1024]{1,0:T(8,128)} fusion(f32[16,56,1024]{2,1,0:T(8,128)} %all-to-all-done.4), kind=kLoop, calls=%fused_computation | loop fusion | flops 737280 | bytes 3342336 | tf_op jit(solution)/shard_map/reduce_sum | solution.py:86
  172.9 34.2 %all-to-all-done.5 = f32[8,48,1024]{2,1,0:T(8,128)S(1)} async-done(((f32[8,48,1024]{2,1,0:T(8,128)}), f32[8,48,1024]{2,1,0:T(8,128)S(1)}, u32[]{:S(2)}, u32[]{:S(2)}) %all-to-all-start.5) | async-done | bytes 1572896 | tf_op jit(solution)/shard_map/all_to_all | solution.py:96
  207.1 0.8 reduce_sum.129
  (20 shorter events, 0.2 us)
Async XLA Ops:
  0.6 31.5 %copy-start.1 = (bf16[48,1024]{1,0:T(8,128)(2,1)S(1)}, bf16[48,1024]{1,0:T(8,128)(2,1)}, u32[]{:S(2)}) copy-start(bf16[48,1024]{1,0:T(8,128)(2,1)} %param.3) | copy-start | bytes 294916
  32.1 10.9 %copy-start.2 = (s32[384]{0:T(512)S(1)}, s32[384]{0:T(512)}, u32[]{:S(2)}) copy-start(s32[384]{0:T(512)} %param.5) | copy-start | bytes 4612
  33.4 26.5 %all-to-all-start.1 = ((bf16[16,48,1024]{2,1,0:T(8,128)(2,1)}), bf16[16,48,1024]{2,1,0:T(8,128)(2,1)S(1)}, u32[]{:S(2)}, u32[]{:S(2)}) async-start(bf16[16,48,1024]{2,1,0:T(8,128)(2,1)} %broadcast_in_dim.21), calls=%async_computation.1 | async-start | bytes 3145728 | tf_op jit(solution)/shard_map/all_to_all | solution.py:15
  40.2 19.8 %collective-permute-start = (bf16[384,1024]{1,0:T(8,128)(2,1)S(1)}, bf16[384,1024]{1,0:T(8,128)(2,1)S(1)}, u32[]{:S(2)}, u32[]{:S(2)}) collective-permute-start(bf16[384,1024]{1,0:T(8,128)(2,1)S(1)} %bitcast.44), channel_id=1, source_target_pairs={{0,8},{8,0},{1,9},{9,1},{2,10},{10,2},{3,11},{11,3},{4,12},{12,4},... | collective-permute-start | bytes 2359304 | tf_op jit(solution)/shard_map/ppermute | solution.py:34
  43.0 13.6 %collective-permute-start.1 = (s32[384]{0:T(512)S(1)}, s32[384]{0:T(512)S(1)}, u32[]{:S(2)}, u32[]{:S(2)}) collective-permute-start(s32[384]{0:T(512)S(1)} %copy-done.2), channel_id=1, source_target_pairs={{0,128},{128,0},{1,129},{129,1},{2,130},{130,2},{3,131},{131,3},{4... | collective-permute-start | bytes 4616 | tf_op jit(solution)/shard_map/ppermute | solution.py:27
  60.0 1.2 copy-start
  61.2 0.9 copy-start.3
  83.1 4.0 %collective-permute-start.2 = (f32[896]{0:T(1024)S(1)}, f32[896]{0:T(1024)S(1)}, u32[]{:S(2)}, u32[]{:S(2)}) collective-permute-start(f32[896]{0:T(1024)S(1)} %concatenate.26), channel_id=1, source_target_pairs={{0,8},{8,0},{1,9},{9,1},{2,10},{10,2},{3,11},{11,3},{4,12},{12,4},... | collective-permute-start | bytes 10760 | tf_op jit(solution)/shard_map/ppermute | solution.py:65
  104.9 58.3 %all-to-all-start.4 = ((f32[16,56,1024]{2,1,0:T(8,128)}), f32[16,56,1024]{2,1,0:T(8,128)}, u32[]{:S(2)}, u32[]{:S(2)}) async-start(f32[16,56,1024]{2,1,0:T(8,128)} %concatenate.29), calls=%async_computation.4 | async-start | bytes 7340032 | tf_op jit(solution)/shard_map/all_to_all | solution.py:85
  112.8 4.8 %collective-permute-start.3 = (f32[384,1024]{1,0:T(8,128)S(1)}, f32[384,1024]{1,0:T(8,128)S(1)}, u32[]{:S(2)}, u32[]{:S(2)}) collective-permute-start(f32[384,1024]{1,0:T(8,128)S(1)} %slice.51), channel_id=1, source_target_pairs={{0,8},{8,0},{1,9},{9,1},{2,10},{10,2},{3,11},{11,3},{4,12},{12,4},... | collective-permute-start | bytes 4718600 | tf_op jit(solution)/shard_map/ppermute | solution.py:95
  163.2 43.9 %all-to-all-start.5 = ((f32[8,48,1024]{2,1,0:T(8,128)}), f32[8,48,1024]{2,1,0:T(8,128)S(1)}, u32[]{:S(2)}, u32[]{:S(2)}) async-start(f32[8,48,1024]{2,1,0:T(8,128)} %bitcast.5), calls=%async_computation.5 | async-start | bytes 3145728 | tf_op jit(solution)/shard_map/all_to_all | solution.py:96

commit v2 on v1

v2 whole, which is shorter than its diff:
```python
import jax
import jax.numpy as jnp
from jax import lax
from jax.sharding import Mesh, PartitionSpec as P

PLANE = ("xl", "y", "xh")
SWAP = [(0, 1), (1, 0)]


def combine(parts):
    high = jnp.max(parts, axis=0)
    return high + jnp.log(jnp.sum(jnp.exp(parts - high[None]), axis=0))


def turn(x, axis, step):
    count = lax.axis_size(axis)
    return lax.ppermute(x, axis, [(i, (i + step) % count) for i in range(count)])


def encode(x, scale):
    scaled = x * scale
    square = scaled * scaled
    fourth = square * square
    return jnp.where(scaled < 0, -fourth, fourth).astype(jnp.bfloat16)


def decode(x, unit):
    wide = x.astype(jnp.float32)
    root = jnp.sqrt(jnp.sqrt(jnp.abs(wide))) * unit
    return jnp.where(wide < 0, -root, root)


def split3(value, shape):
    high = value.astype(jnp.bfloat16)
    rest = value - high.astype(jnp.float32)
    mid = rest.astype(jnp.bfloat16)
    low = (rest - mid.astype(jnp.float32)).astype(jnp.bfloat16)
    row = lax.broadcasted_iota(jnp.int32, shape, len(shape) - 2)
    return jnp.where(row == 0, high, jnp.where(row == 1, mid, jnp.where(row == 2, low, 0)))


def inverse(value):
    return jnp.where(value > 0, 1.0 / value, 1.0)


def shards(image_embed, text_embed, pair_index):
    rows, width = image_embed.shape
    n_xl, n_z, n_c, n_y, n_xh = (lax.axis_size(a) for a in ("xl", "z", "c", "y", "xh"))
    n_plane = n_xl * n_y * n_xh
    pairs = rows * n_plane * n_z * n_c
    inv_root = width ** (-0.5)
    core = lax.axis_index("c")
    z = lax.axis_index("z")
    half = n_z * rows

    pair_other = lax.ppermute(pair_index, "xl", SWAP)
    first = lax.axis_index("xl") == 0
    pair_rows = jnp.concatenate(
        [jnp.where(first, pair_index, pair_other), jnp.where(first, pair_other, pair_index)]
    )

    image = lax.all_to_all(
        jnp.broadcast_to(image_embed[None], (n_plane, rows, width)), PLANE, 0, 0
    ).reshape(n_plane * rows, width)
    text_own = jnp.concatenate([text_embed] + [turn(text_embed, "z", -q) for q in range(1, n_z)])
    text = jnp.concatenate([text_own, lax.ppermute(text_own, "c", SWAP)], axis=0)

    scores = (
        lax.dot_general(image, text, (((1,), (1,)), ((), ())), preferred_element_type=jnp.float32)
        * inv_root
    )
    block = (lax.axis_index("y") * n_xh + lax.axis_index("xh")) * n_xl + lax.axis_index("xl")
    slot = lax.iota(jnp.int32, 2 * half)
    own = slot < half
    within = jnp.where(own, slot, slot - half)
    holder = (z + within // rows) % n_z
    column = ((block * n_z + holder) * n_c + jnp.where(own, core, 1 - core)) * rows + within % rows
    positive = pair_rows[:, None] == column[None, :]
    matched = jnp.sum(jnp.where(positive, scores, 0.0))
    text_max = jnp.max(jnp.abs(text)).astype(jnp.float32)
    image_max = jnp.max(jnp.abs(image)).astype(jnp.float32)

    row_high = jnp.max(scores, axis=1)
    row_part = row_high + jnp.log(jnp.sum(jnp.exp(scores - row_high[:, None]), axis=1))
    col_high = jnp.max(scores, axis=0)
    col_part = col_high + jnp.log(jnp.sum(jnp.exp(scores - col_high[None, :]), axis=0))

    row_sent = jnp.concatenate(
        [row_part, jnp.broadcast_to(matched, (128,)), jnp.broadcast_to(text_max, (128,))]
    )
    row_got = lax.all_to_all(
        jnp.broadcast_to(row_sent[None], (n_plane,) + row_sent.shape), PLANE, 0, 0
    )
    row_lse = combine(row_got[:, : 2 * half])
    row_terms = jnp.sum(row_lse) - 2.0 * jnp.sum(row_got[:, 2 * half])
    text_max = jnp.max(row_got[:, 2 * half + 128])

    ring = jnp.concatenate([col_part.reshape(2, n_z, rows)] * 2, axis=1)
    col_sorted = lax.dynamic_slice_in_dim(ring, n_z - z, n_z, axis=1).reshape(2 * half)
    col_sent = jnp.concatenate([col_sorted, jnp.broadcast_to(image_max, (128,))])
    col_seen = lax.ppermute(col_sent, "c", SWAP)
    col_seen = jnp.concatenate([col_seen[half : 2 * half], col_seen[:half], col_seen[2 * half :]])
    col_pair = jnp.concatenate(
        [
            combine(jnp.stack([col_sent[: 2 * half], col_seen[: 2 * half]])),
            jnp.maximum(col_sent[2 * half :], col_seen[2 * half :]),
        ]
    )
    col_got = jnp.stack([col_pair] + [turn(col_pair, "z", q) for q in range(1, n_z)])
    col_sorted = combine(col_got[:, : 2 * half])
    image_max = jnp.max(col_got[:, 2 * half])
    col_terms = jnp.sum(col_sorted)
    ring = jnp.concatenate([col_sorted.reshape(2, n_z, rows)] * 2, axis=1)
    col_lse = lax.dynamic_slice_in_dim(ring, z, n_z, axis=1).reshape(2 * half)

    probs = 0.5 * (jnp.exp(scores - row_lse[:, None]) + jnp.exp(scores - col_lse[None, :]))
    grad_scores = (probs - positive.astype(jnp.float32)).astype(jnp.bfloat16)

    image_part = jnp.dot(grad_scores, text, preferred_element_type=jnp.float32) * inv_root
    image_sent = jnp.concatenate(
        [
            encode(image_part, inverse(text_max)).reshape(n_plane, rows, width),
            split3(col_terms, (n_plane, 8, width)),
        ],
        axis=1,
    )
    image_got = lax.all_to_all(image_sent, PLANE, 0, 0)

    text_part = (
        lax.dot_general(
            grad_scores, image, (((0,), (0,)), ((), ())), preferred_element_type=jnp.float32
        )
        * inv_root
    )
    row_terms = row_terms + lax.ppermute(row_terms, "c", SWAP)
    text_sum = text_part[:half] + lax.ppermute(text_part[half:], "c", SWAP)
    text_sum = text_sum.reshape(n_z, rows, width)
    text_sent = jnp.concatenate(
        [
            encode(text_sum[1:], inverse(image_max)),
            split3(row_terms, (n_z - 1, 8, width)),
        ],
        axis=1,
    )
    text_got = jnp.stack([turn(text_sent[q - 1], "z", q) for q in range(1, n_z)])
    grad_text = text_sum[0] + jnp.sum(decode(text_got[:, :rows], 1.0 / inverse(image_max)), axis=0)
    grad_image = jnp.sum(decode(image_got[:, :rows], 1.0 / inverse(text_max)), axis=0)
    loss = (
        row_terms
        + jnp.sum(text_got[:, rows : rows + 3, 0].astype(jnp.float32))
        + jnp.sum(image_got[:, rows : rows + 3, 0].astype(jnp.float32))
    ) / (2.0 * pairs)
    return (loss, grad_image, grad_text)


def solution(mesh):
    fine = Mesh(mesh.devices.reshape(2, 8, 2, 4, 2), ("xl", "z", "c", "y", "xh"))
    image_spec = P(("xl", "z", "c", "y", "xh"), None)
    text_spec = P(("y", "xh", "xl", "z", "c"), None)
    return jax.shard_map(
        shards,
        mesh=fine,
        in_specs=(image_spec, text_spec, P(("xl", "z", "c"))),
        out_specs=(P(), image_spec, text_spec),
        check_vma=False,
    )
```

time: 210 us -> 154 us (0.73)
  waiting for transfers between devices: 97.5 us -> 24.4 us
  blocking collectives: 53.3 us -> 0 us
  starting transfers between devices: 24.2 us -> 73 us
  local copies, waits for them, and re-layouts: 8.72 us -> 18.5 us
  other arithmetic: 10.7 us -> 17.7 us
  between operations: 5.19 us -> 10.1 us
    all_to_all x3 -> x0, blocking collectives: 53.3 us -> none  [spread(): lax.all_to_all(jnp.broadcast_to(x[None], (count,) + x.shape), axes, 0, 0)]
    ppermute x4 -> x26, starting transfers between devices: 9.41 us -> 56.4 us  [the longest x21 48.2 us: turn(): lax.ppermute(x, axis, [(i, (i + step) % count) for i in range(count)])]
    all_to_all x1, waiting for transfers between devices: 44.1 us -> 0.01 us  [shards(): image_got = lax.all_to_all(image_sent, PLANE, 0, 0)]
    all_to_all x2, waiting for transfers between devices: 37.5 us -> 6.44 us  [the longest x1 6.44 us: shards(): lax.all_to_all(jnp.broadcast_to(row_sent[None], (n_plane,) + row_sent.sha...]
    unnamed x10 -> x26, local copies, waits for them, and re-layouts: 2.12 us -> 11.2 us
    reduce_max x0 -> x4, other arithmetic: none -> 2.99 us  [the longest x1 0.89 us: shards(): image_max = jnp.max(jnp.abs(image)).astype(jnp.float32)]
    all_to_all x2, starting transfers between devices: 10.3 us -> 12.8 us  [the longest x1 6.89 us: shards(): lax.all_to_all(jnp.broadcast_to(image_embed[None], (n_plane, rows, width)...]
    ppermute x4 -> x26, waiting for transfers between devices: 15.9 us -> 18 us  [the longest x21 16.5 us: turn(): lax.ppermute(x, axis, [(i, (i + step) % count) for i in range(count)])]
  transfers between devices with their start and end apart: 7 -> 29, of which waited for: 6 -> 7; matrix products, arithmetic and copies ran while one was open for 5% -> 17% of each run, Pallas kernels for 0% -> 0%
where the time goes in v2:
time: 154 us
  starting transfers between devices  73 us (47%)
  waiting for transfers between devices  24.4 us (16%)
  local copies, waits for them, and re-layouts  18.5 us (12%)
  other arithmetic  17.7 us (11%)
  between operations  10.1 us (7%)
  matrix products  10 us (6%)
    ppermute x21, starting transfers between devices, turn(): lax.ppermute(x, axis, [(i, (i + step) % count) for i in range(count)])  48.2 us
    ppermute x21, waiting for transfers between devices, turn(): lax.ppermute(x, axis, [(i, (i + step) % count) for i in range(count)])  16.5 us
    unnamed x26, local copies, waits for them, and re-layouts  11.2 us
    all_to_all x1, starting transfers between devices, shards(): lax.all_to_all(jnp.broadcast_to(image_embed[None], (n_plane, rows, width)...  6.89 us
    all_to_all x1, waiting for transfers between devices, shards(): lax.all_to_all(jnp.broadcast_to(row_sent[None], (n_plane,) + row_sent.sha...  6.44 us
    all_to_all x1, starting transfers between devices, shards(): lax.all_to_all(jnp.broadcast_to(row_sent[None], (n_plane,) + row_sent.sha...  5.92 us
    dot_general x1, matrix products, shards(): jnp.dot(grad_scores, text, preferred_element_type=jnp.float32) * inv_root  5.07 us
    all_to_all x1, starting transfers between devices, shards(): image_got = lax.all_to_all(image_sent, PLANE, 0, 0)  3.71 us
  transfers between devices with their start and end apart: 29, of which 7 were waited for; matrix products, arithmetic and copies ran while one was open for 17% of the time, Pallas kernels for 0%

profile of v2, /device:TPU:1, one launch (start us, length us, event | category | flops | bytes accessed | tf_op | source)
XLA Modules:
  0.0 153.6 jit_solution(7397401490290397020)
XLA Ops:
  0.6 3.9 %collective-permute-start.5 = (bf16[48,1024]{1,0:T(8,128)(2,1)}, bf16[48,1024]{1,0:T(8,128)(2,1)S(1)}, u32[]{:S(2)}, u32[]{:S(2)}) collective-permute-start(bf16[48,1024]{1,0:T(8,128)(2,1)} %param.4), channel_id=1, source_target_pairs={{0,32},{16,48},{32,64},{48,80},{64,96},{80,112},{96,0},{112,16},{1... | collective-permute-start | bytes 294920 | tf_op jit(solution)/shard_map/ppermute | solution.py:17
  4.5 4.7 %collective-permute-start.4 = (bf16[48,1024]{1,0:T(8,128)(2,1)}, bf16[48,1024]{1,0:T(8,128)(2,1)S(1)}, u32[]{:S(2)}, u32[]{:S(2)}) collective-permute-start(bf16[48,1024]{1,0:T(8,128)(2,1)} %param.4), channel_id=1, source_target_pairs={{0,48},{16,64},{32,80},{48,96},{64,112},{80,0},{96,16},{112,32},{1... | collective-permute-start | bytes 294920 | tf_op jit(solution)/shard_map/ppermute | solution.py:17
  9.2 1.0 collective-permute-start.3
  10.2 3.9 %collective-permute-start.2 = (bf16[48,1024]{1,0:T(8,128)(2,1)}, bf16[48,1024]{1,0:T(8,128)(2,1)}, u32[]{:S(2)}, u32[]{:S(2)}) collective-permute-start(bf16[48,1024]{1,0:T(8,128)(2,1)} %param.4), channel_id=1, source_target_pairs={{0,80},{16,96},{32,112},{48,0},{64,16},{80,32},{96,48},{112,64},{1... | collective-permute-start | bytes 294920 | tf_op jit(solution)/shard_map/ppermute | solution.py:17
  14.8 2.2 %broadcast_in_dim.69 = bf16[16,48,1024]{2,1,0:T(8,128)(2,1)} broadcast(bf16[48,1024]{1,0:T(8,128)(2,1)} %param.3), dimensions={1,2} | broadcast | bytes 1671168 | tf_op jit(solution)/shard_map/broadcast_in_dim | solution.py:63
  17.1 6.9 %all-to-all-start = ((bf16[16,48,1024]{2,1,0:T(8,128)(2,1)}), bf16[16,48,1024]{2,1,0:T(8,128)(2,1)S(1)}, u32[]{:S(2)}, u32[]{:S(2)}) async-start(bf16[16,48,1024]{2,1,0:T(8,128)(2,1)} %broadcast_in_dim.69), calls=%async_computation | async-start | bytes 3145728 | tf_op jit(solution)/shard_map/all_to_all | solution.py:62
  24.6 2.4 %collective-permute-start.1 = (bf16[48,1024]{1,0:T(8,128)(2,1)S(1)}, bf16[48,1024]{1,0:T(8,128)(2,1)S(1)}, u32[]{:S(2)}, u32[]{:S(2)}) collective-permute-start(bf16[48,1024]{1,0:T(8,128)(2,1)S(1)} %copy-done.3), channel_id=1, source_target_pairs={{0,96},{16,112},{32,0},{48,16},{64,32},{80,48},{96,64},{112,80},{1... | collective-permute-start | bytes 294920 | tf_op jit(solution)/shard_map/ppermute | solution.py:17
  27.0 1.5 %constant_dynamic-update-slice_fusion.6 = (bf16[384,1024]{1,0:T(8,128)(2,1)}, bf16[768,1024]{1,0:T(8,128)(2,1)S(1)}) fusion(bf16[384,1024]{1,0:T(8,128)(2,1)} %get-tuple-element.35, bf16[48,1024]{1,0:T(8,128)(2,1)} %collective-permute-done, bf16[768,1024]{1,0:T(8,128)(2,1)S(1)} %get-tuple-element.36), kind=kLoop, calls=%fused_computation.87 | loop fusion | bytes 294912
  28.6 0.9 collective-permute-done.1
  29.5 6.3 %collective-permute-start.6 = (bf16[48,1024]{1,0:T(8,128)(2,1)S(1)}, bf16[48,1024]{1,0:T(8,128)(2,1)S(1)}, u32[]{:S(2)}, u32[]{:S(2)}) collective-permute-start(bf16[48,1024]{1,0:T(8,128)(2,1)S(1)} %copy-done.3), channel_id=1, source_target_pairs={{0,16},{16,32},{32,48},{48,64},{64,80},{80,96},{96,112},{112,0},{1... | collective-permute-start | bytes 294920 | tf_op jit(solution)/shard_map/ppermute | solution.py:17
  36.4 1.5 %constant_dynamic-update-slice_fusion.4 = (bf16[384,1024]{1,0:T(8,128)(2,1)}, bf16[768,1024]{1,0:T(8,128)(2,1)S(1)}) fusion(bf16[384,1024]{1,0:T(8,128)(2,1)} %get-tuple-element.31, bf16[48,1024]{1,0:T(8,128)(2,1)} %collective-permute-done.2, bf16[768,1024]{1,0:T(8,128)(2,1)S(1)} %get-tuple-element.32), kind=kLoop, calls=%fused_computation.85 | loop fusion | bytes 294912
  40.6 1.0 collective-permute-start.7
  41.5 1.2 collective-permute-start.8
  42.8 1.5 collective-permute-done.8
  44.3 1.2 constant_dynamic-update-slice_fusion.8
  45.5 1.5 fusion.58
  47.0 1.4 copy-done.1
  48.4 1.7 %fusion.14 = (f32[768]{0:T(1024)S(1)}, f32[]{:T(128)}, f32[768]{0:T(1024)S(1)}) fusion(f32[768,768]{1,0:T(8,128)S(1)} %get-tuple-element.43, f32[768]{0:T(1024)S(1)} %get-tuple-element.6, s32[768]{0:T(1024)S(1)} %fusion.42, s32[768]{0:T(1024)S(1)} %pad_add_fusion, f32[768]{0:T(1024)S(1)} %get-tuple-element.7), kind=kLoop, calls=%fused_computation.24 | loop fusion | flops 4127231 | bytes 2377732 | tf_op jit(solution)/shard_map/reduce_sum | solution.py:86
  50.3 0.9 abs_reduce_fusion
  51.8 1.9 %collective-permute-start.10 = (f32[896]{0:T(1024)S(1)}, f32[896]{0:T(1024)S(1)}, u32[]{:S(2)}, u32[]{:S(2)}) collective-permute-start(f32[896]{0:T(1024)S(1)} %concatenate.41), channel_id=1, source_target_pairs={{0,8},{8,0},{1,9},{9,1},{2,10},{10,2},{3,11},{11,3},{4,12},{12,4},... | collective-permute-start | bytes 10760 | tf_op jit(solution)/shard_map/ppermute | solution.py:101
  53.7 0.9 abs_reduce_fusion.1
  55.4 2.0 %collective-permute-start.17 = (f32[896]{0:T(1024)S(1)}, f32[896]{0:T(1024)S(1)}, u32[]{:S(2)}, u32[]{:S(2)}) collective-permute-start(f32[896]{0:T(1024)S(1)} %pad_maximum_fusion.4), channel_id=1, source_target_pairs={{0,112},{16,0},{32,16},{48,32},{64,48},{80,64},{96,80},{112,96},{1... | collective-permute-start | bytes 10760 | tf_op jit(solution)/shard_map/ppermute | solution.py:17
  57.5 2.8 %collective-permute-start.15 = (f32[896]{0:T(1024)S(1)}, f32[896]{0:T(1024)S(1)}, u32[]{:S(2)}, u32[]{:S(2)}) collective-permute-start(f32[896]{0:T(1024)S(1)} %pad_maximum_fusion.4), channel_id=1, source_target_pairs={{0,80},{16,96},{32,112},{48,0},{64,16},{80,32},{96,48},{112,64},{1... | collective-permute-start | bytes 10760 | tf_op jit(solution)/shard_map/ppermute | solution.py:17
  60.3 2.6 %collective-permute-start.14 = (f32[896]{0:T(1024)S(1)}, f32[896]{0:T(1024)S(1)}, u32[]{:S(2)}, u32[]{:S(2)}) collective-permute-start(f32[896]{0:T(1024)S(1)} %pad_maximum_fusion.4), channel_id=1, source_target_pairs={{0,64},{16,80},{32,96},{48,112},{64,0},{80,16},{96,32},{112,48},{1... | collective-permute-start | bytes 10760 | tf_op jit(solution)/shard_map/ppermute | solution.py:17
  62.9 1.1 collective-permute-start.13
  64.0 1.3 collective-permute-start.12
  68.0 5.9 %all-to-all-start.1 = ((f32[16,1,1024]{2,1,0:T(1,128)}), f32[16,1,1024]{2,1,0:T(1,128)S(1)}, u32[]{:S(2)}, u32[]{:S(2)}) async-start(f32[16,1,1024]{2,1,0:T(1,128)} %broadcast_in_dim.75), calls=%async_computation.1 | async-start | bytes 131072 | tf_op jit(solution)/shard_map/all_to_all | solution.py:91
  74.2 6.4 %all-to-all-done.1 = f32[16,1,1024]{2,1,0:T(1,128)S(1)} async-done(((f32[16,1,1024]{2,1,0:T(1,128)}), f32[16,1,1024]{2,1,0:T(1,128)S(1)}, u32[]{:S(2)}, u32[]{:S(2)}) %all-to-all-start.1) | async-done | bytes 65568 | tf_op jit(solution)/shard_map/all_to_all | solution.py:91
  81.5 3.4 %convolution_multiply_fusion = f32[768,1024]{1,0:T(8,128)S(1)} fusion(bf16[768,1024]{1,0:T(8,128)(2,1)S(1)} %bitcast.68, f32[768,768]{1,0:T(8,128)} %copy-done.1, f32[768]{0:T(1024)S(1)} %sub.110, f32[768]{0:T(1024)S(1)} %get-tuple-element.45, s32[768]{0:T(1024)S(1)} %pad_add_fusion, s32[768]{0:T(1024)S(1)} %fusion.42), kind=kOutput, calls=%fused_computation.34 | convolution fusion | flops 1213464576 | bytes 7090176 | tf_op jit(solution)/shard_map/dot_general | solution.py:130
  85.1 1.5 %copy-done = f32[768,1024]{1,0:T(8,128)} copy-done((f32[768,1024]{1,0:T(8,128)}, f32[768,1024]{1,0:T(8,128)S(1)}, u32[]{:S(2)}) %copy-start) | copy-done | bytes 3145752
  86.6 3.1 %collective-permute-start.18 = (f32[384,1024]{1,0:T(8,128)S(1)}, f32[384,1024]{1,0:T(8,128)}, u32[]{:S(2)}, u32[]{:S(2)}) collective-permute-start(f32[384,1024]{1,0:T(8,128)S(1)} %slice.98), channel_id=1, source_target_pairs={{0,8},{8,0},{1,9},{9,1},{2,10},{10,2},{3,11},{11,3},{4,12},{12,4},... | collective-permute-start | bytes 4718600 | tf_op jit(solution)/shard_map/ppermute | solution.py:136
  96.2 1.0 collective-permute-start.9
  97.4 5.1 %fusion.3 = bf16[768,1024]{1,0:T(8,128)(2,1)} fusion(bf16[768,1024]{1,0:T(8,128)(2,1)S(1)} %constant_dynamic-update-slice_fusion.8, f32[]{:T(128)S(6)} %mul.106, f32[768,768]{1,0:T(8,128)} %copy-done.1, f32[768]{0:T(1024)S(1)} %sub.110, f32[768]{0:T(1024)S(1)} %get-tuple-element.45, s32[768]{0:T(1024)S(1)} %pad_add_fusion, s32[768]{0:T(1024)S(1)} %fusion.42), kind=kOutput, calls=%fused_computation.7 | convolution fusion | flops 1218183168 | bytes 5517316 | tf_op jit(solution)/shard_map/dot_general | solution.py:119
  103.2 2.2 %slice_add_fusion = f32[384,1024]{1,0:T(8,128)S(1)} fusion(f32[384,1024]{1,0:T(8,128)} %collective-permute-done.18, f32[768,1024]{1,0:T(8,128)} %copy-done), kind=kLoop, calls=%fused_computation.39 | loop fusion | flops 393216 | bytes 4718592 | tf_op jit(solution)/shard_map/add | solution.py:136
  107.6 1.4 pad_maximum_fusion
  109.0 3.7 %all-to-all-start.2 = ((bf16[16,56,1024]{2,1,0:T(8,128)(2,1)}), bf16[16,56,1024]{2,1,0:T(8,128)(2,1)S(1)}, u32[]{:S(2)}, u32[]{:S(2)}) async-start(bf16[16,56,1024]{2,1,0:T(8,128)(2,1)} %pad_maximum_fusion), calls=%async_computation.2 | async-start | bytes 3670016 | tf_op jit(solution)/shard_map/all_to_all | solution.py:127
  112.7 2.6 %collective-permute-start.25 = (bf16[56,1024]{1,0:T(8,128)(2,1)S(1)}, bf16[56,1024]{1,0:T(8,128)(2,1)S(1)}, u32[]{:S(2)}, u32[]{:S(2)}) collective-permute-start(bf16[56,1024]{1,0:T(8,128)(2,1)S(1)} %get-tuple-element.14), channel_id=1, source_target_pairs={{0,112},{16,0},{32,16},{48,32},{64,48},{80,64},{96,80},{112,96},{1... | collective-permute-start | bytes 344072 | tf_op jit(solution)/shard_map/ppermute | solution.py:17
  115.3 1.7 %collective-permute-start.20 = (bf16[56,1024]{1,0:T(8,128)(2,1)}, bf16[56,1024]{1,0:T(8,128)(2,1)S(1)}, u32[]{:S(2)}, u32[]{:S(2)}) collective-permute-start(bf16[56,1024]{1,0:T(8,128)(2,1)} %get-tuple-element.16), channel_id=1, source_target_pairs={{0,32},{16,48},{32,64},{48,80},{64,96},{80,112},{96,0},{112,16},{1... | collective-permute-start | bytes 344072 | tf_op jit(solution)/shard_map/ppermute | solution.py:17
  116.9 1.7 %collective-permute-start.21 = (bf16[56,1024]{1,0:T(8,128)(2,1)}, bf16[56,1024]{1,0:T(8,128)(2,1)S(1)}, u32[]{:S(2)}, u32[]{:S(2)}) collective-permute-start(bf16[56,1024]{1,0:T(8,128)(2,1)} %get-tuple-element.17), channel_id=1, source_target_pairs={{0,48},{16,64},{32,80},{48,96},{64,112},{80,0},{96,16},{112,32},{1... | collective-permute-start | bytes 344072 | tf_op jit(solution)/shard_map/ppermute | solution.py:17
  118.6 2.6 %collective-permute-start.22 = (bf16[56,1024]{1,0:T(8,128)(2,1)}, bf16[56,1024]{1,0:T(8,128)(2,1)S(1)}, u32[]{:S(2)}, u32[]{:S(2)}) collective-permute-start(bf16[56,1024]{1,0:T(8,128)(2,1)} %get-tuple-element.18), channel_id=1, source_target_pairs={{0,64},{16,80},{32,96},{48,112},{64,0},{80,16},{96,32},{112,48},{1... | collective-permute-start | bytes 344072 | tf_op jit(solution)/shard_map/ppermute | solution.py:17
  121.2 2.7 %collective-permute-start.23 = (bf16[56,1024]{1,0:T(8,128)(2,1)}, bf16[56,1024]{1,0:T(8,128)(2,1)S(1)}, u32[]{:S(2)}, u32[]{:S(2)}) collective-permute-start(bf16[56,1024]{1,0:T(8,128)(2,1)} %get-tuple-element.19), channel_id=1, source_target_pairs={{0,80},{16,96},{32,112},{48,0},{64,16},{80,32},{96,48},{112,64},{1... | collective-permute-start | bytes 344072 | tf_op jit(solution)/shard_map/ppermute | solution.py:17
  124.0 0.9 bitcast_dynamic-update-slice_fusion.6
  125.4 2.9 %collective-permute-start.24 = (bf16[56,1024]{1,0:T(8,128)(2,1)}, bf16[56,1024]{1,0:T(8,128)(2,1)S(1)}, u32[]{:S(2)}, u32[]{:S(2)}) collective-permute-start(bf16[56,1024]{1,0:T(8,128)(2,1)} %get-tuple-element.20), channel_id=1, source_target_pairs={{0,96},{16,112},{32,0},{48,16},{64,32},{80,48},{96,64},{112,80},{1... | collective-permute-start | bytes 344072 | tf_op jit(solution)/shard_map/ppermute | solution.py:17
  128.4 5.3 %collective-permute-done.21 = bf16[56,1024]{1,0:T(8,128)(2,1)S(1)} collective-permute-done((bf16[56,1024]{1,0:T(8,128)(2,1)}, bf16[56,1024]{1,0:T(8,128)(2,1)S(1)}, u32[]{:S(2)}, u32[]{:S(2)}) %collective-permute-start.21) | collective-permute-done | bytes 114720 | tf_op jit(solution)/shard_map/ppermute | solution.py:17
  133.7 2.0 %collective-permute-done.23 = bf16[56,1024]{1,0:T(8,128)(2,1)S(1)} collective-permute-done((bf16[56,1024]{1,0:T(8,128)(2,1)}, bf16[56,1024]{1,0:T(8,128)(2,1)S(1)}, u32[]{:S(2)}, u32[]{:S(2)}) %collective-permute-start.23) | collective-permute-done | bytes 114720 | tf_op jit(solution)/shard_map/ppermute | solution.py:17
  135.7 7.7 %collective-permute-done.24 = bf16[56,1024]{1,0:T(8,128)(2,1)S(1)} collective-permute-done((bf16[56,1024]{1,0:T(8,128)(2,1)}, bf16[56,1024]{1,0:T(8,128)(2,1)S(1)}, u32[]{:S(2)}, u32[]{:S(2)}) %collective-permute-start.24) | collective-permute-done | bytes 114720 | tf_op jit(solution)/shard_map/ppermute | solution.py:17
  145.6 2.1 %fusion.20 = f32[48,1024]{1,0:T(8,128)S(1)} fusion(bf16[7,56,1024]{2,1,0:T(8,128)(2,1)} %copy-done.4, f32[]{:T(128)S(6)} %div.32), kind=kLoop, calls=%fused_computation.46 | loop fusion | flops 2359296 | bytes 884740 | tf_op jit(solution)/shard_map/reduce_sum | solution.py:146
  149.7 2.9 %fusion.4 = f32[48,1024]{1,0:T(8,128)} fusion(bf16[16,56,1024]{2,1,0:T(8,128)(2,1)S(1)} %all-to-all-done.2, f32[]{:T(128)S(6)} %div.31), kind=kLoop, calls=%fused_computation.8 | loop fusion | flops 5455872 | bytes 1769476 | tf_op jit(solution)/shard_map/reduce_sum | solution.py:147
  (103 shorter events, 16.4 us)
Async XLA Ops:
  0.6 38.6 %collective-permute-start.5 = (bf16[48,1024]{1,0:T(8,128)(2,1)}, bf16[48,1024]{1,0:T(8,128)(2,1)S(1)}, u32[]{:S(2)}, u32[]{:S(2)}) collective-permute-start(bf16[48,1024]{1,0:T(8,128)(2,1)} %param.4), channel_id=1, source_target_pairs={{0,32},{16,48},{32,64},{48,80},{64,96},{80,112},{96,0},{112,16},{1... | collective-permute-start | bytes 294920 | tf_op jit(solution)/shard_map/ppermute | solution.py:17
  4.5 34.1 %collective-permute-start.4 = (bf16[48,1024]{1,0:T(8,128)(2,1)}, bf16[48,1024]{1,0:T(8,128)(2,1)S(1)}, u32[]{:S(2)}, u32[]{:S(2)}) collective-permute-start(bf16[48,1024]{1,0:T(8,128)(2,1)} %param.4), channel_id=1, source_target_pairs={{0,48},{16,64},{32,80},{48,96},{64,112},{80,0},{96,16},{112,32},{1... | collective-permute-start | bytes 294920 | tf_op jit(solution)/shard_map/ppermute | solution.py:17
  9.2 28.7 %collective-permute-start.3 = (bf16[48,1024]{1,0:T(8,128)(2,1)}, bf16[48,1024]{1,0:T(8,128)(2,1)S(1)}, u32[]{:S(2)}, u32[]{:S(2)}) collective-permute-start(bf16[48,1024]{1,0:T(8,128)(2,1)} %param.4), channel_id=1, source_target_pairs={{0,64},{16,80},{32,96},{48,112},{64,0},{80,16},{96,32},{112,48},{1... | collective-permute-start | bytes 294920 | tf_op jit(solution)/shard_map/ppermute | solution.py:17
  10.2 26.2 %collective-permute-start.2 = (bf16[48,1024]{1,0:T(8,128)(2,1)}, bf16[48,1024]{1,0:T(8,128)(2,1)}, u32[]{:S(2)}, u32[]{:S(2)}) collective-permute-start(bf16[48,1024]{1,0:T(8,128)(2,1)} %param.4), channel_id=1, source_target_pairs={{0,80},{16,96},{32,112},{48,0},{64,16},{80,32},{96,48},{112,64},{1... | collective-permute-start | bytes 294920 | tf_op jit(solution)/shard_map/ppermute | solution.py:17
  14.1 10.5 %collective-permute-start = (bf16[48,1024]{1,0:T(8,128)(2,1)}, bf16[48,1024]{1,0:T(8,128)(2,1)}, u32[]{:S(2)}, u32[]{:S(2)}) collective-permute-start(bf16[48,1024]{1,0:T(8,128)(2,1)} %param.4), channel_id=1, source_target_pairs={{0,112},{16,0},{32,16},{48,32},{64,48},{80,64},{96,80},{112,96},{1... | collective-permute-start | bytes 294920 | tf_op jit(solution)/shard_map/ppermute | solution.py:17
  17.1 6.9 %copy-start.3 = (bf16[48,1024]{1,0:T(8,128)(2,1)S(1)}, bf16[48,1024]{1,0:T(8,128)(2,1)}, u32[]{:S(2)}) copy-start(bf16[48,1024]{1,0:T(8,128)(2,1)} %param.4) | copy-start | bytes 294916
  17.1 28.4 %all-to-all-start = ((bf16[16,48,1024]{2,1,0:T(8,128)(2,1)}), bf16[16,48,1024]{2,1,0:T(8,128)(2,1)S(1)}, u32[]{:S(2)}, u32[]{:S(2)}) async-start(bf16[16,48,1024]{2,1,0:T(8,128)(2,1)} %broadcast_in_dim.69), calls=%async_computation | async-start | bytes 3145728 | tf_op jit(solution)/shard_map/all_to_all | solution.py:62
  24.0 17.5 %copy-start.5 = (s32[384]{0:T(512)S(1)}, s32[384]{0:T(512)}, u32[]{:S(2)}) copy-start(s32[384]{0:T(512)} %param.5) | copy-start | bytes 4612
  24.6 4.8 %collective-permute-start.1 = (bf16[48,1024]{1,0:T(8,128)(2,1)S(1)}, bf16[48,1024]{1,0:T(8,128)(2,1)S(1)}, u32[]{:S(2)}, u32[]{:S(2)}) collective-permute-start(bf16[48,1024]{1,0:T(8,128)(2,1)S(1)} %copy-done.3), channel_id=1, source_target_pairs={{0,96},{16,112},{32,0},{48,16},{64,32},{80,48},{96,64},{112,80},{1... | collective-permute-start | bytes 294920 | tf_op jit(solution)/shard_map/ppermute | solution.py:17
  29.5 10.4 %collective-permute-start.6 = (bf16[48,1024]{1,0:T(8,128)(2,1)S(1)}, bf16[48,1024]{1,0:T(8,128)(2,1)S(1)}, u32[]{:S(2)}, u32[]{:S(2)}) collective-permute-start(bf16[48,1024]{1,0:T(8,128)(2,1)S(1)} %copy-done.3), channel_id=1, source_target_pairs={{0,16},{16,32},{32,48},{48,64},{64,80},{80,96},{96,112},{112,0},{1... | collective-permute-start | bytes 294920 | tf_op jit(solution)/shard_map/ppermute | solution.py:17
  40.6 3.7 %collective-permute-start.7 = (bf16[384,1024]{1,0:T(8,128)(2,1)}, bf16[384,1024]{1,0:T(8,128)(2,1)}, u32[]{:S(2)}, u32[]{:S(2)}) collective-permute-start(bf16[384,1024]{1,0:T(8,128)(2,1)} %get-tuple-element.21), channel_id=1, source_target_pairs={{0,8},{8,0},{1,9},{9,1},{2,10},{10,2},{3,11},{11,3},{4,12},{12,4},... | collective-permute-start | bytes 2359304 | tf_op jit(solution)/shard_map/ppermute | solution.py:66
  41.5 2.7 %collective-permute-start.8 = (s32[384]{0:T(512)S(1)}, s32[384]{0:T(512)S(1)}, u32[]{:S(2)}, u32[]{:S(2)}) collective-permute-start(s32[384]{0:T(512)S(1)} %copy-done.5), channel_id=1, source_target_pairs={{0,128},{128,0},{1,129},{129,1},{2,130},{130,2},{3,131},{131,3},{4... | collective-permute-start | bytes 4616 | tf_op jit(solution)/shard_map/ppermute | solution.py:56
  47.0 1.4 copy-start.1
  51.8 3.5 %collective-permute-start.10 = (f32[896]{0:T(1024)S(1)}, f32[896]{0:T(1024)S(1)}, u32[]{:S(2)}, u32[]{:S(2)}) collective-permute-start(f32[896]{0:T(1024)S(1)} %concatenate.41), channel_id=1, source_target_pairs={{0,8},{8,0},{1,9},{9,1},{2,10},{10,2},{3,11},{11,3},{4,12},{12,4},... | collective-permute-start | bytes 10760 | tf_op jit(solution)/shard_map/ppermute | solution.py:101
  55.4 8.6 %collective-permute-start.17 = (f32[896]{0:T(1024)S(1)}, f32[896]{0:T(1024)S(1)}, u32[]{:S(2)}, u32[]{:S(2)}) collective-permute-start(f32[896]{0:T(1024)S(1)} %pad_maximum_fusion.4), channel_id=1, source_target_pairs={{0,112},{16,0},{32,16},{48,32},{64,48},{80,64},{96,80},{112,96},{1... | collective-permute-start | bytes 10760 | tf_op jit(solution)/shard_map/ppermute | solution.py:17
  57.5 7.9 %collective-permute-start.16 = (f32[896]{0:T(1024)S(1)}, f32[896]{0:T(1024)S(1)}, u32[]{:S(2)}, u32[]{:S(2)}) collective-permute-start(f32[896]{0:T(1024)S(1)} %pad_maximum_fusion.4), channel_id=1, source_target_pairs={{0,96},{16,112},{32,0},{48,16},{64,32},{80,48},{96,64},{112,80},{1... | collective-permute-start | bytes 10760 | tf_op jit(solution)/shard_map/ppermute | solution.py:17
  57.5 16.5 %collective-permute-start.15 = (f32[896]{0:T(1024)S(1)}, f32[896]{0:T(1024)S(1)}, u32[]{:S(2)}, u32[]{:S(2)}) collective-permute-start(f32[896]{0:T(1024)S(1)} %pad_maximum_fusion.4), channel_id=1, source_target_pairs={{0,80},{16,96},{32,112},{48,0},{64,16},{80,32},{96,48},{112,64},{1... | collective-permute-start | bytes 10760 | tf_op jit(solution)/shard_map/ppermute | solution.py:17
  60.3 13.7 %collective-permute-start.14 = (f32[896]{0:T(1024)S(1)}, f32[896]{0:T(1024)S(1)}, u32[]{:S(2)}, u32[]{:S(2)}) collective-permute-start(f32[896]{0:T(1024)S(1)} %pad_maximum_fusion.4), channel_id=1, source_target_pairs={{0,64},{16,80},{32,96},{48,112},{64,0},{80,16},{96,32},{112,48},{1... | collective-permute-start | bytes 10760 | tf_op jit(solution)/shard_map/ppermute | solution.py:17
  62.9 11.1 %collective-permute-start.13 = (f32[896]{0:T(1024)S(1)}, f32[896]{0:T(1024)S(1)}, u32[]{:S(2)}, u32[]{:S(2)}) collective-permute-start(f32[896]{0:T(1024)S(1)} %pad_maximum_fusion.4), channel_id=1, source_target_pairs={{0,48},{16,64},{32,80},{48,96},{64,112},{80,0},{96,16},{112,32},{1... | collective-permute-start | bytes 10760 | tf_op jit(solution)/shard_map/ppermute | solution.py:17
  64.0 10.1 %collective-permute-start.12 = (f32[896]{0:T(1024)S(1)}, f32[896]{0:T(1024)S(1)}, u32[]{:S(2)}, u32[]{:S(2)}) collective-permute-start(f32[896]{0:T(1024)S(1)} %pad_maximum_fusion.4), channel_id=1, source_target_pairs={{0,32},{16,48},{32,64},{48,80},{64,96},{80,112},{96,0},{112,16},{1... | collective-permute-start | bytes 10760 | tf_op jit(solution)/shard_map/ppermute | solution.py:17
  65.3 8.8 %collective-permute-start.11 = (f32[896]{0:T(1024)S(1)}, f32[896]{0:T(1024)S(1)}, u32[]{:S(2)}, u32[]{:S(2)}) collective-permute-start(f32[896]{0:T(1024)S(1)} %pad_maximum_fusion.4), channel_id=1, source_target_pairs={{0,16},{16,32},{32,48},{48,64},{64,80},{80,96},{96,112},{112,0},{1... | collective-permute-start | bytes 10760 | tf_op jit(solution)/shard_map/ppermute | solution.py:17
  68.0 12.6 %all-to-all-start.1 = ((f32[16,1,1024]{2,1,0:T(1,128)}), f32[16,1,1024]{2,1,0:T(1,128)S(1)}, u32[]{:S(2)}, u32[]{:S(2)}) async-start(f32[16,1,1024]{2,1,0:T(1,128)} %broadcast_in_dim.75), calls=%async_computation.1 | async-start | bytes 131072 | tf_op jit(solution)/shard_map/all_to_all | solution.py:91
  85.0 1.7 %copy-start = (f32[768,1024]{1,0:T(8,128)}, f32[768,1024]{1,0:T(8,128)S(1)}, u32[]{:S(2)}) copy-start(f32[768,1024]{1,0:T(8,128)S(1)} %convolution_multiply_fusion) | copy-start | bytes 9437188
  86.6 16.6 %collective-permute-start.18 = (f32[384,1024]{1,0:T(8,128)S(1)}, f32[384,1024]{1,0:T(8,128)}, u32[]{:S(2)}, u32[]{:S(2)}) collective-permute-start(f32[384,1024]{1,0:T(8,128)S(1)} %slice.98), channel_id=1, source_target_pairs={{0,8},{8,0},{1,9},{9,1},{2,10},{10,2},{3,11},{11,3},{4,12},{12,4},... | collective-permute-start | bytes 4718600 | tf_op jit(solution)/shard_map/ppermute | solution.py:136
  96.2 6.2 %collective-permute-start.9 = (f32[]{:T(128)}, f32[]{:T(128)}, u32[]{:S(2)}, u32[]{:S(2)}) collective-permute-start(f32[]{:T(128)} %sub.100), channel_id=1, source_target_pairs={{0,8},{8,0},{1,9},{9,1},{2,10},{10,2},{3,11},{11,3},{4,12},{12,4},... | collective-permute-start | bytes 20 | tf_op jit(solution)/shard_map/ppermute | solution.py:135
  105.9 1.7 %copy-start.2 = (bf16[768,1024]{1,0:T(8,128)(2,1)S(1)}, bf16[768,1024]{1,0:T(8,128)(2,1)}, u32[]{:S(2)}) copy-start(bf16[768,1024]{1,0:T(8,128)(2,1)} %fusion.3) | copy-start | bytes 4718596
  106.9 14.3 %collective-permute-start.19 = (bf16[56,1024]{1,0:T(8,128)(2,1)}, bf16[56,1024]{1,0:T(8,128)(2,1)}, u32[]{:S(2)}, u32[]{:S(2)}) collective-permute-start(bf16[56,1024]{1,0:T(8,128)(2,1)} %get-tuple-element.15), channel_id=1, source_target_pairs={{0,16},{16,32},{32,48},{48,64},{64,80},{80,96},{96,112},{112,0},{1... | collective-permute-start | bytes 344072 | tf_op jit(solution)/shard_map/ppermute | solution.py:17
  109.0 39.4 %all-to-all-start.2 = ((bf16[16,56,1024]{2,1,0:T(8,128)(2,1)}), bf16[16,56,1024]{2,1,0:T(8,128)(2,1)S(1)}, u32[]{:S(2)}, u32[]{:S(2)}) async-start(bf16[16,56,1024]{2,1,0:T(8,128)(2,1)} %pad_maximum_fusion), calls=%async_computation.2 | async-start | bytes 3670016 | tf_op jit(solution)/shard_map/all_to_all | solution.py:127
  112.7 30.7 %collective-permute-start.25 = (bf16[56,1024]{1,0:T(8,128)(2,1)S(1)}, bf16[56,1024]{1,0:T(8,128)(2,1)S(1)}, u32[]{:S(2)}, u32[]{:S(2)}) collective-permute-start(bf16[56,1024]{1,0:T(8,128)(2,1)S(1)} %get-tuple-element.14), channel_id=1, source_target_pairs={{0,112},{16,0},{32,16},{48,32},{64,48},{80,64},{96,80},{112,96},{1... | collective-permute-start | bytes 344072 | tf_op jit(solution)/shard_map/ppermute | solution.py:17
  115.3 10.2 %collective-permute-start.20 = (bf16[56,1024]{1,0:T(8,128)(2,1)}, bf16[56,1024]{1,0:T(8,128)(2,1)S(1)}, u32[]{:S(2)}, u32[]{:S(2)}) collective-permute-start(bf16[56,1024]{1,0:T(8,128)(2,1)} %get-tuple-element.16), channel_id=1, source_target_pairs={{0,32},{16,48},{32,64},{48,80},{64,96},{80,112},{96,0},{112,16},{1... | collective-permute-start | bytes 344072 | tf_op jit(solution)/shard_map/ppermute | solution.py:17
  116.9 16.7 %collective-permute-start.21 = (bf16[56,1024]{1,0:T(8,128)(2,1)}, bf16[56,1024]{1,0:T(8,128)(2,1)S(1)}, u32[]{:S(2)}, u32[]{:S(2)}) collective-permute-start(bf16[56,1024]{1,0:T(8,128)(2,1)} %get-tuple-element.17), channel_id=1, source_target_pairs={{0,48},{16,64},{32,80},{48,96},{64,112},{80,0},{96,16},{112,32},{1... | collective-permute-start | bytes 344072 | tf_op jit(solution)/shard_map/ppermute | solution.py:17
  118.6 15.1 %collective-permute-start.22 = (bf16[56,1024]{1,0:T(8,128)(2,1)}, bf16[56,1024]{1,0:T(8,128)(2,1)S(1)}, u32[]{:S(2)}, u32[]{:S(2)}) collective-permute-start(bf16[56,1024]{1,0:T(8,128)(2,1)} %get-tuple-element.18), channel_id=1, source_target_pairs={{0,64},{16,80},{32,96},{48,112},{64,0},{80,16},{96,32},{112,48},{1... | collective-permute-start | bytes 344072 | tf_op jit(solution)/shard_map/ppermute | solution.py:17
  121.2 14.5 %collective-permute-start.23 = (bf16[56,1024]{1,0:T(8,128)(2,1)}, bf16[56,1024]{1,0:T(8,128)(2,1)S(1)}, u32[]{:S(2)}, u32[]{:S(2)}) collective-permute-start(bf16[56,1024]{1,0:T(8,128)(2,1)} %get-tuple-element.19), channel_id=1, source_target_pairs={{0,80},{16,96},{32,112},{48,0},{64,16},{80,32},{96,48},{112,64},{1... | collective-permute-start | bytes 344072 | tf_op jit(solution)/shard_map/ppermute | solution.py:17
  125.4 18.0 %collective-permute-start.24 = (bf16[56,1024]{1,0:T(8,128)(2,1)}, bf16[56,1024]{1,0:T(8,128)(2,1)S(1)}, u32[]{:S(2)}, u32[]{:S(2)}) collective-permute-start(bf16[56,1024]{1,0:T(8,128)(2,1)} %get-tuple-element.20), channel_id=1, source_target_pairs={{0,96},{16,112},{32,0},{48,16},{64,32},{80,48},{96,64},{112,80},{1... | collective-permute-start | bytes 344072 | tf_op jit(solution)/shard_map/ppermute | solution.py:17
  143.4 0.9 copy-start.4

commit v3 on v1

v3 whole, which is shorter than its diff:
```python
import functools

import jax
import jax.numpy as jnp
from jax import lax
from jax.experimental import pallas as pl
from jax.experimental.pallas import tpu as pltpu
from jax.sharding import Mesh, PartitionSpec as P

PLANE = ("xl", "y", "xh")
SWAP = [(0, 1), (1, 0)]
LANES = 128
EXTRA = 16
F32 = jnp.float32
BF16 = jnp.bfloat16


def turn(x, axis, step):
    count = lax.axis_size(axis)
    return lax.ppermute(x, axis, [(i, (i + step) % count) for i in range(count)])


def merge(parts):
    high = functools.reduce(jnp.maximum, parts)
    return high + jnp.log(sum(jnp.exp(p - high) for p in parts))


def encode(scaled):
    square = scaled * scaled
    fourth = square * square
    return jnp.where(scaled < 0, -fourth, fourth).astype(BF16)


def decode(x):
    wide = x.astype(F32)
    root = jnp.sqrt(jnp.sqrt(jnp.abs(wide)))
    return jnp.where(wide < 0, -root, root)


def split3(value):
    high = value.astype(BF16).astype(F32)
    mid = (value - high).astype(BF16).astype(F32)
    low = value - high - mid
    row = lax.broadcasted_iota(jnp.int32, (EXTRA, LANES), 0)
    parts = jnp.where(row == 0, high, jnp.where(row == 1, mid, jnp.where(row == 2, low, 0.0)))
    return parts.astype(BF16)


def inverse(value):
    return jnp.where(value > 0, 1.0 / value, 1.0)


def to_column(row):
    return jnp.transpose(jnp.broadcast_to(row, (LANES, row.shape[1])))[:, :1]


def to_row(column):
    return jnp.transpose(jnp.broadcast_to(column, (column.shape[0], LANES)))[:1, :]


def call(body, outs, args, name, flops=0, exps=0, smem_out=None):
    size = sum(a.size * a.dtype.itemsize for a in (*args, *outs))
    spaces = [pltpu.SMEM if i == smem_out else pltpu.VMEM for i in range(len(outs))]
    return pl.pallas_call(
        body,
        out_shape=outs,
        in_specs=[pl.BlockSpec(memory_space=pltpu.VMEM)] * len(args),
        out_specs=tuple(pl.BlockSpec(memory_space=s) for s in spaces),
        cost_estimate=pl.CostEstimate(flops=flops, bytes_accessed=size, transcendentals=exps),
        compiler_params=pltpu.CompilerParams(vmem_limit_bytes=48 * 1024 * 1024),
        name=name,
    )(*args)


def score_body(n_z, inv_root, *refs):
    pieces, (image, pair, ids, scores, text, sent) = refs[: 2 * n_z], refs[2 * n_z :]
    rows = pieces[0].shape[0]
    size = image.shape[0]
    z = lax.axis_index("z")
    high = jnp.zeros(pieces[0].shape, F32)
    for h in range(2):
        for q in range(n_z):
            piece = pieces[h * n_z + q][...]
            start = h * n_z * rows + lax.rem(z + q, n_z) * rows
            text[pl.ds(pl.multiple_of(start, 16), rows), :] = piece
            high = jnp.maximum(high, jnp.abs(piece.astype(F32)))
    found = jnp.zeros((1, size), F32)
    step = 256
    for r in range(0, size, step):
        tile = (
            lax.dot_general(
                image[r : r + step, :],
                text[...],
                (((1,), (1,)), ((), ())),
                preferred_element_type=F32,
            )
            * inv_root
        )
        scores[r : r + step, :] = tile
        top = jnp.max(tile, axis=1, keepdims=True)
        part = top + jnp.log(jnp.sum(jnp.exp(tile - top), axis=1, keepdims=True))
        sent[:, 0, r : r + step] = jnp.broadcast_to(to_row(part), (sent.shape[0], step))
        hit = to_column(pair[:, r : r + step]) == ids[...]
        found += jnp.sum(jnp.where(hit, tile, 0.0), axis=0, keepdims=True)
    sent[:, 0, size : size + LANES] = jnp.full((sent.shape[0], LANES), jnp.sum(found))
    sent[:, 0, size + LANES :] = jnp.full((sent.shape[0], LANES), jnp.max(high))


def column_body(scores, image, sent):
    size = scores.shape[1]
    tile = scores[...]
    top = jnp.max(tile, axis=0, keepdims=True)
    part = top + jnp.log(jnp.sum(jnp.exp(tile - top), axis=0, keepdims=True))
    sent[:, :size] = part
    high = jnp.max(jnp.abs(image[...].astype(F32)))
    sent[:, size:] = jnp.full((1, LANES), high)


def pair_body(mine, seen, out):
    size = mine.shape[1] - LANES
    half = size // 2
    other = jnp.concatenate([seen[:, half:size], seen[:, :half]], axis=1)
    out[:, :size] = merge([mine[:, :size], other])
    out[:, size:] = jnp.maximum(mine[:, size:], seen[:, size:])


def image_body(n_z, inv_root, *refs):
    cols = refs[:n_z]
    scores, text, row_got, pair, ids, grads, sent, terms = refs[n_z:]
    size = scores.shape[0]
    n_plane = sent.shape[0]
    rows = size // n_plane
    col_lse = merge([c[:, :size] for c in cols])
    image_max = functools.reduce(jnp.maximum, [c[:, size:] for c in cols])
    row_lse = merge([row_got[i : i + 1, :size] for i in range(n_plane)])
    matched = jnp.sum(row_got[:, size : size + LANES], axis=0, keepdims=True)
    text_max = jnp.max(row_got[:, size + LANES :], axis=0, keepdims=True)
    row_terms = jnp.sum(row_lse, axis=1, keepdims=True) - 2.0 * matched
    col_terms = jnp.broadcast_to(jnp.sum(col_lse, axis=1, keepdims=True), (1, LANES))
    terms[...] = jnp.concatenate(
        [row_terms, text_max, image_max, jnp.zeros((5, LANES), F32)], axis=0
    )
    extra = split3(col_terms)
    scale = inverse(text_max[:, :1]) * inv_root
    step = 384
    for r in range(0, size, step):
        tile = scores[r : r + step, :]
        probs = 0.5 * (
            jnp.exp(tile - to_column(row_lse[:, r : r + step])) + jnp.exp(tile - col_lse)
        )
        hit = to_column(pair[:, r : r + step]) == ids[...]
        grad = (probs - jnp.where(hit, 1.0, 0.0)).astype(BF16)
        grads[r : r + step, :] = grad
        part = encode(jnp.dot(grad, text[...], preferred_element_type=F32) * scale)
        for p in range(step // rows):
            to = r // rows + p
            for k in range(text.shape[1] // LANES):
                sent[to, k * rows : (k + 1) * rows, :] = part[
                    p * rows : (p + 1) * rows, k * LANES : (k + 1) * LANES
                ]
            sent[to, k * rows + rows :, :] = extra


def text_body(inv_root, grads, image, own, other):
    half = own.shape[0]
    for out, start in ((other, half), (own, 0)):
        out[...] = (
            lax.dot_general(
                grads[:, start : start + half],
                image[...],
                (((0,), (0,)), ((), ())),
                preferred_element_type=F32,
            )
            * inv_root
        )


def send_body(n_z, own, seen, terms, terms_seen, keep, total, *pays):
    rows = keep.shape[0]
    z = lax.axis_index("z")
    row_terms = terms[0:1, :] + terms_seen[0:1, :]
    total[...] = row_terms
    extra = split3(row_terms)
    scale = inverse(terms[2:3, :1])
    for q in range(n_z):
        at = pl.ds(pl.multiple_of(lax.rem(z + q, n_z) * rows, 16), rows)
        block = own[at, :] + seen[at, :]
        if q == 0:
            keep[...] = block
            continue
        pay = pays[q - 1]
        part = encode(block * scale)
        count = block.shape[1] // LANES
        for k in range(count):
            pay[k * rows : (k + 1) * rows, :] = part[:, k * LANES : (k + 1) * LANES]
        pay[count * rows :, :] = extra


def image_sum_body(got, terms, out, side):
    rows, width = out.shape
    unit = terms[1:2, :1]
    unit = jnp.where(unit > 0, unit, 1.0)
    count = width // LANES
    for k in range(count):
        at = slice(k * rows, (k + 1) * rows)
        out[:, k * LANES : (k + 1) * LANES] = unit * sum(
            decode(got[p, at, :]) for p in range(got.shape[0])
        )
    tail = sum(got[p, count * rows :, :].astype(F32) for p in range(got.shape[0]))
    side[...] = jnp.sum(tail, axis=0, keepdims=True)


def text_sum_body(pairs, keep, total, terms, side, *refs):
    pays, out, loss = refs[:-2], refs[-2], refs[-1]
    rows, width = out.shape
    unit = terms[2:3, :1]
    unit = jnp.where(unit > 0, unit, 1.0)
    count = width // LANES
    for k in range(count):
        at = slice(k * rows, (k + 1) * rows)
        lanes = slice(k * LANES, (k + 1) * LANES)
        out[:, lanes] = keep[:, lanes] + unit * sum(decode(p[at, :]) for p in pays)
    tail = sum(p[count * rows :, :].astype(F32) for p in pays)
    full = total[...] + side[...] + jnp.sum(tail, axis=0, keepdims=True)
    loss[0, 0] = jnp.max(full) / (2.0 * pairs)


def shards(image_embed, text_embed, pair_index):
    rows, width = image_embed.shape
    n_xl, n_z, n_c, n_y, n_xh = (lax.axis_size(a) for a in ("xl", "z", "c", "y", "xh"))
    n_plane = n_xl * n_y * n_xh
    size = n_plane * rows
    half = n_z * rows
    pairs = size * n_z * n_c
    inv_root = width ** (-0.5)
    core = lax.axis_index("c")
    shape = jax.ShapeDtypeStruct
    tall = width // LANES * rows + EXTRA

    pair_other = lax.ppermute(pair_index, "xl", SWAP)
    first = lax.axis_index("xl") == 0
    pair = jnp.concatenate(
        [jnp.where(first, pair_index, pair_other), jnp.where(first, pair_other, pair_index)]
    )
    pair = pair.astype(F32)[None, :]
    block = (lax.axis_index("y") * n_xh + lax.axis_index("xh")) * n_xl + lax.axis_index("xl")
    slot = lax.broadcasted_iota(jnp.int32, (1, size), 1)
    own = slot < half
    within = jnp.where(own, slot, slot - half)
    ids = ((block * n_z + within // rows) * n_c + jnp.where(own, core, 1 - core)) * rows
    ids = (ids + within % rows).astype(F32)

    image = lax.all_to_all(
        jnp.broadcast_to(image_embed[None], (n_plane, rows, width)), PLANE, 0, 0
    ).reshape(size, width)
    pieces = [text_embed] + [turn(text_embed, "z", -q) for q in range(1, n_z)]
    pieces = pieces + [lax.ppermute(piece, "c", SWAP) for piece in pieces]

    flops = 2 * size * size * width
    scores, text, row_sent = call(
        functools.partial(score_body, n_z, inv_root),
        (
            shape((size, size), F32),
            shape((size, width), BF16),
            shape((n_plane, 1, size + 2 * LANES), F32),
        ),
        (*pieces, image, pair, ids),
        "scores",
        flops,
        size * size,
    )
    row_got = lax.all_to_all(row_sent, PLANE, 0, 0).reshape(n_plane, size + 2 * LANES)
    (col_sent,) = call(
        column_body, (shape((1, size + LANES), F32),), (scores, image), "columns", 0, size * size
    )
    (col_pair,) = call(
        pair_body,
        (shape((1, size + LANES), F32),),
        (col_sent, lax.ppermute(col_sent, "c", SWAP)),
        "pair",
    )
    cols = [col_pair] + [turn(col_pair, "z", q) for q in range(1, n_z)]

    grads, image_sent, terms = call(
        functools.partial(image_body, n_z, inv_root),
        (
            shape((size, size), BF16),
            shape((n_plane, tall, LANES), BF16),
            shape((8, LANES), F32),
        ),
        (*cols, scores, text, row_got, pair, ids),
        "image_grad",
        flops,
        2 * size * size,
    )
    image_got = lax.all_to_all(image_sent, PLANE, 0, 0)
    text_own, text_other = call(
        functools.partial(text_body, inv_root),
        (shape((half, width), F32), shape((half, width), F32)),
        (grads, image),
        "text_grad",
        flops,
    )
    keep, total, *pays = call(
        functools.partial(send_body, n_z),
        (shape((rows, width), F32), shape((1, LANES), F32))
        + (shape((tall, LANES), BF16),) * (n_z - 1),
        (text_own, lax.ppermute(text_other, "c", SWAP), terms, lax.ppermute(terms, "c", SWAP)),
        "send",
    )
    pays = [turn(pay, "z", q + 1) for q, pay in enumerate(pays)]
    grad_image, side = call(
        image_sum_body,
        (shape((rows, width), F32), shape((1, LANES), F32)),
        (image_got, terms),
        "image_sum",
    )
    grad_text, loss = call(
        functools.partial(text_sum_body, pairs),
        (shape((rows, width), F32), shape((1, 1), F32)),
        (keep, total, terms, side, *pays),
        "text_sum",
        smem_out=1,
    )
    return (loss[0, 0], grad_image, grad_text)


def solution(mesh):
    fine = Mesh(mesh.devices.reshape(2, 8, 2, 4, 2), ("xl", "z", "c", "y", "xh"))
    image_spec = P(("xl", "z", "c", "y", "xh"), None)
    text_spec = P(("y", "xh", "xl", "z", "c"), None)
    return jax.shard_map(
        shards,
        mesh=fine,
        in_specs=(image_spec, text_spec, P(("xl", "z", "c"))),
        out_specs=(P(), image_spec, text_spec),
        check_vma=False,
    )
```

time: 210 us -> 134 us (0.64)
  waiting for transfers between devices: 97.5 us -> 24.9 us
  starting transfers between devices: 24.2 us -> 83.4 us
  blocking collectives: 53.3 us -> 0 us
  Pallas kernels: 0 us -> 18.3 us
  other arithmetic: 10.7 us -> 0.03 us
  matrix products: 9.36 us -> 0 us
  between operations: 5.19 us -> 0.93 us
  local copies, waits for them, and re-layouts: 8.72 us -> 5.13 us
    all_to_all x3 -> x0, blocking collectives: 53.3 us -> none  [spread(): lax.all_to_all(jnp.broadcast_to(x[None], (count,) + x.shape), axes, 0, 0)]
    ppermute x4 -> x33, starting transfers between devices: 9.41 us -> 60.5 us  [the longest x21 42.1 us: turn(): lax.ppermute(x, axis, [(i, (i + step) % count) for i in range(count)])]
    all_to_all x2, waiting for transfers between devices: 37.5 us -> 0.01 us  [the longest x1 0.01 us: shards(): lax.all_to_all(jnp.broadcast_to(image_embed[None], (n_plane, rows, width)...]
    all_to_all x1, waiting for transfers between devices: 44.1 us -> 9.01 us  [shards(): image_got = lax.all_to_all(image_sent, PLANE, 0, 0)]
    pallas_call x0 -> x8, Pallas kernels: none -> 18.3 us  [call(): pl.pallas_call(body, out_shape=outs, in_specs=[pl.BlockSpec(memory_space=...]
    dot_general x3 -> x0, matrix products: 9.36 us -> none  [the longest x1 3.2 us: shards(): lax.dot_general(grad_scores, image, (((0,), (0,)), ((), ())), preferred_e...]
    reduce_sum x11 -> x0, other arithmetic: 9.17 us -> none  [the longest x1 2.77 us: shards(): grad_image = jnp.sum(image_got[:, :rows], axis=0)]
    all_to_all x2, starting transfers between devices: 10.3 us -> 15.9 us  [the longest x1 8.18 us: shards(): lax.all_to_all(row_sent, PLANE, 0, 0).reshape(n_plane, size + 2 * LANES)]
  transfers between devices with their start and end apart: 7 -> 36, of which waited for: 6 -> 13; matrix products, arithmetic and copies ran while one was open for 5% -> 0% of each run, Pallas kernels for 0% -> 3%
where the time goes in v3:
time: 134 us; the launch traced here: 133 us
  starting transfers between devices  83.4 us (62%)
  waiting for transfers between devices  24.9 us (19%)
  Pallas kernels  18.3 us (14%)
  local copies, waits for them, and re-layouts  5.13 us (4%)
    ppermute x21, starting transfers between devices, turn(): lax.ppermute(x, axis, [(i, (i + step) % count) for i in range(count)])  42.1 us
    pallas_call x8, Pallas kernels, call(): pl.pallas_call(body, out_shape=outs, in_specs=[pl.BlockSpec(memory_space=...  18.3 us
    ppermute x8, starting transfers between devices, shards(): pieces = pieces + [lax.ppermute(piece, 'c', SWAP) for piece in pieces]  13 us
    all_to_all x1, waiting for transfers between devices, shards(): image_got = lax.all_to_all(image_sent, PLANE, 0, 0)  9.01 us
    ppermute x1, waiting for transfers between devices, shards(): pair_other = lax.ppermute(pair_index, 'xl', SWAP)  8.65 us
    all_to_all x1, starting transfers between devices, shards(): lax.all_to_all(row_sent, PLANE, 0, 0).reshape(n_plane, size + 2 * LANES)  8.18 us
    all_to_all x1, starting transfers between devices, shards(): lax.all_to_all(jnp.broadcast_to(image_embed[None], (n_plane, rows, width)...  7.72 us
    all_to_all x1, starting transfers between devices, shards(): image_got = lax.all_to_all(image_sent, PLANE, 0, 0)  6.93 us
  transfers between devices with their start and end apart: 36, of which 13 were waited for; matrix products, arithmetic and copies ran while one was open for 0% of the time, Pallas kernels for 3%

profile of v3, /device:TPU:1, one launch (start us, length us, event | category | flops | bytes accessed | tf_op | source)
XLA Modules:
  0.0 132.7 jit_solution(10270436317900382802)
XLA Ops:
  0.6 2.3 %broadcast_in_dim.15 = bf16[16,48,1024]{2,1,0:T(8,128)(2,1)} broadcast(bf16[48,1024]{1,0:T(8,128)(2,1)} %param.3), dimensions={1,2} | broadcast | bytes 1671168 | tf_op jit(solution)/shard_map/broadcast_in_dim | solution.py:254
  2.9 7.7 %all-to-all-start = ((bf16[16,48,1024]{2,1,0:T(8,128)(2,1)}), bf16[16,48,1024]{2,1,0:T(8,128)(2,1)S(1)}, u32[]{:S(2)}, u32[]{:S(2)}) async-start(bf16[16,48,1024]{2,1,0:T(8,128)(2,1)} %broadcast_in_dim.15), calls=%async_computation | async-start | bytes 3145728 | tf_op jit(solution)/shard_map/all_to_all | solution.py:253
  10.6 1.5 %collective-permute-start.15 = (s32[384]{0:T(512)S(1)}, s32[384]{0:T(512)S(1)}, u32[]{:S(2)}, u32[]{:S(2)}) collective-permute-start(s32[384]{0:T(512)S(1)} %copy-done.4), channel_id=1, source_target_pairs={{0,128},{128,0},{1,129},{129,1},{2,130},{130,2},{3,131},{131,3},{4... | collective-permute-start | bytes 4616 | tf_op jit(solution)/shard_map/ppermute | solution.py:240
  12.1 1.6 %collective-permute-start.6 = (bf16[48,1024]{1,0:T(8,128)(2,1)S(1)}, bf16[48,1024]{1,0:T(8,128)(2,1)S(1)}, u32[]{:S(2)}, u32[]{:S(2)}) collective-permute-start(bf16[48,1024]{1,0:T(8,128)(2,1)S(1)} %copy-done.1), channel_id=1, source_target_pairs={{0,16},{16,32},{32,48},{48,64},{64,80},{80,96},{96,112},{112,0},{1... | collective-permute-start | bytes 294920 | tf_op jit(solution)/shard_map/ppermute | solution.py:20
  13.7 3.0 %collective-permute-start.5 = (bf16[48,1024]{1,0:T(8,128)(2,1)S(1)}, bf16[48,1024]{1,0:T(8,128)(2,1)S(1)}, u32[]{:S(2)}, u32[]{:S(2)}) collective-permute-start(bf16[48,1024]{1,0:T(8,128)(2,1)S(1)} %copy-done.1), channel_id=1, source_target_pairs={{0,32},{16,48},{32,64},{48,80},{64,96},{80,112},{96,0},{112,16},{1... | collective-permute-start | bytes 294920 | tf_op jit(solution)/shard_map/ppermute | solution.py:20
  16.7 3.8 %collective-permute-start.4 = (bf16[48,1024]{1,0:T(8,128)(2,1)S(1)}, bf16[48,1024]{1,0:T(8,128)(2,1)S(1)}, u32[]{:S(2)}, u32[]{:S(2)}) collective-permute-start(bf16[48,1024]{1,0:T(8,128)(2,1)S(1)} %copy-done.1), channel_id=1, source_target_pairs={{0,48},{16,64},{32,80},{48,96},{64,112},{80,0},{96,16},{112,32},{1... | collective-permute-start | bytes 294920 | tf_op jit(solution)/shard_map/ppermute | solution.py:20
  20.5 0.5 collective-permute-start.3
  20.9 8.7 %collective-permute-done.15 = s32[384]{0:T(512)S(1)} collective-permute-done((s32[384]{0:T(512)S(1)}, s32[384]{0:T(512)S(1)}, u32[]{:S(2)}, u32[]{:S(2)}) %collective-permute-start.15) | collective-permute-done | bytes 1568 | tf_op jit(solution)/shard_map/ppermute | solution.py:240
  29.6 6.5 %collective-permute-start.2 = (bf16[48,1024]{1,0:T(8,128)(2,1)S(1)}, bf16[48,1024]{1,0:T(8,128)(2,1)S(1)}, u32[]{:S(2)}, u32[]{:S(2)}) collective-permute-start(bf16[48,1024]{1,0:T(8,128)(2,1)S(1)} %copy-done.1), channel_id=1, source_target_pairs={{0,80},{16,96},{32,112},{48,0},{64,16},{80,32},{96,48},{112,64},{1... | collective-permute-start | bytes 294920 | tf_op jit(solution)/shard_map/ppermute | solution.py:20
  36.3 0.5 collective-permute-start
  36.9 2.4 %collective-permute-start.7 = (bf16[48,1024]{1,0:T(8,128)(2,1)S(1)}, bf16[48,1024]{1,0:T(8,128)(2,1)S(1)}, u32[]{:S(2)}, u32[]{:S(2)}) collective-permute-start(bf16[48,1024]{1,0:T(8,128)(2,1)S(1)} %copy-done.1), channel_id=1, source_target_pairs={{0,8},{8,0},{1,9},{9,1},{2,10},{10,2},{3,11},{11,3},{4,12},{12,4},... | collective-permute-start | bytes 294920 | tf_op jit(solution)/shard_map/ppermute | solution.py:257
  39.4 6.1 %collective-permute-start.13 = (bf16[48,1024]{1,0:T(8,128)(2,1)S(1)}, bf16[48,1024]{1,0:T(8,128)(2,1)S(1)}, u32[]{:S(2)}, u32[]{:S(2)}) collective-permute-start(bf16[48,1024]{1,0:T(8,128)(2,1)S(1)} %collective-permute-done.5.refs_6_), channel_id=1, source_target_pairs={{0,8},{8,0},{1,9},{9,1},{2,10},{10,2},{3,11},{11,3},{4,12},{12,4},... | collective-permute-start | bytes 294920 | tf_op jit(solution)/shard_map/ppermute | solution.py:257
  45.5 0.4 collective-permute-done.1.refs_2_
  45.9 2.4 %collective-permute-start.12 = (bf16[48,1024]{1,0:T(8,128)(2,1)S(1)}, bf16[48,1024]{1,0:T(8,128)(2,1)S(1)}, u32[]{:S(2)}, u32[]{:S(2)}) collective-permute-start(bf16[48,1024]{1,0:T(8,128)(2,1)S(1)} %collective-permute-done.4.refs_5_), channel_id=1, source_target_pairs={{0,8},{8,0},{1,9},{9,1},{2,10},{10,2},{3,11},{11,3},{4,12},{12,4},... | collective-permute-start | bytes 294920 | tf_op jit(solution)/shard_map/ppermute | solution.py:257
  48.4 1.2 collective-permute-start.11
  49.6 0.5 collective-permute-start.9
  51.1 0.4 collective-permute-done.8.refs_9_
  51.4 3.6 %scores.1 = (f32[768,768]{1,0:T(8,128)}, bf16[768,1024]{1,0:T(8,128)(2,1)S(1)}, f32[16,1,1024]{2,1,0:T(1,128)}) custom-call(bf16[48,1024]{1,0:T(8,128)(2,1)S(1)} %copy-done.1, bf16[48,1024]{1,0:T(8,128)(2,1)S(1)} %collective-permute-done.refs_1_, bf16[48,1024]{1,0:T(8,128)(2,1)S(1)} %collective-permute-done.1.refs_2_, ...), custom_call_target="tpu_custom_call" | custom-call | flops 1207959552 | bytes 7149568 | tf_op jit(solution)/shard_map/scores/pallas_call | solution.py:64
  55.0 1.2 copy-done.2
  56.2 8.2 %all-to-all-start.1 = ((f32[16,1,1024]{2,1,0:T(1,128)}), f32[16,1,1024]{2,1,0:T(1,128)S(1)}, u32[]{:S(2)}, u32[]{:S(2)}) async-start(f32[16,1,1024]{2,1,0:T(1,128)} %get-tuple-element.26), calls=%async_computation.1 | async-start | bytes 131072 | tf_op jit(solution)/shard_map/all_to_all | solution.py:272
  64.4 1.7 %copy-done = f32[768,768]{1,0:T(8,128)S(1)} copy-done((f32[768,768]{1,0:T(8,128)S(1)}, f32[768,768]{1,0:T(8,128)}, u32[]{:S(2)}) %copy-start) | copy-done | bytes 2359320
  66.0 0.7 columns.1.mine
  66.7 0.6 collective-permute-start.16
  67.4 0.8 collective-permute-done.16.seen
  68.2 3.5 %collective-permute-start.23 = (f32[1,896]{1,0:T(1,128)S(1)}, f32[1,896]{1,0:T(1,128)S(1)}, u32[]{:S(2)}, u32[]{:S(2)}) collective-permute-start(f32[1,896]{1,0:T(1,128)S(1)} %pair.1.refs_0_), channel_id=1, source_target_pairs={{0,112},{16,0},{32,16},{48,32},{64,48},{80,64},{96,80},{112,96},{1... | collective-permute-start | bytes 10760 | tf_op jit(solution)/shard_map/ppermute | solution.py:20
  71.7 0.5 collective-permute-start.21
  72.3 4.9 %collective-permute-start.20 = (f32[1,896]{1,0:T(1,128)S(1)}, f32[1,896]{1,0:T(1,128)S(1)}, u32[]{:S(2)}, u32[]{:S(2)}) collective-permute-start(f32[1,896]{1,0:T(1,128)S(1)} %pair.1.refs_0_), channel_id=1, source_target_pairs={{0,64},{16,80},{32,96},{48,112},{64,0},{80,16},{96,32},{112,48},{1... | collective-permute-start | bytes 10760 | tf_op jit(solution)/shard_map/ppermute | solution.py:20
  77.2 1.8 %collective-permute-start.18 = (f32[1,896]{1,0:T(1,128)S(1)}, f32[1,896]{1,0:T(1,128)S(1)}, u32[]{:S(2)}, u32[]{:S(2)}) collective-permute-start(f32[1,896]{1,0:T(1,128)S(1)} %pair.1.refs_0_), channel_id=1, source_target_pairs={{0,32},{16,48},{32,64},{48,80},{64,96},{80,112},{96,0},{112,16},{1... | collective-permute-start | bytes 10760 | tf_op jit(solution)/shard_map/ppermute | solution.py:20
  79.0 0.7 collective-permute-start.17
  79.8 2.8 %collective-permute-done.19.refs_3_ = f32[1,896]{1,0:T(1,128)S(1)} collective-permute-done((f32[1,896]{1,0:T(1,128)S(1)}, f32[1,896]{1,0:T(1,128)S(1)}, u32[]{:S(2)}, u32[]{:S(2)}) %collective-permute-start.19) | collective-permute-done | bytes 3616 | tf_op jit(solution)/shard_map/ppermute | solution.py:20
  82.9 5.2 %image_grad.1 = (bf16[768,768]{1,0:T(8,128)(2,1)S(1)}, bf16[16,400,128]{2,1,0:T(8,128)(2,1)}, f32[8,128]{1,0:T(8,128)S(1)}) custom-call(f32[1,896]{1,0:T(1,128)S(1)} %pair.1.refs_0_, f32[1,896]{1,0:T(1,128)S(1)} %collective-permute-done.17.refs_1_, f32[1,896]{1,0:T(1,128)S(1)} %collective-permute-done.18.refs_2_, ...), custom_call_target="tpu_custom_call" | custom-call | flops 1207959552 | bytes 6854656 | tf_op jit(solution)/shard_map/image_grad/pallas_call | solution.py:64
  88.1 2.0 %text_grad.1 = (f32[384,1024]{1,0:T(8,128)S(1)}, f32[384,1024]{1,0:T(8,128)}) custom-call(bf16[768,768]{1,0:T(8,128)(2,1)S(1)} %get-tuple-element.27.grads, bf16[768,1024]{1,0:T(8,128)(2,1)S(1)} %bitcast.7), custom_call_target="tpu_custom_call" | custom-call | flops 1207959552 | bytes 5898240 | tf_op jit(solution)/shard_map/text_grad/pallas_call | solution.py:64
  90.1 3.0 %collective-permute-start.24 = (f32[384,1024]{1,0:T(8,128)}, f32[384,1024]{1,0:T(8,128)}, u32[]{:S(2)}, u32[]{:S(2)}) collective-permute-start(f32[384,1024]{1,0:T(8,128)} %get-tuple-element.29), channel_id=1, source_target_pairs={{0,8},{8,0},{1,9},{9,1},{2,10},{10,2},{3,11},{11,3},{4,12},{12,4},... | collective-permute-start | bytes 4718600 | tf_op jit(solution)/shard_map/ppermute | solution.py:308
  93.0 6.9 %all-to-all-start.2 = ((bf16[16,400,128]{2,1,0:T(8,128)(2,1)}), bf16[16,400,128]{2,1,0:T(8,128)(2,1)S(1)}, u32[]{:S(2)}, u32[]{:S(2)}) async-start(bf16[16,400,128]{2,1,0:T(8,128)(2,1)} %get-tuple-element.33), calls=%async_computation.2 | async-start | bytes 3276800 | tf_op jit(solution)/shard_map/all_to_all | solution.py:296
  100.0 0.4 collective-permute-start.25
  100.4 0.9 collective-permute-done.25.terms_seen
  101.2 2.5 %send.1 = (f32[48,1024]{1,0:T(8,128)S(1)}, f32[1,128]{1,0:T(1,128)S(1)}, bf16[400,128]{1,0:T(8,128)(2,1)S(1)}, bf16[400,128]{1,0:T(8,128)(2,1)S(1)}, bf16[400,12...) custom-call(f32[384,1024]{1,0:T(8,128)S(1)} %get-tuple-element.28.ow, ...), custom_call_target="tpu_custom_call" | custom-call | bytes 4067840 | tf_op jit(solution)/shard_map/send/pallas_call | solution.py:64
  103.7 0.8 collective-permute-start.26
  104.5 2.0 %collective-permute-start.27 = (bf16[400,128]{1,0:T(8,128)(2,1)S(1)}, bf16[400,128]{1,0:T(8,128)(2,1)S(1)}, u32[]{:S(2)}, u32[]{:S(2)}) collective-permute-start(bf16[400,128]{1,0:T(8,128)(2,1)S(1)} %get-tuple-element.36), channel_id=1, source_target_pairs={{0,32},{16,48},{32,64},{48,80},{64,96},{80,112},{96,0},{112,16},{1... | collective-permute-start | bytes 307208 | tf_op jit(solution)/shard_map/ppermute | solution.py:20
  106.6 2.4 %collective-permute-start.28 = (bf16[400,128]{1,0:T(8,128)(2,1)}, bf16[400,128]{1,0:T(8,128)(2,1)S(1)}, u32[]{:S(2)}, u32[]{:S(2)}) collective-permute-start(bf16[400,128]{1,0:T(8,128)(2,1)} %get-tuple-element.37), channel_id=1, source_target_pairs={{0,48},{16,64},{32,80},{48,96},{64,112},{80,0},{96,16},{112,32},{1... | collective-permute-start | bytes 307208 | tf_op jit(solution)/shard_map/ppermute | solution.py:20
  108.9 1.3 collective-permute-start.29
  110.2 3.2 %collective-permute-start.30 = (bf16[400,128]{1,0:T(8,128)(2,1)}, bf16[400,128]{1,0:T(8,128)(2,1)S(1)}, u32[]{:S(2)}, u32[]{:S(2)}) collective-permute-start(bf16[400,128]{1,0:T(8,128)(2,1)} %get-tuple-element.39), channel_id=1, source_target_pairs={{0,80},{16,96},{32,112},{48,0},{64,16},{80,32},{96,48},{112,64},{1... | collective-permute-start | bytes 307208 | tf_op jit(solution)/shard_map/ppermute | solution.py:20
  113.4 3.3 %collective-permute-start.31 = (bf16[400,128]{1,0:T(8,128)(2,1)}, bf16[400,128]{1,0:T(8,128)(2,1)S(1)}, u32[]{:S(2)}, u32[]{:S(2)}) collective-permute-start(bf16[400,128]{1,0:T(8,128)(2,1)} %get-tuple-element.40), channel_id=1, source_target_pairs={{0,96},{16,112},{32,0},{48,16},{64,32},{80,48},{96,64},{112,80},{1... | collective-permute-start | bytes 307208 | tf_op jit(solution)/shard_map/ppermute | solution.py:20
  116.7 1.5 %collective-permute-start.32 = (bf16[400,128]{1,0:T(8,128)(2,1)S(1)}, bf16[400,128]{1,0:T(8,128)(2,1)S(1)}, u32[]{:S(2)}, u32[]{:S(2)}) collective-permute-start(bf16[400,128]{1,0:T(8,128)(2,1)S(1)} %get-tuple-element.41), channel_id=1, source_target_pairs={{0,112},{16,0},{32,16},{48,32},{64,48},{80,64},{96,80},{112,96},{1... | collective-permute-start | bytes 307208 | tf_op jit(solution)/shard_map/ppermute | solution.py:20
  118.2 9.0 %all-to-all-done.2.got = bf16[16,400,128]{2,1,0:T(8,128)(2,1)S(1)} async-done(((bf16[16,400,128]{2,1,0:T(8,128)(2,1)}), bf16[16,400,128]{2,1,0:T(8,128)(2,1)S(1)}, u32[]{:S(2)}, u32[]{:S(2)}) %all-to-all-start.2) | async-done | bytes 1638432 | tf_op jit(solution)/shard_map/all_to_all | solution.py:296
  127.2 2.7 %image_sum.1 = (f32[48,1024]{1,0:T(8,128)}, f32[1,128]{1,0:T(1,128)S(1)}) custom-call(bf16[16,400,128]{2,1,0:T(8,128)(2,1)S(1)} %all-to-all-done.2.got, f32[8,128]{1,0:T(8,128)S(1)} %get-tuple-element.30.terms), custom_call_target="tpu_custom_call" | custom-call | bytes 1839616 | tf_op jit(solution)/shard_map/image_sum/pallas_call | solution.py:64
  129.9 1.0 collective-permute-done.31.refs_5_
  130.9 1.6 %text_sum.1 = (f32[48,1024]{1,0:T(8,128)}, f32[1,1]{1,0:T(1,128)}) custom-call(f32[48,1024]{1,0:T(8,128)S(1)} %get-tuple-element.31.keep, f32[1,128]{1,0:T(1,128)S(1)} %get-tuple-element.32.total, f32[8,128]{1,0:T(8,128)S(1)} %get-tuple-element.30.terms, f32[1,128]{1,0:T(1,128)S(1)} %get-tuple-element.34.side, ...), custom_call_target="tpu_custom_call" | custom-call | bytes 1115140 | tf_op jit(solution)/shard_map/text_sum/pallas_call | solution.py:64
  (48 shorter events, 1.7 us)
Async XLA Ops:
  2.9 7.7 %copy-start.4 = (s32[384]{0:T(512)S(1)}, s32[384]{0:T(512)}, u32[]{:S(2)}) copy-start(s32[384]{0:T(512)} %param.5) | copy-start | bytes 4612
  2.9 9.2 %copy-start.1 = (bf16[48,1024]{1,0:T(8,128)(2,1)S(1)}, bf16[48,1024]{1,0:T(8,128)(2,1)}, u32[]{:S(2)}) copy-start(bf16[48,1024]{1,0:T(8,128)(2,1)} %refs_0_.1) | copy-start | bytes 294916
  2.9 48.5 %all-to-all-start = ((bf16[16,48,1024]{2,1,0:T(8,128)(2,1)}), bf16[16,48,1024]{2,1,0:T(8,128)(2,1)S(1)}, u32[]{:S(2)}, u32[]{:S(2)}) async-start(bf16[16,48,1024]{2,1,0:T(8,128)(2,1)} %broadcast_in_dim.15), calls=%async_computation | async-start | bytes 3145728 | tf_op jit(solution)/shard_map/all_to_all | solution.py:253
  10.6 19.0 %collective-permute-start.15 = (s32[384]{0:T(512)S(1)}, s32[384]{0:T(512)S(1)}, u32[]{:S(2)}, u32[]{:S(2)}) collective-permute-start(s32[384]{0:T(512)S(1)} %copy-done.4), channel_id=1, source_target_pairs={{0,128},{128,0},{1,129},{129,1},{2,130},{130,2},{3,131},{131,3},{4... | collective-permute-start | bytes 4616 | tf_op jit(solution)/shard_map/ppermute | solution.py:240
  12.1 24.0 %collective-permute-start.6 = (bf16[48,1024]{1,0:T(8,128)(2,1)S(1)}, bf16[48,1024]{1,0:T(8,128)(2,1)S(1)}, u32[]{:S(2)}, u32[]{:S(2)}) collective-permute-start(bf16[48,1024]{1,0:T(8,128)(2,1)S(1)} %copy-done.1), channel_id=1, source_target_pairs={{0,16},{16,32},{32,48},{48,64},{64,80},{80,96},{96,112},{112,0},{1... | collective-permute-start | bytes 294920 | tf_op jit(solution)/shard_map/ppermute | solution.py:20
  13.7 22.6 %collective-permute-start.5 = (bf16[48,1024]{1,0:T(8,128)(2,1)S(1)}, bf16[48,1024]{1,0:T(8,128)(2,1)S(1)}, u32[]{:S(2)}, u32[]{:S(2)}) collective-permute-start(bf16[48,1024]{1,0:T(8,128)(2,1)S(1)} %copy-done.1), channel_id=1, source_target_pairs={{0,32},{16,48},{32,64},{48,80},{64,96},{80,112},{96,0},{112,16},{1... | collective-permute-start | bytes 294920 | tf_op jit(solution)/shard_map/ppermute | solution.py:20
  16.7 20.2 %collective-permute-start.4 = (bf16[48,1024]{1,0:T(8,128)(2,1)S(1)}, bf16[48,1024]{1,0:T(8,128)(2,1)S(1)}, u32[]{:S(2)}, u32[]{:S(2)}) collective-permute-start(bf16[48,1024]{1,0:T(8,128)(2,1)S(1)} %copy-done.1), channel_id=1, source_target_pairs={{0,48},{16,64},{32,80},{48,96},{64,112},{80,0},{96,16},{112,32},{1... | collective-permute-start | bytes 294920 | tf_op jit(solution)/shard_map/ppermute | solution.py:20
  20.5 18.8 %collective-permute-start.3 = (bf16[48,1024]{1,0:T(8,128)(2,1)S(1)}, bf16[48,1024]{1,0:T(8,128)(2,1)S(1)}, u32[]{:S(2)}, u32[]{:S(2)}) collective-permute-start(bf16[48,1024]{1,0:T(8,128)(2,1)S(1)} %copy-done.1), channel_id=1, source_target_pairs={{0,64},{16,80},{32,96},{48,112},{64,0},{80,16},{96,32},{112,48},{1... | collective-permute-start | bytes 294920 | tf_op jit(solution)/shard_map/ppermute | solution.py:20
  29.6 9.8 %collective-permute-start.2 = (bf16[48,1024]{1,0:T(8,128)(2,1)S(1)}, bf16[48,1024]{1,0:T(8,128)(2,1)S(1)}, u32[]{:S(2)}, u32[]{:S(2)}) collective-permute-start(bf16[48,1024]{1,0:T(8,128)(2,1)S(1)} %copy-done.1), channel_id=1, source_target_pairs={{0,80},{16,96},{32,112},{48,0},{64,16},{80,32},{96,48},{112,64},{1... | collective-permute-start | bytes 294920 | tf_op jit(solution)/shard_map/ppermute | solution.py:20
  36.1 9.8 %collective-permute-start.1 = (bf16[48,1024]{1,0:T(8,128)(2,1)S(1)}, bf16[48,1024]{1,0:T(8,128)(2,1)S(1)}, u32[]{:S(2)}, u32[]{:S(2)}) collective-permute-start(bf16[48,1024]{1,0:T(8,128)(2,1)S(1)} %copy-done.1), channel_id=1, source_target_pairs={{0,96},{16,112},{32,0},{48,16},{64,32},{80,48},{96,64},{112,80},{1... | collective-permute-start | bytes 294920 | tf_op jit(solution)/shard_map/ppermute | solution.py:20
  36.3 12.1 %collective-permute-start = (bf16[48,1024]{1,0:T(8,128)(2,1)S(1)}, bf16[48,1024]{1,0:T(8,128)(2,1)S(1)}, u32[]{:S(2)}, u32[]{:S(2)}) collective-permute-start(bf16[48,1024]{1,0:T(8,128)(2,1)S(1)} %copy-done.1), channel_id=1, source_target_pairs={{0,112},{16,0},{32,16},{48,32},{64,48},{80,64},{96,80},{112,96},{1... | collective-permute-start | bytes 294920 | tf_op jit(solution)/shard_map/ppermute | solution.py:20
  36.9 12.7 %collective-permute-start.7 = (bf16[48,1024]{1,0:T(8,128)(2,1)S(1)}, bf16[48,1024]{1,0:T(8,128)(2,1)S(1)}, u32[]{:S(2)}, u32[]{:S(2)}) collective-permute-start(bf16[48,1024]{1,0:T(8,128)(2,1)S(1)} %copy-done.1), channel_id=1, source_target_pairs={{0,8},{8,0},{1,9},{9,1},{2,10},{10,2},{3,11},{11,3},{4,12},{12,4},... | collective-permute-start | bytes 294920 | tf_op jit(solution)/shard_map/ppermute | solution.py:257
  39.3 10.3 %collective-permute-start.14 = (bf16[48,1024]{1,0:T(8,128)(2,1)S(1)}, bf16[48,1024]{1,0:T(8,128)(2,1)S(1)}, u32[]{:S(2)}, u32[]{:S(2)}) collective-permute-start(bf16[48,1024]{1,0:T(8,128)(2,1)S(1)} %collective-permute-done.6.refs_7_), channel_id=1, source_target_pairs={{0,8},{8,0},{1,9},{9,1},{2,10},{10,2},{3,11},{11,3},{4,12},{12,4},... | collective-permute-start | bytes 294920 | tf_op jit(solution)/shard_map/ppermute | solution.py:257
  39.4 10.7 %collective-permute-start.13 = (bf16[48,1024]{1,0:T(8,128)(2,1)S(1)}, bf16[48,1024]{1,0:T(8,128)(2,1)S(1)}, u32[]{:S(2)}, u32[]{:S(2)}) collective-permute-start(bf16[48,1024]{1,0:T(8,128)(2,1)S(1)} %collective-permute-done.5.refs_6_), channel_id=1, source_target_pairs={{0,8},{8,0},{1,9},{9,1},{2,10},{10,2},{3,11},{11,3},{4,12},{12,4},... | collective-permute-start | bytes 294920 | tf_op jit(solution)/shard_map/ppermute | solution.py:257
  45.9 4.5 %collective-permute-start.12 = (bf16[48,1024]{1,0:T(8,128)(2,1)S(1)}, bf16[48,1024]{1,0:T(8,128)(2,1)S(1)}, u32[]{:S(2)}, u32[]{:S(2)}) collective-permute-start(bf16[48,1024]{1,0:T(8,128)(2,1)S(1)} %collective-permute-done.4.refs_5_), channel_id=1, source_target_pairs={{0,8},{8,0},{1,9},{9,1},{2,10},{10,2},{3,11},{11,3},{4,12},{12,4},... | collective-permute-start | bytes 294920 | tf_op jit(solution)/shard_map/ppermute | solution.py:257
  48.4 2.1 %collective-permute-start.11 = (bf16[48,1024]{1,0:T(8,128)(2,1)S(1)}, bf16[48,1024]{1,0:T(8,128)(2,1)S(1)}, u32[]{:S(2)}, u32[]{:S(2)}) collective-permute-start(bf16[48,1024]{1,0:T(8,128)(2,1)S(1)} %collective-permute-done.3.refs_4_), channel_id=1, source_target_pairs={{0,8},{8,0},{1,9},{9,1},{2,10},{10,2},{3,11},{11,3},{4,12},{12,4},... | collective-permute-start | bytes 294920 | tf_op jit(solution)/shard_map/ppermute | solution.py:257
  49.6 1.3 collective-permute-start.10
  49.6 1.5 %collective-permute-start.9 = (bf16[48,1024]{1,0:T(8,128)(2,1)S(1)}, bf16[48,1024]{1,0:T(8,128)(2,1)S(1)}, u32[]{:S(2)}, u32[]{:S(2)}) collective-permute-start(bf16[48,1024]{1,0:T(8,128)(2,1)S(1)} %collective-permute-done.1.refs_2_), channel_id=1, source_target_pairs={{0,8},{8,0},{1,9},{9,1},{2,10},{10,2},{3,11},{11,3},{4,12},{12,4},... | collective-permute-start | bytes 294920 | tf_op jit(solution)/shard_map/ppermute | solution.py:257
  50.1 1.3 collective-permute-start.8
  55.0 1.2 copy-start.2
  56.2 23.6 %all-to-all-start.1 = ((f32[16,1,1024]{2,1,0:T(1,128)}), f32[16,1,1024]{2,1,0:T(1,128)S(1)}, u32[]{:S(2)}, u32[]{:S(2)}) async-start(f32[16,1,1024]{2,1,0:T(1,128)} %get-tuple-element.26), calls=%async_computation.1 | async-start | bytes 131072 | tf_op jit(solution)/shard_map/all_to_all | solution.py:272
  64.3 1.7 %copy-start = (f32[768,768]{1,0:T(8,128)S(1)}, f32[768,768]{1,0:T(8,128)}, u32[]{:S(2)}) copy-start(f32[768,768]{1,0:T(8,128)} %get-tuple-element.24.scores.refs_8_) | copy-start | bytes 7077892
  66.0 16.9 %copy-start.3 = (bf16[768,1024]{1,0:T(8,128)(2,1)S(1)}, bf16[768,1024]{1,0:T(8,128)(2,1)}, u32[]{:S(2)}) copy-start(bf16[768,1024]{1,0:T(8,128)(2,1)} %copy-done.2) | copy-start | bytes 4718596
  66.7 1.5 %collective-permute-start.16 = (f32[1,896]{1,0:T(1,128)S(1)}, f32[1,896]{1,0:T(1,128)S(1)}, u32[]{:S(2)}, u32[]{:S(2)}) collective-permute-start(f32[1,896]{1,0:T(1,128)S(1)} %columns.1.mine), channel_id=1, source_target_pairs={{0,8},{8,0},{1,9},{9,1},{2,10},{10,2},{3,11},{11,3},{4,12},{12,4},... | collective-permute-start | bytes 10760 | tf_op jit(solution)/shard_map/ppermute | solution.py:279
  68.2 9.0 %collective-permute-start.23 = (f32[1,896]{1,0:T(1,128)S(1)}, f32[1,896]{1,0:T(1,128)S(1)}, u32[]{:S(2)}, u32[]{:S(2)}) collective-permute-start(f32[1,896]{1,0:T(1,128)S(1)} %pair.1.refs_0_), channel_id=1, source_target_pairs={{0,112},{16,0},{32,16},{48,32},{64,48},{80,64},{96,80},{112,96},{1... | collective-permute-start | bytes 10760 | tf_op jit(solution)/shard_map/ppermute | solution.py:20
  71.7 7.3 %collective-permute-start.22 = (f32[1,896]{1,0:T(1,128)S(1)}, f32[1,896]{1,0:T(1,128)S(1)}, u32[]{:S(2)}, u32[]{:S(2)}) collective-permute-start(f32[1,896]{1,0:T(1,128)S(1)} %pair.1.refs_0_), channel_id=1, source_target_pairs={{0,96},{16,112},{32,0},{48,16},{64,32},{80,48},{96,64},{112,80},{1... | collective-permute-start | bytes 10760 | tf_op jit(solution)/shard_map/ppermute | solution.py:20
  71.7 8.1 %collective-permute-start.21 = (f32[1,896]{1,0:T(1,128)S(1)}, f32[1,896]{1,0:T(1,128)S(1)}, u32[]{:S(2)}, u32[]{:S(2)}) collective-permute-start(f32[1,896]{1,0:T(1,128)S(1)} %pair.1.refs_0_), channel_id=1, source_target_pairs={{0,80},{16,96},{32,112},{48,0},{64,16},{80,32},{96,48},{112,64},{1... | collective-permute-start | bytes 10760 | tf_op jit(solution)/shard_map/ppermute | solution.py:20
  72.3 7.5 %collective-permute-start.20 = (f32[1,896]{1,0:T(1,128)S(1)}, f32[1,896]{1,0:T(1,128)S(1)}, u32[]{:S(2)}, u32[]{:S(2)}) collective-permute-start(f32[1,896]{1,0:T(1,128)S(1)} %pair.1.refs_0_), channel_id=1, source_target_pairs={{0,64},{16,80},{32,96},{48,112},{64,0},{80,16},{96,32},{112,48},{1... | collective-permute-start | bytes 10760 | tf_op jit(solution)/shard_map/ppermute | solution.py:20
  77.2 5.5 %collective-permute-start.19 = (f32[1,896]{1,0:T(1,128)S(1)}, f32[1,896]{1,0:T(1,128)S(1)}, u32[]{:S(2)}, u32[]{:S(2)}) collective-permute-start(f32[1,896]{1,0:T(1,128)S(1)} %pair.1.refs_0_), channel_id=1, source_target_pairs={{0,48},{16,64},{32,80},{48,96},{64,112},{80,0},{96,16},{112,32},{1... | collective-permute-start | bytes 10760 | tf_op jit(solution)/shard_map/ppermute | solution.py:20
  77.2 5.7 %collective-permute-start.18 = (f32[1,896]{1,0:T(1,128)S(1)}, f32[1,896]{1,0:T(1,128)S(1)}, u32[]{:S(2)}, u32[]{:S(2)}) collective-permute-start(f32[1,896]{1,0:T(1,128)S(1)} %pair.1.refs_0_), channel_id=1, source_target_pairs={{0,32},{16,48},{32,64},{48,80},{64,96},{80,112},{96,0},{112,16},{1... | collective-permute-start | bytes 10760 | tf_op jit(solution)/shard_map/ppermute | solution.py:20
  79.0 3.9 %collective-permute-start.17 = (f32[1,896]{1,0:T(1,128)S(1)}, f32[1,896]{1,0:T(1,128)S(1)}, u32[]{:S(2)}, u32[]{:S(2)}) collective-permute-start(f32[1,896]{1,0:T(1,128)S(1)} %pair.1.refs_0_), channel_id=1, source_target_pairs={{0,16},{16,32},{32,48},{48,64},{64,80},{80,96},{96,112},{112,0},{1... | collective-permute-start | bytes 10760 | tf_op jit(solution)/shard_map/ppermute | solution.py:20
  90.1 11.2 %collective-permute-start.24 = (f32[384,1024]{1,0:T(8,128)}, f32[384,1024]{1,0:T(8,128)}, u32[]{:S(2)}, u32[]{:S(2)}) collective-permute-start(f32[384,1024]{1,0:T(8,128)} %get-tuple-element.29), channel_id=1, source_target_pairs={{0,8},{8,0},{1,9},{9,1},{2,10},{10,2},{3,11},{11,3},{4,12},{12,4},... | collective-permute-start | bytes 4718600 | tf_op jit(solution)/shard_map/ppermute | solution.py:308
  93.0 34.1 %all-to-all-start.2 = ((bf16[16,400,128]{2,1,0:T(8,128)(2,1)}), bf16[16,400,128]{2,1,0:T(8,128)(2,1)S(1)}, u32[]{:S(2)}, u32[]{:S(2)}) async-start(bf16[16,400,128]{2,1,0:T(8,128)(2,1)} %get-tuple-element.33), calls=%async_computation.2 | async-start | bytes 3276800 | tf_op jit(solution)/shard_map/all_to_all | solution.py:296
  100.0 1.3 collective-permute-start.25
  103.7 9.7 %collective-permute-start.26 = (bf16[400,128]{1,0:T(8,128)(2,1)S(1)}, bf16[400,128]{1,0:T(8,128)(2,1)S(1)}, u32[]{:S(2)}, u32[]{:S(2)}) collective-permute-start(bf16[400,128]{1,0:T(8,128)(2,1)S(1)} %get-tuple-element.35), channel_id=1, source_target_pairs={{0,16},{16,32},{32,48},{48,64},{64,80},{80,96},{96,112},{112,0},{1... | collective-permute-start | bytes 307208 | tf_op jit(solution)/shard_map/ppermute | solution.py:20
  104.5 12.2 %collective-permute-start.27 = (bf16[400,128]{1,0:T(8,128)(2,1)S(1)}, bf16[400,128]{1,0:T(8,128)(2,1)S(1)}, u32[]{:S(2)}, u32[]{:S(2)}) collective-permute-start(bf16[400,128]{1,0:T(8,128)(2,1)S(1)} %get-tuple-element.36), channel_id=1, source_target_pairs={{0,32},{16,48},{32,64},{48,80},{64,96},{80,112},{96,0},{112,16},{1... | collective-permute-start | bytes 307208 | tf_op jit(solution)/shard_map/ppermute | solution.py:20
  106.6 23.3 %collective-permute-start.28 = (bf16[400,128]{1,0:T(8,128)(2,1)}, bf16[400,128]{1,0:T(8,128)(2,1)S(1)}, u32[]{:S(2)}, u32[]{:S(2)}) collective-permute-start(bf16[400,128]{1,0:T(8,128)(2,1)} %get-tuple-element.37), channel_id=1, source_target_pairs={{0,48},{16,64},{32,80},{48,96},{64,112},{80,0},{96,16},{112,32},{1... | collective-permute-start | bytes 307208 | tf_op jit(solution)/shard_map/ppermute | solution.py:20
  108.9 21.0 %collective-permute-start.29 = (bf16[400,128]{1,0:T(8,128)(2,1)}, bf16[400,128]{1,0:T(8,128)(2,1)S(1)}, u32[]{:S(2)}, u32[]{:S(2)}) collective-permute-start(bf16[400,128]{1,0:T(8,128)(2,1)} %get-tuple-element.38), channel_id=1, source_target_pairs={{0,64},{16,80},{32,96},{48,112},{64,0},{80,16},{96,32},{112,48},{1... | collective-permute-start | bytes 307208 | tf_op jit(solution)/shard_map/ppermute | solution.py:20
  110.2 19.7 %collective-permute-start.30 = (bf16[400,128]{1,0:T(8,128)(2,1)}, bf16[400,128]{1,0:T(8,128)(2,1)S(1)}, u32[]{:S(2)}, u32[]{:S(2)}) collective-permute-start(bf16[400,128]{1,0:T(8,128)(2,1)} %get-tuple-element.39), channel_id=1, source_target_pairs={{0,80},{16,96},{32,112},{48,0},{64,16},{80,32},{96,48},{112,64},{1... | collective-permute-start | bytes 307208 | tf_op jit(solution)/shard_map/ppermute | solution.py:20
  113.4 17.5 %collective-permute-start.31 = (bf16[400,128]{1,0:T(8,128)(2,1)}, bf16[400,128]{1,0:T(8,128)(2,1)S(1)}, u32[]{:S(2)}, u32[]{:S(2)}) collective-permute-start(bf16[400,128]{1,0:T(8,128)(2,1)} %get-tuple-element.40), channel_id=1, source_target_pairs={{0,96},{16,112},{32,0},{48,16},{64,32},{80,48},{96,64},{112,80},{1... | collective-permute-start | bytes 307208 | tf_op jit(solution)/shard_map/ppermute | solution.py:20
  116.7 14.2 %collective-permute-start.32 = (bf16[400,128]{1,0:T(8,128)(2,1)S(1)}, bf16[400,128]{1,0:T(8,128)(2,1)S(1)}, u32[]{:S(2)}, u32[]{:S(2)}) collective-permute-start(bf16[400,128]{1,0:T(8,128)(2,1)S(1)} %get-tuple-element.41), channel_id=1, source_target_pairs={{0,112},{16,0},{32,16},{48,32},{64,48},{80,64},{96,80},{112,96},{1... | collective-permute-start | bytes 307208 | tf_op jit(solution)/shard_map/ppermute | solution.py:20

commit v4 on v3

--- a/solution.py
+++ b/solution.py
@@ -33,8 +33,8 @@
 
 def decode(x):
     wide = x.astype(F32)
-    root = jnp.sqrt(jnp.sqrt(jnp.abs(wide)))
-    return jnp.where(wide < 0, -root, root)
+    half = lax.rsqrt(jnp.maximum(jnp.abs(wide), 1e-37))
+    return wide * half * (half * lax.rsqrt(half))
 
 
 def split3(value):
@@ -58,8 +58,9 @@
     return jnp.transpose(jnp.broadcast_to(column, (column.shape[0], LANES)))[:1, :]
 
 
-def call(body, outs, args, name, flops=0, exps=0, smem_out=None):
-    size = sum(a.size * a.dtype.itemsize for a in (*args, *outs))
+def call(body, outs, args, name, flops=0, exps=0, smem_out=None, size=None):
+    if size is None:
+        size = sum(a.size * a.dtype.itemsize for a in (*args, *outs))
     spaces = [pltpu.SMEM if i == smem_out else pltpu.VMEM for i in range(len(outs))]
     return pl.pallas_call(
         body,
@@ -67,13 +68,13 @@
         in_specs=[pl.BlockSpec(memory_space=pltpu.VMEM)] * len(args),
         out_specs=tuple(pl.BlockSpec(memory_space=s) for s in spaces),
         cost_estimate=pl.CostEstimate(flops=flops, bytes_accessed=size, transcendentals=exps),
-        compiler_params=pltpu.CompilerParams(vmem_limit_bytes=48 * 1024 * 1024),
+        compiler_params=pltpu.CompilerParams(vmem_limit_bytes=20 * 1024 * 1024),
         name=name,
     )(*args)
 
 
 def score_body(n_z, inv_root, *refs):
-    pieces, (image, pair, ids, scores, text, sent) = refs[: 2 * n_z], refs[2 * n_z :]
+    pieces, (image, scores, text, sent) = refs[: 2 * n_z], refs[2 * n_z :]
     rows = pieces[0].shape[0]
     size = image.shape[0]
     z = lax.axis_index("z")
@@ -84,7 +85,6 @@
             start = h * n_z * rows + lax.rem(z + q, n_z) * rows
             text[pl.ds(pl.multiple_of(start, 16), rows), :] = piece
             high = jnp.maximum(high, jnp.abs(piece.astype(F32)))
-    found = jnp.zeros((1, size), F32)
     step = 256
     for r in range(0, size, step):
         tile = (
@@ -100,43 +100,46 @@
         top = jnp.max(tile, axis=1, keepdims=True)
         part = top + jnp.log(jnp.sum(jnp.exp(tile - top), axis=1, keepdims=True))
         sent[:, 0, r : r + step] = jnp.broadcast_to(to_row(part), (sent.shape[0], step))
-        hit = to_column(pair[:, r : r + step]) == ids[...]
-        found += jnp.sum(jnp.where(hit, tile, 0.0), axis=0, keepdims=True)
-    sent[:, 0, size : size + LANES] = jnp.full((sent.shape[0], LANES), jnp.sum(found))
-    sent[:, 0, size + LANES :] = jnp.full((sent.shape[0], LANES), jnp.max(high))
-
-
-def column_body(scores, image, sent):
+    sent[:, 0, size:] = jnp.full((sent.shape[0], LANES), jnp.max(high))
+
+
+def column_body(scores, image, pair, ids, sent):
     size = scores.shape[1]
     tile = scores[...]
     top = jnp.max(tile, axis=0, keepdims=True)
     part = top + jnp.log(jnp.sum(jnp.exp(tile - top), axis=0, keepdims=True))
     sent[:, :size] = part
     high = jnp.max(jnp.abs(image[...].astype(F32)))
-    sent[:, size:] = jnp.full((1, LANES), high)
-
-
-def pair_body(mine, seen, out):
-    size = mine.shape[1] - LANES
+    sent[:, size : size + LANES] = jnp.full((1, LANES), high)
+    hit = to_column(pair[...]) == ids[...]
+    found = jnp.sum(jnp.where(hit, tile, 0.0), axis=0, keepdims=True)
+    sent[:, size + LANES :] = jnp.full((1, LANES), jnp.sum(found))
+
+
+def pair_body(crossed, mine, seen, out):
+    size = mine.shape[1] - 2 * LANES
     half = size // 2
-    other = jnp.concatenate([seen[:, half:size], seen[:, :half]], axis=1)
+    other = seen[:, :size]
+    if crossed:
+        other = jnp.concatenate([seen[:, half:size], seen[:, :half]], axis=1)
     out[:, :size] = merge([mine[:, :size], other])
-    out[:, size:] = jnp.maximum(mine[:, size:], seen[:, size:])
-
-
-def image_body(n_z, inv_root, *refs):
-    cols = refs[:n_z]
-    scores, text, row_got, pair, ids, grads, sent, terms = refs[n_z:]
+    at = slice(size, size + LANES)
+    out[:, at] = jnp.maximum(mine[:, at], seen[:, at])
+    at = slice(size + LANES, size + 2 * LANES)
+    out[:, at] = mine[:, at] + seen[:, at]
+
+
+def image_body(inv_root, cols, scores, text, row_got, pair, ids, grads, sent, terms):
     size = scores.shape[0]
     n_plane = sent.shape[0]
     rows = size // n_plane
-    col_lse = merge([c[:, :size] for c in cols])
-    image_max = functools.reduce(jnp.maximum, [c[:, size:] for c in cols])
+    col_lse = cols[:, :size]
+    image_max = cols[:, size : size + LANES]
+    found = cols[:, size + LANES :]
     row_lse = merge([row_got[i : i + 1, :size] for i in range(n_plane)])
-    matched = jnp.sum(row_got[:, size : size + LANES], axis=0, keepdims=True)
-    text_max = jnp.max(row_got[:, size + LANES :], axis=0, keepdims=True)
-    row_terms = jnp.sum(row_lse, axis=1, keepdims=True) - 2.0 * matched
-    col_terms = jnp.broadcast_to(jnp.sum(col_lse, axis=1, keepdims=True), (1, LANES))
+    text_max = jnp.max(row_got[:, size:], axis=0, keepdims=True)
+    row_terms = jnp.broadcast_to(jnp.sum(row_lse, axis=1, keepdims=True), (1, LANES))
+    col_terms = jnp.sum(col_lse, axis=1, keepdims=True) - 2.0 * found
     terms[...] = jnp.concatenate(
         [row_terms, text_max, image_max, jnp.zeros((5, LANES), F32)], axis=0
     )
@@ -196,7 +199,21 @@
         pay[count * rows :, :] = extra
 
 
-def image_sum_body(got, terms, out, side):
+def text_sum_body(keep, total, terms, *refs):
+    pays, out, side = refs[:-2], refs[-2], refs[-1]
+    rows, width = out.shape
+    unit = terms[2:3, :1]
+    unit = jnp.where(unit > 0, unit, 1.0)
+    count = width // LANES
+    for k in range(count):
+        at = slice(k * rows, (k + 1) * rows)
+        lanes = slice(k * LANES, (k + 1) * LANES)
+        out[:, lanes] = keep[:, lanes] + unit * sum(decode(p[at, :]) for p in pays)
+    tail = sum(p[count * rows :, :].astype(F32) for p in pays)
+    side[...] = total[...] + jnp.sum(tail, axis=0, keepdims=True)
+
+
+def image_sum_body(pairs, got, terms, side, out, loss):
     rows, width = out.shape
     unit = terms[1:2, :1]
     unit = jnp.where(unit > 0, unit, 1.0)
@@ -207,21 +224,7 @@
             decode(got[p, at, :]) for p in range(got.shape[0])
         )
     tail = sum(got[p, count * rows :, :].astype(F32) for p in range(got.shape[0]))
-    side[...] = jnp.sum(tail, axis=0, keepdims=True)
-
-
-def text_sum_body(pairs, keep, total, terms, side, *refs):
-    pays, out, loss = refs[:-2], refs[-2], refs[-1]
-    rows, width = out.shape
-    unit = terms[2:3, :1]
-    unit = jnp.where(unit > 0, unit, 1.0)
-    count = width // LANES
-    for k in range(count):
-        at = slice(k * rows, (k + 1) * rows)
-        lanes = slice(k * LANES, (k + 1) * LANES)
-        out[:, lanes] = keep[:, lanes] + unit * sum(decode(p[at, :]) for p in pays)
-    tail = sum(p[count * rows :, :].astype(F32) for p in pays)
-    full = total[...] + side[...] + jnp.sum(tail, axis=0, keepdims=True)
+    full = side[...] + jnp.sum(tail, axis=0, keepdims=True)
     loss[0, 0] = jnp.max(full) / (2.0 * pairs)
 
 
@@ -237,12 +240,6 @@
     shape = jax.ShapeDtypeStruct
     tall = width // LANES * rows + EXTRA
 
-    pair_other = lax.ppermute(pair_index, "xl", SWAP)
-    first = lax.axis_index("xl") == 0
-    pair = jnp.concatenate(
-        [jnp.where(first, pair_index, pair_other), jnp.where(first, pair_other, pair_index)]
-    )
-    pair = pair.astype(F32)[None, :]
     block = (lax.axis_index("y") * n_xh + lax.axis_index("xh")) * n_xl + lax.axis_index("xl")
     slot = lax.broadcasted_iota(jnp.int32, (1, size), 1)
     own = slot < half
@@ -253,6 +250,13 @@
     image = lax.all_to_all(
         jnp.broadcast_to(image_embed[None], (n_plane, rows, width)), PLANE, 0, 0
     ).reshape(size, width)
+    image, pair_index = lax.optimization_barrier((image, pair_index))
+    pair_other = lax.ppermute(pair_index, "xl", SWAP)
+    first = lax.axis_index("xl") == 0
+    pair = jnp.concatenate(
+        [jnp.where(first, pair_index, pair_other), jnp.where(first, pair_other, pair_index)]
+    )
+    pair = pair.astype(F32)[None, :]
     pieces = [text_embed] + [turn(text_embed, "z", -q) for q in range(1, n_z)]
     pieces = pieces + [lax.ppermute(piece, "c", SWAP) for piece in pieces]
 
@@ -262,33 +266,34 @@
         (
             shape((size, size), F32),
             shape((size, width), BF16),
-            shape((n_plane, 1, size + 2 * LANES), F32),
+            shape((n_plane, 1, size + LANES), F32),
         ),
-        (*pieces, image, pair, ids),
+        (*pieces, image),
         "scores",
         flops,
         size * size,
     )
-    row_got = lax.all_to_all(row_sent, PLANE, 0, 0).reshape(n_plane, size + 2 * LANES)
-    (col_sent,) = call(
-        column_body, (shape((1, size + LANES), F32),), (scores, image), "columns", 0, size * size
-    )
-    (col_pair,) = call(
-        pair_body,
-        (shape((1, size + LANES), F32),),
-        (col_sent, lax.ppermute(col_sent, "c", SWAP)),
-        "pair",
-    )
-    cols = [col_pair] + [turn(col_pair, "z", q) for q in range(1, n_z)]
+    row_got = lax.all_to_all(row_sent, PLANE, 0, 0).reshape(n_plane, size + LANES)
+    cols_shape = (shape((1, size + 2 * LANES), F32),)
+    (cols,) = call(
+        column_body, cols_shape, (scores, image, pair, ids), "columns", 0, size * size
+    )
+    seen = lax.ppermute(cols, "c", SWAP)
+    (cols,) = call(functools.partial(pair_body, True), cols_shape, (cols, seen), "pair")
+    step = 1
+    while step < n_z:
+        seen = lax.ppermute(cols, "z", [(i, i ^ step) for i in range(n_z)])
+        (cols,) = call(functools.partial(pair_body, False), cols_shape, (cols, seen), "pair")
+        step *= 2
 
     grads, image_sent, terms = call(
-        functools.partial(image_body, n_z, inv_root),
+        functools.partial(image_body, inv_root),
         (
             shape((size, size), BF16),
             shape((n_plane, tall, LANES), BF16),
             shape((8, LANES), F32),
         ),
-        (*cols, scores, text, row_got, pair, ids),
+        (cols, scores, text, row_got, pair, ids),
         "image_grad",
         flops,
         2 * size * size,
@@ -299,7 +304,7 @@
         (shape((half, width), F32), shape((half, width), F32)),
         (grads, image),
         "text_grad",
-        flops,
+        size=1,
     )
     keep, total, *pays = call(
         functools.partial(send_body, n_z),
@@ -307,19 +312,20 @@
         + (shape((tall, LANES), BF16),) * (n_z - 1),
         (text_own, lax.ppermute(text_other, "c", SWAP), terms, lax.ppermute(terms, "c", SWAP)),
         "send",
+        size=1,
     )
     pays = [turn(pay, "z", q + 1) for q, pay in enumerate(pays)]
-    grad_image, side = call(
-        image_sum_body,
+    grad_text, side = call(
+        text_sum_body,
         (shape((rows, width), F32), shape((1, LANES), F32)),
-        (image_got, terms),
+        (keep, total, terms, *pays),
+        "text_sum",
+    )
+    grad_image, loss = call(
+        functools.partial(image_sum_body, pairs),
+        (shape((rows, width), F32), shape((1, 1), F32)),
+        (image_got, terms, side),
         "image_sum",
-    )
-    grad_text, loss = call(
-        functools.partial(text_sum_body, pairs),
-        (shape((rows, width), F32), shape((1, 1), F32)),
-        (keep, total, terms, side, *pays),
-        "text_sum",
         smem_out=1,
     )
     return (loss[0, 0], grad_image, grad_text)

time: 134 us -> 123 us (0.918)
  starting transfers between devices: 83.4 us -> 73.9 us
  Pallas kernels: 18.3 us -> 13.9 us
  local copies, waits for them, and re-layouts: 5.13 us -> 8.18 us
    ppermute x21 -> x14, starting transfers between devices: 42.1 us -> 28.6 us  [turn(): lax.ppermute(x, axis, [(i, (i + step) % count) for i in range(count)])]
    ppermute x21 -> x14, waiting for transfers between devices: 4.57 us -> 16.5 us  [turn(): lax.ppermute(x, axis, [(i, (i + step) % count) for i in range(count)])]
    all_to_all x1, waiting for transfers between devices: 9.01 us -> 0.01 us  [shards(): image_got = lax.all_to_all(image_sent, PLANE, 0, 0)]
    ppermute x1, waiting for transfers between devices: 8.65 us -> 0.01 us  [shards(): pair_other = lax.ppermute(pair_index, 'xl', SWAP)]
    ppermute x1 -> x4, waiting for transfers between devices: 0.82 us -> 8.16 us  [the longest x3 7.34 us: shards(): seen = lax.ppermute(cols, 'z', [(i, i ^ step) for i in range(n_z)])]
    ppermute x1 -> x4, starting transfers between devices: 0.64 us -> 6.86 us  [the longest x3 5.79 us: shards(): seen = lax.ppermute(cols, 'z', [(i, i ^ step) for i in range(n_z)])]
    pallas_call x8 -> x11, Pallas kernels: 18.3 us -> 13.9 us  [call(): pl.pallas_call(body, out_shape=outs, in_specs=[pl.BlockSpec(memory_space=...]
    unnamed x11 -> x15, local copies, waits for them, and re-layouts: 2.86 us -> 5.9 us
  transfers between devices with their start and end apart: 36 -> 32, of which waited for: 13 -> 11; matrix products, arithmetic and copies ran while one was open for 0% -> 0% of each run, Pallas kernels for 3% -> 4%
where the time goes in v4:
time: 123 us
  starting transfers between devices  73.9 us (60%)
  waiting for transfers between devices  25.6 us (21%)
  Pallas kernels  13.9 us (11%)
  local copies, waits for them, and re-layouts  8.18 us (7%)
    ppermute x14, starting transfers between devices, turn(): lax.ppermute(x, axis, [(i, (i + step) % count) for i in range(count)])  28.6 us
    ppermute x14, waiting for transfers between devices, turn(): lax.ppermute(x, axis, [(i, (i + step) % count) for i in range(count)])  16.5 us
    pallas_call x11, Pallas kernels, call(): pl.pallas_call(body, out_shape=outs, in_specs=[pl.BlockSpec(memory_space=...  13.9 us
    ppermute x8, starting transfers between devices, shards(): pieces = pieces + [lax.ppermute(piece, 'c', SWAP) for piece in pieces]  12.1 us
    all_to_all x1, starting transfers between devices, shards(): lax.all_to_all(jnp.broadcast_to(image_embed[None], (n_plane, rows, width)...  7.72 us
    ppermute x3, waiting for transfers between devices, shards(): seen = lax.ppermute(cols, 'z', [(i, i ^ step) for i in range(n_z)])  7.34 us
    all_to_all x1, starting transfers between devices, shards(): image_got = lax.all_to_all(image_sent, PLANE, 0, 0)  6.93 us
    all_to_all x1, starting transfers between devices, shards(): lax.all_to_all(row_sent, PLANE, 0, 0).reshape(n_plane, size + LANES)  6.18 us
  transfers between devices with their start and end apart: 32, of which 11 were waited for; matrix products, arithmetic and copies ran while one was open for 0% of the time, Pallas kernels for 4%

profile of v4, /device:TPU:1, one launch (start us, length us, event | category | flops | bytes accessed | tf_op | source)
XLA Modules:
  0.0 122.5 jit_solution(2708372130690941387)
XLA Ops:
  0.6 2.3 %broadcast_in_dim.15 = bf16[16,48,1024]{2,1,0:T(8,128)(2,1)} broadcast(bf16[48,1024]{1,0:T(8,128)(2,1)} %param.3), dimensions={1,2} | broadcast | bytes 1671168 | tf_op jit(solution)/shard_map/broadcast_in_dim | solution.py:251
  2.9 7.7 %all-to-all-start = ((bf16[16,48,1024]{2,1,0:T(8,128)(2,1)}), bf16[16,48,1024]{2,1,0:T(8,128)(2,1)S(1)}, u32[]{:S(2)}, u32[]{:S(2)}) async-start(bf16[16,48,1024]{2,1,0:T(8,128)(2,1)} %broadcast_in_dim.15), calls=%async_computation | async-start | bytes 3145728 | tf_op jit(solution)/shard_map/all_to_all | solution.py:250
  10.6 1.7 %collective-permute-start.6 = (bf16[48,1024]{1,0:T(8,128)(2,1)S(1)}, bf16[48,1024]{1,0:T(8,128)(2,1)S(1)}, u32[]{:S(2)}, u32[]{:S(2)}) collective-permute-start(bf16[48,1024]{1,0:T(8,128)(2,1)S(1)} %copy-done.3), channel_id=1, source_target_pairs={{0,16},{16,32},{32,48},{48,64},{64,80},{80,96},{96,112},{112,0},{1... | collective-permute-start | bytes 294920 | tf_op jit(solution)/shard_map/ppermute | solution.py:20
  12.4 3.0 %collective-permute-start.5 = (bf16[48,1024]{1,0:T(8,128)(2,1)S(1)}, bf16[48,1024]{1,0:T(8,128)(2,1)S(1)}, u32[]{:S(2)}, u32[]{:S(2)}) collective-permute-start(bf16[48,1024]{1,0:T(8,128)(2,1)S(1)} %copy-done.3), channel_id=1, source_target_pairs={{0,32},{16,48},{32,64},{48,80},{64,96},{80,112},{96,0},{112,16},{1... | collective-permute-start | bytes 294920 | tf_op jit(solution)/shard_map/ppermute | solution.py:20
  15.3 3.8 %collective-permute-start.4 = (bf16[48,1024]{1,0:T(8,128)(2,1)S(1)}, bf16[48,1024]{1,0:T(8,128)(2,1)S(1)}, u32[]{:S(2)}, u32[]{:S(2)}) collective-permute-start(bf16[48,1024]{1,0:T(8,128)(2,1)S(1)} %copy-done.3), channel_id=1, source_target_pairs={{0,48},{16,64},{32,80},{48,96},{64,112},{80,0},{96,16},{112,32},{1... | collective-permute-start | bytes 294920 | tf_op jit(solution)/shard_map/ppermute | solution.py:20
  19.6 4.5 %collective-permute-start.2 = (bf16[48,1024]{1,0:T(8,128)(2,1)S(1)}, bf16[48,1024]{1,0:T(8,128)(2,1)S(1)}, u32[]{:S(2)}, u32[]{:S(2)}) collective-permute-start(bf16[48,1024]{1,0:T(8,128)(2,1)S(1)} %copy-done.3), channel_id=1, source_target_pairs={{0,80},{16,96},{32,112},{48,0},{64,16},{80,32},{96,48},{112,64},{1... | collective-permute-start | bytes 294920 | tf_op jit(solution)/shard_map/ppermute | solution.py:20
  24.0 2.4 %collective-permute-start.1 = (bf16[48,1024]{1,0:T(8,128)(2,1)S(1)}, bf16[48,1024]{1,0:T(8,128)(2,1)S(1)}, u32[]{:S(2)}, u32[]{:S(2)}) collective-permute-start(bf16[48,1024]{1,0:T(8,128)(2,1)S(1)} %copy-done.3), channel_id=1, source_target_pairs={{0,96},{16,112},{32,0},{48,16},{64,32},{80,48},{96,64},{112,80},{1... | collective-permute-start | bytes 294920 | tf_op jit(solution)/shard_map/ppermute | solution.py:20
  26.4 0.7 collective-permute-start
  27.2 1.5 %collective-permute-done.4.refs_5_ = bf16[48,1024]{1,0:T(8,128)(2,1)S(1)} collective-permute-done((bf16[48,1024]{1,0:T(8,128)(2,1)S(1)}, bf16[48,1024]{1,0:T(8,128)(2,1)S(1)}, u32[]{:S(2)}, u32[]{:S(2)}) %collective-permute-start.4) | collective-permute-done | bytes 98336 | tf_op jit(solution)/shard_map/ppermute | solution.py:20
  28.7 5.4 %collective-permute-start.7 = (bf16[48,1024]{1,0:T(8,128)(2,1)S(1)}, bf16[48,1024]{1,0:T(8,128)(2,1)S(1)}, u32[]{:S(2)}, u32[]{:S(2)}) collective-permute-start(bf16[48,1024]{1,0:T(8,128)(2,1)S(1)} %copy-done.3), channel_id=1, source_target_pairs={{0,8},{8,0},{1,9},{9,1},{2,10},{10,2},{3,11},{11,3},{4,12},{12,4},... | collective-permute-start | bytes 294920 | tf_op jit(solution)/shard_map/ppermute | solution.py:261
  34.0 5.3 %collective-permute-start.13 = (bf16[48,1024]{1,0:T(8,128)(2,1)S(1)}, bf16[48,1024]{1,0:T(8,128)(2,1)S(1)}, u32[]{:S(2)}, u32[]{:S(2)}) collective-permute-start(bf16[48,1024]{1,0:T(8,128)(2,1)S(1)} %collective-permute-done.5.refs_6_), channel_id=1, source_target_pairs={{0,8},{8,0},{1,9},{9,1},{2,10},{10,2},{3,11},{11,3},{4,12},{12,4},... | collective-permute-start | bytes 294920 | tf_op jit(solution)/shard_map/ppermute | solution.py:261
  40.0 0.7 collective-permute-start.11
  40.7 0.5 collective-permute-start.9
  41.3 1.9 %collective-permute-start.15 = (s32[384]{0:T(512)S(1)}, s32[384]{0:T(512)S(1)}, u32[]{:S(2)}, u32[]{:S(2)}) collective-permute-start(s32[384]{0:T(512)S(1)} %copy-done.6), channel_id=1, source_target_pairs={{0,128},{128,0},{1,129},{129,1},{2,130},{130,2},{3,131},{131,3},{4... | collective-permute-start | bytes 4616 | tf_op jit(solution)/shard_map/ppermute | solution.py:254
  43.3 2.6 %scores.1 = (f32[768,768]{1,0:T(8,128)S(1)}, bf16[768,1024]{1,0:T(8,128)(2,1)S(1)}, f32[16,1,896]{2,1,0:T(1,128)}) custom-call(bf16[48,1024]{1,0:T(8,128)(2,1)S(1)} %copy-done.3, bf16[48,1024]{1,0:T(8,128)(2,1)S(1)} %collective-permute-done.refs_1_, bf16[48,1024]{1,0:T(8,128)(2,1)S(1)} %collective-permute-done.1.refs_2_, ...), custom_call_target="tpu_custom_call" | custom-call | flops 1207959552 | bytes 7135232 | tf_op jit(solution)/shard_map/scores/pallas_call | solution.py:65
  45.9 1.4 %copy-done = f32[768,768]{1,0:T(8,128)} copy-done((f32[768,768]{1,0:T(8,128)}, f32[768,768]{1,0:T(8,128)S(1)}, u32[]{:S(2)}) %copy-start) | copy-done | bytes 2359320
  47.3 1.1 copy-done.4
  48.5 6.2 %all-to-all-start.1 = ((f32[16,1,896]{2,1,0:T(1,128)}), f32[16,1,896]{2,1,0:T(1,128)S(1)}, u32[]{:S(2)}, u32[]{:S(2)}) async-start(f32[16,1,896]{2,1,0:T(1,128)} %get-tuple-element.30), calls=%async_computation.1 | async-start | bytes 114688 | tf_op jit(solution)/shard_map/all_to_all | solution.py:276
  54.7 1.7 %copy-done.1 = f32[768,768]{1,0:T(8,128)S(1)} copy-done((f32[768,768]{1,0:T(8,128)S(1)}, f32[768,768]{1,0:T(8,128)}, u32[]{:S(2)}) %copy-start.1) | copy-done | bytes 2359320
  56.4 1.0 columns.1.mine
  57.4 1.1 collective-permute-start.16
  58.4 0.8 collective-permute-done.16.seen
  59.3 1.9 %collective-permute-start.17 = (f32[1,1024]{1,0:T(1,128)S(1)}, f32[1,1024]{1,0:T(1,128)S(1)}, u32[]{:S(2)}, u32[]{:S(2)}) collective-permute-start(f32[1,1024]{1,0:T(1,128)S(1)} %pair.4.mine), channel_id=1, source_target_pairs={{0,16},{16,0},{32,48},{48,32},{64,80},{80,64},{96,112},{112,96},{1... | collective-permute-start | bytes 12296 | tf_op jit(solution)/shard_map/ppermute | solution.py:285
  61.2 1.3 %collective-permute-done.17.seen = f32[1,1024]{1,0:T(1,128)S(1)} collective-permute-done((f32[1,1024]{1,0:T(1,128)S(1)}, f32[1,1024]{1,0:T(1,128)S(1)}, u32[]{:S(2)}, u32[]{:S(2)}) %collective-permute-start.17) | collective-permute-done | bytes 4128 | tf_op jit(solution)/shard_map/ppermute | solution.py:285
  62.5 1.6 %collective-permute-start.18 = (f32[1,1024]{1,0:T(1,128)S(1)}, f32[1,1024]{1,0:T(1,128)S(1)}, u32[]{:S(2)}, u32[]{:S(2)}) collective-permute-start(f32[1,1024]{1,0:T(1,128)S(1)} %pair.5.mine), channel_id=1, source_target_pairs={{0,32},{16,48},{32,0},{48,16},{64,96},{80,112},{96,64},{112,80},{1... | collective-permute-start | bytes 12296 | tf_op jit(solution)/shard_map/ppermute | solution.py:285
  64.1 1.9 %collective-permute-done.18.seen = f32[1,1024]{1,0:T(1,128)S(1)} collective-permute-done((f32[1,1024]{1,0:T(1,128)S(1)}, f32[1,1024]{1,0:T(1,128)S(1)}, u32[]{:S(2)}, u32[]{:S(2)}) %collective-permute-start.18) | collective-permute-done | bytes 4128 | tf_op jit(solution)/shard_map/ppermute | solution.py:285
  66.0 2.3 %collective-permute-start.19 = (f32[1,1024]{1,0:T(1,128)S(1)}, f32[1,1024]{1,0:T(1,128)S(1)}, u32[]{:S(2)}, u32[]{:S(2)}) collective-permute-start(f32[1,1024]{1,0:T(1,128)S(1)} %pair.6.mine), channel_id=1, source_target_pairs={{0,64},{16,80},{32,96},{48,112},{64,0},{80,16},{96,32},{112,48},{1... | collective-permute-start | bytes 12296 | tf_op jit(solution)/shard_map/ppermute | solution.py:285
  68.3 4.2 %collective-permute-done.19.seen = f32[1,1024]{1,0:T(1,128)S(1)} collective-permute-done((f32[1,1024]{1,0:T(1,128)S(1)}, f32[1,1024]{1,0:T(1,128)S(1)}, u32[]{:S(2)}, u32[]{:S(2)}) %collective-permute-start.19) | collective-permute-done | bytes 4128 | tf_op jit(solution)/shard_map/ppermute | solution.py:285
  72.5 1.7 %copy-done.2 = f32[768,768]{1,0:T(8,128)S(1)} copy-done((f32[768,768]{1,0:T(8,128)S(1)}, f32[768,768]{1,0:T(8,128)}, u32[]{:S(2)}) %copy-start.2) | copy-done | bytes 2359320
  74.2 3.5 %image_grad.1 = (bf16[768,768]{1,0:T(8,128)(2,1)S(1)}, bf16[16,400,128]{2,1,0:T(8,128)(2,1)}, f32[8,128]{1,0:T(8,128)S(1)}) custom-call(f32[1,1024]{1,0:T(1,128)S(1)} %pair.7.cols, f32[768,768]{1,0:T(8,128)S(1)} %copy-done.2, bf16[768,1024]{1,0:T(8,128)(2,1)S(1)} %copy-done.5, f32[16,896]{1,0:T(8,128)S(1)} %bitcast.8, f32[1,768]{1,0:T(1,128)S(1)} %get-tuple-element.51.pair, ...), custom_call_target="tpu_custom_call" | custom-call | flops 1207959552 | bytes 6821888 | tf_op jit(solution)/shard_map/image_grad/pallas_call | solution.py:65
  77.7 2.0 %text_grad.1 = (f32[384,1024]{1,0:T(8,128)S(1)}, f32[384,1024]{1,0:T(8,128)}) custom-call(bf16[768,768]{1,0:T(8,128)(2,1)S(1)} %get-tuple-element.33.grads, bf16[768,1024]{1,0:T(8,128)(2,1)S(1)} %bitcast.7), custom_call_target="tpu_custom_call" | custom-call | bytes 1 | tf_op jit(solution)/shard_map/text_grad/pallas_call | solution.py:65
  79.7 3.2 %collective-permute-start.20 = (f32[384,1024]{1,0:T(8,128)}, f32[384,1024]{1,0:T(8,128)}, u32[]{:S(2)}, u32[]{:S(2)}) collective-permute-start(f32[384,1024]{1,0:T(8,128)} %get-tuple-element.35), channel_id=1, source_target_pairs={{0,8},{8,0},{1,9},{9,1},{2,10},{10,2},{3,11},{11,3},{4,12},{12,4},... | collective-permute-start | bytes 4718600 | tf_op jit(solution)/shard_map/ppermute | solution.py:313
  82.9 6.9 %all-to-all-start.2 = ((bf16[16,400,128]{2,1,0:T(8,128)(2,1)}), bf16[16,400,128]{2,1,0:T(8,128)(2,1)S(1)}, u32[]{:S(2)}, u32[]{:S(2)}) async-start(bf16[16,400,128]{2,1,0:T(8,128)(2,1)} %get-tuple-element.31), calls=%async_computation.2 | async-start | bytes 3276800 | tf_op jit(solution)/shard_map/all_to_all | solution.py:301
  90.2 0.9 collective-permute-done.21.terms_seen
  91.1 1.9 %send.1 = (f32[48,1024]{1,0:T(8,128)S(1)}, f32[1,128]{1,0:T(1,128)S(1)}, bf16[400,128]{1,0:T(8,128)(2,1)S(1)}, bf16[400,128]{1,0:T(8,128)(2,1)S(1)}, bf16[400,12...) custom-call(f32[384,1024]{1,0:T(8,128)S(1)} %get-tuple-element.34.ow, ...), custom_call_target="tpu_custom_call" | custom-call | bytes 1 | tf_op jit(solution)/shard_map/send/pallas_call | solution.py:65
  93.0 1.8 %collective-permute-start.22 = (bf16[400,128]{1,0:T(8,128)(2,1)S(1)}, bf16[400,128]{1,0:T(8,128)(2,1)S(1)}, u32[]{:S(2)}, u32[]{:S(2)}) collective-permute-start(bf16[400,128]{1,0:T(8,128)(2,1)S(1)} %get-tuple-element.38), channel_id=1, source_target_pairs={{0,16},{16,32},{32,48},{48,64},{64,80},{80,96},{96,112},{112,0},{1... | collective-permute-start | bytes 307208 | tf_op jit(solution)/shard_map/ppermute | solution.py:20
  94.8 0.9 collective-permute-start.23
  95.7 1.7 %collective-permute-start.24 = (bf16[400,128]{1,0:T(8,128)(2,1)S(1)}, bf16[400,128]{1,0:T(8,128)(2,1)S(1)}, u32[]{:S(2)}, u32[]{:S(2)}) collective-permute-start(bf16[400,128]{1,0:T(8,128)(2,1)S(1)} %get-tuple-element.40), channel_id=1, source_target_pairs={{0,48},{16,64},{32,80},{48,96},{64,112},{80,0},{96,16},{112,32},{1... | collective-permute-start | bytes 307208 | tf_op jit(solution)/shard_map/ppermute | solution.py:20
  97.3 3.2 %collective-permute-start.25 = (bf16[400,128]{1,0:T(8,128)(2,1)S(1)}, bf16[400,128]{1,0:T(8,128)(2,1)S(1)}, u32[]{:S(2)}, u32[]{:S(2)}) collective-permute-start(bf16[400,128]{1,0:T(8,128)(2,1)S(1)} %get-tuple-element.41), channel_id=1, source_target_pairs={{0,64},{16,80},{32,96},{48,112},{64,0},{80,16},{96,32},{112,48},{1... | collective-permute-start | bytes 307208 | tf_op jit(solution)/shard_map/ppermute | solution.py:20
  100.5 2.6 %collective-permute-start.26 = (bf16[400,128]{1,0:T(8,128)(2,1)S(1)}, bf16[400,128]{1,0:T(8,128)(2,1)S(1)}, u32[]{:S(2)}, u32[]{:S(2)}) collective-permute-start(bf16[400,128]{1,0:T(8,128)(2,1)S(1)} %get-tuple-element.42), channel_id=1, source_target_pairs={{0,80},{16,96},{32,112},{48,0},{64,16},{80,32},{96,48},{112,64},{1... | collective-permute-start | bytes 307208 | tf_op jit(solution)/shard_map/ppermute | solution.py:20
  103.1 0.9 collective-permute-start.27
  104.0 1.1 collective-permute-start.28
  105.1 4.6 %collective-permute-done.24.refs_2_ = bf16[400,128]{1,0:T(8,128)(2,1)S(1)} collective-permute-done((bf16[400,128]{1,0:T(8,128)(2,1)S(1)}, bf16[400,128]{1,0:T(8,128)(2,1)S(1)}, u32[]{:S(2)}, u32[]{:S(2)}) %collective-permute-start.24) | collective-permute-done | bytes 102432 | tf_op jit(solution)/shard_map/ppermute | solution.py:20
  109.7 2.9 %collective-permute-done.25.refs_3_ = bf16[400,128]{1,0:T(8,128)(2,1)S(1)} collective-permute-done((bf16[400,128]{1,0:T(8,128)(2,1)S(1)}, bf16[400,128]{1,0:T(8,128)(2,1)S(1)}, u32[]{:S(2)}, u32[]{:S(2)}) %collective-permute-start.25) | collective-permute-done | bytes 102432 | tf_op jit(solution)/shard_map/ppermute | solution.py:20
  112.6 6.0 %collective-permute-done.27.refs_5_ = bf16[400,128]{1,0:T(8,128)(2,1)S(1)} collective-permute-done((bf16[400,128]{1,0:T(8,128)(2,1)S(1)}, bf16[400,128]{1,0:T(8,128)(2,1)S(1)}, u32[]{:S(2)}, u32[]{:S(2)}) %collective-permute-start.27) | collective-permute-done | bytes 102432 | tf_op jit(solution)/shard_map/ppermute | solution.py:20
  118.6 1.0 collective-permute-done.28.refs_6_
  119.6 1.1 text_sum.1
  120.7 1.7 %image_sum.1 = (f32[48,1024]{1,0:T(8,128)}, f32[1,1]{1,0:T(1,128)}) custom-call(bf16[16,400,128]{2,1,0:T(8,128)(2,1)S(1)} %all-to-all-done.2.got, f32[8,128]{1,0:T(8,128)S(1)} %get-tuple-element.32.terms, f32[1,128]{1,0:T(1,128)S(1)} %get-tuple-element.45.side), custom_call_target="tpu_custom_call" | custom-call | bytes 1839620 | tf_op jit(solution)/shard_map/image_sum/pallas_call | solution.py:65
  (47 shorter events, 1.8 us)
Async XLA Ops:
  2.9 7.7 %copy-start.3 = (bf16[48,1024]{1,0:T(8,128)(2,1)S(1)}, bf16[48,1024]{1,0:T(8,128)(2,1)}, u32[]{:S(2)}) copy-start(bf16[48,1024]{1,0:T(8,128)(2,1)} %refs_0_.1) | copy-start | bytes 294916
  2.9 38.4 %copy-start.6 = (s32[384]{0:T(512)S(1)}, s32[384]{0:T(512)}, u32[]{:S(2)}) copy-start(s32[384]{0:T(512)} %param.5) | copy-start | bytes 4612
  2.9 38.4 %all-to-all-start = ((bf16[16,48,1024]{2,1,0:T(8,128)(2,1)}), bf16[16,48,1024]{2,1,0:T(8,128)(2,1)S(1)}, u32[]{:S(2)}, u32[]{:S(2)}) async-start(bf16[16,48,1024]{2,1,0:T(8,128)(2,1)} %broadcast_in_dim.15), calls=%async_computation | async-start | bytes 3145728 | tf_op jit(solution)/shard_map/all_to_all | solution.py:250
  10.6 13.4 %collective-permute-start.6 = (bf16[48,1024]{1,0:T(8,128)(2,1)S(1)}, bf16[48,1024]{1,0:T(8,128)(2,1)S(1)}, u32[]{:S(2)}, u32[]{:S(2)}) collective-permute-start(bf16[48,1024]{1,0:T(8,128)(2,1)S(1)} %copy-done.3), channel_id=1, source_target_pairs={{0,16},{16,32},{32,48},{48,64},{64,80},{80,96},{96,112},{112,0},{1... | collective-permute-start | bytes 294920 | tf_op jit(solution)/shard_map/ppermute | solution.py:20
  12.4 14.1 %collective-permute-start.5 = (bf16[48,1024]{1,0:T(8,128)(2,1)S(1)}, bf16[48,1024]{1,0:T(8,128)(2,1)S(1)}, u32[]{:S(2)}, u32[]{:S(2)}) collective-permute-start(bf16[48,1024]{1,0:T(8,128)(2,1)S(1)} %copy-done.3), channel_id=1, source_target_pairs={{0,32},{16,48},{32,64},{48,80},{64,96},{80,112},{96,0},{112,16},{1... | collective-permute-start | bytes 294920 | tf_op jit(solution)/shard_map/ppermute | solution.py:20
  15.3 13.3 %collective-permute-start.4 = (bf16[48,1024]{1,0:T(8,128)(2,1)S(1)}, bf16[48,1024]{1,0:T(8,128)(2,1)S(1)}, u32[]{:S(2)}, u32[]{:S(2)}) collective-permute-start(bf16[48,1024]{1,0:T(8,128)(2,1)S(1)} %copy-done.3), channel_id=1, source_target_pairs={{0,48},{16,64},{32,80},{48,96},{64,112},{80,0},{96,16},{112,32},{1... | collective-permute-start | bytes 294920 | tf_op jit(solution)/shard_map/ppermute | solution.py:20
  19.1 14.9 %collective-permute-start.3 = (bf16[48,1024]{1,0:T(8,128)(2,1)S(1)}, bf16[48,1024]{1,0:T(8,128)(2,1)S(1)}, u32[]{:S(2)}, u32[]{:S(2)}) collective-permute-start(bf16[48,1024]{1,0:T(8,128)(2,1)S(1)} %copy-done.3), channel_id=1, source_target_pairs={{0,64},{16,80},{32,96},{48,112},{64,0},{80,16},{96,32},{112,48},{1... | collective-permute-start | bytes 294920 | tf_op jit(solution)/shard_map/ppermute | solution.py:20
  19.6 14.5 %collective-permute-start.2 = (bf16[48,1024]{1,0:T(8,128)(2,1)S(1)}, bf16[48,1024]{1,0:T(8,128)(2,1)S(1)}, u32[]{:S(2)}, u32[]{:S(2)}) collective-permute-start(bf16[48,1024]{1,0:T(8,128)(2,1)S(1)} %copy-done.3), channel_id=1, source_target_pairs={{0,80},{16,96},{32,112},{48,0},{64,16},{80,32},{96,48},{112,64},{1... | collective-permute-start | bytes 294920 | tf_op jit(solution)/shard_map/ppermute | solution.py:20
  24.0 15.3 %collective-permute-start.1 = (bf16[48,1024]{1,0:T(8,128)(2,1)S(1)}, bf16[48,1024]{1,0:T(8,128)(2,1)S(1)}, u32[]{:S(2)}, u32[]{:S(2)}) collective-permute-start(bf16[48,1024]{1,0:T(8,128)(2,1)S(1)} %copy-done.3), channel_id=1, source_target_pairs={{0,96},{16,112},{32,0},{48,16},{64,32},{80,48},{96,64},{112,80},{1... | collective-permute-start | bytes 294920 | tf_op jit(solution)/shard_map/ppermute | solution.py:20
  26.4 13.6 %collective-permute-start = (bf16[48,1024]{1,0:T(8,128)(2,1)S(1)}, bf16[48,1024]{1,0:T(8,128)(2,1)S(1)}, u32[]{:S(2)}, u32[]{:S(2)}) collective-permute-start(bf16[48,1024]{1,0:T(8,128)(2,1)S(1)} %copy-done.3), channel_id=1, source_target_pairs={{0,112},{16,0},{32,16},{48,32},{64,48},{80,64},{96,80},{112,96},{1... | collective-permute-start | bytes 294920 | tf_op jit(solution)/shard_map/ppermute | solution.py:20
  28.7 12.0 %collective-permute-start.7 = (bf16[48,1024]{1,0:T(8,128)(2,1)S(1)}, bf16[48,1024]{1,0:T(8,128)(2,1)S(1)}, u32[]{:S(2)}, u32[]{:S(2)}) collective-permute-start(bf16[48,1024]{1,0:T(8,128)(2,1)S(1)} %copy-done.3), channel_id=1, source_target_pairs={{0,8},{8,0},{1,9},{9,1},{2,10},{10,2},{3,11},{11,3},{4,12},{12,4},... | collective-permute-start | bytes 294920 | tf_op jit(solution)/shard_map/ppermute | solution.py:261
  34.0 6.7 %collective-permute-start.14 = (bf16[48,1024]{1,0:T(8,128)(2,1)S(1)}, bf16[48,1024]{1,0:T(8,128)(2,1)S(1)}, u32[]{:S(2)}, u32[]{:S(2)}) collective-permute-start(bf16[48,1024]{1,0:T(8,128)(2,1)S(1)} %collective-permute-done.6.refs_7_), channel_id=1, source_target_pairs={{0,8},{8,0},{1,9},{9,1},{2,10},{10,2},{3,11},{11,3},{4,12},{12,4},... | collective-permute-start | bytes 294920 | tf_op jit(solution)/shard_map/ppermute | solution.py:261
  34.0 7.2 %collective-permute-start.13 = (bf16[48,1024]{1,0:T(8,128)(2,1)S(1)}, bf16[48,1024]{1,0:T(8,128)(2,1)S(1)}, u32[]{:S(2)}, u32[]{:S(2)}) collective-permute-start(bf16[48,1024]{1,0:T(8,128)(2,1)S(1)} %collective-permute-done.5.refs_6_), channel_id=1, source_target_pairs={{0,8},{8,0},{1,9},{9,1},{2,10},{10,2},{3,11},{11,3},{4,12},{12,4},... | collective-permute-start | bytes 294920 | tf_op jit(solution)/shard_map/ppermute | solution.py:261
  39.3 2.0 %collective-permute-start.12 = (bf16[48,1024]{1,0:T(8,128)(2,1)S(1)}, bf16[48,1024]{1,0:T(8,128)(2,1)S(1)}, u32[]{:S(2)}, u32[]{:S(2)}) collective-permute-start(bf16[48,1024]{1,0:T(8,128)(2,1)S(1)} %collective-permute-done.4.refs_5_), channel_id=1, source_target_pairs={{0,8},{8,0},{1,9},{9,1},{2,10},{10,2},{3,11},{11,3},{4,12},{12,4},... | collective-permute-start | bytes 294920 | tf_op jit(solution)/shard_map/ppermute | solution.py:261
  40.0 3.2 %collective-permute-start.11 = (bf16[48,1024]{1,0:T(8,128)(2,1)S(1)}, bf16[48,1024]{1,0:T(8,128)(2,1)S(1)}, u32[]{:S(2)}, u32[]{:S(2)}) collective-permute-start(bf16[48,1024]{1,0:T(8,128)(2,1)S(1)} %collective-permute-done.3.refs_4_), channel_id=1, source_target_pairs={{0,8},{8,0},{1,9},{9,1},{2,10},{10,2},{3,11},{11,3},{4,12},{12,4},... | collective-permute-start | bytes 294920 | tf_op jit(solution)/shard_map/ppermute | solution.py:261
  40.7 2.5 %collective-permute-start.10 = (bf16[48,1024]{1,0:T(8,128)(2,1)S(1)}, bf16[48,1024]{1,0:T(8,128)(2,1)S(1)}, u32[]{:S(2)}, u32[]{:S(2)}) collective-permute-start(bf16[48,1024]{1,0:T(8,128)(2,1)S(1)} %collective-permute-done.2.refs_3_), channel_id=1, source_target_pairs={{0,8},{8,0},{1,9},{9,1},{2,10},{10,2},{3,11},{11,3},{4,12},{12,4},... | collective-permute-start | bytes 294920 | tf_op jit(solution)/shard_map/ppermute | solution.py:261
  40.7 2.5 %collective-permute-start.9 = (bf16[48,1024]{1,0:T(8,128)(2,1)S(1)}, bf16[48,1024]{1,0:T(8,128)(2,1)S(1)}, u32[]{:S(2)}, u32[]{:S(2)}) collective-permute-start(bf16[48,1024]{1,0:T(8,128)(2,1)S(1)} %collective-permute-done.1.refs_2_), channel_id=1, source_target_pairs={{0,8},{8,0},{1,9},{9,1},{2,10},{10,2},{3,11},{11,3},{4,12},{12,4},... | collective-permute-start | bytes 294920 | tf_op jit(solution)/shard_map/ppermute | solution.py:261
  41.2 2.0 %collective-permute-start.8 = (bf16[48,1024]{1,0:T(8,128)(2,1)S(1)}, bf16[48,1024]{1,0:T(8,128)(2,1)S(1)}, u32[]{:S(2)}, u32[]{:S(2)}) collective-permute-start(bf16[48,1024]{1,0:T(8,128)(2,1)S(1)} %collective-permute-done.refs_1_), channel_id=1, source_target_pairs={{0,8},{8,0},{1,9},{9,1},{2,10},{10,2},{3,11},{11,3},{4,12},{12,4},... | collective-permute-start | bytes 294920 | tf_op jit(solution)/shard_map/ppermute | solution.py:261
  41.3 13.3 %collective-permute-start.15 = (s32[384]{0:T(512)S(1)}, s32[384]{0:T(512)S(1)}, u32[]{:S(2)}, u32[]{:S(2)}) collective-permute-start(s32[384]{0:T(512)S(1)} %copy-done.6), channel_id=1, source_target_pairs={{0,128},{128,0},{1,129},{129,1},{2,130},{130,2},{3,131},{131,3},{4... | collective-permute-start | bytes 4616 | tf_op jit(solution)/shard_map/ppermute | solution.py:254
  45.9 1.4 %copy-start = (f32[768,768]{1,0:T(8,128)}, f32[768,768]{1,0:T(8,128)S(1)}, u32[]{:S(2)}) copy-start(f32[768,768]{1,0:T(8,128)S(1)} %get-tuple-element.27.scores) | copy-start | bytes 7077892
  47.3 1.1 copy-start.4
  48.5 24.0 %all-to-all-start.1 = ((f32[16,1,896]{2,1,0:T(1,128)}), f32[16,1,896]{2,1,0:T(1,128)S(1)}, u32[]{:S(2)}, u32[]{:S(2)}) async-start(f32[16,1,896]{2,1,0:T(1,128)} %get-tuple-element.30), calls=%async_computation.1 | async-start | bytes 114688 | tf_op jit(solution)/shard_map/all_to_all | solution.py:276
  54.7 1.7 %copy-start.1 = (f32[768,768]{1,0:T(8,128)S(1)}, f32[768,768]{1,0:T(8,128)}, u32[]{:S(2)}) copy-start(f32[768,768]{1,0:T(8,128)} %copy-done) | copy-start | bytes 7077892
  56.4 16.1 %copy-start.5 = (bf16[768,1024]{1,0:T(8,128)(2,1)S(1)}, bf16[768,1024]{1,0:T(8,128)(2,1)}, u32[]{:S(2)}) copy-start(bf16[768,1024]{1,0:T(8,128)(2,1)} %copy-done.4) | copy-start | bytes 4718596
  57.4 1.9 %collective-permute-start.16 = (f32[1,1024]{1,0:T(1,128)S(1)}, f32[1,1024]{1,0:T(1,128)S(1)}, u32[]{:S(2)}, u32[]{:S(2)}) collective-permute-start(f32[1,1024]{1,0:T(1,128)S(1)} %columns.1.mine), channel_id=1, source_target_pairs={{0,8},{8,0},{1,9},{9,1},{2,10},{10,2},{3,11},{11,3},{4,12},{12,4},... | collective-permute-start | bytes 12296 | tf_op jit(solution)/shard_map/ppermute | solution.py:281
  59.3 3.2 %collective-permute-start.17 = (f32[1,1024]{1,0:T(1,128)S(1)}, f32[1,1024]{1,0:T(1,128)S(1)}, u32[]{:S(2)}, u32[]{:S(2)}) collective-permute-start(f32[1,1024]{1,0:T(1,128)S(1)} %pair.4.mine), channel_id=1, source_target_pairs={{0,16},{16,0},{32,48},{48,32},{64,80},{80,64},{96,112},{112,96},{1... | collective-permute-start | bytes 12296 | tf_op jit(solution)/shard_map/ppermute | solution.py:285
  62.5 3.4 %collective-permute-start.18 = (f32[1,1024]{1,0:T(1,128)S(1)}, f32[1,1024]{1,0:T(1,128)S(1)}, u32[]{:S(2)}, u32[]{:S(2)}) collective-permute-start(f32[1,1024]{1,0:T(1,128)S(1)} %pair.5.mine), channel_id=1, source_target_pairs={{0,32},{16,48},{32,0},{48,16},{64,96},{80,112},{96,64},{112,80},{1... | collective-permute-start | bytes 12296 | tf_op jit(solution)/shard_map/ppermute | solution.py:285
  66.0 6.5 %collective-permute-start.19 = (f32[1,1024]{1,0:T(1,128)S(1)}, f32[1,1024]{1,0:T(1,128)S(1)}, u32[]{:S(2)}, u32[]{:S(2)}) collective-permute-start(f32[1,1024]{1,0:T(1,128)S(1)} %pair.6.mine), channel_id=1, source_target_pairs={{0,64},{16,80},{32,96},{48,112},{64,0},{80,16},{96,32},{112,48},{1... | collective-permute-start | bytes 12296 | tf_op jit(solution)/shard_map/ppermute | solution.py:285
  72.5 1.7 %copy-start.2 = (f32[768,768]{1,0:T(8,128)S(1)}, f32[768,768]{1,0:T(8,128)}, u32[]{:S(2)}) copy-start(f32[768,768]{1,0:T(8,128)} %copy-done) | copy-start | bytes 7077892
  79.7 11.4 %collective-permute-start.20 = (f32[384,1024]{1,0:T(8,128)}, f32[384,1024]{1,0:T(8,128)}, u32[]{:S(2)}, u32[]{:S(2)}) collective-permute-start(f32[384,1024]{1,0:T(8,128)} %get-tuple-element.35), channel_id=1, source_target_pairs={{0,8},{8,0},{1,9},{9,1},{2,10},{10,2},{3,11},{11,3},{4,12},{12,4},... | collective-permute-start | bytes 4718600 | tf_op jit(solution)/shard_map/ppermute | solution.py:313
  82.9 37.8 %all-to-all-start.2 = ((bf16[16,400,128]{2,1,0:T(8,128)(2,1)}), bf16[16,400,128]{2,1,0:T(8,128)(2,1)S(1)}, u32[]{:S(2)}, u32[]{:S(2)}) async-start(bf16[16,400,128]{2,1,0:T(8,128)(2,1)} %get-tuple-element.31), calls=%async_computation.2 | async-start | bytes 3276800 | tf_op jit(solution)/shard_map/all_to_all | solution.py:301
  89.8 1.3 %collective-permute-start.21 = (f32[8,128]{1,0:T(8,128)S(1)}, f32[8,128]{1,0:T(8,128)S(1)}, u32[]{:S(2)}, u32[]{:S(2)}) collective-permute-start(f32[8,128]{1,0:T(8,128)S(1)} %get-tuple-element.32.terms), channel_id=1, source_target_pairs={{0,8},{8,0},{1,9},{9,1},{2,10},{10,2},{3,11},{11,3},{4,12},{12,4},... | collective-permute-start | bytes 12296 | tf_op jit(solution)/shard_map/ppermute | solution.py:313
  93.0 10.1 %collective-permute-start.22 = (bf16[400,128]{1,0:T(8,128)(2,1)S(1)}, bf16[400,128]{1,0:T(8,128)(2,1)S(1)}, u32[]{:S(2)}, u32[]{:S(2)}) collective-permute-start(bf16[400,128]{1,0:T(8,128)(2,1)S(1)} %get-tuple-element.38), channel_id=1, source_target_pairs={{0,16},{16,32},{32,48},{48,64},{64,80},{80,96},{96,112},{112,0},{1... | collective-permute-start | bytes 307208 | tf_op jit(solution)/shard_map/ppermute | solution.py:20
  94.8 9.2 %collective-permute-start.23 = (bf16[400,128]{1,0:T(8,128)(2,1)S(1)}, bf16[400,128]{1,0:T(8,128)(2,1)S(1)}, u32[]{:S(2)}, u32[]{:S(2)}) collective-permute-start(bf16[400,128]{1,0:T(8,128)(2,1)S(1)} %get-tuple-element.39), channel_id=1, source_target_pairs={{0,32},{16,48},{32,64},{48,80},{64,96},{80,112},{96,0},{112,16},{1... | collective-permute-start | bytes 307208 | tf_op jit(solution)/shard_map/ppermute | solution.py:20
  95.7 14.0 %collective-permute-start.24 = (bf16[400,128]{1,0:T(8,128)(2,1)S(1)}, bf16[400,128]{1,0:T(8,128)(2,1)S(1)}, u32[]{:S(2)}, u32[]{:S(2)}) collective-permute-start(bf16[400,128]{1,0:T(8,128)(2,1)S(1)} %get-tuple-element.40), channel_id=1, source_target_pairs={{0,48},{16,64},{32,80},{48,96},{64,112},{80,0},{96,16},{112,32},{1... | collective-permute-start | bytes 307208 | tf_op jit(solution)/shard_map/ppermute | solution.py:20
  97.3 15.2 %collective-permute-start.25 = (bf16[400,128]{1,0:T(8,128)(2,1)S(1)}, bf16[400,128]{1,0:T(8,128)(2,1)S(1)}, u32[]{:S(2)}, u32[]{:S(2)}) collective-permute-start(bf16[400,128]{1,0:T(8,128)(2,1)S(1)} %get-tuple-element.41), channel_id=1, source_target_pairs={{0,64},{16,80},{32,96},{48,112},{64,0},{80,16},{96,32},{112,48},{1... | collective-permute-start | bytes 307208 | tf_op jit(solution)/shard_map/ppermute | solution.py:20
  100.5 12.1 %collective-permute-start.26 = (bf16[400,128]{1,0:T(8,128)(2,1)S(1)}, bf16[400,128]{1,0:T(8,128)(2,1)S(1)}, u32[]{:S(2)}, u32[]{:S(2)}) collective-permute-start(bf16[400,128]{1,0:T(8,128)(2,1)S(1)} %get-tuple-element.42), channel_id=1, source_target_pairs={{0,80},{16,96},{32,112},{48,0},{64,16},{80,32},{96,48},{112,64},{1... | collective-permute-start | bytes 307208 | tf_op jit(solution)/shard_map/ppermute | solution.py:20
  103.1 15.5 %collective-permute-start.27 = (bf16[400,128]{1,0:T(8,128)(2,1)S(1)}, bf16[400,128]{1,0:T(8,128)(2,1)S(1)}, u32[]{:S(2)}, u32[]{:S(2)}) collective-permute-start(bf16[400,128]{1,0:T(8,128)(2,1)S(1)} %get-tuple-element.43), channel_id=1, source_target_pairs={{0,96},{16,112},{32,0},{48,16},{64,32},{80,48},{96,64},{112,80},{1... | collective-permute-start | bytes 307208 | tf_op jit(solution)/shard_map/ppermute | solution.py:20
  104.0 15.6 %collective-permute-start.28 = (bf16[400,128]{1,0:T(8,128)(2,1)S(1)}, bf16[400,128]{1,0:T(8,128)(2,1)S(1)}, u32[]{:S(2)}, u32[]{:S(2)}) collective-permute-start(bf16[400,128]{1,0:T(8,128)(2,1)S(1)} %get-tuple-element.44), channel_id=1, source_target_pairs={{0,112},{16,0},{32,16},{48,32},{64,48},{80,64},{96,80},{112,96},{1... | collective-permute-start | bytes 307208 | tf_op jit(solution)/shard_map/ppermute | solution.py:20

commit v5 on v4

--- a/solution.py
+++ b/solution.py
@@ -73,15 +73,20 @@
     )(*args)
 
 
-def score_body(n_z, inv_root, *refs):
-    pieces, (image, scores, text, sent) = refs[: 2 * n_z], refs[2 * n_z :]
+def score_body(order, inv_root, *refs):
+    n_z = len(order) + 1
+    steps = [0, *order[::-1]]
+    pieces, refs = refs[: 2 * n_z], refs[2 * n_z :]
+    image, pair_mine, pair_seen, scores, text, row_sent, col_sent = refs
     rows = pieces[0].shape[0]
     size = image.shape[0]
+    pair, ids = labels(pair_mine, pair_seen, n_z, rows)
+    found = jnp.zeros((1, size), F32)
     z = lax.axis_index("z")
     high = jnp.zeros(pieces[0].shape, F32)
     for h in range(2):
-        for q in range(n_z):
-            piece = pieces[h * n_z + q][...]
+        for i, q in enumerate(steps):
+            piece = pieces[h * n_z + i][...]
             start = h * n_z * rows + lax.rem(z + q, n_z) * rows
             text[pl.ds(pl.multiple_of(start, 16), rows), :] = piece
             high = jnp.maximum(high, jnp.abs(piece.astype(F32)))
@@ -99,45 +104,59 @@
         scores[r : r + step, :] = tile
         top = jnp.max(tile, axis=1, keepdims=True)
         part = top + jnp.log(jnp.sum(jnp.exp(tile - top), axis=1, keepdims=True))
-        sent[:, 0, r : r + step] = jnp.broadcast_to(to_row(part), (sent.shape[0], step))
-    sent[:, 0, size:] = jnp.full((sent.shape[0], LANES), jnp.max(high))
-
-
-def column_body(scores, image, pair, ids, sent):
-    size = scores.shape[1]
+        row_sent[:, r : r + step] = to_row(part)
+        hit = to_column(pair[:, r : r + step]) == ids
+        found += jnp.sum(jnp.where(hit, tile, 0.0), axis=0, keepdims=True)
+    row_sent[:, size:] = jnp.full((1, LANES), jnp.max(high))
     tile = scores[...]
     top = jnp.max(tile, axis=0, keepdims=True)
-    part = top + jnp.log(jnp.sum(jnp.exp(tile - top), axis=0, keepdims=True))
-    sent[:, :size] = part
+    col_sent[:, :size] = top + jnp.log(jnp.sum(jnp.exp(tile - top), axis=0, keepdims=True))
     high = jnp.max(jnp.abs(image[...].astype(F32)))
-    sent[:, size : size + LANES] = jnp.full((1, LANES), high)
-    hit = to_column(pair[...]) == ids[...]
-    found = jnp.sum(jnp.where(hit, tile, 0.0), axis=0, keepdims=True)
-    sent[:, size + LANES :] = jnp.full((1, LANES), jnp.sum(found))
-
-
-def pair_body(crossed, mine, seen, out):
-    size = mine.shape[1] - 2 * LANES
-    half = size // 2
-    other = seen[:, :size]
+    col_sent[:, size : size + LANES] = jnp.full((1, LANES), high)
+    col_sent[:, size + LANES :] = jnp.full((1, LANES), jnp.sum(found))
+
+
+def labels(mine, seen, n_z, rows):
+    half = n_z * rows
+    first = lax.axis_index("xl") == 0
+    mine, seen = mine[...].astype(F32), seen[...].astype(F32)
+    pair = jnp.concatenate([jnp.where(first, mine, seen), jnp.where(first, seen, mine)], axis=1)
+    n_xl, n_c, n_xh = (lax.axis_size(a) for a in ("xl", "c", "xh"))
+    block = (lax.axis_index("y") * n_xh + lax.axis_index("xh")) * n_xl + lax.axis_index("xl")
+    core = lax.axis_index("c")
+    slot = lax.broadcasted_iota(jnp.int32, (1, 2 * half), 1)
+    own = slot < half
+    within = jnp.where(own, slot, slot - half)
+    holder = jnp.floor((within.astype(F32) + 0.5) * (1.0 / rows)).astype(jnp.int32)
+    ids = ((block * n_z + holder) * n_c + jnp.where(own, core, 1 - core)) * rows
+    return pair, (ids + within - holder * rows).astype(F32)
+
+
+def pair_body(crossed, count, mine, seen, out):
+    half = count // 2
+    other = seen[:, :count]
     if crossed:
-        other = jnp.concatenate([seen[:, half:size], seen[:, :half]], axis=1)
-    out[:, :size] = merge([mine[:, :size], other])
-    at = slice(size, size + LANES)
+        other = jnp.concatenate([seen[:, half:count], seen[:, :half]], axis=1)
+    out[:, :count] = merge([mine[:, :count], other])
+    at = slice(count, count + LANES)
     out[:, at] = jnp.maximum(mine[:, at], seen[:, at])
-    at = slice(size + LANES, size + 2 * LANES)
-    out[:, at] = mine[:, at] + seen[:, at]
-
-
-def image_body(inv_root, cols, scores, text, row_got, pair, ids, grads, sent, terms):
+    if mine.shape[1] > count + LANES:
+        at = slice(count + LANES, count + 2 * LANES)
+        out[:, at] = mine[:, at] + seen[:, at]
+
+
+def image_body(
+    n_z, inv_root, cols, rows_lse, scores, text, pair_mine, pair_seen, grads, sent, terms
+):
     size = scores.shape[0]
     n_plane = sent.shape[0]
     rows = size // n_plane
     col_lse = cols[:, :size]
     image_max = cols[:, size : size + LANES]
     found = cols[:, size + LANES :]
-    row_lse = merge([row_got[i : i + 1, :size] for i in range(n_plane)])
-    text_max = jnp.max(row_got[:, size:], axis=0, keepdims=True)
+    pair, ids = labels(pair_mine, pair_seen, n_z, rows)
+    row_lse = rows_lse[:, :size]
+    text_max = rows_lse[:, size:]
     row_terms = jnp.broadcast_to(jnp.sum(row_lse, axis=1, keepdims=True), (1, LANES))
     col_terms = jnp.sum(col_lse, axis=1, keepdims=True) - 2.0 * found
     terms[...] = jnp.concatenate(
@@ -151,7 +170,7 @@
         probs = 0.5 * (
             jnp.exp(tile - to_column(row_lse[:, r : r + step])) + jnp.exp(tile - col_lse)
         )
-        hit = to_column(pair[:, r : r + step]) == ids[...]
+        hit = to_column(pair[:, r : r + step]) == ids
         grad = (probs - jnp.where(hit, 1.0, 0.0)).astype(BF16)
         grads[r : r + step, :] = grad
         part = encode(jnp.dot(grad, text[...], preferred_element_type=F32) * scale)
@@ -178,20 +197,21 @@
         )
 
 
-def send_body(n_z, own, seen, terms, terms_seen, keep, total, *pays):
+def send_body(order, own, seen, terms, terms_seen, keep, total, *pays):
     rows = keep.shape[0]
     z = lax.axis_index("z")
     row_terms = terms[0:1, :] + terms_seen[0:1, :]
     total[...] = row_terms
     extra = split3(row_terms)
     scale = inverse(terms[2:3, :1])
-    for q in range(n_z):
+    n_z = len(order) + 1
+    for i, q in enumerate([0, *order]):
         at = pl.ds(pl.multiple_of(lax.rem(z + q, n_z) * rows, 16), rows)
         block = own[at, :] + seen[at, :]
         if q == 0:
             keep[...] = block
             continue
-        pay = pays[q - 1]
+        pay = pays[i - 1]
         part = encode(block * scale)
         count = block.shape[1] // LANES
         for k in range(count):
@@ -236,64 +256,52 @@
     half = n_z * rows
     pairs = size * n_z * n_c
     inv_root = width ** (-0.5)
-    core = lax.axis_index("c")
     shape = jax.ShapeDtypeStruct
     tall = width // LANES * rows + EXTRA
 
-    block = (lax.axis_index("y") * n_xh + lax.axis_index("xh")) * n_xl + lax.axis_index("xl")
-    slot = lax.broadcasted_iota(jnp.int32, (1, size), 1)
-    own = slot < half
-    within = jnp.where(own, slot, slot - half)
-    ids = ((block * n_z + within // rows) * n_c + jnp.where(own, core, 1 - core)) * rows
-    ids = (ids + within % rows).astype(F32)
-
-    image = lax.all_to_all(
-        jnp.broadcast_to(image_embed[None], (n_plane, rows, width)), PLANE, 0, 0
-    ).reshape(size, width)
-    image, pair_index = lax.optimization_barrier((image, pair_index))
-    pair_other = lax.ppermute(pair_index, "xl", SWAP)
-    first = lax.axis_index("xl") == 0
-    pair = jnp.concatenate(
-        [jnp.where(first, pair_index, pair_other), jnp.where(first, pair_other, pair_index)]
-    )
-    pair = pair.astype(F32)[None, :]
-    pieces = [text_embed] + [turn(text_embed, "z", -q) for q in range(1, n_z)]
+    pair_mine = pair_index[None, :]
+    pair_seen = lax.ppermute(pair_mine, "xl", SWAP)
+    copies = jnp.broadcast_to(image_embed[None], (n_plane, rows, width))
+    copies, pair_seen = lax.optimization_barrier((copies, pair_seen))
+    image = lax.all_to_all(copies, PLANE, 0, 0).reshape(size, width)
+
+    order = sorted(range(1, n_z), key=lambda q: (abs(q - n_z // 2), q))
+    pieces = [text_embed] + [turn(text_embed, "z", -q) for q in order[::-1]]
     pieces = pieces + [lax.ppermute(piece, "c", SWAP) for piece in pieces]
 
     flops = 2 * size * size * width
-    scores, text, row_sent = call(
-        functools.partial(score_body, n_z, inv_root),
+    scores, text, row_part, col_part = call(
+        functools.partial(score_body, order, inv_root),
         (
             shape((size, size), F32),
             shape((size, width), BF16),
-            shape((n_plane, 1, size + LANES), F32),
+            shape((1, size + LANES), F32),
+            shape((1, size + 2 * LANES), F32),
         ),
-        (*pieces, image),
+        (*pieces, image, pair_mine, pair_seen),
         "scores",
         flops,
-        size * size,
-    )
-    row_got = lax.all_to_all(row_sent, PLANE, 0, 0).reshape(n_plane, size + LANES)
-    cols_shape = (shape((1, size + 2 * LANES), F32),)
-    (cols,) = call(
-        column_body, cols_shape, (scores, image, pair, ids), "columns", 0, size * size
-    )
-    seen = lax.ppermute(cols, "c", SWAP)
-    (cols,) = call(functools.partial(pair_body, True), cols_shape, (cols, seen), "pair")
-    step = 1
-    while step < n_z:
-        seen = lax.ppermute(cols, "z", [(i, i ^ step) for i in range(n_z)])
-        (cols,) = call(functools.partial(pair_body, False), cols_shape, (cols, seen), "pair")
-        step *= 2
+        2 * size * size,
+    )
+    def exchange(part, axis, step):
+        count = lax.axis_size(axis)
+        seen = lax.ppermute(part, axis, [(i, i ^ step) for i in range(count)])
+        merge_body = functools.partial(pair_body, axis == "c", size)
+        return call(merge_body, (shape(part.shape, F32),), (part, seen), "pair")[0]
+
+    for axis, step in (("c", 1), ("z", 1), ("z", 2), ("z", 4)):
+        col_part = exchange(col_part, axis, step)
+    for axis, step in (("xl", 1), ("xh", 1), ("y", 1), ("y", 2)):
+        row_part = exchange(row_part, axis, step)
 
     grads, image_sent, terms = call(
-        functools.partial(image_body, inv_root),
+        functools.partial(image_body, n_z, inv_root),
         (
             shape((size, size), BF16),
             shape((n_plane, tall, LANES), BF16),
             shape((8, LANES), F32),
         ),
-        (cols, scores, text, row_got, pair, ids),
+        (col_part, row_part, scores, text, pair_mine, pair_seen),
         "image_grad",
         flops,
         2 * size * size,
@@ -307,14 +315,14 @@
         size=1,
     )
     keep, total, *pays = call(
-        functools.partial(send_body, n_z),
+        functools.partial(send_body, order),
         (shape((rows, width), F32), shape((1, LANES), F32))
         + (shape((tall, LANES), BF16),) * (n_z - 1),
         (text_own, lax.ppermute(text_other, "c", SWAP), terms, lax.ppermute(terms, "c", SWAP)),
         "send",
         size=1,
     )
-    pays = [turn(pay, "z", q + 1) for q, pay in enumerate(pays)]
+    pays = [turn(pay, "z", q) for q, pay in zip(order, pays)]
     grad_text, side = call(
         text_sum_body,
         (shape((rows, width), F32), shape((1, LANES), F32)),

time: 123 us -> 108 us (0.88)
  waiting for transfers between devices: 25.6 us -> 17.8 us
  local copies, waits for them, and re-layouts: 8.18 us -> 2.95 us
  starting transfers between devices: 73.9 us -> 72.4 us
    ppermute x5 -> x9, starting transfers between devices: 8.77 us -> 17 us  [the longest x8 15 us: exchange(): seen = lax.ppermute(part, axis, [(i, i ^ step) for i in range(count)])]
    all_to_all x2 -> x1, starting transfers between devices: 13.9 us -> 7.14 us  [shards(): image = lax.all_to_all(copies, PLANE, 0, 0).reshape(size, width)]
    ppermute x8, starting transfers between devices: 12.1 us -> 5.45 us  [shards(): pieces = pieces + [lax.ppermute(piece, 'c', SWAP) for piece in pieces]]
    unnamed x15 -> x2, local copies, waits for them, and re-layouts: 5.9 us -> 0.01 us
    ppermute x5 -> x9, waiting for transfers between devices: 8.17 us -> 3.23 us  [the longest x8 2.26 us: exchange(): seen = lax.ppermute(part, axis, [(i, i ^ step) for i in range(count)])]
    ppermute x14, starting transfers between devices: 28.6 us -> 32.7 us  [turn(): lax.ppermute(x, axis, [(i, (i + step) % count) for i in range(count)])]
    ppermute x14, waiting for transfers between devices: 16.5 us -> 12.7 us  [turn(): lax.ppermute(x, axis, [(i, (i + step) % count) for i in range(count)])]
    all_to_all x1, starting transfers between devices: 6.93 us -> 5.3 us  [shards(): image_got = lax.all_to_all(image_sent, PLANE, 0, 0)]
  transfers between devices with their start and end apart: 32 -> 35, of which waited for: 11 -> 13; matrix products, arithmetic and copies ran while one was open for 0% -> 0% of each run, Pallas kernels for 4% -> 1%
where the time goes in v5:
time: 108 us
  starting transfers between devices  72.4 us (67%)
  waiting for transfers between devices  17.8 us (16%)
  Pallas kernels  13.4 us (12%)
  local copies, waits for them, and re-layouts  2.95 us (3%)
    ppermute x14, starting transfers between devices, turn(): lax.ppermute(x, axis, [(i, (i + step) % count) for i in range(count)])  32.7 us
    ppermute x8, starting transfers between devices, exchange(): seen = lax.ppermute(part, axis, [(i, i ^ step) for i in range(count)])  15 us
    pallas_call x14, Pallas kernels, call(): pl.pallas_call(body, out_shape=outs, in_specs=[pl.BlockSpec(memory_space=...  13.4 us
    ppermute x14, waiting for transfers between devices, turn(): lax.ppermute(x, axis, [(i, (i + step) % count) for i in range(count)])  12.7 us
    all_to_all x1, starting transfers between devices, shards(): image = lax.all_to_all(copies, PLANE, 0, 0).reshape(size, width)  7.14 us
    ppermute x8, starting transfers between devices, shards(): pieces = pieces + [lax.ppermute(piece, 'c', SWAP) for piece in pieces]  5.45 us
    all_to_all x1, starting transfers between devices, shards(): image_got = lax.all_to_all(image_sent, PLANE, 0, 0)  5.3 us
    ppermute x1, starting transfers between devices, shards(): lax.ppermute(text_other, 'c', SWAP)  4.24 us
  transfers between devices with their start and end apart: 35, of which 13 were waited for; matrix products, arithmetic and copies ran while one was open for 0% of the time, Pallas kernels for 1%

profile of v5, /device:TPU:1, one launch (start us, length us, event | category | flops | bytes accessed | tf_op | source)
XLA Modules:
  0.0 107.5 jit_solution(14976313068080833274)
XLA Ops:
  0.6 0.7 broadcast_in_dim.10.refs_17_.pair_mine
  1.3 2.0 %collective-permute-start.15 = (s32[1,384]{1,0:T(1,128)S(1)}, s32[1,384]{1,0:T(1,128)S(1)}, u32[]{:S(2)}, u32[]{:S(2)}) collective-permute-start(s32[1,384]{1,0:T(1,128)S(1)} %broadcast_in_dim.10.refs_17_.pair_mine), channel_id=1, source_target_pairs={{0,128},{128,0},{1,129},{129,1},{2,130},{130,2},{3,131},{131,3},{4... | collective-permute-start | bytes 4616 | tf_op jit(solution)/shard_map/ppermute | solution.py:263
  3.4 1.0 collective-permute-done.15.refs_18_.pair_seen
  4.3 2.3 %broadcast_in_dim.4 = bf16[16,48,1024]{2,1,0:T(8,128)(2,1)} broadcast(bf16[48,1024]{1,0:T(8,128)(2,1)} %param.3), dimensions={1,2} | broadcast | bytes 1671168 | tf_op jit(solution)/shard_map/broadcast_in_dim | solution.py:264
  6.6 7.1 %all-to-all-start = ((bf16[16,48,1024]{2,1,0:T(8,128)(2,1)}), bf16[16,48,1024]{2,1,0:T(8,128)(2,1)S(1)}, u32[]{:S(2)}, u32[]{:S(2)}) async-start(bf16[16,48,1024]{2,1,0:T(8,128)(2,1)} %broadcast_in_dim.4), calls=%async_computation | async-start | bytes 3145728 | tf_op jit(solution)/shard_map/all_to_all | solution.py:266
  13.7 7.0 %collective-permute-start.6 = (bf16[48,1024]{1,0:T(8,128)(2,1)S(1)}, bf16[48,1024]{1,0:T(8,128)(2,1)S(1)}, u32[]{:S(2)}, u32[]{:S(2)}) collective-permute-start(bf16[48,1024]{1,0:T(8,128)(2,1)S(1)} %copy-done), channel_id=1, source_target_pairs={{0,64},{16,80},{32,96},{48,112},{64,0},{80,16},{96,32},{112,48},{1... | collective-permute-start | bytes 294920 | tf_op jit(solution)/shard_map/ppermute | solution.py:20
  20.7 3.3 %collective-permute-start.4 = (bf16[48,1024]{1,0:T(8,128)(2,1)S(1)}, bf16[48,1024]{1,0:T(8,128)(2,1)S(1)}, u32[]{:S(2)}, u32[]{:S(2)}) collective-permute-start(bf16[48,1024]{1,0:T(8,128)(2,1)S(1)} %copy-done), channel_id=1, source_target_pairs={{0,48},{16,64},{32,80},{48,96},{64,112},{80,0},{96,16},{112,32},{1... | collective-permute-start | bytes 294920 | tf_op jit(solution)/shard_map/ppermute | solution.py:20
  24.0 0.8 collective-permute-start.3
  24.8 1.6 %collective-permute-start.2 = (bf16[48,1024]{1,0:T(8,128)(2,1)S(1)}, bf16[48,1024]{1,0:T(8,128)(2,1)S(1)}, u32[]{:S(2)}, u32[]{:S(2)}) collective-permute-start(bf16[48,1024]{1,0:T(8,128)(2,1)S(1)} %copy-done), channel_id=1, source_target_pairs={{0,32},{16,48},{32,64},{48,80},{64,96},{80,112},{96,0},{112,16},{1... | collective-permute-start | bytes 294920 | tf_op jit(solution)/shard_map/ppermute | solution.py:20
  26.4 2.2 %collective-permute-start.1 = (bf16[48,1024]{1,0:T(8,128)(2,1)S(1)}, bf16[48,1024]{1,0:T(8,128)(2,1)S(1)}, u32[]{:S(2)}, u32[]{:S(2)}) collective-permute-start(bf16[48,1024]{1,0:T(8,128)(2,1)S(1)} %copy-done), channel_id=1, source_target_pairs={{0,112},{16,0},{32,16},{48,32},{64,48},{80,64},{96,80},{112,96},{1... | collective-permute-start | bytes 294920 | tf_op jit(solution)/shard_map/ppermute | solution.py:20
  28.6 7.2 %collective-permute-start = (bf16[48,1024]{1,0:T(8,128)(2,1)S(1)}, bf16[48,1024]{1,0:T(8,128)(2,1)S(1)}, u32[]{:S(2)}, u32[]{:S(2)}) collective-permute-start(bf16[48,1024]{1,0:T(8,128)(2,1)S(1)} %copy-done), channel_id=1, source_target_pairs={{0,16},{16,32},{32,48},{48,64},{64,80},{80,96},{96,112},{112,0},{1... | collective-permute-start | bytes 294920 | tf_op jit(solution)/shard_map/ppermute | solution.py:20
  35.8 1.4 %collective-permute-start.7 = (bf16[48,1024]{1,0:T(8,128)(2,1)S(1)}, bf16[48,1024]{1,0:T(8,128)(2,1)S(1)}, u32[]{:S(2)}, u32[]{:S(2)}) collective-permute-start(bf16[48,1024]{1,0:T(8,128)(2,1)S(1)} %copy-done), channel_id=1, source_target_pairs={{0,8},{8,0},{1,9},{9,1},{2,10},{10,2},{3,11},{11,3},{4,12},{12,4},... | collective-permute-start | bytes 294920 | tf_op jit(solution)/shard_map/ppermute | solution.py:270
  37.3 1.0 collective-permute-start.14
  38.3 1.7 %collective-permute-start.12 = (bf16[48,1024]{1,0:T(8,128)(2,1)S(1)}, bf16[48,1024]{1,0:T(8,128)(2,1)S(1)}, u32[]{:S(2)}, u32[]{:S(2)}) collective-permute-start(bf16[48,1024]{1,0:T(8,128)(2,1)S(1)} %collective-permute-done.4.refs_5_), channel_id=1, source_target_pairs={{0,8},{8,0},{1,9},{9,1},{2,10},{10,2},{3,11},{11,3},{4,12},{12,4},... | collective-permute-start | bytes 294920 | tf_op jit(solution)/shard_map/ppermute | solution.py:270
  40.0 0.5 collective-permute-start.11
  40.5 0.5 collective-permute-start.9
  41.1 0.3 collective-permute-start.8
  41.5 0.4 collective-permute-done.10.refs_11_
  42.0 0.4 collective-permute-done.8.refs_9_
  42.4 3.1 %scores.1 = (f32[768,768]{1,0:T(8,128)S(1)}, bf16[768,1024]{1,0:T(8,128)(2,1)S(1)}, f32[1,896]{1,0:T(1,128)S(1)}, f32[1,1024]{1,0:T(1,128)S(1)}) custom-call(bf16[48,1024]{1,0:T(8,128)(2,1)S(1)} %copy-done, bf16[48,1024]{1,0:T(8,128)(2,1)S(1)} %collective-permute-done.refs_1_, bf16[48,1024]{1,0:T(8,128)(2,1)S(1)} %collective-permute-done.1.refs_2_, ...), custom_call_target="tpu_custom_call" | custom-call | flops 1207959552 | bytes 7088640 | tf_op jit(solution)/shard_map/scores/pallas_call | solution.py:65
  45.4 0.4 collective-permute-start.16
  45.8 1.6 %collective-permute-start.20 = (f32[1,896]{1,0:T(1,128)S(1)}, f32[1,896]{1,0:T(1,128)S(1)}, u32[]{:S(2)}, u32[]{:S(2)}) collective-permute-start(f32[1,896]{1,0:T(1,128)S(1)} %get-tuple-element.30.mine), channel_id=1, source_target_pairs={{0,128},{128,0},{1,129},{129,1},{2,130},{130,2},{3,131},{131,3},{4... | collective-permute-start | bytes 10760 | tf_op jit(solution)/shard_map/ppermute | solution.py:288
  47.4 0.9 collective-permute-start.17
  48.4 3.1 %collective-permute-start.21 = (f32[1,896]{1,0:T(1,128)S(1)}, f32[1,896]{1,0:T(1,128)S(1)}, u32[]{:S(2)}, u32[]{:S(2)}) collective-permute-start(f32[1,896]{1,0:T(1,128)S(1)} %pair.12.mine), channel_id=1, source_target_pairs={{0,1},{1,0},{2,3},{3,2},{4,5},{5,4},{6,7},{7,6},{8,9},{9,8},{10,11... | collective-permute-start | bytes 10760 | tf_op jit(solution)/shard_map/ppermute | solution.py:288
  51.5 1.2 %collective-permute-start.18 = (f32[1,1024]{1,0:T(1,128)S(1)}, f32[1,1024]{1,0:T(1,128)S(1)}, u32[]{:S(2)}, u32[]{:S(2)}) collective-permute-start(f32[1,1024]{1,0:T(1,128)S(1)} %pair.9.mine), channel_id=1, source_target_pairs={{0,32},{16,48},{32,0},{48,16},{64,96},{80,112},{96,64},{112,80},{1... | collective-permute-start | bytes 12296 | tf_op jit(solution)/shard_map/ppermute | solution.py:288
  52.7 1.3 %collective-permute-start.22 = (f32[1,896]{1,0:T(1,128)S(1)}, f32[1,896]{1,0:T(1,128)S(1)}, u32[]{:S(2)}, u32[]{:S(2)}) collective-permute-start(f32[1,896]{1,0:T(1,128)S(1)} %pair.13.mine), channel_id=1, source_target_pairs={{0,2},{2,0},{4,6},{6,4},{1,3},{3,1},{5,7},{7,5},{8,10},{10,8},{12,... | collective-permute-start | bytes 10760 | tf_op jit(solution)/shard_map/ppermute | solution.py:288
  54.0 0.9 collective-permute-done.18.seen
  54.9 3.7 %collective-permute-start.19 = (f32[1,1024]{1,0:T(1,128)S(1)}, f32[1,1024]{1,0:T(1,128)S(1)}, u32[]{:S(2)}, u32[]{:S(2)}) collective-permute-start(f32[1,1024]{1,0:T(1,128)S(1)} %pair.10.mine), channel_id=1, source_target_pairs={{0,64},{16,80},{32,96},{48,112},{64,0},{80,16},{96,32},{112,48},{1... | collective-permute-start | bytes 12296 | tf_op jit(solution)/shard_map/ppermute | solution.py:288
  58.7 2.8 %collective-permute-start.23 = (f32[1,896]{1,0:T(1,128)S(1)}, f32[1,896]{1,0:T(1,128)S(1)}, u32[]{:S(2)}, u32[]{:S(2)}) collective-permute-start(f32[1,896]{1,0:T(1,128)S(1)} %pair.14.mine), channel_id=1, source_target_pairs={{0,4},{2,6},{4,0},{6,2},{1,5},{3,7},{5,1},{7,3},{8,12},{10,14},{12... | collective-permute-start | bytes 10760 | tf_op jit(solution)/shard_map/ppermute | solution.py:288
  61.5 1.3 %collective-permute-done.23.seen = f32[1,896]{1,0:T(1,128)S(1)} collective-permute-done((f32[1,896]{1,0:T(1,128)S(1)}, f32[1,896]{1,0:T(1,128)S(1)}, u32[]{:S(2)}, u32[]{:S(2)}) %collective-permute-start.23) | collective-permute-done | bytes 3616 | tf_op jit(solution)/shard_map/ppermute | solution.py:288
  62.8 3.6 %image_grad.1 = (bf16[768,768]{1,0:T(8,128)(2,1)S(1)}, bf16[16,400,128]{2,1,0:T(8,128)(2,1)}, f32[8,128]{1,0:T(8,128)S(1)}) custom-call(f32[1,1024]{1,0:T(1,128)S(1)} %pair.11.cols, f32[1,896]{1,0:T(1,128)S(1)} %pair.15.rows_lse, f32[768,768]{1,0:T(8,128)S(1)} %get-tuple-element.31.scores, bf16[768,1024]{1,0:T(8,128)(2,1)S(1)} %get-tuple-element.32.text, ...), custom_call_target="tpu_custom_call" | custom-call | flops 1207959552 | bytes 6765056 | tf_op jit(solution)/shard_map/image_grad/pallas_call | solution.py:65
  66.3 2.0 %text_grad.1 = (f32[384,1024]{1,0:T(8,128)S(1)}, f32[384,1024]{1,0:T(8,128)}) custom-call(bf16[768,768]{1,0:T(8,128)(2,1)S(1)} %get-tuple-element.35.grads, bf16[768,1024]{1,0:T(8,128)(2,1)S(1)} %bitcast.3), custom_call_target="tpu_custom_call" | custom-call | bytes 1 | tf_op jit(solution)/shard_map/text_grad/pallas_call | solution.py:65
  68.3 4.2 %collective-permute-start.24 = (f32[384,1024]{1,0:T(8,128)}, f32[384,1024]{1,0:T(8,128)}, u32[]{:S(2)}, u32[]{:S(2)}) collective-permute-start(f32[384,1024]{1,0:T(8,128)} %get-tuple-element.37), channel_id=1, source_target_pairs={{0,8},{8,0},{1,9},{9,1},{2,10},{10,2},{3,11},{11,3},{4,12},{12,4},... | collective-permute-start | bytes 4718600 | tf_op jit(solution)/shard_map/ppermute | solution.py:321
  72.6 5.3 %all-to-all-start.1 = ((bf16[16,400,128]{2,1,0:T(8,128)(2,1)}), bf16[16,400,128]{2,1,0:T(8,128)(2,1)S(1)}, u32[]{:S(2)}, u32[]{:S(2)}) async-start(bf16[16,400,128]{2,1,0:T(8,128)(2,1)} %get-tuple-element.33), calls=%async_computation.1 | async-start | bytes 3276800 | tf_op jit(solution)/shard_map/all_to_all | solution.py:309
  77.9 0.6 collective-permute-start.25
  78.5 0.9 collective-permute-done.25.terms_seen
  79.4 1.9 %send.1 = (f32[48,1024]{1,0:T(8,128)S(1)}, f32[1,128]{1,0:T(1,128)S(1)}, bf16[400,128]{1,0:T(8,128)(2,1)S(1)}, bf16[400,128]{1,0:T(8,128)(2,1)S(1)}, bf16[400,12...) custom-call(f32[384,1024]{1,0:T(8,128)S(1)} %get-tuple-element.36.ow, ...), custom_call_target="tpu_custom_call" | custom-call | bytes 1 | tf_op jit(solution)/shard_map/send/pallas_call | solution.py:65
  81.3 2.1 %collective-permute-start.26 = (bf16[400,128]{1,0:T(8,128)(2,1)S(1)}, bf16[400,128]{1,0:T(8,128)(2,1)S(1)}, u32[]{:S(2)}, u32[]{:S(2)}) collective-permute-start(bf16[400,128]{1,0:T(8,128)(2,1)S(1)} %get-tuple-element.40), channel_id=1, source_target_pairs={{0,64},{16,80},{32,96},{48,112},{64,0},{80,16},{96,32},{112,48},{1... | collective-permute-start | bytes 307208 | tf_op jit(solution)/shard_map/ppermute | solution.py:20
  83.4 1.7 %collective-permute-start.27 = (bf16[400,128]{1,0:T(8,128)(2,1)S(1)}, bf16[400,128]{1,0:T(8,128)(2,1)S(1)}, u32[]{:S(2)}, u32[]{:S(2)}) collective-permute-start(bf16[400,128]{1,0:T(8,128)(2,1)S(1)} %get-tuple-element.41), channel_id=1, source_target_pairs={{0,48},{16,64},{32,80},{48,96},{64,112},{80,0},{96,16},{112,32},{1... | collective-permute-start | bytes 307208 | tf_op jit(solution)/shard_map/ppermute | solution.py:20
  85.1 2.7 %collective-permute-start.28 = (bf16[400,128]{1,0:T(8,128)(2,1)S(1)}, bf16[400,128]{1,0:T(8,128)(2,1)S(1)}, u32[]{:S(2)}, u32[]{:S(2)}) collective-permute-start(bf16[400,128]{1,0:T(8,128)(2,1)S(1)} %get-tuple-element.42), channel_id=1, source_target_pairs={{0,80},{16,96},{32,112},{48,0},{64,16},{80,32},{96,48},{112,64},{1... | collective-permute-start | bytes 307208 | tf_op jit(solution)/shard_map/ppermute | solution.py:20
  87.8 1.2 %collective-permute-start.29 = (bf16[400,128]{1,0:T(8,128)(2,1)S(1)}, bf16[400,128]{1,0:T(8,128)(2,1)S(1)}, u32[]{:S(2)}, u32[]{:S(2)}) collective-permute-start(bf16[400,128]{1,0:T(8,128)(2,1)S(1)} %get-tuple-element.43), channel_id=1, source_target_pairs={{0,32},{16,48},{32,64},{48,80},{64,96},{80,112},{96,0},{112,16},{1... | collective-permute-start | bytes 307208 | tf_op jit(solution)/shard_map/ppermute | solution.py:20
  89.1 2.3 %collective-permute-start.30 = (bf16[400,128]{1,0:T(8,128)(2,1)S(1)}, bf16[400,128]{1,0:T(8,128)(2,1)S(1)}, u32[]{:S(2)}, u32[]{:S(2)}) collective-permute-start(bf16[400,128]{1,0:T(8,128)(2,1)S(1)} %get-tuple-element.44), channel_id=1, source_target_pairs={{0,96},{16,112},{32,0},{48,16},{64,32},{80,48},{96,64},{112,80},{1... | collective-permute-start | bytes 307208 | tf_op jit(solution)/shard_map/ppermute | solution.py:20
  91.4 0.5 collective-permute-start.31
  91.9 7.4 %collective-permute-done.27.refs_1_ = bf16[400,128]{1,0:T(8,128)(2,1)S(1)} collective-permute-done((bf16[400,128]{1,0:T(8,128)(2,1)S(1)}, bf16[400,128]{1,0:T(8,128)(2,1)S(1)}, u32[]{:S(2)}, u32[]{:S(2)}) %collective-permute-start.27) | collective-permute-done | bytes 102432 | tf_op jit(solution)/shard_map/ppermute | solution.py:20
  99.6 2.3 %collective-permute-done.30.refs_4_ = bf16[400,128]{1,0:T(8,128)(2,1)S(1)} collective-permute-done((bf16[400,128]{1,0:T(8,128)(2,1)S(1)}, bf16[400,128]{1,0:T(8,128)(2,1)S(1)}, u32[]{:S(2)}, u32[]{:S(2)}) %collective-permute-start.30) | collective-permute-done | bytes 102432 | tf_op jit(solution)/shard_map/ppermute | solution.py:20
  101.9 2.6 %collective-permute-done.31.refs_5_ = bf16[400,128]{1,0:T(8,128)(2,1)S(1)} collective-permute-done((bf16[400,128]{1,0:T(8,128)(2,1)S(1)}, bf16[400,128]{1,0:T(8,128)(2,1)S(1)}, u32[]{:S(2)}, u32[]{:S(2)}) %collective-permute-start.31) | collective-permute-done | bytes 102432 | tf_op jit(solution)/shard_map/ppermute | solution.py:20
  104.6 1.1 %text_sum.1 = (f32[48,1024]{1,0:T(8,128)}, f32[1,128]{1,0:T(1,128)S(1)}) custom-call(f32[48,1024]{1,0:T(8,128)S(1)} %get-tuple-element.38.keep, f32[1,128]{1,0:T(1,128)S(1)} %get-tuple-element.39.total, f32[8,128]{1,0:T(8,128)S(1)} %get-tuple-element.34.terms, bf16[400,128]{1,0:T(8,128)(2,1)S(1)} %collective-permute-done.26.refs_0_, ...), custom_call_target="tpu_custom_call" | custom-call | bytes 1115136 | tf_op jit(solution)/shard_map/text_sum/pallas_call | solution.py:65
  105.7 1.7 %image_sum.1 = (f32[48,1024]{1,0:T(8,128)}, f32[1,1]{1,0:T(1,128)}) custom-call(bf16[16,400,128]{2,1,0:T(8,128)(2,1)S(1)} %all-to-all-done.1.got, f32[8,128]{1,0:T(8,128)S(1)} %get-tuple-element.34.terms, f32[1,128]{1,0:T(1,128)S(1)} %get-tuple-element.47.side), custom_call_target="tpu_custom_call" | custom-call | bytes 1839620 | tf_op jit(solution)/shard_map/image_sum/pallas_call | solution.py:65
  (40 shorter events, 0.8 us)
Async XLA Ops:
  1.3 3.0 %collective-permute-start.15 = (s32[1,384]{1,0:T(1,128)S(1)}, s32[1,384]{1,0:T(1,128)S(1)}, u32[]{:S(2)}, u32[]{:S(2)}) collective-permute-start(s32[1,384]{1,0:T(1,128)S(1)} %broadcast_in_dim.10.refs_17_.pair_mine), channel_id=1, source_target_pairs={{0,128},{128,0},{1,129},{129,1},{2,130},{130,2},{3,131},{131,3},{4... | collective-permute-start | bytes 4616 | tf_op jit(solution)/shard_map/ppermute | solution.py:263
  6.6 7.2 %copy-start = (bf16[48,1024]{1,0:T(8,128)(2,1)S(1)}, bf16[48,1024]{1,0:T(8,128)(2,1)}, u32[]{:S(2)}) copy-start(bf16[48,1024]{1,0:T(8,128)(2,1)} %refs_0_.1) | copy-start | bytes 294916
  6.6 35.8 %all-to-all-start = ((bf16[16,48,1024]{2,1,0:T(8,128)(2,1)}), bf16[16,48,1024]{2,1,0:T(8,128)(2,1)S(1)}, u32[]{:S(2)}, u32[]{:S(2)}) async-start(bf16[16,48,1024]{2,1,0:T(8,128)(2,1)} %broadcast_in_dim.4), calls=%async_computation | async-start | bytes 3145728 | tf_op jit(solution)/shard_map/all_to_all | solution.py:266
  13.7 12.7 %collective-permute-start.6 = (bf16[48,1024]{1,0:T(8,128)(2,1)S(1)}, bf16[48,1024]{1,0:T(8,128)(2,1)S(1)}, u32[]{:S(2)}, u32[]{:S(2)}) collective-permute-start(bf16[48,1024]{1,0:T(8,128)(2,1)S(1)} %copy-done), channel_id=1, source_target_pairs={{0,64},{16,80},{32,96},{48,112},{64,0},{80,16},{96,32},{112,48},{1... | collective-permute-start | bytes 294920 | tf_op jit(solution)/shard_map/ppermute | solution.py:20
  20.7 7.9 %collective-permute-start.5 = (bf16[48,1024]{1,0:T(8,128)(2,1)S(1)}, bf16[48,1024]{1,0:T(8,128)(2,1)S(1)}, u32[]{:S(2)}, u32[]{:S(2)}) collective-permute-start(bf16[48,1024]{1,0:T(8,128)(2,1)S(1)} %copy-done), channel_id=1, source_target_pairs={{0,80},{16,96},{32,112},{48,0},{64,16},{80,32},{96,48},{112,64},{1... | collective-permute-start | bytes 294920 | tf_op jit(solution)/shard_map/ppermute | solution.py:20
  20.7 15.1 %collective-permute-start.4 = (bf16[48,1024]{1,0:T(8,128)(2,1)S(1)}, bf16[48,1024]{1,0:T(8,128)(2,1)S(1)}, u32[]{:S(2)}, u32[]{:S(2)}) collective-permute-start(bf16[48,1024]{1,0:T(8,128)(2,1)S(1)} %copy-done), channel_id=1, source_target_pairs={{0,48},{16,64},{32,80},{48,96},{64,112},{80,0},{96,16},{112,32},{1... | collective-permute-start | bytes 294920 | tf_op jit(solution)/shard_map/ppermute | solution.py:20
  24.0 13.3 %collective-permute-start.3 = (bf16[48,1024]{1,0:T(8,128)(2,1)S(1)}, bf16[48,1024]{1,0:T(8,128)(2,1)S(1)}, u32[]{:S(2)}, u32[]{:S(2)}) collective-permute-start(bf16[48,1024]{1,0:T(8,128)(2,1)S(1)} %copy-done), channel_id=1, source_target_pairs={{0,96},{16,112},{32,0},{48,16},{64,32},{80,48},{96,64},{112,80},{1... | collective-permute-start | bytes 294920 | tf_op jit(solution)/shard_map/ppermute | solution.py:20
  24.8 13.5 %collective-permute-start.2 = (bf16[48,1024]{1,0:T(8,128)(2,1)S(1)}, bf16[48,1024]{1,0:T(8,128)(2,1)S(1)}, u32[]{:S(2)}, u32[]{:S(2)}) collective-permute-start(bf16[48,1024]{1,0:T(8,128)(2,1)S(1)} %copy-done), channel_id=1, source_target_pairs={{0,32},{16,48},{32,64},{48,80},{64,96},{80,112},{96,0},{112,16},{1... | collective-permute-start | bytes 294920 | tf_op jit(solution)/shard_map/ppermute | solution.py:20
  26.4 11.9 %collective-permute-start.1 = (bf16[48,1024]{1,0:T(8,128)(2,1)S(1)}, bf16[48,1024]{1,0:T(8,128)(2,1)S(1)}, u32[]{:S(2)}, u32[]{:S(2)}) collective-permute-start(bf16[48,1024]{1,0:T(8,128)(2,1)S(1)} %copy-done), channel_id=1, source_target_pairs={{0,112},{16,0},{32,16},{48,32},{64,48},{80,64},{96,80},{112,96},{1... | collective-permute-start | bytes 294920 | tf_op jit(solution)/shard_map/ppermute | solution.py:20
  28.6 11.4 %collective-permute-start = (bf16[48,1024]{1,0:T(8,128)(2,1)S(1)}, bf16[48,1024]{1,0:T(8,128)(2,1)S(1)}, u32[]{:S(2)}, u32[]{:S(2)}) collective-permute-start(bf16[48,1024]{1,0:T(8,128)(2,1)S(1)} %copy-done), channel_id=1, source_target_pairs={{0,16},{16,32},{32,48},{48,64},{64,80},{80,96},{96,112},{112,0},{1... | collective-permute-start | bytes 294920 | tf_op jit(solution)/shard_map/ppermute | solution.py:20
  35.8 4.7 %collective-permute-start.7 = (bf16[48,1024]{1,0:T(8,128)(2,1)S(1)}, bf16[48,1024]{1,0:T(8,128)(2,1)S(1)}, u32[]{:S(2)}, u32[]{:S(2)}) collective-permute-start(bf16[48,1024]{1,0:T(8,128)(2,1)S(1)} %copy-done), channel_id=1, source_target_pairs={{0,8},{8,0},{1,9},{9,1},{2,10},{10,2},{3,11},{11,3},{4,12},{12,4},... | collective-permute-start | bytes 294920 | tf_op jit(solution)/shard_map/ppermute | solution.py:270
  37.3 3.2 %collective-permute-start.14 = (bf16[48,1024]{1,0:T(8,128)(2,1)S(1)}, bf16[48,1024]{1,0:T(8,128)(2,1)S(1)}, u32[]{:S(2)}, u32[]{:S(2)}) collective-permute-start(bf16[48,1024]{1,0:T(8,128)(2,1)S(1)} %collective-permute-done.6.refs_7_), channel_id=1, source_target_pairs={{0,8},{8,0},{1,9},{9,1},{2,10},{10,2},{3,11},{11,3},{4,12},{12,4},... | collective-permute-start | bytes 294920 | tf_op jit(solution)/shard_map/ppermute | solution.py:270
  38.3 2.8 %collective-permute-start.13 = (bf16[48,1024]{1,0:T(8,128)(2,1)S(1)}, bf16[48,1024]{1,0:T(8,128)(2,1)S(1)}, u32[]{:S(2)}, u32[]{:S(2)}) collective-permute-start(bf16[48,1024]{1,0:T(8,128)(2,1)S(1)} %collective-permute-done.5.refs_6_), channel_id=1, source_target_pairs={{0,8},{8,0},{1,9},{9,1},{2,10},{10,2},{3,11},{11,3},{4,12},{12,4},... | collective-permute-start | bytes 294920 | tf_op jit(solution)/shard_map/ppermute | solution.py:270
  38.3 3.0 %collective-permute-start.12 = (bf16[48,1024]{1,0:T(8,128)(2,1)S(1)}, bf16[48,1024]{1,0:T(8,128)(2,1)S(1)}, u32[]{:S(2)}, u32[]{:S(2)}) collective-permute-start(bf16[48,1024]{1,0:T(8,128)(2,1)S(1)} %collective-permute-done.4.refs_5_), channel_id=1, source_target_pairs={{0,8},{8,0},{1,9},{9,1},{2,10},{10,2},{3,11},{11,3},{4,12},{12,4},... | collective-permute-start | bytes 294920 | tf_op jit(solution)/shard_map/ppermute | solution.py:270
  40.0 1.5 %collective-permute-start.11 = (bf16[48,1024]{1,0:T(8,128)(2,1)S(1)}, bf16[48,1024]{1,0:T(8,128)(2,1)S(1)}, u32[]{:S(2)}, u32[]{:S(2)}) collective-permute-start(bf16[48,1024]{1,0:T(8,128)(2,1)S(1)} %collective-permute-done.3.refs_4_), channel_id=1, source_target_pairs={{0,8},{8,0},{1,9},{9,1},{2,10},{10,2},{3,11},{11,3},{4,12},{12,4},... | collective-permute-start | bytes 294920 | tf_op jit(solution)/shard_map/ppermute | solution.py:270
  40.5 1.3 %collective-permute-start.10 = (bf16[48,1024]{1,0:T(8,128)(2,1)S(1)}, bf16[48,1024]{1,0:T(8,128)(2,1)S(1)}, u32[]{:S(2)}, u32[]{:S(2)}) collective-permute-start(bf16[48,1024]{1,0:T(8,128)(2,1)S(1)} %collective-permute-done.2.refs_3_), channel_id=1, source_target_pairs={{0,8},{8,0},{1,9},{9,1},{2,10},{10,2},{3,11},{11,3},{4,12},{12,4},... | collective-permute-start | bytes 294920 | tf_op jit(solution)/shard_map/ppermute | solution.py:270
  40.5 1.5 %collective-permute-start.9 = (bf16[48,1024]{1,0:T(8,128)(2,1)S(1)}, bf16[48,1024]{1,0:T(8,128)(2,1)S(1)}, u32[]{:S(2)}, u32[]{:S(2)}) collective-permute-start(bf16[48,1024]{1,0:T(8,128)(2,1)S(1)} %collective-permute-done.1.refs_2_), channel_id=1, source_target_pairs={{0,8},{8,0},{1,9},{9,1},{2,10},{10,2},{3,11},{11,3},{4,12},{12,4},... | collective-permute-start | bytes 294920 | tf_op jit(solution)/shard_map/ppermute | solution.py:270
  41.1 1.3 %collective-permute-start.8 = (bf16[48,1024]{1,0:T(8,128)(2,1)S(1)}, bf16[48,1024]{1,0:T(8,128)(2,1)S(1)}, u32[]{:S(2)}, u32[]{:S(2)}) collective-permute-start(bf16[48,1024]{1,0:T(8,128)(2,1)S(1)} %collective-permute-done.refs_1_), channel_id=1, source_target_pairs={{0,8},{8,0},{1,9},{9,1},{2,10},{10,2},{3,11},{11,3},{4,12},{12,4},... | collective-permute-start | bytes 294920 | tf_op jit(solution)/shard_map/ppermute | solution.py:270
  45.4 2.0 %collective-permute-start.16 = (f32[1,1024]{1,0:T(1,128)S(1)}, f32[1,1024]{1,0:T(1,128)S(1)}, u32[]{:S(2)}, u32[]{:S(2)}) collective-permute-start(f32[1,1024]{1,0:T(1,128)S(1)} %get-tuple-element.29.mine), channel_id=1, source_target_pairs={{0,8},{8,0},{1,9},{9,1},{2,10},{10,2},{3,11},{11,3},{4,12},{12,4},... | collective-permute-start | bytes 12296 | tf_op jit(solution)/shard_map/ppermute | solution.py:288
  45.8 2.6 %collective-permute-start.20 = (f32[1,896]{1,0:T(1,128)S(1)}, f32[1,896]{1,0:T(1,128)S(1)}, u32[]{:S(2)}, u32[]{:S(2)}) collective-permute-start(f32[1,896]{1,0:T(1,128)S(1)} %get-tuple-element.30.mine), channel_id=1, source_target_pairs={{0,128},{128,0},{1,129},{129,1},{2,130},{130,2},{3,131},{131,3},{4... | collective-permute-start | bytes 10760 | tf_op jit(solution)/shard_map/ppermute | solution.py:288
  47.4 4.0 %collective-permute-start.17 = (f32[1,1024]{1,0:T(1,128)S(1)}, f32[1,1024]{1,0:T(1,128)S(1)}, u32[]{:S(2)}, u32[]{:S(2)}) collective-permute-start(f32[1,1024]{1,0:T(1,128)S(1)} %pair.8.mine), channel_id=1, source_target_pairs={{0,16},{16,0},{32,48},{48,32},{64,80},{80,64},{96,112},{112,96},{1... | collective-permute-start | bytes 12296 | tf_op jit(solution)/shard_map/ppermute | solution.py:288
  48.4 4.3 %collective-permute-start.21 = (f32[1,896]{1,0:T(1,128)S(1)}, f32[1,896]{1,0:T(1,128)S(1)}, u32[]{:S(2)}, u32[]{:S(2)}) collective-permute-start(f32[1,896]{1,0:T(1,128)S(1)} %pair.12.mine), channel_id=1, source_target_pairs={{0,1},{1,0},{2,3},{3,2},{4,5},{5,4},{6,7},{7,6},{8,9},{9,8},{10,11... | collective-permute-start | bytes 10760 | tf_op jit(solution)/shard_map/ppermute | solution.py:288
  51.5 3.4 %collective-permute-start.18 = (f32[1,1024]{1,0:T(1,128)S(1)}, f32[1,1024]{1,0:T(1,128)S(1)}, u32[]{:S(2)}, u32[]{:S(2)}) collective-permute-start(f32[1,1024]{1,0:T(1,128)S(1)} %pair.9.mine), channel_id=1, source_target_pairs={{0,32},{16,48},{32,0},{48,16},{64,96},{80,112},{96,64},{112,80},{1... | collective-permute-start | bytes 12296 | tf_op jit(solution)/shard_map/ppermute | solution.py:288
  52.7 6.0 %collective-permute-start.22 = (f32[1,896]{1,0:T(1,128)S(1)}, f32[1,896]{1,0:T(1,128)S(1)}, u32[]{:S(2)}, u32[]{:S(2)}) collective-permute-start(f32[1,896]{1,0:T(1,128)S(1)} %pair.13.mine), channel_id=1, source_target_pairs={{0,2},{2,0},{4,6},{6,4},{1,3},{3,1},{5,7},{7,5},{8,10},{10,8},{12,... | collective-permute-start | bytes 10760 | tf_op jit(solution)/shard_map/ppermute | solution.py:288
  54.9 7.8 %collective-permute-start.19 = (f32[1,1024]{1,0:T(1,128)S(1)}, f32[1,1024]{1,0:T(1,128)S(1)}, u32[]{:S(2)}, u32[]{:S(2)}) collective-permute-start(f32[1,1024]{1,0:T(1,128)S(1)} %pair.10.mine), channel_id=1, source_target_pairs={{0,64},{16,80},{32,96},{48,112},{64,0},{80,16},{96,32},{112,48},{1... | collective-permute-start | bytes 12296 | tf_op jit(solution)/shard_map/ppermute | solution.py:288
  58.7 4.0 %collective-permute-start.23 = (f32[1,896]{1,0:T(1,128)S(1)}, f32[1,896]{1,0:T(1,128)S(1)}, u32[]{:S(2)}, u32[]{:S(2)}) collective-permute-start(f32[1,896]{1,0:T(1,128)S(1)} %pair.14.mine), channel_id=1, source_target_pairs={{0,4},{2,6},{4,0},{6,2},{1,5},{3,7},{5,1},{7,3},{8,12},{10,14},{12... | collective-permute-start | bytes 10760 | tf_op jit(solution)/shard_map/ppermute | solution.py:288
  68.3 11.0 %collective-permute-start.24 = (f32[384,1024]{1,0:T(8,128)}, f32[384,1024]{1,0:T(8,128)}, u32[]{:S(2)}, u32[]{:S(2)}) collective-permute-start(f32[384,1024]{1,0:T(8,128)} %get-tuple-element.37), channel_id=1, source_target_pairs={{0,8},{8,0},{1,9},{9,1},{2,10},{10,2},{3,11},{11,3},{4,12},{12,4},... | collective-permute-start | bytes 4718600 | tf_op jit(solution)/shard_map/ppermute | solution.py:321
  72.6 33.1 %all-to-all-start.1 = ((bf16[16,400,128]{2,1,0:T(8,128)(2,1)}), bf16[16,400,128]{2,1,0:T(8,128)(2,1)S(1)}, u32[]{:S(2)}, u32[]{:S(2)}) async-start(bf16[16,400,128]{2,1,0:T(8,128)(2,1)} %get-tuple-element.33), calls=%async_computation.1 | async-start | bytes 3276800 | tf_op jit(solution)/shard_map/all_to_all | solution.py:309
  77.9 1.5 %collective-permute-start.25 = (f32[8,128]{1,0:T(8,128)S(1)}, f32[8,128]{1,0:T(8,128)S(1)}, u32[]{:S(2)}, u32[]{:S(2)}) collective-permute-start(f32[8,128]{1,0:T(8,128)S(1)} %get-tuple-element.34.terms), channel_id=1, source_target_pairs={{0,8},{8,0},{1,9},{9,1},{2,10},{10,2},{3,11},{11,3},{4,12},{12,4},... | collective-permute-start | bytes 12296 | tf_op jit(solution)/shard_map/ppermute | solution.py:321
  81.3 10.2 %collective-permute-start.26 = (bf16[400,128]{1,0:T(8,128)(2,1)S(1)}, bf16[400,128]{1,0:T(8,128)(2,1)S(1)}, u32[]{:S(2)}, u32[]{:S(2)}) collective-permute-start(bf16[400,128]{1,0:T(8,128)(2,1)S(1)} %get-tuple-element.40), channel_id=1, source_target_pairs={{0,64},{16,80},{32,96},{48,112},{64,0},{80,16},{96,32},{112,48},{1... | collective-permute-start | bytes 307208 | tf_op jit(solution)/shard_map/ppermute | solution.py:20
  83.4 16.0 %collective-permute-start.27 = (bf16[400,128]{1,0:T(8,128)(2,1)S(1)}, bf16[400,128]{1,0:T(8,128)(2,1)S(1)}, u32[]{:S(2)}, u32[]{:S(2)}) collective-permute-start(bf16[400,128]{1,0:T(8,128)(2,1)S(1)} %get-tuple-element.41), channel_id=1, source_target_pairs={{0,48},{16,64},{32,80},{48,96},{64,112},{80,0},{96,16},{112,32},{1... | collective-permute-start | bytes 307208 | tf_op jit(solution)/shard_map/ppermute | solution.py:20
  85.1 14.2 %collective-permute-start.28 = (bf16[400,128]{1,0:T(8,128)(2,1)S(1)}, bf16[400,128]{1,0:T(8,128)(2,1)S(1)}, u32[]{:S(2)}, u32[]{:S(2)}) collective-permute-start(bf16[400,128]{1,0:T(8,128)(2,1)S(1)} %get-tuple-element.42), channel_id=1, source_target_pairs={{0,80},{16,96},{32,112},{48,0},{64,16},{80,32},{96,48},{112,64},{1... | collective-permute-start | bytes 307208 | tf_op jit(solution)/shard_map/ppermute | solution.py:20
  87.8 11.8 %collective-permute-start.29 = (bf16[400,128]{1,0:T(8,128)(2,1)S(1)}, bf16[400,128]{1,0:T(8,128)(2,1)S(1)}, u32[]{:S(2)}, u32[]{:S(2)}) collective-permute-start(bf16[400,128]{1,0:T(8,128)(2,1)S(1)} %get-tuple-element.43), channel_id=1, source_target_pairs={{0,32},{16,48},{32,64},{48,80},{64,96},{80,112},{96,0},{112,16},{1... | collective-permute-start | bytes 307208 | tf_op jit(solution)/shard_map/ppermute | solution.py:20
  89.1 12.8 %collective-permute-start.30 = (bf16[400,128]{1,0:T(8,128)(2,1)S(1)}, bf16[400,128]{1,0:T(8,128)(2,1)S(1)}, u32[]{:S(2)}, u32[]{:S(2)}) collective-permute-start(bf16[400,128]{1,0:T(8,128)(2,1)S(1)} %get-tuple-element.44), channel_id=1, source_target_pairs={{0,96},{16,112},{32,0},{48,16},{64,32},{80,48},{96,64},{112,80},{1... | collective-permute-start | bytes 307208 | tf_op jit(solution)/shard_map/ppermute | solution.py:20
  91.4 13.1 %collective-permute-start.31 = (bf16[400,128]{1,0:T(8,128)(2,1)S(1)}, bf16[400,128]{1,0:T(8,128)(2,1)S(1)}, u32[]{:S(2)}, u32[]{:S(2)}) collective-permute-start(bf16[400,128]{1,0:T(8,128)(2,1)S(1)} %get-tuple-element.45), channel_id=1, source_target_pairs={{0,16},{16,32},{32,48},{48,64},{64,80},{80,96},{96,112},{112,0},{1... | collective-permute-start | bytes 307208 | tf_op jit(solution)/shard_map/ppermute | solution.py:20
  99.3 5.2 %collective-permute-start.32 = (bf16[400,128]{1,0:T(8,128)(2,1)S(1)}, bf16[400,128]{1,0:T(8,128)(2,1)S(1)}, u32[]{:S(2)}, u32[]{:S(2)}) collective-permute-start(bf16[400,128]{1,0:T(8,128)(2,1)S(1)} %get-tuple-element.46), channel_id=1, source_target_pairs={{0,112},{16,0},{32,16},{48,32},{64,48},{80,64},{96,80},{112,96},{1... | collective-permute-start | bytes 307208 | tf_op jit(solution)/shard_map/ppermute | solution.py:20

commit v6 on v5

--- a/solution.py
+++ b/solution.py
@@ -73,23 +73,47 @@
     )(*args)
 
 
-def score_body(order, inv_root, *refs):
-    n_z = len(order) + 1
-    steps = [0, *order[::-1]]
-    pieces, refs = refs[: 2 * n_z], refs[2 * n_z :]
-    image, pair_mine, pair_seen, scores, text, row_sent, col_sent = refs
-    rows = pieces[0].shape[0]
+def copies_body(source, out, sems):
+    copies = [
+        pltpu.make_async_copy(source, out.at[i], sems.at[i]) for i in range(out.shape[0])
+    ]
+    for copy in copies:
+        copy.start()
+    for copy in copies:
+        copy.wait()
+
+
+def join_body(near, far, mine, seen, out, pair):
+    first = lax.axis_index("xl") == 0
+    left = mine[...].astype(F32)[None, :]
+    right = seen[...].astype(F32)[None, :]
+    pair[...] = jnp.concatenate(
+        [jnp.where(first, left, right), jnp.where(first, right, left)], axis=1
+    )
+    rows = near.shape[0]
+    out[:rows, :] = near[...]
+    out[rows:, :] = far[...]
+
+
+def score_body(steps, inv_root, *refs):
+    n_z = 2 * len(steps)
+    pieces, refs = refs[:n_z], refs[n_z:]
+    image, pair, scores, text, row_sent, col_sent = refs
+    rows = pieces[0].shape[0] // 2
     size = image.shape[0]
-    pair, ids = labels(pair_mine, pair_seen, n_z, rows)
+    ids = labels(n_z, rows)
     found = jnp.zeros((1, size), F32)
     z = lax.axis_index("z")
     high = jnp.zeros(pieces[0].shape, F32)
     for h in range(2):
         for i, q in enumerate(steps):
-            piece = pieces[h * n_z + i][...]
-            start = h * n_z * rows + lax.rem(z + q, n_z) * rows
-            text[pl.ds(pl.multiple_of(start, 16), rows), :] = piece
-            high = jnp.maximum(high, jnp.abs(piece.astype(F32)))
+            piece = pieces[h * n_z // 2 + i]
+            high = jnp.maximum(high, jnp.abs(piece[...].astype(F32)))
+            for k in range(2):
+                start = (h * n_z + lax.rem(z + q + (k + 2) * n_z // 2, n_z)) * rows
+                text[pl.ds(pl.multiple_of(start, 16), rows), :] = piece[
+                    k * rows : (k + 1) * rows, :
+                ]
     step = 256
     for r in range(0, size, step):
         tile = (
@@ -116,11 +140,8 @@
     col_sent[:, size + LANES :] = jnp.full((1, LANES), jnp.sum(found))
 
 
-def labels(mine, seen, n_z, rows):
+def labels(n_z, rows):
     half = n_z * rows
-    first = lax.axis_index("xl") == 0
-    mine, seen = mine[...].astype(F32), seen[...].astype(F32)
-    pair = jnp.concatenate([jnp.where(first, mine, seen), jnp.where(first, seen, mine)], axis=1)
     n_xl, n_c, n_xh = (lax.axis_size(a) for a in ("xl", "c", "xh"))
     block = (lax.axis_index("y") * n_xh + lax.axis_index("xh")) * n_xl + lax.axis_index("xl")
     core = lax.axis_index("c")
@@ -129,7 +150,7 @@
     within = jnp.where(own, slot, slot - half)
     holder = jnp.floor((within.astype(F32) + 0.5) * (1.0 / rows)).astype(jnp.int32)
     ids = ((block * n_z + holder) * n_c + jnp.where(own, core, 1 - core)) * rows
-    return pair, (ids + within - holder * rows).astype(F32)
+    return (ids + within - holder * rows).astype(F32)
 
 
 def pair_body(crossed, count, mine, seen, out):
@@ -145,16 +166,14 @@
         out[:, at] = mine[:, at] + seen[:, at]
 
 
-def image_body(
-    n_z, inv_root, cols, rows_lse, scores, text, pair_mine, pair_seen, grads, sent, terms
-):
+def image_body(n_z, inv_root, cols, rows_lse, scores, text, pair, grads, sent, terms):
     size = scores.shape[0]
     n_plane = sent.shape[0]
     rows = size // n_plane
     col_lse = cols[:, :size]
     image_max = cols[:, size : size + LANES]
     found = cols[:, size + LANES :]
-    pair, ids = labels(pair_mine, pair_seen, n_z, rows)
+    ids = labels(n_z, rows)
     row_lse = rows_lse[:, :size]
     text_max = rows_lse[:, size:]
     row_terms = jnp.broadcast_to(jnp.sum(row_lse, axis=1, keepdims=True), (1, LANES))
@@ -197,55 +216,81 @@
         )
 
 
-def send_body(order, own, seen, terms, terms_seen, keep, total, *pays):
-    rows = keep.shape[0]
+def pack(pay, blocks, extra):
+    rows, width = blocks[0].shape
+    at = 0
+    for block in blocks:
+        coded = encode(block)
+        for k in range(width // LANES):
+            pay[at : at + rows, :] = coded[:, k * LANES : (k + 1) * LANES]
+            at += rows
+    pay[at:, :] = extra
+
+
+def send_body(steps, own, seen, terms, terms_seen, keep, total, *pays):
+    n_z = 2 * len(steps)
+    rows = keep.shape[0] // 2
     z = lax.axis_index("z")
     row_terms = terms[0:1, :] + terms_seen[0:1, :]
     total[...] = row_terms
     extra = split3(row_terms)
     scale = inverse(terms[2:3, :1])
-    n_z = len(order) + 1
-    for i, q in enumerate([0, *order]):
-        at = pl.ds(pl.multiple_of(lax.rem(z + q, n_z) * rows, 16), rows)
-        block = own[at, :] + seen[at, :]
-        if q == 0:
-            keep[...] = block
-            continue
-        pay = pays[i - 1]
-        part = encode(block * scale)
-        count = block.shape[1] // LANES
-        for k in range(count):
-            pay[k * rows : (k + 1) * rows, :] = part[:, k * LANES : (k + 1) * LANES]
-        pay[count * rows :, :] = extra
-
-
-def text_sum_body(keep, total, terms, *refs):
-    pays, out, side = refs[:-2], refs[-2], refs[-1]
+    for i, q in enumerate(steps):
+        blocks = []
+        for k in range(2):
+            start = lax.rem(z + q + (k + 2) * n_z // 2, n_z) * rows
+            at = pl.ds(pl.multiple_of(start, 16), rows)
+            blocks.append((own[at, :] + seen[at, :]) * scale)
+        if i == 0:
+            keep[:rows, :] = blocks[0]
+            keep[rows:, :] = blocks[1]
+        else:
+            pack(pays[i - 1], blocks, extra)
+
+
+def unpack(pays, at, rows, width):
+    return jnp.concatenate(
+        [
+            sum(decode(p[at + k * rows : at + (k + 1) * rows, :]) for p in pays)
+            for k in range(width // LANES)
+        ],
+        axis=1,
+    )
+
+
+def tails(pays):
+    tail = sum(p[p.shape[0] - EXTRA :, :].astype(F32) for p in pays)
+    return jnp.sum(tail, axis=0, keepdims=True)
+
+
+def relay_body(keep, total, *refs):
+    pays, near, far, total_out = refs[:-3], refs[-3], refs[-2], refs[-1]
+    rows, width = near.shape
+    near[...] = keep[:rows, :] + unpack(pays, 0, rows, width)
+    sums = total[...] + tails(pays)
+    total_out[...] = sums
+    block = keep[rows:, :] + unpack(pays, rows * width // LANES, rows, width)
+    pack(far, [block], split3(sums))
+
+
+def text_sum_body(pairs, near, total, terms, side, pay, out, loss):
     rows, width = out.shape
     unit = terms[2:3, :1]
     unit = jnp.where(unit > 0, unit, 1.0)
-    count = width // LANES
-    for k in range(count):
-        at = slice(k * rows, (k + 1) * rows)
-        lanes = slice(k * LANES, (k + 1) * LANES)
-        out[:, lanes] = keep[:, lanes] + unit * sum(decode(p[at, :]) for p in pays)
-    tail = sum(p[count * rows :, :].astype(F32) for p in pays)
-    side[...] = total[...] + jnp.sum(tail, axis=0, keepdims=True)
-
-
-def image_sum_body(pairs, got, terms, side, out, loss):
+    out[...] = unit * (near[...] + unpack([pay], 0, rows, width))
+    full = total[...] + side[...] + tails([pay])
+    loss[0, 0] = jnp.max(full) / (2.0 * pairs)
+
+
+def image_sum_body(got, terms, out, side):
     rows, width = out.shape
     unit = terms[1:2, :1]
     unit = jnp.where(unit > 0, unit, 1.0)
-    count = width // LANES
-    for k in range(count):
+    pays = [got.at[p] for p in range(got.shape[0])]
+    for k in range(width // LANES):
         at = slice(k * rows, (k + 1) * rows)
-        out[:, k * LANES : (k + 1) * LANES] = unit * sum(
-            decode(got[p, at, :]) for p in range(got.shape[0])
-        )
-    tail = sum(got[p, count * rows :, :].astype(F32) for p in range(got.shape[0]))
-    full = side[...] + jnp.sum(tail, axis=0, keepdims=True)
-    loss[0, 0] = jnp.max(full) / (2.0 * pairs)
+        out[:, k * LANES : (k + 1) * LANES] = unit * sum(decode(p[at, :]) for p in pays)
+    side[...] = tails(pays)
 
 
 def shards(image_embed, text_embed, pair_index):
@@ -259,26 +304,39 @@
     shape = jax.ShapeDtypeStruct
     tall = width // LANES * rows + EXTRA
 
-    pair_mine = pair_index[None, :]
-    pair_seen = lax.ppermute(pair_mine, "xl", SWAP)
-    copies = jnp.broadcast_to(image_embed[None], (n_plane, rows, width))
-    copies, pair_seen = lax.optimization_barrier((copies, pair_seen))
+    pair_seen = lax.ppermute(pair_index, "xl", SWAP)
+    copies = pl.pallas_call(
+        copies_body,
+        out_shape=shape((n_plane, rows, width), BF16),
+        in_specs=[pl.BlockSpec(memory_space=pltpu.VMEM)],
+        out_specs=pl.BlockSpec(memory_space=pl.ANY),
+        scratch_shapes=[pltpu.SemaphoreType.DMA((n_plane,))],
+        name="copies",
+    )(image_embed)
     image = lax.all_to_all(copies, PLANE, 0, 0).reshape(size, width)
 
-    order = sorted(range(1, n_z), key=lambda q: (abs(q - n_z // 2), q))
-    pieces = [text_embed] + [turn(text_embed, "z", -q) for q in order[::-1]]
+    steps = [q if q <= n_z // 4 else q - n_z // 2 for q in range(n_z // 2)]
+    far = turn(text_embed, "z", n_z // 2)
+    joined, pair = call(
+        join_body,
+        (shape((2 * rows, width), BF16), shape((1, size), F32)),
+        (text_embed, far, pair_index, pair_seen),
+        "join",
+        10**11,
+    )
+    pieces = [joined] + [turn(joined, "z", -q) for q in steps[1:]]
     pieces = pieces + [lax.ppermute(piece, "c", SWAP) for piece in pieces]
 
     flops = 2 * size * size * width
     scores, text, row_part, col_part = call(
-        functools.partial(score_body, order, inv_root),
+        functools.partial(score_body, steps, inv_root),
         (
             shape((size, size), F32),
             shape((size, width), BF16),
             shape((1, size + LANES), F32),
             shape((1, size + 2 * LANES), F32),
         ),
-        (*pieces, image, pair_mine, pair_seen),
+        (*pieces, image, pair),
         "scores",
         flops,
         2 * size * size,
@@ -301,7 +359,7 @@
             shape((n_plane, tall, LANES), BF16),
             shape((8, LANES), F32),
         ),
-        (col_part, row_part, scores, text, pair_mine, pair_seen),
+        (col_part, row_part, scores, text, pair),
         "image_grad",
         flops,
         2 * size * size,
@@ -315,25 +373,32 @@
         size=1,
     )
     keep, total, *pays = call(
-        functools.partial(send_body, order),
-        (shape((rows, width), F32), shape((1, LANES), F32))
-        + (shape((tall, LANES), BF16),) * (n_z - 1),
+        functools.partial(send_body, steps),
+        (shape((2 * rows, width), F32), shape((1, LANES), F32))
+        + (shape((2 * tall - EXTRA, LANES), BF16),) * len(steps[1:]),
         (text_own, lax.ppermute(text_other, "c", SWAP), terms, lax.ppermute(terms, "c", SWAP)),
         "send",
         size=1,
     )
-    pays = [turn(pay, "z", q) for q, pay in zip(order, pays)]
-    grad_text, side = call(
-        text_sum_body,
+    pays = [turn(pay, "z", q) for q, pay in zip(steps[1:], pays)]
+    near, far, total = call(
+        relay_body,
+        (shape((rows, width), F32), shape((tall, LANES), BF16), shape((1, LANES), F32)),
+        (keep, total, *pays),
+        "relay",
+        size=1,
+    )
+    grad_image, side = call(
+        image_sum_body,
         (shape((rows, width), F32), shape((1, LANES), F32)),
-        (keep, total, terms, *pays),
+        (image_got, terms),
+        "image_sum",
+    )
+    grad_text, loss = call(
+        functools.partial(text_sum_body, pairs),
+        (shape((rows, width), F32), shape((1, 1), F32)),
+        (near, total, terms, side, turn(far, "z", n_z // 2)),
         "text_sum",
-    )
-    grad_image, loss = call(
-        functools.partial(image_sum_body, pairs),
-        (shape((rows, width), F32), shape((1, 1), F32)),
-        (image_got, terms, side),
-        "image_sum",
         smem_out=1,
     )
     return (loss[0, 0], grad_image, grad_text)

time: 108 us -> 104 us (0.963)
  starting transfers between devices: 72.4 us -> 53.7 us
  waiting for transfers between devices: 17.8 us -> 33.9 us
  local copies, waits for them, and re-layouts: 2.95 us -> 0.01 us
  Pallas kernels: 13.4 us -> 15.6 us
    ppermute x14 -> x8, starting transfers between devices: 32.7 us -> 17.4 us  [turn(): lax.ppermute(x, axis, [(i, (i + step) % count) for i in range(count)])]
    all_to_all x1, waiting for transfers between devices: 0.01 us -> 7.71 us  [shards(): image_got = lax.all_to_all(image_sent, PLANE, 0, 0)]
    ppermute x8, waiting for transfers between devices: 2.26 us -> 6.55 us  [exchange(): seen = lax.ppermute(part, axis, [(i, i ^ step) for i in range(count)])]
    ppermute x8 -> x4, starting transfers between devices: 5.45 us -> 8.81 us  [shards(): pieces = pieces + [lax.ppermute(piece, 'c', SWAP) for piece in pieces]]
    broadcast_in_dim x2 -> x0, local copies, waits for them, and re-layouts: 2.94 us -> none  [the longest x1 2.26 us: shards(): copies = jnp.broadcast_to(image_embed[None], (n_plane, rows, width))]
    ppermute x8, starting transfers between devices: 15 us -> 12.1 us  [exchange(): seen = lax.ppermute(part, axis, [(i, i ^ step) for i in range(count)])]
    ppermute x14 -> x8, waiting for transfers between devices: 12.7 us -> 15.5 us  [turn(): lax.ppermute(x, axis, [(i, (i + step) % count) for i in range(count)])]
    pallas_call x0 -> x1, Pallas kernels: none -> 2.21 us  [shards(): pl.pallas_call(copies_body, out_shape=shape((n_plane, rows, width), BF16)...]
  transfers between devices with their start and end apart: 35 -> 25, of which waited for: 13 -> 13; matrix products, arithmetic and copies ran while one was open for 0% -> 0% of each run, Pallas kernels for 1% -> 4%
where the time goes in v6:
time: 104 us
  starting transfers between devices  53.7 us (52%)
  waiting for transfers between devices  33.9 us (33%)
  Pallas kernels  15.6 us (15%)
    ppermute x8, starting transfers between devices, turn(): lax.ppermute(x, axis, [(i, (i + step) % count) for i in range(count)])  17.4 us
    ppermute x8, waiting for transfers between devices, turn(): lax.ppermute(x, axis, [(i, (i + step) % count) for i in range(count)])  15.5 us
    pallas_call x16, Pallas kernels, call(): pl.pallas_call(body, out_shape=outs, in_specs=[pl.BlockSpec(memory_space=...  13.4 us
    ppermute x8, starting transfers between devices, exchange(): seen = lax.ppermute(part, axis, [(i, i ^ step) for i in range(count)])  12.1 us
    ppermute x4, starting transfers between devices, shards(): pieces = pieces + [lax.ppermute(piece, 'c', SWAP) for piece in pieces]  8.81 us
    all_to_all x1, waiting for transfers between devices, shards(): image_got = lax.all_to_all(image_sent, PLANE, 0, 0)  7.71 us
    all_to_all x1, starting transfers between devices, shards(): image = lax.all_to_all(copies, PLANE, 0, 0).reshape(size, width)  6.6 us
    ppermute x8, waiting for transfers between devices, exchange(): seen = lax.ppermute(part, axis, [(i, i ^ step) for i in range(count)])  6.55 us
  transfers between devices with their start and end apart: 25, of which 13 were waited for; matrix products, arithmetic and copies ran while one was open for 0% of the time, Pallas kernels for 4%

profile of v6, /device:TPU:1, one launch (start us, length us, event | category | flops | bytes accessed | tf_op | source)
XLA Modules:
  0.0 104.1 jit_solution(7378923775345918612)
XLA Ops:
  0.6 7.8 %collective-permute-start = (bf16[48,1024]{1,0:T(8,128)(2,1)}, bf16[48,1024]{1,0:T(8,128)(2,1)S(1)}, u32[]{:S(2)}, u32[]{:S(2)}) collective-permute-start(bf16[48,1024]{1,0:T(8,128)(2,1)} %near.1), channel_id=1, source_target_pairs={{0,64},{16,80},{32,96},{48,112},{64,0},{80,16},{96,32},{112,48},{1... | collective-permute-start | bytes 294920 | tf_op jit(solution)/shard_map/ppermute | solution.py:20
  8.5 1.2 %collective-permute-start.1 = (s32[384]{0:T(512)}, s32[384]{0:T(512)S(1)}, u32[]{:S(2)}, u32[]{:S(2)}) collective-permute-start(s32[384]{0:T(512)} %mine.1), channel_id=1, source_target_pairs={{0,128},{128,0},{1,129},{129,1},{2,130},{130,2},{3,131},{131,3},{4... | collective-permute-start | bytes 4616 | tf_op jit(solution)/shard_map/ppermute | solution.py:307
  9.7 2.2 %copies.1 = bf16[16,48,1024]{2,1,0:T(8,128)(2,1)} custom-call(bf16[48,1024]{1,0:T(8,128)(2,1)} %source.1), custom_call_target="tpu_custom_call" | custom-call | tf_op jit(solution)/shard_map/copies/pallas_call | solution.py:308
  11.9 0.0 copy-start
  11.9 0.0 copy-start.1
  11.9 6.6 %all-to-all-start = ((bf16[16,48,1024]{2,1,0:T(8,128)(2,1)}), bf16[16,48,1024]{2,1,0:T(8,128)(2,1)S(1)}, u32[]{:S(2)}, u32[]{:S(2)}) async-start(bf16[16,48,1024]{2,1,0:T(8,128)(2,1)} %copies.1), calls=%async_computation | async-start | bytes 3145728 | tf_op jit(solution)/shard_map/all_to_all | solution.py:316
  18.6 0.8 collective-permute-start.4
  19.4 0.3 collective-permute-start.3
  19.7 1.7 %collective-permute-start.2 = (bf16[96,1024]{1,0:T(8,128)(2,1)S(1)}, bf16[96,1024]{1,0:T(8,128)(2,1)S(1)}, u32[]{:S(2)}, u32[]{:S(2)}) collective-permute-start(bf16[96,1024]{1,0:T(8,128)(2,1)S(1)} %get-tuple-element.26.refs_0_), channel_id=1, source_target_pairs={{0,112},{16,0},{32,16},{48,32},{64,48},{80,64},{96,80},{112,96},{1... | collective-permute-start | bytes 589832 | tf_op jit(solution)/shard_map/ppermute | solution.py:20
  21.3 2.1 %collective-permute-start.5 = (bf16[96,1024]{1,0:T(8,128)(2,1)S(1)}, bf16[96,1024]{1,0:T(8,128)(2,1)S(1)}, u32[]{:S(2)}, u32[]{:S(2)}) collective-permute-start(bf16[96,1024]{1,0:T(8,128)(2,1)S(1)} %get-tuple-element.26.refs_0_), channel_id=1, source_target_pairs={{0,8},{8,0},{1,9},{9,1},{2,10},{10,2},{3,11},{11,3},{4,12},{12,4},... | collective-permute-start | bytes 589832 | tf_op jit(solution)/shard_map/ppermute | solution.py:328
  23.4 1.3 %collective-permute-done.4.refs_3_ = bf16[96,1024]{1,0:T(8,128)(2,1)S(1)} collective-permute-done((bf16[96,1024]{1,0:T(8,128)(2,1)S(1)}, bf16[96,1024]{1,0:T(8,128)(2,1)S(1)}, u32[]{:S(2)}, u32[]{:S(2)}) %collective-permute-start.4) | collective-permute-done | bytes 196640 | tf_op jit(solution)/shard_map/ppermute | solution.py:20
  24.8 2.4 %collective-permute-start.8 = (bf16[96,1024]{1,0:T(8,128)(2,1)S(1)}, bf16[96,1024]{1,0:T(8,128)(2,1)S(1)}, u32[]{:S(2)}, u32[]{:S(2)}) collective-permute-start(bf16[96,1024]{1,0:T(8,128)(2,1)S(1)} %collective-permute-done.4.refs_3_), channel_id=1, source_target_pairs={{0,8},{8,0},{1,9},{9,1},{2,10},{10,2},{3,11},{11,3},{4,12},{12,4},... | collective-permute-start | bytes 589832 | tf_op jit(solution)/shard_map/ppermute | solution.py:328
  27.2 3.1 %collective-permute-done.3.refs_2_ = bf16[96,1024]{1,0:T(8,128)(2,1)S(1)} collective-permute-done((bf16[96,1024]{1,0:T(8,128)(2,1)S(1)}, bf16[96,1024]{1,0:T(8,128)(2,1)S(1)}, u32[]{:S(2)}, u32[]{:S(2)}) %collective-permute-start.3) | collective-permute-done | bytes 196640 | tf_op jit(solution)/shard_map/ppermute | solution.py:20
  30.2 1.9 %collective-permute-start.7 = (bf16[96,1024]{1,0:T(8,128)(2,1)S(1)}, bf16[96,1024]{1,0:T(8,128)(2,1)S(1)}, u32[]{:S(2)}, u32[]{:S(2)}) collective-permute-start(bf16[96,1024]{1,0:T(8,128)(2,1)S(1)} %collective-permute-done.3.refs_2_), channel_id=1, source_target_pairs={{0,8},{8,0},{1,9},{9,1},{2,10},{10,2},{3,11},{11,3},{4,12},{12,4},... | collective-permute-start | bytes 589832 | tf_op jit(solution)/shard_map/ppermute | solution.py:328
  32.2 1.8 %collective-permute-done.2.refs_1_ = bf16[96,1024]{1,0:T(8,128)(2,1)S(1)} collective-permute-done((bf16[96,1024]{1,0:T(8,128)(2,1)S(1)}, bf16[96,1024]{1,0:T(8,128)(2,1)S(1)}, u32[]{:S(2)}, u32[]{:S(2)}) %collective-permute-start.2) | collective-permute-done | bytes 196640 | tf_op jit(solution)/shard_map/ppermute | solution.py:20
  33.9 2.4 %collective-permute-start.6 = (bf16[96,1024]{1,0:T(8,128)(2,1)S(1)}, bf16[96,1024]{1,0:T(8,128)(2,1)S(1)}, u32[]{:S(2)}, u32[]{:S(2)}) collective-permute-start(bf16[96,1024]{1,0:T(8,128)(2,1)S(1)} %collective-permute-done.2.refs_1_), channel_id=1, source_target_pairs={{0,8},{8,0},{1,9},{9,1},{2,10},{10,2},{3,11},{11,3},{4,12},{12,4},... | collective-permute-start | bytes 589832 | tf_op jit(solution)/shard_map/ppermute | solution.py:328
  36.3 1.1 %collective-permute-done.6.refs_5_ = bf16[96,1024]{1,0:T(8,128)(2,1)S(1)} collective-permute-done((bf16[96,1024]{1,0:T(8,128)(2,1)S(1)}, bf16[96,1024]{1,0:T(8,128)(2,1)S(1)}, u32[]{:S(2)}, u32[]{:S(2)}) %collective-permute-start.6) | collective-permute-done | bytes 196640 | tf_op jit(solution)/shard_map/ppermute | solution.py:328
  37.4 1.9 %all-to-all-done = bf16[16,48,1024]{2,1,0:T(8,128)(2,1)S(1)} async-done(((bf16[16,48,1024]{2,1,0:T(8,128)(2,1)}), bf16[16,48,1024]{2,1,0:T(8,128)(2,1)S(1)}, u32[]{:S(2)}, u32[]{:S(2)}) %all-to-all-start) | async-done | bytes 1572896 | tf_op jit(solution)/shard_map/all_to_all | solution.py:316
  39.3 3.0 %scores.1 = (f32[768,768]{1,0:T(8,128)S(1)}, bf16[768,1024]{1,0:T(8,128)(2,1)S(1)}, f32[1,896]{1,0:T(1,128)S(1)}, f32[1,1024]{1,0:T(1,128)S(1)}) custom-call(bf16[96,1024]{1,0:T(8,128)(2,1)S(1)} %get-tuple-element.26.refs_0_, bf16[96,1024]{1,0:T(8,128)(2,1)S(1)} %collective-permute-done.2.refs_1_, bf16[96,1024]{1,0:T(8,128)(2,1)S(1)} %collective-permute-done.3.refs_2_, ...), custom_call_target="tpu_custom_call" | custom-call | flops 1207959552 | bytes 7088640 | tf_op jit(solution)/shard_map/scores/pallas_call | solution.py:65
  42.3 2.6 %collective-permute-start.9 = (f32[1,1024]{1,0:T(1,128)S(1)}, f32[1,1024]{1,0:T(1,128)S(1)}, u32[]{:S(2)}, u32[]{:S(2)}) collective-permute-start(f32[1,1024]{1,0:T(1,128)S(1)} %get-tuple-element.28.mine), channel_id=1, source_target_pairs={{0,8},{8,0},{1,9},{9,1},{2,10},{10,2},{3,11},{11,3},{4,12},{12,4},... | collective-permute-start | bytes 12296 | tf_op jit(solution)/shard_map/ppermute | solution.py:346
  45.0 1.5 %collective-permute-start.13 = (f32[1,896]{1,0:T(1,128)S(1)}, f32[1,896]{1,0:T(1,128)S(1)}, u32[]{:S(2)}, u32[]{:S(2)}) collective-permute-start(f32[1,896]{1,0:T(1,128)S(1)} %get-tuple-element.29.mine), channel_id=1, source_target_pairs={{0,128},{128,0},{1,129},{129,1},{2,130},{130,2},{3,131},{131,3},{4... | collective-permute-start | bytes 10760 | tf_op jit(solution)/shard_map/ppermute | solution.py:346
  46.4 0.8 collective-permute-start.10
  47.3 0.2 collective-permute-done.13.seen
  47.4 3.7 %collective-permute-start.14 = (f32[1,896]{1,0:T(1,128)S(1)}, f32[1,896]{1,0:T(1,128)S(1)}, u32[]{:S(2)}, u32[]{:S(2)}) collective-permute-start(f32[1,896]{1,0:T(1,128)S(1)} %pair.12.mine), channel_id=1, source_target_pairs={{0,1},{1,0},{2,3},{3,2},{4,5},{5,4},{6,7},{7,6},{8,9},{9,8},{10,11... | collective-permute-start | bytes 10760 | tf_op jit(solution)/shard_map/ppermute | solution.py:346
  51.1 1.3 %collective-permute-start.11 = (f32[1,1024]{1,0:T(1,128)S(1)}, f32[1,1024]{1,0:T(1,128)S(1)}, u32[]{:S(2)}, u32[]{:S(2)}) collective-permute-start(f32[1,1024]{1,0:T(1,128)S(1)} %pair.9.mine), channel_id=1, source_target_pairs={{0,32},{16,48},{32,0},{48,16},{64,96},{80,112},{96,64},{112,80},{1... | collective-permute-start | bytes 12296 | tf_op jit(solution)/shard_map/ppermute | solution.py:346
  52.4 0.3 collective-permute-start.15
  52.7 1.9 %collective-permute-done.11.seen = f32[1,1024]{1,0:T(1,128)S(1)} collective-permute-done((f32[1,1024]{1,0:T(1,128)S(1)}, f32[1,1024]{1,0:T(1,128)S(1)}, u32[]{:S(2)}, u32[]{:S(2)}) %collective-permute-start.11) | collective-permute-done | bytes 4128 | tf_op jit(solution)/shard_map/ppermute | solution.py:346
  54.6 0.8 collective-permute-start.12
  55.4 1.1 %collective-permute-start.16 = (f32[1,896]{1,0:T(1,128)S(1)}, f32[1,896]{1,0:T(1,128)S(1)}, u32[]{:S(2)}, u32[]{:S(2)}) collective-permute-start(f32[1,896]{1,0:T(1,128)S(1)} %pair.14.mine), channel_id=1, source_target_pairs={{0,4},{2,6},{4,0},{6,2},{1,5},{3,7},{5,1},{7,3},{8,12},{10,14},{12... | collective-permute-start | bytes 10760 | tf_op jit(solution)/shard_map/ppermute | solution.py:346
  56.5 2.9 %collective-permute-done.16.seen = f32[1,896]{1,0:T(1,128)S(1)} collective-permute-done((f32[1,896]{1,0:T(1,128)S(1)}, f32[1,896]{1,0:T(1,128)S(1)}, u32[]{:S(2)}, u32[]{:S(2)}) %collective-permute-start.16) | collective-permute-done | bytes 3616 | tf_op jit(solution)/shard_map/ppermute | solution.py:346
  59.5 1.6 %collective-permute-done.12.seen = f32[1,1024]{1,0:T(1,128)S(1)} collective-permute-done((f32[1,1024]{1,0:T(1,128)S(1)}, f32[1,1024]{1,0:T(1,128)S(1)}, u32[]{:S(2)}, u32[]{:S(2)}) %collective-permute-start.12) | collective-permute-done | bytes 4128 | tf_op jit(solution)/shard_map/ppermute | solution.py:346
  61.1 3.6 %image_grad.1 = (bf16[768,768]{1,0:T(8,128)(2,1)S(1)}, bf16[16,400,128]{2,1,0:T(8,128)(2,1)}, f32[8,128]{1,0:T(8,128)S(1)}) custom-call(f32[1,1024]{1,0:T(1,128)S(1)} %pair.11.cols, f32[1,896]{1,0:T(1,128)S(1)} %pair.15.rows_lse, f32[768,768]{1,0:T(8,128)S(1)} %get-tuple-element.30.scores, bf16[768,1024]{1,0:T(8,128)(2,1)S(1)} %get-tuple-element.31.text, ...), custom_call_target="tpu_custom_call" | custom-call | flops 1207959552 | bytes 6765056 | tf_op jit(solution)/shard_map/image_grad/pallas_call | solution.py:65
  64.6 2.0 %text_grad.1 = (f32[384,1024]{1,0:T(8,128)S(1)}, f32[384,1024]{1,0:T(8,128)}) custom-call(bf16[768,768]{1,0:T(8,128)(2,1)S(1)} %get-tuple-element.32.grads, bf16[768,1024]{1,0:T(8,128)(2,1)S(1)} %bitcast.3), custom_call_target="tpu_custom_call" | custom-call | bytes 1 | tf_op jit(solution)/shard_map/text_grad/pallas_call | solution.py:65
  66.6 3.8 %collective-permute-start.17 = (f32[384,1024]{1,0:T(8,128)}, f32[384,1024]{1,0:T(8,128)}, u32[]{:S(2)}, u32[]{:S(2)}) collective-permute-start(f32[384,1024]{1,0:T(8,128)} %get-tuple-element.34), channel_id=1, source_target_pairs={{0,8},{8,0},{1,9},{9,1},{2,10},{10,2},{3,11},{11,3},{4,12},{12,4},... | collective-permute-start | bytes 4718600 | tf_op jit(solution)/shard_map/ppermute | solution.py:379
  70.4 3.7 %all-to-all-start.1 = ((bf16[16,400,128]{2,1,0:T(8,128)(2,1)}), bf16[16,400,128]{2,1,0:T(8,128)(2,1)S(1)}, u32[]{:S(2)}, u32[]{:S(2)}) async-start(bf16[16,400,128]{2,1,0:T(8,128)(2,1)} %get-tuple-element.43), calls=%async_computation.1 | async-start | bytes 3276800 | tf_op jit(solution)/shard_map/all_to_all | solution.py:367
  74.1 0.1 collective-permute-start.18
  74.2 1.2 %collective-permute-done.18.terms_seen = f32[8,128]{1,0:T(8,128)S(1)} collective-permute-done((f32[8,128]{1,0:T(8,128)S(1)}, f32[8,128]{1,0:T(8,128)S(1)}, u32[]{:S(2)}, u32[]{:S(2)}) %collective-permute-start.18) | collective-permute-done | bytes 4128 | tf_op jit(solution)/shard_map/ppermute | solution.py:379
  75.4 1.9 %send.1 = (f32[96,1024]{1,0:T(8,128)S(1)}, f32[1,128]{1,0:T(1,128)S(1)}, bf16[784,128]{1,0:T(8,128)(2,1)S(1)}, bf16[784,128]{1,0:T(8,128)(2,1)S(1)}, bf16[784,128]{1,0:T(8,128)(2,1)S(1)}) custom-call(f32[384,1024]{1,0:T(8,128)S(1)} %get-tuple-element.33.own, f32[384,1024]{1,0:T(8,128)} %collective-permute-done.17.seen, ...), custom_call_target="tpu_custom_call" | custom-call | bytes 1 | tf_op jit(solution)/shard_map/send/pallas_call | solution.py:65
  77.2 0.8 collective-permute-start.19
  78.1 1.2 %collective-permute-start.20 = (bf16[784,128]{1,0:T(8,128)(2,1)S(1)}, bf16[784,128]{1,0:T(8,128)(2,1)S(1)}, u32[]{:S(2)}, u32[]{:S(2)}) collective-permute-start(bf16[784,128]{1,0:T(8,128)(2,1)S(1)} %get-tuple-element.39), channel_id=1, source_target_pairs={{0,32},{16,48},{32,64},{48,80},{64,96},{80,112},{96,0},{112,16},{1... | collective-permute-start | bytes 602120 | tf_op jit(solution)/shard_map/ppermute | solution.py:20
  79.2 1.9 %collective-permute-start.21 = (bf16[784,128]{1,0:T(8,128)(2,1)S(1)}, bf16[784,128]{1,0:T(8,128)(2,1)S(1)}, u32[]{:S(2)}, u32[]{:S(2)}) collective-permute-start(bf16[784,128]{1,0:T(8,128)(2,1)S(1)} %get-tuple-element.40), channel_id=1, source_target_pairs={{0,112},{16,0},{32,16},{48,32},{64,48},{80,64},{96,80},{112,96},{1... | collective-permute-start | bytes 602120 | tf_op jit(solution)/shard_map/ppermute | solution.py:20
  81.2 3.8 %collective-permute-done.19.refs_0_ = bf16[784,128]{1,0:T(8,128)(2,1)S(1)} collective-permute-done((bf16[784,128]{1,0:T(8,128)(2,1)S(1)}, bf16[784,128]{1,0:T(8,128)(2,1)S(1)}, u32[]{:S(2)}, u32[]{:S(2)}) %collective-permute-start.19) | collective-permute-done | bytes 200736 | tf_op jit(solution)/shard_map/ppermute | solution.py:20
  85.0 5.6 %collective-permute-done.20.refs_1_ = bf16[784,128]{1,0:T(8,128)(2,1)S(1)} collective-permute-done((bf16[784,128]{1,0:T(8,128)(2,1)S(1)}, bf16[784,128]{1,0:T(8,128)(2,1)S(1)}, u32[]{:S(2)}, u32[]{:S(2)}) %collective-permute-start.20) | collective-permute-done | bytes 200736 | tf_op jit(solution)/shard_map/ppermute | solution.py:20
  90.6 0.4 relay.1
  91.0 2.9 %collective-permute-start.22 = (bf16[400,128]{1,0:T(8,128)(2,1)S(1)}, bf16[400,128]{1,0:T(8,128)(2,1)S(1)}, u32[]{:S(2)}, u32[]{:S(2)}) collective-permute-start(bf16[400,128]{1,0:T(8,128)(2,1)S(1)} %get-tuple-element.45), channel_id=1, source_target_pairs={{0,64},{16,80},{32,96},{48,112},{64,0},{80,16},{96,32},{112,48},{1... | collective-permute-start | bytes 307208 | tf_op jit(solution)/shard_map/ppermute | solution.py:20
  93.8 7.7 %all-to-all-done.1.got = bf16[16,400,128]{2,1,0:T(8,128)(2,1)S(1)} async-done(((bf16[16,400,128]{2,1,0:T(8,128)(2,1)}), bf16[16,400,128]{2,1,0:T(8,128)(2,1)S(1)}, u32[]{:S(2)}, u32[]{:S(2)}) %all-to-all-start.1) | async-done | bytes 1638432 | tf_op jit(solution)/shard_map/all_to_all | solution.py:367
  101.6 1.6 %image_sum.1 = (f32[48,1024]{1,0:T(8,128)}, f32[1,128]{1,0:T(1,128)S(1)}) custom-call(bf16[16,400,128]{2,1,0:T(8,128)(2,1)S(1)} %all-to-all-done.1.got, f32[8,128]{1,0:T(8,128)S(1)} %get-tuple-element.35.terms), custom_call_target="tpu_custom_call" | custom-call | bytes 1839616 | tf_op jit(solution)/shard_map/image_sum/pallas_call | solution.py:65
  103.2 0.8 text_sum.1
  (23 shorter events, 0.2 us)
Async XLA Ops:
  0.6 17.9 %collective-permute-start = (bf16[48,1024]{1,0:T(8,128)(2,1)}, bf16[48,1024]{1,0:T(8,128)(2,1)S(1)}, u32[]{:S(2)}, u32[]{:S(2)}) collective-permute-start(bf16[48,1024]{1,0:T(8,128)(2,1)} %near.1), channel_id=1, source_target_pairs={{0,64},{16,80},{32,96},{48,112},{64,0},{80,16},{96,32},{112,48},{1... | collective-permute-start | bytes 294920 | tf_op jit(solution)/shard_map/ppermute | solution.py:20
  8.5 10.1 %collective-permute-start.1 = (s32[384]{0:T(512)}, s32[384]{0:T(512)S(1)}, u32[]{:S(2)}, u32[]{:S(2)}) collective-permute-start(s32[384]{0:T(512)} %mine.1), channel_id=1, source_target_pairs={{0,128},{128,0},{1,129},{129,1},{2,130},{130,2},{3,131},{131,3},{4... | collective-permute-start | bytes 4616 | tf_op jit(solution)/shard_map/ppermute | solution.py:307
  11.9 6.7 %copy-start = (bf16[48,1024]{1,0:T(8,128)(2,1)S(1)}, bf16[48,1024]{1,0:T(8,128)(2,1)}, u32[]{:S(2)}) copy-start(bf16[48,1024]{1,0:T(8,128)(2,1)} %near.1) | copy-start | bytes 294916
  11.9 6.7 %copy-start.1 = (s32[384]{0:T(512)S(1)}, s32[384]{0:T(512)}, u32[]{:S(2)}) copy-start(s32[384]{0:T(512)} %mine.1) | copy-start | bytes 4612
  11.9 27.4 %all-to-all-start = ((bf16[16,48,1024]{2,1,0:T(8,128)(2,1)}), bf16[16,48,1024]{2,1,0:T(8,128)(2,1)S(1)}, u32[]{:S(2)}, u32[]{:S(2)}) async-start(bf16[16,48,1024]{2,1,0:T(8,128)(2,1)} %copies.1), calls=%async_computation | async-start | bytes 3145728 | tf_op jit(solution)/shard_map/all_to_all | solution.py:316
  18.6 6.2 %collective-permute-start.4 = (bf16[96,1024]{1,0:T(8,128)(2,1)S(1)}, bf16[96,1024]{1,0:T(8,128)(2,1)S(1)}, u32[]{:S(2)}, u32[]{:S(2)}) collective-permute-start(bf16[96,1024]{1,0:T(8,128)(2,1)S(1)} %get-tuple-element.26.refs_0_), channel_id=1, source_target_pairs={{0,16},{16,32},{32,48},{48,64},{64,80},{80,96},{96,112},{112,0},{1... | collective-permute-start | bytes 589832 | tf_op jit(solution)/shard_map/ppermute | solution.py:20
  19.4 10.8 %collective-permute-start.3 = (bf16[96,1024]{1,0:T(8,128)(2,1)S(1)}, bf16[96,1024]{1,0:T(8,128)(2,1)S(1)}, u32[]{:S(2)}, u32[]{:S(2)}) collective-permute-start(bf16[96,1024]{1,0:T(8,128)(2,1)S(1)} %get-tuple-element.26.refs_0_), channel_id=1, source_target_pairs={{0,96},{16,112},{32,0},{48,16},{64,32},{80,48},{96,64},{112,80},{1... | collective-permute-start | bytes 589832 | tf_op jit(solution)/shard_map/ppermute | solution.py:20
  19.7 14.3 %collective-permute-start.2 = (bf16[96,1024]{1,0:T(8,128)(2,1)S(1)}, bf16[96,1024]{1,0:T(8,128)(2,1)S(1)}, u32[]{:S(2)}, u32[]{:S(2)}) collective-permute-start(bf16[96,1024]{1,0:T(8,128)(2,1)S(1)} %get-tuple-element.26.refs_0_), channel_id=1, source_target_pairs={{0,112},{16,0},{32,16},{48,32},{64,48},{80,64},{96,80},{112,96},{1... | collective-permute-start | bytes 589832 | tf_op jit(solution)/shard_map/ppermute | solution.py:20
  21.3 14.9 %collective-permute-start.5 = (bf16[96,1024]{1,0:T(8,128)(2,1)S(1)}, bf16[96,1024]{1,0:T(8,128)(2,1)S(1)}, u32[]{:S(2)}, u32[]{:S(2)}) collective-permute-start(bf16[96,1024]{1,0:T(8,128)(2,1)S(1)} %get-tuple-element.26.refs_0_), channel_id=1, source_target_pairs={{0,8},{8,0},{1,9},{9,1},{2,10},{10,2},{3,11},{11,3},{4,12},{12,4},... | collective-permute-start | bytes 589832 | tf_op jit(solution)/shard_map/ppermute | solution.py:328
  24.8 11.5 %collective-permute-start.8 = (bf16[96,1024]{1,0:T(8,128)(2,1)S(1)}, bf16[96,1024]{1,0:T(8,128)(2,1)S(1)}, u32[]{:S(2)}, u32[]{:S(2)}) collective-permute-start(bf16[96,1024]{1,0:T(8,128)(2,1)S(1)} %collective-permute-done.4.refs_3_), channel_id=1, source_target_pairs={{0,8},{8,0},{1,9},{9,1},{2,10},{10,2},{3,11},{11,3},{4,12},{12,4},... | collective-permute-start | bytes 589832 | tf_op jit(solution)/shard_map/ppermute | solution.py:328
  30.2 6.1 %collective-permute-start.7 = (bf16[96,1024]{1,0:T(8,128)(2,1)S(1)}, bf16[96,1024]{1,0:T(8,128)(2,1)S(1)}, u32[]{:S(2)}, u32[]{:S(2)}) collective-permute-start(bf16[96,1024]{1,0:T(8,128)(2,1)S(1)} %collective-permute-done.3.refs_2_), channel_id=1, source_target_pairs={{0,8},{8,0},{1,9},{9,1},{2,10},{10,2},{3,11},{11,3},{4,12},{12,4},... | collective-permute-start | bytes 589832 | tf_op jit(solution)/shard_map/ppermute | solution.py:328
  33.9 3.4 %collective-permute-start.6 = (bf16[96,1024]{1,0:T(8,128)(2,1)S(1)}, bf16[96,1024]{1,0:T(8,128)(2,1)S(1)}, u32[]{:S(2)}, u32[]{:S(2)}) collective-permute-start(bf16[96,1024]{1,0:T(8,128)(2,1)S(1)} %collective-permute-done.2.refs_1_), channel_id=1, source_target_pairs={{0,8},{8,0},{1,9},{9,1},{2,10},{10,2},{3,11},{11,3},{4,12},{12,4},... | collective-permute-start | bytes 589832 | tf_op jit(solution)/shard_map/ppermute | solution.py:328
  42.3 4.1 %collective-permute-start.9 = (f32[1,1024]{1,0:T(1,128)S(1)}, f32[1,1024]{1,0:T(1,128)S(1)}, u32[]{:S(2)}, u32[]{:S(2)}) collective-permute-start(f32[1,1024]{1,0:T(1,128)S(1)} %get-tuple-element.28.mine), channel_id=1, source_target_pairs={{0,8},{8,0},{1,9},{9,1},{2,10},{10,2},{3,11},{11,3},{4,12},{12,4},... | collective-permute-start | bytes 12296 | tf_op jit(solution)/shard_map/ppermute | solution.py:346
  45.0 2.5 %collective-permute-start.13 = (f32[1,896]{1,0:T(1,128)S(1)}, f32[1,896]{1,0:T(1,128)S(1)}, u32[]{:S(2)}, u32[]{:S(2)}) collective-permute-start(f32[1,896]{1,0:T(1,128)S(1)} %get-tuple-element.29.mine), channel_id=1, source_target_pairs={{0,128},{128,0},{1,129},{129,1},{2,130},{130,2},{3,131},{131,3},{4... | collective-permute-start | bytes 10760 | tf_op jit(solution)/shard_map/ppermute | solution.py:346
  46.4 4.7 %collective-permute-start.10 = (f32[1,1024]{1,0:T(1,128)S(1)}, f32[1,1024]{1,0:T(1,128)S(1)}, u32[]{:S(2)}, u32[]{:S(2)}) collective-permute-start(f32[1,1024]{1,0:T(1,128)S(1)} %pair.8.mine), channel_id=1, source_target_pairs={{0,16},{16,0},{32,48},{48,32},{64,80},{80,64},{96,112},{112,96},{1... | collective-permute-start | bytes 12296 | tf_op jit(solution)/shard_map/ppermute | solution.py:346
  47.4 5.0 %collective-permute-start.14 = (f32[1,896]{1,0:T(1,128)S(1)}, f32[1,896]{1,0:T(1,128)S(1)}, u32[]{:S(2)}, u32[]{:S(2)}) collective-permute-start(f32[1,896]{1,0:T(1,128)S(1)} %pair.12.mine), channel_id=1, source_target_pairs={{0,1},{1,0},{2,3},{3,2},{4,5},{5,4},{6,7},{7,6},{8,9},{9,8},{10,11... | collective-permute-start | bytes 10760 | tf_op jit(solution)/shard_map/ppermute | solution.py:346
  51.1 3.4 %collective-permute-start.11 = (f32[1,1024]{1,0:T(1,128)S(1)}, f32[1,1024]{1,0:T(1,128)S(1)}, u32[]{:S(2)}, u32[]{:S(2)}) collective-permute-start(f32[1,1024]{1,0:T(1,128)S(1)} %pair.9.mine), channel_id=1, source_target_pairs={{0,32},{16,48},{32,0},{48,16},{64,96},{80,112},{96,64},{112,80},{1... | collective-permute-start | bytes 12296 | tf_op jit(solution)/shard_map/ppermute | solution.py:346
  52.4 3.0 %collective-permute-start.15 = (f32[1,896]{1,0:T(1,128)S(1)}, f32[1,896]{1,0:T(1,128)S(1)}, u32[]{:S(2)}, u32[]{:S(2)}) collective-permute-start(f32[1,896]{1,0:T(1,128)S(1)} %pair.13.mine), channel_id=1, source_target_pairs={{0,2},{2,0},{4,6},{6,4},{1,3},{3,1},{5,7},{7,5},{8,10},{10,8},{12,... | collective-permute-start | bytes 10760 | tf_op jit(solution)/shard_map/ppermute | solution.py:346
  54.6 6.5 %collective-permute-start.12 = (f32[1,1024]{1,0:T(1,128)S(1)}, f32[1,1024]{1,0:T(1,128)S(1)}, u32[]{:S(2)}, u32[]{:S(2)}) collective-permute-start(f32[1,1024]{1,0:T(1,128)S(1)} %pair.10.mine), channel_id=1, source_target_pairs={{0,64},{16,80},{32,96},{48,112},{64,0},{80,16},{96,32},{112,48},{1... | collective-permute-start | bytes 12296 | tf_op jit(solution)/shard_map/ppermute | solution.py:346
  55.4 4.0 %collective-permute-start.16 = (f32[1,896]{1,0:T(1,128)S(1)}, f32[1,896]{1,0:T(1,128)S(1)}, u32[]{:S(2)}, u32[]{:S(2)}) collective-permute-start(f32[1,896]{1,0:T(1,128)S(1)} %pair.14.mine), channel_id=1, source_target_pairs={{0,4},{2,6},{4,0},{6,2},{1,5},{3,7},{5,1},{7,3},{8,12},{10,14},{12... | collective-permute-start | bytes 10760 | tf_op jit(solution)/shard_map/ppermute | solution.py:346
  66.6 8.8 %collective-permute-start.17 = (f32[384,1024]{1,0:T(8,128)}, f32[384,1024]{1,0:T(8,128)}, u32[]{:S(2)}, u32[]{:S(2)}) collective-permute-start(f32[384,1024]{1,0:T(8,128)} %get-tuple-element.34), channel_id=1, source_target_pairs={{0,8},{8,0},{1,9},{9,1},{2,10},{10,2},{3,11},{11,3},{4,12},{12,4},... | collective-permute-start | bytes 4718600 | tf_op jit(solution)/shard_map/ppermute | solution.py:379
  70.4 31.1 %all-to-all-start.1 = ((bf16[16,400,128]{2,1,0:T(8,128)(2,1)}), bf16[16,400,128]{2,1,0:T(8,128)(2,1)S(1)}, u32[]{:S(2)}, u32[]{:S(2)}) async-start(bf16[16,400,128]{2,1,0:T(8,128)(2,1)} %get-tuple-element.43), calls=%async_computation.1 | async-start | bytes 3276800 | tf_op jit(solution)/shard_map/all_to_all | solution.py:367
  74.1 1.3 %collective-permute-start.18 = (f32[8,128]{1,0:T(8,128)S(1)}, f32[8,128]{1,0:T(8,128)S(1)}, u32[]{:S(2)}, u32[]{:S(2)}) collective-permute-start(f32[8,128]{1,0:T(8,128)S(1)} %get-tuple-element.35.terms), channel_id=1, source_target_pairs={{0,8},{8,0},{1,9},{9,1},{2,10},{10,2},{3,11},{11,3},{4,12},{12,4},... | collective-permute-start | bytes 12296 | tf_op jit(solution)/shard_map/ppermute | solution.py:379
  77.2 7.7 %collective-permute-start.19 = (bf16[784,128]{1,0:T(8,128)(2,1)S(1)}, bf16[784,128]{1,0:T(8,128)(2,1)S(1)}, u32[]{:S(2)}, u32[]{:S(2)}) collective-permute-start(bf16[784,128]{1,0:T(8,128)(2,1)S(1)} %get-tuple-element.38), channel_id=1, source_target_pairs={{0,16},{16,32},{32,48},{48,64},{64,80},{80,96},{96,112},{112,0},{1... | collective-permute-start | bytes 602120 | tf_op jit(solution)/shard_map/ppermute | solution.py:20
  78.1 12.5 %collective-permute-start.20 = (bf16[784,128]{1,0:T(8,128)(2,1)S(1)}, bf16[784,128]{1,0:T(8,128)(2,1)S(1)}, u32[]{:S(2)}, u32[]{:S(2)}) collective-permute-start(bf16[784,128]{1,0:T(8,128)(2,1)S(1)} %get-tuple-element.39), channel_id=1, source_target_pairs={{0,32},{16,48},{32,64},{48,80},{64,96},{80,112},{96,0},{112,16},{1... | collective-permute-start | bytes 602120 | tf_op jit(solution)/shard_map/ppermute | solution.py:20
  79.2 11.3 %collective-permute-start.21 = (bf16[784,128]{1,0:T(8,128)(2,1)S(1)}, bf16[784,128]{1,0:T(8,128)(2,1)S(1)}, u32[]{:S(2)}, u32[]{:S(2)}) collective-permute-start(bf16[784,128]{1,0:T(8,128)(2,1)S(1)} %get-tuple-element.40), channel_id=1, source_target_pairs={{0,112},{16,0},{32,16},{48,32},{64,48},{80,64},{96,80},{112,96},{1... | collective-permute-start | bytes 602120 | tf_op jit(solution)/shard_map/ppermute | solution.py:20
  91.0 12.2 %collective-permute-start.22 = (bf16[400,128]{1,0:T(8,128)(2,1)S(1)}, bf16[400,128]{1,0:T(8,128)(2,1)S(1)}, u32[]{:S(2)}, u32[]{:S(2)}) collective-permute-start(bf16[400,128]{1,0:T(8,128)(2,1)S(1)} %get-tuple-element.45), channel_id=1, source_target_pairs={{0,64},{16,80},{32,96},{48,112},{64,0},{80,16},{96,32},{112,48},{1... | collective-permute-start | bytes 307208 | tf_op jit(solution)/shard_map/ppermute | solution.py:20

commit v7 on v6

--- a/solution.py
+++ b/solution.py
@@ -7,7 +7,6 @@
 from jax.experimental.pallas import tpu as pltpu
 from jax.sharding import Mesh, PartitionSpec as P
 
-PLANE = ("xl", "y", "xh")
 SWAP = [(0, 1), (1, 0)]
 LANES = 128
 EXTRA = 16
@@ -18,6 +17,22 @@
 def turn(x, axis, step):
     count = lax.axis_size(axis)
     return lax.ppermute(x, axis, [(i, (i + step) % count) for i in range(count)])
+
+
+def turn_x(x, step):
+    n_xl, n_xh = lax.axis_size("xl"), lax.axis_size("xh")
+    count = n_xl * n_xh
+    place = [(i % n_xl) * n_xh + i // n_xl for i in range(count)]
+    pairs = [(place[i], place[(i + step) % count]) for i in range(count)]
+    return lax.ppermute(x, ("xl", "xh"), pairs)
+
+
+def image_slot(step_x, step_y):
+    n_xl, n_y, n_xh = (lax.axis_size(a) for a in ("xl", "y", "xh"))
+    x = lax.axis_index("xh") * n_xl + lax.axis_index("xl")
+    x = lax.rem(x + step_x + n_xl * n_xh, n_xl * n_xh)
+    y = lax.rem(lax.axis_index("y") + step_y + n_y, n_y)
+    return (lax.rem(x, n_xl) * n_y + y) * n_xh + lax.div(x, n_xl)
 
 
 def merge(parts):
@@ -58,7 +73,7 @@
     return jnp.transpose(jnp.broadcast_to(column, (column.shape[0], LANES)))[:1, :]
 
 
-def call(body, outs, args, name, flops=0, exps=0, smem_out=None, size=None):
+def call(body, outs, args, name, flops=0, exps=0, smem_out=None, size=None, scratch=()):
     if size is None:
         size = sum(a.size * a.dtype.itemsize for a in (*args, *outs))
     spaces = [pltpu.SMEM if i == smem_out else pltpu.VMEM for i in range(len(outs))]
@@ -67,23 +82,15 @@
         out_shape=outs,
         in_specs=[pl.BlockSpec(memory_space=pltpu.VMEM)] * len(args),
         out_specs=tuple(pl.BlockSpec(memory_space=s) for s in spaces),
+        scratch_shapes=scratch,
         cost_estimate=pl.CostEstimate(flops=flops, bytes_accessed=size, transcendentals=exps),
         compiler_params=pltpu.CompilerParams(vmem_limit_bytes=20 * 1024 * 1024),
         name=name,
     )(*args)
 
 
-def copies_body(source, out, sems):
-    copies = [
-        pltpu.make_async_copy(source, out.at[i], sems.at[i]) for i in range(out.shape[0])
-    ]
-    for copy in copies:
-        copy.start()
-    for copy in copies:
-        copy.wait()
-
-
-def join_body(near, far, mine, seen, out, pair):
+def join_body(near, far, mine, seen, *refs):
+    images, (out, lined, pair) = refs[:-3], refs[-3:]
     first = lax.axis_index("xl") == 0
     left = mine[...].astype(F32)[None, :]
     right = seen[...].astype(F32)[None, :]
@@ -93,14 +100,21 @@
     rows = near.shape[0]
     out[:rows, :] = near[...]
     out[rows:, :] = far[...]
-
-
-def score_body(steps, inv_root, *refs):
+    for i, ref in enumerate(images):
+        lined[i * rows : (i + 1) * rows, :] = ref[...]
+
+
+def score_body(steps, steps_x, steps_y, inv_root, *refs):
     n_z = 2 * len(steps)
     pieces, refs = refs[:n_z], refs[n_z:]
-    image, pair, scores, text, row_sent, col_sent = refs
+    images, refs = refs[: len(steps_y)], refs[len(steps_y) :]
+    pair, scores, text, image, row_sent, col_sent = refs
     rows = pieces[0].shape[0] // 2
     size = image.shape[0]
+    for step_y, ref in zip(steps_y, images):
+        for i, step_x in enumerate(steps_x):
+            start = pl.multiple_of(image_slot(step_x, step_y) * rows, 16)
+            image[pl.ds(start, rows), :] = ref[i * rows : (i + 1) * rows, :]
     ids = labels(n_z, rows)
     found = jnp.zeros((1, size), F32)
     z = lax.axis_index("z")
@@ -166,10 +180,10 @@
         out[:, at] = mine[:, at] + seen[:, at]
 
 
-def image_body(n_z, inv_root, cols, rows_lse, scores, text, pair, grads, sent, terms):
+def image_body(n_z, steps_x, steps_y, inv_root, cols, rows_lse, scores, text, pair, *refs):
+    grads, terms, keep, *pays, marks = refs
     size = scores.shape[0]
-    n_plane = sent.shape[0]
-    rows = size // n_plane
+    rows = keep.shape[0] // len(steps_x)
     col_lse = cols[:, :size]
     image_max = cols[:, size : size + LANES]
     found = cols[:, size + LANES :]
@@ -179,27 +193,30 @@
     row_terms = jnp.broadcast_to(jnp.sum(row_lse, axis=1, keepdims=True), (1, LANES))
     col_terms = jnp.sum(col_lse, axis=1, keepdims=True) - 2.0 * found
     terms[...] = jnp.concatenate(
-        [row_terms, text_max, image_max, jnp.zeros((5, LANES), F32)], axis=0
+        [row_terms, text_max, image_max, col_terms, jnp.zeros((4, LANES), F32)], axis=0
     )
     extra = split3(col_terms)
+    marks[...] = jnp.transpose(
+        jnp.concatenate([row_lse, pair[...], jnp.zeros((LANES - 2, size), F32)], axis=0)
+    )
     scale = inverse(text_max[:, :1]) * inv_root
-    step = 384
-    for r in range(0, size, step):
-        tile = scores[r : r + step, :]
-        probs = 0.5 * (
-            jnp.exp(tile - to_column(row_lse[:, r : r + step])) + jnp.exp(tile - col_lse)
-        )
-        hit = to_column(pair[:, r : r + step]) == ids
-        grad = (probs - jnp.where(hit, 1.0, 0.0)).astype(BF16)
-        grads[r : r + step, :] = grad
-        part = encode(jnp.dot(grad, text[...], preferred_element_type=F32) * scale)
-        for p in range(step // rows):
-            to = r // rows + p
-            for k in range(text.shape[1] // LANES):
-                sent[to, k * rows : (k + 1) * rows, :] = part[
-                    p * rows : (p + 1) * rows, k * LANES : (k + 1) * LANES
-                ]
-            sent[to, k * rows + rows :, :] = extra
+    for i, step_y in enumerate(steps_y):
+        spots = [
+            pl.ds(pl.multiple_of(image_slot(step_x, step_y) * rows, 16), rows)
+            for step_x in steps_x
+        ]
+        tile = jnp.concatenate([scores[at, :] for at in spots], axis=0)
+        mark = jnp.concatenate([marks[at, :] for at in spots], axis=0)
+        probs = 0.5 * (jnp.exp(tile - mark[:, :1]) + jnp.exp(tile - col_lse))
+        grad = (probs - jnp.where(mark[:, 1:2] == ids, 1.0, 0.0)).astype(BF16)
+        for k, at in enumerate(spots):
+            grads[at, :] = grad[k * rows : (k + 1) * rows, :]
+        part = jnp.dot(grad, text[...], preferred_element_type=F32) * scale
+        if i == 0:
+            keep[...] = part
+        else:
+            blocks = [part[k * rows : (k + 1) * rows, :] for k in range(len(spots))]
+            pack(pays[i - 1], blocks, extra)
 
 
 def text_body(inv_root, grads, image, own, other):
@@ -263,14 +280,19 @@
     return jnp.sum(tail, axis=0, keepdims=True)
 
 
-def relay_body(keep, total, *refs):
-    pays, near, far, total_out = refs[:-3], refs[-3], refs[-2], refs[-1]
+def relay_body(row, count, n_in, keep, total, *refs):
+    pays, (near, total_out, *outs) = refs[:n_in], refs[n_in:]
     rows, width = near.shape
-    near[...] = keep[:rows, :] + unpack(pays, 0, rows, width)
-    sums = total[...] + tails(pays)
+    sums = total[row : row + 1, :] + tails(pays)
     total_out[...] = sums
-    block = keep[rows:, :] + unpack(pays, rows * width // LANES, rows, width)
-    pack(far, [block], split3(sums))
+    extra = split3(sums)
+    for k in range(count):
+        block = keep[k * rows : (k + 1) * rows, :]
+        block = block + unpack(pays, k * rows * width // LANES, rows, width)
+        if k == 0:
+            near[...] = block
+        else:
+            pack(outs[k - 1], [block], extra)
 
 
 def text_sum_body(pairs, near, total, terms, side, pay, out, loss):
@@ -282,15 +304,13 @@
     loss[0, 0] = jnp.max(full) / (2.0 * pairs)
 
 
-def image_sum_body(got, terms, out, side):
+def image_sum_body(near, total, terms, *refs):
+    pays, (out, side) = refs[:-2], refs[-2:]
     rows, width = out.shape
     unit = terms[1:2, :1]
     unit = jnp.where(unit > 0, unit, 1.0)
-    pays = [got.at[p] for p in range(got.shape[0])]
-    for k in range(width // LANES):
-        at = slice(k * rows, (k + 1) * rows)
-        out[:, k * LANES : (k + 1) * LANES] = unit * sum(decode(p[at, :]) for p in pays)
-    side[...] = tails(pays)
+    out[...] = unit * (near[...] + unpack(pays, 0, rows, width))
+    side[...] = total[...] + tails(pays)
 
 
 def shards(image_embed, text_embed, pair_index):
@@ -305,38 +325,36 @@
     tall = width // LANES * rows + EXTRA
 
     pair_seen = lax.ppermute(pair_index, "xl", SWAP)
-    copies = pl.pallas_call(
-        copies_body,
-        out_shape=shape((n_plane, rows, width), BF16),
-        in_specs=[pl.BlockSpec(memory_space=pltpu.VMEM)],
-        out_specs=pl.BlockSpec(memory_space=pl.ANY),
-        scratch_shapes=[pltpu.SemaphoreType.DMA((n_plane,))],
-        name="copies",
-    )(image_embed)
-    image = lax.all_to_all(copies, PLANE, 0, 0).reshape(size, width)
-
+    steps_x = [0, 1, -1, 2]
+    steps_y = [0, 1, -1, 2]
     steps = [q if q <= n_z // 4 else q - n_z // 2 for q in range(n_z // 2)]
     far = turn(text_embed, "z", n_z // 2)
-    joined, pair = call(
+    line = [image_embed] + [turn_x(image_embed, -q) for q in steps_x[1:]]
+    joined, lined, pair = call(
         join_body,
-        (shape((2 * rows, width), BF16), shape((1, size), F32)),
-        (text_embed, far, pair_index, pair_seen),
+        (
+            shape((2 * rows, width), BF16),
+            shape((len(line) * rows, width), BF16),
+            shape((1, size), F32),
+        ),
+        (text_embed, far, pair_index, pair_seen, *line),
         "join",
-        10**11,
-    )
+    )
+    images = [lined] + [turn(lined, "y", -q) for q in steps_y[1:]]
     pieces = [joined] + [turn(joined, "z", -q) for q in steps[1:]]
     pieces = pieces + [lax.ppermute(piece, "c", SWAP) for piece in pieces]
 
     flops = 2 * size * size * width
-    scores, text, row_part, col_part = call(
-        functools.partial(score_body, steps, inv_root),
+    scores, text, image, row_part, col_part = call(
+        functools.partial(score_body, steps, steps_x, steps_y, inv_root),
         (
             shape((size, size), F32),
+            shape((size, width), BF16),
             shape((size, width), BF16),
             shape((1, size + LANES), F32),
             shape((1, size + 2 * LANES), F32),
         ),
-        (*pieces, image, pair),
+        (*pieces, *images, pair),
         "scores",
         flops,
         2 * size * size,
@@ -352,25 +370,27 @@
     for axis, step in (("xl", 1), ("xh", 1), ("y", 1), ("y", 2)):
         row_part = exchange(row_part, axis, step)
 
-    grads, image_sent, terms = call(
-        functools.partial(image_body, n_z, inv_root),
+    grads, terms, image_keep, *image_pays = call(
+        functools.partial(image_body, n_z, steps_x, steps_y, inv_root),
         (
             shape((size, size), BF16),
-            shape((n_plane, tall, LANES), BF16),
             shape((8, LANES), F32),
-        ),
+            shape((len(steps_x) * rows, width), F32),
+        )
+        + (shape((len(steps_x) * (tall - EXTRA) + EXTRA, LANES), BF16),) * len(steps_y[1:]),
         (col_part, row_part, scores, text, pair),
         "image_grad",
         flops,
         2 * size * size,
-    )
-    image_got = lax.all_to_all(image_sent, PLANE, 0, 0)
+        scratch=[pltpu.VMEM((size, LANES), F32)],
+    )
+    image_pays = [turn(pay, "y", q) for q, pay in zip(steps_y[1:], image_pays)]
     text_own, text_other = call(
         functools.partial(text_body, inv_root),
         (shape((half, width), F32), shape((half, width), F32)),
         (grads, image),
         "text_grad",
-        size=1,
+        10**10,
     )
     keep, total, *pays = call(
         functools.partial(send_body, steps),
@@ -381,17 +401,21 @@
         size=1,
     )
     pays = [turn(pay, "z", q) for q, pay in zip(steps[1:], pays)]
-    near, far, total = call(
-        relay_body,
-        (shape((rows, width), F32), shape((tall, LANES), BF16), shape((1, LANES), F32)),
-        (keep, total, *pays),
-        "relay",
-        size=1,
-    )
+    def relay(row, keep, total, pays, count, name):
+        outs = (shape((rows, width), F32), shape((1, LANES), F32))
+        outs = outs + (shape((tall, LANES), BF16),) * (count - 1)
+        body = functools.partial(relay_body, row, count, len(pays))
+        return call(body, outs, (keep, total, *pays), name, size=1)
+
+    image_near, image_total, *image_pays = relay(
+        3, image_keep, terms, image_pays, len(steps_x), "image_relay"
+    )
+    image_pays = [turn_x(pay, q) for q, pay in zip(steps_x[1:], image_pays)]
+    near, total, far = relay(0, keep, total, pays, 2, "text_relay")
     grad_image, side = call(
         image_sum_body,
         (shape((rows, width), F32), shape((1, LANES), F32)),
-        (image_got, terms),
+        (image_near, image_total, terms, *image_pays),
         "image_sum",
     )
     grad_text, loss = call(

time: 104 us -> 110 us (1.058)
  the two profiles are of different devices: /device:TPU:1 before, /device:TPU:32 now
where the time goes in v7:
time: 110 us
  starting transfers between devices  52.2 us (47%)
  waiting for transfers between devices  43.4 us (39%)
  Pallas kernels  10.7 us (10%)
  local copies, waits for them, and re-layouts  2.47 us (2%)
    ppermute x14, starting transfers between devices, turn(): lax.ppermute(x, axis, [(i, (i + step) % count) for i in range(count)])  28.9 us
    ppermute x14, waiting for transfers between devices, turn(): lax.ppermute(x, axis, [(i, (i + step) % count) for i in range(count)])  28.7 us
    ppermute x8, starting transfers between devices, exchange(): seen = lax.ppermute(part, axis, [(i, i ^ step) for i in range(count)])  13.2 us
    pallas_call x17, Pallas kernels, call(): pl.pallas_call(body, out_shape=outs, in_specs=[pl.BlockSpec(memory_space=...  10.7 us
    ppermute x6, starting transfers between devices, turn_x(): return lax.ppermute(x, ('xl', 'xh'), pairs)  8.96 us
    ppermute x8, waiting for transfers between devices, exchange(): seen = lax.ppermute(part, axis, [(i, i ^ step) for i in range(count)])  5.63 us
    ppermute x6, waiting for transfers between devices, turn_x(): return lax.ppermute(x, ('xl', 'xh'), pairs)  3.49 us
    ppermute x1, waiting for transfers between devices, shards(): pair_seen = lax.ppermute(pair_index, 'xl', SWAP)  3.2 us
  transfers between devices with their start and end apart: 35, of which 18 were waited for; matrix products, arithmetic and copies ran while one was open for 0% of the time, Pallas kernels for 2%

profile of v7, /device:TPU:32, one launch (start us, length us, event | category | flops | bytes accessed | tf_op | source)
XLA Modules:
  0.0 109.7 jit_solution(15755013904615455488)
XLA Ops:
  0.6 6.4 %collective-permute-start = (bf16[48,1024]{1,0:T(8,128)(2,1)}, bf16[48,1024]{1,0:T(8,128)(2,1)S(1)}, u32[]{:S(2)}, u32[]{:S(2)}) collective-permute-start(bf16[48,1024]{1,0:T(8,128)(2,1)} %near.1), channel_id=1, source_target_pairs={{0,64},{16,80},{32,96},{48,112},{64,0},{80,16},{96,32},{112,48},{1... | collective-permute-start | bytes 294920 | tf_op jit(solution)/shard_map/ppermute | solution.py:19
  7.0 1.5 %collective-permute-start.3 = (bf16[48,1024]{1,0:T(8,128)(2,1)}, bf16[48,1024]{1,0:T(8,128)(2,1)S(1)}, u32[]{:S(2)}, u32[]{:S(2)}) collective-permute-start(bf16[48,1024]{1,0:T(8,128)(2,1)} %refs_0_.1), channel_id=1, source_target_pairs={{0,128},{128,1},{1,129},{129,0},{2,130},{130,3},{3,131},{131,2},{4... | collective-permute-start | bytes 294920 | tf_op jit(solution)/shard_map/ppermute | solution.py:27
  8.5 1.7 %collective-permute-start.2 = (bf16[48,1024]{1,0:T(8,128)(2,1)}, bf16[48,1024]{1,0:T(8,128)(2,1)S(1)}, u32[]{:S(2)}, u32[]{:S(2)}) collective-permute-start(bf16[48,1024]{1,0:T(8,128)(2,1)} %refs_0_.1), channel_id=1, source_target_pairs={{0,129},{128,0},{1,128},{129,1},{2,131},{130,2},{3,130},{131,3},{4... | collective-permute-start | bytes 294920 | tf_op jit(solution)/shard_map/ppermute | solution.py:27
  10.2 1.8 %collective-permute-start.4 = (bf16[48,1024]{1,0:T(8,128)(2,1)}, bf16[48,1024]{1,0:T(8,128)(2,1)S(1)}, u32[]{:S(2)}, u32[]{:S(2)}) collective-permute-start(bf16[48,1024]{1,0:T(8,128)(2,1)} %refs_0_.1), channel_id=1, source_target_pairs={{0,1},{128,129},{1,0},{129,128},{2,3},{130,131},{3,2},{131,130},{4... | collective-permute-start | bytes 294920 | tf_op jit(solution)/shard_map/ppermute | solution.py:27
  12.7 3.2 %collective-permute-done.1.seen = s32[384]{0:T(512)S(1)} collective-permute-done((s32[384]{0:T(512)}, s32[384]{0:T(512)S(1)}, u32[]{:S(2)}, u32[]{:S(2)}) %collective-permute-start.1) | collective-permute-done | bytes 1568 | tf_op jit(solution)/shard_map/ppermute | solution.py:327
  15.9 0.7 collective-permute-done.4.refs_3_
  16.6 0.9 copy-done
  17.5 0.9 copy-done.1
  18.4 0.7 copy-done.2
  19.1 1.1 collective-permute-start.7
  20.2 2.7 %collective-permute-start.6 = (bf16[96,1024]{1,0:T(8,128)(2,1)S(1)}, bf16[96,1024]{1,0:T(8,128)(2,1)S(1)}, u32[]{:S(2)}, u32[]{:S(2)}) collective-permute-start(bf16[96,1024]{1,0:T(8,128)(2,1)S(1)} %get-tuple-element.36.refs_0_), channel_id=1, source_target_pairs={{0,96},{16,112},{32,0},{48,16},{64,32},{80,48},{96,64},{112,80},{1... | collective-permute-start | bytes 589832 | tf_op jit(solution)/shard_map/ppermute | solution.py:19
  22.9 3.2 %collective-permute-start.14 = (bf16[192,1024]{1,0:T(8,128)(2,1)S(1)}, bf16[192,1024]{1,0:T(8,128)(2,1)S(1)}, u32[]{:S(2)}, u32[]{:S(2)}) collective-permute-start(bf16[192,1024]{1,0:T(8,128)(2,1)S(1)} %get-tuple-element.37.refs_8_), channel_id=1, source_target_pairs={{0,4},{2,6},{4,0},{6,2},{1,5},{3,7},{5,1},{7,3},{8,12},{10,14},{12... | collective-permute-start | bytes 1179656 | tf_op jit(solution)/shard_map/ppermute | solution.py:19
  26.1 0.8 collective-permute-start.13
  26.8 4.8 %collective-permute-done.6.refs_2_ = bf16[96,1024]{1,0:T(8,128)(2,1)S(1)} collective-permute-done((bf16[96,1024]{1,0:T(8,128)(2,1)S(1)}, bf16[96,1024]{1,0:T(8,128)(2,1)S(1)}, u32[]{:S(2)}, u32[]{:S(2)}) %collective-permute-start.6) | collective-permute-done | bytes 196640 | tf_op jit(solution)/shard_map/ppermute | solution.py:19
  31.6 3.0 %collective-permute-start.12 = (bf16[192,1024]{1,0:T(8,128)(2,1)S(1)}, bf16[192,1024]{1,0:T(8,128)(2,1)S(1)}, u32[]{:S(2)}, u32[]{:S(2)}) collective-permute-start(bf16[192,1024]{1,0:T(8,128)(2,1)S(1)} %get-tuple-element.37.refs_8_), channel_id=1, source_target_pairs={{0,6},{2,0},{4,2},{6,4},{1,7},{3,1},{5,3},{7,5},{8,14},{10,8},{12,... | collective-permute-start | bytes 1179656 | tf_op jit(solution)/shard_map/ppermute | solution.py:19
  34.6 1.7 %collective-permute-done.5.refs_1_ = bf16[96,1024]{1,0:T(8,128)(2,1)S(1)} collective-permute-done((bf16[96,1024]{1,0:T(8,128)(2,1)S(1)}, bf16[96,1024]{1,0:T(8,128)(2,1)S(1)}, u32[]{:S(2)}, u32[]{:S(2)}) %collective-permute-start.5) | collective-permute-done | bytes 196640 | tf_op jit(solution)/shard_map/ppermute | solution.py:19
  36.9 0.9 collective-permute-done.10.refs_6_
  38.1 5.9 %collective-permute-done.13.refs_10_ = bf16[192,1024]{1,0:T(8,128)(2,1)S(1)} collective-permute-done((bf16[192,1024]{1,0:T(8,128)(2,1)S(1)}, bf16[192,1024]{1,0:T(8,128)(2,1)S(1)}, u32[]{:S(2)}, u32[]{:S(2)}) %collective-permute-start.13) | collective-permute-done | bytes 393248 | tf_op jit(solution)/shard_map/ppermute | solution.py:19
  44.4 3.1 %scores.1 = (f32[768,768]{1,0:T(8,128)S(1)}, bf16[768,1024]{1,0:T(8,128)(2,1)S(1)}, bf16[768,1024]{1,0:T(8,128)(2,1)S(1)}, f32[1,896]{1,0:T(1,128)S(1)}, f32[1,1024]{1,0:T(1,128)S(1)}) custom-call(bf16[96,1024]{1,0:T(8,128)(2,1)S(1)} %get-tuple-element.36.refs_0_, bf16[96,1024]{1,0:T(8,128)(2,1)S(1)} %collective-permute-done.5.refs_1_, ...), custom_call_target="tpu_custom_call" | custom-call | flops 1207959552 | bytes 8661504 | tf_op jit(solution)/shard_map/scores/pallas_call | solution.py:80
  48.1 0.7 collective-permute-done.15.seen
  48.8 0.6 collective-permute-start.16
  49.4 1.9 %collective-permute-done.19.seen = f32[1,896]{1,0:T(1,128)S(1)} collective-permute-done((f32[1,896]{1,0:T(1,128)S(1)}, f32[1,896]{1,0:T(1,128)S(1)}, u32[]{:S(2)}, u32[]{:S(2)}) %collective-permute-start.19) | collective-permute-done | bytes 3616 | tf_op jit(solution)/shard_map/ppermute | solution.py:364
  51.3 1.9 %collective-permute-start.20 = (f32[1,896]{1,0:T(1,128)S(1)}, f32[1,896]{1,0:T(1,128)S(1)}, u32[]{:S(2)}, u32[]{:S(2)}) collective-permute-start(f32[1,896]{1,0:T(1,128)S(1)} %pair.12.mine), channel_id=1, source_target_pairs={{0,1},{1,0},{2,3},{3,2},{4,5},{5,4},{6,7},{7,6},{8,9},{9,8},{10,11... | collective-permute-start | bytes 10760 | tf_op jit(solution)/shard_map/ppermute | solution.py:364
  53.2 2.0 %collective-permute-start.17 = (f32[1,1024]{1,0:T(1,128)S(1)}, f32[1,1024]{1,0:T(1,128)S(1)}, u32[]{:S(2)}, u32[]{:S(2)}) collective-permute-start(f32[1,1024]{1,0:T(1,128)S(1)} %pair.9.mine), channel_id=1, source_target_pairs={{0,32},{16,48},{32,0},{48,16},{64,96},{80,112},{96,64},{112,80},{1... | collective-permute-start | bytes 12296 | tf_op jit(solution)/shard_map/ppermute | solution.py:364
  55.2 1.3 %collective-permute-done.20.seen = f32[1,896]{1,0:T(1,128)S(1)} collective-permute-done((f32[1,896]{1,0:T(1,128)S(1)}, f32[1,896]{1,0:T(1,128)S(1)}, u32[]{:S(2)}, u32[]{:S(2)}) %collective-permute-start.20) | collective-permute-done | bytes 3616 | tf_op jit(solution)/shard_map/ppermute | solution.py:364
  56.5 1.5 %collective-permute-start.21 = (f32[1,896]{1,0:T(1,128)S(1)}, f32[1,896]{1,0:T(1,128)S(1)}, u32[]{:S(2)}, u32[]{:S(2)}) collective-permute-start(f32[1,896]{1,0:T(1,128)S(1)} %pair.13.mine), channel_id=1, source_target_pairs={{0,2},{2,0},{4,6},{6,4},{1,3},{3,1},{5,7},{7,5},{8,10},{10,8},{12,... | collective-permute-start | bytes 10760 | tf_op jit(solution)/shard_map/ppermute | solution.py:364
  58.0 3.2 %collective-permute-start.18 = (f32[1,1024]{1,0:T(1,128)S(1)}, f32[1,1024]{1,0:T(1,128)S(1)}, u32[]{:S(2)}, u32[]{:S(2)}) collective-permute-start(f32[1,1024]{1,0:T(1,128)S(1)} %pair.10.mine), channel_id=1, source_target_pairs={{0,64},{16,80},{32,96},{48,112},{64,0},{80,16},{96,32},{112,48},{1... | collective-permute-start | bytes 12296 | tf_op jit(solution)/shard_map/ppermute | solution.py:364
  61.2 3.4 %collective-permute-start.22 = (f32[1,896]{1,0:T(1,128)S(1)}, f32[1,896]{1,0:T(1,128)S(1)}, u32[]{:S(2)}, u32[]{:S(2)}) collective-permute-start(f32[1,896]{1,0:T(1,128)S(1)} %pair.14.mine), channel_id=1, source_target_pairs={{0,4},{2,6},{4,0},{6,2},{1,5},{3,7},{5,1},{7,3},{8,12},{10,14},{12... | collective-permute-start | bytes 10760 | tf_op jit(solution)/shard_map/ppermute | solution.py:364
  64.6 1.8 %collective-permute-done.22.seen = f32[1,896]{1,0:T(1,128)S(1)} collective-permute-done((f32[1,896]{1,0:T(1,128)S(1)}, f32[1,896]{1,0:T(1,128)S(1)}, u32[]{:S(2)}, u32[]{:S(2)}) %collective-permute-start.22) | collective-permute-done | bytes 3616 | tf_op jit(solution)/shard_map/ppermute | solution.py:364
  66.4 2.6 %image_grad.1 = (bf16[768,768]{1,0:T(8,128)(2,1)S(1)}, f32[8,128]{1,0:T(8,128)S(1)}, f32[192,1024]{1,0:T(8,128)S(1)}, bf16[1552,128]{1,0:T(8,128)(2,1)S(1)}, bf1...) custom-call(f32[1,1024]{1,0:T(1,128)S(1)} %pair.11.cols, f32[1,896]{1,0:T(1,128)S(1)} %pair.15.rows_lse, ...), custom_call_target="tpu_custom_call" | custom-call | flops 1207959552 | bytes 7105024 | tf_op jit(solution)/shard_map/image_grad/pallas_call | solution.py:80
  69.1 1.4 %text_grad.1 = (f32[384,1024]{1,0:T(8,128)S(1)}, f32[384,1024]{1,0:T(8,128)S(1)}) custom-call(bf16[768,768]{1,0:T(8,128)(2,1)S(1)} %get-tuple-element.43.grads, bf16[768,1024]{1,0:T(8,128)(2,1)S(1)} %get-tuple-element.44.image), custom_call_target="tpu_custom_call" | custom-call | flops 10000000000 | bytes 5898240 | tf_op jit(solution)/shard_map/text_grad/pallas_call | solution.py:80
  70.6 1.3 %collective-permute-start.28 = (bf16[1552,128]{1,0:T(8,128)(2,1)S(1)}, bf16[1552,128]{1,0:T(8,128)(2,1)S(1)}, u32[]{:S(2)}, u32[]{:S(2)}) collective-permute-start(bf16[1552,128]{1,0:T(8,128)(2,1)S(1)} %get-tuple-element.56), channel_id=1, source_target_pairs={{0,2},{2,4},{4,6},{6,0},{1,3},{3,5},{5,7},{7,1},{8,10},{10,12},{12... | collective-permute-start | bytes 1191944 | tf_op jit(solution)/shard_map/ppermute | solution.py:19
  71.9 2.1 %collective-permute-start.29 = (bf16[1552,128]{1,0:T(8,128)(2,1)S(1)}, bf16[1552,128]{1,0:T(8,128)(2,1)S(1)}, u32[]{:S(2)}, u32[]{:S(2)}) collective-permute-start(bf16[1552,128]{1,0:T(8,128)(2,1)S(1)} %get-tuple-element.57), channel_id=1, source_target_pairs={{0,6},{2,0},{4,2},{6,4},{1,7},{3,1},{5,3},{7,5},{8,14},{10,8},{12,... | collective-permute-start | bytes 1191944 | tf_op jit(solution)/shard_map/ppermute | solution.py:19
  73.9 2.1 %collective-permute-start.30 = (bf16[1552,128]{1,0:T(8,128)(2,1)S(1)}, bf16[1552,128]{1,0:T(8,128)(2,1)S(1)}, u32[]{:S(2)}, u32[]{:S(2)}) collective-permute-start(bf16[1552,128]{1,0:T(8,128)(2,1)S(1)} %get-tuple-element.58), channel_id=1, source_target_pairs={{0,4},{2,6},{4,0},{6,2},{1,5},{3,7},{5,1},{7,3},{8,12},{10,14},{12... | collective-permute-start | bytes 1191944 | tf_op jit(solution)/shard_map/ppermute | solution.py:19
  76.0 1.2 %collective-permute-done.24.terms_seen = f32[8,128]{1,0:T(8,128)S(1)} collective-permute-done((f32[8,128]{1,0:T(8,128)S(1)}, f32[8,128]{1,0:T(8,128)S(1)}, u32[]{:S(2)}, u32[]{:S(2)}) %collective-permute-start.24) | collective-permute-done | bytes 4128 | tf_op jit(solution)/shard_map/ppermute | solution.py:399
  77.6 1.5 %collective-permute-start.25 = (bf16[784,128]{1,0:T(8,128)(2,1)S(1)}, bf16[784,128]{1,0:T(8,128)(2,1)S(1)}, u32[]{:S(2)}, u32[]{:S(2)}) collective-permute-start(bf16[784,128]{1,0:T(8,128)(2,1)S(1)} %get-tuple-element.50), channel_id=1, source_target_pairs={{0,16},{16,32},{32,48},{48,64},{64,80},{80,96},{96,112},{112,0},{1... | collective-permute-start | bytes 602120 | tf_op jit(solution)/shard_map/ppermute | solution.py:19
  79.1 1.5 %collective-permute-start.26 = (bf16[784,128]{1,0:T(8,128)(2,1)S(1)}, bf16[784,128]{1,0:T(8,128)(2,1)S(1)}, u32[]{:S(2)}, u32[]{:S(2)}) collective-permute-start(bf16[784,128]{1,0:T(8,128)(2,1)S(1)} %get-tuple-element.51), channel_id=1, source_target_pairs={{0,32},{16,48},{32,64},{48,80},{64,96},{80,112},{96,0},{112,16},{1... | collective-permute-start | bytes 602120 | tf_op jit(solution)/shard_map/ppermute | solution.py:19
  80.7 2.8 %collective-permute-done.28.refs_0_ = bf16[1552,128]{1,0:T(8,128)(2,1)S(1)} collective-permute-done((bf16[1552,128]{1,0:T(8,128)(2,1)S(1)}, bf16[1552,128]{1,0:T(8,128)(2,1)S(1)}, u32[]{:S(2)}, u32[]{:S(2)}) %collective-permute-start.28) | collective-permute-done | bytes 397344 | tf_op jit(solution)/shard_map/ppermute | solution.py:19
  83.4 1.0 collective-permute-start.27
  84.4 8.7 %collective-permute-done.30.refs_2_ = bf16[1552,128]{1,0:T(8,128)(2,1)S(1)} collective-permute-done((bf16[1552,128]{1,0:T(8,128)(2,1)S(1)}, bf16[1552,128]{1,0:T(8,128)(2,1)S(1)}, u32[]{:S(2)}, u32[]{:S(2)}) %collective-permute-start.30) | collective-permute-done | bytes 397344 | tf_op jit(solution)/shard_map/ppermute | solution.py:19
  93.1 0.8 image_relay.1
  93.9 0.9 collective-permute-start.31
  94.8 2.4 %collective-permute-start.32 = (bf16[400,128]{1,0:T(8,128)(2,1)S(1)}, bf16[400,128]{1,0:T(8,128)(2,1)S(1)}, u32[]{:S(2)}, u32[]{:S(2)}) collective-permute-start(bf16[400,128]{1,0:T(8,128)(2,1)S(1)} %get-tuple-element.62), channel_id=1, source_target_pairs={{0,129},{128,0},{1,128},{129,1},{2,131},{130,2},{3,130},{131,3},{4... | collective-permute-start | bytes 307208 | tf_op jit(solution)/shard_map/ppermute | solution.py:27
  98.2 2.4 %collective-permute-start.34 = (bf16[400,128]{1,0:T(8,128)(2,1)S(1)}, bf16[400,128]{1,0:T(8,128)(2,1)S(1)}, u32[]{:S(2)}, u32[]{:S(2)}) collective-permute-start(bf16[400,128]{1,0:T(8,128)(2,1)S(1)} %get-tuple-element.65), channel_id=1, source_target_pairs={{0,64},{16,80},{32,96},{48,112},{64,0},{80,16},{96,32},{112,48},{1... | collective-permute-start | bytes 307208 | tf_op jit(solution)/shard_map/ppermute | solution.py:19
  101.1 2.3 %collective-permute-done.33.refs_2_ = bf16[400,128]{1,0:T(8,128)(2,1)S(1)} collective-permute-done((bf16[400,128]{1,0:T(8,128)(2,1)S(1)}, bf16[400,128]{1,0:T(8,128)(2,1)S(1)}, u32[]{:S(2)}, u32[]{:S(2)}) %collective-permute-start.33) | collective-permute-done | bytes 102432 | tf_op jit(solution)/shard_map/ppermute | solution.py:27
  103.4 0.9 image_sum.1
  104.3 4.4 %collective-permute-done.34.pay = bf16[400,128]{1,0:T(8,128)(2,1)S(1)} collective-permute-done((bf16[400,128]{1,0:T(8,128)(2,1)S(1)}, bf16[400,128]{1,0:T(8,128)(2,1)S(1)}, u32[]{:S(2)}, u32[]{:S(2)}) %collective-permute-start.34) | collective-permute-done | bytes 102432 | tf_op jit(solution)/shard_map/ppermute | solution.py:19
  108.7 0.8 text_sum.1
  (45 shorter events, 4.6 us)
Async XLA Ops:
  0.6 15.2 %collective-permute-start = (bf16[48,1024]{1,0:T(8,128)(2,1)}, bf16[48,1024]{1,0:T(8,128)(2,1)S(1)}, u32[]{:S(2)}, u32[]{:S(2)}) collective-permute-start(bf16[48,1024]{1,0:T(8,128)(2,1)} %near.1), channel_id=1, source_target_pairs={{0,64},{16,80},{32,96},{48,112},{64,0},{80,16},{96,32},{112,48},{1... | collective-permute-start | bytes 294920 | tf_op jit(solution)/shard_map/ppermute | solution.py:19
  7.0 8.9 %collective-permute-start.3 = (bf16[48,1024]{1,0:T(8,128)(2,1)}, bf16[48,1024]{1,0:T(8,128)(2,1)S(1)}, u32[]{:S(2)}, u32[]{:S(2)}) collective-permute-start(bf16[48,1024]{1,0:T(8,128)(2,1)} %refs_0_.1), channel_id=1, source_target_pairs={{0,128},{128,1},{1,129},{129,0},{2,130},{130,3},{3,131},{131,2},{4... | collective-permute-start | bytes 294920 | tf_op jit(solution)/shard_map/ppermute | solution.py:27
  8.5 7.4 %collective-permute-start.2 = (bf16[48,1024]{1,0:T(8,128)(2,1)}, bf16[48,1024]{1,0:T(8,128)(2,1)S(1)}, u32[]{:S(2)}, u32[]{:S(2)}) collective-permute-start(bf16[48,1024]{1,0:T(8,128)(2,1)} %refs_0_.1), channel_id=1, source_target_pairs={{0,129},{128,0},{1,128},{129,1},{2,131},{130,2},{3,130},{131,3},{4... | collective-permute-start | bytes 294920 | tf_op jit(solution)/shard_map/ppermute | solution.py:27
  10.2 6.3 %collective-permute-start.4 = (bf16[48,1024]{1,0:T(8,128)(2,1)}, bf16[48,1024]{1,0:T(8,128)(2,1)S(1)}, u32[]{:S(2)}, u32[]{:S(2)}) collective-permute-start(bf16[48,1024]{1,0:T(8,128)(2,1)} %refs_0_.1), channel_id=1, source_target_pairs={{0,1},{128,129},{1,0},{129,128},{2,3},{130,131},{3,2},{131,130},{4... | collective-permute-start | bytes 294920 | tf_op jit(solution)/shard_map/ppermute | solution.py:27
  12.1 3.8 %collective-permute-start.1 = (s32[384]{0:T(512)}, s32[384]{0:T(512)S(1)}, u32[]{:S(2)}, u32[]{:S(2)}) collective-permute-start(s32[384]{0:T(512)} %mine.1), channel_id=1, source_target_pairs={{0,128},{128,0},{1,129},{129,1},{2,130},{130,2},{3,131},{131,3},{4... | collective-permute-start | bytes 4616 | tf_op jit(solution)/shard_map/ppermute | solution.py:327
  16.6 0.9 copy-start
  17.5 0.9 copy-start.1
  18.4 0.7 copy-start.2
  19.1 7.0 %collective-permute-start.7 = (bf16[96,1024]{1,0:T(8,128)(2,1)S(1)}, bf16[96,1024]{1,0:T(8,128)(2,1)S(1)}, u32[]{:S(2)}, u32[]{:S(2)}) collective-permute-start(bf16[96,1024]{1,0:T(8,128)(2,1)S(1)} %get-tuple-element.36.refs_0_), channel_id=1, source_target_pairs={{0,16},{16,32},{32,48},{48,64},{64,80},{80,96},{96,112},{112,0},{1... | collective-permute-start | bytes 589832 | tf_op jit(solution)/shard_map/ppermute | solution.py:19
  20.2 5.9 %collective-permute-start.8 = (bf16[96,1024]{1,0:T(8,128)(2,1)S(1)}, bf16[96,1024]{1,0:T(8,128)(2,1)S(1)}, u32[]{:S(2)}, u32[]{:S(2)}) collective-permute-start(bf16[96,1024]{1,0:T(8,128)(2,1)S(1)} %get-tuple-element.36.refs_0_), channel_id=1, source_target_pairs={{0,8},{8,0},{1,9},{9,1},{2,10},{10,2},{3,11},{11,3},{4,12},{12,4},... | collective-permute-start | bytes 589832 | tf_op jit(solution)/shard_map/ppermute | solution.py:345
  20.2 11.4 %collective-permute-start.6 = (bf16[96,1024]{1,0:T(8,128)(2,1)S(1)}, bf16[96,1024]{1,0:T(8,128)(2,1)S(1)}, u32[]{:S(2)}, u32[]{:S(2)}) collective-permute-start(bf16[96,1024]{1,0:T(8,128)(2,1)S(1)} %get-tuple-element.36.refs_0_), channel_id=1, source_target_pairs={{0,96},{16,112},{32,0},{48,16},{64,32},{80,48},{96,64},{112,80},{1... | collective-permute-start | bytes 589832 | tf_op jit(solution)/shard_map/ppermute | solution.py:19
  22.9 13.5 %collective-permute-start.5 = (bf16[96,1024]{1,0:T(8,128)(2,1)S(1)}, bf16[96,1024]{1,0:T(8,128)(2,1)S(1)}, u32[]{:S(2)}, u32[]{:S(2)}) collective-permute-start(bf16[96,1024]{1,0:T(8,128)(2,1)S(1)} %get-tuple-element.36.refs_0_), channel_id=1, source_target_pairs={{0,112},{16,0},{32,16},{48,32},{64,48},{80,64},{96,80},{112,96},{1... | collective-permute-start | bytes 589832 | tf_op jit(solution)/shard_map/ppermute | solution.py:19
  22.9 15.2 %collective-permute-start.14 = (bf16[192,1024]{1,0:T(8,128)(2,1)S(1)}, bf16[192,1024]{1,0:T(8,128)(2,1)S(1)}, u32[]{:S(2)}, u32[]{:S(2)}) collective-permute-start(bf16[192,1024]{1,0:T(8,128)(2,1)S(1)} %get-tuple-element.37.refs_8_), channel_id=1, source_target_pairs={{0,4},{2,6},{4,0},{6,2},{1,5},{3,7},{5,1},{7,3},{8,12},{10,14},{12... | collective-permute-start | bytes 1179656 | tf_op jit(solution)/shard_map/ppermute | solution.py:19
  26.1 10.3 %collective-permute-start.11 = (bf16[96,1024]{1,0:T(8,128)(2,1)S(1)}, bf16[96,1024]{1,0:T(8,128)(2,1)S(1)}, u32[]{:S(2)}, u32[]{:S(2)}) collective-permute-start(bf16[96,1024]{1,0:T(8,128)(2,1)S(1)} %collective-permute-done.7.refs_3_), channel_id=1, source_target_pairs={{0,8},{8,0},{1,9},{9,1},{2,10},{10,2},{3,11},{11,3},{4,12},{12,4},... | collective-permute-start | bytes 589832 | tf_op jit(solution)/shard_map/ppermute | solution.py:345
  26.1 18.0 %collective-permute-start.13 = (bf16[192,1024]{1,0:T(8,128)(2,1)S(1)}, bf16[192,1024]{1,0:T(8,128)(2,1)S(1)}, u32[]{:S(2)}, u32[]{:S(2)}) collective-permute-start(bf16[192,1024]{1,0:T(8,128)(2,1)S(1)} %get-tuple-element.37.refs_8_), channel_id=1, source_target_pairs={{0,2},{2,4},{4,6},{6,0},{1,3},{3,5},{5,7},{7,1},{8,10},{10,12},{12... | collective-permute-start | bytes 1179656 | tf_op jit(solution)/shard_map/ppermute | solution.py:19
  31.6 12.8 %collective-permute-start.12 = (bf16[192,1024]{1,0:T(8,128)(2,1)S(1)}, bf16[192,1024]{1,0:T(8,128)(2,1)S(1)}, u32[]{:S(2)}, u32[]{:S(2)}) collective-permute-start(bf16[192,1024]{1,0:T(8,128)(2,1)S(1)} %get-tuple-element.37.refs_8_), channel_id=1, source_target_pairs={{0,6},{2,0},{4,2},{6,4},{1,7},{3,1},{5,3},{7,5},{8,14},{10,8},{12,... | collective-permute-start | bytes 1179656 | tf_op jit(solution)/shard_map/ppermute | solution.py:19
  36.4 1.4 %collective-permute-start.10 = (bf16[96,1024]{1,0:T(8,128)(2,1)S(1)}, bf16[96,1024]{1,0:T(8,128)(2,1)S(1)}, u32[]{:S(2)}, u32[]{:S(2)}) collective-permute-start(bf16[96,1024]{1,0:T(8,128)(2,1)S(1)} %collective-permute-done.6.refs_2_), channel_id=1, source_target_pairs={{0,8},{8,0},{1,9},{9,1},{2,10},{10,2},{3,11},{11,3},{4,12},{12,4},... | collective-permute-start | bytes 589832 | tf_op jit(solution)/shard_map/ppermute | solution.py:345
  36.4 1.7 %collective-permute-start.9 = (bf16[96,1024]{1,0:T(8,128)(2,1)S(1)}, bf16[96,1024]{1,0:T(8,128)(2,1)S(1)}, u32[]{:S(2)}, u32[]{:S(2)}) collective-permute-start(bf16[96,1024]{1,0:T(8,128)(2,1)S(1)} %collective-permute-done.5.refs_1_), channel_id=1, source_target_pairs={{0,8},{8,0},{1,9},{9,1},{2,10},{10,2},{3,11},{11,3},{4,12},{12,4},... | collective-permute-start | bytes 589832 | tf_op jit(solution)/shard_map/ppermute | solution.py:345
  47.5 1.3 %collective-permute-start.15 = (f32[1,1024]{1,0:T(1,128)S(1)}, f32[1,1024]{1,0:T(1,128)S(1)}, u32[]{:S(2)}, u32[]{:S(2)}) collective-permute-start(f32[1,1024]{1,0:T(1,128)S(1)} %get-tuple-element.39.mine), channel_id=1, source_target_pairs={{0,8},{8,0},{1,9},{9,1},{2,10},{10,2},{3,11},{11,3},{4,12},{12,4},... | collective-permute-start | bytes 12296 | tf_op jit(solution)/shard_map/ppermute | solution.py:364
  47.6 3.7 %collective-permute-start.19 = (f32[1,896]{1,0:T(1,128)S(1)}, f32[1,896]{1,0:T(1,128)S(1)}, u32[]{:S(2)}, u32[]{:S(2)}) collective-permute-start(f32[1,896]{1,0:T(1,128)S(1)} %get-tuple-element.40.mine), channel_id=1, source_target_pairs={{0,128},{128,0},{1,129},{129,1},{2,130},{130,2},{3,131},{131,3},{4... | collective-permute-start | bytes 10760 | tf_op jit(solution)/shard_map/ppermute | solution.py:364
  48.8 4.4 %collective-permute-start.16 = (f32[1,1024]{1,0:T(1,128)S(1)}, f32[1,1024]{1,0:T(1,128)S(1)}, u32[]{:S(2)}, u32[]{:S(2)}) collective-permute-start(f32[1,1024]{1,0:T(1,128)S(1)} %pair.8.mine), channel_id=1, source_target_pairs={{0,16},{16,0},{32,48},{48,32},{64,80},{80,64},{96,112},{112,96},{1... | collective-permute-start | bytes 12296 | tf_op jit(solution)/shard_map/ppermute | solution.py:364
  51.3 5.2 %collective-permute-start.20 = (f32[1,896]{1,0:T(1,128)S(1)}, f32[1,896]{1,0:T(1,128)S(1)}, u32[]{:S(2)}, u32[]{:S(2)}) collective-permute-start(f32[1,896]{1,0:T(1,128)S(1)} %pair.12.mine), channel_id=1, source_target_pairs={{0,1},{1,0},{2,3},{3,2},{4,5},{5,4},{6,7},{7,6},{8,9},{9,8},{10,11... | collective-permute-start | bytes 10760 | tf_op jit(solution)/shard_map/ppermute | solution.py:364
  53.2 4.8 %collective-permute-start.17 = (f32[1,1024]{1,0:T(1,128)S(1)}, f32[1,1024]{1,0:T(1,128)S(1)}, u32[]{:S(2)}, u32[]{:S(2)}) collective-permute-start(f32[1,1024]{1,0:T(1,128)S(1)} %pair.9.mine), channel_id=1, source_target_pairs={{0,32},{16,48},{32,0},{48,16},{64,96},{80,112},{96,64},{112,80},{1... | collective-permute-start | bytes 12296 | tf_op jit(solution)/shard_map/ppermute | solution.py:364
  56.5 4.7 %collective-permute-start.21 = (f32[1,896]{1,0:T(1,128)S(1)}, f32[1,896]{1,0:T(1,128)S(1)}, u32[]{:S(2)}, u32[]{:S(2)}) collective-permute-start(f32[1,896]{1,0:T(1,128)S(1)} %pair.13.mine), channel_id=1, source_target_pairs={{0,2},{2,0},{4,6},{6,4},{1,3},{3,1},{5,7},{7,5},{8,10},{10,8},{12,... | collective-permute-start | bytes 10760 | tf_op jit(solution)/shard_map/ppermute | solution.py:364
  58.0 8.4 %collective-permute-start.18 = (f32[1,1024]{1,0:T(1,128)S(1)}, f32[1,1024]{1,0:T(1,128)S(1)}, u32[]{:S(2)}, u32[]{:S(2)}) collective-permute-start(f32[1,1024]{1,0:T(1,128)S(1)} %pair.10.mine), channel_id=1, source_target_pairs={{0,64},{16,80},{32,96},{48,112},{64,0},{80,16},{96,32},{112,48},{1... | collective-permute-start | bytes 12296 | tf_op jit(solution)/shard_map/ppermute | solution.py:364
  61.2 5.2 %collective-permute-start.22 = (f32[1,896]{1,0:T(1,128)S(1)}, f32[1,896]{1,0:T(1,128)S(1)}, u32[]{:S(2)}, u32[]{:S(2)}) collective-permute-start(f32[1,896]{1,0:T(1,128)S(1)} %pair.14.mine), channel_id=1, source_target_pairs={{0,4},{2,6},{4,0},{6,2},{1,5},{3,7},{5,1},{7,3},{8,12},{10,14},{12... | collective-permute-start | bytes 10760 | tf_op jit(solution)/shard_map/ppermute | solution.py:364
  70.5 6.7 %collective-permute-start.23 = (f32[384,1024]{1,0:T(8,128)S(1)}, f32[384,1024]{1,0:T(8,128)S(1)}, u32[]{:S(2)}, u32[]{:S(2)}) collective-permute-start(f32[384,1024]{1,0:T(8,128)S(1)} %get-tuple-element.46), channel_id=1, source_target_pairs={{0,8},{8,0},{1,9},{9,1},{2,10},{10,2},{3,11},{11,3},{4,12},{12,4},... | collective-permute-start | bytes 4718600 | tf_op jit(solution)/shard_map/ppermute | solution.py:399
  70.6 12.8 %collective-permute-start.28 = (bf16[1552,128]{1,0:T(8,128)(2,1)S(1)}, bf16[1552,128]{1,0:T(8,128)(2,1)S(1)}, u32[]{:S(2)}, u32[]{:S(2)}) collective-permute-start(bf16[1552,128]{1,0:T(8,128)(2,1)S(1)} %get-tuple-element.56), channel_id=1, source_target_pairs={{0,2},{2,4},{4,6},{6,0},{1,3},{3,5},{5,7},{7,1},{8,10},{10,12},{12... | collective-permute-start | bytes 1191944 | tf_op jit(solution)/shard_map/ppermute | solution.py:19
  71.9 12.6 %collective-permute-start.29 = (bf16[1552,128]{1,0:T(8,128)(2,1)S(1)}, bf16[1552,128]{1,0:T(8,128)(2,1)S(1)}, u32[]{:S(2)}, u32[]{:S(2)}) collective-permute-start(bf16[1552,128]{1,0:T(8,128)(2,1)S(1)} %get-tuple-element.57), channel_id=1, source_target_pairs={{0,6},{2,0},{4,2},{6,4},{1,7},{3,1},{5,3},{7,5},{8,14},{10,8},{12,... | collective-permute-start | bytes 1191944 | tf_op jit(solution)/shard_map/ppermute | solution.py:19
  73.9 19.2 %collective-permute-start.30 = (bf16[1552,128]{1,0:T(8,128)(2,1)S(1)}, bf16[1552,128]{1,0:T(8,128)(2,1)S(1)}, u32[]{:S(2)}, u32[]{:S(2)}) collective-permute-start(bf16[1552,128]{1,0:T(8,128)(2,1)S(1)} %get-tuple-element.58), channel_id=1, source_target_pairs={{0,4},{2,6},{4,0},{6,2},{1,5},{3,7},{5,1},{7,3},{8,12},{10,14},{12... | collective-permute-start | bytes 1191944 | tf_op jit(solution)/shard_map/ppermute | solution.py:19
  76.0 1.2 %collective-permute-start.24 = (f32[8,128]{1,0:T(8,128)S(1)}, f32[8,128]{1,0:T(8,128)S(1)}, u32[]{:S(2)}, u32[]{:S(2)}) collective-permute-start(f32[8,128]{1,0:T(8,128)S(1)} %get-tuple-element.47.terms.total), channel_id=1, source_target_pairs={{0,8},{8,0},{1,9},{9,1},{2,10},{10,2},{3,11},{11,3},{4,12},{12,4},... | collective-permute-start | bytes 12296 | tf_op jit(solution)/shard_map/ppermute | solution.py:399
  77.6 19.6 %collective-permute-start.25 = (bf16[784,128]{1,0:T(8,128)(2,1)S(1)}, bf16[784,128]{1,0:T(8,128)(2,1)S(1)}, u32[]{:S(2)}, u32[]{:S(2)}) collective-permute-start(bf16[784,128]{1,0:T(8,128)(2,1)S(1)} %get-tuple-element.50), channel_id=1, source_target_pairs={{0,16},{16,32},{32,48},{48,64},{64,80},{80,96},{96,112},{112,0},{1... | collective-permute-start | bytes 602120 | tf_op jit(solution)/shard_map/ppermute | solution.py:19
  79.1 18.7 %collective-permute-start.26 = (bf16[784,128]{1,0:T(8,128)(2,1)S(1)}, bf16[784,128]{1,0:T(8,128)(2,1)S(1)}, u32[]{:S(2)}, u32[]{:S(2)}) collective-permute-start(bf16[784,128]{1,0:T(8,128)(2,1)S(1)} %get-tuple-element.51), channel_id=1, source_target_pairs={{0,32},{16,48},{32,64},{48,80},{64,96},{80,112},{96,0},{112,16},{1... | collective-permute-start | bytes 602120 | tf_op jit(solution)/shard_map/ppermute | solution.py:19
  83.4 14.4 %collective-permute-start.27 = (bf16[784,128]{1,0:T(8,128)(2,1)S(1)}, bf16[784,128]{1,0:T(8,128)(2,1)S(1)}, u32[]{:S(2)}, u32[]{:S(2)}) collective-permute-start(bf16[784,128]{1,0:T(8,128)(2,1)S(1)} %get-tuple-element.52), channel_id=1, source_target_pairs={{0,112},{16,0},{32,16},{48,32},{64,48},{80,64},{96,80},{112,96},{1... | collective-permute-start | bytes 602120 | tf_op jit(solution)/shard_map/ppermute | solution.py:19
  93.9 6.7 %collective-permute-start.31 = (bf16[400,128]{1,0:T(8,128)(2,1)S(1)}, bf16[400,128]{1,0:T(8,128)(2,1)S(1)}, u32[]{:S(2)}, u32[]{:S(2)}) collective-permute-start(bf16[400,128]{1,0:T(8,128)(2,1)S(1)} %get-tuple-element.61), channel_id=1, source_target_pairs={{0,128},{128,1},{1,129},{129,0},{2,130},{130,3},{3,131},{131,2},{4... | collective-permute-start | bytes 307208 | tf_op jit(solution)/shard_map/ppermute | solution.py:27
  94.8 6.3 %collective-permute-start.32 = (bf16[400,128]{1,0:T(8,128)(2,1)S(1)}, bf16[400,128]{1,0:T(8,128)(2,1)S(1)}, u32[]{:S(2)}, u32[]{:S(2)}) collective-permute-start(bf16[400,128]{1,0:T(8,128)(2,1)S(1)} %get-tuple-element.62), channel_id=1, source_target_pairs={{0,129},{128,0},{1,128},{129,1},{2,131},{130,2},{3,130},{131,3},{4... | collective-permute-start | bytes 307208 | tf_op jit(solution)/shard_map/ppermute | solution.py:27
  97.2 6.2 %collective-permute-start.33 = (bf16[400,128]{1,0:T(8,128)(2,1)S(1)}, bf16[400,128]{1,0:T(8,128)(2,1)S(1)}, u32[]{:S(2)}, u32[]{:S(2)}) collective-permute-start(bf16[400,128]{1,0:T(8,128)(2,1)S(1)} %get-tuple-element.63), channel_id=1, source_target_pairs={{0,1},{128,129},{1,0},{129,128},{2,3},{130,131},{3,2},{131,130},{4... | collective-permute-start | bytes 307208 | tf_op jit(solution)/shard_map/ppermute | solution.py:27
  98.2 10.5 %collective-permute-start.34 = (bf16[400,128]{1,0:T(8,128)(2,1)S(1)}, bf16[400,128]{1,0:T(8,128)(2,1)S(1)}, u32[]{:S(2)}, u32[]{:S(2)}) collective-permute-start(bf16[400,128]{1,0:T(8,128)(2,1)S(1)} %get-tuple-element.65), channel_id=1, source_target_pairs={{0,64},{16,80},{32,96},{48,112},{64,0},{80,16},{96,32},{112,48},{1... | collective-permute-start | bytes 307208 | tf_op jit(solution)/shard_map/ppermute | solution.py:19

commit v8 on v6

--- a/solution.py
+++ b/solution.py
@@ -1,4 +1,5 @@
 import functools
+import math
 
 import jax
 import jax.numpy as jnp
@@ -58,15 +59,22 @@
     return jnp.transpose(jnp.broadcast_to(column, (column.shape[0], LANES)))[:1, :]
 
 
-def call(body, outs, args, name, flops=0, exps=0, smem_out=None, size=None):
+def call(
+    body, outs, args, name, flops=0, exps=0, smem_out=None, size=None, hbm_out=(), scratch=()
+):
     if size is None:
-        size = sum(a.size * a.dtype.itemsize for a in (*args, *outs))
-    spaces = [pltpu.SMEM if i == smem_out else pltpu.VMEM for i in range(len(outs))]
+        size = sum(math.prod(a.shape) * a.dtype.itemsize for a in (*args, *outs))
+    spaces = [pltpu.VMEM] * len(outs)
+    if smem_out is not None:
+        spaces[smem_out] = pltpu.SMEM
+    for i in hbm_out:
+        spaces[i] = pltpu.HBM
     return pl.pallas_call(
         body,
         out_shape=outs,
         in_specs=[pl.BlockSpec(memory_space=pltpu.VMEM)] * len(args),
         out_specs=tuple(pl.BlockSpec(memory_space=s) for s in spaces),
+        scratch_shapes=scratch,
         cost_estimate=pl.CostEstimate(flops=flops, bytes_accessed=size, transcendentals=exps),
         compiler_params=pltpu.CompilerParams(vmem_limit_bytes=20 * 1024 * 1024),
         name=name,
@@ -166,7 +174,9 @@
         out[:, at] = mine[:, at] + seen[:, at]
 
 
-def image_body(n_z, inv_root, cols, rows_lse, scores, text, pair, grads, sent, terms):
+def image_body(
+    n_z, inv_root, cols, rows_lse, scores, text, pair, grads, sent, terms, kept, held, sems
+):
     size = scores.shape[0]
     n_plane = sent.shape[0]
     rows = size // n_plane
@@ -183,7 +193,8 @@
     )
     extra = split3(col_terms)
     scale = inverse(text_max[:, :1]) * inv_root
-    step = 384
+    step = size // 4
+    copies = []
     for r in range(0, size, step):
         tile = scores[r : r + step, :]
         probs = 0.5 * (
@@ -191,29 +202,36 @@
         )
         hit = to_column(pair[:, r : r + step]) == ids
         grad = (probs - jnp.where(hit, 1.0, 0.0)).astype(BF16)
-        grads[r : r + step, :] = grad
+        at = pl.ds(r, step)
+        kept[at, :] = grad
+        sem = sems.at[n_plane + r // step]
+        copies.append(pltpu.make_async_copy(kept.at[at], grads.at[at], sem))
+        copies[-1].start()
         part = encode(jnp.dot(grad, text[...], preferred_element_type=F32) * scale)
         for p in range(step // rows):
             to = r // rows + p
             for k in range(text.shape[1] // LANES):
-                sent[to, k * rows : (k + 1) * rows, :] = part[
+                held[to, k * rows : (k + 1) * rows, :] = part[
                     p * rows : (p + 1) * rows, k * LANES : (k + 1) * LANES
                 ]
-            sent[to, k * rows + rows :, :] = extra
-
-
-def text_body(inv_root, grads, image, own, other):
+            held[to, k * rows + rows :, :] = extra
+            copies.append(pltpu.make_async_copy(held.at[to], sent.at[to], sems.at[to]))
+            copies[-1].start()
+    for copy in copies:
+        copy.wait()
+
+
+def text_body(inv_root, grads, image, terms_seen, own, other):
     half = own.shape[0]
+    scale = inverse(terms_seen[2:3, :1]) * inv_root
     for out, start in ((other, half), (own, 0)):
-        out[...] = (
-            lax.dot_general(
-                grads[:, start : start + half],
-                image[...],
-                (((0,), (0,)), ((), ())),
-                preferred_element_type=F32,
-            )
-            * inv_root
+        part = lax.dot_general(
+            grads[:, start : start + half],
+            image[...],
+            (((0,), (0,)), ((), ())),
+            preferred_element_type=F32,
         )
+        out[...] = encode(part * scale) if out.dtype == BF16 else part * scale
 
 
 def pack(pay, blocks, extra):
@@ -234,13 +252,12 @@
     row_terms = terms[0:1, :] + terms_seen[0:1, :]
     total[...] = row_terms
     extra = split3(row_terms)
-    scale = inverse(terms[2:3, :1])
     for i, q in enumerate(steps):
         blocks = []
         for k in range(2):
             start = lax.rem(z + q + (k + 2) * n_z // 2, n_z) * rows
             at = pl.ds(pl.multiple_of(start, 16), rows)
-            blocks.append((own[at, :] + seen[at, :]) * scale)
+            blocks.append(own[at, :] + decode(seen[at, :]))
         if i == 0:
             keep[:rows, :] = blocks[0]
             keep[rows:, :] = blocks[1]
@@ -273,16 +290,15 @@
     pack(far, [block], split3(sums))
 
 
-def text_sum_body(pairs, near, total, terms, side, pay, out, loss):
+def text_sum_body(near, total, terms, pay, out, side):
     rows, width = out.shape
     unit = terms[2:3, :1]
     unit = jnp.where(unit > 0, unit, 1.0)
     out[...] = unit * (near[...] + unpack([pay], 0, rows, width))
-    full = total[...] + side[...] + tails([pay])
-    loss[0, 0] = jnp.max(full) / (2.0 * pairs)
-
-
-def image_sum_body(got, terms, out, side):
+    side[...] = total[...] + tails([pay])
+
+
+def image_sum_body(pairs, got, terms, side, out, loss):
     rows, width = out.shape
     unit = terms[1:2, :1]
     unit = jnp.where(unit > 0, unit, 1.0)
@@ -290,7 +306,8 @@
     for k in range(width // LANES):
         at = slice(k * rows, (k + 1) * rows)
         out[:, k * LANES : (k + 1) * LANES] = unit * sum(decode(p[at, :]) for p in pays)
-    side[...] = tails(pays)
+    full = side[...] + tails(pays)
+    loss[0, 0] = jnp.max(full) / (2.0 * pairs)
 
 
 def shards(image_embed, text_embed, pair_index):
@@ -308,7 +325,7 @@
     copies = pl.pallas_call(
         copies_body,
         out_shape=shape((n_plane, rows, width), BF16),
-        in_specs=[pl.BlockSpec(memory_space=pltpu.VMEM)],
+        in_specs=[pl.BlockSpec(memory_space=pl.ANY)],
         out_specs=pl.BlockSpec(memory_space=pl.ANY),
         scratch_shapes=[pltpu.SemaphoreType.DMA((n_plane,))],
         name="copies",
@@ -355,28 +372,36 @@
     grads, image_sent, terms = call(
         functools.partial(image_body, n_z, inv_root),
         (
-            shape((size, size), BF16),
-            shape((n_plane, tall, LANES), BF16),
+            pltpu.HBM((size, size), BF16),
+            pltpu.HBM((n_plane, tall, LANES), BF16),
             shape((8, LANES), F32),
         ),
         (col_part, row_part, scores, text, pair),
         "image_grad",
         flops,
         2 * size * size,
+        hbm_out=(0, 1),
+        scratch=[
+            pltpu.VMEM((size, size), BF16),
+            pltpu.VMEM((n_plane, tall, LANES), BF16),
+            pltpu.SemaphoreType.DMA((n_plane + 4,)),
+        ],
     )
     image_got = lax.all_to_all(image_sent, PLANE, 0, 0)
+    terms_seen = lax.ppermute(terms, "c", SWAP)
     text_own, text_other = call(
         functools.partial(text_body, inv_root),
-        (shape((half, width), F32), shape((half, width), F32)),
-        (grads, image),
+        (shape((half, width), F32), shape((half, width), BF16)),
+        (grads, image, terms_seen),
         "text_grad",
+        10**11,
         size=1,
     )
     keep, total, *pays = call(
         functools.partial(send_body, steps),
         (shape((2 * rows, width), F32), shape((1, LANES), F32))
         + (shape((2 * tall - EXTRA, LANES), BF16),) * len(steps[1:]),
-        (text_own, lax.ppermute(text_other, "c", SWAP), terms, lax.ppermute(terms, "c", SWAP)),
+        (text_own, lax.ppermute(text_other, "c", SWAP), terms, terms_seen),
         "send",
         size=1,
     )
@@ -388,17 +413,18 @@
         "relay",
         size=1,
     )
-    grad_image, side = call(
-        image_sum_body,
+    grad_text, side = call(
+        text_sum_body,
         (shape((rows, width), F32), shape((1, LANES), F32)),
-        (image_got, terms),
+        (near, total, terms, turn(far, "z", n_z // 2)),
+        "text_sum",
+        size=1,
+    )
+    grad_image, loss = call(
+        functools.partial(image_sum_body, pairs),
+        (shape((rows, width), F32), shape((1, 1), F32)),
+        (image_got, terms, side),
         "image_sum",
-    )
-    grad_text, loss = call(
-        functools.partial(text_sum_body, pairs),
-        (shape((rows, width), F32), shape((1, 1), F32)),
-        (near, total, terms, side, turn(far, "z", n_z // 2)),
-        "text_sum",
         smem_out=1,
     )
     return (loss[0, 0], grad_image, grad_text)

time: 104 us -> 154 us (1.48); the launches traced: 104 us -> 151 us
  Pallas kernels: 15.6 us -> 60.7 us
    pallas_call x1, Pallas kernels: 2.21 us -> 48.9 us  [shards(): pl.pallas_call(copies_body, out_shape=shape((n_plane, rows, width), BF16)...]
    all_to_all x1, waiting for transfers between devices: 7.71 us -> 0.01 us  [shards(): image_got = lax.all_to_all(image_sent, PLANE, 0, 0)]
    ppermute x8, waiting for transfers between devices: 15.5 us -> 22.4 us  [turn(): lax.ppermute(x, axis, [(i, (i + step) % count) for i in range(count)])]
    ppermute x1, starting transfers between devices: 0.09 us -> 3.89 us  [shards(): terms_seen = lax.ppermute(terms, 'c', SWAP)]
    ppermute x1, starting transfers between devices: 3.81 us -> 0.13 us  [shards(): lax.ppermute(text_other, 'c', SWAP)]
    ppermute x1, waiting for transfers between devices: 0.01 us -> 2.25 us  [shards(): lax.ppermute(text_other, 'c', SWAP)]
    pallas_call x16, Pallas kernels: 13.4 us -> 11.8 us  [call(): pl.pallas_call(body, out_shape=outs, in_specs=[pl.BlockSpec(memory_space=...]
  transfers between devices with their start and end apart: 25 -> 25, of which waited for: 13 -> 13; matrix products, arithmetic and copies ran while one was open for 0% -> 0% of each run, Pallas kernels for 4% -> 34%
where the time goes in v8:
time: 154 us; the launch traced here: 151 us
  Pallas kernels  60.7 us (39%)
  starting transfers between devices  53.8 us (35%)
  waiting for transfers between devices  34.2 us (22%)
    pallas_call x1, Pallas kernels, shards(): pl.pallas_call(copies_body, out_shape=shape((n_plane, rows, width), BF16)...  48.9 us
    ppermute x8, waiting for transfers between devices, turn(): lax.ppermute(x, axis, [(i, (i + step) % count) for i in range(count)])  22.4 us
    ppermute x8, starting transfers between devices, turn(): lax.ppermute(x, axis, [(i, (i + step) % count) for i in range(count)])  17.4 us
    ppermute x8, starting transfers between devices, exchange(): seen = lax.ppermute(part, axis, [(i, i ^ step) for i in range(count)])  12 us
    pallas_call x16, Pallas kernels, call(): pl.pallas_call(body, out_shape=outs, in_specs=[pl.BlockSpec(memory_space=...  11.8 us
    ppermute x4, starting transfers between devices, shards(): pieces = pieces + [lax.ppermute(piece, 'c', SWAP) for piece in pieces]  8.81 us
    all_to_all x1, starting transfers between devices, shards(): image = lax.all_to_all(copies, PLANE, 0, 0).reshape(size, width)  6.6 us
    ppermute x8, waiting for transfers between devices, exchange(): seen = lax.ppermute(part, axis, [(i, i ^ step) for i in range(count)])  6.57 us
  transfers between devices with their start and end apart: 25, of which 13 were waited for; matrix products, arithmetic and copies ran while one was open for 0% of the time, Pallas kernels for 34%

profile of v8, /device:TPU:1, one launch (start us, length us, event | category | flops | bytes accessed | tf_op | source)
XLA Modules:
  0.0 150.9 jit_solution(16688091643526693820)
XLA Ops:
  0.6 7.8 %collective-permute-start = (bf16[48,1024]{1,0:T(8,128)(2,1)}, bf16[48,1024]{1,0:T(8,128)(2,1)S(1)}, u32[]{:S(2)}, u32[]{:S(2)}) collective-permute-start(bf16[48,1024]{1,0:T(8,128)(2,1)} %near.1), channel_id=1, source_target_pairs={{0,64},{16,80},{32,96},{48,112},{64,0},{80,16},{96,32},{112,48},{1... | collective-permute-start | bytes 294920 | tf_op jit(solution)/shard_map/ppermute | solution.py:21
  8.5 1.2 collective-permute-start.1
  9.7 48.9 %copies.1 = bf16[16,48,1024]{2,1,0:T(8,128)(2,1)} custom-call(bf16[48,1024]{1,0:T(8,128)(2,1)} %source.1), custom_call_target="tpu_custom_call" | custom-call | tf_op jit(solution)/shard_map/copies/pallas_call | solution.py:325
  58.6 0.0 copy-start
  58.6 6.6 %all-to-all-start = ((bf16[16,48,1024]{2,1,0:T(8,128)(2,1)}), bf16[16,48,1024]{2,1,0:T(8,128)(2,1)S(1)}, u32[]{:S(2)}, u32[]{:S(2)}) async-start(bf16[16,48,1024]{2,1,0:T(8,128)(2,1)} %copies.1), calls=%async_computation | async-start | bytes 3145728 | tf_op jit(solution)/shard_map/all_to_all | solution.py:333
  65.3 0.8 collective-permute-start.4
  66.1 0.3 collective-permute-start.3
  66.4 1.7 %collective-permute-start.2 = (bf16[96,1024]{1,0:T(8,128)(2,1)S(1)}, bf16[96,1024]{1,0:T(8,128)(2,1)S(1)}, u32[]{:S(2)}, u32[]{:S(2)}) collective-permute-start(bf16[96,1024]{1,0:T(8,128)(2,1)S(1)} %get-tuple-element.26.refs_0_), channel_id=1, source_target_pairs={{0,112},{16,0},{32,16},{48,32},{64,48},{80,64},{96,80},{112,96},{1... | collective-permute-start | bytes 589832 | tf_op jit(solution)/shard_map/ppermute | solution.py:21
  68.0 2.1 %collective-permute-start.5 = (bf16[96,1024]{1,0:T(8,128)(2,1)S(1)}, bf16[96,1024]{1,0:T(8,128)(2,1)S(1)}, u32[]{:S(2)}, u32[]{:S(2)}) collective-permute-start(bf16[96,1024]{1,0:T(8,128)(2,1)S(1)} %get-tuple-element.26.refs_0_), channel_id=1, source_target_pairs={{0,8},{8,0},{1,9},{9,1},{2,10},{10,2},{3,11},{11,3},{4,12},{12,4},... | collective-permute-start | bytes 589832 | tf_op jit(solution)/shard_map/ppermute | solution.py:345
  70.1 1.3 collective-permute-done.4.refs_3_
  71.4 2.4 %collective-permute-start.8 = (bf16[96,1024]{1,0:T(8,128)(2,1)S(1)}, bf16[96,1024]{1,0:T(8,128)(2,1)S(1)}, u32[]{:S(2)}, u32[]{:S(2)}) collective-permute-start(bf16[96,1024]{1,0:T(8,128)(2,1)S(1)} %collective-permute-done.4.refs_3_), channel_id=1, source_target_pairs={{0,8},{8,0},{1,9},{9,1},{2,10},{10,2},{3,11},{11,3},{4,12},{12,4},... | collective-permute-start | bytes 589832 | tf_op jit(solution)/shard_map/ppermute | solution.py:345
  73.9 3.1 %collective-permute-done.3.refs_2_ = bf16[96,1024]{1,0:T(8,128)(2,1)S(1)} collective-permute-done((bf16[96,1024]{1,0:T(8,128)(2,1)S(1)}, bf16[96,1024]{1,0:T(8,128)(2,1)S(1)}, u32[]{:S(2)}, u32[]{:S(2)}) %collective-permute-start.3) | collective-permute-done | bytes 196640 | tf_op jit(solution)/shard_map/ppermute | solution.py:21
  76.9 1.9 %collective-permute-start.7 = (bf16[96,1024]{1,0:T(8,128)(2,1)S(1)}, bf16[96,1024]{1,0:T(8,128)(2,1)S(1)}, u32[]{:S(2)}, u32[]{:S(2)}) collective-permute-start(bf16[96,1024]{1,0:T(8,128)(2,1)S(1)} %collective-permute-done.3.refs_2_), channel_id=1, source_target_pairs={{0,8},{8,0},{1,9},{9,1},{2,10},{10,2},{3,11},{11,3},{4,12},{12,4},... | collective-permute-start | bytes 589832 | tf_op jit(solution)/shard_map/ppermute | solution.py:345
  78.9 1.8 %collective-permute-done.2.refs_1_ = bf16[96,1024]{1,0:T(8,128)(2,1)S(1)} collective-permute-done((bf16[96,1024]{1,0:T(8,128)(2,1)S(1)}, bf16[96,1024]{1,0:T(8,128)(2,1)S(1)}, u32[]{:S(2)}, u32[]{:S(2)}) %collective-permute-start.2) | collective-permute-done | bytes 196640 | tf_op jit(solution)/shard_map/ppermute | solution.py:21
  80.6 2.4 %collective-permute-start.6 = (bf16[96,1024]{1,0:T(8,128)(2,1)S(1)}, bf16[96,1024]{1,0:T(8,128)(2,1)S(1)}, u32[]{:S(2)}, u32[]{:S(2)}) collective-permute-start(bf16[96,1024]{1,0:T(8,128)(2,1)S(1)} %collective-permute-done.2.refs_1_), channel_id=1, source_target_pairs={{0,8},{8,0},{1,9},{9,1},{2,10},{10,2},{3,11},{11,3},{4,12},{12,4},... | collective-permute-start | bytes 589832 | tf_op jit(solution)/shard_map/ppermute | solution.py:345
  83.0 1.1 collective-permute-done.6.refs_5_
  84.0 1.9 %all-to-all-done = bf16[16,48,1024]{2,1,0:T(8,128)(2,1)S(1)} async-done(((bf16[16,48,1024]{2,1,0:T(8,128)(2,1)}), bf16[16,48,1024]{2,1,0:T(8,128)(2,1)S(1)}, u32[]{:S(2)}, u32[]{:S(2)}) %all-to-all-start) | async-done | bytes 1572896 | tf_op jit(solution)/shard_map/all_to_all | solution.py:333
  85.9 3.0 %scores.1 = (f32[768,768]{1,0:T(8,128)S(1)}, bf16[768,1024]{1,0:T(8,128)(2,1)S(1)}, f32[1,896]{1,0:T(1,128)S(1)}, f32[1,1024]{1,0:T(1,128)S(1)}) custom-call(bf16[96,1024]{1,0:T(8,128)(2,1)S(1)} %get-tuple-element.26.refs_0_, bf16[96,1024]{1,0:T(8,128)(2,1)S(1)} %collective-permute-done.2.refs_1_, bf16[96,1024]{1,0:T(8,128)(2,1)S(1)} %collective-permute-done.3.refs_2_, ...), custom_call_target="tpu_custom_call" | custom-call | flops 1207959552 | bytes 7088640 | tf_op jit(solution)/shard_map/scores/pallas_call | solution.py:72
  89.0 2.6 %collective-permute-start.9 = (f32[1,1024]{1,0:T(1,128)S(1)}, f32[1,1024]{1,0:T(1,128)S(1)}, u32[]{:S(2)}, u32[]{:S(2)}) collective-permute-start(f32[1,1024]{1,0:T(1,128)S(1)} %get-tuple-element.28.mine), channel_id=1, source_target_pairs={{0,8},{8,0},{1,9},{9,1},{2,10},{10,2},{3,11},{11,3},{4,12},{12,4},... | collective-permute-start | bytes 12296 | tf_op jit(solution)/shard_map/ppermute | solution.py:363
  91.6 1.4 collective-permute-start.13
  93.1 0.8 collective-permute-start.10
  93.9 0.2 collective-permute-done.13.seen
  94.1 3.7 %collective-permute-start.14 = (f32[1,896]{1,0:T(1,128)S(1)}, f32[1,896]{1,0:T(1,128)S(1)}, u32[]{:S(2)}, u32[]{:S(2)}) collective-permute-start(f32[1,896]{1,0:T(1,128)S(1)} %pair.12.mine), channel_id=1, source_target_pairs={{0,1},{1,0},{2,3},{3,2},{4,5},{5,4},{6,7},{7,6},{8,9},{9,8},{10,11... | collective-permute-start | bytes 10760 | tf_op jit(solution)/shard_map/ppermute | solution.py:363
  97.8 1.3 collective-permute-start.11
  99.1 0.3 collective-permute-start.15
  99.4 1.9 %collective-permute-done.11.seen = f32[1,1024]{1,0:T(1,128)S(1)} collective-permute-done((f32[1,1024]{1,0:T(1,128)S(1)}, f32[1,1024]{1,0:T(1,128)S(1)}, u32[]{:S(2)}, u32[]{:S(2)}) %collective-permute-start.11) | collective-permute-done | bytes 4128 | tf_op jit(solution)/shard_map/ppermute | solution.py:363
  101.3 0.8 collective-permute-start.12
  102.1 1.1 collective-permute-start.16
  103.2 2.9 %collective-permute-done.16.seen = f32[1,896]{1,0:T(1,128)S(1)} collective-permute-done((f32[1,896]{1,0:T(1,128)S(1)}, f32[1,896]{1,0:T(1,128)S(1)}, u32[]{:S(2)}, u32[]{:S(2)}) %collective-permute-start.16) | collective-permute-done | bytes 3616 | tf_op jit(solution)/shard_map/ppermute | solution.py:363
  106.1 1.6 %collective-permute-done.12.seen = f32[1,1024]{1,0:T(1,128)S(1)} collective-permute-done((f32[1,1024]{1,0:T(1,128)S(1)}, f32[1,1024]{1,0:T(1,128)S(1)}, u32[]{:S(2)}, u32[]{:S(2)}) %collective-permute-start.12) | collective-permute-done | bytes 4128 | tf_op jit(solution)/shard_map/ppermute | solution.py:363
  107.7 3.5 %image_grad.1 = (bf16[768,768]{1,0:T(8,128)(2,1)}, bf16[16,400,128]{2,1,0:T(8,128)(2,1)}, f32[8,128]{1,0:T(8,128)S(1)}) custom-call(f32[1,1024]{1,0:T(1,128)S(1)} %pair.11.cols, f32[1,896]{1,0:T(1,128)S(1)} %pair.15.rows_lse, f32[768,768]{1,0:T(8,128)S(1)} %get-tuple-element.30.scores, bf16[768,1024]{1,0:T(8,128)(2,1)S(1)} %get-tuple-element.31.text, ...), custom_call_target="tpu_custom_call" | custom-call | flops 1207959552 | bytes 6765056 | tf_op jit(solution)/shard_map/image_grad/pallas_call | solution.py:72
  111.2 3.9 %collective-permute-start.17 = (f32[8,128]{1,0:T(8,128)S(1)}, f32[8,128]{1,0:T(8,128)S(1)}, u32[]{:S(2)}, u32[]{:S(2)}) collective-permute-start(f32[8,128]{1,0:T(8,128)S(1)} %get-tuple-element.33.terms), channel_id=1, source_target_pairs={{0,8},{8,0},{1,9},{9,1},{2,10},{10,2},{3,11},{11,3},{4,12},{12,4},... | collective-permute-start | bytes 12296 | tf_op jit(solution)/shard_map/ppermute | solution.py:391
  115.1 3.7 %all-to-all-start.1 = ((bf16[16,400,128]{2,1,0:T(8,128)(2,1)}), bf16[16,400,128]{2,1,0:T(8,128)(2,1)S(1)}, u32[]{:S(2)}, u32[]{:S(2)}) async-start(bf16[16,400,128]{2,1,0:T(8,128)(2,1)} %get-tuple-element.32), calls=%async_computation.1 | async-start | bytes 3276800 | tf_op jit(solution)/shard_map/all_to_all | solution.py:390
  118.9 1.3 copy-done.2
  120.1 1.6 %text_grad.1 = (f32[384,1024]{1,0:T(8,128)S(1)}, bf16[384,1024]{1,0:T(8,128)(2,1)S(1)}) custom-call(bf16[768,768]{1,0:T(8,128)(2,1)S(1)} %copy-done.2, bf16[768,1024]{1,0:T(8,128)(2,1)S(1)} %bitcast.3, f32[8,128]{1,0:T(8,128)S(1)} %collective-permute-done.17.terms_seen), custom_call_target="tpu_custom_call" | custom-call | flops 99999997952 | bytes 1 | tf_op jit(solution)/shard_map/text_grad/pallas_call | solution.py:72
  121.7 0.1 collective-permute-start.18
  121.9 2.2 %collective-permute-done.18.seen = bf16[384,1024]{1,0:T(8,128)(2,1)S(1)} collective-permute-done((bf16[384,1024]{1,0:T(8,128)(2,1)S(1)}, bf16[384,1024]{1,0:T(8,128)(2,1)S(1)}, u32[]{:S(2)}, u32[]{:S(2)}) %collective-permute-start.18) | collective-permute-done | bytes 786464 | tf_op jit(solution)/shard_map/ppermute | solution.py:404
  124.1 0.7 send.1
  124.8 0.8 collective-permute-start.19
  125.6 1.2 collective-permute-start.20
  126.8 1.9 %collective-permute-start.21 = (bf16[784,128]{1,0:T(8,128)(2,1)S(1)}, bf16[784,128]{1,0:T(8,128)(2,1)S(1)}, u32[]{:S(2)}, u32[]{:S(2)}) collective-permute-start(bf16[784,128]{1,0:T(8,128)(2,1)S(1)} %get-tuple-element.41), channel_id=1, source_target_pairs={{0,112},{16,0},{32,16},{48,32},{64,48},{80,64},{96,80},{112,96},{1... | collective-permute-start | bytes 602120 | tf_op jit(solution)/shard_map/ppermute | solution.py:21
  128.7 3.8 %collective-permute-done.19.refs_0_ = bf16[784,128]{1,0:T(8,128)(2,1)S(1)} collective-permute-done((bf16[784,128]{1,0:T(8,128)(2,1)S(1)}, bf16[784,128]{1,0:T(8,128)(2,1)S(1)}, u32[]{:S(2)}, u32[]{:S(2)}) %collective-permute-start.19) | collective-permute-done | bytes 200736 | tf_op jit(solution)/shard_map/ppermute | solution.py:21
  132.5 5.6 %collective-permute-done.20.refs_1_ = bf16[784,128]{1,0:T(8,128)(2,1)S(1)} collective-permute-done((bf16[784,128]{1,0:T(8,128)(2,1)S(1)}, bf16[784,128]{1,0:T(8,128)(2,1)S(1)}, u32[]{:S(2)}, u32[]{:S(2)}) %collective-permute-start.20) | collective-permute-done | bytes 200736 | tf_op jit(solution)/shard_map/ppermute | solution.py:21
  138.1 0.4 relay.1
  138.5 2.9 %collective-permute-start.22 = (bf16[400,128]{1,0:T(8,128)(2,1)S(1)}, bf16[400,128]{1,0:T(8,128)(2,1)S(1)}, u32[]{:S(2)}, u32[]{:S(2)}) collective-permute-start(bf16[400,128]{1,0:T(8,128)(2,1)S(1)} %get-tuple-element.44), channel_id=1, source_target_pairs={{0,64},{16,80},{32,96},{48,112},{64,0},{80,16},{96,32},{112,48},{1... | collective-permute-start | bytes 307208 | tf_op jit(solution)/shard_map/ppermute | solution.py:21
  141.4 6.9 %collective-permute-done.22.pay = bf16[400,128]{1,0:T(8,128)(2,1)S(1)} collective-permute-done((bf16[400,128]{1,0:T(8,128)(2,1)S(1)}, bf16[400,128]{1,0:T(8,128)(2,1)S(1)}, u32[]{:S(2)}, u32[]{:S(2)}) %collective-permute-start.22) | collective-permute-done | bytes 102432 | tf_op jit(solution)/shard_map/ppermute | solution.py:21
  148.3 0.8 text_sum.1
  149.0 1.7 %image_sum.1 = (f32[48,1024]{1,0:T(8,128)}, f32[1,1]{1,0:T(1,128)}) custom-call(bf16[16,400,128]{2,1,0:T(8,128)(2,1)S(1)} %all-to-all-done.1.got, f32[8,128]{1,0:T(8,128)S(1)} %get-tuple-element.33.terms, f32[1,128]{1,0:T(1,128)S(1)} %get-tuple-element.45.side), custom_call_target="tpu_custom_call" | custom-call | bytes 1839620 | tf_op jit(solution)/shard_map/image_sum/pallas_call | solution.py:72
  (25 shorter events, 0.2 us)
Async XLA Ops:
  0.6 64.6 %collective-permute-start = (bf16[48,1024]{1,0:T(8,128)(2,1)}, bf16[48,1024]{1,0:T(8,128)(2,1)S(1)}, u32[]{:S(2)}, u32[]{:S(2)}) collective-permute-start(bf16[48,1024]{1,0:T(8,128)(2,1)} %near.1), channel_id=1, source_target_pairs={{0,64},{16,80},{32,96},{48,112},{64,0},{80,16},{96,32},{112,48},{1... | collective-permute-start | bytes 294920 | tf_op jit(solution)/shard_map/ppermute | solution.py:21
  8.5 56.7 %collective-permute-start.1 = (s32[384]{0:T(512)}, s32[384]{0:T(512)S(1)}, u32[]{:S(2)}, u32[]{:S(2)}) collective-permute-start(s32[384]{0:T(512)} %mine.1), channel_id=1, source_target_pairs={{0,128},{128,0},{1,129},{129,1},{2,130},{130,2},{3,131},{131,3},{4... | collective-permute-start | bytes 4616 | tf_op jit(solution)/shard_map/ppermute | solution.py:324
  58.6 6.7 %copy-start = (bf16[48,1024]{1,0:T(8,128)(2,1)S(1)}, bf16[48,1024]{1,0:T(8,128)(2,1)}, u32[]{:S(2)}) copy-start(bf16[48,1024]{1,0:T(8,128)(2,1)} %near.1) | copy-start | bytes 294916
  58.6 6.7 %copy-start.1 = (s32[384]{0:T(512)S(1)}, s32[384]{0:T(512)}, u32[]{:S(2)}) copy-start(s32[384]{0:T(512)} %mine.1) | copy-start | bytes 4612
  58.6 27.4 %all-to-all-start = ((bf16[16,48,1024]{2,1,0:T(8,128)(2,1)}), bf16[16,48,1024]{2,1,0:T(8,128)(2,1)S(1)}, u32[]{:S(2)}, u32[]{:S(2)}) async-start(bf16[16,48,1024]{2,1,0:T(8,128)(2,1)} %copies.1), calls=%async_computation | async-start | bytes 3145728 | tf_op jit(solution)/shard_map/all_to_all | solution.py:333
  65.3 6.2 %collective-permute-start.4 = (bf16[96,1024]{1,0:T(8,128)(2,1)S(1)}, bf16[96,1024]{1,0:T(8,128)(2,1)S(1)}, u32[]{:S(2)}, u32[]{:S(2)}) collective-permute-start(bf16[96,1024]{1,0:T(8,128)(2,1)S(1)} %get-tuple-element.26.refs_0_), channel_id=1, source_target_pairs={{0,16},{16,32},{32,48},{48,64},{64,80},{80,96},{96,112},{112,0},{1... | collective-permute-start | bytes 589832 | tf_op jit(solution)/shard_map/ppermute | solution.py:21
  66.1 10.8 %collective-permute-start.3 = (bf16[96,1024]{1,0:T(8,128)(2,1)S(1)}, bf16[96,1024]{1,0:T(8,128)(2,1)S(1)}, u32[]{:S(2)}, u32[]{:S(2)}) collective-permute-start(bf16[96,1024]{1,0:T(8,128)(2,1)S(1)} %get-tuple-element.26.refs_0_), channel_id=1, source_target_pairs={{0,96},{16,112},{32,0},{48,16},{64,32},{80,48},{96,64},{112,80},{1... | collective-permute-start | bytes 589832 | tf_op jit(solution)/shard_map/ppermute | solution.py:21
  66.4 14.3 %collective-permute-start.2 = (bf16[96,1024]{1,0:T(8,128)(2,1)S(1)}, bf16[96,1024]{1,0:T(8,128)(2,1)S(1)}, u32[]{:S(2)}, u32[]{:S(2)}) collective-permute-start(bf16[96,1024]{1,0:T(8,128)(2,1)S(1)} %get-tuple-element.26.refs_0_), channel_id=1, source_target_pairs={{0,112},{16,0},{32,16},{48,32},{64,48},{80,64},{96,80},{112,96},{1... | collective-permute-start | bytes 589832 | tf_op jit(solution)/shard_map/ppermute | solution.py:21
  68.0 14.9 %collective-permute-start.5 = (bf16[96,1024]{1,0:T(8,128)(2,1)S(1)}, bf16[96,1024]{1,0:T(8,128)(2,1)S(1)}, u32[]{:S(2)}, u32[]{:S(2)}) collective-permute-start(bf16[96,1024]{1,0:T(8,128)(2,1)S(1)} %get-tuple-element.26.refs_0_), channel_id=1, source_target_pairs={{0,8},{8,0},{1,9},{9,1},{2,10},{10,2},{3,11},{11,3},{4,12},{12,4},... | collective-permute-start | bytes 589832 | tf_op jit(solution)/shard_map/ppermute | solution.py:345
  71.4 11.5 %collective-permute-start.8 = (bf16[96,1024]{1,0:T(8,128)(2,1)S(1)}, bf16[96,1024]{1,0:T(8,128)(2,1)S(1)}, u32[]{:S(2)}, u32[]{:S(2)}) collective-permute-start(bf16[96,1024]{1,0:T(8,128)(2,1)S(1)} %collective-permute-done.4.refs_3_), channel_id=1, source_target_pairs={{0,8},{8,0},{1,9},{9,1},{2,10},{10,2},{3,11},{11,3},{4,12},{12,4},... | collective-permute-start | bytes 589832 | tf_op jit(solution)/shard_map/ppermute | solution.py:345
  76.9 6.1 %collective-permute-start.7 = (bf16[96,1024]{1,0:T(8,128)(2,1)S(1)}, bf16[96,1024]{1,0:T(8,128)(2,1)S(1)}, u32[]{:S(2)}, u32[]{:S(2)}) collective-permute-start(bf16[96,1024]{1,0:T(8,128)(2,1)S(1)} %collective-permute-done.3.refs_2_), channel_id=1, source_target_pairs={{0,8},{8,0},{1,9},{9,1},{2,10},{10,2},{3,11},{11,3},{4,12},{12,4},... | collective-permute-start | bytes 589832 | tf_op jit(solution)/shard_map/ppermute | solution.py:345
  80.6 3.4 %collective-permute-start.6 = (bf16[96,1024]{1,0:T(8,128)(2,1)S(1)}, bf16[96,1024]{1,0:T(8,128)(2,1)S(1)}, u32[]{:S(2)}, u32[]{:S(2)}) collective-permute-start(bf16[96,1024]{1,0:T(8,128)(2,1)S(1)} %collective-permute-done.2.refs_1_), channel_id=1, source_target_pairs={{0,8},{8,0},{1,9},{9,1},{2,10},{10,2},{3,11},{11,3},{4,12},{12,4},... | collective-permute-start | bytes 589832 | tf_op jit(solution)/shard_map/ppermute | solution.py:345
  89.0 4.1 %collective-permute-start.9 = (f32[1,1024]{1,0:T(1,128)S(1)}, f32[1,1024]{1,0:T(1,128)S(1)}, u32[]{:S(2)}, u32[]{:S(2)}) collective-permute-start(f32[1,1024]{1,0:T(1,128)S(1)} %get-tuple-element.28.mine), channel_id=1, source_target_pairs={{0,8},{8,0},{1,9},{9,1},{2,10},{10,2},{3,11},{11,3},{4,12},{12,4},... | collective-permute-start | bytes 12296 | tf_op jit(solution)/shard_map/ppermute | solution.py:363
  91.6 2.5 %collective-permute-start.13 = (f32[1,896]{1,0:T(1,128)S(1)}, f32[1,896]{1,0:T(1,128)S(1)}, u32[]{:S(2)}, u32[]{:S(2)}) collective-permute-start(f32[1,896]{1,0:T(1,128)S(1)} %get-tuple-element.29.mine), channel_id=1, source_target_pairs={{0,128},{128,0},{1,129},{129,1},{2,130},{130,2},{3,131},{131,3},{4... | collective-permute-start | bytes 10760 | tf_op jit(solution)/shard_map/ppermute | solution.py:363
  93.1 4.7 %collective-permute-start.10 = (f32[1,1024]{1,0:T(1,128)S(1)}, f32[1,1024]{1,0:T(1,128)S(1)}, u32[]{:S(2)}, u32[]{:S(2)}) collective-permute-start(f32[1,1024]{1,0:T(1,128)S(1)} %pair.8.mine), channel_id=1, source_target_pairs={{0,16},{16,0},{32,48},{48,32},{64,80},{80,64},{96,112},{112,96},{1... | collective-permute-start | bytes 12296 | tf_op jit(solution)/shard_map/ppermute | solution.py:363
  94.1 5.0 %collective-permute-start.14 = (f32[1,896]{1,0:T(1,128)S(1)}, f32[1,896]{1,0:T(1,128)S(1)}, u32[]{:S(2)}, u32[]{:S(2)}) collective-permute-start(f32[1,896]{1,0:T(1,128)S(1)} %pair.12.mine), channel_id=1, source_target_pairs={{0,1},{1,0},{2,3},{3,2},{4,5},{5,4},{6,7},{7,6},{8,9},{9,8},{10,11... | collective-permute-start | bytes 10760 | tf_op jit(solution)/shard_map/ppermute | solution.py:363
  97.8 3.4 %collective-permute-start.11 = (f32[1,1024]{1,0:T(1,128)S(1)}, f32[1,1024]{1,0:T(1,128)S(1)}, u32[]{:S(2)}, u32[]{:S(2)}) collective-permute-start(f32[1,1024]{1,0:T(1,128)S(1)} %pair.9.mine), channel_id=1, source_target_pairs={{0,32},{16,48},{32,0},{48,16},{64,96},{80,112},{96,64},{112,80},{1... | collective-permute-start | bytes 12296 | tf_op jit(solution)/shard_map/ppermute | solution.py:363
  99.1 3.0 %collective-permute-start.15 = (f32[1,896]{1,0:T(1,128)S(1)}, f32[1,896]{1,0:T(1,128)S(1)}, u32[]{:S(2)}, u32[]{:S(2)}) collective-permute-start(f32[1,896]{1,0:T(1,128)S(1)} %pair.13.mine), channel_id=1, source_target_pairs={{0,2},{2,0},{4,6},{6,4},{1,3},{3,1},{5,7},{7,5},{8,10},{10,8},{12,... | collective-permute-start | bytes 10760 | tf_op jit(solution)/shard_map/ppermute | solution.py:363
  101.3 6.5 %collective-permute-start.12 = (f32[1,1024]{1,0:T(1,128)S(1)}, f32[1,1024]{1,0:T(1,128)S(1)}, u32[]{:S(2)}, u32[]{:S(2)}) collective-permute-start(f32[1,1024]{1,0:T(1,128)S(1)} %pair.10.mine), channel_id=1, source_target_pairs={{0,64},{16,80},{32,96},{48,112},{64,0},{80,16},{96,32},{112,48},{1... | collective-permute-start | bytes 12296 | tf_op jit(solution)/shard_map/ppermute | solution.py:363
  102.1 4.0 %collective-permute-start.16 = (f32[1,896]{1,0:T(1,128)S(1)}, f32[1,896]{1,0:T(1,128)S(1)}, u32[]{:S(2)}, u32[]{:S(2)}) collective-permute-start(f32[1,896]{1,0:T(1,128)S(1)} %pair.14.mine), channel_id=1, source_target_pairs={{0,4},{2,6},{4,0},{6,2},{1,5},{3,7},{5,1},{7,3},{8,12},{10,14},{12... | collective-permute-start | bytes 10760 | tf_op jit(solution)/shard_map/ppermute | solution.py:363
  111.2 7.6 %collective-permute-start.17 = (f32[8,128]{1,0:T(8,128)S(1)}, f32[8,128]{1,0:T(8,128)S(1)}, u32[]{:S(2)}, u32[]{:S(2)}) collective-permute-start(f32[8,128]{1,0:T(8,128)S(1)} %get-tuple-element.33.terms), channel_id=1, source_target_pairs={{0,8},{8,0},{1,9},{9,1},{2,10},{10,2},{3,11},{11,3},{4,12},{12,4},... | collective-permute-start | bytes 12296 | tf_op jit(solution)/shard_map/ppermute | solution.py:391
  115.1 33.9 %all-to-all-start.1 = ((bf16[16,400,128]{2,1,0:T(8,128)(2,1)}), bf16[16,400,128]{2,1,0:T(8,128)(2,1)S(1)}, u32[]{:S(2)}, u32[]{:S(2)}) async-start(bf16[16,400,128]{2,1,0:T(8,128)(2,1)} %get-tuple-element.32), calls=%async_computation.1 | async-start | bytes 3276800 | tf_op jit(solution)/shard_map/all_to_all | solution.py:390
  118.9 1.3 copy-start.2
  121.7 2.4 %collective-permute-start.18 = (bf16[384,1024]{1,0:T(8,128)(2,1)S(1)}, bf16[384,1024]{1,0:T(8,128)(2,1)S(1)}, u32[]{:S(2)}, u32[]{:S(2)}) collective-permute-start(bf16[384,1024]{1,0:T(8,128)(2,1)S(1)} %get-tuple-element.36), channel_id=1, source_target_pairs={{0,8},{8,0},{1,9},{9,1},{2,10},{10,2},{3,11},{11,3},{4,12},{12,4},... | collective-permute-start | bytes 2359304 | tf_op jit(solution)/shard_map/ppermute | solution.py:404
  124.8 7.7 %collective-permute-start.19 = (bf16[784,128]{1,0:T(8,128)(2,1)S(1)}, bf16[784,128]{1,0:T(8,128)(2,1)S(1)}, u32[]{:S(2)}, u32[]{:S(2)}) collective-permute-start(bf16[784,128]{1,0:T(8,128)(2,1)S(1)} %get-tuple-element.39), channel_id=1, source_target_pairs={{0,16},{16,32},{32,48},{48,64},{64,80},{80,96},{96,112},{112,0},{1... | collective-permute-start | bytes 602120 | tf_op jit(solution)/shard_map/ppermute | solution.py:21
  125.6 12.5 %collective-permute-start.20 = (bf16[784,128]{1,0:T(8,128)(2,1)S(1)}, bf16[784,128]{1,0:T(8,128)(2,1)S(1)}, u32[]{:S(2)}, u32[]{:S(2)}) collective-permute-start(bf16[784,128]{1,0:T(8,128)(2,1)S(1)} %get-tuple-element.40), channel_id=1, source_target_pairs={{0,32},{16,48},{32,64},{48,80},{64,96},{80,112},{96,0},{112,16},{1... | collective-permute-start | bytes 602120 | tf_op jit(solution)/shard_map/ppermute | solution.py:21
  126.8 11.3 %collective-permute-start.21 = (bf16[784,128]{1,0:T(8,128)(2,1)S(1)}, bf16[784,128]{1,0:T(8,128)(2,1)S(1)}, u32[]{:S(2)}, u32[]{:S(2)}) collective-permute-start(bf16[784,128]{1,0:T(8,128)(2,1)S(1)} %get-tuple-element.41), channel_id=1, source_target_pairs={{0,112},{16,0},{32,16},{48,32},{64,48},{80,64},{96,80},{112,96},{1... | collective-permute-start | bytes 602120 | tf_op jit(solution)/shard_map/ppermute | solution.py:21
  138.5 9.7 %collective-permute-start.22 = (bf16[400,128]{1,0:T(8,128)(2,1)S(1)}, bf16[400,128]{1,0:T(8,128)(2,1)S(1)}, u32[]{:S(2)}, u32[]{:S(2)}) collective-permute-start(bf16[400,128]{1,0:T(8,128)(2,1)S(1)} %get-tuple-element.44), channel_id=1, source_target_pairs={{0,64},{16,80},{32,96},{48,112},{64,0},{80,16},{96,32},{112,48},{1... | collective-permute-start | bytes 307208 | tf_op jit(solution)/shard_map/ppermute | solution.py:21

commit v9 on v8

--- a/solution.py
+++ b/solution.py
@@ -174,12 +174,10 @@
         out[:, at] = mine[:, at] + seen[:, at]
 
 
-def image_body(
-    n_z, inv_root, cols, rows_lse, scores, text, pair, grads, sent, terms, kept, held, sems
-):
+def text_body(n_z, inv_root, cols, rows_lse, scores, image, pair, grads, terms, own, other):
     size = scores.shape[0]
-    n_plane = sent.shape[0]
-    rows = size // n_plane
+    half = own.shape[0]
+    rows = half // n_z
     col_lse = cols[:, :size]
     image_max = cols[:, size : size + LANES]
     found = cols[:, size + LANES :]
@@ -189,49 +187,50 @@
     row_terms = jnp.broadcast_to(jnp.sum(row_lse, axis=1, keepdims=True), (1, LANES))
     col_terms = jnp.sum(col_lse, axis=1, keepdims=True) - 2.0 * found
     terms[...] = jnp.concatenate(
-        [row_terms, text_max, image_max, jnp.zeros((5, LANES), F32)], axis=0
-    )
-    extra = split3(col_terms)
-    scale = inverse(text_max[:, :1]) * inv_root
+        [row_terms, text_max, image_max, col_terms, jnp.zeros((4, LANES), F32)], axis=0
+    )
+    scale = inverse(image_max[:, :1]) * inv_root
+    row_column = to_column(row_lse)
+    pair_column = to_column(pair[...])
+    for start in (half, 0):
+        at = slice(start, start + half)
+        tile = scores[:, at]
+        probs = 0.5 * (jnp.exp(tile - row_column) + jnp.exp(tile - col_lse[:, at]))
+        grad = (probs - jnp.where(pair_column == ids[:, at], 1.0, 0.0)).astype(BF16)
+        grads[:, at] = grad
+        part = lax.dot_general(
+            grad, image[...], (((0,), (0,)), ((), ())), preferred_element_type=F32
+        )
+        if start == 0:
+            own[...] = part * scale
+        else:
+            other[:half, :] = encode(part * scale)
+    extra = split3(row_terms)
+    other[half:, :] = jnp.concatenate([extra] * (other.shape[1] // LANES), axis=1)
+
+
+def image_body(inv_root, grads, text, terms, sent, held, sems):
+    size = grads.shape[0]
+    n_plane, tall, _ = sent.shape
+    rows = size // n_plane
+    extra = split3(terms[3:4, :])
+    scale = inverse(terms[1:2, :1]) * inv_root
     step = size // 4
     copies = []
     for r in range(0, size, step):
-        tile = scores[r : r + step, :]
-        probs = 0.5 * (
-            jnp.exp(tile - to_column(row_lse[:, r : r + step])) + jnp.exp(tile - col_lse)
-        )
-        hit = to_column(pair[:, r : r + step]) == ids
-        grad = (probs - jnp.where(hit, 1.0, 0.0)).astype(BF16)
-        at = pl.ds(r, step)
-        kept[at, :] = grad
-        sem = sems.at[n_plane + r // step]
-        copies.append(pltpu.make_async_copy(kept.at[at], grads.at[at], sem))
-        copies[-1].start()
-        part = encode(jnp.dot(grad, text[...], preferred_element_type=F32) * scale)
+        part = jnp.dot(grads[r : r + step, :], text[...], preferred_element_type=F32)
+        part = encode(part * scale)
         for p in range(step // rows):
             to = r // rows + p
             for k in range(text.shape[1] // LANES):
                 held[to, k * rows : (k + 1) * rows, :] = part[
                     p * rows : (p + 1) * rows, k * LANES : (k + 1) * LANES
                 ]
-            held[to, k * rows + rows :, :] = extra
+            held[to, tall - EXTRA :, :] = extra
             copies.append(pltpu.make_async_copy(held.at[to], sent.at[to], sems.at[to]))
             copies[-1].start()
     for copy in copies:
         copy.wait()
-
-
-def text_body(inv_root, grads, image, terms_seen, own, other):
-    half = own.shape[0]
-    scale = inverse(terms_seen[2:3, :1]) * inv_root
-    for out, start in ((other, half), (own, 0)):
-        part = lax.dot_general(
-            grads[:, start : start + half],
-            image[...],
-            (((0,), (0,)), ((), ())),
-            preferred_element_type=F32,
-        )
-        out[...] = encode(part * scale) if out.dtype == BF16 else part * scale
 
 
 def pack(pay, blocks, extra):
@@ -245,11 +244,13 @@
     pay[at:, :] = extra
 
 
-def send_body(steps, own, seen, terms, terms_seen, keep, total, *pays):
+def send_body(steps, own, seen, terms, keep, total, *pays):
     n_z = 2 * len(steps)
     rows = keep.shape[0] // 2
     z = lax.axis_index("z")
-    row_terms = terms[0:1, :] + terms_seen[0:1, :]
+    half = own.shape[0]
+    tail = seen[half:, :LANES].astype(F32)
+    row_terms = terms[0:1, :] + jnp.sum(tail, axis=0, keepdims=True)
     total[...] = row_terms
     extra = split3(row_terms)
     for i, q in enumerate(steps):
@@ -325,7 +326,7 @@
     copies = pl.pallas_call(
         copies_body,
         out_shape=shape((n_plane, rows, width), BF16),
-        in_specs=[pl.BlockSpec(memory_space=pl.ANY)],
+        in_specs=[pl.BlockSpec(memory_space=pltpu.VMEM)],
         out_specs=pl.BlockSpec(memory_space=pl.ANY),
         scratch_shapes=[pltpu.SemaphoreType.DMA((n_plane,))],
         name="copies",
@@ -369,39 +370,37 @@
     for axis, step in (("xl", 1), ("xh", 1), ("y", 1), ("y", 2)):
         row_part = exchange(row_part, axis, step)
 
-    grads, image_sent, terms = call(
-        functools.partial(image_body, n_z, inv_root),
+    grads, terms, text_own, text_other = call(
+        functools.partial(text_body, n_z, inv_root),
         (
-            pltpu.HBM((size, size), BF16),
-            pltpu.HBM((n_plane, tall, LANES), BF16),
+            shape((size, size), BF16),
             shape((8, LANES), F32),
+            shape((half, width), F32),
+            shape((half + EXTRA, width), BF16),
         ),
-        (col_part, row_part, scores, text, pair),
+        (col_part, row_part, scores, image, pair),
+        "text_grad",
+        flops,
+        2 * size * size,
+    )
+    (image_sent,) = call(
+        functools.partial(image_body, inv_root),
+        (pltpu.HBM((n_plane, tall, LANES), BF16),),
+        (grads, text, terms),
         "image_grad",
         flops,
-        2 * size * size,
-        hbm_out=(0, 1),
+        hbm_out=(0,),
         scratch=[
-            pltpu.VMEM((size, size), BF16),
             pltpu.VMEM((n_plane, tall, LANES), BF16),
-            pltpu.SemaphoreType.DMA((n_plane + 4,)),
+            pltpu.SemaphoreType.DMA((n_plane,)),
         ],
     )
     image_got = lax.all_to_all(image_sent, PLANE, 0, 0)
-    terms_seen = lax.ppermute(terms, "c", SWAP)
-    text_own, text_other = call(
-        functools.partial(text_body, inv_root),
-        (shape((half, width), F32), shape((half, width), BF16)),
-        (grads, image, terms_seen),
-        "text_grad",
-        10**11,
-        size=1,
-    )
     keep, total, *pays = call(
         functools.partial(send_body, steps),
         (shape((2 * rows, width), F32), shape((1, LANES), F32))
         + (shape((2 * tall - EXTRA, LANES), BF16),) * len(steps[1:]),
-        (text_own, lax.ppermute(text_other, "c", SWAP), terms, terms_seen),
+        (text_own, lax.ppermute(text_other, "c", SWAP), terms),
         "send",
         size=1,
     )
@@ -411,6 +410,7 @@
         (shape((rows, width), F32), shape((tall, LANES), BF16), shape((1, LANES), F32)),
         (keep, total, *pays),
         "relay",
+        10**11,
         size=1,
     )
     grad_text, side = call(

time: 154 us -> 107 us (0.69)
  the two profiles are of different devices: /device:TPU:1 before, /device:TPU:6 now
where the time goes in v9:
time: 107 us
  waiting for transfers between devices  53.4 us (50%)
  starting transfers between devices  38.2 us (36%)
  Pallas kernels  14.1 us (13%)
    ppermute x8, waiting for transfers between devices, turn(): lax.ppermute(x, axis, [(i, (i + step) % count) for i in range(count)])  21 us
    ppermute x8, starting transfers between devices, turn(): lax.ppermute(x, axis, [(i, (i + step) % count) for i in range(count)])  18.5 us
    ppermute x8, waiting for transfers between devices, exchange(): seen = lax.ppermute(part, axis, [(i, i ^ step) for i in range(count)])  12.1 us
    pallas_call x16, Pallas kernels, call(): pl.pallas_call(body, out_shape=outs, in_specs=[pl.BlockSpec(memory_space=...  11.9 us
    all_to_all x1, waiting for transfers between devices, shards(): image_got = lax.all_to_all(image_sent, PLANE, 0, 0)  11.6 us
    all_to_all x1, starting transfers between devices, shards(): image = lax.all_to_all(copies, PLANE, 0, 0).reshape(size, width)  7.94 us
    ppermute x8, starting transfers between devices, exchange(): seen = lax.ppermute(part, axis, [(i, i ^ step) for i in range(count)])  5.9 us
    all_to_all x1, waiting for transfers between devices, shards(): image = lax.all_to_all(copies, PLANE, 0, 0).reshape(size, width)  4.99 us
  transfers between devices with their start and end apart: 24, of which 16 were waited for; matrix products, arithmetic and copies ran while one was open for 0% of the time, Pallas kernels for 6%

profile of v9, /device:TPU:6, one launch (start us, length us, event | category | flops | bytes accessed | tf_op | source)
XLA Modules:
  0.0 106.7 jit_solution(17324096866760577763)
XLA Ops:
  0.6 7.3 %collective-permute-start = (bf16[48,1024]{1,0:T(8,128)(2,1)}, bf16[48,1024]{1,0:T(8,128)(2,1)S(1)}, u32[]{:S(2)}, u32[]{:S(2)}) collective-permute-start(bf16[48,1024]{1,0:T(8,128)(2,1)} %near.1), channel_id=1, source_target_pairs={{0,64},{16,80},{32,96},{48,112},{64,0},{80,16},{96,32},{112,48},{1... | collective-permute-start | bytes 294920 | tf_op jit(solution)/shard_map/ppermute | solution.py:21
  7.9 0.8 collective-permute-start.1
  8.7 2.2 %copies.1 = bf16[16,48,1024]{2,1,0:T(8,128)(2,1)} custom-call(bf16[48,1024]{1,0:T(8,128)(2,1)} %source.1), custom_call_target="tpu_custom_call" | custom-call | tf_op jit(solution)/shard_map/copies/pallas_call | solution.py:326
  11.0 0.0 copy-start
  11.0 0.0 copy-start.1
  11.0 7.9 %all-to-all-start = ((bf16[16,48,1024]{2,1,0:T(8,128)(2,1)}), bf16[16,48,1024]{2,1,0:T(8,128)(2,1)S(1)}, u32[]{:S(2)}, u32[]{:S(2)}) async-start(bf16[16,48,1024]{2,1,0:T(8,128)(2,1)} %copies.1), calls=%async_computation | async-start | bytes 3145728 | tf_op jit(solution)/shard_map/all_to_all | solution.py:334
  18.9 0.0 collective-permute-done.far
  19.0 1.1 %collective-permute-start.4 = (bf16[96,1024]{1,0:T(8,128)(2,1)S(1)}, bf16[96,1024]{1,0:T(8,128)(2,1)S(1)}, u32[]{:S(2)}, u32[]{:S(2)}) collective-permute-start(bf16[96,1024]{1,0:T(8,128)(2,1)S(1)} %get-tuple-element.25.refs_0_), channel_id=1, source_target_pairs={{0,16},{16,32},{32,48},{48,64},{64,80},{80,96},{96,112},{112,0},{1... | collective-permute-start | bytes 589832 | tf_op jit(solution)/shard_map/ppermute | solution.py:21
  20.1 0.6 collective-permute-start.3
  20.6 1.7 %collective-permute-start.2 = (bf16[96,1024]{1,0:T(8,128)(2,1)S(1)}, bf16[96,1024]{1,0:T(8,128)(2,1)S(1)}, u32[]{:S(2)}, u32[]{:S(2)}) collective-permute-start(bf16[96,1024]{1,0:T(8,128)(2,1)S(1)} %get-tuple-element.25.refs_0_), channel_id=1, source_target_pairs={{0,112},{16,0},{32,16},{48,32},{64,48},{80,64},{96,80},{112,96},{1... | collective-permute-start | bytes 589832 | tf_op jit(solution)/shard_map/ppermute | solution.py:21
  22.3 0.0 collective-permute-start.5
  22.3 3.6 %collective-permute-done.4.refs_3_ = bf16[96,1024]{1,0:T(8,128)(2,1)S(1)} collective-permute-done((bf16[96,1024]{1,0:T(8,128)(2,1)S(1)}, bf16[96,1024]{1,0:T(8,128)(2,1)S(1)}, u32[]{:S(2)}, u32[]{:S(2)}) %collective-permute-start.4) | collective-permute-done | bytes 196640 | tf_op jit(solution)/shard_map/ppermute | solution.py:21
  25.9 4.7 %collective-permute-done.3.refs_2_ = bf16[96,1024]{1,0:T(8,128)(2,1)S(1)} collective-permute-done((bf16[96,1024]{1,0:T(8,128)(2,1)S(1)}, bf16[96,1024]{1,0:T(8,128)(2,1)S(1)}, u32[]{:S(2)}, u32[]{:S(2)}) %collective-permute-start.3) | collective-permute-done | bytes 196640 | tf_op jit(solution)/shard_map/ppermute | solution.py:21
  30.7 4.2 %collective-permute-done.2.refs_1_ = bf16[96,1024]{1,0:T(8,128)(2,1)S(1)} collective-permute-done((bf16[96,1024]{1,0:T(8,128)(2,1)S(1)}, bf16[96,1024]{1,0:T(8,128)(2,1)S(1)}, u32[]{:S(2)}, u32[]{:S(2)}) %collective-permute-start.2) | collective-permute-done | bytes 196640 | tf_op jit(solution)/shard_map/ppermute | solution.py:21
  34.9 1.4 %collective-permute-done.6.refs_5_ = bf16[96,1024]{1,0:T(8,128)(2,1)S(1)} collective-permute-done((bf16[96,1024]{1,0:T(8,128)(2,1)S(1)}, bf16[96,1024]{1,0:T(8,128)(2,1)S(1)}, u32[]{:S(2)}, u32[]{:S(2)}) %collective-permute-start.6) | collective-permute-done | bytes 196640 | tf_op jit(solution)/shard_map/ppermute | solution.py:346
  36.3 5.0 %all-to-all-done = bf16[16,48,1024]{2,1,0:T(8,128)(2,1)S(1)} async-done(((bf16[16,48,1024]{2,1,0:T(8,128)(2,1)}), bf16[16,48,1024]{2,1,0:T(8,128)(2,1)S(1)}, u32[]{:S(2)}, u32[]{:S(2)}) %all-to-all-start) | async-done | bytes 1572896 | tf_op jit(solution)/shard_map/all_to_all | solution.py:334
  41.3 3.0 %scores.1 = (f32[768,768]{1,0:T(8,128)S(1)}, bf16[768,1024]{1,0:T(8,128)(2,1)S(1)}, f32[1,896]{1,0:T(1,128)S(1)}, f32[1,1024]{1,0:T(1,128)S(1)}) custom-call(bf16[96,1024]{1,0:T(8,128)(2,1)S(1)} %get-tuple-element.25.refs_0_, bf16[96,1024]{1,0:T(8,128)(2,1)S(1)} %collective-permute-done.2.refs_1_, bf16[96,1024]{1,0:T(8,128)(2,1)S(1)} %collective-permute-done.3.refs_2_, ...), custom_call_target="tpu_custom_call" | custom-call | flops 1207959552 | bytes 7088640 | tf_op jit(solution)/shard_map/scores/pallas_call | solution.py:72
  44.4 0.1 collective-permute-start.9
  44.5 0.8 collective-permute-start.13
  45.2 0.4 collective-permute-done.9.seen
  45.6 1.1 %collective-permute-start.10 = (f32[1,1024]{1,0:T(1,128)S(1)}, f32[1,1024]{1,0:T(1,128)S(1)}, u32[]{:S(2)}, u32[]{:S(2)}) collective-permute-start(f32[1,1024]{1,0:T(1,128)S(1)} %pair.8.mine), channel_id=1, source_target_pairs={{0,16},{16,0},{32,48},{48,32},{64,80},{80,64},{96,112},{112,96},{1... | collective-permute-start | bytes 12296 | tf_op jit(solution)/shard_map/ppermute | solution.py:364
  46.7 1.4 %collective-permute-done.13.seen = f32[1,896]{1,0:T(1,128)S(1)} collective-permute-done((f32[1,896]{1,0:T(1,128)S(1)}, f32[1,896]{1,0:T(1,128)S(1)}, u32[]{:S(2)}, u32[]{:S(2)}) %collective-permute-start.13) | collective-permute-done | bytes 3616 | tf_op jit(solution)/shard_map/ppermute | solution.py:364
  48.2 0.7 collective-permute-start.14
  48.9 0.5 collective-permute-done.10.seen
  49.3 1.6 %collective-permute-start.11 = (f32[1,1024]{1,0:T(1,128)S(1)}, f32[1,1024]{1,0:T(1,128)S(1)}, u32[]{:S(2)}, u32[]{:S(2)}) collective-permute-start(f32[1,1024]{1,0:T(1,128)S(1)} %pair.9.mine), channel_id=1, source_target_pairs={{0,32},{16,48},{32,0},{48,16},{64,96},{80,112},{96,64},{112,80},{1... | collective-permute-start | bytes 12296 | tf_op jit(solution)/shard_map/ppermute | solution.py:364
  50.9 2.4 %collective-permute-done.14.seen = f32[1,896]{1,0:T(1,128)S(1)} collective-permute-done((f32[1,896]{1,0:T(1,128)S(1)}, f32[1,896]{1,0:T(1,128)S(1)}, u32[]{:S(2)}, u32[]{:S(2)}) %collective-permute-start.14) | collective-permute-done | bytes 3616 | tf_op jit(solution)/shard_map/ppermute | solution.py:364
  53.4 0.3 collective-permute-start.15
  53.6 0.3 collective-permute-done.11.seen
  54.0 1.3 %collective-permute-start.12 = (f32[1,1024]{1,0:T(1,128)S(1)}, f32[1,1024]{1,0:T(1,128)S(1)}, u32[]{:S(2)}, u32[]{:S(2)}) collective-permute-start(f32[1,1024]{1,0:T(1,128)S(1)} %pair.10.mine), channel_id=1, source_target_pairs={{0,64},{16,80},{32,96},{48,112},{64,0},{80,16},{96,32},{112,48},{1... | collective-permute-start | bytes 12296 | tf_op jit(solution)/shard_map/ppermute | solution.py:364
  55.3 2.0 %collective-permute-done.15.seen = f32[1,896]{1,0:T(1,128)S(1)} collective-permute-done((f32[1,896]{1,0:T(1,128)S(1)}, f32[1,896]{1,0:T(1,128)S(1)}, u32[]{:S(2)}, u32[]{:S(2)}) %collective-permute-start.15) | collective-permute-done | bytes 3616 | tf_op jit(solution)/shard_map/ppermute | solution.py:364
  57.2 0.1 collective-permute-start.16
  57.3 5.1 %collective-permute-done.16.seen = f32[1,896]{1,0:T(1,128)S(1)} collective-permute-done((f32[1,896]{1,0:T(1,128)S(1)}, f32[1,896]{1,0:T(1,128)S(1)}, u32[]{:S(2)}, u32[]{:S(2)}) %collective-permute-start.16) | collective-permute-done | bytes 3616 | tf_op jit(solution)/shard_map/ppermute | solution.py:364
  62.5 2.7 %text_grad.1 = (bf16[768,768]{1,0:T(8,128)(2,1)S(1)}, f32[8,128]{1,0:T(8,128)S(1)}, f32[384,1024]{1,0:T(8,128)S(1)}, bf16[400,1024]{1,0:T(8,128)(2,1)S(1)}) custom-call(f32[1,1024]{1,0:T(1,128)S(1)} %pair.11.cols, f32[1,896]{1,0:T(1,128)S(1)} %pair.15.rows_lse, f32[768,768]{1,0:T(8,128)S(1)} %get-tuple-element.29.scores, bf16[768,1024]{1,0:T(8,128)(2,1)S(1)} %bitcast.3, ...), custom_call_target="tpu_custom_call" | custom-call | flops 1207959552 | bytes 7518720 | tf_op jit(solution)/shard_map/text_grad/pallas_call | solution.py:72
  65.2 0.1 collective-permute-start.17
  65.3 2.3 %collective-permute-done.17.seen = bf16[400,1024]{1,0:T(8,128)(2,1)S(1)} collective-permute-done((bf16[400,1024]{1,0:T(8,128)(2,1)S(1)}, bf16[400,1024]{1,0:T(8,128)(2,1)S(1)}, u32[]{:S(2)}, u32[]{:S(2)}) %collective-permute-start.17) | collective-permute-done | bytes 819232 | tf_op jit(solution)/shard_map/ppermute | solution.py:403
  67.6 0.7 send.1
  68.3 1.1 %collective-permute-start.18 = (bf16[784,128]{1,0:T(8,128)(2,1)S(1)}, bf16[784,128]{1,0:T(8,128)(2,1)S(1)}, u32[]{:S(2)}, u32[]{:S(2)}) collective-permute-start(bf16[784,128]{1,0:T(8,128)(2,1)S(1)} %get-tuple-element.37), channel_id=1, source_target_pairs={{0,16},{16,32},{32,48},{48,64},{64,80},{80,96},{96,112},{112,0},{1... | collective-permute-start | bytes 602120 | tf_op jit(solution)/shard_map/ppermute | solution.py:21
  69.4 1.5 %collective-permute-start.19 = (bf16[784,128]{1,0:T(8,128)(2,1)S(1)}, bf16[784,128]{1,0:T(8,128)(2,1)S(1)}, u32[]{:S(2)}, u32[]{:S(2)}) collective-permute-start(bf16[784,128]{1,0:T(8,128)(2,1)S(1)} %get-tuple-element.38), channel_id=1, source_target_pairs={{0,32},{16,48},{32,64},{48,80},{64,96},{80,112},{96,0},{112,16},{1... | collective-permute-start | bytes 602120 | tf_op jit(solution)/shard_map/ppermute | solution.py:21
  70.9 2.2 %collective-permute-start.20 = (bf16[784,128]{1,0:T(8,128)(2,1)S(1)}, bf16[784,128]{1,0:T(8,128)(2,1)S(1)}, u32[]{:S(2)}, u32[]{:S(2)}) collective-permute-start(bf16[784,128]{1,0:T(8,128)(2,1)S(1)} %get-tuple-element.39), channel_id=1, source_target_pairs={{0,112},{16,0},{32,16},{48,32},{64,48},{80,64},{96,80},{112,96},{1... | collective-permute-start | bytes 602120 | tf_op jit(solution)/shard_map/ppermute | solution.py:21
  73.1 2.5 %image_grad.1 = bf16[16,400,128]{2,1,0:T(8,128)(2,1)} custom-call(bf16[768,768]{1,0:T(8,128)(2,1)S(1)} %get-tuple-element.30.grads, bf16[768,1024]{1,0:T(8,128)(2,1)S(1)} %get-tuple-element.31.text, f32[8,128]{1,0:T(8,128)S(1)} %get-tuple-element.32.terms), custom_call_target="tpu_custom_call" | custom-call | flops 1207959552 | bytes 4395008 | tf_op jit(solution)/shard_map/image_grad/pallas_call | solution.py:72
  75.6 5.0 %all-to-all-start.1 = ((bf16[16,400,128]{2,1,0:T(8,128)(2,1)}), bf16[16,400,128]{2,1,0:T(8,128)(2,1)S(1)}, u32[]{:S(2)}, u32[]{:S(2)}) async-start(bf16[16,400,128]{2,1,0:T(8,128)(2,1)} %image_grad.1), calls=%async_computation.1 | async-start | bytes 3276800 | tf_op jit(solution)/shard_map/all_to_all | solution.py:398
  80.6 1.3 %collective-permute-done.19.refs_1_ = bf16[784,128]{1,0:T(8,128)(2,1)S(1)} collective-permute-done((bf16[784,128]{1,0:T(8,128)(2,1)S(1)}, bf16[784,128]{1,0:T(8,128)(2,1)S(1)}, u32[]{:S(2)}, u32[]{:S(2)}) %collective-permute-start.19) | collective-permute-done | bytes 200736 | tf_op jit(solution)/shard_map/ppermute | solution.py:21
  81.9 0.4 relay.1
  82.3 3.1 %collective-permute-start.21 = (bf16[400,128]{1,0:T(8,128)(2,1)S(1)}, bf16[400,128]{1,0:T(8,128)(2,1)S(1)}, u32[]{:S(2)}, u32[]{:S(2)}) collective-permute-start(bf16[400,128]{1,0:T(8,128)(2,1)S(1)} %get-tuple-element.42), channel_id=1, source_target_pairs={{0,64},{16,80},{32,96},{48,112},{64,0},{80,16},{96,32},{112,48},{1... | collective-permute-start | bytes 307208 | tf_op jit(solution)/shard_map/ppermute | solution.py:21
  85.4 7.1 %collective-permute-done.21.pay = bf16[400,128]{1,0:T(8,128)(2,1)S(1)} collective-permute-done((bf16[400,128]{1,0:T(8,128)(2,1)S(1)}, bf16[400,128]{1,0:T(8,128)(2,1)S(1)}, u32[]{:S(2)}, u32[]{:S(2)}) %collective-permute-start.21) | collective-permute-done | bytes 102432 | tf_op jit(solution)/shard_map/ppermute | solution.py:21
  92.5 0.8 text_sum.1
  93.3 11.6 %all-to-all-done.1.got = bf16[16,400,128]{2,1,0:T(8,128)(2,1)S(1)} async-done(((bf16[16,400,128]{2,1,0:T(8,128)(2,1)}), bf16[16,400,128]{2,1,0:T(8,128)(2,1)S(1)}, u32[]{:S(2)}, u32[]{:S(2)}) %all-to-all-start.1) | async-done | bytes 1638432 | tf_op jit(solution)/shard_map/all_to_all | solution.py:398
  104.8 1.7 %image_sum.1 = (f32[48,1024]{1,0:T(8,128)}, f32[1,1]{1,0:T(1,128)}) custom-call(bf16[16,400,128]{2,1,0:T(8,128)(2,1)S(1)} %all-to-all-done.1.got, f32[8,128]{1,0:T(8,128)S(1)} %get-tuple-element.32.terms, f32[1,128]{1,0:T(1,128)S(1)} %get-tuple-element.43.side), custom_call_target="tpu_custom_call" | custom-call | bytes 1839620 | tf_op jit(solution)/shard_map/image_sum/pallas_call | solution.py:72
  (21 shorter events, 0.2 us)
Async XLA Ops:
  0.6 18.3 %collective-permute-start = (bf16[48,1024]{1,0:T(8,128)(2,1)}, bf16[48,1024]{1,0:T(8,128)(2,1)S(1)}, u32[]{:S(2)}, u32[]{:S(2)}) collective-permute-start(bf16[48,1024]{1,0:T(8,128)(2,1)} %near.1), channel_id=1, source_target_pairs={{0,64},{16,80},{32,96},{48,112},{64,0},{80,16},{96,32},{112,48},{1... | collective-permute-start | bytes 294920 | tf_op jit(solution)/shard_map/ppermute | solution.py:21
  7.9 11.0 %collective-permute-start.1 = (s32[384]{0:T(512)}, s32[384]{0:T(512)S(1)}, u32[]{:S(2)}, u32[]{:S(2)}) collective-permute-start(s32[384]{0:T(512)} %mine.1), channel_id=1, source_target_pairs={{0,128},{128,0},{1,129},{129,1},{2,130},{130,2},{3,131},{131,3},{4... | collective-permute-start | bytes 4616 | tf_op jit(solution)/shard_map/ppermute | solution.py:325
  11.0 8.0 %copy-start = (bf16[48,1024]{1,0:T(8,128)(2,1)S(1)}, bf16[48,1024]{1,0:T(8,128)(2,1)}, u32[]{:S(2)}) copy-start(bf16[48,1024]{1,0:T(8,128)(2,1)} %near.1) | copy-start | bytes 294916
  11.0 8.0 %copy-start.1 = (s32[384]{0:T(512)S(1)}, s32[384]{0:T(512)}, u32[]{:S(2)}) copy-start(s32[384]{0:T(512)} %mine.1) | copy-start | bytes 4612
  11.0 30.3 %all-to-all-start = ((bf16[16,48,1024]{2,1,0:T(8,128)(2,1)}), bf16[16,48,1024]{2,1,0:T(8,128)(2,1)S(1)}, u32[]{:S(2)}, u32[]{:S(2)}) async-start(bf16[16,48,1024]{2,1,0:T(8,128)(2,1)} %copies.1), calls=%async_computation | async-start | bytes 3145728 | tf_op jit(solution)/shard_map/all_to_all | solution.py:334
  19.0 7.0 %collective-permute-start.4 = (bf16[96,1024]{1,0:T(8,128)(2,1)S(1)}, bf16[96,1024]{1,0:T(8,128)(2,1)S(1)}, u32[]{:S(2)}, u32[]{:S(2)}) collective-permute-start(bf16[96,1024]{1,0:T(8,128)(2,1)S(1)} %get-tuple-element.25.refs_0_), channel_id=1, source_target_pairs={{0,16},{16,32},{32,48},{48,64},{64,80},{80,96},{96,112},{112,0},{1... | collective-permute-start | bytes 589832 | tf_op jit(solution)/shard_map/ppermute | solution.py:21
  20.1 10.6 %collective-permute-start.3 = (bf16[96,1024]{1,0:T(8,128)(2,1)S(1)}, bf16[96,1024]{1,0:T(8,128)(2,1)S(1)}, u32[]{:S(2)}, u32[]{:S(2)}) collective-permute-start(bf16[96,1024]{1,0:T(8,128)(2,1)S(1)} %get-tuple-element.25.refs_0_), channel_id=1, source_target_pairs={{0,96},{16,112},{32,0},{48,16},{64,32},{80,48},{96,64},{112,80},{1... | collective-permute-start | bytes 589832 | tf_op jit(solution)/shard_map/ppermute | solution.py:21
  20.6 14.3 %collective-permute-start.2 = (bf16[96,1024]{1,0:T(8,128)(2,1)S(1)}, bf16[96,1024]{1,0:T(8,128)(2,1)S(1)}, u32[]{:S(2)}, u32[]{:S(2)}) collective-permute-start(bf16[96,1024]{1,0:T(8,128)(2,1)S(1)} %get-tuple-element.25.refs_0_), channel_id=1, source_target_pairs={{0,112},{16,0},{32,16},{48,32},{64,48},{80,64},{96,80},{112,96},{1... | collective-permute-start | bytes 589832 | tf_op jit(solution)/shard_map/ppermute | solution.py:21
  22.3 12.6 %collective-permute-start.5 = (bf16[96,1024]{1,0:T(8,128)(2,1)S(1)}, bf16[96,1024]{1,0:T(8,128)(2,1)S(1)}, u32[]{:S(2)}, u32[]{:S(2)}) collective-permute-start(bf16[96,1024]{1,0:T(8,128)(2,1)S(1)} %get-tuple-element.25.refs_0_), channel_id=1, source_target_pairs={{0,8},{8,0},{1,9},{9,1},{2,10},{10,2},{3,11},{11,3},{4,12},{12,4},... | collective-permute-start | bytes 589832 | tf_op jit(solution)/shard_map/ppermute | solution.py:346
  25.9 9.0 %collective-permute-start.8 = (bf16[96,1024]{1,0:T(8,128)(2,1)S(1)}, bf16[96,1024]{1,0:T(8,128)(2,1)S(1)}, u32[]{:S(2)}, u32[]{:S(2)}) collective-permute-start(bf16[96,1024]{1,0:T(8,128)(2,1)S(1)} %collective-permute-done.4.refs_3_), channel_id=1, source_target_pairs={{0,8},{8,0},{1,9},{9,1},{2,10},{10,2},{3,11},{11,3},{4,12},{12,4},... | collective-permute-start | bytes 589832 | tf_op jit(solution)/shard_map/ppermute | solution.py:346
  30.7 4.3 %collective-permute-start.7 = (bf16[96,1024]{1,0:T(8,128)(2,1)S(1)}, bf16[96,1024]{1,0:T(8,128)(2,1)S(1)}, u32[]{:S(2)}, u32[]{:S(2)}) collective-permute-start(bf16[96,1024]{1,0:T(8,128)(2,1)S(1)} %collective-permute-done.3.refs_2_), channel_id=1, source_target_pairs={{0,8},{8,0},{1,9},{9,1},{2,10},{10,2},{3,11},{11,3},{4,12},{12,4},... | collective-permute-start | bytes 589832 | tf_op jit(solution)/shard_map/ppermute | solution.py:346
  34.9 1.4 %collective-permute-start.6 = (bf16[96,1024]{1,0:T(8,128)(2,1)S(1)}, bf16[96,1024]{1,0:T(8,128)(2,1)S(1)}, u32[]{:S(2)}, u32[]{:S(2)}) collective-permute-start(bf16[96,1024]{1,0:T(8,128)(2,1)S(1)} %collective-permute-done.2.refs_1_), channel_id=1, source_target_pairs={{0,8},{8,0},{1,9},{9,1},{2,10},{10,2},{3,11},{11,3},{4,12},{12,4},... | collective-permute-start | bytes 589832 | tf_op jit(solution)/shard_map/ppermute | solution.py:346
  44.4 1.3 %collective-permute-start.9 = (f32[1,1024]{1,0:T(1,128)S(1)}, f32[1,1024]{1,0:T(1,128)S(1)}, u32[]{:S(2)}, u32[]{:S(2)}) collective-permute-start(f32[1,1024]{1,0:T(1,128)S(1)} %get-tuple-element.27.mine), channel_id=1, source_target_pairs={{0,8},{8,0},{1,9},{9,1},{2,10},{10,2},{3,11},{11,3},{4,12},{12,4},... | collective-permute-start | bytes 12296 | tf_op jit(solution)/shard_map/ppermute | solution.py:364
  44.5 3.7 %collective-permute-start.13 = (f32[1,896]{1,0:T(1,128)S(1)}, f32[1,896]{1,0:T(1,128)S(1)}, u32[]{:S(2)}, u32[]{:S(2)}) collective-permute-start(f32[1,896]{1,0:T(1,128)S(1)} %get-tuple-element.28.mine), channel_id=1, source_target_pairs={{0,128},{128,0},{1,129},{129,1},{2,130},{130,2},{3,131},{131,3},{4... | collective-permute-start | bytes 10760 | tf_op jit(solution)/shard_map/ppermute | solution.py:364
  45.6 3.7 %collective-permute-start.10 = (f32[1,1024]{1,0:T(1,128)S(1)}, f32[1,1024]{1,0:T(1,128)S(1)}, u32[]{:S(2)}, u32[]{:S(2)}) collective-permute-start(f32[1,1024]{1,0:T(1,128)S(1)} %pair.8.mine), channel_id=1, source_target_pairs={{0,16},{16,0},{32,48},{48,32},{64,80},{80,64},{96,112},{112,96},{1... | collective-permute-start | bytes 12296 | tf_op jit(solution)/shard_map/ppermute | solution.py:364
  48.2 5.2 %collective-permute-start.14 = (f32[1,896]{1,0:T(1,128)S(1)}, f32[1,896]{1,0:T(1,128)S(1)}, u32[]{:S(2)}, u32[]{:S(2)}) collective-permute-start(f32[1,896]{1,0:T(1,128)S(1)} %pair.12.mine), channel_id=1, source_target_pairs={{0,1},{1,0},{2,3},{3,2},{4,5},{5,4},{6,7},{7,6},{8,9},{9,8},{10,11... | collective-permute-start | bytes 10760 | tf_op jit(solution)/shard_map/ppermute | solution.py:364
  49.3 4.6 %collective-permute-start.11 = (f32[1,1024]{1,0:T(1,128)S(1)}, f32[1,1024]{1,0:T(1,128)S(1)}, u32[]{:S(2)}, u32[]{:S(2)}) collective-permute-start(f32[1,1024]{1,0:T(1,128)S(1)} %pair.9.mine), channel_id=1, source_target_pairs={{0,32},{16,48},{32,0},{48,16},{64,96},{80,112},{96,64},{112,80},{1... | collective-permute-start | bytes 12296 | tf_op jit(solution)/shard_map/ppermute | solution.py:364
  53.4 3.9 %collective-permute-start.15 = (f32[1,896]{1,0:T(1,128)S(1)}, f32[1,896]{1,0:T(1,128)S(1)}, u32[]{:S(2)}, u32[]{:S(2)}) collective-permute-start(f32[1,896]{1,0:T(1,128)S(1)} %pair.13.mine), channel_id=1, source_target_pairs={{0,2},{2,0},{4,6},{6,4},{1,3},{3,1},{5,7},{7,5},{8,10},{10,8},{12,... | collective-permute-start | bytes 10760 | tf_op jit(solution)/shard_map/ppermute | solution.py:364
  54.0 8.5 %collective-permute-start.12 = (f32[1,1024]{1,0:T(1,128)S(1)}, f32[1,1024]{1,0:T(1,128)S(1)}, u32[]{:S(2)}, u32[]{:S(2)}) collective-permute-start(f32[1,1024]{1,0:T(1,128)S(1)} %pair.10.mine), channel_id=1, source_target_pairs={{0,64},{16,80},{32,96},{48,112},{64,0},{80,16},{96,32},{112,48},{1... | collective-permute-start | bytes 12296 | tf_op jit(solution)/shard_map/ppermute | solution.py:364
  57.2 5.2 %collective-permute-start.16 = (f32[1,896]{1,0:T(1,128)S(1)}, f32[1,896]{1,0:T(1,128)S(1)}, u32[]{:S(2)}, u32[]{:S(2)}) collective-permute-start(f32[1,896]{1,0:T(1,128)S(1)} %pair.14.mine), channel_id=1, source_target_pairs={{0,4},{2,6},{4,0},{6,2},{1,5},{3,7},{5,1},{7,3},{8,12},{10,14},{12... | collective-permute-start | bytes 10760 | tf_op jit(solution)/shard_map/ppermute | solution.py:364
  65.2 2.4 %collective-permute-start.17 = (bf16[400,1024]{1,0:T(8,128)(2,1)S(1)}, bf16[400,1024]{1,0:T(8,128)(2,1)S(1)}, u32[]{:S(2)}, u32[]{:S(2)}) collective-permute-start(bf16[400,1024]{1,0:T(8,128)(2,1)S(1)} %get-tuple-element.34), channel_id=1, source_target_pairs={{0,8},{8,0},{1,9},{9,1},{2,10},{10,2},{3,11},{11,3},{4,12},{12,4},... | collective-permute-start | bytes 2457608 | tf_op jit(solution)/shard_map/ppermute | solution.py:403
  68.3 12.3 %collective-permute-start.18 = (bf16[784,128]{1,0:T(8,128)(2,1)S(1)}, bf16[784,128]{1,0:T(8,128)(2,1)S(1)}, u32[]{:S(2)}, u32[]{:S(2)}) collective-permute-start(bf16[784,128]{1,0:T(8,128)(2,1)S(1)} %get-tuple-element.37), channel_id=1, source_target_pairs={{0,16},{16,32},{32,48},{48,64},{64,80},{80,96},{96,112},{112,0},{1... | collective-permute-start | bytes 602120 | tf_op jit(solution)/shard_map/ppermute | solution.py:21
  69.4 12.5 %collective-permute-start.19 = (bf16[784,128]{1,0:T(8,128)(2,1)S(1)}, bf16[784,128]{1,0:T(8,128)(2,1)S(1)}, u32[]{:S(2)}, u32[]{:S(2)}) collective-permute-start(bf16[784,128]{1,0:T(8,128)(2,1)S(1)} %get-tuple-element.38), channel_id=1, source_target_pairs={{0,32},{16,48},{32,64},{48,80},{64,96},{80,112},{96,0},{112,16},{1... | collective-permute-start | bytes 602120 | tf_op jit(solution)/shard_map/ppermute | solution.py:21
  70.9 11.0 %collective-permute-start.20 = (bf16[784,128]{1,0:T(8,128)(2,1)S(1)}, bf16[784,128]{1,0:T(8,128)(2,1)S(1)}, u32[]{:S(2)}, u32[]{:S(2)}) collective-permute-start(bf16[784,128]{1,0:T(8,128)(2,1)S(1)} %get-tuple-element.39), channel_id=1, source_target_pairs={{0,112},{16,0},{32,16},{48,32},{64,48},{80,64},{96,80},{112,96},{1... | collective-permute-start | bytes 602120 | tf_op jit(solution)/shard_map/ppermute | solution.py:21
  75.6 29.2 %all-to-all-start.1 = ((bf16[16,400,128]{2,1,0:T(8,128)(2,1)}), bf16[16,400,128]{2,1,0:T(8,128)(2,1)S(1)}, u32[]{:S(2)}, u32[]{:S(2)}) async-start(bf16[16,400,128]{2,1,0:T(8,128)(2,1)} %image_grad.1), calls=%async_computation.1 | async-start | bytes 3276800 | tf_op jit(solution)/shard_map/all_to_all | solution.py:398
  82.3 10.2 %collective-permute-start.21 = (bf16[400,128]{1,0:T(8,128)(2,1)S(1)}, bf16[400,128]{1,0:T(8,128)(2,1)S(1)}, u32[]{:S(2)}, u32[]{:S(2)}) collective-permute-start(bf16[400,128]{1,0:T(8,128)(2,1)S(1)} %get-tuple-element.42), channel_id=1, source_target_pairs={{0,64},{16,80},{32,96},{48,112},{64,0},{80,16},{96,32},{112,48},{1... | collective-permute-start | bytes 307208 | tf_op jit(solution)/shard_map/ppermute | solution.py:21

commit v10 on v9

--- a/solution.py
+++ b/solution.py
@@ -91,22 +91,27 @@
         copy.wait()
 
 
-def join_body(near, far, mine, seen, out, pair):
+def join_body(near, far, out):
+    rows = near.shape[0]
+    out[:rows, :] = near[...]
+    out[rows:, :] = far[...]
+
+
+def pair_row(mine, seen):
     first = lax.axis_index("xl") == 0
     left = mine[...].astype(F32)[None, :]
     right = seen[...].astype(F32)[None, :]
-    pair[...] = jnp.concatenate(
+    return jnp.concatenate(
         [jnp.where(first, left, right), jnp.where(first, right, left)], axis=1
     )
-    rows = near.shape[0]
-    out[:rows, :] = near[...]
-    out[rows:, :] = far[...]
 
 
 def score_body(steps, inv_root, *refs):
     n_z = 2 * len(steps)
     pieces, refs = refs[:n_z], refs[n_z:]
-    image, pair, scores, text, row_sent, col_sent = refs
+    image, pair_mine, pair_seen, pair_out, row_exp, col_exp, text, row_sent, col_sent, tops = refs
+    pair = pair_row(pair_mine, pair_seen)
+    pair_out[...] = pair
     rows = pieces[0].shape[0] // 2
     size = image.shape[0]
     ids = labels(n_z, rows)
@@ -133,16 +138,22 @@
             )
             * inv_root
         )
-        scores[r : r + step, :] = tile
+        col_exp[r : r + step, :] = tile
         top = jnp.max(tile, axis=1, keepdims=True)
-        part = top + jnp.log(jnp.sum(jnp.exp(tile - top), axis=1, keepdims=True))
-        row_sent[:, r : r + step] = to_row(part)
+        mass = jnp.exp(tile - top)
+        row_exp[r : r + step, :] = mass
+        part = jnp.log(jnp.sum(mass, axis=1, keepdims=True))
+        tops[0:1, r : r + step] = to_row(top)
+        row_sent[:, r : r + step] = to_row(top + part)
         hit = to_column(pair[:, r : r + step]) == ids
         found += jnp.sum(jnp.where(hit, tile, 0.0), axis=0, keepdims=True)
     row_sent[:, size:] = jnp.full((1, LANES), jnp.max(high))
-    tile = scores[...]
+    tile = col_exp[...]
     top = jnp.max(tile, axis=0, keepdims=True)
-    col_sent[:, :size] = top + jnp.log(jnp.sum(jnp.exp(tile - top), axis=0, keepdims=True))
+    mass = jnp.exp(tile - top)
+    col_exp[...] = mass
+    tops[1:2, :] = top
+    col_sent[:, :size] = top + jnp.log(jnp.sum(mass, axis=0, keepdims=True))
     high = jnp.max(jnp.abs(image[...].astype(F32)))
     col_sent[:, size : size + LANES] = jnp.full((1, LANES), high)
     col_sent[:, size + LANES :] = jnp.full((1, LANES), jnp.sum(found))
@@ -174,10 +185,13 @@
         out[:, at] = mine[:, at] + seen[:, at]
 
 
-def text_body(n_z, inv_root, cols, rows_lse, scores, image, pair, grads, terms, own, other):
-    size = scores.shape[0]
+def grad_body(n_z, inv_root, *refs):
+    cols, rows_lse, tops, row_exp, col_exp, text, image, pair = refs[:8]
+    terms, own, other, sent, grads, held, crossing, staying, sems = refs[8:]
+    size = grads.shape[0]
     half = own.shape[0]
     rows = half // n_z
+    _, tall, _ = sent.shape
     col_lse = cols[:, :size]
     image_max = cols[:, size : size + LANES]
     found = cols[:, size + LANES :]
@@ -187,39 +201,21 @@
     row_terms = jnp.broadcast_to(jnp.sum(row_lse, axis=1, keepdims=True), (1, LANES))
     col_terms = jnp.sum(col_lse, axis=1, keepdims=True) - 2.0 * found
     terms[...] = jnp.concatenate(
-        [row_terms, text_max, image_max, col_terms, jnp.zeros((4, LANES), F32)], axis=0
-    )
-    scale = inverse(image_max[:, :1]) * inv_root
-    row_column = to_column(row_lse)
+        [row_terms, text_max, image_max, jnp.zeros((5, LANES), F32)], axis=0
+    )
+    row_part = to_column(0.5 * jnp.exp(tops[0:1, :] - row_lse))
+    col_part = 0.5 * jnp.exp(tops[1:2, :] - col_lse)
     pair_column = to_column(pair[...])
-    for start in (half, 0):
-        at = slice(start, start + half)
-        tile = scores[:, at]
-        probs = 0.5 * (jnp.exp(tile - row_column) + jnp.exp(tile - col_lse[:, at]))
-        grad = (probs - jnp.where(pair_column == ids[:, at], 1.0, 0.0)).astype(BF16)
-        grads[:, at] = grad
-        part = lax.dot_general(
-            grad, image[...], (((0,), (0,)), ((), ())), preferred_element_type=F32
-        )
-        if start == 0:
-            own[...] = part * scale
-        else:
-            other[:half, :] = encode(part * scale)
-    extra = split3(row_terms)
-    other[half:, :] = jnp.concatenate([extra] * (other.shape[1] // LANES), axis=1)
-
-
-def image_body(inv_root, grads, text, terms, sent, held, sems):
-    size = grads.shape[0]
-    n_plane, tall, _ = sent.shape
-    rows = size // n_plane
-    extra = split3(terms[3:4, :])
-    scale = inverse(terms[1:2, :1]) * inv_root
+    extra = split3(col_terms)
+    scale = inverse(text_max[:, :1]) * inv_root
     step = size // 4
     copies = []
     for r in range(0, size, step):
-        part = jnp.dot(grads[r : r + step, :], text[...], preferred_element_type=F32)
-        part = encode(part * scale)
+        at = slice(r, r + step)
+        probs = row_exp[at, :] * row_part[at, :] + col_exp[at, :] * col_part
+        grad = (probs - jnp.where(pair_column[at, :] == ids, 1.0, 0.0)).astype(BF16)
+        grads[at, :] = grad
+        part = encode(jnp.dot(grad, text[...], preferred_element_type=F32) * scale)
         for p in range(step // rows):
             to = r // rows + p
             for k in range(text.shape[1] // LANES):
@@ -229,6 +225,23 @@
             held[to, tall - EXTRA :, :] = extra
             copies.append(pltpu.make_async_copy(held.at[to], sent.at[to], sems.at[to]))
             copies[-1].start()
+    scale = inverse(image_max[:, :1]) * inv_root
+    extra = split3(row_terms)
+    crossing[half:, :] = jnp.concatenate([extra] * (own.shape[1] // LANES), axis=1)
+    for start in (0, half):
+        part = lax.dot_general(
+            grads[:, start : start + half],
+            image[...],
+            (((0,), (0,)), ((), ())),
+            preferred_element_type=F32,
+        )
+        if start == 0:
+            staying[...] = part * scale
+            copies.append(pltpu.make_async_copy(staying, own, sems.at[sent.shape[0]]))
+        else:
+            crossing[:half, :] = encode(part * scale)
+            copies.append(pltpu.make_async_copy(crossing, other, sems.at[sent.shape[0] + 1]))
+        copies[-1].start()
     for copy in copies:
         copy.wait()
 
@@ -323,38 +336,37 @@
     tall = width // LANES * rows + EXTRA
 
     pair_seen = lax.ppermute(pair_index, "xl", SWAP)
-    copies = pl.pallas_call(
+    (copies,) = call(
         copies_body,
-        out_shape=shape((n_plane, rows, width), BF16),
-        in_specs=[pl.BlockSpec(memory_space=pltpu.VMEM)],
-        out_specs=pl.BlockSpec(memory_space=pl.ANY),
-        scratch_shapes=[pltpu.SemaphoreType.DMA((n_plane,))],
-        name="copies",
-    )(image_embed)
+        (pltpu.HBM((n_plane, rows, width), BF16),),
+        (image_embed,),
+        "copies",
+        hbm_out=(0,),
+        scratch=[pltpu.SemaphoreType.DMA((n_plane,))],
+    )
     image = lax.all_to_all(copies, PLANE, 0, 0).reshape(size, width)
 
     steps = [q if q <= n_z // 4 else q - n_z // 2 for q in range(n_z // 2)]
     far = turn(text_embed, "z", n_z // 2)
-    joined, pair = call(
-        join_body,
-        (shape((2 * rows, width), BF16), shape((1, size), F32)),
-        (text_embed, far, pair_index, pair_seen),
-        "join",
-        10**11,
+    (joined,) = call(
+        join_body, (shape((2 * rows, width), BF16),), (text_embed, far), "join", 10**11
     )
     pieces = [joined] + [turn(joined, "z", -q) for q in steps[1:]]
     pieces = pieces + [lax.ppermute(piece, "c", SWAP) for piece in pieces]
 
     flops = 2 * size * size * width
-    scores, text, row_part, col_part = call(
+    pair, row_exp, col_exp, text, row_part, col_part, tops = call(
         functools.partial(score_body, steps, inv_root),
         (
+            shape((1, size), F32),
+            shape((size, size), F32),
             shape((size, size), F32),
             shape((size, width), BF16),
             shape((1, size + LANES), F32),
             shape((1, size + 2 * LANES), F32),
+            shape((2, size), F32),
         ),
-        (*pieces, image, pair),
+        (*pieces, image, pair_index, pair_seen),
         "scores",
         flops,
         2 * size * size,
@@ -370,29 +382,25 @@
     for axis, step in (("xl", 1), ("xh", 1), ("y", 1), ("y", 2)):
         row_part = exchange(row_part, axis, step)
 
-    grads, terms, text_own, text_other = call(
-        functools.partial(text_body, n_z, inv_root),
+    terms, text_own, text_other, image_sent = call(
+        functools.partial(grad_body, n_z, inv_root),
         (
-            shape((size, size), BF16),
             shape((8, LANES), F32),
-            shape((half, width), F32),
-            shape((half + EXTRA, width), BF16),
+            pltpu.HBM((half, width), F32),
+            pltpu.HBM((half + EXTRA, width), BF16),
+            pltpu.HBM((n_plane, tall, LANES), BF16),
         ),
-        (col_part, row_part, scores, image, pair),
-        "text_grad",
-        flops,
-        2 * size * size,
-    )
-    (image_sent,) = call(
-        functools.partial(image_body, inv_root),
-        (pltpu.HBM((n_plane, tall, LANES), BF16),),
-        (grads, text, terms),
-        "image_grad",
-        flops,
-        hbm_out=(0,),
+        (col_part, row_part, tops, row_exp, col_exp, text, image, pair),
+        "grads",
+        2 * flops,
+        0,
+        hbm_out=(1, 2, 3),
         scratch=[
+            pltpu.VMEM((size, size), BF16),
             pltpu.VMEM((n_plane, tall, LANES), BF16),
-            pltpu.SemaphoreType.DMA((n_plane,)),
+            pltpu.VMEM((half + EXTRA, width), BF16),
+            pltpu.VMEM((half, width), F32),
+            pltpu.SemaphoreType.DMA((n_plane + 2,)),
         ],
     )
     image_got = lax.all_to_all(image_sent, PLANE, 0, 0)
@@ -402,6 +410,7 @@
         + (shape((2 * tall - EXTRA, LANES), BF16),) * len(steps[1:]),
         (text_own, lax.ppermute(text_other, "c", SWAP), terms),
         "send",
+        10**10,
         size=1,
     )
     pays = [turn(pay, "z", q) for q, pay in zip(steps[1:], pays)]
@@ -410,7 +419,6 @@
         (shape((rows, width), F32), shape((tall, LANES), BF16), shape((1, LANES), F32)),
         (keep, total, *pays),
         "relay",
-        10**11,
         size=1,
     )
     grad_text, side = call(

time: 107 us -> 105 us (0.981)
  the two profiles are of different devices: /device:TPU:6 before, /device:TPU:1 now
where the time goes in v10:
time: 105 us; the launch traced here: 103 us
  starting transfers between devices  53.3 us (51%)
  waiting for transfers between devices  32.8 us (31%)
  Pallas kernels  13.6 us (13%)
  local copies, waits for them, and re-layouts  2.31 us (2%)
    ppermute x8, waiting for transfers between devices, turn(): lax.ppermute(x, axis, [(i, (i + step) % count) for i in range(count)])  23.8 us
    ppermute x8, starting transfers between devices, turn(): lax.ppermute(x, axis, [(i, (i + step) % count) for i in range(count)])  17.4 us
    pallas_call x16, Pallas kernels, call(): pl.pallas_call(body, out_shape=outs, in_specs=[pl.BlockSpec(memory_space=...  13.6 us
    ppermute x8, starting transfers between devices, exchange(): seen = lax.ppermute(part, axis, [(i, i ^ step) for i in range(count)])  11.8 us
    ppermute x4, starting transfers between devices, shards(): pieces = pieces + [lax.ppermute(piece, 'c', SWAP) for piece in pieces]  8.32 us
    all_to_all x1, starting transfers between devices, shards(): image = lax.all_to_all(copies, PLANE, 0, 0).reshape(size, width)  6.9 us
    ppermute x8, waiting for transfers between devices, exchange(): seen = lax.ppermute(part, axis, [(i, i ^ step) for i in range(count)])  6.78 us
    ppermute x1, starting transfers between devices, shards(): lax.ppermute(text_other, 'c', SWAP)  3.89 us
  transfers between devices with their start and end apart: 24, of which 13 were waited for; matrix products, arithmetic and copies ran while one was open for 0% of the time, Pallas kernels for 3%

profile of v10, /device:TPU:1, one launch (start us, length us, event | category | flops | bytes accessed | tf_op | source)
XLA Modules:
  0.0 103.0 jit_solution(9299880730166133177)
XLA Ops:
  0.6 7.8 %collective-permute-start = (bf16[48,1024]{1,0:T(8,128)(2,1)}, bf16[48,1024]{1,0:T(8,128)(2,1)S(1)}, u32[]{:S(2)}, u32[]{:S(2)}) collective-permute-start(bf16[48,1024]{1,0:T(8,128)(2,1)} %near.1), channel_id=1, source_target_pairs={{0,64},{16,80},{32,96},{48,112},{64,0},{80,16},{96,32},{112,48},{1... | collective-permute-start | bytes 294920 | tf_op jit(solution)/shard_map/ppermute | solution.py:21
  8.5 0.9 copy-done
  9.3 1.3 %copies.1 = bf16[16,48,1024]{2,1,0:T(8,128)(2,1)} custom-call(bf16[48,1024]{1,0:T(8,128)(2,1)S(1)} %copy-done), custom_call_target="tpu_custom_call" | custom-call | bytes 1671168 | tf_op jit(solution)/shard_map/copies/pallas_call | solution.py:72
  10.7 0.0 copy-start.1
  10.7 6.9 %all-to-all-start = ((bf16[16,48,1024]{2,1,0:T(8,128)(2,1)}), bf16[16,48,1024]{2,1,0:T(8,128)(2,1)S(1)}, u32[]{:S(2)}, u32[]{:S(2)}) async-start(bf16[16,48,1024]{2,1,0:T(8,128)(2,1)} %copies.1), calls=%async_computation | async-start | bytes 3145728 | tf_op jit(solution)/shard_map/all_to_all | solution.py:347
  17.6 0.0 copy-start.2
  17.6 0.8 collective-permute-start.3
  18.5 0.3 collective-permute-start.2
  18.7 1.7 %collective-permute-start.1 = (bf16[96,1024]{1,0:T(8,128)(2,1)S(1)}, bf16[96,1024]{1,0:T(8,128)(2,1)S(1)}, u32[]{:S(2)}, u32[]{:S(2)}) collective-permute-start(bf16[96,1024]{1,0:T(8,128)(2,1)S(1)} %join.1.refs_0_), channel_id=1, source_target_pairs={{0,112},{16,0},{32,16},{48,32},{64,48},{80,64},{96,80},{112,96},{1... | collective-permute-start | bytes 589832 | tf_op jit(solution)/shard_map/ppermute | solution.py:21
  20.4 1.8 %collective-permute-start.4 = (bf16[96,1024]{1,0:T(8,128)(2,1)S(1)}, bf16[96,1024]{1,0:T(8,128)(2,1)S(1)}, u32[]{:S(2)}, u32[]{:S(2)}) collective-permute-start(bf16[96,1024]{1,0:T(8,128)(2,1)S(1)} %join.1.refs_0_), channel_id=1, source_target_pairs={{0,8},{8,0},{1,9},{9,1},{2,10},{10,2},{3,11},{11,3},{4,12},{12,4},... | collective-permute-start | bytes 589832 | tf_op jit(solution)/shard_map/ppermute | solution.py:355
  22.2 1.9 %collective-permute-done.3.refs_3_ = bf16[96,1024]{1,0:T(8,128)(2,1)S(1)} collective-permute-done((bf16[96,1024]{1,0:T(8,128)(2,1)S(1)}, bf16[96,1024]{1,0:T(8,128)(2,1)S(1)}, u32[]{:S(2)}, u32[]{:S(2)}) %collective-permute-start.3) | collective-permute-done | bytes 196640 | tf_op jit(solution)/shard_map/ppermute | solution.py:21
  24.1 2.2 %collective-permute-start.7 = (bf16[96,1024]{1,0:T(8,128)(2,1)S(1)}, bf16[96,1024]{1,0:T(8,128)(2,1)S(1)}, u32[]{:S(2)}, u32[]{:S(2)}) collective-permute-start(bf16[96,1024]{1,0:T(8,128)(2,1)S(1)} %collective-permute-done.3.refs_3_), channel_id=1, source_target_pairs={{0,8},{8,0},{1,9},{9,1},{2,10},{10,2},{3,11},{11,3},{4,12},{12,4},... | collective-permute-start | bytes 589832 | tf_op jit(solution)/shard_map/ppermute | solution.py:355
  26.3 2.9 %collective-permute-done.2.refs_2_ = bf16[96,1024]{1,0:T(8,128)(2,1)S(1)} collective-permute-done((bf16[96,1024]{1,0:T(8,128)(2,1)S(1)}, bf16[96,1024]{1,0:T(8,128)(2,1)S(1)}, u32[]{:S(2)}, u32[]{:S(2)}) %collective-permute-start.2) | collective-permute-done | bytes 196640 | tf_op jit(solution)/shard_map/ppermute | solution.py:21
  29.2 2.0 %collective-permute-start.6 = (bf16[96,1024]{1,0:T(8,128)(2,1)S(1)}, bf16[96,1024]{1,0:T(8,128)(2,1)S(1)}, u32[]{:S(2)}, u32[]{:S(2)}) collective-permute-start(bf16[96,1024]{1,0:T(8,128)(2,1)S(1)} %collective-permute-done.2.refs_2_), channel_id=1, source_target_pairs={{0,8},{8,0},{1,9},{9,1},{2,10},{10,2},{3,11},{11,3},{4,12},{12,4},... | collective-permute-start | bytes 589832 | tf_op jit(solution)/shard_map/ppermute | solution.py:355
  31.1 1.8 %collective-permute-done.1.refs_1_ = bf16[96,1024]{1,0:T(8,128)(2,1)S(1)} collective-permute-done((bf16[96,1024]{1,0:T(8,128)(2,1)S(1)}, bf16[96,1024]{1,0:T(8,128)(2,1)S(1)}, u32[]{:S(2)}, u32[]{:S(2)}) %collective-permute-start.1) | collective-permute-done | bytes 196640 | tf_op jit(solution)/shard_map/ppermute | solution.py:21
  33.0 2.4 %collective-permute-start.5 = (bf16[96,1024]{1,0:T(8,128)(2,1)S(1)}, bf16[96,1024]{1,0:T(8,128)(2,1)S(1)}, u32[]{:S(2)}, u32[]{:S(2)}) collective-permute-start(bf16[96,1024]{1,0:T(8,128)(2,1)S(1)} %collective-permute-done.1.refs_1_), channel_id=1, source_target_pairs={{0,8},{8,0},{1,9},{9,1},{2,10},{10,2},{3,11},{11,3},{4,12},{12,4},... | collective-permute-start | bytes 589832 | tf_op jit(solution)/shard_map/ppermute | solution.py:355
  35.4 1.4 %collective-permute-start.8 = (s32[384]{0:T(512)S(1)}, s32[384]{0:T(512)S(1)}, u32[]{:S(2)}, u32[]{:S(2)}) collective-permute-start(s32[384]{0:T(512)S(1)} %copy-done.2), channel_id=1, source_target_pairs={{0,128},{128,0},{1,129},{129,1},{2,130},{130,2},{3,131},{131,3},{4... | collective-permute-start | bytes 4616 | tf_op jit(solution)/shard_map/ppermute | solution.py:338
  36.7 1.4 %collective-permute-done.8.refs_10_ = s32[384]{0:T(512)S(1)} collective-permute-done((s32[384]{0:T(512)S(1)}, s32[384]{0:T(512)S(1)}, u32[]{:S(2)}, u32[]{:S(2)}) %collective-permute-start.8) | collective-permute-done | bytes 1568 | tf_op jit(solution)/shard_map/ppermute | solution.py:338
  38.1 0.8 all-to-all-done
  39.0 3.7 %scores.1 = (f32[1,768]{1,0:T(1,128)S(1)}, f32[768,768]{1,0:T(8,128)S(1)}, f32[768,768]{1,0:T(8,128)S(1)}, bf16[768,1024]{1,0:T(8,128)(2,1)S(1)}, f32[1,896]{1,0...) custom-call(bf16[96,1024]{1,0:T(8,128)(2,1)S(1)} %join.1.refs_0_, ...), custom_call_target="tpu_custom_call" | custom-call | flops 1207959552 | bytes 9457152 | tf_op jit(solution)/shard_map/scores/pallas_call | solution.py:72
  42.6 2.4 %collective-permute-start.9 = (f32[1,1024]{1,0:T(1,128)S(1)}, f32[1,1024]{1,0:T(1,128)S(1)}, u32[]{:S(2)}, u32[]{:S(2)}) collective-permute-start(f32[1,1024]{1,0:T(1,128)S(1)} %get-tuple-element.26.mine), channel_id=1, source_target_pairs={{0,8},{8,0},{1,9},{9,1},{2,10},{10,2},{3,11},{11,3},{4,12},{12,4},... | collective-permute-start | bytes 12296 | tf_op jit(solution)/shard_map/ppermute | solution.py:376
  45.0 1.6 %collective-permute-start.13 = (f32[1,896]{1,0:T(1,128)S(1)}, f32[1,896]{1,0:T(1,128)S(1)}, u32[]{:S(2)}, u32[]{:S(2)}) collective-permute-start(f32[1,896]{1,0:T(1,128)S(1)} %get-tuple-element.27.mine), channel_id=1, source_target_pairs={{0,128},{128,0},{1,129},{129,1},{2,130},{130,2},{3,131},{131,3},{4... | collective-permute-start | bytes 10760 | tf_op jit(solution)/shard_map/ppermute | solution.py:376
  46.6 0.8 collective-permute-start.10
  47.5 0.1 collective-permute-done.13.seen
  47.6 3.8 %collective-permute-start.14 = (f32[1,896]{1,0:T(1,128)S(1)}, f32[1,896]{1,0:T(1,128)S(1)}, u32[]{:S(2)}, u32[]{:S(2)}) collective-permute-start(f32[1,896]{1,0:T(1,128)S(1)} %pair.12.mine), channel_id=1, source_target_pairs={{0,1},{1,0},{2,3},{3,2},{4,5},{5,4},{6,7},{7,6},{8,9},{9,8},{10,11... | collective-permute-start | bytes 10760 | tf_op jit(solution)/shard_map/ppermute | solution.py:376
  51.4 1.3 %collective-permute-start.11 = (f32[1,1024]{1,0:T(1,128)S(1)}, f32[1,1024]{1,0:T(1,128)S(1)}, u32[]{:S(2)}, u32[]{:S(2)}) collective-permute-start(f32[1,1024]{1,0:T(1,128)S(1)} %pair.9.mine), channel_id=1, source_target_pairs={{0,32},{16,48},{32,0},{48,16},{64,96},{80,112},{96,64},{112,80},{1... | collective-permute-start | bytes 12296 | tf_op jit(solution)/shard_map/ppermute | solution.py:376
  52.7 0.3 collective-permute-start.15
  53.0 1.9 %collective-permute-done.11.seen = f32[1,1024]{1,0:T(1,128)S(1)} collective-permute-done((f32[1,1024]{1,0:T(1,128)S(1)}, f32[1,1024]{1,0:T(1,128)S(1)}, u32[]{:S(2)}, u32[]{:S(2)}) %collective-permute-start.11) | collective-permute-done | bytes 4128 | tf_op jit(solution)/shard_map/ppermute | solution.py:376
  54.9 0.1 collective-permute-start.12
  55.0 0.4 collective-permute-done.15.seen
  55.4 1.5 %collective-permute-start.16 = (f32[1,896]{1,0:T(1,128)S(1)}, f32[1,896]{1,0:T(1,128)S(1)}, u32[]{:S(2)}, u32[]{:S(2)}) collective-permute-start(f32[1,896]{1,0:T(1,128)S(1)} %pair.14.mine), channel_id=1, source_target_pairs={{0,4},{2,6},{4,0},{6,2},{1,5},{3,7},{5,1},{7,3},{8,12},{10,14},{12... | collective-permute-start | bytes 10760 | tf_op jit(solution)/shard_map/ppermute | solution.py:376
  57.0 2.5 %collective-permute-done.16.seen = f32[1,896]{1,0:T(1,128)S(1)} collective-permute-done((f32[1,896]{1,0:T(1,128)S(1)}, f32[1,896]{1,0:T(1,128)S(1)}, u32[]{:S(2)}, u32[]{:S(2)}) %collective-permute-start.16) | collective-permute-done | bytes 3616 | tf_op jit(solution)/shard_map/ppermute | solution.py:376
  59.5 1.8 %collective-permute-done.12.seen = f32[1,1024]{1,0:T(1,128)S(1)} collective-permute-done((f32[1,1024]{1,0:T(1,128)S(1)}, f32[1,1024]{1,0:T(1,128)S(1)}, u32[]{:S(2)}, u32[]{:S(2)}) %collective-permute-start.12) | collective-permute-done | bytes 4128 | tf_op jit(solution)/shard_map/ppermute | solution.py:376
  61.3 4.9 %grads.1 = (f32[8,128]{1,0:T(8,128)S(1)}, f32[384,1024]{1,0:T(8,128)}, bf16[400,1024]{1,0:T(8,128)(2,1)}, bf16[16,400,128]{2,1,0:T(8,128)(2,1)}) custom-call(f32[1,1024]{1,0:T(1,128)S(1)} %pair.11.refs_0_, f32[1,896]{1,0:T(1,128)S(1)} %pair.15.refs_1_, f32[2,768]{1,0:T(2,128)S(1)} %get-tuple-element.28.refs_2_, f32[768,768]{1,0:T(8,128)S(1)} %get-tuple-element.29.refs_3_, ...), custom_call_target="tpu_custom_call" | custom-call | flops 2415919104 | bytes 11915776 | tf_op jit(solution)/shard_map/grads/pallas_call | solution.py:72
  66.3 3.9 %collective-permute-start.17 = (bf16[400,1024]{1,0:T(8,128)(2,1)}, bf16[400,1024]{1,0:T(8,128)(2,1)S(1)}, u32[]{:S(2)}, u32[]{:S(2)}) collective-permute-start(bf16[400,1024]{1,0:T(8,128)(2,1)} %get-tuple-element.36), channel_id=1, source_target_pairs={{0,8},{8,0},{1,9},{9,1},{2,10},{10,2},{3,11},{11,3},{4,12},{12,4},... | collective-permute-start | bytes 2457608 | tf_op jit(solution)/shard_map/ppermute | solution.py:411
  70.2 3.7 %all-to-all-start.1 = ((bf16[16,400,128]{2,1,0:T(8,128)(2,1)}), bf16[16,400,128]{2,1,0:T(8,128)(2,1)S(1)}, u32[]{:S(2)}, u32[]{:S(2)}) async-start(bf16[16,400,128]{2,1,0:T(8,128)(2,1)} %get-tuple-element.33), calls=%async_computation.1 | async-start | bytes 3276800 | tf_op jit(solution)/shard_map/all_to_all | solution.py:406
  73.9 1.4 %copy-done.3 = f32[384,1024]{1,0:T(8,128)S(1)} copy-done((f32[384,1024]{1,0:T(8,128)S(1)}, f32[384,1024]{1,0:T(8,128)}, u32[]{:S(2)}) %copy-start.3) | copy-done | bytes 1572888
  75.3 0.7 send.1
  76.0 0.8 collective-permute-start.18
  76.8 1.2 %collective-permute-start.19 = (bf16[784,128]{1,0:T(8,128)(2,1)S(1)}, bf16[784,128]{1,0:T(8,128)(2,1)S(1)}, u32[]{:S(2)}, u32[]{:S(2)}) collective-permute-start(bf16[784,128]{1,0:T(8,128)(2,1)S(1)} %get-tuple-element.40), channel_id=1, source_target_pairs={{0,32},{16,48},{32,64},{48,80},{64,96},{80,112},{96,0},{112,16},{1... | collective-permute-start | bytes 602120 | tf_op jit(solution)/shard_map/ppermute | solution.py:21
  78.0 1.9 %collective-permute-start.20 = (bf16[784,128]{1,0:T(8,128)(2,1)S(1)}, bf16[784,128]{1,0:T(8,128)(2,1)S(1)}, u32[]{:S(2)}, u32[]{:S(2)}) collective-permute-start(bf16[784,128]{1,0:T(8,128)(2,1)S(1)} %get-tuple-element.41), channel_id=1, source_target_pairs={{0,112},{16,0},{32,16},{48,32},{64,48},{80,64},{96,80},{112,96},{1... | collective-permute-start | bytes 602120 | tf_op jit(solution)/shard_map/ppermute | solution.py:21
  80.0 3.8 %collective-permute-done.18.refs_0_ = bf16[784,128]{1,0:T(8,128)(2,1)S(1)} collective-permute-done((bf16[784,128]{1,0:T(8,128)(2,1)S(1)}, bf16[784,128]{1,0:T(8,128)(2,1)S(1)}, u32[]{:S(2)}, u32[]{:S(2)}) %collective-permute-start.18) | collective-permute-done | bytes 200736 | tf_op jit(solution)/shard_map/ppermute | solution.py:21
  83.8 5.7 %collective-permute-done.19.refs_1_ = bf16[784,128]{1,0:T(8,128)(2,1)S(1)} collective-permute-done((bf16[784,128]{1,0:T(8,128)(2,1)S(1)}, bf16[784,128]{1,0:T(8,128)(2,1)S(1)}, u32[]{:S(2)}, u32[]{:S(2)}) %collective-permute-start.19) | collective-permute-done | bytes 200736 | tf_op jit(solution)/shard_map/ppermute | solution.py:21
  89.4 0.4 relay.1
  89.8 2.8 %collective-permute-start.21 = (bf16[400,128]{1,0:T(8,128)(2,1)S(1)}, bf16[400,128]{1,0:T(8,128)(2,1)S(1)}, u32[]{:S(2)}, u32[]{:S(2)}) collective-permute-start(bf16[400,128]{1,0:T(8,128)(2,1)S(1)} %get-tuple-element.44), channel_id=1, source_target_pairs={{0,64},{16,80},{32,96},{48,112},{64,0},{80,16},{96,32},{112,48},{1... | collective-permute-start | bytes 307208 | tf_op jit(solution)/shard_map/ppermute | solution.py:21
  92.7 7.7 %collective-permute-done.21.pay = bf16[400,128]{1,0:T(8,128)(2,1)S(1)} collective-permute-done((bf16[400,128]{1,0:T(8,128)(2,1)S(1)}, bf16[400,128]{1,0:T(8,128)(2,1)S(1)}, u32[]{:S(2)}, u32[]{:S(2)}) %collective-permute-start.21) | collective-permute-done | bytes 102432 | tf_op jit(solution)/shard_map/ppermute | solution.py:21
  100.4 0.8 text_sum.1
  101.2 1.7 %image_sum.1 = (f32[48,1024]{1,0:T(8,128)}, f32[1,1]{1,0:T(1,128)}) custom-call(bf16[16,400,128]{2,1,0:T(8,128)(2,1)S(1)} %all-to-all-done.1.got, f32[8,128]{1,0:T(8,128)S(1)} %get-tuple-element.34.terms, f32[1,128]{1,0:T(1,128)S(1)} %get-tuple-element.45.side), custom_call_target="tpu_custom_call" | custom-call | bytes 1839620 | tf_op jit(solution)/shard_map/image_sum/pallas_call | solution.py:72
  (24 shorter events, 0.2 us)
Async XLA Ops:
  0.6 17.0 %collective-permute-start = (bf16[48,1024]{1,0:T(8,128)(2,1)}, bf16[48,1024]{1,0:T(8,128)(2,1)S(1)}, u32[]{:S(2)}, u32[]{:S(2)}) collective-permute-start(bf16[48,1024]{1,0:T(8,128)(2,1)} %near.1), channel_id=1, source_target_pairs={{0,64},{16,80},{32,96},{48,112},{64,0},{80,16},{96,32},{112,48},{1... | collective-permute-start | bytes 294920 | tf_op jit(solution)/shard_map/ppermute | solution.py:21
  8.5 0.9 copy-start
  10.7 6.9 %copy-start.1 = (bf16[48,1024]{1,0:T(8,128)(2,1)S(1)}, bf16[48,1024]{1,0:T(8,128)(2,1)}, u32[]{:S(2)}) copy-start(bf16[48,1024]{1,0:T(8,128)(2,1)} %near.1) | copy-start | bytes 294916
  10.7 28.3 %all-to-all-start = ((bf16[16,48,1024]{2,1,0:T(8,128)(2,1)}), bf16[16,48,1024]{2,1,0:T(8,128)(2,1)S(1)}, u32[]{:S(2)}, u32[]{:S(2)}) async-start(bf16[16,48,1024]{2,1,0:T(8,128)(2,1)} %copies.1), calls=%async_computation | async-start | bytes 3145728 | tf_op jit(solution)/shard_map/all_to_all | solution.py:347
  17.6 17.8 %copy-start.2 = (s32[384]{0:T(512)S(1)}, s32[384]{0:T(512)}, u32[]{:S(2)}) copy-start(s32[384]{0:T(512)} %refs_9_.1) | copy-start | bytes 4612
  17.6 6.4 %collective-permute-start.3 = (bf16[96,1024]{1,0:T(8,128)(2,1)S(1)}, bf16[96,1024]{1,0:T(8,128)(2,1)S(1)}, u32[]{:S(2)}, u32[]{:S(2)}) collective-permute-start(bf16[96,1024]{1,0:T(8,128)(2,1)S(1)} %join.1.refs_0_), channel_id=1, source_target_pairs={{0,16},{16,32},{32,48},{48,64},{64,80},{80,96},{96,112},{112,0},{1... | collective-permute-start | bytes 589832 | tf_op jit(solution)/shard_map/ppermute | solution.py:21
  18.5 10.7 %collective-permute-start.2 = (bf16[96,1024]{1,0:T(8,128)(2,1)S(1)}, bf16[96,1024]{1,0:T(8,128)(2,1)S(1)}, u32[]{:S(2)}, u32[]{:S(2)}) collective-permute-start(bf16[96,1024]{1,0:T(8,128)(2,1)S(1)} %join.1.refs_0_), channel_id=1, source_target_pairs={{0,96},{16,112},{32,0},{48,16},{64,32},{80,48},{96,64},{112,80},{1... | collective-permute-start | bytes 589832 | tf_op jit(solution)/shard_map/ppermute | solution.py:21
  18.7 14.2 %collective-permute-start.1 = (bf16[96,1024]{1,0:T(8,128)(2,1)S(1)}, bf16[96,1024]{1,0:T(8,128)(2,1)S(1)}, u32[]{:S(2)}, u32[]{:S(2)}) collective-permute-start(bf16[96,1024]{1,0:T(8,128)(2,1)S(1)} %join.1.refs_0_), channel_id=1, source_target_pairs={{0,112},{16,0},{32,16},{48,32},{64,48},{80,64},{96,80},{112,96},{1... | collective-permute-start | bytes 589832 | tf_op jit(solution)/shard_map/ppermute | solution.py:21
  20.4 17.7 %collective-permute-start.4 = (bf16[96,1024]{1,0:T(8,128)(2,1)S(1)}, bf16[96,1024]{1,0:T(8,128)(2,1)S(1)}, u32[]{:S(2)}, u32[]{:S(2)}) collective-permute-start(bf16[96,1024]{1,0:T(8,128)(2,1)S(1)} %join.1.refs_0_), channel_id=1, source_target_pairs={{0,8},{8,0},{1,9},{9,1},{2,10},{10,2},{3,11},{11,3},{4,12},{12,4},... | collective-permute-start | bytes 589832 | tf_op jit(solution)/shard_map/ppermute | solution.py:355
  24.1 14.0 %collective-permute-start.7 = (bf16[96,1024]{1,0:T(8,128)(2,1)S(1)}, bf16[96,1024]{1,0:T(8,128)(2,1)S(1)}, u32[]{:S(2)}, u32[]{:S(2)}) collective-permute-start(bf16[96,1024]{1,0:T(8,128)(2,1)S(1)} %collective-permute-done.3.refs_3_), channel_id=1, source_target_pairs={{0,8},{8,0},{1,9},{9,1},{2,10},{10,2},{3,11},{11,3},{4,12},{12,4},... | collective-permute-start | bytes 589832 | tf_op jit(solution)/shard_map/ppermute | solution.py:355
  29.2 8.9 %collective-permute-start.6 = (bf16[96,1024]{1,0:T(8,128)(2,1)S(1)}, bf16[96,1024]{1,0:T(8,128)(2,1)S(1)}, u32[]{:S(2)}, u32[]{:S(2)}) collective-permute-start(bf16[96,1024]{1,0:T(8,128)(2,1)S(1)} %collective-permute-done.2.refs_2_), channel_id=1, source_target_pairs={{0,8},{8,0},{1,9},{9,1},{2,10},{10,2},{3,11},{11,3},{4,12},{12,4},... | collective-permute-start | bytes 589832 | tf_op jit(solution)/shard_map/ppermute | solution.py:355
  33.0 5.1 %collective-permute-start.5 = (bf16[96,1024]{1,0:T(8,128)(2,1)S(1)}, bf16[96,1024]{1,0:T(8,128)(2,1)S(1)}, u32[]{:S(2)}, u32[]{:S(2)}) collective-permute-start(bf16[96,1024]{1,0:T(8,128)(2,1)S(1)} %collective-permute-done.1.refs_1_), channel_id=1, source_target_pairs={{0,8},{8,0},{1,9},{9,1},{2,10},{10,2},{3,11},{11,3},{4,12},{12,4},... | collective-permute-start | bytes 589832 | tf_op jit(solution)/shard_map/ppermute | solution.py:355
  35.4 2.7 %collective-permute-start.8 = (s32[384]{0:T(512)S(1)}, s32[384]{0:T(512)S(1)}, u32[]{:S(2)}, u32[]{:S(2)}) collective-permute-start(s32[384]{0:T(512)S(1)} %copy-done.2), channel_id=1, source_target_pairs={{0,128},{128,0},{1,129},{129,1},{2,130},{130,2},{3,131},{131,3},{4... | collective-permute-start | bytes 4616 | tf_op jit(solution)/shard_map/ppermute | solution.py:338
  42.6 4.0 %collective-permute-start.9 = (f32[1,1024]{1,0:T(1,128)S(1)}, f32[1,1024]{1,0:T(1,128)S(1)}, u32[]{:S(2)}, u32[]{:S(2)}) collective-permute-start(f32[1,1024]{1,0:T(1,128)S(1)} %get-tuple-element.26.mine), channel_id=1, source_target_pairs={{0,8},{8,0},{1,9},{9,1},{2,10},{10,2},{3,11},{11,3},{4,12},{12,4},... | collective-permute-start | bytes 12296 | tf_op jit(solution)/shard_map/ppermute | solution.py:376
  45.0 2.6 %collective-permute-start.13 = (f32[1,896]{1,0:T(1,128)S(1)}, f32[1,896]{1,0:T(1,128)S(1)}, u32[]{:S(2)}, u32[]{:S(2)}) collective-permute-start(f32[1,896]{1,0:T(1,128)S(1)} %get-tuple-element.27.mine), channel_id=1, source_target_pairs={{0,128},{128,0},{1,129},{129,1},{2,130},{130,2},{3,131},{131,3},{4... | collective-permute-start | bytes 10760 | tf_op jit(solution)/shard_map/ppermute | solution.py:376
  46.6 4.8 %collective-permute-start.10 = (f32[1,1024]{1,0:T(1,128)S(1)}, f32[1,1024]{1,0:T(1,128)S(1)}, u32[]{:S(2)}, u32[]{:S(2)}) collective-permute-start(f32[1,1024]{1,0:T(1,128)S(1)} %pair.8.mine), channel_id=1, source_target_pairs={{0,16},{16,0},{32,48},{48,32},{64,80},{80,64},{96,112},{112,96},{1... | collective-permute-start | bytes 12296 | tf_op jit(solution)/shard_map/ppermute | solution.py:376
  47.6 5.1 %collective-permute-start.14 = (f32[1,896]{1,0:T(1,128)S(1)}, f32[1,896]{1,0:T(1,128)S(1)}, u32[]{:S(2)}, u32[]{:S(2)}) collective-permute-start(f32[1,896]{1,0:T(1,128)S(1)} %pair.12.mine), channel_id=1, source_target_pairs={{0,1},{1,0},{2,3},{3,2},{4,5},{5,4},{6,7},{7,6},{8,9},{9,8},{10,11... | collective-permute-start | bytes 10760 | tf_op jit(solution)/shard_map/ppermute | solution.py:376
  51.4 3.4 %collective-permute-start.11 = (f32[1,1024]{1,0:T(1,128)S(1)}, f32[1,1024]{1,0:T(1,128)S(1)}, u32[]{:S(2)}, u32[]{:S(2)}) collective-permute-start(f32[1,1024]{1,0:T(1,128)S(1)} %pair.9.mine), channel_id=1, source_target_pairs={{0,32},{16,48},{32,0},{48,16},{64,96},{80,112},{96,64},{112,80},{1... | collective-permute-start | bytes 12296 | tf_op jit(solution)/shard_map/ppermute | solution.py:376
  52.7 2.7 %collective-permute-start.15 = (f32[1,896]{1,0:T(1,128)S(1)}, f32[1,896]{1,0:T(1,128)S(1)}, u32[]{:S(2)}, u32[]{:S(2)}) collective-permute-start(f32[1,896]{1,0:T(1,128)S(1)} %pair.13.mine), channel_id=1, source_target_pairs={{0,2},{2,0},{4,6},{6,4},{1,3},{3,1},{5,7},{7,5},{8,10},{10,8},{12,... | collective-permute-start | bytes 10760 | tf_op jit(solution)/shard_map/ppermute | solution.py:376
  54.9 6.5 %collective-permute-start.12 = (f32[1,1024]{1,0:T(1,128)S(1)}, f32[1,1024]{1,0:T(1,128)S(1)}, u32[]{:S(2)}, u32[]{:S(2)}) collective-permute-start(f32[1,1024]{1,0:T(1,128)S(1)} %pair.10.mine), channel_id=1, source_target_pairs={{0,64},{16,80},{32,96},{48,112},{64,0},{80,16},{96,32},{112,48},{1... | collective-permute-start | bytes 12296 | tf_op jit(solution)/shard_map/ppermute | solution.py:376
  55.4 4.0 %collective-permute-start.16 = (f32[1,896]{1,0:T(1,128)S(1)}, f32[1,896]{1,0:T(1,128)S(1)}, u32[]{:S(2)}, u32[]{:S(2)}) collective-permute-start(f32[1,896]{1,0:T(1,128)S(1)} %pair.14.mine), channel_id=1, source_target_pairs={{0,4},{2,6},{4,0},{6,2},{1,5},{3,7},{5,1},{7,3},{8,12},{10,14},{12... | collective-permute-start | bytes 10760 | tf_op jit(solution)/shard_map/ppermute | solution.py:376
  66.3 7.6 %collective-permute-start.17 = (bf16[400,1024]{1,0:T(8,128)(2,1)}, bf16[400,1024]{1,0:T(8,128)(2,1)S(1)}, u32[]{:S(2)}, u32[]{:S(2)}) collective-permute-start(bf16[400,1024]{1,0:T(8,128)(2,1)} %get-tuple-element.36), channel_id=1, source_target_pairs={{0,8},{8,0},{1,9},{9,1},{2,10},{10,2},{3,11},{11,3},{4,12},{12,4},... | collective-permute-start | bytes 2457608 | tf_op jit(solution)/shard_map/ppermute | solution.py:411
  70.2 31.0 %all-to-all-start.1 = ((bf16[16,400,128]{2,1,0:T(8,128)(2,1)}), bf16[16,400,128]{2,1,0:T(8,128)(2,1)S(1)}, u32[]{:S(2)}, u32[]{:S(2)}) async-start(bf16[16,400,128]{2,1,0:T(8,128)(2,1)} %get-tuple-element.33), calls=%async_computation.1 | async-start | bytes 3276800 | tf_op jit(solution)/shard_map/all_to_all | solution.py:406
  73.9 1.4 %copy-start.3 = (f32[384,1024]{1,0:T(8,128)S(1)}, f32[384,1024]{1,0:T(8,128)}, u32[]{:S(2)}) copy-start(f32[384,1024]{1,0:T(8,128)} %get-tuple-element.35.own) | copy-start | bytes 4718596
  76.0 7.7 %collective-permute-start.18 = (bf16[784,128]{1,0:T(8,128)(2,1)S(1)}, bf16[784,128]{1,0:T(8,128)(2,1)S(1)}, u32[]{:S(2)}, u32[]{:S(2)}) collective-permute-start(bf16[784,128]{1,0:T(8,128)(2,1)S(1)} %get-tuple-element.39), channel_id=1, source_target_pairs={{0,16},{16,32},{32,48},{48,64},{64,80},{80,96},{96,112},{112,0},{1... | collective-permute-start | bytes 602120 | tf_op jit(solution)/shard_map/ppermute | solution.py:21
  76.8 12.6 %collective-permute-start.19 = (bf16[784,128]{1,0:T(8,128)(2,1)S(1)}, bf16[784,128]{1,0:T(8,128)(2,1)S(1)}, u32[]{:S(2)}, u32[]{:S(2)}) collective-permute-start(bf16[784,128]{1,0:T(8,128)(2,1)S(1)} %get-tuple-element.40), channel_id=1, source_target_pairs={{0,32},{16,48},{32,64},{48,80},{64,96},{80,112},{96,0},{112,16},{1... | collective-permute-start | bytes 602120 | tf_op jit(solution)/shard_map/ppermute | solution.py:21
  78.0 11.4 %collective-permute-start.20 = (bf16[784,128]{1,0:T(8,128)(2,1)S(1)}, bf16[784,128]{1,0:T(8,128)(2,1)S(1)}, u32[]{:S(2)}, u32[]{:S(2)}) collective-permute-start(bf16[784,128]{1,0:T(8,128)(2,1)S(1)} %get-tuple-element.41), channel_id=1, source_target_pairs={{0,112},{16,0},{32,16},{48,32},{64,48},{80,64},{96,80},{112,96},{1... | collective-permute-start | bytes 602120 | tf_op jit(solution)/shard_map/ppermute | solution.py:21
  89.8 10.5 %collective-permute-start.21 = (bf16[400,128]{1,0:T(8,128)(2,1)S(1)}, bf16[400,128]{1,0:T(8,128)(2,1)S(1)}, u32[]{:S(2)}, u32[]{:S(2)}) collective-permute-start(bf16[400,128]{1,0:T(8,128)(2,1)S(1)} %get-tuple-element.44), channel_id=1, source_target_pairs={{0,64},{16,80},{32,96},{48,112},{64,0},{80,16},{96,32},{112,48},{1... | collective-permute-start | bytes 307208 | tf_op jit(solution)/shard_map/ppermute | solution.py:21

commit v11 on v8

--- a/solution.py
+++ b/solution.py
@@ -91,22 +91,27 @@
         copy.wait()
 
 
-def join_body(near, far, mine, seen, out, pair):
+def join_body(near, far, out):
+    rows = near.shape[0]
+    out[:rows, :] = near[...]
+    out[rows:, :] = far[...]
+
+
+def pair_row(mine, seen):
     first = lax.axis_index("xl") == 0
     left = mine[...].astype(F32)[None, :]
     right = seen[...].astype(F32)[None, :]
-    pair[...] = jnp.concatenate(
+    return jnp.concatenate(
         [jnp.where(first, left, right), jnp.where(first, right, left)], axis=1
     )
-    rows = near.shape[0]
-    out[:rows, :] = near[...]
-    out[rows:, :] = far[...]
 
 
 def score_body(steps, inv_root, *refs):
     n_z = 2 * len(steps)
     pieces, refs = refs[:n_z], refs[n_z:]
-    image, pair, scores, text, row_sent, col_sent = refs
+    image, pair_mine, pair_seen, pair_out, scores, text, row_sent, col_sent = refs
+    pair = pair_row(pair_mine, pair_seen)
+    pair_out[...] = pair
     rows = pieces[0].shape[0] // 2
     size = image.shape[0]
     ids = labels(n_z, rows)
@@ -118,7 +123,7 @@
             piece = pieces[h * n_z // 2 + i]
             high = jnp.maximum(high, jnp.abs(piece[...].astype(F32)))
             for k in range(2):
-                start = (h * n_z + lax.rem(z + q + (k + 2) * n_z // 2, n_z)) * rows
+                start = (h * n_z + lax.rem(z + q + k + n_z, n_z)) * rows
                 text[pl.ds(pl.multiple_of(start, 16), rows), :] = piece[
                     k * rows : (k + 1) * rows, :
                 ]
@@ -255,7 +260,7 @@
     for i, q in enumerate(steps):
         blocks = []
         for k in range(2):
-            start = lax.rem(z + q + (k + 2) * n_z // 2, n_z) * rows
+            start = lax.rem(z + q + k + n_z, n_z) * rows
             at = pl.ds(pl.multiple_of(start, 16), rows)
             blocks.append(own[at, :] + decode(seen[at, :]))
         if i == 0:
@@ -325,35 +330,32 @@
     copies = pl.pallas_call(
         copies_body,
         out_shape=shape((n_plane, rows, width), BF16),
-        in_specs=[pl.BlockSpec(memory_space=pl.ANY)],
+        in_specs=[pl.BlockSpec(memory_space=pltpu.VMEM)],
         out_specs=pl.BlockSpec(memory_space=pl.ANY),
         scratch_shapes=[pltpu.SemaphoreType.DMA((n_plane,))],
         name="copies",
     )(image_embed)
     image = lax.all_to_all(copies, PLANE, 0, 0).reshape(size, width)
 
-    steps = [q if q <= n_z // 4 else q - n_z // 2 for q in range(n_z // 2)]
-    far = turn(text_embed, "z", n_z // 2)
-    joined, pair = call(
-        join_body,
-        (shape((2 * rows, width), BF16), shape((1, size), F32)),
-        (text_embed, far, pair_index, pair_seen),
-        "join",
-        10**11,
+    steps = [0, n_z // 2] + [q for k in range(2, n_z // 2, 2) for q in (k, -k)]
+    far = turn(text_embed, "z", -1)
+    (joined,) = call(
+        join_body, (shape((2 * rows, width), BF16),), (text_embed, far), "join", 10**11
     )
     pieces = [joined] + [turn(joined, "z", -q) for q in steps[1:]]
     pieces = pieces + [lax.ppermute(piece, "c", SWAP) for piece in pieces]
 
     flops = 2 * size * size * width
-    scores, text, row_part, col_part = call(
+    pair, scores, text, row_part, col_part = call(
         functools.partial(score_body, steps, inv_root),
         (
+            shape((1, size), F32),
             shape((size, size), F32),
             shape((size, width), BF16),
             shape((1, size + LANES), F32),
             shape((1, size + 2 * LANES), F32),
         ),
-        (*pieces, image, pair),
+        (*pieces, image, pair_index, pair_seen),
         "scores",
         flops,
         2 * size * size,
@@ -416,7 +418,7 @@
     grad_text, side = call(
         text_sum_body,
         (shape((rows, width), F32), shape((1, LANES), F32)),
-        (near, total, terms, turn(far, "z", n_z // 2)),
+        (near, total, terms, turn(far, "z", 1)),
         "text_sum",
         size=1,
     )

time: 154 us -> 111 us (0.72); the launches traced: 151 us -> 110 us
  Pallas kernels: 60.7 us -> 13.8 us
  starting transfers between devices: 53.8 us -> 64.8 us
  waiting for transfers between devices: 34.2 us -> 29.5 us
    pallas_call x1, Pallas kernels: 48.9 us -> 2.21 us  [shards(): pl.pallas_call(copies_body, out_shape=shape((n_plane, rows, width), BF16)...]
    ppermute x8, starting transfers between devices: 12 us -> 16 us  [exchange(): seen = lax.ppermute(part, axis, [(i, i ^ step) for i in range(count)])]
    ppermute x8, starting transfers between devices: 17.4 us -> 21.1 us  [turn(): lax.ppermute(x, axis, [(i, (i + step) % count) for i in range(count)])]
    ppermute x8, waiting for transfers between devices: 6.57 us -> 3.05 us  [exchange(): seen = lax.ppermute(part, axis, [(i, i ^ step) for i in range(count)])]
    all_to_all x1, waiting for transfers between devices: 1.9 us -> 0.01 us  [shards(): image = lax.all_to_all(copies, PLANE, 0, 0).reshape(size, width)]
    all_to_all x1, starting transfers between devices: 3.71 us -> 5.5 us  [shards(): image_got = lax.all_to_all(image_sent, PLANE, 0, 0)]
  transfers between devices with their start and end apart: 25 -> 25, of which waited for: 13 -> 12; matrix products, arithmetic and copies ran while one was open for 0% -> 0% of each run, Pallas kernels for 34% -> 5%
where the time goes in v11:
time: 111 us; the launch traced here: 110 us
  starting transfers between devices  64.8 us (58%)
  waiting for transfers between devices  29.5 us (27%)
  Pallas kernels  13.8 us (12%)
  local copies, waits for them, and re-layouts  1.28 us (1%)
    ppermute x8, waiting for transfers between devices, turn(): lax.ppermute(x, axis, [(i, (i + step) % count) for i in range(count)])  23 us
    ppermute x8, starting transfers between devices, turn(): lax.ppermute(x, axis, [(i, (i + step) % count) for i in range(count)])  21.1 us
    ppermute x8, starting transfers between devices, exchange(): seen = lax.ppermute(part, axis, [(i, i ^ step) for i in range(count)])  16 us
    pallas_call x16, Pallas kernels, call(): pl.pallas_call(body, out_shape=outs, in_specs=[pl.BlockSpec(memory_space=...  11.6 us
    ppermute x4, starting transfers between devices, shards(): pieces = pieces + [lax.ppermute(piece, 'c', SWAP) for piece in pieces]  10.1 us
    all_to_all x1, starting transfers between devices, shards(): image = lax.all_to_all(copies, PLANE, 0, 0).reshape(size, width)  6.9 us
    all_to_all x1, starting transfers between devices, shards(): image_got = lax.all_to_all(image_sent, PLANE, 0, 0)  5.5 us
    ppermute x1, starting transfers between devices, shards(): terms_seen = lax.ppermute(terms, 'c', SWAP)  3.31 us
  transfers between devices with their start and end apart: 25, of which 12 were waited for; matrix products, arithmetic and copies ran while one was open for 0% of the time, Pallas kernels for 5%

profile of v11, /device:TPU:1, one launch (start us, length us, event | category | flops | bytes accessed | tf_op | source)
XLA Modules:
  0.0 110.3 jit_solution(17763314704982614614)
XLA Ops:
  0.6 6.5 %collective-permute-start = (bf16[48,1024]{1,0:T(8,128)(2,1)}, bf16[48,1024]{1,0:T(8,128)(2,1)S(1)}, u32[]{:S(2)}, u32[]{:S(2)}) collective-permute-start(bf16[48,1024]{1,0:T(8,128)(2,1)} %near.1), channel_id=1, source_target_pairs={{0,112},{16,0},{32,16},{48,32},{64,48},{80,64},{96,80},{112,96},{1... | collective-permute-start | bytes 294920 | tf_op jit(solution)/shard_map/ppermute | solution.py:21
  7.1 2.2 %copies.1 = bf16[16,48,1024]{2,1,0:T(8,128)(2,1)} custom-call(bf16[48,1024]{1,0:T(8,128)(2,1)} %source.1), custom_call_target="tpu_custom_call" | custom-call | tf_op jit(solution)/shard_map/copies/pallas_call | solution.py:330
  9.3 0.0 copy-start
  9.3 6.9 %all-to-all-start = ((bf16[16,48,1024]{2,1,0:T(8,128)(2,1)}), bf16[16,48,1024]{2,1,0:T(8,128)(2,1)S(1)}, u32[]{:S(2)}, u32[]{:S(2)}) async-start(bf16[16,48,1024]{2,1,0:T(8,128)(2,1)} %copies.1), calls=%async_computation | async-start | bytes 3145728 | tf_op jit(solution)/shard_map/all_to_all | solution.py:338
  16.2 0.0 copy-start.1
  16.3 0.1 collective-permute-start.3
  16.4 3.6 %collective-permute-start.2 = (bf16[96,1024]{1,0:T(8,128)(2,1)S(1)}, bf16[96,1024]{1,0:T(8,128)(2,1)S(1)}, u32[]{:S(2)}, u32[]{:S(2)}) collective-permute-start(bf16[96,1024]{1,0:T(8,128)(2,1)S(1)} %join.1.refs_0_), channel_id=1, source_target_pairs={{0,96},{16,112},{32,0},{48,16},{64,32},{80,48},{96,64},{112,80},{1... | collective-permute-start | bytes 589832 | tf_op jit(solution)/shard_map/ppermute | solution.py:21
  20.0 1.4 %collective-permute-start.1 = (bf16[96,1024]{1,0:T(8,128)(2,1)S(1)}, bf16[96,1024]{1,0:T(8,128)(2,1)S(1)}, u32[]{:S(2)}, u32[]{:S(2)}) collective-permute-start(bf16[96,1024]{1,0:T(8,128)(2,1)S(1)} %join.1.refs_0_), channel_id=1, source_target_pairs={{0,64},{16,80},{32,96},{48,112},{64,0},{80,16},{96,32},{112,48},{1... | collective-permute-start | bytes 589832 | tf_op jit(solution)/shard_map/ppermute | solution.py:21
  21.3 1.9 %collective-permute-start.4 = (bf16[96,1024]{1,0:T(8,128)(2,1)S(1)}, bf16[96,1024]{1,0:T(8,128)(2,1)S(1)}, u32[]{:S(2)}, u32[]{:S(2)}) collective-permute-start(bf16[96,1024]{1,0:T(8,128)(2,1)S(1)} %join.1.refs_0_), channel_id=1, source_target_pairs={{0,8},{8,0},{1,9},{9,1},{2,10},{10,2},{3,11},{11,3},{4,12},{12,4},... | collective-permute-start | bytes 589832 | tf_op jit(solution)/shard_map/ppermute | solution.py:346
  23.2 3.1 %collective-permute-done.3.refs_3_ = bf16[96,1024]{1,0:T(8,128)(2,1)S(1)} collective-permute-done((bf16[96,1024]{1,0:T(8,128)(2,1)S(1)}, bf16[96,1024]{1,0:T(8,128)(2,1)S(1)}, u32[]{:S(2)}, u32[]{:S(2)}) %collective-permute-start.3) | collective-permute-done | bytes 196640 | tf_op jit(solution)/shard_map/ppermute | solution.py:21
  26.3 5.5 %collective-permute-start.7 = (bf16[96,1024]{1,0:T(8,128)(2,1)S(1)}, bf16[96,1024]{1,0:T(8,128)(2,1)S(1)}, u32[]{:S(2)}, u32[]{:S(2)}) collective-permute-start(bf16[96,1024]{1,0:T(8,128)(2,1)S(1)} %collective-permute-done.3.refs_3_), channel_id=1, source_target_pairs={{0,8},{8,0},{1,9},{9,1},{2,10},{10,2},{3,11},{11,3},{4,12},{12,4},... | collective-permute-start | bytes 589832 | tf_op jit(solution)/shard_map/ppermute | solution.py:346
  31.8 1.8 %collective-permute-done.2.refs_2_ = bf16[96,1024]{1,0:T(8,128)(2,1)S(1)} collective-permute-done((bf16[96,1024]{1,0:T(8,128)(2,1)S(1)}, bf16[96,1024]{1,0:T(8,128)(2,1)S(1)}, u32[]{:S(2)}, u32[]{:S(2)}) %collective-permute-start.2) | collective-permute-done | bytes 196640 | tf_op jit(solution)/shard_map/ppermute | solution.py:21
  33.6 2.7 %collective-permute-start.6 = (bf16[96,1024]{1,0:T(8,128)(2,1)S(1)}, bf16[96,1024]{1,0:T(8,128)(2,1)S(1)}, u32[]{:S(2)}, u32[]{:S(2)}) collective-permute-start(bf16[96,1024]{1,0:T(8,128)(2,1)S(1)} %collective-permute-done.2.refs_2_), channel_id=1, source_target_pairs={{0,8},{8,0},{1,9},{9,1},{2,10},{10,2},{3,11},{11,3},{4,12},{12,4},... | collective-permute-start | bytes 589832 | tf_op jit(solution)/shard_map/ppermute | solution.py:346
  36.3 0.0 collective-permute-start.5
  36.3 1.5 %collective-permute-start.8 = (s32[384]{0:T(512)S(1)}, s32[384]{0:T(512)S(1)}, u32[]{:S(2)}, u32[]{:S(2)}) collective-permute-start(s32[384]{0:T(512)S(1)} %copy-done.1), channel_id=1, source_target_pairs={{0,128},{128,0},{1,129},{129,1},{2,130},{130,2},{3,131},{131,3},{4... | collective-permute-start | bytes 4616 | tf_op jit(solution)/shard_map/ppermute | solution.py:329
  37.8 1.4 %collective-permute-done.8.refs_10_ = s32[384]{0:T(512)S(1)} collective-permute-done((s32[384]{0:T(512)S(1)}, s32[384]{0:T(512)S(1)}, u32[]{:S(2)}, u32[]{:S(2)}) %collective-permute-start.8) | collective-permute-done | bytes 1568 | tf_op jit(solution)/shard_map/ppermute | solution.py:329
  39.2 3.0 %scores.1 = (f32[1,768]{1,0:T(1,128)S(1)}, f32[768,768]{1,0:T(8,128)S(1)}, bf16[768,1024]{1,0:T(8,128)(2,1)S(1)}, f32[1,896]{1,0:T(1,128)S(1)}, f32[1,1024]{1,0:T(1,128)S(1)}) custom-call(bf16[96,1024]{1,0:T(8,128)(2,1)S(1)} %join.1.refs_0_, bf16[96,1024]{1,0:T(8,128)(2,1)S(1)} %collective-permute-done.1.refs_1_, ...), custom_call_target="tpu_custom_call" | custom-call | flops 1207959552 | bytes 7091712 | tf_op jit(solution)/shard_map/scores/pallas_call | solution.py:72
  42.2 1.4 %collective-permute-start.9 = (f32[1,1024]{1,0:T(1,128)S(1)}, f32[1,1024]{1,0:T(1,128)S(1)}, u32[]{:S(2)}, u32[]{:S(2)}) collective-permute-start(f32[1,1024]{1,0:T(1,128)S(1)} %get-tuple-element.25.mine), channel_id=1, source_target_pairs={{0,8},{8,0},{1,9},{9,1},{2,10},{10,2},{3,11},{11,3},{4,12},{12,4},... | collective-permute-start | bytes 12296 | tf_op jit(solution)/shard_map/ppermute | solution.py:365
  43.6 1.4 %collective-permute-start.13 = (f32[1,896]{1,0:T(1,128)S(1)}, f32[1,896]{1,0:T(1,128)S(1)}, u32[]{:S(2)}, u32[]{:S(2)}) collective-permute-start(f32[1,896]{1,0:T(1,128)S(1)} %get-tuple-element.26.mine), channel_id=1, source_target_pairs={{0,128},{128,0},{1,129},{129,1},{2,130},{130,2},{3,131},{131,3},{4... | collective-permute-start | bytes 10760 | tf_op jit(solution)/shard_map/ppermute | solution.py:365
  45.0 4.0 %collective-permute-start.10 = (f32[1,1024]{1,0:T(1,128)S(1)}, f32[1,1024]{1,0:T(1,128)S(1)}, u32[]{:S(2)}, u32[]{:S(2)}) collective-permute-start(f32[1,1024]{1,0:T(1,128)S(1)} %pair.8.mine), channel_id=1, source_target_pairs={{0,16},{16,0},{32,48},{48,32},{64,80},{80,64},{96,112},{112,96},{1... | collective-permute-start | bytes 12296 | tf_op jit(solution)/shard_map/ppermute | solution.py:365
  49.0 2.5 %collective-permute-start.14 = (f32[1,896]{1,0:T(1,128)S(1)}, f32[1,896]{1,0:T(1,128)S(1)}, u32[]{:S(2)}, u32[]{:S(2)}) collective-permute-start(f32[1,896]{1,0:T(1,128)S(1)} %pair.12.mine), channel_id=1, source_target_pairs={{0,1},{1,0},{2,3},{3,2},{4,5},{5,4},{6,7},{7,6},{8,9},{9,8},{10,11... | collective-permute-start | bytes 10760 | tf_op jit(solution)/shard_map/ppermute | solution.py:365
  51.5 0.8 collective-permute-start.11
  52.3 0.8 collective-permute-done.14.seen
  53.1 1.5 %collective-permute-start.15 = (f32[1,896]{1,0:T(1,128)S(1)}, f32[1,896]{1,0:T(1,128)S(1)}, u32[]{:S(2)}, u32[]{:S(2)}) collective-permute-start(f32[1,896]{1,0:T(1,128)S(1)} %pair.13.mine), channel_id=1, source_target_pairs={{0,2},{2,0},{4,6},{6,4},{1,3},{3,1},{5,7},{7,5},{8,10},{10,8},{12,... | collective-permute-start | bytes 10760 | tf_op jit(solution)/shard_map/ppermute | solution.py:365
  54.5 0.4 collective-permute-done.11.seen
  55.0 2.1 %collective-permute-start.12 = (f32[1,1024]{1,0:T(1,128)S(1)}, f32[1,1024]{1,0:T(1,128)S(1)}, u32[]{:S(2)}, u32[]{:S(2)}) collective-permute-start(f32[1,1024]{1,0:T(1,128)S(1)} %pair.10.mine), channel_id=1, source_target_pairs={{0,64},{16,80},{32,96},{48,112},{64,0},{80,16},{96,32},{112,48},{1... | collective-permute-start | bytes 12296 | tf_op jit(solution)/shard_map/ppermute | solution.py:365
  57.0 2.5 %collective-permute-start.16 = (f32[1,896]{1,0:T(1,128)S(1)}, f32[1,896]{1,0:T(1,128)S(1)}, u32[]{:S(2)}, u32[]{:S(2)}) collective-permute-start(f32[1,896]{1,0:T(1,128)S(1)} %pair.14.mine), channel_id=1, source_target_pairs={{0,4},{2,6},{4,0},{6,2},{1,5},{3,7},{5,1},{7,3},{8,12},{10,14},{12... | collective-permute-start | bytes 10760 | tf_op jit(solution)/shard_map/ppermute | solution.py:365
  59.5 1.6 %collective-permute-done.16.seen = f32[1,896]{1,0:T(1,128)S(1)} collective-permute-done((f32[1,896]{1,0:T(1,128)S(1)}, f32[1,896]{1,0:T(1,128)S(1)}, u32[]{:S(2)}, u32[]{:S(2)}) %collective-permute-start.16) | collective-permute-done | bytes 3616 | tf_op jit(solution)/shard_map/ppermute | solution.py:365
  61.1 0.3 collective-permute-done.12.seen
  61.4 3.4 %image_grad.1 = (bf16[768,768]{1,0:T(8,128)(2,1)}, bf16[16,400,128]{2,1,0:T(8,128)(2,1)}, f32[8,128]{1,0:T(8,128)S(1)}) custom-call(f32[1,1024]{1,0:T(1,128)S(1)} %pair.11.cols, f32[1,896]{1,0:T(1,128)S(1)} %pair.15.rows_lse, f32[768,768]{1,0:T(8,128)S(1)} %get-tuple-element.27.scores, bf16[768,1024]{1,0:T(8,128)(2,1)S(1)} %get-tuple-element.28.text, ...), custom_call_target="tpu_custom_call" | custom-call | flops 1207959552 | bytes 6765056 | tf_op jit(solution)/shard_map/image_grad/pallas_call | solution.py:72
  64.8 3.3 %collective-permute-start.17 = (f32[8,128]{1,0:T(8,128)S(1)}, f32[8,128]{1,0:T(8,128)S(1)}, u32[]{:S(2)}, u32[]{:S(2)}) collective-permute-start(f32[8,128]{1,0:T(8,128)S(1)} %get-tuple-element.31.terms), channel_id=1, source_target_pairs={{0,8},{8,0},{1,9},{9,1},{2,10},{10,2},{3,11},{11,3},{4,12},{12,4},... | collective-permute-start | bytes 12296 | tf_op jit(solution)/shard_map/ppermute | solution.py:393
  68.1 5.5 %all-to-all-start.1 = ((bf16[16,400,128]{2,1,0:T(8,128)(2,1)}), bf16[16,400,128]{2,1,0:T(8,128)(2,1)S(1)}, u32[]{:S(2)}, u32[]{:S(2)}) async-start(bf16[16,400,128]{2,1,0:T(8,128)(2,1)} %get-tuple-element.30), calls=%async_computation.1 | async-start | bytes 3276800 | tf_op jit(solution)/shard_map/all_to_all | solution.py:392
  73.7 1.3 %copy-done.2 = bf16[768,768]{1,0:T(8,128)(2,1)S(1)} copy-done((bf16[768,768]{1,0:T(8,128)(2,1)S(1)}, bf16[768,768]{1,0:T(8,128)(2,1)}, u32[]{:S(2)}) %copy-start.2) | copy-done | bytes 1179672
  74.9 1.6 %text_grad.1 = (f32[384,1024]{1,0:T(8,128)S(1)}, bf16[384,1024]{1,0:T(8,128)(2,1)S(1)}) custom-call(bf16[768,768]{1,0:T(8,128)(2,1)S(1)} %copy-done.2, bf16[768,1024]{1,0:T(8,128)(2,1)S(1)} %bitcast.3, f32[8,128]{1,0:T(8,128)S(1)} %collective-permute-done.17.terms_seen), custom_call_target="tpu_custom_call" | custom-call | flops 99999997952 | bytes 1 | tf_op jit(solution)/shard_map/text_grad/pallas_call | solution.py:72
  76.5 0.4 collective-permute-start.18
  76.9 2.0 %collective-permute-done.18.seen = bf16[384,1024]{1,0:T(8,128)(2,1)S(1)} collective-permute-done((bf16[384,1024]{1,0:T(8,128)(2,1)S(1)}, bf16[384,1024]{1,0:T(8,128)(2,1)S(1)}, u32[]{:S(2)}, u32[]{:S(2)}) %collective-permute-start.18) | collective-permute-done | bytes 786464 | tf_op jit(solution)/shard_map/ppermute | solution.py:406
  78.9 0.7 send.1
  79.6 3.4 %collective-permute-start.19 = (bf16[784,128]{1,0:T(8,128)(2,1)S(1)}, bf16[784,128]{1,0:T(8,128)(2,1)S(1)}, u32[]{:S(2)}, u32[]{:S(2)}) collective-permute-start(bf16[784,128]{1,0:T(8,128)(2,1)S(1)} %get-tuple-element.37), channel_id=1, source_target_pairs={{0,64},{16,80},{32,96},{48,112},{64,0},{80,16},{96,32},{112,48},{1... | collective-permute-start | bytes 602120 | tf_op jit(solution)/shard_map/ppermute | solution.py:21
  83.0 1.3 %collective-permute-start.20 = (bf16[784,128]{1,0:T(8,128)(2,1)S(1)}, bf16[784,128]{1,0:T(8,128)(2,1)S(1)}, u32[]{:S(2)}, u32[]{:S(2)}) collective-permute-start(bf16[784,128]{1,0:T(8,128)(2,1)S(1)} %get-tuple-element.38), channel_id=1, source_target_pairs={{0,32},{16,48},{32,64},{48,80},{64,96},{80,112},{96,0},{112,16},{1... | collective-permute-start | bytes 602120 | tf_op jit(solution)/shard_map/ppermute | solution.py:21
  84.3 2.3 %collective-permute-start.21 = (bf16[784,128]{1,0:T(8,128)(2,1)S(1)}, bf16[784,128]{1,0:T(8,128)(2,1)S(1)}, u32[]{:S(2)}, u32[]{:S(2)}) collective-permute-start(bf16[784,128]{1,0:T(8,128)(2,1)S(1)} %get-tuple-element.39), channel_id=1, source_target_pairs={{0,96},{16,112},{32,0},{48,16},{64,32},{80,48},{96,64},{112,80},{1... | collective-permute-start | bytes 602120 | tf_op jit(solution)/shard_map/ppermute | solution.py:21
  86.6 4.3 %collective-permute-done.19.refs_0_ = bf16[784,128]{1,0:T(8,128)(2,1)S(1)} collective-permute-done((bf16[784,128]{1,0:T(8,128)(2,1)S(1)}, bf16[784,128]{1,0:T(8,128)(2,1)S(1)}, u32[]{:S(2)}, u32[]{:S(2)}) %collective-permute-start.19) | collective-permute-done | bytes 200736 | tf_op jit(solution)/shard_map/ppermute | solution.py:21
  90.9 8.4 %collective-permute-done.20.refs_1_ = bf16[784,128]{1,0:T(8,128)(2,1)S(1)} collective-permute-done((bf16[784,128]{1,0:T(8,128)(2,1)S(1)}, bf16[784,128]{1,0:T(8,128)(2,1)S(1)}, u32[]{:S(2)}, u32[]{:S(2)}) %collective-permute-start.20) | collective-permute-done | bytes 200736 | tf_op jit(solution)/shard_map/ppermute | solution.py:21
  99.3 2.8 %collective-permute-done.21.refs_2_ = bf16[784,128]{1,0:T(8,128)(2,1)S(1)} collective-permute-done((bf16[784,128]{1,0:T(8,128)(2,1)S(1)}, bf16[784,128]{1,0:T(8,128)(2,1)S(1)}, u32[]{:S(2)}, u32[]{:S(2)}) %collective-permute-start.21) | collective-permute-done | bytes 200736 | tf_op jit(solution)/shard_map/ppermute | solution.py:21
  102.1 0.4 relay.1
  102.5 2.7 %collective-permute-start.22 = (bf16[400,128]{1,0:T(8,128)(2,1)S(1)}, bf16[400,128]{1,0:T(8,128)(2,1)S(1)}, u32[]{:S(2)}, u32[]{:S(2)}) collective-permute-start(bf16[400,128]{1,0:T(8,128)(2,1)S(1)} %get-tuple-element.42), channel_id=1, source_target_pairs={{0,16},{16,32},{32,48},{48,64},{64,80},{80,96},{96,112},{112,0},{1... | collective-permute-start | bytes 307208 | tf_op jit(solution)/shard_map/ppermute | solution.py:21
  105.1 2.6 %collective-permute-done.22.pay = bf16[400,128]{1,0:T(8,128)(2,1)S(1)} collective-permute-done((bf16[400,128]{1,0:T(8,128)(2,1)S(1)}, bf16[400,128]{1,0:T(8,128)(2,1)S(1)}, u32[]{:S(2)}, u32[]{:S(2)}) %collective-permute-start.22) | collective-permute-done | bytes 102432 | tf_op jit(solution)/shard_map/ppermute | solution.py:21
  107.7 0.8 text_sum.1
  108.5 1.7 %image_sum.1 = (f32[48,1024]{1,0:T(8,128)}, f32[1,1]{1,0:T(1,128)}) custom-call(bf16[16,400,128]{2,1,0:T(8,128)(2,1)S(1)} %all-to-all-done.1.got, f32[8,128]{1,0:T(8,128)S(1)} %get-tuple-element.31.terms, f32[1,128]{1,0:T(1,128)S(1)} %get-tuple-element.43.side), custom_call_target="tpu_custom_call" | custom-call | bytes 1839620 | tf_op jit(solution)/shard_map/image_sum/pallas_call | solution.py:72
  (25 shorter events, 0.2 us)
Async XLA Ops:
  0.6 15.6 %collective-permute-start = (bf16[48,1024]{1,0:T(8,128)(2,1)}, bf16[48,1024]{1,0:T(8,128)(2,1)S(1)}, u32[]{:S(2)}, u32[]{:S(2)}) collective-permute-start(bf16[48,1024]{1,0:T(8,128)(2,1)} %near.1), channel_id=1, source_target_pairs={{0,112},{16,0},{32,16},{48,32},{64,48},{80,64},{96,80},{112,96},{1... | collective-permute-start | bytes 294920 | tf_op jit(solution)/shard_map/ppermute | solution.py:21
  9.3 6.9 %copy-start = (bf16[48,1024]{1,0:T(8,128)(2,1)S(1)}, bf16[48,1024]{1,0:T(8,128)(2,1)}, u32[]{:S(2)}) copy-start(bf16[48,1024]{1,0:T(8,128)(2,1)} %near.1) | copy-start | bytes 294916
  9.3 29.9 %all-to-all-start = ((bf16[16,48,1024]{2,1,0:T(8,128)(2,1)}), bf16[16,48,1024]{2,1,0:T(8,128)(2,1)S(1)}, u32[]{:S(2)}, u32[]{:S(2)}) async-start(bf16[16,48,1024]{2,1,0:T(8,128)(2,1)} %copies.1), calls=%async_computation | async-start | bytes 3145728 | tf_op jit(solution)/shard_map/all_to_all | solution.py:338
  16.2 20.1 %copy-start.1 = (s32[384]{0:T(512)S(1)}, s32[384]{0:T(512)}, u32[]{:S(2)}) copy-start(s32[384]{0:T(512)} %refs_9_.1) | copy-start | bytes 4612
  16.3 10.0 %collective-permute-start.3 = (bf16[96,1024]{1,0:T(8,128)(2,1)S(1)}, bf16[96,1024]{1,0:T(8,128)(2,1)S(1)}, u32[]{:S(2)}, u32[]{:S(2)}) collective-permute-start(bf16[96,1024]{1,0:T(8,128)(2,1)S(1)} %join.1.refs_0_), channel_id=1, source_target_pairs={{0,32},{16,48},{32,64},{48,80},{64,96},{80,112},{96,0},{112,16},{1... | collective-permute-start | bytes 589832 | tf_op jit(solution)/shard_map/ppermute | solution.py:21
  16.4 17.2 %collective-permute-start.2 = (bf16[96,1024]{1,0:T(8,128)(2,1)S(1)}, bf16[96,1024]{1,0:T(8,128)(2,1)S(1)}, u32[]{:S(2)}, u32[]{:S(2)}) collective-permute-start(bf16[96,1024]{1,0:T(8,128)(2,1)S(1)} %join.1.refs_0_), channel_id=1, source_target_pairs={{0,96},{16,112},{32,0},{48,16},{64,32},{80,48},{96,64},{112,80},{1... | collective-permute-start | bytes 589832 | tf_op jit(solution)/shard_map/ppermute | solution.py:21
  20.0 16.4 %collective-permute-start.1 = (bf16[96,1024]{1,0:T(8,128)(2,1)S(1)}, bf16[96,1024]{1,0:T(8,128)(2,1)S(1)}, u32[]{:S(2)}, u32[]{:S(2)}) collective-permute-start(bf16[96,1024]{1,0:T(8,128)(2,1)S(1)} %join.1.refs_0_), channel_id=1, source_target_pairs={{0,64},{16,80},{32,96},{48,112},{64,0},{80,16},{96,32},{112,48},{1... | collective-permute-start | bytes 589832 | tf_op jit(solution)/shard_map/ppermute | solution.py:21
  21.3 17.9 %collective-permute-start.4 = (bf16[96,1024]{1,0:T(8,128)(2,1)S(1)}, bf16[96,1024]{1,0:T(8,128)(2,1)S(1)}, u32[]{:S(2)}, u32[]{:S(2)}) collective-permute-start(bf16[96,1024]{1,0:T(8,128)(2,1)S(1)} %join.1.refs_0_), channel_id=1, source_target_pairs={{0,8},{8,0},{1,9},{9,1},{2,10},{10,2},{3,11},{11,3},{4,12},{12,4},... | collective-permute-start | bytes 589832 | tf_op jit(solution)/shard_map/ppermute | solution.py:346
  26.3 12.9 %collective-permute-start.7 = (bf16[96,1024]{1,0:T(8,128)(2,1)S(1)}, bf16[96,1024]{1,0:T(8,128)(2,1)S(1)}, u32[]{:S(2)}, u32[]{:S(2)}) collective-permute-start(bf16[96,1024]{1,0:T(8,128)(2,1)S(1)} %collective-permute-done.3.refs_3_), channel_id=1, source_target_pairs={{0,8},{8,0},{1,9},{9,1},{2,10},{10,2},{3,11},{11,3},{4,12},{12,4},... | collective-permute-start | bytes 589832 | tf_op jit(solution)/shard_map/ppermute | solution.py:346
  33.6 5.6 %collective-permute-start.6 = (bf16[96,1024]{1,0:T(8,128)(2,1)S(1)}, bf16[96,1024]{1,0:T(8,128)(2,1)S(1)}, u32[]{:S(2)}, u32[]{:S(2)}) collective-permute-start(bf16[96,1024]{1,0:T(8,128)(2,1)S(1)} %collective-permute-done.2.refs_2_), channel_id=1, source_target_pairs={{0,8},{8,0},{1,9},{9,1},{2,10},{10,2},{3,11},{11,3},{4,12},{12,4},... | collective-permute-start | bytes 589832 | tf_op jit(solution)/shard_map/ppermute | solution.py:346
  36.3 2.8 %collective-permute-start.5 = (bf16[96,1024]{1,0:T(8,128)(2,1)S(1)}, bf16[96,1024]{1,0:T(8,128)(2,1)S(1)}, u32[]{:S(2)}, u32[]{:S(2)}) collective-permute-start(bf16[96,1024]{1,0:T(8,128)(2,1)S(1)} %collective-permute-done.1.refs_1_), channel_id=1, source_target_pairs={{0,8},{8,0},{1,9},{9,1},{2,10},{10,2},{3,11},{11,3},{4,12},{12,4},... | collective-permute-start | bytes 589832 | tf_op jit(solution)/shard_map/ppermute | solution.py:346
  36.3 2.8 %collective-permute-start.8 = (s32[384]{0:T(512)S(1)}, s32[384]{0:T(512)S(1)}, u32[]{:S(2)}, u32[]{:S(2)}) collective-permute-start(s32[384]{0:T(512)S(1)} %copy-done.1), channel_id=1, source_target_pairs={{0,128},{128,0},{1,129},{129,1},{2,130},{130,2},{3,131},{131,3},{4... | collective-permute-start | bytes 4616 | tf_op jit(solution)/shard_map/ppermute | solution.py:329
  42.2 2.7 %collective-permute-start.9 = (f32[1,1024]{1,0:T(1,128)S(1)}, f32[1,1024]{1,0:T(1,128)S(1)}, u32[]{:S(2)}, u32[]{:S(2)}) collective-permute-start(f32[1,1024]{1,0:T(1,128)S(1)} %get-tuple-element.25.mine), channel_id=1, source_target_pairs={{0,8},{8,0},{1,9},{9,1},{2,10},{10,2},{3,11},{11,3},{4,12},{12,4},... | collective-permute-start | bytes 12296 | tf_op jit(solution)/shard_map/ppermute | solution.py:365
  43.6 5.4 %collective-permute-start.13 = (f32[1,896]{1,0:T(1,128)S(1)}, f32[1,896]{1,0:T(1,128)S(1)}, u32[]{:S(2)}, u32[]{:S(2)}) collective-permute-start(f32[1,896]{1,0:T(1,128)S(1)} %get-tuple-element.26.mine), channel_id=1, source_target_pairs={{0,128},{128,0},{1,129},{129,1},{2,130},{130,2},{3,131},{131,3},{4... | collective-permute-start | bytes 10760 | tf_op jit(solution)/shard_map/ppermute | solution.py:365
  45.0 6.5 %collective-permute-start.10 = (f32[1,1024]{1,0:T(1,128)S(1)}, f32[1,1024]{1,0:T(1,128)S(1)}, u32[]{:S(2)}, u32[]{:S(2)}) collective-permute-start(f32[1,1024]{1,0:T(1,128)S(1)} %pair.8.mine), channel_id=1, source_target_pairs={{0,16},{16,0},{32,48},{48,32},{64,80},{80,64},{96,112},{112,96},{1... | collective-permute-start | bytes 12296 | tf_op jit(solution)/shard_map/ppermute | solution.py:365
  49.0 4.0 %collective-permute-start.14 = (f32[1,896]{1,0:T(1,128)S(1)}, f32[1,896]{1,0:T(1,128)S(1)}, u32[]{:S(2)}, u32[]{:S(2)}) collective-permute-start(f32[1,896]{1,0:T(1,128)S(1)} %pair.12.mine), channel_id=1, source_target_pairs={{0,1},{1,0},{2,3},{3,2},{4,5},{5,4},{6,7},{7,6},{8,9},{9,8},{10,11... | collective-permute-start | bytes 10760 | tf_op jit(solution)/shard_map/ppermute | solution.py:365
  51.5 3.4 %collective-permute-start.11 = (f32[1,1024]{1,0:T(1,128)S(1)}, f32[1,1024]{1,0:T(1,128)S(1)}, u32[]{:S(2)}, u32[]{:S(2)}) collective-permute-start(f32[1,1024]{1,0:T(1,128)S(1)} %pair.9.mine), channel_id=1, source_target_pairs={{0,32},{16,48},{32,0},{48,16},{64,96},{80,112},{96,64},{112,80},{1... | collective-permute-start | bytes 12296 | tf_op jit(solution)/shard_map/ppermute | solution.py:365
  53.1 4.0 %collective-permute-start.15 = (f32[1,896]{1,0:T(1,128)S(1)}, f32[1,896]{1,0:T(1,128)S(1)}, u32[]{:S(2)}, u32[]{:S(2)}) collective-permute-start(f32[1,896]{1,0:T(1,128)S(1)} %pair.13.mine), channel_id=1, source_target_pairs={{0,2},{2,0},{4,6},{6,4},{1,3},{3,1},{5,7},{7,5},{8,10},{10,8},{12,... | collective-permute-start | bytes 10760 | tf_op jit(solution)/shard_map/ppermute | solution.py:365
  55.0 6.5 %collective-permute-start.12 = (f32[1,1024]{1,0:T(1,128)S(1)}, f32[1,1024]{1,0:T(1,128)S(1)}, u32[]{:S(2)}, u32[]{:S(2)}) collective-permute-start(f32[1,1024]{1,0:T(1,128)S(1)} %pair.10.mine), channel_id=1, source_target_pairs={{0,64},{16,80},{32,96},{48,112},{64,0},{80,16},{96,32},{112,48},{1... | collective-permute-start | bytes 12296 | tf_op jit(solution)/shard_map/ppermute | solution.py:365
  57.0 4.0 %collective-permute-start.16 = (f32[1,896]{1,0:T(1,128)S(1)}, f32[1,896]{1,0:T(1,128)S(1)}, u32[]{:S(2)}, u32[]{:S(2)}) collective-permute-start(f32[1,896]{1,0:T(1,128)S(1)} %pair.14.mine), channel_id=1, source_target_pairs={{0,4},{2,6},{4,0},{6,2},{1,5},{3,7},{5,1},{7,3},{8,12},{10,14},{12... | collective-permute-start | bytes 10760 | tf_op jit(solution)/shard_map/ppermute | solution.py:365
  64.8 8.8 %collective-permute-start.17 = (f32[8,128]{1,0:T(8,128)S(1)}, f32[8,128]{1,0:T(8,128)S(1)}, u32[]{:S(2)}, u32[]{:S(2)}) collective-permute-start(f32[8,128]{1,0:T(8,128)S(1)} %get-tuple-element.31.terms), channel_id=1, source_target_pairs={{0,8},{8,0},{1,9},{9,1},{2,10},{10,2},{3,11},{11,3},{4,12},{12,4},... | collective-permute-start | bytes 12296 | tf_op jit(solution)/shard_map/ppermute | solution.py:393
  68.1 40.4 %all-to-all-start.1 = ((bf16[16,400,128]{2,1,0:T(8,128)(2,1)}), bf16[16,400,128]{2,1,0:T(8,128)(2,1)S(1)}, u32[]{:S(2)}, u32[]{:S(2)}) async-start(bf16[16,400,128]{2,1,0:T(8,128)(2,1)} %get-tuple-element.30), calls=%async_computation.1 | async-start | bytes 3276800 | tf_op jit(solution)/shard_map/all_to_all | solution.py:392
  73.6 1.3 %copy-start.2 = (bf16[768,768]{1,0:T(8,128)(2,1)S(1)}, bf16[768,768]{1,0:T(8,128)(2,1)}, u32[]{:S(2)}) copy-start(bf16[768,768]{1,0:T(8,128)(2,1)} %get-tuple-element.32.grads) | copy-start | bytes 3538948
  76.5 2.4 %collective-permute-start.18 = (bf16[384,1024]{1,0:T(8,128)(2,1)S(1)}, bf16[384,1024]{1,0:T(8,128)(2,1)S(1)}, u32[]{:S(2)}, u32[]{:S(2)}) collective-permute-start(bf16[384,1024]{1,0:T(8,128)(2,1)S(1)} %get-tuple-element.34), channel_id=1, source_target_pairs={{0,8},{8,0},{1,9},{9,1},{2,10},{10,2},{3,11},{11,3},{4,12},{12,4},... | collective-permute-start | bytes 2359304 | tf_op jit(solution)/shard_map/ppermute | solution.py:406
  79.6 11.3 %collective-permute-start.19 = (bf16[784,128]{1,0:T(8,128)(2,1)S(1)}, bf16[784,128]{1,0:T(8,128)(2,1)S(1)}, u32[]{:S(2)}, u32[]{:S(2)}) collective-permute-start(bf16[784,128]{1,0:T(8,128)(2,1)S(1)} %get-tuple-element.37), channel_id=1, source_target_pairs={{0,64},{16,80},{32,96},{48,112},{64,0},{80,16},{96,32},{112,48},{1... | collective-permute-start | bytes 602120 | tf_op jit(solution)/shard_map/ppermute | solution.py:21
  83.0 16.3 %collective-permute-start.20 = (bf16[784,128]{1,0:T(8,128)(2,1)S(1)}, bf16[784,128]{1,0:T(8,128)(2,1)S(1)}, u32[]{:S(2)}, u32[]{:S(2)}) collective-permute-start(bf16[784,128]{1,0:T(8,128)(2,1)S(1)} %get-tuple-element.38), channel_id=1, source_target_pairs={{0,32},{16,48},{32,64},{48,80},{64,96},{80,112},{96,0},{112,16},{1... | collective-permute-start | bytes 602120 | tf_op jit(solution)/shard_map/ppermute | solution.py:21
  84.3 17.8 %collective-permute-start.21 = (bf16[784,128]{1,0:T(8,128)(2,1)S(1)}, bf16[784,128]{1,0:T(8,128)(2,1)S(1)}, u32[]{:S(2)}, u32[]{:S(2)}) collective-permute-start(bf16[784,128]{1,0:T(8,128)(2,1)S(1)} %get-tuple-element.39), channel_id=1, source_target_pairs={{0,96},{16,112},{32,0},{48,16},{64,32},{80,48},{96,64},{112,80},{1... | collective-permute-start | bytes 602120 | tf_op jit(solution)/shard_map/ppermute | solution.py:21
  102.5 5.2 %collective-permute-start.22 = (bf16[400,128]{1,0:T(8,128)(2,1)S(1)}, bf16[400,128]{1,0:T(8,128)(2,1)S(1)}, u32[]{:S(2)}, u32[]{:S(2)}) collective-permute-start(bf16[400,128]{1,0:T(8,128)(2,1)S(1)} %get-tuple-element.42), channel_id=1, source_target_pairs={{0,16},{16,32},{32,48},{48,64},{64,80},{80,96},{96,112},{112,0},{1... | collective-permute-start | bytes 307208 | tf_op jit(solution)/shard_map/ppermute | solution.py:21

commit v12 on v10

--- a/solution.py
+++ b/solution.py
@@ -8,6 +8,7 @@
 from jax.experimental.pallas import tpu as pltpu
 from jax.sharding import Mesh, PartitionSpec as P
 
+AXES = ("xl", "z", "c", "y", "xh")
 PLANE = ("xl", "y", "xh")
 SWAP = [(0, 1), (1, 0)]
 LANES = 128
@@ -19,6 +20,37 @@
 def turn(x, axis, step):
     count = lax.axis_size(axis)
     return lax.ppermute(x, axis, [(i, (i + step) % count) for i in range(count)])
+
+
+def lean(q, z, count):
+    return q * (1 - 2 * (z % 2)) if abs(q) == count // 4 else q
+
+
+def turn_z(x, q, back):
+    count = lax.axis_size("z")
+    pairs = [((i + lean(q, i, count)) % count, i) for i in range(count)]
+    return lax.ppermute(x, "z", pairs if back else [(b, a) for a, b in pairs])
+
+
+def turn_both(x, step_z, step_x, step_y):
+    sizes = [lax.axis_size(a) for a in AXES]
+    n_xl, n_z, n_c, n_y, n_xh = sizes
+    n_x = n_xl * n_xh
+    pairs = []
+    for i in range(math.prod(sizes)):
+        rest, xh = divmod(i, n_xh)
+        rest, y = divmod(rest, n_y)
+        rest, c = divmod(rest, n_c)
+        xl, z = divmod(rest, n_z)
+        if c == 0:
+            if step_z is None:
+                continue
+            z = (z + step_z) % n_z
+        else:
+            xh, xl = divmod((xh * n_xl + xl + step_x) % n_x, n_xl)
+            y = (y + step_y) % n_y
+        pairs.append((i, (((xl * n_z + z) * n_c + c) * n_y + y) * n_xh + xh))
+    return lax.ppermute(x, AXES, pairs)
 
 
 def merge(parts):
@@ -109,7 +141,7 @@
 def score_body(steps, inv_root, *refs):
     n_z = 2 * len(steps)
     pieces, refs = refs[:n_z], refs[n_z:]
-    image, pair_mine, pair_seen, pair_out, row_exp, col_exp, text, row_sent, col_sent, tops = refs
+    image, pair_mine, pair_seen, pair_out, scores, text, hold, cross = refs
     pair = pair_row(pair_mine, pair_seen)
     pair_out[...] = pair
     rows = pieces[0].shape[0] // 2
@@ -123,10 +155,12 @@
             piece = pieces[h * n_z // 2 + i]
             high = jnp.maximum(high, jnp.abs(piece[...].astype(F32)))
             for k in range(2):
-                start = (h * n_z + lax.rem(z + q + (k + 2) * n_z // 2, n_z)) * rows
+                to = lax.rem(z + lean(q, z, n_z) + (k + 2) * n_z // 2, n_z)
+                start = (h * n_z + to) * rows
                 text[pl.ds(pl.multiple_of(start, 16), rows), :] = piece[
                     k * rows : (k + 1) * rows, :
                 ]
+    lanes = []
     step = 256
     for r in range(0, size, step):
         tile = (
@@ -138,25 +172,56 @@
             )
             * inv_root
         )
-        col_exp[r : r + step, :] = tile
+        scores[r : r + step, :] = tile
         top = jnp.max(tile, axis=1, keepdims=True)
-        mass = jnp.exp(tile - top)
-        row_exp[r : r + step, :] = mass
-        part = jnp.log(jnp.sum(mass, axis=1, keepdims=True))
-        tops[0:1, r : r + step] = to_row(top)
-        row_sent[:, r : r + step] = to_row(top + part)
+        part = jnp.log(jnp.sum(jnp.exp(tile - top), axis=1, keepdims=True))
+        lanes.append(to_row(top + part))
         hit = to_column(pair[:, r : r + step]) == ids
         found += jnp.sum(jnp.where(hit, tile, 0.0), axis=0, keepdims=True)
-    row_sent[:, size:] = jnp.full((1, LANES), jnp.max(high))
-    tile = col_exp[...]
+    tile = scores[...]
     top = jnp.max(tile, axis=0, keepdims=True)
-    mass = jnp.exp(tile - top)
-    col_exp[...] = mass
-    tops[1:2, :] = top
-    col_sent[:, :size] = top + jnp.log(jnp.sum(mass, axis=0, keepdims=True))
-    high = jnp.max(jnp.abs(image[...].astype(F32)))
-    col_sent[:, size : size + LANES] = jnp.full((1, LANES), high)
-    col_sent[:, size + LANES :] = jnp.full((1, LANES), jnp.sum(found))
+    col = top + jnp.log(jnp.sum(jnp.exp(tile - top), axis=0, keepdims=True))
+    image_max = jnp.max(jnp.abs(image[...].astype(F32)))
+    zero = jnp.zeros((1, LANES), F32)
+    rows_out = jnp.concatenate([*lanes, zero + jnp.max(high), zero], axis=1)
+    cols_out = jnp.concatenate([col, zero + image_max, zero + jnp.sum(found)], axis=1)
+    first = lax.axis_index("c") == 0
+    hold[...] = jnp.where(first, cols_out, rows_out)
+    cross[...] = jnp.where(first, rows_out, cols_out)
+
+
+def crossed(cols):
+    half = cols.shape[1] // 2
+    return jnp.concatenate([cols[:, half:], cols[:, :half]], axis=1)
+
+
+def meet_body(hold, seen, out):
+    size = hold.shape[1] - 2 * LANES
+    first = lax.axis_index("c") == 0
+    mine, other = hold[:, :size], seen[:, :size]
+    out[:, :size] = jnp.where(first, merge([mine, crossed(other)]), mine)
+    out[:, size : 2 * size] = jnp.where(first, 0.0, other)
+    high = jnp.maximum(hold[:, size : size + LANES], seen[:, size : size + LANES])
+    total = hold[:, size + LANES :] + seen[:, size + LANES :]
+    out[:, 2 * size :] = jnp.concatenate([high, total], axis=1)
+
+
+def round_body(last, mine, one, two, three, *outs):
+    size = mine.shape[1] // 2 - LANES
+    first = lax.axis_index("c") == 0
+    parts = [mine[:, : 2 * size], one[:, : 2 * size]]
+    for ref in (two, three):
+        part = ref[:, : 2 * size]
+        parts.append(jnp.where(first, -1e38, part) if last else part)
+    lse = merge(parts)
+    refs = (mine, one, two, three)
+    at = slice(2 * size, 2 * size + LANES)
+    high = functools.reduce(jnp.maximum, [ref[:, at] for ref in refs])
+    total = sum(ref[:, 2 * size + LANES :] for ref in refs)
+    outs[0][...] = jnp.concatenate([lse, high, total], axis=1)
+    if last:
+        kept = jnp.where(first, lse[:, :size], lse[:, size:])
+        outs[1][...] = jnp.concatenate([kept, high, total], axis=1)
 
 
 def labels(n_z, rows):
@@ -172,39 +237,28 @@
     return (ids + within - holder * rows).astype(F32)
 
 
-def pair_body(crossed, count, mine, seen, out):
-    half = count // 2
-    other = seen[:, :count]
-    if crossed:
-        other = jnp.concatenate([seen[:, half:count], seen[:, :half]], axis=1)
-    out[:, :count] = merge([mine[:, :count], other])
-    at = slice(count, count + LANES)
-    out[:, at] = jnp.maximum(mine[:, at], seen[:, at])
-    if mine.shape[1] > count + LANES:
-        at = slice(count + LANES, count + 2 * LANES)
-        out[:, at] = mine[:, at] + seen[:, at]
-
-
 def grad_body(n_z, inv_root, *refs):
-    cols, rows_lse, tops, row_exp, col_exp, text, image, pair = refs[:8]
-    terms, own, other, sent, grads, held, crossing, staying, sems = refs[8:]
+    mine, seen, scores, text, image, pair = refs[:6]
+    terms, own, other, sent, grads, held, crossing, sems = refs[6:]
     size = grads.shape[0]
     half = own.shape[0]
     rows = half // n_z
     _, tall, _ = sent.shape
-    col_lse = cols[:, :size]
-    image_max = cols[:, size : size + LANES]
-    found = cols[:, size + LANES :]
     ids = labels(n_z, rows)
-    row_lse = rows_lse[:, :size]
-    text_max = rows_lse[:, size:]
+    first = lax.axis_index("c") == 0
+    seen_lse, seen_high = seen[:, :size], seen[:, size : size + LANES]
+    mine_lse, mine_high = mine[:, :size], mine[:, 2 * size : 2 * size + LANES]
+    col_lse = jnp.where(first, mine_lse, crossed(seen_lse))
+    row_lse = jnp.where(first, seen_lse, mine_lse)
+    image_max = jnp.where(first, mine_high, seen_high)
+    text_max = jnp.where(first, seen_high, mine_high)
+    found = jnp.where(first, mine[:, 2 * size + LANES :], seen[:, size + LANES :])
     row_terms = jnp.broadcast_to(jnp.sum(row_lse, axis=1, keepdims=True), (1, LANES))
     col_terms = jnp.sum(col_lse, axis=1, keepdims=True) - 2.0 * found
     terms[...] = jnp.concatenate(
         [row_terms, text_max, image_max, jnp.zeros((5, LANES), F32)], axis=0
     )
-    row_part = to_column(0.5 * jnp.exp(tops[0:1, :] - row_lse))
-    col_part = 0.5 * jnp.exp(tops[1:2, :] - col_lse)
+    row_column = to_column(row_lse)
     pair_column = to_column(pair[...])
     extra = split3(col_terms)
     scale = inverse(text_max[:, :1]) * inv_root
@@ -212,7 +266,8 @@
     copies = []
     for r in range(0, size, step):
         at = slice(r, r + step)
-        probs = row_exp[at, :] * row_part[at, :] + col_exp[at, :] * col_part
+        tile = scores[at, :]
+        probs = 0.5 * (jnp.exp(tile - row_column[at, :]) + jnp.exp(tile - col_lse))
         grad = (probs - jnp.where(pair_column[at, :] == ids, 1.0, 0.0)).astype(BF16)
         grads[at, :] = grad
         part = encode(jnp.dot(grad, text[...], preferred_element_type=F32) * scale)
@@ -228,7 +283,7 @@
     scale = inverse(image_max[:, :1]) * inv_root
     extra = split3(row_terms)
     crossing[half:, :] = jnp.concatenate([extra] * (own.shape[1] // LANES), axis=1)
-    for start in (0, half):
+    for start in (half, 0):
         part = lax.dot_general(
             grads[:, start : start + half],
             image[...],
@@ -236,12 +291,11 @@
             preferred_element_type=F32,
         )
         if start == 0:
-            staying[...] = part * scale
-            copies.append(pltpu.make_async_copy(staying, own, sems.at[sent.shape[0]]))
+            own[...] = encode(part * scale)
         else:
             crossing[:half, :] = encode(part * scale)
-            copies.append(pltpu.make_async_copy(crossing, other, sems.at[sent.shape[0] + 1]))
-        copies[-1].start()
+            copies.append(pltpu.make_async_copy(crossing, other, sems.at[sent.shape[0]]))
+            copies[-1].start()
     for copy in copies:
         copy.wait()
 
@@ -269,9 +323,10 @@
     for i, q in enumerate(steps):
         blocks = []
         for k in range(2):
-            start = lax.rem(z + q + (k + 2) * n_z // 2, n_z) * rows
+            to = lax.rem(z + lean(q, z, n_z) + (k + 2) * n_z // 2, n_z)
+            start = to * rows
             at = pl.ds(pl.multiple_of(start, 16), rows)
-            blocks.append(own[at, :] + decode(seen[at, :]))
+            blocks.append(decode(own[at, :]) + decode(seen[at, :]))
         if i == 0:
             keep[:rows, :] = blocks[0]
             keep[rows:, :] = blocks[1]
@@ -351,56 +406,53 @@
     (joined,) = call(
         join_body, (shape((2 * rows, width), BF16),), (text_embed, far), "join", 10**11
     )
-    pieces = [joined] + [turn(joined, "z", -q) for q in steps[1:]]
+    pieces = [joined] + [turn_z(joined, q, True) for q in steps[1:]]
     pieces = pieces + [lax.ppermute(piece, "c", SWAP) for piece in pieces]
 
     flops = 2 * size * size * width
-    pair, row_exp, col_exp, text, row_part, col_part, tops = call(
+    pair, scores, text, hold, cross = call(
         functools.partial(score_body, steps, inv_root),
         (
             shape((1, size), F32),
             shape((size, size), F32),
-            shape((size, size), F32),
             shape((size, width), BF16),
-            shape((1, size + LANES), F32),
             shape((1, size + 2 * LANES), F32),
-            shape((2, size), F32),
+            shape((1, size + 2 * LANES), F32),
         ),
         (*pieces, image, pair_index, pair_seen),
         "scores",
         flops,
         2 * size * size,
     )
-    def exchange(part, axis, step):
-        count = lax.axis_size(axis)
-        seen = lax.ppermute(part, axis, [(i, i ^ step) for i in range(count)])
-        merge_body = functools.partial(pair_body, axis == "c", size)
-        return call(merge_body, (shape(part.shape, F32),), (part, seen), "pair")[0]
-
-    for axis, step in (("c", 1), ("z", 1), ("z", 2), ("z", 4)):
-        col_part = exchange(col_part, axis, step)
-    for axis, step in (("xl", 1), ("xh", 1), ("y", 1), ("y", 2)):
-        row_part = exchange(row_part, axis, step)
+    full = shape((1, 2 * size + 2 * LANES), F32)
+    (stats,) = call(meet_body, (full,), (hold, lax.ppermute(cross, "c", SWAP)), "meet")
+    around = [turn_both(stats, q, q, 0) for q in (1, -1, 2)]
+    (stats,) = call(functools.partial(round_body, False), (full,), (stats, *around), "round")
+    far_z = (n_z // 2, None, None)
+    around = [turn_both(stats, f, 0, q) for f, q in zip(far_z, (1, -1, 2))]
+    stats, cross = call(
+        functools.partial(round_body, True), (full, shape(cross.shape, F32)), (stats, *around), "last"
+    )
+    seen = lax.ppermute(cross, "c", SWAP)
 
     terms, text_own, text_other, image_sent = call(
         functools.partial(grad_body, n_z, inv_root),
         (
             shape((8, LANES), F32),
-            pltpu.HBM((half, width), F32),
+            shape((half, width), BF16),
             pltpu.HBM((half + EXTRA, width), BF16),
             pltpu.HBM((n_plane, tall, LANES), BF16),
         ),
-        (col_part, row_part, tops, row_exp, col_exp, text, image, pair),
+        (stats, seen, scores, text, image, pair),
         "grads",
         2 * flops,
-        0,
-        hbm_out=(1, 2, 3),
+        2 * size * size,
+        hbm_out=(2, 3),
         scratch=[
             pltpu.VMEM((size, size), BF16),
             pltpu.VMEM((n_plane, tall, LANES), BF16),
             pltpu.VMEM((half + EXTRA, width), BF16),
-            pltpu.VMEM((half, width), F32),
-            pltpu.SemaphoreType.DMA((n_plane + 2,)),
+            pltpu.SemaphoreType.DMA((n_plane + 1,)),
         ],
     )
     image_got = lax.all_to_all(image_sent, PLANE, 0, 0)
@@ -413,7 +465,7 @@
         10**10,
         size=1,
     )
-    pays = [turn(pay, "z", q) for q, pay in zip(steps[1:], pays)]
+    pays = [turn_z(pay, q, False) for q, pay in zip(steps[1:], pays)]
     near, far, total = call(
         relay_body,
         (shape((rows, width), F32), shape((tall, LANES), BF16), shape((1, LANES), F32)),

time: 105 us -> 104 us (level); the launches traced: 103 us -> 104 us
  waiting for transfers between devices: 32.8 us -> 36.6 us
  starting transfers between devices: 53.3 us -> 51.5 us
  local copies, waits for them, and re-layouts: 2.31 us -> 0.9 us
    ppermute x8 -> x2, waiting for transfers between devices: 23.8 us -> 7.53 us  [turn(): lax.ppermute(x, axis, [(i, (i + step) % count) for i in range(count)])]
    ppermute x8 -> x14, waiting for transfers between devices: 6.78 us -> 18.7 us  [the longest x6 10.7 us: turn_z(): return lax.ppermute(x, 'z', pairs if back else [(b, a) for a, b in pairs])]
    ppermute x8 -> x14, starting transfers between devices: 11.8 us -> 20.8 us  [the longest x6 11.3 us: turn_both(): return lax.ppermute(x, AXES, pairs)]
    ppermute x8 -> x2, starting transfers between devices: 17.4 us -> 8.66 us  [turn(): lax.ppermute(x, axis, [(i, (i + step) % count) for i in range(count)])]
    ppermute x1, starting transfers between devices: 3.89 us -> 0.4 us  [shards(): lax.ppermute(text_other, 'c', SWAP)]
    all_to_all x1, waiting for transfers between devices: 0.01 us -> 3.09 us  [shards(): image_got = lax.all_to_all(image_sent, PLANE, 0, 0)]
    ppermute x1, waiting for transfers between devices: 1.37 us -> 3.95 us  [shards(): pair_seen = lax.ppermute(pair_index, 'xl', SWAP)]
    all_to_all x1, waiting for transfers between devices: 0.84 us -> 3.34 us  [shards(): image = lax.all_to_all(copies, PLANE, 0, 0).reshape(size, width)]
  transfers between devices with their start and end apart: 24 -> 24, of which waited for: 13 -> 14; matrix products, arithmetic and copies ran while one was open for 0% -> 0% of each run, Pallas kernels for 3% -> 2%
where the time goes in v12:
time: 104 us
  starting transfers between devices  51.5 us (50%)
  waiting for transfers between devices  36.6 us (35%)
  Pallas kernels  13.8 us (13%)
    pallas_call x11, Pallas kernels, call(): pl.pallas_call(body, out_shape=outs, in_specs=[pl.BlockSpec(memory_space=...  13.8 us
    ppermute x6, starting transfers between devices, turn_both(): return lax.ppermute(x, AXES, pairs)  11.3 us
    ppermute x6, waiting for transfers between devices, turn_z(): return lax.ppermute(x, 'z', pairs if back else [(b, a) for a, b in pairs])  10.7 us
    ppermute x2, starting transfers between devices, turn(): lax.ppermute(x, axis, [(i, (i + step) % count) for i in range(count)])  8.66 us
    ppermute x4, starting transfers between devices, shards(): pieces = pieces + [lax.ppermute(piece, 'c', SWAP) for piece in pieces]  7.89 us
    ppermute x2, waiting for transfers between devices, turn(): lax.ppermute(x, axis, [(i, (i + step) % count) for i in range(count)])  7.53 us
    all_to_all x1, starting transfers between devices, shards(): image = lax.all_to_all(copies, PLANE, 0, 0).reshape(size, width)  6.9 us
    ppermute x6, starting transfers between devices, turn_z(): return lax.ppermute(x, 'z', pairs if back else [(b, a) for a, b in pairs])  6.69 us
  transfers between devices with their start and end apart: 24, of which 14 were waited for; matrix products, arithmetic and copies ran while one was open for 0% of the time, Pallas kernels for 2%

profile of v12, /device:TPU:1, one launch (start us, length us, event | category | flops | bytes accessed | tf_op | source)
XLA Modules:
  0.0 103.8 jit_solution(18227037864959664221)
XLA Ops:
  0.6 7.8 %collective-permute-start = (bf16[48,1024]{1,0:T(8,128)(2,1)}, bf16[48,1024]{1,0:T(8,128)(2,1)S(1)}, u32[]{:S(2)}, u32[]{:S(2)}) collective-permute-start(bf16[48,1024]{1,0:T(8,128)(2,1)} %near.1), channel_id=1, source_target_pairs={{0,64},{16,80},{32,96},{48,112},{64,0},{80,16},{96,32},{112,48},{1... | collective-permute-start | bytes 294920 | tf_op jit(solution)/shard_map/ppermute | solution.py:22
  8.5 0.9 copy-done
  9.3 1.3 %copies.1 = bf16[16,48,1024]{2,1,0:T(8,128)(2,1)} custom-call(bf16[48,1024]{1,0:T(8,128)(2,1)S(1)} %copy-done), custom_call_target="tpu_custom_call" | custom-call | bytes 1671168 | tf_op jit(solution)/shard_map/copies/pallas_call | solution.py:104
  10.7 0.0 copy-start.1
  10.7 6.9 %all-to-all-start = ((bf16[16,48,1024]{2,1,0:T(8,128)(2,1)}), bf16[16,48,1024]{2,1,0:T(8,128)(2,1)S(1)}, u32[]{:S(2)}, u32[]{:S(2)}) async-start(bf16[16,48,1024]{2,1,0:T(8,128)(2,1)} %copies.1), calls=%async_computation | async-start | bytes 3145728 | tf_op jit(solution)/shard_map/all_to_all | solution.py:402
  17.6 0.0 copy-start.2
  17.6 0.8 collective-permute-start.3
  18.5 0.3 collective-permute-start.2
  18.7 2.9 %collective-permute-start.1 = (bf16[96,1024]{1,0:T(8,128)(2,1)S(1)}, bf16[96,1024]{1,0:T(8,128)(2,1)S(1)}, u32[]{:S(2)}, u32[]{:S(2)}) collective-permute-start(bf16[96,1024]{1,0:T(8,128)(2,1)S(1)} %join.1.refs_0_), channel_id=1, source_target_pairs={{16,0},{32,16},{48,32},{64,48},{80,64},{96,80},{112,96},{0,112},{1... | collective-permute-start | bytes 589832 | tf_op jit(solution)/shard_map/ppermute | solution.py:32
  21.6 2.1 %collective-permute-start.4 = (bf16[96,1024]{1,0:T(8,128)(2,1)S(1)}, bf16[96,1024]{1,0:T(8,128)(2,1)S(1)}, u32[]{:S(2)}, u32[]{:S(2)}) collective-permute-start(bf16[96,1024]{1,0:T(8,128)(2,1)S(1)} %join.1.refs_0_), channel_id=1, source_target_pairs={{0,8},{8,0},{1,9},{9,1},{2,10},{10,2},{3,11},{11,3},{4,12},{12,4},... | collective-permute-start | bytes 589832 | tf_op jit(solution)/shard_map/ppermute | solution.py:410
  23.7 0.4 collective-permute-done.3.refs_3_
  24.1 3.9 %collective-permute-start.7 = (bf16[96,1024]{1,0:T(8,128)(2,1)S(1)}, bf16[96,1024]{1,0:T(8,128)(2,1)S(1)}, u32[]{:S(2)}, u32[]{:S(2)}) collective-permute-start(bf16[96,1024]{1,0:T(8,128)(2,1)S(1)} %collective-permute-done.3.refs_3_), channel_id=1, source_target_pairs={{0,8},{8,0},{1,9},{9,1},{2,10},{10,2},{3,11},{11,3},{4,12},{12,4},... | collective-permute-start | bytes 589832 | tf_op jit(solution)/shard_map/ppermute | solution.py:410
  28.0 0.7 collective-permute-start.6
  28.7 0.4 collective-permute-done.1.refs_1_
  29.1 1.2 %collective-permute-start.5 = (bf16[96,1024]{1,0:T(8,128)(2,1)S(1)}, bf16[96,1024]{1,0:T(8,128)(2,1)S(1)}, u32[]{:S(2)}, u32[]{:S(2)}) collective-permute-start(bf16[96,1024]{1,0:T(8,128)(2,1)S(1)} %collective-permute-done.1.refs_1_), channel_id=1, source_target_pairs={{0,8},{8,0},{1,9},{9,1},{2,10},{10,2},{3,11},{11,3},{4,12},{12,4},... | collective-permute-start | bytes 589832 | tf_op jit(solution)/shard_map/ppermute | solution.py:410
  30.3 1.4 %collective-permute-start.8 = (s32[384]{0:T(512)S(1)}, s32[384]{0:T(512)S(1)}, u32[]{:S(2)}, u32[]{:S(2)}) collective-permute-start(s32[384]{0:T(512)S(1)} %copy-done.2), channel_id=1, source_target_pairs={{0,128},{128,0},{1,129},{129,1},{2,130},{130,2},{3,131},{131,3},{4... | collective-permute-start | bytes 4616 | tf_op jit(solution)/shard_map/ppermute | solution.py:393
  31.6 4.0 %collective-permute-done.8.refs_10_ = s32[384]{0:T(512)S(1)} collective-permute-done((s32[384]{0:T(512)S(1)}, s32[384]{0:T(512)S(1)}, u32[]{:S(2)}, u32[]{:S(2)}) %collective-permute-start.8) | collective-permute-done | bytes 1568 | tf_op jit(solution)/shard_map/ppermute | solution.py:393
  35.6 3.3 %all-to-all-done = bf16[16,48,1024]{2,1,0:T(8,128)(2,1)S(1)} async-done(((bf16[16,48,1024]{2,1,0:T(8,128)(2,1)}), bf16[16,48,1024]{2,1,0:T(8,128)(2,1)S(1)}, u32[]{:S(2)}, u32[]{:S(2)}) %all-to-all-start) | async-done | bytes 1572896 | tf_op jit(solution)/shard_map/all_to_all | solution.py:402
  39.0 3.0 %scores.1 = (f32[1,768]{1,0:T(1,128)S(1)}, f32[768,768]{1,0:T(8,128)S(1)}, bf16[768,1024]{1,0:T(8,128)(2,1)S(1)}, f32[1,1024]{1,0:T(1,128)S(1)}, f32[1,1024]{1,0:T(1,128)S(1)}) custom-call(bf16[96,1024]{1,0:T(8,128)(2,1)S(1)} %join.1.refs_0_, bf16[96,1024]{1,0:T(8,128)(2,1)S(1)} %collective-permute-done.1.refs_1_, ...), custom_call_target="tpu_custom_call" | custom-call | flops 1207959552 | bytes 7092224 | tf_op jit(solution)/shard_map/scores/pallas_call | solution.py:104
  42.0 2.4 %collective-permute-start.9 = (f32[1,1024]{1,0:T(1,128)S(1)}, f32[1,1024]{1,0:T(1,128)S(1)}, u32[]{:S(2)}, u32[]{:S(2)}) collective-permute-start(f32[1,1024]{1,0:T(1,128)S(1)} %get-tuple-element.27), channel_id=1, source_target_pairs={{0,8},{8,0},{1,9},{9,1},{2,10},{10,2},{3,11},{11,3},{4,12},{12,4},... | collective-permute-start | bytes 12296 | tf_op jit(solution)/shard_map/ppermute | solution.py:428
  44.4 0.8 collective-permute-done.9.seen
  45.2 3.9 %collective-permute-start.12 = (f32[1,1792]{1,0:T(1,128)S(1)}, f32[1,1792]{1,0:T(1,128)S(1)}, u32[]{:S(2)}, u32[]{:S(2)}) collective-permute-start(f32[1,1792]{1,0:T(1,128)S(1)} %meet.1.mine), channel_id=1, source_target_pairs={{0,32},{1,33},{2,34},{3,35},{4,36},{5,37},{6,38},{7,39},{8,9},{9,8... | collective-permute-start | bytes 21512 | tf_op jit(solution)/shard_map/ppermute | solution.py:53
  49.2 0.2 collective-permute-start.11
  49.4 1.3 %collective-permute-start.10 = (f32[1,1792]{1,0:T(1,128)S(1)}, f32[1,1792]{1,0:T(1,128)S(1)}, u32[]{:S(2)}, u32[]{:S(2)}) collective-permute-start(f32[1,1792]{1,0:T(1,128)S(1)} %meet.1.mine), channel_id=1, source_target_pairs={{0,16},{1,17},{2,18},{3,19},{4,20},{5,21},{6,22},{7,23},{8,136},{9... | collective-permute-start | bytes 21512 | tf_op jit(solution)/shard_map/ppermute | solution.py:53
  50.7 1.0 collective-permute-done.11.two
  51.7 1.4 %collective-permute-done.10.one = f32[1,1792]{1,0:T(1,128)S(1)} collective-permute-done((f32[1,1792]{1,0:T(1,128)S(1)}, f32[1,1792]{1,0:T(1,128)S(1)}, u32[]{:S(2)}, u32[]{:S(2)}) %collective-permute-start.10) | collective-permute-done | bytes 7200 | tf_op jit(solution)/shard_map/ppermute | solution.py:53
  53.1 2.1 %collective-permute-start.15 = (f32[1,1792]{1,0:T(1,128)S(1)}, f32[1,1792]{1,0:T(1,128)S(1)}, u32[]{:S(2)}, u32[]{:S(2)}) collective-permute-start(f32[1,1792]{1,0:T(1,128)S(1)} %round.1.mine), channel_id=1, source_target_pairs={{8,12},{9,13},{10,14},{11,15},{12,8},{13,9},{14,10},{15,11},{24,28... | collective-permute-start | bytes 21512 | tf_op jit(solution)/shard_map/ppermute | solution.py:53
  55.3 3.5 %collective-permute-start.14 = (f32[1,1792]{1,0:T(1,128)S(1)}, f32[1,1792]{1,0:T(1,128)S(1)}, u32[]{:S(2)}, u32[]{:S(2)}) collective-permute-start(f32[1,1792]{1,0:T(1,128)S(1)} %round.1.mine), channel_id=1, source_target_pairs={{8,14},{9,15},{10,8},{11,9},{12,10},{13,11},{14,12},{15,13},{24,30... | collective-permute-start | bytes 21512 | tf_op jit(solution)/shard_map/ppermute | solution.py:53
  58.7 0.3 collective-permute-start.13
  59.0 0.6 collective-permute-done.14.two
  59.7 3.3 %collective-permute-done.13.one = f32[1,1792]{1,0:T(1,128)S(1)} collective-permute-done((f32[1,1792]{1,0:T(1,128)S(1)}, f32[1,1792]{1,0:T(1,128)S(1)}, u32[]{:S(2)}, u32[]{:S(2)}) %collective-permute-start.13) | collective-permute-done | bytes 7200 | tf_op jit(solution)/shard_map/ppermute | solution.py:53
  63.0 0.5 collective-permute-start.16
  63.5 0.8 collective-permute-done.16.refs_1_
  64.3 5.3 %grads.1 = (f32[8,128]{1,0:T(8,128)S(1)}, bf16[384,1024]{1,0:T(8,128)(2,1)S(1)}, bf16[400,1024]{1,0:T(8,128)(2,1)}, bf16[16,400,128]{2,1,0:T(8,128)(2,1)}) custom-call(f32[1,1792]{1,0:T(1,128)S(1)} %get-tuple-element.28.refs_0_, f32[1,1024]{1,0:T(1,128)S(1)} %collective-permute-done.16.refs_1_, f32[768,768]{1,0:T(8,128)S(1)} %get-tuple-element.30.refs_2_, ...), custom_call_target="tpu_custom_call" | custom-call | flops 2415919104 | bytes 8767488 | tf_op jit(solution)/shard_map/grads/pallas_call | solution.py:104
  69.7 0.4 collective-permute-start.17
  70.1 5.4 %all-to-all-start.1 = ((bf16[16,400,128]{2,1,0:T(8,128)(2,1)}), bf16[16,400,128]{2,1,0:T(8,128)(2,1)S(1)}, u32[]{:S(2)}, u32[]{:S(2)}) async-start(bf16[16,400,128]{2,1,0:T(8,128)(2,1)} %get-tuple-element.33), calls=%async_computation.1 | async-start | bytes 3276800 | tf_op jit(solution)/shard_map/all_to_all | solution.py:458
  75.5 1.1 %send.1 = (f32[96,1024]{1,0:T(8,128)S(1)}, f32[1,128]{1,0:T(1,128)S(1)}, bf16[784,128]{1,0:T(8,128)(2,1)S(1)}, bf16[784,128]{1,0:T(8,128)(2,1)S(1)}, bf16[784,128]{1,0:T(8,128)(2,1)S(1)}) custom-call(bf16[384,1024]{1,0:T(8,128)(2,1)S(1)} %get-tuple-element.35.own, bf16[400,1024]{1,0:T(8,128)(2,1)S(1)} %collective-permute-done.17.seen, ...), custom_call_target="tpu_custom_call" | custom-call | flops 10000000000 | bytes 1 | tf_op jit(solution)/shard_map/send/pallas_call | solution.py:104
  76.6 0.1 collective-permute-start.18
  76.7 0.1 collective-permute-start.19
  76.8 2.6 %collective-permute-start.20 = (bf16[784,128]{1,0:T(8,128)(2,1)S(1)}, bf16[784,128]{1,0:T(8,128)(2,1)S(1)}, u32[]{:S(2)}, u32[]{:S(2)}) collective-permute-start(bf16[784,128]{1,0:T(8,128)(2,1)S(1)} %get-tuple-element.41), channel_id=1, source_target_pairs={{0,112},{16,0},{32,16},{48,32},{64,48},{80,64},{96,80},{112,96},{1... | collective-permute-start | bytes 602120 | tf_op jit(solution)/shard_map/ppermute | solution.py:32
  79.4 8.9 %collective-permute-done.18.refs_0_ = bf16[784,128]{1,0:T(8,128)(2,1)S(1)} collective-permute-done((bf16[784,128]{1,0:T(8,128)(2,1)S(1)}, bf16[784,128]{1,0:T(8,128)(2,1)S(1)}, u32[]{:S(2)}, u32[]{:S(2)}) %collective-permute-start.18) | collective-permute-done | bytes 200736 | tf_op jit(solution)/shard_map/ppermute | solution.py:32
  88.3 1.0 collective-permute-done.20.refs_2_
  89.3 0.4 relay.1
  89.7 0.8 collective-permute-start.21
  90.5 7.5 %collective-permute-done.21.pay = bf16[400,128]{1,0:T(8,128)(2,1)S(1)} collective-permute-done((bf16[400,128]{1,0:T(8,128)(2,1)S(1)}, bf16[400,128]{1,0:T(8,128)(2,1)S(1)}, u32[]{:S(2)}, u32[]{:S(2)}) %collective-permute-start.21) | collective-permute-done | bytes 102432 | tf_op jit(solution)/shard_map/ppermute | solution.py:22
  98.1 0.8 text_sum.1
  98.8 3.1 %all-to-all-done.1.got = bf16[16,400,128]{2,1,0:T(8,128)(2,1)S(1)} async-done(((bf16[16,400,128]{2,1,0:T(8,128)(2,1)}), bf16[16,400,128]{2,1,0:T(8,128)(2,1)S(1)}, u32[]{:S(2)}, u32[]{:S(2)}) %all-to-all-start.1) | async-done | bytes 1638432 | tf_op jit(solution)/shard_map/all_to_all | solution.py:458
  101.9 1.7 %image_sum.1 = (f32[48,1024]{1,0:T(8,128)}, f32[1,1]{1,0:T(1,128)}) custom-call(bf16[16,400,128]{2,1,0:T(8,128)(2,1)S(1)} %all-to-all-done.1.got, f32[8,128]{1,0:T(8,128)S(1)} %get-tuple-element.34.terms, f32[1,128]{1,0:T(1,128)S(1)} %get-tuple-element.45.side), custom_call_target="tpu_custom_call" | custom-call | bytes 1839620 | tf_op jit(solution)/shard_map/image_sum/pallas_call | solution.py:104
  (17 shorter events, 0.1 us)
Async XLA Ops:
  0.6 17.0 %collective-permute-start = (bf16[48,1024]{1,0:T(8,128)(2,1)}, bf16[48,1024]{1,0:T(8,128)(2,1)S(1)}, u32[]{:S(2)}, u32[]{:S(2)}) collective-permute-start(bf16[48,1024]{1,0:T(8,128)(2,1)} %near.1), channel_id=1, source_target_pairs={{0,64},{16,80},{32,96},{48,112},{64,0},{80,16},{96,32},{112,48},{1... | collective-permute-start | bytes 294920 | tf_op jit(solution)/shard_map/ppermute | solution.py:22
  8.5 0.9 copy-start
  10.7 6.9 %copy-start.1 = (bf16[48,1024]{1,0:T(8,128)(2,1)S(1)}, bf16[48,1024]{1,0:T(8,128)(2,1)}, u32[]{:S(2)}) copy-start(bf16[48,1024]{1,0:T(8,128)(2,1)} %near.1) | copy-start | bytes 294916
  10.7 28.3 %all-to-all-start = ((bf16[16,48,1024]{2,1,0:T(8,128)(2,1)}), bf16[16,48,1024]{2,1,0:T(8,128)(2,1)S(1)}, u32[]{:S(2)}, u32[]{:S(2)}) async-start(bf16[16,48,1024]{2,1,0:T(8,128)(2,1)} %copies.1), calls=%async_computation | async-start | bytes 3145728 | tf_op jit(solution)/shard_map/all_to_all | solution.py:402
  17.6 12.7 %copy-start.2 = (s32[384]{0:T(512)S(1)}, s32[384]{0:T(512)}, u32[]{:S(2)}) copy-start(s32[384]{0:T(512)} %refs_9_.1) | copy-start | bytes 4612
  17.6 6.4 %collective-permute-start.3 = (bf16[96,1024]{1,0:T(8,128)(2,1)S(1)}, bf16[96,1024]{1,0:T(8,128)(2,1)S(1)}, u32[]{:S(2)}, u32[]{:S(2)}) collective-permute-start(bf16[96,1024]{1,0:T(8,128)(2,1)S(1)} %join.1.refs_0_), channel_id=1, source_target_pairs={{112,0},{0,16},{16,32},{32,48},{48,64},{64,80},{80,96},{96,112},{1... | collective-permute-start | bytes 589832 | tf_op jit(solution)/shard_map/ppermute | solution.py:32
  18.5 9.6 %collective-permute-start.2 = (bf16[96,1024]{1,0:T(8,128)(2,1)S(1)}, bf16[96,1024]{1,0:T(8,128)(2,1)S(1)}, u32[]{:S(2)}, u32[]{:S(2)}) collective-permute-start(bf16[96,1024]{1,0:T(8,128)(2,1)S(1)} %join.1.refs_0_), channel_id=1, source_target_pairs={{32,0},{112,16},{64,32},{16,48},{96,64},{48,80},{0,96},{80,112},{3... | collective-permute-start | bytes 589832 | tf_op jit(solution)/shard_map/ppermute | solution.py:32
  18.7 10.3 %collective-permute-start.1 = (bf16[96,1024]{1,0:T(8,128)(2,1)S(1)}, bf16[96,1024]{1,0:T(8,128)(2,1)S(1)}, u32[]{:S(2)}, u32[]{:S(2)}) collective-permute-start(bf16[96,1024]{1,0:T(8,128)(2,1)S(1)} %join.1.refs_0_), channel_id=1, source_target_pairs={{16,0},{32,16},{48,32},{64,48},{80,64},{96,80},{112,96},{0,112},{1... | collective-permute-start | bytes 589832 | tf_op jit(solution)/shard_map/ppermute | solution.py:32
  21.6 14.0 %collective-permute-start.4 = (bf16[96,1024]{1,0:T(8,128)(2,1)S(1)}, bf16[96,1024]{1,0:T(8,128)(2,1)S(1)}, u32[]{:S(2)}, u32[]{:S(2)}) collective-permute-start(bf16[96,1024]{1,0:T(8,128)(2,1)S(1)} %join.1.refs_0_), channel_id=1, source_target_pairs={{0,8},{8,0},{1,9},{9,1},{2,10},{10,2},{3,11},{11,3},{4,12},{12,4},... | collective-permute-start | bytes 589832 | tf_op jit(solution)/shard_map/ppermute | solution.py:410
  24.1 11.5 %collective-permute-start.7 = (bf16[96,1024]{1,0:T(8,128)(2,1)S(1)}, bf16[96,1024]{1,0:T(8,128)(2,1)S(1)}, u32[]{:S(2)}, u32[]{:S(2)}) collective-permute-start(bf16[96,1024]{1,0:T(8,128)(2,1)S(1)} %collective-permute-done.3.refs_3_), channel_id=1, source_target_pairs={{0,8},{8,0},{1,9},{9,1},{2,10},{10,2},{3,11},{11,3},{4,12},{12,4},... | collective-permute-start | bytes 589832 | tf_op jit(solution)/shard_map/ppermute | solution.py:410
  28.0 7.6 %collective-permute-start.6 = (bf16[96,1024]{1,0:T(8,128)(2,1)S(1)}, bf16[96,1024]{1,0:T(8,128)(2,1)S(1)}, u32[]{:S(2)}, u32[]{:S(2)}) collective-permute-start(bf16[96,1024]{1,0:T(8,128)(2,1)S(1)} %collective-permute-done.2.refs_2_), channel_id=1, source_target_pairs={{0,8},{8,0},{1,9},{9,1},{2,10},{10,2},{3,11},{11,3},{4,12},{12,4},... | collective-permute-start | bytes 589832 | tf_op jit(solution)/shard_map/ppermute | solution.py:410
  29.1 6.5 %collective-permute-start.5 = (bf16[96,1024]{1,0:T(8,128)(2,1)S(1)}, bf16[96,1024]{1,0:T(8,128)(2,1)S(1)}, u32[]{:S(2)}, u32[]{:S(2)}) collective-permute-start(bf16[96,1024]{1,0:T(8,128)(2,1)S(1)} %collective-permute-done.1.refs_1_), channel_id=1, source_target_pairs={{0,8},{8,0},{1,9},{9,1},{2,10},{10,2},{3,11},{11,3},{4,12},{12,4},... | collective-permute-start | bytes 589832 | tf_op jit(solution)/shard_map/ppermute | solution.py:410
  30.3 5.3 %collective-permute-start.8 = (s32[384]{0:T(512)S(1)}, s32[384]{0:T(512)S(1)}, u32[]{:S(2)}, u32[]{:S(2)}) collective-permute-start(s32[384]{0:T(512)S(1)} %copy-done.2), channel_id=1, source_target_pairs={{0,128},{128,0},{1,129},{129,1},{2,130},{130,2},{3,131},{131,3},{4... | collective-permute-start | bytes 4616 | tf_op jit(solution)/shard_map/ppermute | solution.py:393
  42.0 3.2 %collective-permute-start.9 = (f32[1,1024]{1,0:T(1,128)S(1)}, f32[1,1024]{1,0:T(1,128)S(1)}, u32[]{:S(2)}, u32[]{:S(2)}) collective-permute-start(f32[1,1024]{1,0:T(1,128)S(1)} %get-tuple-element.27), channel_id=1, source_target_pairs={{0,8},{8,0},{1,9},{9,1},{2,10},{10,2},{3,11},{11,3},{4,12},{12,4},... | collective-permute-start | bytes 12296 | tf_op jit(solution)/shard_map/ppermute | solution.py:428
  45.2 5.4 %collective-permute-start.12 = (f32[1,1792]{1,0:T(1,128)S(1)}, f32[1,1792]{1,0:T(1,128)S(1)}, u32[]{:S(2)}, u32[]{:S(2)}) collective-permute-start(f32[1,1792]{1,0:T(1,128)S(1)} %meet.1.mine), channel_id=1, source_target_pairs={{0,32},{1,33},{2,34},{3,35},{4,36},{5,37},{6,38},{7,39},{8,9},{9,8... | collective-permute-start | bytes 21512 | tf_op jit(solution)/shard_map/ppermute | solution.py:53
  49.2 2.5 %collective-permute-start.11 = (f32[1,1792]{1,0:T(1,128)S(1)}, f32[1,1792]{1,0:T(1,128)S(1)}, u32[]{:S(2)}, u32[]{:S(2)}) collective-permute-start(f32[1,1792]{1,0:T(1,128)S(1)} %meet.1.mine), channel_id=1, source_target_pairs={{0,112},{1,113},{2,114},{3,115},{4,116},{5,117},{6,118},{7,119},{8... | collective-permute-start | bytes 21512 | tf_op jit(solution)/shard_map/ppermute | solution.py:53
  49.4 3.7 %collective-permute-start.10 = (f32[1,1792]{1,0:T(1,128)S(1)}, f32[1,1792]{1,0:T(1,128)S(1)}, u32[]{:S(2)}, u32[]{:S(2)}) collective-permute-start(f32[1,1792]{1,0:T(1,128)S(1)} %meet.1.mine), channel_id=1, source_target_pairs={{0,16},{1,17},{2,18},{3,19},{4,20},{5,21},{6,22},{7,23},{8,136},{9... | collective-permute-start | bytes 21512 | tf_op jit(solution)/shard_map/ppermute | solution.py:53
  53.1 5.9 %collective-permute-start.15 = (f32[1,1792]{1,0:T(1,128)S(1)}, f32[1,1792]{1,0:T(1,128)S(1)}, u32[]{:S(2)}, u32[]{:S(2)}) collective-permute-start(f32[1,1792]{1,0:T(1,128)S(1)} %round.1.mine), channel_id=1, source_target_pairs={{8,12},{9,13},{10,14},{11,15},{12,8},{13,9},{14,10},{15,11},{24,28... | collective-permute-start | bytes 21512 | tf_op jit(solution)/shard_map/ppermute | solution.py:53
  55.3 4.4 %collective-permute-start.14 = (f32[1,1792]{1,0:T(1,128)S(1)}, f32[1,1792]{1,0:T(1,128)S(1)}, u32[]{:S(2)}, u32[]{:S(2)}) collective-permute-start(f32[1,1792]{1,0:T(1,128)S(1)} %round.1.mine), channel_id=1, source_target_pairs={{8,14},{9,15},{10,8},{11,9},{12,10},{13,11},{14,12},{15,13},{24,30... | collective-permute-start | bytes 21512 | tf_op jit(solution)/shard_map/ppermute | solution.py:53
  58.7 4.3 %collective-permute-start.13 = (f32[1,1792]{1,0:T(1,128)S(1)}, f32[1,1792]{1,0:T(1,128)S(1)}, u32[]{:S(2)}, u32[]{:S(2)}) collective-permute-start(f32[1,1792]{1,0:T(1,128)S(1)} %round.1.mine), channel_id=1, source_target_pairs={{0,64},{1,65},{2,66},{3,67},{4,68},{5,69},{6,70},{7,71},{8,10},{9,... | collective-permute-start | bytes 21512 | tf_op jit(solution)/shard_map/ppermute | solution.py:53
  63.0 1.3 %collective-permute-start.16 = (f32[1,1024]{1,0:T(1,128)S(1)}, f32[1,1024]{1,0:T(1,128)S(1)}, u32[]{:S(2)}, u32[]{:S(2)}) collective-permute-start(f32[1,1024]{1,0:T(1,128)S(1)} %get-tuple-element.29), channel_id=1, source_target_pairs={{0,8},{8,0},{1,9},{9,1},{2,10},{10,2},{3,11},{11,3},{4,12},{12,4},... | collective-permute-start | bytes 12296 | tf_op jit(solution)/shard_map/ppermute | solution.py:436
  69.7 5.8 %collective-permute-start.17 = (bf16[400,1024]{1,0:T(8,128)(2,1)}, bf16[400,1024]{1,0:T(8,128)(2,1)S(1)}, u32[]{:S(2)}, u32[]{:S(2)}) collective-permute-start(bf16[400,1024]{1,0:T(8,128)(2,1)} %get-tuple-element.36), channel_id=1, source_target_pairs={{0,8},{8,0},{1,9},{9,1},{2,10},{10,2},{3,11},{11,3},{4,12},{12,4},... | collective-permute-start | bytes 2457608 | tf_op jit(solution)/shard_map/ppermute | solution.py:463
  70.1 31.8 %all-to-all-start.1 = ((bf16[16,400,128]{2,1,0:T(8,128)(2,1)}), bf16[16,400,128]{2,1,0:T(8,128)(2,1)S(1)}, u32[]{:S(2)}, u32[]{:S(2)}) async-start(bf16[16,400,128]{2,1,0:T(8,128)(2,1)} %get-tuple-element.33), calls=%async_computation.1 | async-start | bytes 3276800 | tf_op jit(solution)/shard_map/all_to_all | solution.py:458
  76.6 11.7 %collective-permute-start.18 = (bf16[784,128]{1,0:T(8,128)(2,1)S(1)}, bf16[784,128]{1,0:T(8,128)(2,1)S(1)}, u32[]{:S(2)}, u32[]{:S(2)}) collective-permute-start(bf16[784,128]{1,0:T(8,128)(2,1)S(1)} %get-tuple-element.39), channel_id=1, source_target_pairs={{0,16},{16,32},{32,48},{48,64},{64,80},{80,96},{96,112},{112,0},{1... | collective-permute-start | bytes 602120 | tf_op jit(solution)/shard_map/ppermute | solution.py:32
  76.7 11.6 %collective-permute-start.19 = (bf16[784,128]{1,0:T(8,128)(2,1)S(1)}, bf16[784,128]{1,0:T(8,128)(2,1)S(1)}, u32[]{:S(2)}, u32[]{:S(2)}) collective-permute-start(bf16[784,128]{1,0:T(8,128)(2,1)S(1)} %get-tuple-element.40), channel_id=1, source_target_pairs={{0,32},{16,112},{32,64},{48,16},{64,96},{80,48},{96,0},{112,80},{1... | collective-permute-start | bytes 602120 | tf_op jit(solution)/shard_map/ppermute | solution.py:32
  76.8 12.5 %collective-permute-start.20 = (bf16[784,128]{1,0:T(8,128)(2,1)S(1)}, bf16[784,128]{1,0:T(8,128)(2,1)S(1)}, u32[]{:S(2)}, u32[]{:S(2)}) collective-permute-start(bf16[784,128]{1,0:T(8,128)(2,1)S(1)} %get-tuple-element.41), channel_id=1, source_target_pairs={{0,112},{16,0},{32,16},{48,32},{64,48},{80,64},{96,80},{112,96},{1... | collective-permute-start | bytes 602120 | tf_op jit(solution)/shard_map/ppermute | solution.py:32
  89.7 8.4 %collective-permute-start.21 = (bf16[400,128]{1,0:T(8,128)(2,1)S(1)}, bf16[400,128]{1,0:T(8,128)(2,1)S(1)}, u32[]{:S(2)}, u32[]{:S(2)}) collective-permute-start(bf16[400,128]{1,0:T(8,128)(2,1)S(1)} %get-tuple-element.44), channel_id=1, source_target_pairs={{0,64},{16,80},{32,96},{48,112},{64,0},{80,16},{96,32},{112,48},{1... | collective-permute-start | bytes 307208 | tf_op jit(solution)/shard_map/ppermute | solution.py:22

commit v13 on v12

--- a/solution.py
+++ b/solution.py
@@ -237,13 +237,12 @@
     return (ids + within - holder * rows).astype(F32)
 
 
-def grad_body(n_z, inv_root, *refs):
-    mine, seen, scores, text, image, pair = refs[:6]
-    terms, own, other, sent, grads, held, crossing, sems = refs[6:]
-    size = grads.shape[0]
-    half = own.shape[0]
-    rows = half // n_z
-    _, tall, _ = sent.shape
+def image_body(n_z, inv_root, *refs):
+    mine, seen, scores, text, pair = refs[:5]
+    terms, grads, sent, kept, held, sems = refs[5:]
+    size = scores.shape[0]
+    n_plane, tall, _ = sent.shape
+    rows = size // n_plane
     ids = labels(n_z, rows)
     first = lax.axis_index("c") == 0
     seen_lse, seen_high = seen[:, :size], seen[:, size : size + LANES]
@@ -265,11 +264,15 @@
     step = size // 4
     copies = []
     for r in range(0, size, step):
-        at = slice(r, r + step)
+        at = pl.ds(r, step)
         tile = scores[at, :]
-        probs = 0.5 * (jnp.exp(tile - row_column[at, :]) + jnp.exp(tile - col_lse))
-        grad = (probs - jnp.where(pair_column[at, :] == ids, 1.0, 0.0)).astype(BF16)
-        grads[at, :] = grad
+        probs = 0.5 * (jnp.exp(tile - row_column[r : r + step, :]) + jnp.exp(tile - col_lse))
+        hit = pair_column[r : r + step, :] == ids
+        grad = (probs - jnp.where(hit, 1.0, 0.0)).astype(BF16)
+        kept[at, :] = grad
+        sem = sems.at[n_plane + r // step]
+        copies.append(pltpu.make_async_copy(kept.at[at], grads.at[at], sem))
+        copies[-1].start()
         part = encode(jnp.dot(grad, text[...], preferred_element_type=F32) * scale)
         for p in range(step // rows):
             to = r // rows + p
@@ -280,24 +283,21 @@
             held[to, tall - EXTRA :, :] = extra
             copies.append(pltpu.make_async_copy(held.at[to], sent.at[to], sems.at[to]))
             copies[-1].start()
-    scale = inverse(image_max[:, :1]) * inv_root
-    extra = split3(row_terms)
-    crossing[half:, :] = jnp.concatenate([extra] * (own.shape[1] // LANES), axis=1)
-    for start in (half, 0):
+    for copy in copies:
+        copy.wait()
+
+
+def text_body(inv_root, grads, image, terms, terms_seen, own, other):
+    half = own.shape[0]
+    scale = inverse(terms_seen[2:3, :1]) * inv_root
+    for out, start in ((other, half), (own, 0)):
         part = lax.dot_general(
             grads[:, start : start + half],
             image[...],
             (((0,), (0,)), ((), ())),
             preferred_element_type=F32,
         )
-        if start == 0:
-            own[...] = encode(part * scale)
-        else:
-            crossing[:half, :] = encode(part * scale)
-            copies.append(pltpu.make_async_copy(crossing, other, sems.at[sent.shape[0]]))
-            copies[-1].start()
-    for copy in copies:
-        copy.wait()
+        out[:half, :] = encode(part * scale) if out.dtype == BF16 else part * scale
 
 
 def pack(pay, blocks, extra):
@@ -311,27 +311,19 @@
     pay[at:, :] = extra
 
 
-def send_body(steps, own, seen, terms, keep, total, *pays):
-    n_z = 2 * len(steps)
-    rows = keep.shape[0] // 2
-    z = lax.axis_index("z")
-    half = own.shape[0]
-    tail = seen[half:, :LANES].astype(F32)
-    row_terms = terms[0:1, :] + jnp.sum(tail, axis=0, keepdims=True)
+def place(step, n_z, rows):
+    slot = lax.rem(lax.axis_index("z") + step + n_z, n_z)
+    return pl.ds(pl.multiple_of(slot * rows, 16), rows)
+
+
+def send_body(n_z, own, seen, terms, terms_seen, sums, total, *pays):
+    rows = own.shape[0] // n_z
+    row_terms = terms[0:1, :] + terms_seen[0:1, :]
     total[...] = row_terms
     extra = split3(row_terms)
-    for i, q in enumerate(steps):
-        blocks = []
-        for k in range(2):
-            to = lax.rem(z + lean(q, z, n_z) + (k + 2) * n_z // 2, n_z)
-            start = to * rows
-            at = pl.ds(pl.multiple_of(start, 16), rows)
-            blocks.append(decode(own[at, :]) + decode(seen[at, :]))
-        if i == 0:
-            keep[:rows, :] = blocks[0]
-            keep[rows:, :] = blocks[1]
-        else:
-            pack(pays[i - 1], blocks, extra)
+    sums[...] = own[...] + decode(seen[...])
+    for pay, step in zip(pays, (n_z // 2, 1 - n_z // 2)):
+        pack(pay, [sums[place(step, n_z, rows), :]], extra)
 
 
 def unpack(pays, at, rows, width):
@@ -349,22 +341,22 @@
     return jnp.sum(tail, axis=0, keepdims=True)
 
 
-def relay_body(keep, total, *refs):
-    pays, near, far, total_out = refs[:-3], refs[-3], refs[-2], refs[-1]
-    rows, width = near.shape
-    near[...] = keep[:rows, :] + unpack(pays, 0, rows, width)
-    sums = total[...] + tails(pays)
-    total_out[...] = sums
-    block = keep[rows:, :] + unpack(pays, rows * width // LANES, rows, width)
-    pack(far, [block], split3(sums))
-
-
-def text_sum_body(near, total, terms, pay, out, side):
+def relay_body(steps, sums, total, *refs):
+    n_z = 2 * steps[0][1]
+    rows, width = sums.shape[0] // n_z, sums.shape[1]
+    count = len(refs) // 2
+    for pay, out, (step, _) in zip(refs[:count], refs[count:], steps):
+        block = sums[place(step, n_z, rows), :] + unpack([pay], 0, rows, width)
+        pack(out, [block], split3(total[...] + tails([pay])))
+
+
+def text_sum_body(sums, total, terms, up, down, out, side):
     rows, width = out.shape
+    n_z = sums.shape[0] // rows
     unit = terms[2:3, :1]
     unit = jnp.where(unit > 0, unit, 1.0)
-    out[...] = unit * (near[...] + unpack([pay], 0, rows, width))
-    side[...] = total[...] + tails([pay])
+    out[...] = unit * (sums[place(0, n_z, rows), :] + unpack([up, down], 0, rows, width))
+    side[...] = total[...] + tails([up, down])
 
 
 def image_sum_body(pairs, got, terms, side, out, loss):
@@ -435,48 +427,59 @@
     )
     seen = lax.ppermute(cross, "c", SWAP)
 
-    terms, text_own, text_other, image_sent = call(
-        functools.partial(grad_body, n_z, inv_root),
+    terms, grads, image_sent = call(
+        functools.partial(image_body, n_z, inv_root),
         (
             shape((8, LANES), F32),
-            shape((half, width), BF16),
-            pltpu.HBM((half + EXTRA, width), BF16),
+            pltpu.HBM((size, size), BF16),
             pltpu.HBM((n_plane, tall, LANES), BF16),
         ),
-        (stats, seen, scores, text, image, pair),
-        "grads",
-        2 * flops,
+        (stats, seen, scores, text, pair),
+        "image_grad",
+        flops,
         2 * size * size,
-        hbm_out=(2, 3),
+        hbm_out=(1, 2),
         scratch=[
             pltpu.VMEM((size, size), BF16),
             pltpu.VMEM((n_plane, tall, LANES), BF16),
-            pltpu.VMEM((half + EXTRA, width), BF16),
-            pltpu.SemaphoreType.DMA((n_plane + 1,)),
+            pltpu.SemaphoreType.DMA((n_plane + 4,)),
         ],
     )
     image_got = lax.all_to_all(image_sent, PLANE, 0, 0)
-    keep, total, *pays = call(
-        functools.partial(send_body, steps),
-        (shape((2 * rows, width), F32), shape((1, LANES), F32))
-        + (shape((2 * tall - EXTRA, LANES), BF16),) * len(steps[1:]),
-        (text_own, lax.ppermute(text_other, "c", SWAP), terms),
+    terms_seen = lax.ppermute(terms, "c", SWAP)
+    text_own, text_other = call(
+        functools.partial(text_body, inv_root),
+        (shape((half, width), F32), shape((half, width), BF16)),
+        (grads, image, terms, terms_seen),
+        "text_grad",
+        10**11,
+        size=1,
+    )
+    pay_shape = shape((tall, LANES), BF16)
+    sums, total, up, down = call(
+        functools.partial(send_body, n_z),
+        (shape((half, width), F32), shape((1, LANES), F32), pay_shape, pay_shape),
+        (text_own, lax.ppermute(text_other, "c", SWAP), terms, terms_seen),
         "send",
-        10**10,
         size=1,
     )
-    pays = [turn_z(pay, q, False) for q, pay in zip(steps[1:], pays)]
-    near, far, total = call(
-        relay_body,
-        (shape((rows, width), F32), shape((tall, LANES), BF16), shape((1, LANES), F32)),
-        (keep, total, *pays),
-        "relay",
-        size=1,
-    )
+    up, down = turn(up, "z", 1), turn(down, "z", -1)
+    for left in range(n_z // 2 - 1, 0, -1):
+        hops = [(left, n_z // 2), (1 - left, n_z // 2)][: 2 if left > 1 else 1]
+        moved = call(
+            functools.partial(relay_body, hops),
+            (pay_shape,) * len(hops),
+            (sums, total, up, down)[: 2 + len(hops)],
+            "relay",
+            size=1,
+        )
+        up = turn(moved[0], "z", 1)
+        if left > 1:
+            down = turn(moved[1], "z", -1)
     grad_text, side = call(
         text_sum_body,
         (shape((rows, width), F32), shape((1, LANES), F32)),
-        (near, total, terms, turn(far, "z", n_z // 2)),
+        (sums, total, terms, up, down),
         "text_sum",
         size=1,
     )

time: 104 us -> 107 us (1.029)
  the two profiles are of different devices: /device:TPU:1 before, /device:TPU:2 now
where the time goes in v13:
time: 107 us; the launch traced here: 106 us
  waiting for transfers between devices  47 us (44%)
  starting transfers between devices  42.8 us (40%)
  Pallas kernels  13.5 us (13%)
  local copies, waits for them, and re-layouts  2.17 us (2%)
    ppermute x8, starting transfers between devices, turn(): lax.ppermute(x, axis, [(i, (i + step) % count) for i in range(count)])  17.4 us
    ppermute x8, waiting for transfers between devices, turn(): lax.ppermute(x, axis, [(i, (i + step) % count) for i in range(count)])  13.9 us
    pallas_call x14, Pallas kernels, call(): pl.pallas_call(body, out_shape=outs, in_specs=[pl.BlockSpec(memory_space=...  13.5 us
    ppermute x6, waiting for transfers between devices, turn_both(): return lax.ppermute(x, AXES, pairs)  11.4 us
    all_to_all x1, starting transfers between devices, shards(): image = lax.all_to_all(copies, PLANE, 0, 0).reshape(size, width)  7.62 us
    ppermute x1, waiting for transfers between devices, shards(): pair_seen = lax.ppermute(pair_index, 'xl', SWAP)  6.71 us
    ppermute x6, starting transfers between devices, turn_both(): return lax.ppermute(x, AXES, pairs)  6.34 us
    ppermute x3, waiting for transfers between devices, turn_z(): return lax.ppermute(x, 'z', pairs if back else [(b, a) for a, b in pairs])  6.3 us
  transfers between devices with their start and end apart: 28, of which 15 were waited for; matrix products, arithmetic and copies ran while one was open for 0% of the time, Pallas kernels for 4%

profile of v13, /device:TPU:2, one launch (start us, length us, event | category | flops | bytes accessed | tf_op | source)
XLA Modules:
  0.0 106.5 jit_solution(507540346807647033)
XLA Ops:
  0.6 7.3 %collective-permute-start = (bf16[48,1024]{1,0:T(8,128)(2,1)}, bf16[48,1024]{1,0:T(8,128)(2,1)S(1)}, u32[]{:S(2)}, u32[]{:S(2)}) collective-permute-start(bf16[48,1024]{1,0:T(8,128)(2,1)} %near.1), channel_id=1, source_target_pairs={{0,64},{16,80},{32,96},{48,112},{64,0},{80,16},{96,32},{112,48},{1... | collective-permute-start | bytes 294920 | tf_op jit(solution)/shard_map/ppermute | solution.py:22
  7.9 0.9 copy-done
  8.8 1.3 %copies.1 = bf16[16,48,1024]{2,1,0:T(8,128)(2,1)} custom-call(bf16[48,1024]{1,0:T(8,128)(2,1)S(1)} %copy-done), custom_call_target="tpu_custom_call" | custom-call | bytes 1671168 | tf_op jit(solution)/shard_map/copies/pallas_call | solution.py:104
  10.1 7.6 %all-to-all-start = ((bf16[16,48,1024]{2,1,0:T(8,128)(2,1)}), bf16[16,48,1024]{2,1,0:T(8,128)(2,1)S(1)}, u32[]{:S(2)}, u32[]{:S(2)}) async-start(bf16[16,48,1024]{2,1,0:T(8,128)(2,1)} %copies.1), calls=%async_computation | async-start | bytes 3145728 | tf_op jit(solution)/shard_map/all_to_all | solution.py:394
  17.8 1.1 %collective-permute-start.3 = (bf16[96,1024]{1,0:T(8,128)(2,1)S(1)}, bf16[96,1024]{1,0:T(8,128)(2,1)S(1)}, u32[]{:S(2)}, u32[]{:S(2)}) collective-permute-start(bf16[96,1024]{1,0:T(8,128)(2,1)S(1)} %join.1.refs_0_), channel_id=1, source_target_pairs={{112,0},{0,16},{16,32},{32,48},{48,64},{64,80},{80,96},{96,112},{1... | collective-permute-start | bytes 589832 | tf_op jit(solution)/shard_map/ppermute | solution.py:32
  18.9 0.6 collective-permute-start.2
  19.5 3.1 %collective-permute-start.1 = (bf16[96,1024]{1,0:T(8,128)(2,1)S(1)}, bf16[96,1024]{1,0:T(8,128)(2,1)S(1)}, u32[]{:S(2)}, u32[]{:S(2)}) collective-permute-start(bf16[96,1024]{1,0:T(8,128)(2,1)S(1)} %join.1.refs_0_), channel_id=1, source_target_pairs={{16,0},{32,16},{48,32},{64,48},{80,64},{96,80},{112,96},{0,112},{1... | collective-permute-start | bytes 589832 | tf_op jit(solution)/shard_map/ppermute | solution.py:32
  22.6 4.3 %collective-permute-done.3.refs_3_ = bf16[96,1024]{1,0:T(8,128)(2,1)S(1)} collective-permute-done((bf16[96,1024]{1,0:T(8,128)(2,1)S(1)}, bf16[96,1024]{1,0:T(8,128)(2,1)S(1)}, u32[]{:S(2)}, u32[]{:S(2)}) %collective-permute-start.3) | collective-permute-done | bytes 196640 | tf_op jit(solution)/shard_map/ppermute | solution.py:32
  26.9 0.6 collective-permute-done.2.refs_2_
  27.5 1.4 %collective-permute-done.1.refs_1_ = bf16[96,1024]{1,0:T(8,128)(2,1)S(1)} collective-permute-done((bf16[96,1024]{1,0:T(8,128)(2,1)S(1)}, bf16[96,1024]{1,0:T(8,128)(2,1)S(1)}, u32[]{:S(2)}, u32[]{:S(2)}) %collective-permute-start.1) | collective-permute-done | bytes 196640 | tf_op jit(solution)/shard_map/ppermute | solution.py:32
  28.9 0.4 collective-permute-start.8
  29.3 6.7 %collective-permute-done.8.refs_10_ = s32[384]{0:T(512)S(1)} collective-permute-done((s32[384]{0:T(512)S(1)}, s32[384]{0:T(512)S(1)}, u32[]{:S(2)}, u32[]{:S(2)}) %collective-permute-start.8) | collective-permute-done | bytes 1568 | tf_op jit(solution)/shard_map/ppermute | solution.py:385
  36.0 4.1 %all-to-all-done = bf16[16,48,1024]{2,1,0:T(8,128)(2,1)S(1)} async-done(((bf16[16,48,1024]{2,1,0:T(8,128)(2,1)}), bf16[16,48,1024]{2,1,0:T(8,128)(2,1)S(1)}, u32[]{:S(2)}, u32[]{:S(2)}) %all-to-all-start) | async-done | bytes 1572896 | tf_op jit(solution)/shard_map/all_to_all | solution.py:394
  40.2 3.0 %scores.1 = (f32[1,768]{1,0:T(1,128)S(1)}, f32[768,768]{1,0:T(8,128)S(1)}, bf16[768,1024]{1,0:T(8,128)(2,1)S(1)}, f32[1,1024]{1,0:T(1,128)S(1)}, f32[1,1024]{1,0:T(1,128)S(1)}) custom-call(bf16[96,1024]{1,0:T(8,128)(2,1)S(1)} %join.1.refs_0_, bf16[96,1024]{1,0:T(8,128)(2,1)S(1)} %collective-permute-done.1.refs_1_, ...), custom_call_target="tpu_custom_call" | custom-call | flops 1207959552 | bytes 7092224 | tf_op jit(solution)/shard_map/scores/pallas_call | solution.py:104
  43.2 0.1 collective-permute-start.9
  43.3 1.2 %collective-permute-done.9.seen = f32[1,1024]{1,0:T(1,128)S(1)} collective-permute-done((f32[1,1024]{1,0:T(1,128)S(1)}, f32[1,1024]{1,0:T(1,128)S(1)}, u32[]{:S(2)}, u32[]{:S(2)}) %collective-permute-start.9) | collective-permute-done | bytes 4128 | tf_op jit(solution)/shard_map/ppermute | solution.py:420
  44.5 1.5 %collective-permute-start.12 = (f32[1,1792]{1,0:T(1,128)S(1)}, f32[1,1792]{1,0:T(1,128)S(1)}, u32[]{:S(2)}, u32[]{:S(2)}) collective-permute-start(f32[1,1792]{1,0:T(1,128)S(1)} %meet.1.mine), channel_id=1, source_target_pairs={{0,32},{1,33},{2,34},{3,35},{4,36},{5,37},{6,38},{7,39},{8,9},{9,8... | collective-permute-start | bytes 21512 | tf_op jit(solution)/shard_map/ppermute | solution.py:53
  46.0 2.2 %collective-permute-start.11 = (f32[1,1792]{1,0:T(1,128)S(1)}, f32[1,1792]{1,0:T(1,128)S(1)}, u32[]{:S(2)}, u32[]{:S(2)}) collective-permute-start(f32[1,1792]{1,0:T(1,128)S(1)} %meet.1.mine), channel_id=1, source_target_pairs={{0,112},{1,113},{2,114},{3,115},{4,116},{5,117},{6,118},{7,119},{8... | collective-permute-start | bytes 21512 | tf_op jit(solution)/shard_map/ppermute | solution.py:53
  48.2 2.1 %collective-permute-done.12.three = f32[1,1792]{1,0:T(1,128)S(1)} collective-permute-done((f32[1,1792]{1,0:T(1,128)S(1)}, f32[1,1792]{1,0:T(1,128)S(1)}, u32[]{:S(2)}, u32[]{:S(2)}) %collective-permute-start.12) | collective-permute-done | bytes 7200 | tf_op jit(solution)/shard_map/ppermute | solution.py:53
  50.3 2.8 %collective-permute-done.10.one = f32[1,1792]{1,0:T(1,128)S(1)} collective-permute-done((f32[1,1792]{1,0:T(1,128)S(1)}, f32[1,1792]{1,0:T(1,128)S(1)}, u32[]{:S(2)}, u32[]{:S(2)}) %collective-permute-start.10) | collective-permute-done | bytes 7200 | tf_op jit(solution)/shard_map/ppermute | solution.py:53
  53.1 0.7 collective-permute-start.15
  53.8 0.7 collective-permute-start.14
  54.5 1.3 %collective-permute-start.13 = (f32[1,1792]{1,0:T(1,128)S(1)}, f32[1,1792]{1,0:T(1,128)S(1)}, u32[]{:S(2)}, u32[]{:S(2)}) collective-permute-start(f32[1,1792]{1,0:T(1,128)S(1)} %round.1.mine), channel_id=1, source_target_pairs={{0,64},{1,65},{2,66},{3,67},{4,68},{5,69},{6,70},{7,71},{8,10},{9,... | collective-permute-start | bytes 21512 | tf_op jit(solution)/shard_map/ppermute | solution.py:53
  55.7 6.5 %collective-permute-done.13.one = f32[1,1792]{1,0:T(1,128)S(1)} collective-permute-done((f32[1,1792]{1,0:T(1,128)S(1)}, f32[1,1792]{1,0:T(1,128)S(1)}, u32[]{:S(2)}, u32[]{:S(2)}) %collective-permute-start.13) | collective-permute-done | bytes 7200 | tf_op jit(solution)/shard_map/ppermute | solution.py:53
  62.3 0.1 collective-permute-start.16
  62.4 1.2 %collective-permute-done.16.refs_1_ = f32[1,1024]{1,0:T(1,128)S(1)} collective-permute-done((f32[1,1024]{1,0:T(1,128)S(1)}, f32[1,1024]{1,0:T(1,128)S(1)}, u32[]{:S(2)}, u32[]{:S(2)}) %collective-permute-start.16) | collective-permute-done | bytes 4128 | tf_op jit(solution)/shard_map/ppermute | solution.py:428
  63.6 3.4 %image_grad.1 = (f32[8,128]{1,0:T(8,128)S(1)}, bf16[768,768]{1,0:T(8,128)(2,1)}, bf16[16,400,128]{2,1,0:T(8,128)(2,1)}) custom-call(f32[1,1792]{1,0:T(1,128)S(1)} %get-tuple-element.29.refs_0_, f32[1,1024]{1,0:T(1,128)S(1)} %collective-permute-done.16.refs_1_, f32[768,768]{1,0:T(8,128)S(1)} %get-tuple-element.31.refs_2_, ...), custom_call_target="tpu_custom_call" | custom-call | flops 1207959552 | bytes 6768640 | tf_op jit(solution)/shard_map/image_grad/pallas_call | solution.py:104
  66.9 0.2 collective-permute-start.17
  67.2 5.7 %all-to-all-start.1 = ((bf16[16,400,128]{2,1,0:T(8,128)(2,1)}), bf16[16,400,128]{2,1,0:T(8,128)(2,1)S(1)}, u32[]{:S(2)}, u32[]{:S(2)}) async-start(bf16[16,400,128]{2,1,0:T(8,128)(2,1)} %get-tuple-element.34), calls=%async_computation.1 | async-start | bytes 3276800 | tf_op jit(solution)/shard_map/all_to_all | solution.py:448
  72.9 1.3 %copy-done.3 = bf16[768,768]{1,0:T(8,128)(2,1)S(1)} copy-done((bf16[768,768]{1,0:T(8,128)(2,1)S(1)}, bf16[768,768]{1,0:T(8,128)(2,1)}, u32[]{:S(2)}) %copy-start.3) | copy-done | bytes 1179672
  74.2 1.6 %text_grad.1 = (f32[384,1024]{1,0:T(8,128)S(1)}, bf16[384,1024]{1,0:T(8,128)(2,1)S(1)}) custom-call(bf16[768,768]{1,0:T(8,128)(2,1)S(1)} %copy-done.3, bf16[768,1024]{1,0:T(8,128)(2,1)S(1)} %bitcast.3, f32[8,128]{1,0:T(8,128)S(1)} %get-tuple-element.35.terms, f32[8,128]{1,0:T(8,128)S(1)} %collective-permute-done.17.terms_seen), custom_call_target="tpu_custom_call" | custom-call | flops 99999997952 | bytes 1 | tf_op jit(solution)/shard_map/text_grad/pallas_call | solution.py:104
  75.8 0.1 collective-permute-start.18
  75.9 2.3 %collective-permute-done.18.seen = bf16[384,1024]{1,0:T(8,128)(2,1)S(1)} collective-permute-done((bf16[384,1024]{1,0:T(8,128)(2,1)S(1)}, bf16[384,1024]{1,0:T(8,128)(2,1)S(1)}, u32[]{:S(2)}, u32[]{:S(2)}) %collective-permute-start.18) | collective-permute-done | bytes 786464 | tf_op jit(solution)/shard_map/ppermute | solution.py:462
  78.1 1.1 send.1
  79.2 0.1 collective-permute-start.19
  79.3 3.2 %collective-permute-start.20 = (bf16[400,128]{1,0:T(8,128)(2,1)S(1)}, bf16[400,128]{1,0:T(8,128)(2,1)S(1)}, u32[]{:S(2)}, u32[]{:S(2)}) collective-permute-start(bf16[400,128]{1,0:T(8,128)(2,1)S(1)} %get-tuple-element.42), channel_id=1, source_target_pairs={{0,112},{16,0},{32,16},{48,32},{64,48},{80,64},{96,80},{112,96},{1... | collective-permute-start | bytes 307208 | tf_op jit(solution)/shard_map/ppermute | solution.py:22
  82.5 2.9 %collective-permute-done.19.refs_0_ = bf16[400,128]{1,0:T(8,128)(2,1)S(1)} collective-permute-done((bf16[400,128]{1,0:T(8,128)(2,1)S(1)}, bf16[400,128]{1,0:T(8,128)(2,1)S(1)}, u32[]{:S(2)}, u32[]{:S(2)}) %collective-permute-start.19) | collective-permute-done | bytes 102432 | tf_op jit(solution)/shard_map/ppermute | solution.py:22
  85.4 0.2 relay.3
  85.6 0.1 collective-permute-start.21
  85.7 3.2 %collective-permute-start.22 = (bf16[400,128]{1,0:T(8,128)(2,1)S(1)}, bf16[400,128]{1,0:T(8,128)(2,1)S(1)}, u32[]{:S(2)}, u32[]{:S(2)}) collective-permute-start(bf16[400,128]{1,0:T(8,128)(2,1)S(1)} %get-tuple-element.44), channel_id=1, source_target_pairs={{0,112},{16,0},{32,16},{48,32},{64,48},{80,64},{96,80},{112,96},{1... | collective-permute-start | bytes 307208 | tf_op jit(solution)/shard_map/ppermute | solution.py:22
  88.9 2.6 %collective-permute-done.21.refs_0_ = bf16[400,128]{1,0:T(8,128)(2,1)S(1)} collective-permute-done((bf16[400,128]{1,0:T(8,128)(2,1)S(1)}, bf16[400,128]{1,0:T(8,128)(2,1)S(1)}, u32[]{:S(2)}, u32[]{:S(2)}) %collective-permute-start.21) | collective-permute-done | bytes 102432 | tf_op jit(solution)/shard_map/ppermute | solution.py:22
  91.6 0.2 relay.4
  91.9 3.3 %collective-permute-start.25 = (bf16[400,128]{1,0:T(8,128)(2,1)S(1)}, bf16[400,128]{1,0:T(8,128)(2,1)S(1)}, u32[]{:S(2)}, u32[]{:S(2)}) collective-permute-start(bf16[400,128]{1,0:T(8,128)(2,1)S(1)} %get-tuple-element.46), channel_id=1, source_target_pairs={{0,112},{16,0},{32,16},{48,32},{64,48},{80,64},{96,80},{112,96},{1... | collective-permute-start | bytes 307208 | tf_op jit(solution)/shard_map/ppermute | solution.py:22
  95.2 2.5 %collective-permute-done.23.refs_0_ = bf16[400,128]{1,0:T(8,128)(2,1)S(1)} collective-permute-done((bf16[400,128]{1,0:T(8,128)(2,1)S(1)}, bf16[400,128]{1,0:T(8,128)(2,1)S(1)}, u32[]{:S(2)}, u32[]{:S(2)}) %collective-permute-start.23) | collective-permute-done | bytes 102432 | tf_op jit(solution)/shard_map/ppermute | solution.py:22
  97.7 0.1 relay.5
  97.9 5.8 %collective-permute-done.24.up = bf16[400,128]{1,0:T(8,128)(2,1)S(1)} collective-permute-done((bf16[400,128]{1,0:T(8,128)(2,1)S(1)}, bf16[400,128]{1,0:T(8,128)(2,1)S(1)}, u32[]{:S(2)}, u32[]{:S(2)}) %collective-permute-start.24) | collective-permute-done | bytes 102432 | tf_op jit(solution)/shard_map/ppermute | solution.py:22
  103.8 0.8 text_sum.1
  104.6 1.7 %image_sum.1 = (f32[48,1024]{1,0:T(8,128)}, f32[1,1]{1,0:T(1,128)}) custom-call(bf16[16,400,128]{2,1,0:T(8,128)(2,1)S(1)} %all-to-all-done.1.got, f32[8,128]{1,0:T(8,128)S(1)} %get-tuple-element.35.terms, f32[1,128]{1,0:T(1,128)S(1)} %get-tuple-element.47.side), custom_call_target="tpu_custom_call" | custom-call | bytes 1839620 | tf_op jit(solution)/shard_map/image_sum/pallas_call | solution.py:104
  (30 shorter events, 0.3 us)
Async XLA Ops:
  0.6 17.1 %collective-permute-start = (bf16[48,1024]{1,0:T(8,128)(2,1)}, bf16[48,1024]{1,0:T(8,128)(2,1)S(1)}, u32[]{:S(2)}, u32[]{:S(2)}) collective-permute-start(bf16[48,1024]{1,0:T(8,128)(2,1)} %near.1), channel_id=1, source_target_pairs={{0,64},{16,80},{32,96},{48,112},{64,0},{80,16},{96,32},{112,48},{1... | collective-permute-start | bytes 294920 | tf_op jit(solution)/shard_map/ppermute | solution.py:22
  7.9 0.9 copy-start
  10.1 7.7 %copy-start.1 = (bf16[48,1024]{1,0:T(8,128)(2,1)S(1)}, bf16[48,1024]{1,0:T(8,128)(2,1)}, u32[]{:S(2)}) copy-start(bf16[48,1024]{1,0:T(8,128)(2,1)} %near.1) | copy-start | bytes 294916
  10.1 30.0 %all-to-all-start = ((bf16[16,48,1024]{2,1,0:T(8,128)(2,1)}), bf16[16,48,1024]{2,1,0:T(8,128)(2,1)S(1)}, u32[]{:S(2)}, u32[]{:S(2)}) async-start(bf16[16,48,1024]{2,1,0:T(8,128)(2,1)} %copies.1), calls=%async_computation | async-start | bytes 3145728 | tf_op jit(solution)/shard_map/all_to_all | solution.py:394
  17.8 11.2 %copy-start.2 = (s32[384]{0:T(512)S(1)}, s32[384]{0:T(512)}, u32[]{:S(2)}) copy-start(s32[384]{0:T(512)} %refs_9_.1) | copy-start | bytes 4612
  17.8 9.1 %collective-permute-start.3 = (bf16[96,1024]{1,0:T(8,128)(2,1)S(1)}, bf16[96,1024]{1,0:T(8,128)(2,1)S(1)}, u32[]{:S(2)}, u32[]{:S(2)}) collective-permute-start(bf16[96,1024]{1,0:T(8,128)(2,1)S(1)} %join.1.refs_0_), channel_id=1, source_target_pairs={{112,0},{0,16},{16,32},{32,48},{48,64},{64,80},{80,96},{96,112},{1... | collective-permute-start | bytes 589832 | tf_op jit(solution)/shard_map/ppermute | solution.py:32
  18.9 8.6 %collective-permute-start.2 = (bf16[96,1024]{1,0:T(8,128)(2,1)S(1)}, bf16[96,1024]{1,0:T(8,128)(2,1)S(1)}, u32[]{:S(2)}, u32[]{:S(2)}) collective-permute-start(bf16[96,1024]{1,0:T(8,128)(2,1)S(1)} %join.1.refs_0_), channel_id=1, source_target_pairs={{32,0},{112,16},{64,32},{16,48},{96,64},{48,80},{0,96},{80,112},{3... | collective-permute-start | bytes 589832 | tf_op jit(solution)/shard_map/ppermute | solution.py:32
  19.5 9.5 %collective-permute-start.1 = (bf16[96,1024]{1,0:T(8,128)(2,1)S(1)}, bf16[96,1024]{1,0:T(8,128)(2,1)S(1)}, u32[]{:S(2)}, u32[]{:S(2)}) collective-permute-start(bf16[96,1024]{1,0:T(8,128)(2,1)S(1)} %join.1.refs_0_), channel_id=1, source_target_pairs={{16,0},{32,16},{48,32},{64,48},{80,64},{96,80},{112,96},{0,112},{1... | collective-permute-start | bytes 589832 | tf_op jit(solution)/shard_map/ppermute | solution.py:32
  22.6 13.4 %collective-permute-start.4 = (bf16[96,1024]{1,0:T(8,128)(2,1)S(1)}, bf16[96,1024]{1,0:T(8,128)(2,1)S(1)}, u32[]{:S(2)}, u32[]{:S(2)}) collective-permute-start(bf16[96,1024]{1,0:T(8,128)(2,1)S(1)} %join.1.refs_0_), channel_id=1, source_target_pairs={{0,8},{8,0},{1,9},{9,1},{2,10},{10,2},{3,11},{11,3},{4,12},{12,4},... | collective-permute-start | bytes 589832 | tf_op jit(solution)/shard_map/ppermute | solution.py:402
  26.9 9.1 %collective-permute-start.7 = (bf16[96,1024]{1,0:T(8,128)(2,1)S(1)}, bf16[96,1024]{1,0:T(8,128)(2,1)S(1)}, u32[]{:S(2)}, u32[]{:S(2)}) collective-permute-start(bf16[96,1024]{1,0:T(8,128)(2,1)S(1)} %collective-permute-done.3.refs_3_), channel_id=1, source_target_pairs={{0,8},{8,0},{1,9},{9,1},{2,10},{10,2},{3,11},{11,3},{4,12},{12,4},... | collective-permute-start | bytes 589832 | tf_op jit(solution)/shard_map/ppermute | solution.py:402
  27.5 8.5 %collective-permute-start.6 = (bf16[96,1024]{1,0:T(8,128)(2,1)S(1)}, bf16[96,1024]{1,0:T(8,128)(2,1)S(1)}, u32[]{:S(2)}, u32[]{:S(2)}) collective-permute-start(bf16[96,1024]{1,0:T(8,128)(2,1)S(1)} %collective-permute-done.2.refs_2_), channel_id=1, source_target_pairs={{0,8},{8,0},{1,9},{9,1},{2,10},{10,2},{3,11},{11,3},{4,12},{12,4},... | collective-permute-start | bytes 589832 | tf_op jit(solution)/shard_map/ppermute | solution.py:402
  28.9 7.1 %collective-permute-start.5 = (bf16[96,1024]{1,0:T(8,128)(2,1)S(1)}, bf16[96,1024]{1,0:T(8,128)(2,1)S(1)}, u32[]{:S(2)}, u32[]{:S(2)}) collective-permute-start(bf16[96,1024]{1,0:T(8,128)(2,1)S(1)} %collective-permute-done.1.refs_1_), channel_id=1, source_target_pairs={{0,8},{8,0},{1,9},{9,1},{2,10},{10,2},{3,11},{11,3},{4,12},{12,4},... | collective-permute-start | bytes 589832 | tf_op jit(solution)/shard_map/ppermute | solution.py:402
  28.9 7.1 %collective-permute-start.8 = (s32[384]{0:T(512)S(1)}, s32[384]{0:T(512)S(1)}, u32[]{:S(2)}, u32[]{:S(2)}) collective-permute-start(s32[384]{0:T(512)S(1)} %copy-done.2), channel_id=1, source_target_pairs={{0,128},{128,0},{1,129},{129,1},{2,130},{130,2},{3,131},{131,3},{4... | collective-permute-start | bytes 4616 | tf_op jit(solution)/shard_map/ppermute | solution.py:385
  43.2 1.3 %collective-permute-start.9 = (f32[1,1024]{1,0:T(1,128)S(1)}, f32[1,1024]{1,0:T(1,128)S(1)}, u32[]{:S(2)}, u32[]{:S(2)}) collective-permute-start(f32[1,1024]{1,0:T(1,128)S(1)} %get-tuple-element.28), channel_id=1, source_target_pairs={{0,8},{8,0},{1,9},{9,1},{2,10},{10,2},{3,11},{11,3},{4,12},{12,4},... | collective-permute-start | bytes 12296 | tf_op jit(solution)/shard_map/ppermute | solution.py:420
  44.5 5.8 %collective-permute-start.12 = (f32[1,1792]{1,0:T(1,128)S(1)}, f32[1,1792]{1,0:T(1,128)S(1)}, u32[]{:S(2)}, u32[]{:S(2)}) collective-permute-start(f32[1,1792]{1,0:T(1,128)S(1)} %meet.1.mine), channel_id=1, source_target_pairs={{0,32},{1,33},{2,34},{3,35},{4,36},{5,37},{6,38},{7,39},{8,9},{9,8... | collective-permute-start | bytes 21512 | tf_op jit(solution)/shard_map/ppermute | solution.py:53
  46.0 4.3 %collective-permute-start.11 = (f32[1,1792]{1,0:T(1,128)S(1)}, f32[1,1792]{1,0:T(1,128)S(1)}, u32[]{:S(2)}, u32[]{:S(2)}) collective-permute-start(f32[1,1792]{1,0:T(1,128)S(1)} %meet.1.mine), channel_id=1, source_target_pairs={{0,112},{1,113},{2,114},{3,115},{4,116},{5,117},{6,118},{7,119},{8... | collective-permute-start | bytes 21512 | tf_op jit(solution)/shard_map/ppermute | solution.py:53
  48.2 4.9 %collective-permute-start.10 = (f32[1,1792]{1,0:T(1,128)S(1)}, f32[1,1792]{1,0:T(1,128)S(1)}, u32[]{:S(2)}, u32[]{:S(2)}) collective-permute-start(f32[1,1792]{1,0:T(1,128)S(1)} %meet.1.mine), channel_id=1, source_target_pairs={{0,16},{1,17},{2,18},{3,19},{4,20},{5,21},{6,22},{7,23},{8,136},{9... | collective-permute-start | bytes 21512 | tf_op jit(solution)/shard_map/ppermute | solution.py:53
  53.1 2.6 %collective-permute-start.15 = (f32[1,1792]{1,0:T(1,128)S(1)}, f32[1,1792]{1,0:T(1,128)S(1)}, u32[]{:S(2)}, u32[]{:S(2)}) collective-permute-start(f32[1,1792]{1,0:T(1,128)S(1)} %round.1.mine), channel_id=1, source_target_pairs={{8,12},{9,13},{10,14},{11,15},{12,8},{13,9},{14,10},{15,11},{24,28... | collective-permute-start | bytes 21512 | tf_op jit(solution)/shard_map/ppermute | solution.py:53
  53.8 1.9 %collective-permute-start.14 = (f32[1,1792]{1,0:T(1,128)S(1)}, f32[1,1792]{1,0:T(1,128)S(1)}, u32[]{:S(2)}, u32[]{:S(2)}) collective-permute-start(f32[1,1792]{1,0:T(1,128)S(1)} %round.1.mine), channel_id=1, source_target_pairs={{8,14},{9,15},{10,8},{11,9},{12,10},{13,11},{14,12},{15,13},{24,30... | collective-permute-start | bytes 21512 | tf_op jit(solution)/shard_map/ppermute | solution.py:53
  54.5 7.8 %collective-permute-start.13 = (f32[1,1792]{1,0:T(1,128)S(1)}, f32[1,1792]{1,0:T(1,128)S(1)}, u32[]{:S(2)}, u32[]{:S(2)}) collective-permute-start(f32[1,1792]{1,0:T(1,128)S(1)} %round.1.mine), channel_id=1, source_target_pairs={{0,64},{1,65},{2,66},{3,67},{4,68},{5,69},{6,70},{7,71},{8,10},{9,... | collective-permute-start | bytes 21512 | tf_op jit(solution)/shard_map/ppermute | solution.py:53
  62.3 1.3 %collective-permute-start.16 = (f32[1,1024]{1,0:T(1,128)S(1)}, f32[1,1024]{1,0:T(1,128)S(1)}, u32[]{:S(2)}, u32[]{:S(2)}) collective-permute-start(f32[1,1024]{1,0:T(1,128)S(1)} %get-tuple-element.30), channel_id=1, source_target_pairs={{0,8},{8,0},{1,9},{9,1},{2,10},{10,2},{3,11},{11,3},{4,12},{12,4},... | collective-permute-start | bytes 12296 | tf_op jit(solution)/shard_map/ppermute | solution.py:428
  66.9 6.0 %collective-permute-start.17 = (f32[8,128]{1,0:T(8,128)S(1)}, f32[8,128]{1,0:T(8,128)S(1)}, u32[]{:S(2)}, u32[]{:S(2)}) collective-permute-start(f32[8,128]{1,0:T(8,128)S(1)} %get-tuple-element.35.terms), channel_id=1, source_target_pairs={{0,8},{8,0},{1,9},{9,1},{2,10},{10,2},{3,11},{11,3},{4,12},{12,4},... | collective-permute-start | bytes 12296 | tf_op jit(solution)/shard_map/ppermute | solution.py:449
  67.2 37.5 %all-to-all-start.1 = ((bf16[16,400,128]{2,1,0:T(8,128)(2,1)}), bf16[16,400,128]{2,1,0:T(8,128)(2,1)S(1)}, u32[]{:S(2)}, u32[]{:S(2)}) async-start(bf16[16,400,128]{2,1,0:T(8,128)(2,1)} %get-tuple-element.34), calls=%async_computation.1 | async-start | bytes 3276800 | tf_op jit(solution)/shard_map/all_to_all | solution.py:448
  72.9 1.3 %copy-start.3 = (bf16[768,768]{1,0:T(8,128)(2,1)S(1)}, bf16[768,768]{1,0:T(8,128)(2,1)}, u32[]{:S(2)}) copy-start(bf16[768,768]{1,0:T(8,128)(2,1)} %get-tuple-element.36.grads) | copy-start | bytes 3538948
  75.8 2.4 %collective-permute-start.18 = (bf16[384,1024]{1,0:T(8,128)(2,1)S(1)}, bf16[384,1024]{1,0:T(8,128)(2,1)S(1)}, u32[]{:S(2)}, u32[]{:S(2)}) collective-permute-start(bf16[384,1024]{1,0:T(8,128)(2,1)S(1)} %get-tuple-element.38), channel_id=1, source_target_pairs={{0,8},{8,0},{1,9},{9,1},{2,10},{10,2},{3,11},{11,3},{4,12},{12,4},... | collective-permute-start | bytes 2359304 | tf_op jit(solution)/shard_map/ppermute | solution.py:462
  79.2 6.2 %collective-permute-start.19 = (bf16[400,128]{1,0:T(8,128)(2,1)S(1)}, bf16[400,128]{1,0:T(8,128)(2,1)S(1)}, u32[]{:S(2)}, u32[]{:S(2)}) collective-permute-start(bf16[400,128]{1,0:T(8,128)(2,1)S(1)} %get-tuple-element.41), channel_id=1, source_target_pairs={{0,16},{16,32},{32,48},{48,64},{64,80},{80,96},{96,112},{112,0},{1... | collective-permute-start | bytes 307208 | tf_op jit(solution)/shard_map/ppermute | solution.py:22
  79.3 6.1 %collective-permute-start.20 = (bf16[400,128]{1,0:T(8,128)(2,1)S(1)}, bf16[400,128]{1,0:T(8,128)(2,1)S(1)}, u32[]{:S(2)}, u32[]{:S(2)}) collective-permute-start(bf16[400,128]{1,0:T(8,128)(2,1)S(1)} %get-tuple-element.42), channel_id=1, source_target_pairs={{0,112},{16,0},{32,16},{48,32},{64,48},{80,64},{96,80},{112,96},{1... | collective-permute-start | bytes 307208 | tf_op jit(solution)/shard_map/ppermute | solution.py:22
  85.6 5.9 %collective-permute-start.21 = (bf16[400,128]{1,0:T(8,128)(2,1)S(1)}, bf16[400,128]{1,0:T(8,128)(2,1)S(1)}, u32[]{:S(2)}, u32[]{:S(2)}) collective-permute-start(bf16[400,128]{1,0:T(8,128)(2,1)S(1)} %get-tuple-element.43), channel_id=1, source_target_pairs={{0,16},{16,32},{32,48},{48,64},{64,80},{80,96},{96,112},{112,0},{1... | collective-permute-start | bytes 307208 | tf_op jit(solution)/shard_map/ppermute | solution.py:22
  85.7 5.9 %collective-permute-start.22 = (bf16[400,128]{1,0:T(8,128)(2,1)S(1)}, bf16[400,128]{1,0:T(8,128)(2,1)S(1)}, u32[]{:S(2)}, u32[]{:S(2)}) collective-permute-start(bf16[400,128]{1,0:T(8,128)(2,1)S(1)} %get-tuple-element.44), channel_id=1, source_target_pairs={{0,112},{16,0},{32,16},{48,32},{64,48},{80,64},{96,80},{112,96},{1... | collective-permute-start | bytes 307208 | tf_op jit(solution)/shard_map/ppermute | solution.py:22
  91.8 5.9 %collective-permute-start.23 = (bf16[400,128]{1,0:T(8,128)(2,1)S(1)}, bf16[400,128]{1,0:T(8,128)(2,1)S(1)}, u32[]{:S(2)}, u32[]{:S(2)}) collective-permute-start(bf16[400,128]{1,0:T(8,128)(2,1)S(1)} %get-tuple-element.45), channel_id=1, source_target_pairs={{0,16},{16,32},{32,48},{48,64},{64,80},{80,96},{96,112},{112,0},{1... | collective-permute-start | bytes 307208 | tf_op jit(solution)/shard_map/ppermute | solution.py:22
  91.9 6.1 %collective-permute-start.25 = (bf16[400,128]{1,0:T(8,128)(2,1)S(1)}, bf16[400,128]{1,0:T(8,128)(2,1)S(1)}, u32[]{:S(2)}, u32[]{:S(2)}) collective-permute-start(bf16[400,128]{1,0:T(8,128)(2,1)S(1)} %get-tuple-element.46), channel_id=1, source_target_pairs={{0,112},{16,0},{32,16},{48,32},{64,48},{80,64},{96,80},{112,96},{1... | collective-permute-start | bytes 307208 | tf_op jit(solution)/shard_map/ppermute | solution.py:22
  97.8 5.9 %collective-permute-start.24 = (bf16[400,128]{1,0:T(8,128)(2,1)S(1)}, bf16[400,128]{1,0:T(8,128)(2,1)S(1)}, u32[]{:S(2)}, u32[]{:S(2)}) collective-permute-start(bf16[400,128]{1,0:T(8,128)(2,1)S(1)} %relay.5), channel_id=1, source_target_pairs={{0,16},{16,32},{32,48},{48,64},{64,80},{80,96},{96,112},{112,0},{1... | collective-permute-start | bytes 307208 | tf_op jit(solution)/shard_map/ppermute | solution.py:22

commit v14 on v12

--- a/solution.py
+++ b/solution.py
@@ -59,9 +59,7 @@
 
 
 def encode(scaled):
-    square = scaled * scaled
-    fourth = square * square
-    return jnp.where(scaled < 0, -fourth, fourth).astype(BF16)
+    return ((scaled * scaled) * (scaled * jnp.abs(scaled))).astype(BF16)
 
 
 def decode(x):
@@ -209,8 +207,8 @@
 def round_body(last, mine, one, two, three, *outs):
     size = mine.shape[1] // 2 - LANES
     first = lax.axis_index("c") == 0
-    parts = [mine[:, : 2 * size], one[:, : 2 * size]]
-    for ref in (two, three):
+    parts = [mine[:, : 2 * size], three[:, : 2 * size]]
+    for ref in (one, two):
         part = ref[:, : 2 * size]
         parts.append(jnp.where(first, -1e38, part) if last else part)
     lse = merge(parts)
@@ -258,7 +256,8 @@
     terms[...] = jnp.concatenate(
         [row_terms, text_max, image_max, jnp.zeros((5, LANES), F32)], axis=0
     )
-    row_column = to_column(row_lse)
+    row_column = to_column(row_lse + math.log(2.0))
+    col_row = col_lse + math.log(2.0)
     pair_column = to_column(pair[...])
     extra = split3(col_terms)
     scale = inverse(text_max[:, :1]) * inv_root
@@ -267,7 +266,7 @@
     for r in range(0, size, step):
         at = slice(r, r + step)
         tile = scores[at, :]
-        probs = 0.5 * (jnp.exp(tile - row_column[at, :]) + jnp.exp(tile - col_lse))
+        probs = jnp.exp(tile - row_column[at, :]) + jnp.exp(tile - col_row)
         grad = (probs - jnp.where(pair_column[at, :] == ids, 1.0, 0.0)).astype(BF16)
         grads[at, :] = grad
         part = encode(jnp.dot(grad, text[...], preferred_element_type=F32) * scale)
@@ -428,7 +427,7 @@
     (stats,) = call(meet_body, (full,), (hold, lax.ppermute(cross, "c", SWAP)), "meet")
     around = [turn_both(stats, q, q, 0) for q in (1, -1, 2)]
     (stats,) = call(functools.partial(round_body, False), (full,), (stats, *around), "round")
-    far_z = (n_z // 2, None, None)
+    far_z = (None, None, n_z // 2)
     around = [turn_both(stats, f, 0, q) for f, q in zip(far_z, (1, -1, 2))]
     stats, cross = call(
         functools.partial(round_body, True), (full, shape(cross.shape, F32)), (stats, *around), "last"

time: 104 us -> 103 us (level)
  starting transfers between devices: 51.5 us -> 50.1 us
  transfers between devices with their start and end apart: 24 -> 24, of which waited for: 14 -> 13; matrix products, arithmetic and copies ran while one was open for 0% -> 0% of each run, Pallas kernels for 2% -> 2%
where the time goes in v14:
time: 103 us; the launch traced here: 102 us
  starting transfers between devices  50.1 us (49%)
  waiting for transfers between devices  36.8 us (36%)
  Pallas kernels  13.5 us (13%)
    pallas_call x11, Pallas kernels, call(): pl.pallas_call(body, out_shape=outs, in_specs=[pl.BlockSpec(memory_space=...  13.5 us
    ppermute x6, starting transfers between devices, turn_both(): return lax.ppermute(x, AXES, pairs)  11.3 us
    ppermute x6, waiting for transfers between devices, turn_z(): return lax.ppermute(x, 'z', pairs if back else [(b, a) for a, b in pairs])  10.7 us
    ppermute x2, starting transfers between devices, turn(): lax.ppermute(x, axis, [(i, (i + step) % count) for i in range(count)])  8.64 us
    ppermute x4, starting transfers between devices, shards(): pieces = pieces + [lax.ppermute(piece, 'c', SWAP) for piece in pieces]  7.89 us
    ppermute x2, waiting for transfers between devices, turn(): lax.ppermute(x, axis, [(i, (i + step) % count) for i in range(count)])  7.54 us
    all_to_all x1, starting transfers between devices, shards(): image = lax.all_to_all(copies, PLANE, 0, 0).reshape(size, width)  6.9 us
    ppermute x6, starting transfers between devices, turn_z(): return lax.ppermute(x, 'z', pairs if back else [(b, a) for a, b in pairs])  6.7 us
  transfers between devices with their start and end apart: 24, of which 13 were waited for; matrix products, arithmetic and copies ran while one was open for 0% of the time, Pallas kernels for 2%

profile of v14, /device:TPU:1, one launch (start us, length us, event | category | flops | bytes accessed | tf_op | source)
XLA Modules:
  0.0 102.4 jit_solution(11217813940102942991)
XLA Ops:
  0.6 7.8 %collective-permute-start = (bf16[48,1024]{1,0:T(8,128)(2,1)}, bf16[48,1024]{1,0:T(8,128)(2,1)S(1)}, u32[]{:S(2)}, u32[]{:S(2)}) collective-permute-start(bf16[48,1024]{1,0:T(8,128)(2,1)} %near.1), channel_id=1, source_target_pairs={{0,64},{16,80},{32,96},{48,112},{64,0},{80,16},{96,32},{112,48},{1... | collective-permute-start | bytes 294920 | tf_op jit(solution)/shard_map/ppermute | solution.py:22
  8.5 0.9 copy-done
  9.3 1.3 %copies.1 = bf16[16,48,1024]{2,1,0:T(8,128)(2,1)} custom-call(bf16[48,1024]{1,0:T(8,128)(2,1)S(1)} %copy-done), custom_call_target="tpu_custom_call" | custom-call | bytes 1671168 | tf_op jit(solution)/shard_map/copies/pallas_call | solution.py:102
  10.7 0.0 copy-start.1
  10.7 6.9 %all-to-all-start = ((bf16[16,48,1024]{2,1,0:T(8,128)(2,1)}), bf16[16,48,1024]{2,1,0:T(8,128)(2,1)S(1)}, u32[]{:S(2)}, u32[]{:S(2)}) async-start(bf16[16,48,1024]{2,1,0:T(8,128)(2,1)} %copies.1), calls=%async_computation | async-start | bytes 3145728 | tf_op jit(solution)/shard_map/all_to_all | solution.py:401
  17.6 0.0 copy-start.2
  17.6 0.8 collective-permute-start.3
  18.5 0.3 collective-permute-start.2
  18.7 2.9 %collective-permute-start.1 = (bf16[96,1024]{1,0:T(8,128)(2,1)S(1)}, bf16[96,1024]{1,0:T(8,128)(2,1)S(1)}, u32[]{:S(2)}, u32[]{:S(2)}) collective-permute-start(bf16[96,1024]{1,0:T(8,128)(2,1)S(1)} %join.1.refs_0_), channel_id=1, source_target_pairs={{16,0},{32,16},{48,32},{64,48},{80,64},{96,80},{112,96},{0,112},{1... | collective-permute-start | bytes 589832 | tf_op jit(solution)/shard_map/ppermute | solution.py:32
  21.6 2.1 %collective-permute-start.4 = (bf16[96,1024]{1,0:T(8,128)(2,1)S(1)}, bf16[96,1024]{1,0:T(8,128)(2,1)S(1)}, u32[]{:S(2)}, u32[]{:S(2)}) collective-permute-start(bf16[96,1024]{1,0:T(8,128)(2,1)S(1)} %join.1.refs_0_), channel_id=1, source_target_pairs={{0,8},{8,0},{1,9},{9,1},{2,10},{10,2},{3,11},{11,3},{4,12},{12,4},... | collective-permute-start | bytes 589832 | tf_op jit(solution)/shard_map/ppermute | solution.py:409
  23.7 0.4 collective-permute-done.3.refs_3_
  24.1 3.9 %collective-permute-start.7 = (bf16[96,1024]{1,0:T(8,128)(2,1)S(1)}, bf16[96,1024]{1,0:T(8,128)(2,1)S(1)}, u32[]{:S(2)}, u32[]{:S(2)}) collective-permute-start(bf16[96,1024]{1,0:T(8,128)(2,1)S(1)} %collective-permute-done.3.refs_3_), channel_id=1, source_target_pairs={{0,8},{8,0},{1,9},{9,1},{2,10},{10,2},{3,11},{11,3},{4,12},{12,4},... | collective-permute-start | bytes 589832 | tf_op jit(solution)/shard_map/ppermute | solution.py:409
  28.0 0.0 collective-permute-done.2.refs_2_
  28.0 0.7 collective-permute-start.6
  28.7 0.4 collective-permute-done.1.refs_1_
  29.1 1.2 %collective-permute-start.5 = (bf16[96,1024]{1,0:T(8,128)(2,1)S(1)}, bf16[96,1024]{1,0:T(8,128)(2,1)S(1)}, u32[]{:S(2)}, u32[]{:S(2)}) collective-permute-start(bf16[96,1024]{1,0:T(8,128)(2,1)S(1)} %collective-permute-done.1.refs_1_), channel_id=1, source_target_pairs={{0,8},{8,0},{1,9},{9,1},{2,10},{10,2},{3,11},{11,3},{4,12},{12,4},... | collective-permute-start | bytes 589832 | tf_op jit(solution)/shard_map/ppermute | solution.py:409
  30.3 1.4 %collective-permute-start.8 = (s32[384]{0:T(512)S(1)}, s32[384]{0:T(512)S(1)}, u32[]{:S(2)}, u32[]{:S(2)}) collective-permute-start(s32[384]{0:T(512)S(1)} %copy-done.2), channel_id=1, source_target_pairs={{0,128},{128,0},{1,129},{129,1},{2,130},{130,2},{3,131},{131,3},{4... | collective-permute-start | bytes 4616 | tf_op jit(solution)/shard_map/ppermute | solution.py:392
  31.6 4.0 %collective-permute-done.8.refs_10_ = s32[384]{0:T(512)S(1)} collective-permute-done((s32[384]{0:T(512)S(1)}, s32[384]{0:T(512)S(1)}, u32[]{:S(2)}, u32[]{:S(2)}) %collective-permute-start.8) | collective-permute-done | bytes 1568 | tf_op jit(solution)/shard_map/ppermute | solution.py:392
  35.6 3.3 %all-to-all-done = bf16[16,48,1024]{2,1,0:T(8,128)(2,1)S(1)} async-done(((bf16[16,48,1024]{2,1,0:T(8,128)(2,1)}), bf16[16,48,1024]{2,1,0:T(8,128)(2,1)S(1)}, u32[]{:S(2)}, u32[]{:S(2)}) %all-to-all-start) | async-done | bytes 1572896 | tf_op jit(solution)/shard_map/all_to_all | solution.py:401
  39.0 3.0 %scores.1 = (f32[1,768]{1,0:T(1,128)S(1)}, f32[768,768]{1,0:T(8,128)S(1)}, bf16[768,1024]{1,0:T(8,128)(2,1)S(1)}, f32[1,1024]{1,0:T(1,128)S(1)}, f32[1,1024]{1,0:T(1,128)S(1)}) custom-call(bf16[96,1024]{1,0:T(8,128)(2,1)S(1)} %join.1.refs_0_, bf16[96,1024]{1,0:T(8,128)(2,1)S(1)} %collective-permute-done.1.refs_1_, ...), custom_call_target="tpu_custom_call" | custom-call | flops 1207959552 | bytes 7092224 | tf_op jit(solution)/shard_map/scores/pallas_call | solution.py:102
  42.0 2.4 %collective-permute-start.9 = (f32[1,1024]{1,0:T(1,128)S(1)}, f32[1,1024]{1,0:T(1,128)S(1)}, u32[]{:S(2)}, u32[]{:S(2)}) collective-permute-start(f32[1,1024]{1,0:T(1,128)S(1)} %get-tuple-element.27), channel_id=1, source_target_pairs={{0,8},{8,0},{1,9},{9,1},{2,10},{10,2},{3,11},{11,3},{4,12},{12,4},... | collective-permute-start | bytes 12296 | tf_op jit(solution)/shard_map/ppermute | solution.py:427
  44.4 0.8 collective-permute-done.9.seen
  45.2 3.9 %collective-permute-start.12 = (f32[1,1792]{1,0:T(1,128)S(1)}, f32[1,1792]{1,0:T(1,128)S(1)}, u32[]{:S(2)}, u32[]{:S(2)}) collective-permute-start(f32[1,1792]{1,0:T(1,128)S(1)} %meet.1.mine), channel_id=1, source_target_pairs={{0,32},{1,33},{2,34},{3,35},{4,36},{5,37},{6,38},{7,39},{8,9},{9,8... | collective-permute-start | bytes 21512 | tf_op jit(solution)/shard_map/ppermute | solution.py:53
  49.2 0.2 collective-permute-start.11
  49.4 1.3 %collective-permute-start.10 = (f32[1,1792]{1,0:T(1,128)S(1)}, f32[1,1792]{1,0:T(1,128)S(1)}, u32[]{:S(2)}, u32[]{:S(2)}) collective-permute-start(f32[1,1792]{1,0:T(1,128)S(1)} %meet.1.mine), channel_id=1, source_target_pairs={{0,16},{1,17},{2,18},{3,19},{4,20},{5,21},{6,22},{7,23},{8,136},{9... | collective-permute-start | bytes 21512 | tf_op jit(solution)/shard_map/ppermute | solution.py:53
  50.7 1.0 collective-permute-done.11.two
  51.7 1.4 %collective-permute-done.10.one = f32[1,1792]{1,0:T(1,128)S(1)} collective-permute-done((f32[1,1792]{1,0:T(1,128)S(1)}, f32[1,1792]{1,0:T(1,128)S(1)}, u32[]{:S(2)}, u32[]{:S(2)}) %collective-permute-start.10) | collective-permute-done | bytes 7200 | tf_op jit(solution)/shard_map/ppermute | solution.py:53
  53.1 0.5 collective-permute-start.15
  53.6 3.4 %collective-permute-start.14 = (f32[1,1792]{1,0:T(1,128)S(1)}, f32[1,1792]{1,0:T(1,128)S(1)}, u32[]{:S(2)}, u32[]{:S(2)}) collective-permute-start(f32[1,1792]{1,0:T(1,128)S(1)} %round.1.mine), channel_id=1, source_target_pairs={{8,14},{9,15},{10,8},{11,9},{12,10},{13,11},{14,12},{15,13},{24,30... | collective-permute-start | bytes 21512 | tf_op jit(solution)/shard_map/ppermute | solution.py:53
  57.1 1.9 %collective-permute-start.13 = (f32[1,1792]{1,0:T(1,128)S(1)}, f32[1,1792]{1,0:T(1,128)S(1)}, u32[]{:S(2)}, u32[]{:S(2)}) collective-permute-start(f32[1,1792]{1,0:T(1,128)S(1)} %round.1.mine), channel_id=1, source_target_pairs={{8,10},{9,11},{10,12},{11,13},{12,14},{13,15},{14,8},{15,9},{24,26... | collective-permute-start | bytes 21512 | tf_op jit(solution)/shard_map/ppermute | solution.py:53
  59.0 3.6 %collective-permute-done.13.one = f32[1,1792]{1,0:T(1,128)S(1)} collective-permute-done((f32[1,1792]{1,0:T(1,128)S(1)}, f32[1,1792]{1,0:T(1,128)S(1)}, u32[]{:S(2)}, u32[]{:S(2)}) %collective-permute-start.13) | collective-permute-done | bytes 7200 | tf_op jit(solution)/shard_map/ppermute | solution.py:53
  62.7 0.1 collective-permute-start.16
  62.8 1.2 %collective-permute-done.16.refs_1_ = f32[1,1024]{1,0:T(1,128)S(1)} collective-permute-done((f32[1,1024]{1,0:T(1,128)S(1)}, f32[1,1024]{1,0:T(1,128)S(1)}, u32[]{:S(2)}, u32[]{:S(2)}) %collective-permute-start.16) | collective-permute-done | bytes 4128 | tf_op jit(solution)/shard_map/ppermute | solution.py:435
  64.0 5.1 %grads.1 = (f32[8,128]{1,0:T(8,128)S(1)}, bf16[384,1024]{1,0:T(8,128)(2,1)S(1)}, bf16[400,1024]{1,0:T(8,128)(2,1)}, bf16[16,400,128]{2,1,0:T(8,128)(2,1)}) custom-call(f32[1,1792]{1,0:T(1,128)S(1)} %get-tuple-element.28.refs_0_, f32[1,1024]{1,0:T(1,128)S(1)} %collective-permute-done.16.refs_1_, f32[768,768]{1,0:T(8,128)S(1)} %get-tuple-element.30.refs_2_, ...), custom_call_target="tpu_custom_call" | custom-call | flops 2415919104 | bytes 8767488 | tf_op jit(solution)/shard_map/grads/pallas_call | solution.py:102
  69.1 0.3 collective-permute-start.17
  69.3 4.6 %all-to-all-start.1 = ((bf16[16,400,128]{2,1,0:T(8,128)(2,1)}), bf16[16,400,128]{2,1,0:T(8,128)(2,1)S(1)}, u32[]{:S(2)}, u32[]{:S(2)}) async-start(bf16[16,400,128]{2,1,0:T(8,128)(2,1)} %get-tuple-element.33), calls=%async_computation.1 | async-start | bytes 3276800 | tf_op jit(solution)/shard_map/all_to_all | solution.py:457
  74.0 1.1 %send.1 = (f32[96,1024]{1,0:T(8,128)S(1)}, f32[1,128]{1,0:T(1,128)S(1)}, bf16[784,128]{1,0:T(8,128)(2,1)S(1)}, bf16[784,128]{1,0:T(8,128)(2,1)S(1)}, bf16[784,128]{1,0:T(8,128)(2,1)S(1)}) custom-call(bf16[384,1024]{1,0:T(8,128)(2,1)S(1)} %get-tuple-element.35.own, bf16[400,1024]{1,0:T(8,128)(2,1)S(1)} %collective-permute-done.17.seen, ...), custom_call_target="tpu_custom_call" | custom-call | flops 10000000000 | bytes 1 | tf_op jit(solution)/shard_map/send/pallas_call | solution.py:102
  75.1 0.1 collective-permute-start.18
  75.2 1.0 collective-permute-start.19
  76.1 1.7 %collective-permute-start.20 = (bf16[784,128]{1,0:T(8,128)(2,1)S(1)}, bf16[784,128]{1,0:T(8,128)(2,1)S(1)}, u32[]{:S(2)}, u32[]{:S(2)}) collective-permute-start(bf16[784,128]{1,0:T(8,128)(2,1)S(1)} %get-tuple-element.41), channel_id=1, source_target_pairs={{0,112},{16,0},{32,16},{48,32},{64,48},{80,64},{96,80},{112,96},{1... | collective-permute-start | bytes 602120 | tf_op jit(solution)/shard_map/ppermute | solution.py:32
  77.8 9.0 %collective-permute-done.18.refs_0_ = bf16[784,128]{1,0:T(8,128)(2,1)S(1)} collective-permute-done((bf16[784,128]{1,0:T(8,128)(2,1)S(1)}, bf16[784,128]{1,0:T(8,128)(2,1)S(1)}, u32[]{:S(2)}, u32[]{:S(2)}) %collective-permute-start.18) | collective-permute-done | bytes 200736 | tf_op jit(solution)/shard_map/ppermute | solution.py:32
  86.8 1.0 collective-permute-done.20.refs_2_
  87.7 0.4 relay.1
  88.1 0.8 collective-permute-start.21
  89.0 7.5 %collective-permute-done.21.pay = bf16[400,128]{1,0:T(8,128)(2,1)S(1)} collective-permute-done((bf16[400,128]{1,0:T(8,128)(2,1)S(1)}, bf16[400,128]{1,0:T(8,128)(2,1)S(1)}, u32[]{:S(2)}, u32[]{:S(2)}) %collective-permute-start.21) | collective-permute-done | bytes 102432 | tf_op jit(solution)/shard_map/ppermute | solution.py:22
  96.5 0.8 text_sum.1
  97.3 3.3 %all-to-all-done.1.got = bf16[16,400,128]{2,1,0:T(8,128)(2,1)S(1)} async-done(((bf16[16,400,128]{2,1,0:T(8,128)(2,1)}), bf16[16,400,128]{2,1,0:T(8,128)(2,1)S(1)}, u32[]{:S(2)}, u32[]{:S(2)}) %all-to-all-start.1) | async-done | bytes 1638432 | tf_op jit(solution)/shard_map/all_to_all | solution.py:457
  100.5 1.7 %image_sum.1 = (f32[48,1024]{1,0:T(8,128)}, f32[1,1]{1,0:T(1,128)}) custom-call(bf16[16,400,128]{2,1,0:T(8,128)(2,1)S(1)} %all-to-all-done.1.got, f32[8,128]{1,0:T(8,128)S(1)} %get-tuple-element.34.terms, f32[1,128]{1,0:T(1,128)S(1)} %get-tuple-element.45.side), custom_call_target="tpu_custom_call" | custom-call | bytes 1839620 | tf_op jit(solution)/shard_map/image_sum/pallas_call | solution.py:102
  (17 shorter events, 0.1 us)
Async XLA Ops:
  0.6 17.0 %collective-permute-start = (bf16[48,1024]{1,0:T(8,128)(2,1)}, bf16[48,1024]{1,0:T(8,128)(2,1)S(1)}, u32[]{:S(2)}, u32[]{:S(2)}) collective-permute-start(bf16[48,1024]{1,0:T(8,128)(2,1)} %near.1), channel_id=1, source_target_pairs={{0,64},{16,80},{32,96},{48,112},{64,0},{80,16},{96,32},{112,48},{1... | collective-permute-start | bytes 294920 | tf_op jit(solution)/shard_map/ppermute | solution.py:22
  8.5 0.9 copy-start
  10.7 6.9 %copy-start.1 = (bf16[48,1024]{1,0:T(8,128)(2,1)S(1)}, bf16[48,1024]{1,0:T(8,128)(2,1)}, u32[]{:S(2)}) copy-start(bf16[48,1024]{1,0:T(8,128)(2,1)} %near.1) | copy-start | bytes 294916
  10.7 28.3 %all-to-all-start = ((bf16[16,48,1024]{2,1,0:T(8,128)(2,1)}), bf16[16,48,1024]{2,1,0:T(8,128)(2,1)S(1)}, u32[]{:S(2)}, u32[]{:S(2)}) async-start(bf16[16,48,1024]{2,1,0:T(8,128)(2,1)} %copies.1), calls=%async_computation | async-start | bytes 3145728 | tf_op jit(solution)/shard_map/all_to_all | solution.py:401
  17.6 12.7 %copy-start.2 = (s32[384]{0:T(512)S(1)}, s32[384]{0:T(512)}, u32[]{:S(2)}) copy-start(s32[384]{0:T(512)} %refs_9_.1) | copy-start | bytes 4612
  17.6 6.4 %collective-permute-start.3 = (bf16[96,1024]{1,0:T(8,128)(2,1)S(1)}, bf16[96,1024]{1,0:T(8,128)(2,1)S(1)}, u32[]{:S(2)}, u32[]{:S(2)}) collective-permute-start(bf16[96,1024]{1,0:T(8,128)(2,1)S(1)} %join.1.refs_0_), channel_id=1, source_target_pairs={{112,0},{0,16},{16,32},{32,48},{48,64},{64,80},{80,96},{96,112},{1... | collective-permute-start | bytes 589832 | tf_op jit(solution)/shard_map/ppermute | solution.py:32
  18.5 9.6 %collective-permute-start.2 = (bf16[96,1024]{1,0:T(8,128)(2,1)S(1)}, bf16[96,1024]{1,0:T(8,128)(2,1)S(1)}, u32[]{:S(2)}, u32[]{:S(2)}) collective-permute-start(bf16[96,1024]{1,0:T(8,128)(2,1)S(1)} %join.1.refs_0_), channel_id=1, source_target_pairs={{32,0},{112,16},{64,32},{16,48},{96,64},{48,80},{0,96},{80,112},{3... | collective-permute-start | bytes 589832 | tf_op jit(solution)/shard_map/ppermute | solution.py:32
  18.7 10.3 %collective-permute-start.1 = (bf16[96,1024]{1,0:T(8,128)(2,1)S(1)}, bf16[96,1024]{1,0:T(8,128)(2,1)S(1)}, u32[]{:S(2)}, u32[]{:S(2)}) collective-permute-start(bf16[96,1024]{1,0:T(8,128)(2,1)S(1)} %join.1.refs_0_), channel_id=1, source_target_pairs={{16,0},{32,16},{48,32},{64,48},{80,64},{96,80},{112,96},{0,112},{1... | collective-permute-start | bytes 589832 | tf_op jit(solution)/shard_map/ppermute | solution.py:32
  21.6 14.0 %collective-permute-start.4 = (bf16[96,1024]{1,0:T(8,128)(2,1)S(1)}, bf16[96,1024]{1,0:T(8,128)(2,1)S(1)}, u32[]{:S(2)}, u32[]{:S(2)}) collective-permute-start(bf16[96,1024]{1,0:T(8,128)(2,1)S(1)} %join.1.refs_0_), channel_id=1, source_target_pairs={{0,8},{8,0},{1,9},{9,1},{2,10},{10,2},{3,11},{11,3},{4,12},{12,4},... | collective-permute-start | bytes 589832 | tf_op jit(solution)/shard_map/ppermute | solution.py:409
  24.1 11.5 %collective-permute-start.7 = (bf16[96,1024]{1,0:T(8,128)(2,1)S(1)}, bf16[96,1024]{1,0:T(8,128)(2,1)S(1)}, u32[]{:S(2)}, u32[]{:S(2)}) collective-permute-start(bf16[96,1024]{1,0:T(8,128)(2,1)S(1)} %collective-permute-done.3.refs_3_), channel_id=1, source_target_pairs={{0,8},{8,0},{1,9},{9,1},{2,10},{10,2},{3,11},{11,3},{4,12},{12,4},... | collective-permute-start | bytes 589832 | tf_op jit(solution)/shard_map/ppermute | solution.py:409
  28.0 7.6 %collective-permute-start.6 = (bf16[96,1024]{1,0:T(8,128)(2,1)S(1)}, bf16[96,1024]{1,0:T(8,128)(2,1)S(1)}, u32[]{:S(2)}, u32[]{:S(2)}) collective-permute-start(bf16[96,1024]{1,0:T(8,128)(2,1)S(1)} %collective-permute-done.2.refs_2_), channel_id=1, source_target_pairs={{0,8},{8,0},{1,9},{9,1},{2,10},{10,2},{3,11},{11,3},{4,12},{12,4},... | collective-permute-start | bytes 589832 | tf_op jit(solution)/shard_map/ppermute | solution.py:409
  29.1 6.5 %collective-permute-start.5 = (bf16[96,1024]{1,0:T(8,128)(2,1)S(1)}, bf16[96,1024]{1,0:T(8,128)(2,1)S(1)}, u32[]{:S(2)}, u32[]{:S(2)}) collective-permute-start(bf16[96,1024]{1,0:T(8,128)(2,1)S(1)} %collective-permute-done.1.refs_1_), channel_id=1, source_target_pairs={{0,8},{8,0},{1,9},{9,1},{2,10},{10,2},{3,11},{11,3},{4,12},{12,4},... | collective-permute-start | bytes 589832 | tf_op jit(solution)/shard_map/ppermute | solution.py:409
  30.3 5.3 %collective-permute-start.8 = (s32[384]{0:T(512)S(1)}, s32[384]{0:T(512)S(1)}, u32[]{:S(2)}, u32[]{:S(2)}) collective-permute-start(s32[384]{0:T(512)S(1)} %copy-done.2), channel_id=1, source_target_pairs={{0,128},{128,0},{1,129},{129,1},{2,130},{130,2},{3,131},{131,3},{4... | collective-permute-start | bytes 4616 | tf_op jit(solution)/shard_map/ppermute | solution.py:392
  42.0 3.2 %collective-permute-start.9 = (f32[1,1024]{1,0:T(1,128)S(1)}, f32[1,1024]{1,0:T(1,128)S(1)}, u32[]{:S(2)}, u32[]{:S(2)}) collective-permute-start(f32[1,1024]{1,0:T(1,128)S(1)} %get-tuple-element.27), channel_id=1, source_target_pairs={{0,8},{8,0},{1,9},{9,1},{2,10},{10,2},{3,11},{11,3},{4,12},{12,4},... | collective-permute-start | bytes 12296 | tf_op jit(solution)/shard_map/ppermute | solution.py:427
  45.2 5.4 %collective-permute-start.12 = (f32[1,1792]{1,0:T(1,128)S(1)}, f32[1,1792]{1,0:T(1,128)S(1)}, u32[]{:S(2)}, u32[]{:S(2)}) collective-permute-start(f32[1,1792]{1,0:T(1,128)S(1)} %meet.1.mine), channel_id=1, source_target_pairs={{0,32},{1,33},{2,34},{3,35},{4,36},{5,37},{6,38},{7,39},{8,9},{9,8... | collective-permute-start | bytes 21512 | tf_op jit(solution)/shard_map/ppermute | solution.py:53
  49.2 2.5 %collective-permute-start.11 = (f32[1,1792]{1,0:T(1,128)S(1)}, f32[1,1792]{1,0:T(1,128)S(1)}, u32[]{:S(2)}, u32[]{:S(2)}) collective-permute-start(f32[1,1792]{1,0:T(1,128)S(1)} %meet.1.mine), channel_id=1, source_target_pairs={{0,112},{1,113},{2,114},{3,115},{4,116},{5,117},{6,118},{7,119},{8... | collective-permute-start | bytes 21512 | tf_op jit(solution)/shard_map/ppermute | solution.py:53
  49.4 3.7 %collective-permute-start.10 = (f32[1,1792]{1,0:T(1,128)S(1)}, f32[1,1792]{1,0:T(1,128)S(1)}, u32[]{:S(2)}, u32[]{:S(2)}) collective-permute-start(f32[1,1792]{1,0:T(1,128)S(1)} %meet.1.mine), channel_id=1, source_target_pairs={{0,16},{1,17},{2,18},{3,19},{4,20},{5,21},{6,22},{7,23},{8,136},{9... | collective-permute-start | bytes 21512 | tf_op jit(solution)/shard_map/ppermute | solution.py:53
  53.1 5.9 %collective-permute-start.15 = (f32[1,1792]{1,0:T(1,128)S(1)}, f32[1,1792]{1,0:T(1,128)S(1)}, u32[]{:S(2)}, u32[]{:S(2)}) collective-permute-start(f32[1,1792]{1,0:T(1,128)S(1)} %round.1.mine), channel_id=1, source_target_pairs={{0,64},{1,65},{2,66},{3,67},{4,68},{5,69},{6,70},{7,71},{8,12},{9,... | collective-permute-start | bytes 21512 | tf_op jit(solution)/shard_map/ppermute | solution.py:53
  53.6 5.4 %collective-permute-start.14 = (f32[1,1792]{1,0:T(1,128)S(1)}, f32[1,1792]{1,0:T(1,128)S(1)}, u32[]{:S(2)}, u32[]{:S(2)}) collective-permute-start(f32[1,1792]{1,0:T(1,128)S(1)} %round.1.mine), channel_id=1, source_target_pairs={{8,14},{9,15},{10,8},{11,9},{12,10},{13,11},{14,12},{15,13},{24,30... | collective-permute-start | bytes 21512 | tf_op jit(solution)/shard_map/ppermute | solution.py:53
  57.1 5.6 %collective-permute-start.13 = (f32[1,1792]{1,0:T(1,128)S(1)}, f32[1,1792]{1,0:T(1,128)S(1)}, u32[]{:S(2)}, u32[]{:S(2)}) collective-permute-start(f32[1,1792]{1,0:T(1,128)S(1)} %round.1.mine), channel_id=1, source_target_pairs={{8,10},{9,11},{10,12},{11,13},{12,14},{13,15},{14,8},{15,9},{24,26... | collective-permute-start | bytes 21512 | tf_op jit(solution)/shard_map/ppermute | solution.py:53
  62.7 1.3 %collective-permute-start.16 = (f32[1,1024]{1,0:T(1,128)S(1)}, f32[1,1024]{1,0:T(1,128)S(1)}, u32[]{:S(2)}, u32[]{:S(2)}) collective-permute-start(f32[1,1024]{1,0:T(1,128)S(1)} %get-tuple-element.29), channel_id=1, source_target_pairs={{0,8},{8,0},{1,9},{9,1},{2,10},{10,2},{3,11},{11,3},{4,12},{12,4},... | collective-permute-start | bytes 12296 | tf_op jit(solution)/shard_map/ppermute | solution.py:435
  69.1 4.9 %collective-permute-start.17 = (bf16[400,1024]{1,0:T(8,128)(2,1)}, bf16[400,1024]{1,0:T(8,128)(2,1)S(1)}, u32[]{:S(2)}, u32[]{:S(2)}) collective-permute-start(bf16[400,1024]{1,0:T(8,128)(2,1)} %get-tuple-element.36), channel_id=1, source_target_pairs={{0,8},{8,0},{1,9},{9,1},{2,10},{10,2},{3,11},{11,3},{4,12},{12,4},... | collective-permute-start | bytes 2457608 | tf_op jit(solution)/shard_map/ppermute | solution.py:462
  69.3 31.2 %all-to-all-start.1 = ((bf16[16,400,128]{2,1,0:T(8,128)(2,1)}), bf16[16,400,128]{2,1,0:T(8,128)(2,1)S(1)}, u32[]{:S(2)}, u32[]{:S(2)}) async-start(bf16[16,400,128]{2,1,0:T(8,128)(2,1)} %get-tuple-element.33), calls=%async_computation.1 | async-start | bytes 3276800 | tf_op jit(solution)/shard_map/all_to_all | solution.py:457
  75.1 11.7 %collective-permute-start.18 = (bf16[784,128]{1,0:T(8,128)(2,1)S(1)}, bf16[784,128]{1,0:T(8,128)(2,1)S(1)}, u32[]{:S(2)}, u32[]{:S(2)}) collective-permute-start(bf16[784,128]{1,0:T(8,128)(2,1)S(1)} %get-tuple-element.39), channel_id=1, source_target_pairs={{0,16},{16,32},{32,48},{48,64},{64,80},{80,96},{96,112},{112,0},{1... | collective-permute-start | bytes 602120 | tf_op jit(solution)/shard_map/ppermute | solution.py:32
  75.2 11.6 %collective-permute-start.19 = (bf16[784,128]{1,0:T(8,128)(2,1)S(1)}, bf16[784,128]{1,0:T(8,128)(2,1)S(1)}, u32[]{:S(2)}, u32[]{:S(2)}) collective-permute-start(bf16[784,128]{1,0:T(8,128)(2,1)S(1)} %get-tuple-element.40), channel_id=1, source_target_pairs={{0,32},{16,112},{32,64},{48,16},{64,96},{80,48},{96,0},{112,80},{1... | collective-permute-start | bytes 602120 | tf_op jit(solution)/shard_map/ppermute | solution.py:32
  76.1 11.6 %collective-permute-start.20 = (bf16[784,128]{1,0:T(8,128)(2,1)S(1)}, bf16[784,128]{1,0:T(8,128)(2,1)S(1)}, u32[]{:S(2)}, u32[]{:S(2)}) collective-permute-start(bf16[784,128]{1,0:T(8,128)(2,1)S(1)} %get-tuple-element.41), channel_id=1, source_target_pairs={{0,112},{16,0},{32,16},{48,32},{64,48},{80,64},{96,80},{112,96},{1... | collective-permute-start | bytes 602120 | tf_op jit(solution)/shard_map/ppermute | solution.py:32
  88.1 8.3 %collective-permute-start.21 = (bf16[400,128]{1,0:T(8,128)(2,1)S(1)}, bf16[400,128]{1,0:T(8,128)(2,1)S(1)}, u32[]{:S(2)}, u32[]{:S(2)}) collective-permute-start(bf16[400,128]{1,0:T(8,128)(2,1)S(1)} %get-tuple-element.44), channel_id=1, source_target_pairs={{0,64},{16,80},{32,96},{48,112},{64,0},{80,16},{96,32},{112,48},{1... | collective-permute-start | bytes 307208 | tf_op jit(solution)/shard_map/ppermute | solution.py:22

commit v15 on v14

--- a/solution.py
+++ b/solution.py
@@ -55,7 +55,7 @@
 
 def merge(parts):
     high = functools.reduce(jnp.maximum, parts)
-    return high + jnp.log(sum(jnp.exp(p - high) for p in parts))
+    return high + jnp.log2(sum(jnp.exp2(p - high) for p in parts))
 
 
 def encode(scaled):
@@ -111,10 +111,12 @@
     )(*args)
 
 
-def copies_body(source, out, sems):
-    copies = [
-        pltpu.make_async_copy(source, out.at[i], sems.at[i]) for i in range(out.shape[0])
-    ]
+def copies_body(source, out, held, sems):
+    count = out.shape[0]
+    load = pltpu.make_async_copy(source, held, sems.at[count])
+    load.start()
+    load.wait()
+    copies = [pltpu.make_async_copy(held, out.at[i], sems.at[i]) for i in range(count)]
     for copy in copies:
         copy.start()
     for copy in copies:
@@ -159,6 +161,7 @@
                     k * rows : (k + 1) * rows, :
                 ]
     lanes = []
+    col_top = jnp.full((1, size), -1e38, F32)
     step = 256
     for r in range(0, size, step):
         tile = (
@@ -168,17 +171,17 @@
                 (((1,), (1,)), ((), ())),
                 preferred_element_type=F32,
             )
-            * inv_root
+            * (inv_root / math.log(2.0))
         )
         scores[r : r + step, :] = tile
+        col_top = jnp.maximum(col_top, jnp.max(tile, axis=0, keepdims=True))
         top = jnp.max(tile, axis=1, keepdims=True)
-        part = jnp.log(jnp.sum(jnp.exp(tile - top), axis=1, keepdims=True))
+        part = jnp.log2(jnp.sum(jnp.exp2(tile - top), axis=1, keepdims=True))
         lanes.append(to_row(top + part))
         hit = to_column(pair[:, r : r + step]) == ids
         found += jnp.sum(jnp.where(hit, tile, 0.0), axis=0, keepdims=True)
-    tile = scores[...]
-    top = jnp.max(tile, axis=0, keepdims=True)
-    col = top + jnp.log(jnp.sum(jnp.exp(tile - top), axis=0, keepdims=True))
+    mass = jnp.exp2(scores[...] - col_top)
+    col = col_top + jnp.log2(jnp.sum(mass, axis=0, keepdims=True))
     image_max = jnp.max(jnp.abs(image[...].astype(F32)))
     zero = jnp.zeros((1, LANES), F32)
     rows_out = jnp.concatenate([*lanes, zero + jnp.max(high), zero], axis=1)
@@ -256,8 +259,8 @@
     terms[...] = jnp.concatenate(
         [row_terms, text_max, image_max, jnp.zeros((5, LANES), F32)], axis=0
     )
-    row_column = to_column(row_lse + math.log(2.0))
-    col_row = col_lse + math.log(2.0)
+    row_column = to_column(row_lse + 1.0)
+    col_row = col_lse + 1.0
     pair_column = to_column(pair[...])
     extra = split3(col_terms)
     scale = inverse(text_max[:, :1]) * inv_root
@@ -266,7 +269,7 @@
     for r in range(0, size, step):
         at = slice(r, r + step)
         tile = scores[at, :]
-        probs = jnp.exp(tile - row_column[at, :]) + jnp.exp(tile - col_row)
+        probs = jnp.exp2(tile - row_column[at, :]) + jnp.exp2(tile - col_row)
         grad = (probs - jnp.where(pair_column[at, :] == ids, 1.0, 0.0)).astype(BF16)
         grads[at, :] = grad
         part = encode(jnp.dot(grad, text[...], preferred_element_type=F32) * scale)
@@ -358,15 +361,16 @@
     pack(far, [block], split3(sums))
 
 
-def text_sum_body(near, total, terms, pay, out, side):
+def text_sum_body(pairs, near, total, terms, side, pay, out, loss):
     rows, width = out.shape
     unit = terms[2:3, :1]
     unit = jnp.where(unit > 0, unit, 1.0)
     out[...] = unit * (near[...] + unpack([pay], 0, rows, width))
-    side[...] = total[...] + tails([pay])
-
-
-def image_sum_body(pairs, got, terms, side, out, loss):
+    full = total[...] + side[...] + tails([pay])
+    loss[0, 0] = jnp.max(full) * (math.log(2.0) / (2.0 * pairs))
+
+
+def image_sum_body(got, terms, out, side):
     rows, width = out.shape
     unit = terms[1:2, :1]
     unit = jnp.where(unit > 0, unit, 1.0)
@@ -374,8 +378,7 @@
     for k in range(width // LANES):
         at = slice(k * rows, (k + 1) * rows)
         out[:, k * LANES : (k + 1) * LANES] = unit * sum(decode(p[at, :]) for p in pays)
-    full = side[...] + tails(pays)
-    loss[0, 0] = jnp.max(full) / (2.0 * pairs)
+    side[...] = tails(pays)
 
 
 def shards(image_embed, text_embed, pair_index):
@@ -390,14 +393,14 @@
     tall = width // LANES * rows + EXTRA
 
     pair_seen = lax.ppermute(pair_index, "xl", SWAP)
-    (copies,) = call(
+    copies = pl.pallas_call(
         copies_body,
-        (pltpu.HBM((n_plane, rows, width), BF16),),
-        (image_embed,),
-        "copies",
-        hbm_out=(0,),
-        scratch=[pltpu.SemaphoreType.DMA((n_plane,))],
-    )
+        out_shape=pltpu.HBM((n_plane, rows, width), BF16),
+        in_specs=[pl.BlockSpec(memory_space=pl.ANY)],
+        out_specs=pl.BlockSpec(memory_space=pltpu.HBM),
+        scratch_shapes=[pltpu.VMEM((rows, width), BF16), pltpu.SemaphoreType.DMA((n_plane + 1,))],
+        name="copies",
+    )(image_embed)
     image = lax.all_to_all(copies, PLANE, 0, 0).reshape(size, width)
 
     steps = [q if q <= n_z // 4 else q - n_z // 2 for q in range(n_z // 2)]
@@ -472,19 +475,20 @@
         "relay",
         size=1,
     )
-    grad_text, side = call(
-        text_sum_body,
+    grad_image, side = call(
+        image_sum_body,
         (shape((rows, width), F32), shape((1, LANES), F32)),
-        (near, total, terms, turn(far, "z", n_z // 2)),
+        (image_got, terms),
+        "image_sum",
+        size=1,
+    )
+    grad_text, loss = call(
+        functools.partial(text_sum_body, pairs),
+        (shape((rows, width), F32), shape((1, 1), F32)),
+        (near, total, terms, side, turn(far, "z", n_z // 2)),
         "text_sum",
+        smem_out=1,
         size=1,
-    )
-    grad_image, loss = call(
-        functools.partial(image_sum_body, pairs),
-        (shape((rows, width), F32), shape((1, 1), F32)),
-        (image_got, terms, side),
-        "image_sum",
-        smem_out=1,
     )
     return (loss[0, 0], grad_image, grad_text)
 

time: 103 us -> 103 us (level)
    all_to_all x1, waiting for transfers between devices: 3.26 us -> 11.3 us  [shards(): image_got = lax.all_to_all(image_sent, PLANE, 0, 0)]
    ppermute x2, waiting for transfers between devices: 7.54 us -> 0.01 us  [turn(): lax.ppermute(x, axis, [(i, (i + step) % count) for i in range(count)])]
    pallas_call x0 -> x1, Pallas kernels: none -> 2.22 us  [shards(): pl.pallas_call(copies_body, out_shape=pltpu.HBM((n_plane, rows, width), B...]
    pallas_call x11 -> x10, Pallas kernels: 13.5 us -> 11.7 us  [call(): pl.pallas_call(body, out_shape=outs, in_specs=[pl.BlockSpec(memory_space=...]
  transfers between devices with their start and end apart: 24 -> 24, of which waited for: 13 -> 12; matrix products, arithmetic and copies ran while one was open for 0% -> 0% of each run, Pallas kernels for 2% -> 4%
where the time goes in v15:
time: 103 us; the launch traced here: 102 us
  starting transfers between devices  50.2 us (49%)
  waiting for transfers between devices  37.3 us (36%)
  Pallas kernels  14 us (14%)
    pallas_call x10, Pallas kernels, call(): pl.pallas_call(body, out_shape=outs, in_specs=[pl.BlockSpec(memory_space=...  11.7 us
    all_to_all x1, waiting for transfers between devices, shards(): image_got = lax.all_to_all(image_sent, PLANE, 0, 0)  11.3 us
    ppermute x6, starting transfers between devices, turn_both(): return lax.ppermute(x, AXES, pairs)  11.3 us
    ppermute x6, waiting for transfers between devices, turn_z(): return lax.ppermute(x, 'z', pairs if back else [(b, a) for a, b in pairs])  10.7 us
    ppermute x2, starting transfers between devices, turn(): lax.ppermute(x, axis, [(i, (i + step) % count) for i in range(count)])  8.86 us
    ppermute x4, starting transfers between devices, shards(): pieces = pieces + [lax.ppermute(piece, 'c', SWAP) for piece in pieces]  7.89 us
    all_to_all x1, starting transfers between devices, shards(): image = lax.all_to_all(copies, PLANE, 0, 0).reshape(size, width)  6.9 us
    ppermute x6, starting transfers between devices, turn_z(): return lax.ppermute(x, 'z', pairs if back else [(b, a) for a, b in pairs])  6.7 us
  transfers between devices with their start and end apart: 24, of which 12 were waited for; matrix products, arithmetic and copies ran while one was open for 0% of the time, Pallas kernels for 4%

profile of v15, /device:TPU:1, one launch (start us, length us, event | category | flops | bytes accessed | tf_op | source)
XLA Modules:
  0.0 102.5 jit_solution(15759354077854959891)
XLA Ops:
  0.6 7.8 %collective-permute-start = (bf16[48,1024]{1,0:T(8,128)(2,1)}, bf16[48,1024]{1,0:T(8,128)(2,1)S(1)}, u32[]{:S(2)}, u32[]{:S(2)}) collective-permute-start(bf16[48,1024]{1,0:T(8,128)(2,1)} %near.1), channel_id=1, source_target_pairs={{0,64},{16,80},{32,96},{48,112},{64,0},{80,16},{96,32},{112,48},{1... | collective-permute-start | bytes 294920 | tf_op jit(solution)/shard_map/ppermute | solution.py:22
  8.5 2.2 %copies.1 = bf16[16,48,1024]{2,1,0:T(8,128)(2,1)} custom-call(bf16[48,1024]{1,0:T(8,128)(2,1)} %source.1), custom_call_target="tpu_custom_call" | custom-call | tf_op jit(solution)/shard_map/copies/pallas_call | solution.py:396
  10.7 0.0 copy-start
  10.7 6.9 %all-to-all-start = ((bf16[16,48,1024]{2,1,0:T(8,128)(2,1)}), bf16[16,48,1024]{2,1,0:T(8,128)(2,1)S(1)}, u32[]{:S(2)}, u32[]{:S(2)}) async-start(bf16[16,48,1024]{2,1,0:T(8,128)(2,1)} %copies.1), calls=%async_computation | async-start | bytes 3145728 | tf_op jit(solution)/shard_map/all_to_all | solution.py:404
  17.6 0.0 copy-start.1
  17.7 0.8 collective-permute-start.3
  18.5 0.3 collective-permute-start.2
  18.7 2.9 %collective-permute-start.1 = (bf16[96,1024]{1,0:T(8,128)(2,1)S(1)}, bf16[96,1024]{1,0:T(8,128)(2,1)S(1)}, u32[]{:S(2)}, u32[]{:S(2)}) collective-permute-start(bf16[96,1024]{1,0:T(8,128)(2,1)S(1)} %join.1.refs_0_), channel_id=1, source_target_pairs={{16,0},{32,16},{48,32},{64,48},{80,64},{96,80},{112,96},{0,112},{1... | collective-permute-start | bytes 589832 | tf_op jit(solution)/shard_map/ppermute | solution.py:32
  21.6 2.1 %collective-permute-start.4 = (bf16[96,1024]{1,0:T(8,128)(2,1)S(1)}, bf16[96,1024]{1,0:T(8,128)(2,1)S(1)}, u32[]{:S(2)}, u32[]{:S(2)}) collective-permute-start(bf16[96,1024]{1,0:T(8,128)(2,1)S(1)} %join.1.refs_0_), channel_id=1, source_target_pairs={{0,8},{8,0},{1,9},{9,1},{2,10},{10,2},{3,11},{11,3},{4,12},{12,4},... | collective-permute-start | bytes 589832 | tf_op jit(solution)/shard_map/ppermute | solution.py:412
  23.7 0.4 collective-permute-done.3.refs_3_
  24.1 3.9 %collective-permute-start.7 = (bf16[96,1024]{1,0:T(8,128)(2,1)S(1)}, bf16[96,1024]{1,0:T(8,128)(2,1)S(1)}, u32[]{:S(2)}, u32[]{:S(2)}) collective-permute-start(bf16[96,1024]{1,0:T(8,128)(2,1)S(1)} %collective-permute-done.3.refs_3_), channel_id=1, source_target_pairs={{0,8},{8,0},{1,9},{9,1},{2,10},{10,2},{3,11},{11,3},{4,12},{12,4},... | collective-permute-start | bytes 589832 | tf_op jit(solution)/shard_map/ppermute | solution.py:412
  28.0 0.0 collective-permute-done.2.refs_2_
  28.0 0.7 collective-permute-start.6
  28.7 0.4 collective-permute-done.1.refs_1_
  29.1 1.2 %collective-permute-start.5 = (bf16[96,1024]{1,0:T(8,128)(2,1)S(1)}, bf16[96,1024]{1,0:T(8,128)(2,1)S(1)}, u32[]{:S(2)}, u32[]{:S(2)}) collective-permute-start(bf16[96,1024]{1,0:T(8,128)(2,1)S(1)} %collective-permute-done.1.refs_1_), channel_id=1, source_target_pairs={{0,8},{8,0},{1,9},{9,1},{2,10},{10,2},{3,11},{11,3},{4,12},{12,4},... | collective-permute-start | bytes 589832 | tf_op jit(solution)/shard_map/ppermute | solution.py:412
  30.3 1.4 %collective-permute-start.8 = (s32[384]{0:T(512)S(1)}, s32[384]{0:T(512)S(1)}, u32[]{:S(2)}, u32[]{:S(2)}) collective-permute-start(s32[384]{0:T(512)S(1)} %copy-done.1), channel_id=1, source_target_pairs={{0,128},{128,0},{1,129},{129,1},{2,130},{130,2},{3,131},{131,3},{4... | collective-permute-start | bytes 4616 | tf_op jit(solution)/shard_map/ppermute | solution.py:395
  31.6 4.0 %collective-permute-done.8.refs_10_ = s32[384]{0:T(512)S(1)} collective-permute-done((s32[384]{0:T(512)S(1)}, s32[384]{0:T(512)S(1)}, u32[]{:S(2)}, u32[]{:S(2)}) %collective-permute-start.8) | collective-permute-done | bytes 1568 | tf_op jit(solution)/shard_map/ppermute | solution.py:395
  35.6 0.0 collective-permute-done.6.refs_6_
  35.6 0.0 collective-permute-done.5.refs_5_
  35.6 3.3 %all-to-all-done = bf16[16,48,1024]{2,1,0:T(8,128)(2,1)S(1)} async-done(((bf16[16,48,1024]{2,1,0:T(8,128)(2,1)}), bf16[16,48,1024]{2,1,0:T(8,128)(2,1)S(1)}, u32[]{:S(2)}, u32[]{:S(2)}) %all-to-all-start) | async-done | bytes 1572896 | tf_op jit(solution)/shard_map/all_to_all | solution.py:404
  39.0 2.8 %scores.1 = (f32[1,768]{1,0:T(1,128)S(1)}, f32[768,768]{1,0:T(8,128)S(1)}, bf16[768,1024]{1,0:T(8,128)(2,1)S(1)}, f32[1,1024]{1,0:T(1,128)S(1)}, f32[1,1024]{1,0:T(1,128)S(1)}) custom-call(bf16[96,1024]{1,0:T(8,128)(2,1)S(1)} %join.1.refs_0_, bf16[96,1024]{1,0:T(8,128)(2,1)S(1)} %collective-permute-done.1.refs_1_, ...), custom_call_target="tpu_custom_call" | custom-call | flops 1207959552 | bytes 7092224 | tf_op jit(solution)/shard_map/scores/pallas_call | solution.py:102
  41.8 2.4 %collective-permute-start.9 = (f32[1,1024]{1,0:T(1,128)S(1)}, f32[1,1024]{1,0:T(1,128)S(1)}, u32[]{:S(2)}, u32[]{:S(2)}) collective-permute-start(f32[1,1024]{1,0:T(1,128)S(1)} %get-tuple-element.27), channel_id=1, source_target_pairs={{0,8},{8,0},{1,9},{9,1},{2,10},{10,2},{3,11},{11,3},{4,12},{12,4},... | collective-permute-start | bytes 12296 | tf_op jit(solution)/shard_map/ppermute | solution.py:430
  44.2 0.8 collective-permute-done.9.seen
  45.0 3.9 %collective-permute-start.12 = (f32[1,1792]{1,0:T(1,128)S(1)}, f32[1,1792]{1,0:T(1,128)S(1)}, u32[]{:S(2)}, u32[]{:S(2)}) collective-permute-start(f32[1,1792]{1,0:T(1,128)S(1)} %meet.1.mine), channel_id=1, source_target_pairs={{0,32},{1,33},{2,34},{3,35},{4,36},{5,37},{6,38},{7,39},{8,9},{9,8... | collective-permute-start | bytes 21512 | tf_op jit(solution)/shard_map/ppermute | solution.py:53
  48.9 0.2 collective-permute-start.11
  49.1 1.3 %collective-permute-start.10 = (f32[1,1792]{1,0:T(1,128)S(1)}, f32[1,1792]{1,0:T(1,128)S(1)}, u32[]{:S(2)}, u32[]{:S(2)}) collective-permute-start(f32[1,1792]{1,0:T(1,128)S(1)} %meet.1.mine), channel_id=1, source_target_pairs={{0,16},{1,17},{2,18},{3,19},{4,20},{5,21},{6,22},{7,23},{8,136},{9... | collective-permute-start | bytes 21512 | tf_op jit(solution)/shard_map/ppermute | solution.py:53
  50.4 1.0 collective-permute-done.11.two
  51.4 1.4 %collective-permute-done.10.one = f32[1,1792]{1,0:T(1,128)S(1)} collective-permute-done((f32[1,1792]{1,0:T(1,128)S(1)}, f32[1,1792]{1,0:T(1,128)S(1)}, u32[]{:S(2)}, u32[]{:S(2)}) %collective-permute-start.10) | collective-permute-done | bytes 7200 | tf_op jit(solution)/shard_map/ppermute | solution.py:53
  52.9 0.3 collective-permute-start.15
  53.2 3.6 %collective-permute-start.14 = (f32[1,1792]{1,0:T(1,128)S(1)}, f32[1,1792]{1,0:T(1,128)S(1)}, u32[]{:S(2)}, u32[]{:S(2)}) collective-permute-start(f32[1,1792]{1,0:T(1,128)S(1)} %round.1.mine), channel_id=1, source_target_pairs={{8,14},{9,15},{10,8},{11,9},{12,10},{13,11},{14,12},{15,13},{24,30... | collective-permute-start | bytes 21512 | tf_op jit(solution)/shard_map/ppermute | solution.py:53
  56.8 1.9 %collective-permute-start.13 = (f32[1,1792]{1,0:T(1,128)S(1)}, f32[1,1792]{1,0:T(1,128)S(1)}, u32[]{:S(2)}, u32[]{:S(2)}) collective-permute-start(f32[1,1792]{1,0:T(1,128)S(1)} %round.1.mine), channel_id=1, source_target_pairs={{8,10},{9,11},{10,12},{11,13},{12,14},{13,15},{14,8},{15,9},{24,26... | collective-permute-start | bytes 21512 | tf_op jit(solution)/shard_map/ppermute | solution.py:53
  58.8 3.6 %collective-permute-done.13.one = f32[1,1792]{1,0:T(1,128)S(1)} collective-permute-done((f32[1,1792]{1,0:T(1,128)S(1)}, f32[1,1792]{1,0:T(1,128)S(1)}, u32[]{:S(2)}, u32[]{:S(2)}) %collective-permute-start.13) | collective-permute-done | bytes 7200 | tf_op jit(solution)/shard_map/ppermute | solution.py:53
  62.5 0.1 collective-permute-start.16
  62.6 1.2 %collective-permute-done.16.refs_1_ = f32[1,1024]{1,0:T(1,128)S(1)} collective-permute-done((f32[1,1024]{1,0:T(1,128)S(1)}, f32[1,1024]{1,0:T(1,128)S(1)}, u32[]{:S(2)}, u32[]{:S(2)}) %collective-permute-start.16) | collective-permute-done | bytes 4128 | tf_op jit(solution)/shard_map/ppermute | solution.py:438
  63.7 5.0 %grads.1 = (f32[8,128]{1,0:T(8,128)S(1)}, bf16[384,1024]{1,0:T(8,128)(2,1)S(1)}, bf16[400,1024]{1,0:T(8,128)(2,1)}, bf16[16,400,128]{2,1,0:T(8,128)(2,1)}) custom-call(f32[1,1792]{1,0:T(1,128)S(1)} %get-tuple-element.28.refs_0_, f32[1,1024]{1,0:T(1,128)S(1)} %collective-permute-done.16.refs_1_, f32[768,768]{1,0:T(8,128)S(1)} %get-tuple-element.30.refs_2_, ...), custom_call_target="tpu_custom_call" | custom-call | flops 2415919104 | bytes 8767488 | tf_op jit(solution)/shard_map/grads/pallas_call | solution.py:102
  68.7 0.3 collective-permute-start.17
  69.0 4.4 %all-to-all-start.1 = ((bf16[16,400,128]{2,1,0:T(8,128)(2,1)}), bf16[16,400,128]{2,1,0:T(8,128)(2,1)S(1)}, u32[]{:S(2)}, u32[]{:S(2)}) async-start(bf16[16,400,128]{2,1,0:T(8,128)(2,1)} %get-tuple-element.43), calls=%async_computation.1 | async-start | bytes 3276800 | tf_op jit(solution)/shard_map/all_to_all | solution.py:460
  73.5 1.1 %send.1 = (f32[96,1024]{1,0:T(8,128)S(1)}, f32[1,128]{1,0:T(1,128)S(1)}, bf16[784,128]{1,0:T(8,128)(2,1)S(1)}, bf16[784,128]{1,0:T(8,128)(2,1)S(1)}, bf16[784,128]{1,0:T(8,128)(2,1)S(1)}) custom-call(bf16[384,1024]{1,0:T(8,128)(2,1)S(1)} %get-tuple-element.33.own, bf16[400,1024]{1,0:T(8,128)(2,1)S(1)} %collective-permute-done.17.seen, ...), custom_call_target="tpu_custom_call" | custom-call | flops 10000000000 | bytes 1 | tf_op jit(solution)/shard_map/send/pallas_call | solution.py:102
  74.5 0.1 collective-permute-start.18
  74.6 1.2 %collective-permute-start.19 = (bf16[784,128]{1,0:T(8,128)(2,1)S(1)}, bf16[784,128]{1,0:T(8,128)(2,1)S(1)}, u32[]{:S(2)}, u32[]{:S(2)}) collective-permute-start(bf16[784,128]{1,0:T(8,128)(2,1)S(1)} %get-tuple-element.39), channel_id=1, source_target_pairs={{0,32},{16,112},{32,64},{48,16},{64,96},{80,48},{96,0},{112,80},{1... | collective-permute-start | bytes 602120 | tf_op jit(solution)/shard_map/ppermute | solution.py:32
  75.8 1.5 %collective-permute-start.20 = (bf16[784,128]{1,0:T(8,128)(2,1)S(1)}, bf16[784,128]{1,0:T(8,128)(2,1)S(1)}, u32[]{:S(2)}, u32[]{:S(2)}) collective-permute-start(bf16[784,128]{1,0:T(8,128)(2,1)S(1)} %get-tuple-element.40), channel_id=1, source_target_pairs={{0,112},{16,0},{32,16},{48,32},{64,48},{80,64},{96,80},{112,96},{1... | collective-permute-start | bytes 602120 | tf_op jit(solution)/shard_map/ppermute | solution.py:32
  77.3 8.9 %collective-permute-done.18.refs_0_ = bf16[784,128]{1,0:T(8,128)(2,1)S(1)} collective-permute-done((bf16[784,128]{1,0:T(8,128)(2,1)S(1)}, bf16[784,128]{1,0:T(8,128)(2,1)S(1)}, u32[]{:S(2)}, u32[]{:S(2)}) %collective-permute-start.18) | collective-permute-done | bytes 200736 | tf_op jit(solution)/shard_map/ppermute | solution.py:32
  86.2 1.0 collective-permute-done.20.refs_2_
  87.2 0.4 relay.1
  87.6 1.0 %collective-permute-start.21 = (bf16[400,128]{1,0:T(8,128)(2,1)S(1)}, bf16[400,128]{1,0:T(8,128)(2,1)S(1)}, u32[]{:S(2)}, u32[]{:S(2)}) collective-permute-start(bf16[400,128]{1,0:T(8,128)(2,1)S(1)} %get-tuple-element.45), channel_id=1, source_target_pairs={{0,64},{16,80},{32,96},{48,112},{64,0},{80,16},{96,32},{112,48},{1... | collective-permute-start | bytes 307208 | tf_op jit(solution)/shard_map/ppermute | solution.py:22
  88.6 11.3 %all-to-all-done.1.got = bf16[16,400,128]{2,1,0:T(8,128)(2,1)S(1)} async-done(((bf16[16,400,128]{2,1,0:T(8,128)(2,1)}), bf16[16,400,128]{2,1,0:T(8,128)(2,1)S(1)}, u32[]{:S(2)}, u32[]{:S(2)}) %all-to-all-start.1) | async-done | bytes 1638432 | tf_op jit(solution)/shard_map/all_to_all | solution.py:460
  99.9 1.6 %image_sum.1 = (f32[48,1024]{1,0:T(8,128)}, f32[1,128]{1,0:T(1,128)S(1)}) custom-call(bf16[16,400,128]{2,1,0:T(8,128)(2,1)S(1)} %all-to-all-done.1.got, f32[8,128]{1,0:T(8,128)S(1)} %get-tuple-element.35.terms), custom_call_target="tpu_custom_call" | custom-call | bytes 1 | tf_op jit(solution)/shard_map/image_sum/pallas_call | solution.py:102
  101.5 0.8 text_sum.1
  (15 shorter events, 0.1 us)
Async XLA Ops:
  0.6 17.0 %collective-permute-start = (bf16[48,1024]{1,0:T(8,128)(2,1)}, bf16[48,1024]{1,0:T(8,128)(2,1)S(1)}, u32[]{:S(2)}, u32[]{:S(2)}) collective-permute-start(bf16[48,1024]{1,0:T(8,128)(2,1)} %near.1), channel_id=1, source_target_pairs={{0,64},{16,80},{32,96},{48,112},{64,0},{80,16},{96,32},{112,48},{1... | collective-permute-start | bytes 294920 | tf_op jit(solution)/shard_map/ppermute | solution.py:22
  10.7 6.9 %copy-start = (bf16[48,1024]{1,0:T(8,128)(2,1)S(1)}, bf16[48,1024]{1,0:T(8,128)(2,1)}, u32[]{:S(2)}) copy-start(bf16[48,1024]{1,0:T(8,128)(2,1)} %near.1) | copy-start | bytes 294916
  10.7 28.3 %all-to-all-start = ((bf16[16,48,1024]{2,1,0:T(8,128)(2,1)}), bf16[16,48,1024]{2,1,0:T(8,128)(2,1)S(1)}, u32[]{:S(2)}, u32[]{:S(2)}) async-start(bf16[16,48,1024]{2,1,0:T(8,128)(2,1)} %copies.1), calls=%async_computation | async-start | bytes 3145728 | tf_op jit(solution)/shard_map/all_to_all | solution.py:404
  17.6 12.7 %copy-start.1 = (s32[384]{0:T(512)S(1)}, s32[384]{0:T(512)}, u32[]{:S(2)}) copy-start(s32[384]{0:T(512)} %refs_9_.1) | copy-start | bytes 4612
  17.7 6.4 %collective-permute-start.3 = (bf16[96,1024]{1,0:T(8,128)(2,1)S(1)}, bf16[96,1024]{1,0:T(8,128)(2,1)S(1)}, u32[]{:S(2)}, u32[]{:S(2)}) collective-permute-start(bf16[96,1024]{1,0:T(8,128)(2,1)S(1)} %join.1.refs_0_), channel_id=1, source_target_pairs={{112,0},{0,16},{16,32},{32,48},{48,64},{64,80},{80,96},{96,112},{1... | collective-permute-start | bytes 589832 | tf_op jit(solution)/shard_map/ppermute | solution.py:32
  18.5 9.6 %collective-permute-start.2 = (bf16[96,1024]{1,0:T(8,128)(2,1)S(1)}, bf16[96,1024]{1,0:T(8,128)(2,1)S(1)}, u32[]{:S(2)}, u32[]{:S(2)}) collective-permute-start(bf16[96,1024]{1,0:T(8,128)(2,1)S(1)} %join.1.refs_0_), channel_id=1, source_target_pairs={{32,0},{112,16},{64,32},{16,48},{96,64},{48,80},{0,96},{80,112},{3... | collective-permute-start | bytes 589832 | tf_op jit(solution)/shard_map/ppermute | solution.py:32
  18.7 10.3 %collective-permute-start.1 = (bf16[96,1024]{1,0:T(8,128)(2,1)S(1)}, bf16[96,1024]{1,0:T(8,128)(2,1)S(1)}, u32[]{:S(2)}, u32[]{:S(2)}) collective-permute-start(bf16[96,1024]{1,0:T(8,128)(2,1)S(1)} %join.1.refs_0_), channel_id=1, source_target_pairs={{16,0},{32,16},{48,32},{64,48},{80,64},{96,80},{112,96},{0,112},{1... | collective-permute-start | bytes 589832 | tf_op jit(solution)/shard_map/ppermute | solution.py:32
  21.6 14.0 %collective-permute-start.4 = (bf16[96,1024]{1,0:T(8,128)(2,1)S(1)}, bf16[96,1024]{1,0:T(8,128)(2,1)S(1)}, u32[]{:S(2)}, u32[]{:S(2)}) collective-permute-start(bf16[96,1024]{1,0:T(8,128)(2,1)S(1)} %join.1.refs_0_), channel_id=1, source_target_pairs={{0,8},{8,0},{1,9},{9,1},{2,10},{10,2},{3,11},{11,3},{4,12},{12,4},... | collective-permute-start | bytes 589832 | tf_op jit(solution)/shard_map/ppermute | solution.py:412
  24.1 11.5 %collective-permute-start.7 = (bf16[96,1024]{1,0:T(8,128)(2,1)S(1)}, bf16[96,1024]{1,0:T(8,128)(2,1)S(1)}, u32[]{:S(2)}, u32[]{:S(2)}) collective-permute-start(bf16[96,1024]{1,0:T(8,128)(2,1)S(1)} %collective-permute-done.3.refs_3_), channel_id=1, source_target_pairs={{0,8},{8,0},{1,9},{9,1},{2,10},{10,2},{3,11},{11,3},{4,12},{12,4},... | collective-permute-start | bytes 589832 | tf_op jit(solution)/shard_map/ppermute | solution.py:412
  28.0 7.6 %collective-permute-start.6 = (bf16[96,1024]{1,0:T(8,128)(2,1)S(1)}, bf16[96,1024]{1,0:T(8,128)(2,1)S(1)}, u32[]{:S(2)}, u32[]{:S(2)}) collective-permute-start(bf16[96,1024]{1,0:T(8,128)(2,1)S(1)} %collective-permute-done.2.refs_2_), channel_id=1, source_target_pairs={{0,8},{8,0},{1,9},{9,1},{2,10},{10,2},{3,11},{11,3},{4,12},{12,4},... | collective-permute-start | bytes 589832 | tf_op jit(solution)/shard_map/ppermute | solution.py:412
  29.1 6.5 %collective-permute-start.5 = (bf16[96,1024]{1,0:T(8,128)(2,1)S(1)}, bf16[96,1024]{1,0:T(8,128)(2,1)S(1)}, u32[]{:S(2)}, u32[]{:S(2)}) collective-permute-start(bf16[96,1024]{1,0:T(8,128)(2,1)S(1)} %collective-permute-done.1.refs_1_), channel_id=1, source_target_pairs={{0,8},{8,0},{1,9},{9,1},{2,10},{10,2},{3,11},{11,3},{4,12},{12,4},... | collective-permute-start | bytes 589832 | tf_op jit(solution)/shard_map/ppermute | solution.py:412
  30.3 5.3 %collective-permute-start.8 = (s32[384]{0:T(512)S(1)}, s32[384]{0:T(512)S(1)}, u32[]{:S(2)}, u32[]{:S(2)}) collective-permute-start(s32[384]{0:T(512)S(1)} %copy-done.1), channel_id=1, source_target_pairs={{0,128},{128,0},{1,129},{129,1},{2,130},{130,2},{3,131},{131,3},{4... | collective-permute-start | bytes 4616 | tf_op jit(solution)/shard_map/ppermute | solution.py:395
  41.8 3.2 %collective-permute-start.9 = (f32[1,1024]{1,0:T(1,128)S(1)}, f32[1,1024]{1,0:T(1,128)S(1)}, u32[]{:S(2)}, u32[]{:S(2)}) collective-permute-start(f32[1,1024]{1,0:T(1,128)S(1)} %get-tuple-element.27), channel_id=1, source_target_pairs={{0,8},{8,0},{1,9},{9,1},{2,10},{10,2},{3,11},{11,3},{4,12},{12,4},... | collective-permute-start | bytes 12296 | tf_op jit(solution)/shard_map/ppermute | solution.py:430
  45.0 5.4 %collective-permute-start.12 = (f32[1,1792]{1,0:T(1,128)S(1)}, f32[1,1792]{1,0:T(1,128)S(1)}, u32[]{:S(2)}, u32[]{:S(2)}) collective-permute-start(f32[1,1792]{1,0:T(1,128)S(1)} %meet.1.mine), channel_id=1, source_target_pairs={{0,32},{1,33},{2,34},{3,35},{4,36},{5,37},{6,38},{7,39},{8,9},{9,8... | collective-permute-start | bytes 21512 | tf_op jit(solution)/shard_map/ppermute | solution.py:53
  48.9 2.5 %collective-permute-start.11 = (f32[1,1792]{1,0:T(1,128)S(1)}, f32[1,1792]{1,0:T(1,128)S(1)}, u32[]{:S(2)}, u32[]{:S(2)}) collective-permute-start(f32[1,1792]{1,0:T(1,128)S(1)} %meet.1.mine), channel_id=1, source_target_pairs={{0,112},{1,113},{2,114},{3,115},{4,116},{5,117},{6,118},{7,119},{8... | collective-permute-start | bytes 21512 | tf_op jit(solution)/shard_map/ppermute | solution.py:53
  49.1 3.7 %collective-permute-start.10 = (f32[1,1792]{1,0:T(1,128)S(1)}, f32[1,1792]{1,0:T(1,128)S(1)}, u32[]{:S(2)}, u32[]{:S(2)}) collective-permute-start(f32[1,1792]{1,0:T(1,128)S(1)} %meet.1.mine), channel_id=1, source_target_pairs={{0,16},{1,17},{2,18},{3,19},{4,20},{5,21},{6,22},{7,23},{8,136},{9... | collective-permute-start | bytes 21512 | tf_op jit(solution)/shard_map/ppermute | solution.py:53
  52.9 5.9 %collective-permute-start.15 = (f32[1,1792]{1,0:T(1,128)S(1)}, f32[1,1792]{1,0:T(1,128)S(1)}, u32[]{:S(2)}, u32[]{:S(2)}) collective-permute-start(f32[1,1792]{1,0:T(1,128)S(1)} %round.1.mine), channel_id=1, source_target_pairs={{0,64},{1,65},{2,66},{3,67},{4,68},{5,69},{6,70},{7,71},{8,12},{9,... | collective-permute-start | bytes 21512 | tf_op jit(solution)/shard_map/ppermute | solution.py:53
  53.2 5.6 %collective-permute-start.14 = (f32[1,1792]{1,0:T(1,128)S(1)}, f32[1,1792]{1,0:T(1,128)S(1)}, u32[]{:S(2)}, u32[]{:S(2)}) collective-permute-start(f32[1,1792]{1,0:T(1,128)S(1)} %round.1.mine), channel_id=1, source_target_pairs={{8,14},{9,15},{10,8},{11,9},{12,10},{13,11},{14,12},{15,13},{24,30... | collective-permute-start | bytes 21512 | tf_op jit(solution)/shard_map/ppermute | solution.py:53
  56.8 5.6 %collective-permute-start.13 = (f32[1,1792]{1,0:T(1,128)S(1)}, f32[1,1792]{1,0:T(1,128)S(1)}, u32[]{:S(2)}, u32[]{:S(2)}) collective-permute-start(f32[1,1792]{1,0:T(1,128)S(1)} %round.1.mine), channel_id=1, source_target_pairs={{8,10},{9,11},{10,12},{11,13},{12,14},{13,15},{14,8},{15,9},{24,26... | collective-permute-start | bytes 21512 | tf_op jit(solution)/shard_map/ppermute | solution.py:53
  62.5 1.3 %collective-permute-start.16 = (f32[1,1024]{1,0:T(1,128)S(1)}, f32[1,1024]{1,0:T(1,128)S(1)}, u32[]{:S(2)}, u32[]{:S(2)}) collective-permute-start(f32[1,1024]{1,0:T(1,128)S(1)} %get-tuple-element.29), channel_id=1, source_target_pairs={{0,8},{8,0},{1,9},{9,1},{2,10},{10,2},{3,11},{11,3},{4,12},{12,4},... | collective-permute-start | bytes 12296 | tf_op jit(solution)/shard_map/ppermute | solution.py:438
  68.7 4.7 %collective-permute-start.17 = (bf16[400,1024]{1,0:T(8,128)(2,1)}, bf16[400,1024]{1,0:T(8,128)(2,1)S(1)}, u32[]{:S(2)}, u32[]{:S(2)}) collective-permute-start(bf16[400,1024]{1,0:T(8,128)(2,1)} %get-tuple-element.34), channel_id=1, source_target_pairs={{0,8},{8,0},{1,9},{9,1},{2,10},{10,2},{3,11},{11,3},{4,12},{12,4},... | collective-permute-start | bytes 2457608 | tf_op jit(solution)/shard_map/ppermute | solution.py:465
  69.0 30.9 %all-to-all-start.1 = ((bf16[16,400,128]{2,1,0:T(8,128)(2,1)}), bf16[16,400,128]{2,1,0:T(8,128)(2,1)S(1)}, u32[]{:S(2)}, u32[]{:S(2)}) async-start(bf16[16,400,128]{2,1,0:T(8,128)(2,1)} %get-tuple-element.43), calls=%async_computation.1 | async-start | bytes 3276800 | tf_op jit(solution)/shard_map/all_to_all | solution.py:460
  74.5 11.7 %collective-permute-start.18 = (bf16[784,128]{1,0:T(8,128)(2,1)S(1)}, bf16[784,128]{1,0:T(8,128)(2,1)S(1)}, u32[]{:S(2)}, u32[]{:S(2)}) collective-permute-start(bf16[784,128]{1,0:T(8,128)(2,1)S(1)} %get-tuple-element.38), channel_id=1, source_target_pairs={{0,16},{16,32},{32,48},{48,64},{64,80},{80,96},{96,112},{112,0},{1... | collective-permute-start | bytes 602120 | tf_op jit(solution)/shard_map/ppermute | solution.py:32
  74.6 11.6 %collective-permute-start.19 = (bf16[784,128]{1,0:T(8,128)(2,1)S(1)}, bf16[784,128]{1,0:T(8,128)(2,1)S(1)}, u32[]{:S(2)}, u32[]{:S(2)}) collective-permute-start(bf16[784,128]{1,0:T(8,128)(2,1)S(1)} %get-tuple-element.39), channel_id=1, source_target_pairs={{0,32},{16,112},{32,64},{48,16},{64,96},{80,48},{96,0},{112,80},{1... | collective-permute-start | bytes 602120 | tf_op jit(solution)/shard_map/ppermute | solution.py:32
  75.8 11.4 %collective-permute-start.20 = (bf16[784,128]{1,0:T(8,128)(2,1)S(1)}, bf16[784,128]{1,0:T(8,128)(2,1)S(1)}, u32[]{:S(2)}, u32[]{:S(2)}) collective-permute-start(bf16[784,128]{1,0:T(8,128)(2,1)S(1)} %get-tuple-element.40), channel_id=1, source_target_pairs={{0,112},{16,0},{32,16},{48,32},{64,48},{80,64},{96,80},{112,96},{1... | collective-permute-start | bytes 602120 | tf_op jit(solution)/shard_map/ppermute | solution.py:32
  87.6 13.9 %collective-permute-start.21 = (bf16[400,128]{1,0:T(8,128)(2,1)S(1)}, bf16[400,128]{1,0:T(8,128)(2,1)S(1)}, u32[]{:S(2)}, u32[]{:S(2)}) collective-permute-start(bf16[400,128]{1,0:T(8,128)(2,1)S(1)} %get-tuple-element.45), channel_id=1, source_target_pairs={{0,64},{16,80},{32,96},{48,112},{64,0},{80,16},{96,32},{112,48},{1... | collective-permute-start | bytes 307208 | tf_op jit(solution)/shard_map/ppermute | solution.py:22

commit v16 on v15

--- a/solution.py
+++ b/solution.py
@@ -361,16 +361,15 @@
     pack(far, [block], split3(sums))
 
 
-def text_sum_body(pairs, near, total, terms, side, pay, out, loss):
+def text_sum_body(near, total, terms, pay, out, side):
     rows, width = out.shape
     unit = terms[2:3, :1]
     unit = jnp.where(unit > 0, unit, 1.0)
     out[...] = unit * (near[...] + unpack([pay], 0, rows, width))
-    full = total[...] + side[...] + tails([pay])
-    loss[0, 0] = jnp.max(full) * (math.log(2.0) / (2.0 * pairs))
-
-
-def image_sum_body(got, terms, out, side):
+    side[...] = total[...] + tails([pay])
+
+
+def image_sum_body(pairs, got, terms, side, out, loss):
     rows, width = out.shape
     unit = terms[1:2, :1]
     unit = jnp.where(unit > 0, unit, 1.0)
@@ -378,7 +377,8 @@
     for k in range(width // LANES):
         at = slice(k * rows, (k + 1) * rows)
         out[:, k * LANES : (k + 1) * LANES] = unit * sum(decode(p[at, :]) for p in pays)
-    side[...] = tails(pays)
+    full = side[...] + tails(pays)
+    loss[0, 0] = jnp.max(full) * (math.log(2.0) / (2.0 * pairs))
 
 
 def shards(image_embed, text_embed, pair_index):
@@ -475,20 +475,19 @@
         "relay",
         size=1,
     )
-    grad_image, side = call(
-        image_sum_body,
+    grad_text, side = call(
+        text_sum_body,
         (shape((rows, width), F32), shape((1, LANES), F32)),
-        (image_got, terms),
+        (near, total, terms, turn(far, "z", n_z // 2)),
+        "text_sum",
+        size=1,
+    )
+    grad_image, loss = call(
+        functools.partial(image_sum_body, pairs),
+        (shape((rows, width), F32), shape((1, 1), F32)),
+        (image_got, terms, side),
         "image_sum",
-        size=1,
-    )
-    grad_text, loss = call(
-        functools.partial(text_sum_body, pairs),
-        (shape((rows, width), F32), shape((1, 1), F32)),
-        (near, total, terms, side, turn(far, "z", n_z // 2)),
-        "text_sum",
         smem_out=1,
-        size=1,
     )
     return (loss[0, 0], grad_image, grad_text)
 

time: 103 us -> 102 us (level)
    all_to_all x1, waiting for transfers between devices: 11.3 us -> 3 us  [shards(): image_got = lax.all_to_all(image_sent, PLANE, 0, 0)]
    ppermute x2, waiting for transfers between devices: 0.01 us -> 7.53 us  [turn(): lax.ppermute(x, axis, [(i, (i + step) % count) for i in range(count)])]
  transfers between devices with their start and end apart: 24 -> 24, of which waited for: 12 -> 13; matrix products, arithmetic and copies ran while one was open for 0% -> 0% of each run, Pallas kernels for 4% -> 3%
where the time goes in v16:
time: 102 us
  starting transfers between devices  50.2 us (49%)
  waiting for transfers between devices  36.6 us (36%)
  Pallas kernels  14 us (14%)
    pallas_call x10, Pallas kernels, call(): pl.pallas_call(body, out_shape=outs, in_specs=[pl.BlockSpec(memory_space=...  11.8 us
    ppermute x6, starting transfers between devices, turn_both(): return lax.ppermute(x, AXES, pairs)  11.3 us
    ppermute x6, waiting for transfers between devices, turn_z(): return lax.ppermute(x, 'z', pairs if back else [(b, a) for a, b in pairs])  10.7 us
    ppermute x2, starting transfers between devices, turn(): lax.ppermute(x, axis, [(i, (i + step) % count) for i in range(count)])  8.86 us
    ppermute x4, starting transfers between devices, shards(): pieces = pieces + [lax.ppermute(piece, 'c', SWAP) for piece in pieces]  7.89 us
    ppermute x2, waiting for transfers between devices, turn(): lax.ppermute(x, axis, [(i, (i + step) % count) for i in range(count)])  7.53 us
    all_to_all x1, starting transfers between devices, shards(): image = lax.all_to_all(copies, PLANE, 0, 0).reshape(size, width)  6.9 us
    ppermute x6, starting transfers between devices, turn_z(): return lax.ppermute(x, 'z', pairs if back else [(b, a) for a, b in pairs])  6.7 us
  transfers between devices with their start and end apart: 24, of which 13 were waited for; matrix products, arithmetic and copies ran while one was open for 0% of the time, Pallas kernels for 3%

profile of v16, /device:TPU:1, one launch (start us, length us, event | category | flops | bytes accessed | tf_op | source)
XLA Modules:
  0.0 101.8 jit_solution(8442522928529486303)
XLA Ops:
  0.6 7.8 %collective-permute-start = (bf16[48,1024]{1,0:T(8,128)(2,1)}, bf16[48,1024]{1,0:T(8,128)(2,1)S(1)}, u32[]{:S(2)}, u32[]{:S(2)}) collective-permute-start(bf16[48,1024]{1,0:T(8,128)(2,1)} %near.1), channel_id=1, source_target_pairs={{0,64},{16,80},{32,96},{48,112},{64,0},{80,16},{96,32},{112,48},{1... | collective-permute-start | bytes 294920 | tf_op jit(solution)/shard_map/ppermute | solution.py:22
  8.5 2.2 %copies.1 = bf16[16,48,1024]{2,1,0:T(8,128)(2,1)} custom-call(bf16[48,1024]{1,0:T(8,128)(2,1)} %source.1), custom_call_target="tpu_custom_call" | custom-call | tf_op jit(solution)/shard_map/copies/pallas_call | solution.py:396
  10.7 0.0 copy-start
  10.7 6.9 %all-to-all-start = ((bf16[16,48,1024]{2,1,0:T(8,128)(2,1)}), bf16[16,48,1024]{2,1,0:T(8,128)(2,1)S(1)}, u32[]{:S(2)}, u32[]{:S(2)}) async-start(bf16[16,48,1024]{2,1,0:T(8,128)(2,1)} %copies.1), calls=%async_computation | async-start | bytes 3145728 | tf_op jit(solution)/shard_map/all_to_all | solution.py:404
  17.6 0.0 copy-start.1
  17.6 0.0 collective-permute-done.far
  17.7 0.8 collective-permute-start.3
  18.5 0.3 collective-permute-start.2
  18.7 2.9 %collective-permute-start.1 = (bf16[96,1024]{1,0:T(8,128)(2,1)S(1)}, bf16[96,1024]{1,0:T(8,128)(2,1)S(1)}, u32[]{:S(2)}, u32[]{:S(2)}) collective-permute-start(bf16[96,1024]{1,0:T(8,128)(2,1)S(1)} %join.1.refs_0_), channel_id=1, source_target_pairs={{16,0},{32,16},{48,32},{64,48},{80,64},{96,80},{112,96},{0,112},{1... | collective-permute-start | bytes 589832 | tf_op jit(solution)/shard_map/ppermute | solution.py:32
  21.6 2.1 %collective-permute-start.4 = (bf16[96,1024]{1,0:T(8,128)(2,1)S(1)}, bf16[96,1024]{1,0:T(8,128)(2,1)S(1)}, u32[]{:S(2)}, u32[]{:S(2)}) collective-permute-start(bf16[96,1024]{1,0:T(8,128)(2,1)S(1)} %join.1.refs_0_), channel_id=1, source_target_pairs={{0,8},{8,0},{1,9},{9,1},{2,10},{10,2},{3,11},{11,3},{4,12},{12,4},... | collective-permute-start | bytes 589832 | tf_op jit(solution)/shard_map/ppermute | solution.py:412
  23.7 0.4 collective-permute-done.3.refs_3_
  24.1 3.9 %collective-permute-start.7 = (bf16[96,1024]{1,0:T(8,128)(2,1)S(1)}, bf16[96,1024]{1,0:T(8,128)(2,1)S(1)}, u32[]{:S(2)}, u32[]{:S(2)}) collective-permute-start(bf16[96,1024]{1,0:T(8,128)(2,1)S(1)} %collective-permute-done.3.refs_3_), channel_id=1, source_target_pairs={{0,8},{8,0},{1,9},{9,1},{2,10},{10,2},{3,11},{11,3},{4,12},{12,4},... | collective-permute-start | bytes 589832 | tf_op jit(solution)/shard_map/ppermute | solution.py:412
  28.0 0.7 collective-permute-start.6
  28.7 0.4 collective-permute-done.1.refs_1_
  29.1 1.2 %collective-permute-start.5 = (bf16[96,1024]{1,0:T(8,128)(2,1)S(1)}, bf16[96,1024]{1,0:T(8,128)(2,1)S(1)}, u32[]{:S(2)}, u32[]{:S(2)}) collective-permute-start(bf16[96,1024]{1,0:T(8,128)(2,1)S(1)} %collective-permute-done.1.refs_1_), channel_id=1, source_target_pairs={{0,8},{8,0},{1,9},{9,1},{2,10},{10,2},{3,11},{11,3},{4,12},{12,4},... | collective-permute-start | bytes 589832 | tf_op jit(solution)/shard_map/ppermute | solution.py:412
  30.3 1.4 %collective-permute-start.8 = (s32[384]{0:T(512)S(1)}, s32[384]{0:T(512)S(1)}, u32[]{:S(2)}, u32[]{:S(2)}) collective-permute-start(s32[384]{0:T(512)S(1)} %copy-done.1), channel_id=1, source_target_pairs={{0,128},{128,0},{1,129},{129,1},{2,130},{130,2},{3,131},{131,3},{4... | collective-permute-start | bytes 4616 | tf_op jit(solution)/shard_map/ppermute | solution.py:395
  31.6 4.0 %collective-permute-done.8.refs_10_ = s32[384]{0:T(512)S(1)} collective-permute-done((s32[384]{0:T(512)S(1)}, s32[384]{0:T(512)S(1)}, u32[]{:S(2)}, u32[]{:S(2)}) %collective-permute-start.8) | collective-permute-done | bytes 1568 | tf_op jit(solution)/shard_map/ppermute | solution.py:395
  35.6 0.0 collective-permute-done.4.refs_4_
  35.6 3.3 %all-to-all-done = bf16[16,48,1024]{2,1,0:T(8,128)(2,1)S(1)} async-done(((bf16[16,48,1024]{2,1,0:T(8,128)(2,1)}), bf16[16,48,1024]{2,1,0:T(8,128)(2,1)S(1)}, u32[]{:S(2)}, u32[]{:S(2)}) %all-to-all-start) | async-done | bytes 1572896 | tf_op jit(solution)/shard_map/all_to_all | solution.py:404
  39.0 2.8 %scores.1 = (f32[1,768]{1,0:T(1,128)S(1)}, f32[768,768]{1,0:T(8,128)S(1)}, bf16[768,1024]{1,0:T(8,128)(2,1)S(1)}, f32[1,1024]{1,0:T(1,128)S(1)}, f32[1,1024]{1,0:T(1,128)S(1)}) custom-call(bf16[96,1024]{1,0:T(8,128)(2,1)S(1)} %join.1.refs_0_, bf16[96,1024]{1,0:T(8,128)(2,1)S(1)} %collective-permute-done.1.refs_1_, ...), custom_call_target="tpu_custom_call" | custom-call | flops 1207959552 | bytes 7092224 | tf_op jit(solution)/shard_map/scores/pallas_call | solution.py:102
  41.8 2.4 %collective-permute-start.9 = (f32[1,1024]{1,0:T(1,128)S(1)}, f32[1,1024]{1,0:T(1,128)S(1)}, u32[]{:S(2)}, u32[]{:S(2)}) collective-permute-start(f32[1,1024]{1,0:T(1,128)S(1)} %get-tuple-element.27), channel_id=1, source_target_pairs={{0,8},{8,0},{1,9},{9,1},{2,10},{10,2},{3,11},{11,3},{4,12},{12,4},... | collective-permute-start | bytes 12296 | tf_op jit(solution)/shard_map/ppermute | solution.py:430
  44.2 0.8 collective-permute-done.9.seen
  45.0 3.9 %collective-permute-start.12 = (f32[1,1792]{1,0:T(1,128)S(1)}, f32[1,1792]{1,0:T(1,128)S(1)}, u32[]{:S(2)}, u32[]{:S(2)}) collective-permute-start(f32[1,1792]{1,0:T(1,128)S(1)} %meet.1.mine), channel_id=1, source_target_pairs={{0,32},{1,33},{2,34},{3,35},{4,36},{5,37},{6,38},{7,39},{8,9},{9,8... | collective-permute-start | bytes 21512 | tf_op jit(solution)/shard_map/ppermute | solution.py:53
  48.9 0.2 collective-permute-start.11
  49.1 1.3 %collective-permute-start.10 = (f32[1,1792]{1,0:T(1,128)S(1)}, f32[1,1792]{1,0:T(1,128)S(1)}, u32[]{:S(2)}, u32[]{:S(2)}) collective-permute-start(f32[1,1792]{1,0:T(1,128)S(1)} %meet.1.mine), channel_id=1, source_target_pairs={{0,16},{1,17},{2,18},{3,19},{4,20},{5,21},{6,22},{7,23},{8,136},{9... | collective-permute-start | bytes 21512 | tf_op jit(solution)/shard_map/ppermute | solution.py:53
  50.4 1.0 %collective-permute-done.11.two = f32[1,1792]{1,0:T(1,128)S(1)} collective-permute-done((f32[1,1792]{1,0:T(1,128)S(1)}, f32[1,1792]{1,0:T(1,128)S(1)}, u32[]{:S(2)}, u32[]{:S(2)}) %collective-permute-start.11) | collective-permute-done | bytes 7200 | tf_op jit(solution)/shard_map/ppermute | solution.py:53
  51.4 1.4 %collective-permute-done.10.one = f32[1,1792]{1,0:T(1,128)S(1)} collective-permute-done((f32[1,1792]{1,0:T(1,128)S(1)}, f32[1,1792]{1,0:T(1,128)S(1)}, u32[]{:S(2)}, u32[]{:S(2)}) %collective-permute-start.10) | collective-permute-done | bytes 7200 | tf_op jit(solution)/shard_map/ppermute | solution.py:53
  52.9 0.3 collective-permute-start.15
  53.2 3.6 %collective-permute-start.14 = (f32[1,1792]{1,0:T(1,128)S(1)}, f32[1,1792]{1,0:T(1,128)S(1)}, u32[]{:S(2)}, u32[]{:S(2)}) collective-permute-start(f32[1,1792]{1,0:T(1,128)S(1)} %round.1.mine), channel_id=1, source_target_pairs={{8,14},{9,15},{10,8},{11,9},{12,10},{13,11},{14,12},{15,13},{24,30... | collective-permute-start | bytes 21512 | tf_op jit(solution)/shard_map/ppermute | solution.py:53
  56.8 1.9 %collective-permute-start.13 = (f32[1,1792]{1,0:T(1,128)S(1)}, f32[1,1792]{1,0:T(1,128)S(1)}, u32[]{:S(2)}, u32[]{:S(2)}) collective-permute-start(f32[1,1792]{1,0:T(1,128)S(1)} %round.1.mine), channel_id=1, source_target_pairs={{8,10},{9,11},{10,12},{11,13},{12,14},{13,15},{14,8},{15,9},{24,26... | collective-permute-start | bytes 21512 | tf_op jit(solution)/shard_map/ppermute | solution.py:53
  58.8 3.6 %collective-permute-done.13.one = f32[1,1792]{1,0:T(1,128)S(1)} collective-permute-done((f32[1,1792]{1,0:T(1,128)S(1)}, f32[1,1792]{1,0:T(1,128)S(1)}, u32[]{:S(2)}, u32[]{:S(2)}) %collective-permute-start.13) | collective-permute-done | bytes 7200 | tf_op jit(solution)/shard_map/ppermute | solution.py:53
  62.5 0.1 collective-permute-start.16
  62.6 1.2 %collective-permute-done.16.refs_1_ = f32[1,1024]{1,0:T(1,128)S(1)} collective-permute-done((f32[1,1024]{1,0:T(1,128)S(1)}, f32[1,1024]{1,0:T(1,128)S(1)}, u32[]{:S(2)}, u32[]{:S(2)}) %collective-permute-start.16) | collective-permute-done | bytes 4128 | tf_op jit(solution)/shard_map/ppermute | solution.py:438
  63.7 5.0 %grads.1 = (f32[8,128]{1,0:T(8,128)S(1)}, bf16[384,1024]{1,0:T(8,128)(2,1)S(1)}, bf16[400,1024]{1,0:T(8,128)(2,1)}, bf16[16,400,128]{2,1,0:T(8,128)(2,1)}) custom-call(f32[1,1792]{1,0:T(1,128)S(1)} %get-tuple-element.28.refs_0_, f32[1,1024]{1,0:T(1,128)S(1)} %collective-permute-done.16.refs_1_, f32[768,768]{1,0:T(8,128)S(1)} %get-tuple-element.30.refs_2_, ...), custom_call_target="tpu_custom_call" | custom-call | flops 2415919104 | bytes 8767488 | tf_op jit(solution)/shard_map/grads/pallas_call | solution.py:102
  68.7 0.3 collective-permute-start.17
  69.0 4.4 %all-to-all-start.1 = ((bf16[16,400,128]{2,1,0:T(8,128)(2,1)}), bf16[16,400,128]{2,1,0:T(8,128)(2,1)S(1)}, u32[]{:S(2)}, u32[]{:S(2)}) async-start(bf16[16,400,128]{2,1,0:T(8,128)(2,1)} %get-tuple-element.33), calls=%async_computation.1 | async-start | bytes 3276800 | tf_op jit(solution)/shard_map/all_to_all | solution.py:460
  73.5 1.1 %send.1 = (f32[96,1024]{1,0:T(8,128)S(1)}, f32[1,128]{1,0:T(1,128)S(1)}, bf16[784,128]{1,0:T(8,128)(2,1)S(1)}, bf16[784,128]{1,0:T(8,128)(2,1)S(1)}, bf16[784,128]{1,0:T(8,128)(2,1)S(1)}) custom-call(bf16[384,1024]{1,0:T(8,128)(2,1)S(1)} %get-tuple-element.35.own, bf16[400,1024]{1,0:T(8,128)(2,1)S(1)} %collective-permute-done.17.seen, ...), custom_call_target="tpu_custom_call" | custom-call | flops 10000000000 | bytes 1 | tf_op jit(solution)/shard_map/send/pallas_call | solution.py:102
  74.5 0.1 collective-permute-start.18
  74.6 1.2 %collective-permute-start.19 = (bf16[784,128]{1,0:T(8,128)(2,1)S(1)}, bf16[784,128]{1,0:T(8,128)(2,1)S(1)}, u32[]{:S(2)}, u32[]{:S(2)}) collective-permute-start(bf16[784,128]{1,0:T(8,128)(2,1)S(1)} %get-tuple-element.40), channel_id=1, source_target_pairs={{0,32},{16,112},{32,64},{48,16},{64,96},{80,48},{96,0},{112,80},{1... | collective-permute-start | bytes 602120 | tf_op jit(solution)/shard_map/ppermute | solution.py:32
  75.8 1.5 %collective-permute-start.20 = (bf16[784,128]{1,0:T(8,128)(2,1)S(1)}, bf16[784,128]{1,0:T(8,128)(2,1)S(1)}, u32[]{:S(2)}, u32[]{:S(2)}) collective-permute-start(bf16[784,128]{1,0:T(8,128)(2,1)S(1)} %get-tuple-element.41), channel_id=1, source_target_pairs={{0,112},{16,0},{32,16},{48,32},{64,48},{80,64},{96,80},{112,96},{1... | collective-permute-start | bytes 602120 | tf_op jit(solution)/shard_map/ppermute | solution.py:32
  77.3 8.9 %collective-permute-done.18.refs_0_ = bf16[784,128]{1,0:T(8,128)(2,1)S(1)} collective-permute-done((bf16[784,128]{1,0:T(8,128)(2,1)S(1)}, bf16[784,128]{1,0:T(8,128)(2,1)S(1)}, u32[]{:S(2)}, u32[]{:S(2)}) %collective-permute-start.18) | collective-permute-done | bytes 200736 | tf_op jit(solution)/shard_map/ppermute | solution.py:32
  86.2 1.0 collective-permute-done.20.refs_2_
  87.2 0.4 relay.1
  87.6 1.0 %collective-permute-start.21 = (bf16[400,128]{1,0:T(8,128)(2,1)S(1)}, bf16[400,128]{1,0:T(8,128)(2,1)S(1)}, u32[]{:S(2)}, u32[]{:S(2)}) collective-permute-start(bf16[400,128]{1,0:T(8,128)(2,1)S(1)} %get-tuple-element.44), channel_id=1, source_target_pairs={{0,64},{16,80},{32,96},{48,112},{64,0},{80,16},{96,32},{112,48},{1... | collective-permute-start | bytes 307208 | tf_op jit(solution)/shard_map/ppermute | solution.py:22
  88.6 7.5 %collective-permute-done.21.pay = bf16[400,128]{1,0:T(8,128)(2,1)S(1)} collective-permute-done((bf16[400,128]{1,0:T(8,128)(2,1)S(1)}, bf16[400,128]{1,0:T(8,128)(2,1)S(1)}, u32[]{:S(2)}, u32[]{:S(2)}) %collective-permute-start.21) | collective-permute-done | bytes 102432 | tf_op jit(solution)/shard_map/ppermute | solution.py:22
  96.2 0.8 text_sum.1
  96.9 3.0 %all-to-all-done.1.got = bf16[16,400,128]{2,1,0:T(8,128)(2,1)S(1)} async-done(((bf16[16,400,128]{2,1,0:T(8,128)(2,1)}), bf16[16,400,128]{2,1,0:T(8,128)(2,1)S(1)}, u32[]{:S(2)}, u32[]{:S(2)}) %all-to-all-start.1) | async-done | bytes 1638432 | tf_op jit(solution)/shard_map/all_to_all | solution.py:460
  99.9 1.7 %image_sum.1 = (f32[48,1024]{1,0:T(8,128)}, f32[1,1]{1,0:T(1,128)}) custom-call(bf16[16,400,128]{2,1,0:T(8,128)(2,1)S(1)} %all-to-all-done.1.got, f32[8,128]{1,0:T(8,128)S(1)} %get-tuple-element.34.terms, f32[1,128]{1,0:T(1,128)S(1)} %get-tuple-element.45.side), custom_call_target="tpu_custom_call" | custom-call | bytes 1839620 | tf_op jit(solution)/shard_map/image_sum/pallas_call | solution.py:102
  (15 shorter events, 0.1 us)
Async XLA Ops:
  0.6 17.0 %collective-permute-start = (bf16[48,1024]{1,0:T(8,128)(2,1)}, bf16[48,1024]{1,0:T(8,128)(2,1)S(1)}, u32[]{:S(2)}, u32[]{:S(2)}) collective-permute-start(bf16[48,1024]{1,0:T(8,128)(2,1)} %near.1), channel_id=1, source_target_pairs={{0,64},{16,80},{32,96},{48,112},{64,0},{80,16},{96,32},{112,48},{1... | collective-permute-start | bytes 294920 | tf_op jit(solution)/shard_map/ppermute | solution.py:22
  10.7 6.9 %copy-start = (bf16[48,1024]{1,0:T(8,128)(2,1)S(1)}, bf16[48,1024]{1,0:T(8,128)(2,1)}, u32[]{:S(2)}) copy-start(bf16[48,1024]{1,0:T(8,128)(2,1)} %near.1) | copy-start | bytes 294916
  10.7 28.3 %all-to-all-start = ((bf16[16,48,1024]{2,1,0:T(8,128)(2,1)}), bf16[16,48,1024]{2,1,0:T(8,128)(2,1)S(1)}, u32[]{:S(2)}, u32[]{:S(2)}) async-start(bf16[16,48,1024]{2,1,0:T(8,128)(2,1)} %copies.1), calls=%async_computation | async-start | bytes 3145728 | tf_op jit(solution)/shard_map/all_to_all | solution.py:404
  17.6 12.7 %copy-start.1 = (s32[384]{0:T(512)S(1)}, s32[384]{0:T(512)}, u32[]{:S(2)}) copy-start(s32[384]{0:T(512)} %refs_9_.1) | copy-start | bytes 4612
  17.7 6.4 %collective-permute-start.3 = (bf16[96,1024]{1,0:T(8,128)(2,1)S(1)}, bf16[96,1024]{1,0:T(8,128)(2,1)S(1)}, u32[]{:S(2)}, u32[]{:S(2)}) collective-permute-start(bf16[96,1024]{1,0:T(8,128)(2,1)S(1)} %join.1.refs_0_), channel_id=1, source_target_pairs={{112,0},{0,16},{16,32},{32,48},{48,64},{64,80},{80,96},{96,112},{1... | collective-permute-start | bytes 589832 | tf_op jit(solution)/shard_map/ppermute | solution.py:32
  18.5 9.6 %collective-permute-start.2 = (bf16[96,1024]{1,0:T(8,128)(2,1)S(1)}, bf16[96,1024]{1,0:T(8,128)(2,1)S(1)}, u32[]{:S(2)}, u32[]{:S(2)}) collective-permute-start(bf16[96,1024]{1,0:T(8,128)(2,1)S(1)} %join.1.refs_0_), channel_id=1, source_target_pairs={{32,0},{112,16},{64,32},{16,48},{96,64},{48,80},{0,96},{80,112},{3... | collective-permute-start | bytes 589832 | tf_op jit(solution)/shard_map/ppermute | solution.py:32
  18.7 10.3 %collective-permute-start.1 = (bf16[96,1024]{1,0:T(8,128)(2,1)S(1)}, bf16[96,1024]{1,0:T(8,128)(2,1)S(1)}, u32[]{:S(2)}, u32[]{:S(2)}) collective-permute-start(bf16[96,1024]{1,0:T(8,128)(2,1)S(1)} %join.1.refs_0_), channel_id=1, source_target_pairs={{16,0},{32,16},{48,32},{64,48},{80,64},{96,80},{112,96},{0,112},{1... | collective-permute-start | bytes 589832 | tf_op jit(solution)/shard_map/ppermute | solution.py:32
  21.6 14.0 %collective-permute-start.4 = (bf16[96,1024]{1,0:T(8,128)(2,1)S(1)}, bf16[96,1024]{1,0:T(8,128)(2,1)S(1)}, u32[]{:S(2)}, u32[]{:S(2)}) collective-permute-start(bf16[96,1024]{1,0:T(8,128)(2,1)S(1)} %join.1.refs_0_), channel_id=1, source_target_pairs={{0,8},{8,0},{1,9},{9,1},{2,10},{10,2},{3,11},{11,3},{4,12},{12,4},... | collective-permute-start | bytes 589832 | tf_op jit(solution)/shard_map/ppermute | solution.py:412
  24.1 11.5 %collective-permute-start.7 = (bf16[96,1024]{1,0:T(8,128)(2,1)S(1)}, bf16[96,1024]{1,0:T(8,128)(2,1)S(1)}, u32[]{:S(2)}, u32[]{:S(2)}) collective-permute-start(bf16[96,1024]{1,0:T(8,128)(2,1)S(1)} %collective-permute-done.3.refs_3_), channel_id=1, source_target_pairs={{0,8},{8,0},{1,9},{9,1},{2,10},{10,2},{3,11},{11,3},{4,12},{12,4},... | collective-permute-start | bytes 589832 | tf_op jit(solution)/shard_map/ppermute | solution.py:412
  28.0 7.6 %collective-permute-start.6 = (bf16[96,1024]{1,0:T(8,128)(2,1)S(1)}, bf16[96,1024]{1,0:T(8,128)(2,1)S(1)}, u32[]{:S(2)}, u32[]{:S(2)}) collective-permute-start(bf16[96,1024]{1,0:T(8,128)(2,1)S(1)} %collective-permute-done.2.refs_2_), channel_id=1, source_target_pairs={{0,8},{8,0},{1,9},{9,1},{2,10},{10,2},{3,11},{11,3},{4,12},{12,4},... | collective-permute-start | bytes 589832 | tf_op jit(solution)/shard_map/ppermute | solution.py:412
  29.1 6.5 %collective-permute-start.5 = (bf16[96,1024]{1,0:T(8,128)(2,1)S(1)}, bf16[96,1024]{1,0:T(8,128)(2,1)S(1)}, u32[]{:S(2)}, u32[]{:S(2)}) collective-permute-start(bf16[96,1024]{1,0:T(8,128)(2,1)S(1)} %collective-permute-done.1.refs_1_), channel_id=1, source_target_pairs={{0,8},{8,0},{1,9},{9,1},{2,10},{10,2},{3,11},{11,3},{4,12},{12,4},... | collective-permute-start | bytes 589832 | tf_op jit(solution)/shard_map/ppermute | solution.py:412
  30.3 5.3 %collective-permute-start.8 = (s32[384]{0:T(512)S(1)}, s32[384]{0:T(512)S(1)}, u32[]{:S(2)}, u32[]{:S(2)}) collective-permute-start(s32[384]{0:T(512)S(1)} %copy-done.1), channel_id=1, source_target_pairs={{0,128},{128,0},{1,129},{129,1},{2,130},{130,2},{3,131},{131,3},{4... | collective-permute-start | bytes 4616 | tf_op jit(solution)/shard_map/ppermute | solution.py:395
  41.8 3.2 %collective-permute-start.9 = (f32[1,1024]{1,0:T(1,128)S(1)}, f32[1,1024]{1,0:T(1,128)S(1)}, u32[]{:S(2)}, u32[]{:S(2)}) collective-permute-start(f32[1,1024]{1,0:T(1,128)S(1)} %get-tuple-element.27), channel_id=1, source_target_pairs={{0,8},{8,0},{1,9},{9,1},{2,10},{10,2},{3,11},{11,3},{4,12},{12,4},... | collective-permute-start | bytes 12296 | tf_op jit(solution)/shard_map/ppermute | solution.py:430
  45.0 5.4 %collective-permute-start.12 = (f32[1,1792]{1,0:T(1,128)S(1)}, f32[1,1792]{1,0:T(1,128)S(1)}, u32[]{:S(2)}, u32[]{:S(2)}) collective-permute-start(f32[1,1792]{1,0:T(1,128)S(1)} %meet.1.mine), channel_id=1, source_target_pairs={{0,32},{1,33},{2,34},{3,35},{4,36},{5,37},{6,38},{7,39},{8,9},{9,8... | collective-permute-start | bytes 21512 | tf_op jit(solution)/shard_map/ppermute | solution.py:53
  48.9 2.5 %collective-permute-start.11 = (f32[1,1792]{1,0:T(1,128)S(1)}, f32[1,1792]{1,0:T(1,128)S(1)}, u32[]{:S(2)}, u32[]{:S(2)}) collective-permute-start(f32[1,1792]{1,0:T(1,128)S(1)} %meet.1.mine), channel_id=1, source_target_pairs={{0,112},{1,113},{2,114},{3,115},{4,116},{5,117},{6,118},{7,119},{8... | collective-permute-start | bytes 21512 | tf_op jit(solution)/shard_map/ppermute | solution.py:53
  49.1 3.7 %collective-permute-start.10 = (f32[1,1792]{1,0:T(1,128)S(1)}, f32[1,1792]{1,0:T(1,128)S(1)}, u32[]{:S(2)}, u32[]{:S(2)}) collective-permute-start(f32[1,1792]{1,0:T(1,128)S(1)} %meet.1.mine), channel_id=1, source_target_pairs={{0,16},{1,17},{2,18},{3,19},{4,20},{5,21},{6,22},{7,23},{8,136},{9... | collective-permute-start | bytes 21512 | tf_op jit(solution)/shard_map/ppermute | solution.py:53
  52.9 5.9 %collective-permute-start.15 = (f32[1,1792]{1,0:T(1,128)S(1)}, f32[1,1792]{1,0:T(1,128)S(1)}, u32[]{:S(2)}, u32[]{:S(2)}) collective-permute-start(f32[1,1792]{1,0:T(1,128)S(1)} %round.1.mine), channel_id=1, source_target_pairs={{0,64},{1,65},{2,66},{3,67},{4,68},{5,69},{6,70},{7,71},{8,12},{9,... | collective-permute-start | bytes 21512 | tf_op jit(solution)/shard_map/ppermute | solution.py:53
  53.2 5.6 %collective-permute-start.14 = (f32[1,1792]{1,0:T(1,128)S(1)}, f32[1,1792]{1,0:T(1,128)S(1)}, u32[]{:S(2)}, u32[]{:S(2)}) collective-permute-start(f32[1,1792]{1,0:T(1,128)S(1)} %round.1.mine), channel_id=1, source_target_pairs={{8,14},{9,15},{10,8},{11,9},{12,10},{13,11},{14,12},{15,13},{24,30... | collective-permute-start | bytes 21512 | tf_op jit(solution)/shard_map/ppermute | solution.py:53
  56.8 5.6 %collective-permute-start.13 = (f32[1,1792]{1,0:T(1,128)S(1)}, f32[1,1792]{1,0:T(1,128)S(1)}, u32[]{:S(2)}, u32[]{:S(2)}) collective-permute-start(f32[1,1792]{1,0:T(1,128)S(1)} %round.1.mine), channel_id=1, source_target_pairs={{8,10},{9,11},{10,12},{11,13},{12,14},{13,15},{14,8},{15,9},{24,26... | collective-permute-start | bytes 21512 | tf_op jit(solution)/shard_map/ppermute | solution.py:53
  62.5 1.3 %collective-permute-start.16 = (f32[1,1024]{1,0:T(1,128)S(1)}, f32[1,1024]{1,0:T(1,128)S(1)}, u32[]{:S(2)}, u32[]{:S(2)}) collective-permute-start(f32[1,1024]{1,0:T(1,128)S(1)} %get-tuple-element.29), channel_id=1, source_target_pairs={{0,8},{8,0},{1,9},{9,1},{2,10},{10,2},{3,11},{11,3},{4,12},{12,4},... | collective-permute-start | bytes 12296 | tf_op jit(solution)/shard_map/ppermute | solution.py:438
  68.7 4.7 %collective-permute-start.17 = (bf16[400,1024]{1,0:T(8,128)(2,1)}, bf16[400,1024]{1,0:T(8,128)(2,1)S(1)}, u32[]{:S(2)}, u32[]{:S(2)}) collective-permute-start(bf16[400,1024]{1,0:T(8,128)(2,1)} %get-tuple-element.36), channel_id=1, source_target_pairs={{0,8},{8,0},{1,9},{9,1},{2,10},{10,2},{3,11},{11,3},{4,12},{12,4},... | collective-permute-start | bytes 2457608 | tf_op jit(solution)/shard_map/ppermute | solution.py:465
  69.0 30.9 %all-to-all-start.1 = ((bf16[16,400,128]{2,1,0:T(8,128)(2,1)}), bf16[16,400,128]{2,1,0:T(8,128)(2,1)S(1)}, u32[]{:S(2)}, u32[]{:S(2)}) async-start(bf16[16,400,128]{2,1,0:T(8,128)(2,1)} %get-tuple-element.33), calls=%async_computation.1 | async-start | bytes 3276800 | tf_op jit(solution)/shard_map/all_to_all | solution.py:460
  74.5 11.7 %collective-permute-start.18 = (bf16[784,128]{1,0:T(8,128)(2,1)S(1)}, bf16[784,128]{1,0:T(8,128)(2,1)S(1)}, u32[]{:S(2)}, u32[]{:S(2)}) collective-permute-start(bf16[784,128]{1,0:T(8,128)(2,1)S(1)} %get-tuple-element.39), channel_id=1, source_target_pairs={{0,16},{16,32},{32,48},{48,64},{64,80},{80,96},{96,112},{112,0},{1... | collective-permute-start | bytes 602120 | tf_op jit(solution)/shard_map/ppermute | solution.py:32
  74.6 11.6 %collective-permute-start.19 = (bf16[784,128]{1,0:T(8,128)(2,1)S(1)}, bf16[784,128]{1,0:T(8,128)(2,1)S(1)}, u32[]{:S(2)}, u32[]{:S(2)}) collective-permute-start(bf16[784,128]{1,0:T(8,128)(2,1)S(1)} %get-tuple-element.40), channel_id=1, source_target_pairs={{0,32},{16,112},{32,64},{48,16},{64,96},{80,48},{96,0},{112,80},{1... | collective-permute-start | bytes 602120 | tf_op jit(solution)/shard_map/ppermute | solution.py:32
  75.8 11.4 %collective-permute-start.20 = (bf16[784,128]{1,0:T(8,128)(2,1)S(1)}, bf16[784,128]{1,0:T(8,128)(2,1)S(1)}, u32[]{:S(2)}, u32[]{:S(2)}) collective-permute-start(bf16[784,128]{1,0:T(8,128)(2,1)S(1)} %get-tuple-element.41), channel_id=1, source_target_pairs={{0,112},{16,0},{32,16},{48,32},{64,48},{80,64},{96,80},{112,96},{1... | collective-permute-start | bytes 602120 | tf_op jit(solution)/shard_map/ppermute | solution.py:32
  87.6 8.6 %collective-permute-start.21 = (bf16[400,128]{1,0:T(8,128)(2,1)S(1)}, bf16[400,128]{1,0:T(8,128)(2,1)S(1)}, u32[]{:S(2)}, u32[]{:S(2)}) collective-permute-start(bf16[400,128]{1,0:T(8,128)(2,1)S(1)} %get-tuple-element.44), channel_id=1, source_target_pairs={{0,64},{16,80},{32,96},{48,112},{64,0},{80,16},{96,32},{112,48},{1... | collective-permute-start | bytes 307208 | tf_op jit(solution)/shard_map/ppermute | solution.py:22

commit v17 on v16

--- a/solution.py
+++ b/solution.py
@@ -403,17 +403,19 @@
     )(image_embed)
     image = lax.all_to_all(copies, PLANE, 0, 0).reshape(size, width)
 
-    steps = [q if q <= n_z // 4 else q - n_z // 2 for q in range(n_z // 2)]
+    signed = [q if q <= n_z // 4 else q - n_z // 2 for q in range(n_z // 2)]
+    steps = sorted(signed, key=lambda q: (q != 0, -abs(q)))
+    inward = [0, *steps[:0:-1]]
     far = turn(text_embed, "z", n_z // 2)
     (joined,) = call(
         join_body, (shape((2 * rows, width), BF16),), (text_embed, far), "join", 10**11
     )
-    pieces = [joined] + [turn_z(joined, q, True) for q in steps[1:]]
+    pieces = [joined] + [turn_z(joined, q, True) for q in inward[1:]]
     pieces = pieces + [lax.ppermute(piece, "c", SWAP) for piece in pieces]
 
     flops = 2 * size * size * width
     pair, scores, text, hold, cross = call(
-        functools.partial(score_body, steps, inv_root),
+        functools.partial(score_body, inward, inv_root),
         (
             shape((1, size), F32),
             shape((size, size), F32),

time: 102 us -> 102 us (level)
  no operation moved by 1% of the time
where the time goes in v17:
time: 102 us
  starting transfers between devices  50.5 us (50%)
  waiting for transfers between devices  36.2 us (35%)
  Pallas kernels  14 us (14%)
    pallas_call x10, Pallas kernels, call(): pl.pallas_call(body, out_shape=outs, in_specs=[pl.BlockSpec(memory_space=...  11.8 us
    ppermute x6, waiting for transfers between devices, turn_z(): return lax.ppermute(x, 'z', pairs if back else [(b, a) for a, b in pairs])  11.5 us
    ppermute x6, starting transfers between devices, turn_both(): return lax.ppermute(x, AXES, pairs)  11.3 us
    ppermute x2, starting transfers between devices, turn(): lax.ppermute(x, axis, [(i, (i + step) % count) for i in range(count)])  9.6 us
    ppermute x4, starting transfers between devices, shards(): pieces = pieces + [lax.ppermute(piece, 'c', SWAP) for piece in pieces]  7.81 us
    ppermute x2, waiting for transfers between devices, turn(): lax.ppermute(x, axis, [(i, (i + step) % count) for i in range(count)])  7.16 us
    all_to_all x1, starting transfers between devices, shards(): image = lax.all_to_all(copies, PLANE, 0, 0).reshape(size, width)  6.9 us
    ppermute x6, starting transfers between devices, turn_z(): return lax.ppermute(x, 'z', pairs if back else [(b, a) for a, b in pairs])  6.39 us
  transfers between devices with their start and end apart: 24, of which 13 were waited for; matrix products, arithmetic and copies ran while one was open for 0% of the time, Pallas kernels for 3%

profile of v17, /device:TPU:1, one launch (start us, length us, event | category | flops | bytes accessed | tf_op | source)
XLA Modules:
  0.0 101.8 jit_solution(6312137209672183178)
XLA Ops:
  0.6 7.8 %collective-permute-start = (bf16[48,1024]{1,0:T(8,128)(2,1)}, bf16[48,1024]{1,0:T(8,128)(2,1)S(1)}, u32[]{:S(2)}, u32[]{:S(2)}) collective-permute-start(bf16[48,1024]{1,0:T(8,128)(2,1)} %near.1), channel_id=1, source_target_pairs={{0,64},{16,80},{32,96},{48,112},{64,0},{80,16},{96,32},{112,48},{1... | collective-permute-start | bytes 294920 | tf_op jit(solution)/shard_map/ppermute | solution.py:22
  8.5 2.2 %copies.1 = bf16[16,48,1024]{2,1,0:T(8,128)(2,1)} custom-call(bf16[48,1024]{1,0:T(8,128)(2,1)} %source.1), custom_call_target="tpu_custom_call" | custom-call | tf_op jit(solution)/shard_map/copies/pallas_call | solution.py:396
  10.7 0.0 copy-start
  10.7 6.9 %all-to-all-start = ((bf16[16,48,1024]{2,1,0:T(8,128)(2,1)}), bf16[16,48,1024]{2,1,0:T(8,128)(2,1)S(1)}, u32[]{:S(2)}, u32[]{:S(2)}) async-start(bf16[16,48,1024]{2,1,0:T(8,128)(2,1)} %copies.1), calls=%async_computation | async-start | bytes 3145728 | tf_op jit(solution)/shard_map/all_to_all | solution.py:404
  17.6 0.0 copy-start.1
  17.6 0.0 collective-permute-done.far
  17.7 0.1 collective-permute-start.3
  17.8 3.1 %collective-permute-start.2 = (bf16[96,1024]{1,0:T(8,128)(2,1)S(1)}, bf16[96,1024]{1,0:T(8,128)(2,1)S(1)}, u32[]{:S(2)}, u32[]{:S(2)}) collective-permute-start(bf16[96,1024]{1,0:T(8,128)(2,1)S(1)} %join.1.refs_0_), channel_id=1, source_target_pairs={{16,0},{32,16},{48,32},{64,48},{80,64},{96,80},{112,96},{0,112},{1... | collective-permute-start | bytes 589832 | tf_op jit(solution)/shard_map/ppermute | solution.py:32
  20.9 0.0 collective-permute-start.1
  20.9 1.8 %collective-permute-start.4 = (bf16[96,1024]{1,0:T(8,128)(2,1)S(1)}, bf16[96,1024]{1,0:T(8,128)(2,1)S(1)}, u32[]{:S(2)}, u32[]{:S(2)}) collective-permute-start(bf16[96,1024]{1,0:T(8,128)(2,1)S(1)} %join.1.refs_0_), channel_id=1, source_target_pairs={{0,8},{8,0},{1,9},{9,1},{2,10},{10,2},{3,11},{11,3},{4,12},{12,4},... | collective-permute-start | bytes 589832 | tf_op jit(solution)/shard_map/ppermute | solution.py:414
  22.7 1.2 %collective-permute-done.3.refs_3_ = bf16[96,1024]{1,0:T(8,128)(2,1)S(1)} collective-permute-done((bf16[96,1024]{1,0:T(8,128)(2,1)S(1)}, bf16[96,1024]{1,0:T(8,128)(2,1)S(1)}, u32[]{:S(2)}, u32[]{:S(2)}) %collective-permute-start.3) | collective-permute-done | bytes 196640 | tf_op jit(solution)/shard_map/ppermute | solution.py:32
  23.9 3.8 %collective-permute-start.7 = (bf16[96,1024]{1,0:T(8,128)(2,1)S(1)}, bf16[96,1024]{1,0:T(8,128)(2,1)S(1)}, u32[]{:S(2)}, u32[]{:S(2)}) collective-permute-start(bf16[96,1024]{1,0:T(8,128)(2,1)S(1)} %collective-permute-done.3.refs_3_), channel_id=1, source_target_pairs={{0,8},{8,0},{1,9},{9,1},{2,10},{10,2},{3,11},{11,3},{4,12},{12,4},... | collective-permute-start | bytes 589832 | tf_op jit(solution)/shard_map/ppermute | solution.py:414
  27.7 1.0 %collective-permute-done.2.refs_2_ = bf16[96,1024]{1,0:T(8,128)(2,1)S(1)} collective-permute-done((bf16[96,1024]{1,0:T(8,128)(2,1)S(1)}, bf16[96,1024]{1,0:T(8,128)(2,1)S(1)}, u32[]{:S(2)}, u32[]{:S(2)}) %collective-permute-start.2) | collective-permute-done | bytes 196640 | tf_op jit(solution)/shard_map/ppermute | solution.py:32
  28.7 1.0 collective-permute-start.6
  29.7 0.0 collective-permute-done.1.refs_1_
  29.7 1.2 %collective-permute-start.5 = (bf16[96,1024]{1,0:T(8,128)(2,1)S(1)}, bf16[96,1024]{1,0:T(8,128)(2,1)S(1)}, u32[]{:S(2)}, u32[]{:S(2)}) collective-permute-start(bf16[96,1024]{1,0:T(8,128)(2,1)S(1)} %collective-permute-done.1.refs_1_), channel_id=1, source_target_pairs={{0,8},{8,0},{1,9},{9,1},{2,10},{10,2},{3,11},{11,3},{4,12},{12,4},... | collective-permute-start | bytes 589832 | tf_op jit(solution)/shard_map/ppermute | solution.py:414
  30.9 1.4 %collective-permute-start.8 = (s32[384]{0:T(512)S(1)}, s32[384]{0:T(512)S(1)}, u32[]{:S(2)}, u32[]{:S(2)}) collective-permute-start(s32[384]{0:T(512)S(1)} %copy-done.1), channel_id=1, source_target_pairs={{0,128},{128,0},{1,129},{129,1},{2,130},{130,2},{3,131},{131,3},{4... | collective-permute-start | bytes 4616 | tf_op jit(solution)/shard_map/ppermute | solution.py:395
  32.3 3.3 %collective-permute-done.8.refs_10_ = s32[384]{0:T(512)S(1)} collective-permute-done((s32[384]{0:T(512)S(1)}, s32[384]{0:T(512)S(1)}, u32[]{:S(2)}, u32[]{:S(2)}) %collective-permute-start.8) | collective-permute-done | bytes 1568 | tf_op jit(solution)/shard_map/ppermute | solution.py:395
  35.6 3.3 %all-to-all-done = bf16[16,48,1024]{2,1,0:T(8,128)(2,1)S(1)} async-done(((bf16[16,48,1024]{2,1,0:T(8,128)(2,1)}), bf16[16,48,1024]{2,1,0:T(8,128)(2,1)S(1)}, u32[]{:S(2)}, u32[]{:S(2)}) %all-to-all-start) | async-done | bytes 1572896 | tf_op jit(solution)/shard_map/all_to_all | solution.py:404
  39.0 2.8 %scores.1 = (f32[1,768]{1,0:T(1,128)S(1)}, f32[768,768]{1,0:T(8,128)S(1)}, bf16[768,1024]{1,0:T(8,128)(2,1)S(1)}, f32[1,1024]{1,0:T(1,128)S(1)}, f32[1,1024]{1,0:T(1,128)S(1)}) custom-call(bf16[96,1024]{1,0:T(8,128)(2,1)S(1)} %join.1.refs_0_, bf16[96,1024]{1,0:T(8,128)(2,1)S(1)} %collective-permute-done.1.refs_1_, ...), custom_call_target="tpu_custom_call" | custom-call | flops 1207959552 | bytes 7092224 | tf_op jit(solution)/shard_map/scores/pallas_call | solution.py:102
  41.8 2.4 %collective-permute-start.9 = (f32[1,1024]{1,0:T(1,128)S(1)}, f32[1,1024]{1,0:T(1,128)S(1)}, u32[]{:S(2)}, u32[]{:S(2)}) collective-permute-start(f32[1,1024]{1,0:T(1,128)S(1)} %get-tuple-element.27), channel_id=1, source_target_pairs={{0,8},{8,0},{1,9},{9,1},{2,10},{10,2},{3,11},{11,3},{4,12},{12,4},... | collective-permute-start | bytes 12296 | tf_op jit(solution)/shard_map/ppermute | solution.py:432
  44.1 0.8 collective-permute-done.9.seen
  45.0 3.9 %collective-permute-start.12 = (f32[1,1792]{1,0:T(1,128)S(1)}, f32[1,1792]{1,0:T(1,128)S(1)}, u32[]{:S(2)}, u32[]{:S(2)}) collective-permute-start(f32[1,1792]{1,0:T(1,128)S(1)} %meet.1.mine), channel_id=1, source_target_pairs={{0,32},{1,33},{2,34},{3,35},{4,36},{5,37},{6,38},{7,39},{8,9},{9,8... | collective-permute-start | bytes 21512 | tf_op jit(solution)/shard_map/ppermute | solution.py:53
  48.9 0.2 collective-permute-start.11
  49.1 1.3 %collective-permute-start.10 = (f32[1,1792]{1,0:T(1,128)S(1)}, f32[1,1792]{1,0:T(1,128)S(1)}, u32[]{:S(2)}, u32[]{:S(2)}) collective-permute-start(f32[1,1792]{1,0:T(1,128)S(1)} %meet.1.mine), channel_id=1, source_target_pairs={{0,16},{1,17},{2,18},{3,19},{4,20},{5,21},{6,22},{7,23},{8,136},{9... | collective-permute-start | bytes 21512 | tf_op jit(solution)/shard_map/ppermute | solution.py:53
  50.4 1.0 %collective-permute-done.11.two = f32[1,1792]{1,0:T(1,128)S(1)} collective-permute-done((f32[1,1792]{1,0:T(1,128)S(1)}, f32[1,1792]{1,0:T(1,128)S(1)}, u32[]{:S(2)}, u32[]{:S(2)}) %collective-permute-start.11) | collective-permute-done | bytes 7200 | tf_op jit(solution)/shard_map/ppermute | solution.py:53
  51.4 1.4 %collective-permute-done.10.one = f32[1,1792]{1,0:T(1,128)S(1)} collective-permute-done((f32[1,1792]{1,0:T(1,128)S(1)}, f32[1,1792]{1,0:T(1,128)S(1)}, u32[]{:S(2)}, u32[]{:S(2)}) %collective-permute-start.10) | collective-permute-done | bytes 7200 | tf_op jit(solution)/shard_map/ppermute | solution.py:53
  52.9 0.3 collective-permute-start.15
  53.2 3.6 %collective-permute-start.14 = (f32[1,1792]{1,0:T(1,128)S(1)}, f32[1,1792]{1,0:T(1,128)S(1)}, u32[]{:S(2)}, u32[]{:S(2)}) collective-permute-start(f32[1,1792]{1,0:T(1,128)S(1)} %round.1.mine), channel_id=1, source_target_pairs={{8,14},{9,15},{10,8},{11,9},{12,10},{13,11},{14,12},{15,13},{24,30... | collective-permute-start | bytes 21512 | tf_op jit(solution)/shard_map/ppermute | solution.py:53
  56.8 1.9 %collective-permute-start.13 = (f32[1,1792]{1,0:T(1,128)S(1)}, f32[1,1792]{1,0:T(1,128)S(1)}, u32[]{:S(2)}, u32[]{:S(2)}) collective-permute-start(f32[1,1792]{1,0:T(1,128)S(1)} %round.1.mine), channel_id=1, source_target_pairs={{8,10},{9,11},{10,12},{11,13},{12,14},{13,15},{14,8},{15,9},{24,26... | collective-permute-start | bytes 21512 | tf_op jit(solution)/shard_map/ppermute | solution.py:53
  58.8 3.6 %collective-permute-done.13.one = f32[1,1792]{1,0:T(1,128)S(1)} collective-permute-done((f32[1,1792]{1,0:T(1,128)S(1)}, f32[1,1792]{1,0:T(1,128)S(1)}, u32[]{:S(2)}, u32[]{:S(2)}) %collective-permute-start.13) | collective-permute-done | bytes 7200 | tf_op jit(solution)/shard_map/ppermute | solution.py:53
  62.5 0.1 collective-permute-start.16
  62.6 1.2 %collective-permute-done.16.refs_1_ = f32[1,1024]{1,0:T(1,128)S(1)} collective-permute-done((f32[1,1024]{1,0:T(1,128)S(1)}, f32[1,1024]{1,0:T(1,128)S(1)}, u32[]{:S(2)}, u32[]{:S(2)}) %collective-permute-start.16) | collective-permute-done | bytes 4128 | tf_op jit(solution)/shard_map/ppermute | solution.py:440
  63.7 5.0 %grads.1 = (f32[8,128]{1,0:T(8,128)S(1)}, bf16[384,1024]{1,0:T(8,128)(2,1)S(1)}, bf16[400,1024]{1,0:T(8,128)(2,1)}, bf16[16,400,128]{2,1,0:T(8,128)(2,1)}) custom-call(f32[1,1792]{1,0:T(1,128)S(1)} %get-tuple-element.28.refs_0_, f32[1,1024]{1,0:T(1,128)S(1)} %collective-permute-done.16.refs_1_, f32[768,768]{1,0:T(8,128)S(1)} %get-tuple-element.30.refs_2_, ...), custom_call_target="tpu_custom_call" | custom-call | flops 2415919104 | bytes 8767488 | tf_op jit(solution)/shard_map/grads/pallas_call | solution.py:102
  68.7 0.3 collective-permute-start.17
  69.0 4.5 %all-to-all-start.1 = ((bf16[16,400,128]{2,1,0:T(8,128)(2,1)}), bf16[16,400,128]{2,1,0:T(8,128)(2,1)S(1)}, u32[]{:S(2)}, u32[]{:S(2)}) async-start(bf16[16,400,128]{2,1,0:T(8,128)(2,1)} %get-tuple-element.33), calls=%async_computation.1 | async-start | bytes 3276800 | tf_op jit(solution)/shard_map/all_to_all | solution.py:462
  73.5 1.1 %send.1 = (f32[96,1024]{1,0:T(8,128)S(1)}, f32[1,128]{1,0:T(1,128)S(1)}, bf16[784,128]{1,0:T(8,128)(2,1)S(1)}, bf16[784,128]{1,0:T(8,128)(2,1)S(1)}, bf16[784,128]{1,0:T(8,128)(2,1)S(1)}) custom-call(bf16[384,1024]{1,0:T(8,128)(2,1)S(1)} %get-tuple-element.35.own, bf16[400,1024]{1,0:T(8,128)(2,1)S(1)} %collective-permute-done.17.seen, ...), custom_call_target="tpu_custom_call" | custom-call | flops 10000000000 | bytes 1 | tf_op jit(solution)/shard_map/send/pallas_call | solution.py:102
  74.5 0.5 collective-permute-start.18
  75.0 0.5 collective-permute-start.19
  75.5 2.2 %collective-permute-start.20 = (bf16[784,128]{1,0:T(8,128)(2,1)S(1)}, bf16[784,128]{1,0:T(8,128)(2,1)S(1)}, u32[]{:S(2)}, u32[]{:S(2)}) collective-permute-start(bf16[784,128]{1,0:T(8,128)(2,1)S(1)} %get-tuple-element.41), channel_id=1, source_target_pairs={{0,112},{16,0},{32,16},{48,32},{64,48},{80,64},{96,80},{112,96},{1... | collective-permute-start | bytes 602120 | tf_op jit(solution)/shard_map/ppermute | solution.py:32
  77.7 5.2 %collective-permute-done.18.refs_0_ = bf16[784,128]{1,0:T(8,128)(2,1)S(1)} collective-permute-done((bf16[784,128]{1,0:T(8,128)(2,1)S(1)}, bf16[784,128]{1,0:T(8,128)(2,1)S(1)}, u32[]{:S(2)}, u32[]{:S(2)}) %collective-permute-start.18) | collective-permute-done | bytes 200736 | tf_op jit(solution)/shard_map/ppermute | solution.py:32
  82.9 4.1 %collective-permute-done.19.refs_1_ = bf16[784,128]{1,0:T(8,128)(2,1)S(1)} collective-permute-done((bf16[784,128]{1,0:T(8,128)(2,1)S(1)}, bf16[784,128]{1,0:T(8,128)(2,1)S(1)}, u32[]{:S(2)}, u32[]{:S(2)}) %collective-permute-start.19) | collective-permute-done | bytes 200736 | tf_op jit(solution)/shard_map/ppermute | solution.py:32
  87.0 0.4 relay.1
  87.4 1.8 %collective-permute-start.21 = (bf16[400,128]{1,0:T(8,128)(2,1)S(1)}, bf16[400,128]{1,0:T(8,128)(2,1)S(1)}, u32[]{:S(2)}, u32[]{:S(2)}) collective-permute-start(bf16[400,128]{1,0:T(8,128)(2,1)S(1)} %get-tuple-element.44), channel_id=1, source_target_pairs={{0,64},{16,80},{32,96},{48,112},{64,0},{80,16},{96,32},{112,48},{1... | collective-permute-start | bytes 307208 | tf_op jit(solution)/shard_map/ppermute | solution.py:22
  89.2 7.2 %collective-permute-done.21.pay = bf16[400,128]{1,0:T(8,128)(2,1)S(1)} collective-permute-done((bf16[400,128]{1,0:T(8,128)(2,1)S(1)}, bf16[400,128]{1,0:T(8,128)(2,1)S(1)}, u32[]{:S(2)}, u32[]{:S(2)}) %collective-permute-start.21) | collective-permute-done | bytes 102432 | tf_op jit(solution)/shard_map/ppermute | solution.py:22
  96.3 0.8 text_sum.1
  97.1 2.8 %all-to-all-done.1.got = bf16[16,400,128]{2,1,0:T(8,128)(2,1)S(1)} async-done(((bf16[16,400,128]{2,1,0:T(8,128)(2,1)}), bf16[16,400,128]{2,1,0:T(8,128)(2,1)S(1)}, u32[]{:S(2)}, u32[]{:S(2)}) %all-to-all-start.1) | async-done | bytes 1638432 | tf_op jit(solution)/shard_map/all_to_all | solution.py:462
  99.9 1.7 %image_sum.1 = (f32[48,1024]{1,0:T(8,128)}, f32[1,1]{1,0:T(1,128)}) custom-call(bf16[16,400,128]{2,1,0:T(8,128)(2,1)S(1)} %all-to-all-done.1.got, f32[8,128]{1,0:T(8,128)S(1)} %get-tuple-element.34.terms, f32[1,128]{1,0:T(1,128)S(1)} %get-tuple-element.45.side), custom_call_target="tpu_custom_call" | custom-call | bytes 1839620 | tf_op jit(solution)/shard_map/image_sum/pallas_call | solution.py:102
  (15 shorter events, 0.1 us)
Async XLA Ops:
  0.6 17.0 %collective-permute-start = (bf16[48,1024]{1,0:T(8,128)(2,1)}, bf16[48,1024]{1,0:T(8,128)(2,1)S(1)}, u32[]{:S(2)}, u32[]{:S(2)}) collective-permute-start(bf16[48,1024]{1,0:T(8,128)(2,1)} %near.1), channel_id=1, source_target_pairs={{0,64},{16,80},{32,96},{48,112},{64,0},{80,16},{96,32},{112,48},{1... | collective-permute-start | bytes 294920 | tf_op jit(solution)/shard_map/ppermute | solution.py:22
  10.7 6.9 %copy-start = (bf16[48,1024]{1,0:T(8,128)(2,1)S(1)}, bf16[48,1024]{1,0:T(8,128)(2,1)}, u32[]{:S(2)}) copy-start(bf16[48,1024]{1,0:T(8,128)(2,1)} %near.1) | copy-start | bytes 294916
  10.7 28.3 %all-to-all-start = ((bf16[16,48,1024]{2,1,0:T(8,128)(2,1)}), bf16[16,48,1024]{2,1,0:T(8,128)(2,1)S(1)}, u32[]{:S(2)}, u32[]{:S(2)}) async-start(bf16[16,48,1024]{2,1,0:T(8,128)(2,1)} %copies.1), calls=%async_computation | async-start | bytes 3145728 | tf_op jit(solution)/shard_map/all_to_all | solution.py:404
  17.6 13.3 %copy-start.1 = (s32[384]{0:T(512)S(1)}, s32[384]{0:T(512)}, u32[]{:S(2)}) copy-start(s32[384]{0:T(512)} %refs_9_.1) | copy-start | bytes 4612
  17.7 6.2 %collective-permute-start.3 = (bf16[96,1024]{1,0:T(8,128)(2,1)S(1)}, bf16[96,1024]{1,0:T(8,128)(2,1)S(1)}, u32[]{:S(2)}, u32[]{:S(2)}) collective-permute-start(bf16[96,1024]{1,0:T(8,128)(2,1)S(1)} %join.1.refs_0_), channel_id=1, source_target_pairs={{32,0},{112,16},{64,32},{16,48},{96,64},{48,80},{0,96},{80,112},{3... | collective-permute-start | bytes 589832 | tf_op jit(solution)/shard_map/ppermute | solution.py:32
  17.8 11.0 %collective-permute-start.2 = (bf16[96,1024]{1,0:T(8,128)(2,1)S(1)}, bf16[96,1024]{1,0:T(8,128)(2,1)S(1)}, u32[]{:S(2)}, u32[]{:S(2)}) collective-permute-start(bf16[96,1024]{1,0:T(8,128)(2,1)S(1)} %join.1.refs_0_), channel_id=1, source_target_pairs={{16,0},{32,16},{48,32},{64,48},{80,64},{96,80},{112,96},{0,112},{1... | collective-permute-start | bytes 589832 | tf_op jit(solution)/shard_map/ppermute | solution.py:32
  20.9 8.9 %collective-permute-start.1 = (bf16[96,1024]{1,0:T(8,128)(2,1)S(1)}, bf16[96,1024]{1,0:T(8,128)(2,1)S(1)}, u32[]{:S(2)}, u32[]{:S(2)}) collective-permute-start(bf16[96,1024]{1,0:T(8,128)(2,1)S(1)} %join.1.refs_0_), channel_id=1, source_target_pairs={{112,0},{0,16},{16,32},{32,48},{48,64},{64,80},{80,96},{96,112},{1... | collective-permute-start | bytes 589832 | tf_op jit(solution)/shard_map/ppermute | solution.py:32
  20.9 14.7 %collective-permute-start.4 = (bf16[96,1024]{1,0:T(8,128)(2,1)S(1)}, bf16[96,1024]{1,0:T(8,128)(2,1)S(1)}, u32[]{:S(2)}, u32[]{:S(2)}) collective-permute-start(bf16[96,1024]{1,0:T(8,128)(2,1)S(1)} %join.1.refs_0_), channel_id=1, source_target_pairs={{0,8},{8,0},{1,9},{9,1},{2,10},{10,2},{3,11},{11,3},{4,12},{12,4},... | collective-permute-start | bytes 589832 | tf_op jit(solution)/shard_map/ppermute | solution.py:414
  23.9 11.7 %collective-permute-start.7 = (bf16[96,1024]{1,0:T(8,128)(2,1)S(1)}, bf16[96,1024]{1,0:T(8,128)(2,1)S(1)}, u32[]{:S(2)}, u32[]{:S(2)}) collective-permute-start(bf16[96,1024]{1,0:T(8,128)(2,1)S(1)} %collective-permute-done.3.refs_3_), channel_id=1, source_target_pairs={{0,8},{8,0},{1,9},{9,1},{2,10},{10,2},{3,11},{11,3},{4,12},{12,4},... | collective-permute-start | bytes 589832 | tf_op jit(solution)/shard_map/ppermute | solution.py:414
  28.7 6.9 %collective-permute-start.6 = (bf16[96,1024]{1,0:T(8,128)(2,1)S(1)}, bf16[96,1024]{1,0:T(8,128)(2,1)S(1)}, u32[]{:S(2)}, u32[]{:S(2)}) collective-permute-start(bf16[96,1024]{1,0:T(8,128)(2,1)S(1)} %collective-permute-done.2.refs_2_), channel_id=1, source_target_pairs={{0,8},{8,0},{1,9},{9,1},{2,10},{10,2},{3,11},{11,3},{4,12},{12,4},... | collective-permute-start | bytes 589832 | tf_op jit(solution)/shard_map/ppermute | solution.py:414
  29.7 5.9 %collective-permute-start.5 = (bf16[96,1024]{1,0:T(8,128)(2,1)S(1)}, bf16[96,1024]{1,0:T(8,128)(2,1)S(1)}, u32[]{:S(2)}, u32[]{:S(2)}) collective-permute-start(bf16[96,1024]{1,0:T(8,128)(2,1)S(1)} %collective-permute-done.1.refs_1_), channel_id=1, source_target_pairs={{0,8},{8,0},{1,9},{9,1},{2,10},{10,2},{3,11},{11,3},{4,12},{12,4},... | collective-permute-start | bytes 589832 | tf_op jit(solution)/shard_map/ppermute | solution.py:414
  30.9 4.7 %collective-permute-start.8 = (s32[384]{0:T(512)S(1)}, s32[384]{0:T(512)S(1)}, u32[]{:S(2)}, u32[]{:S(2)}) collective-permute-start(s32[384]{0:T(512)S(1)} %copy-done.1), channel_id=1, source_target_pairs={{0,128},{128,0},{1,129},{129,1},{2,130},{130,2},{3,131},{131,3},{4... | collective-permute-start | bytes 4616 | tf_op jit(solution)/shard_map/ppermute | solution.py:395
  41.8 3.2 %collective-permute-start.9 = (f32[1,1024]{1,0:T(1,128)S(1)}, f32[1,1024]{1,0:T(1,128)S(1)}, u32[]{:S(2)}, u32[]{:S(2)}) collective-permute-start(f32[1,1024]{1,0:T(1,128)S(1)} %get-tuple-element.27), channel_id=1, source_target_pairs={{0,8},{8,0},{1,9},{9,1},{2,10},{10,2},{3,11},{11,3},{4,12},{12,4},... | collective-permute-start | bytes 12296 | tf_op jit(solution)/shard_map/ppermute | solution.py:432
  45.0 5.4 %collective-permute-start.12 = (f32[1,1792]{1,0:T(1,128)S(1)}, f32[1,1792]{1,0:T(1,128)S(1)}, u32[]{:S(2)}, u32[]{:S(2)}) collective-permute-start(f32[1,1792]{1,0:T(1,128)S(1)} %meet.1.mine), channel_id=1, source_target_pairs={{0,32},{1,33},{2,34},{3,35},{4,36},{5,37},{6,38},{7,39},{8,9},{9,8... | collective-permute-start | bytes 21512 | tf_op jit(solution)/shard_map/ppermute | solution.py:53
  48.9 2.5 %collective-permute-start.11 = (f32[1,1792]{1,0:T(1,128)S(1)}, f32[1,1792]{1,0:T(1,128)S(1)}, u32[]{:S(2)}, u32[]{:S(2)}) collective-permute-start(f32[1,1792]{1,0:T(1,128)S(1)} %meet.1.mine), channel_id=1, source_target_pairs={{0,112},{1,113},{2,114},{3,115},{4,116},{5,117},{6,118},{7,119},{8... | collective-permute-start | bytes 21512 | tf_op jit(solution)/shard_map/ppermute | solution.py:53
  49.1 3.7 %collective-permute-start.10 = (f32[1,1792]{1,0:T(1,128)S(1)}, f32[1,1792]{1,0:T(1,128)S(1)}, u32[]{:S(2)}, u32[]{:S(2)}) collective-permute-start(f32[1,1792]{1,0:T(1,128)S(1)} %meet.1.mine), channel_id=1, source_target_pairs={{0,16},{1,17},{2,18},{3,19},{4,20},{5,21},{6,22},{7,23},{8,136},{9... | collective-permute-start | bytes 21512 | tf_op jit(solution)/shard_map/ppermute | solution.py:53
  52.9 5.9 %collective-permute-start.15 = (f32[1,1792]{1,0:T(1,128)S(1)}, f32[1,1792]{1,0:T(1,128)S(1)}, u32[]{:S(2)}, u32[]{:S(2)}) collective-permute-start(f32[1,1792]{1,0:T(1,128)S(1)} %round.1.mine), channel_id=1, source_target_pairs={{0,64},{1,65},{2,66},{3,67},{4,68},{5,69},{6,70},{7,71},{8,12},{9,... | collective-permute-start | bytes 21512 | tf_op jit(solution)/shard_map/ppermute | solution.py:53
  53.2 5.6 %collective-permute-start.14 = (f32[1,1792]{1,0:T(1,128)S(1)}, f32[1,1792]{1,0:T(1,128)S(1)}, u32[]{:S(2)}, u32[]{:S(2)}) collective-permute-start(f32[1,1792]{1,0:T(1,128)S(1)} %round.1.mine), channel_id=1, source_target_pairs={{8,14},{9,15},{10,8},{11,9},{12,10},{13,11},{14,12},{15,13},{24,30... | collective-permute-start | bytes 21512 | tf_op jit(solution)/shard_map/ppermute | solution.py:53
  56.8 5.6 %collective-permute-start.13 = (f32[1,1792]{1,0:T(1,128)S(1)}, f32[1,1792]{1,0:T(1,128)S(1)}, u32[]{:S(2)}, u32[]{:S(2)}) collective-permute-start(f32[1,1792]{1,0:T(1,128)S(1)} %round.1.mine), channel_id=1, source_target_pairs={{8,10},{9,11},{10,12},{11,13},{12,14},{13,15},{14,8},{15,9},{24,26... | collective-permute-start | bytes 21512 | tf_op jit(solution)/shard_map/ppermute | solution.py:53
  62.5 1.3 %collective-permute-start.16 = (f32[1,1024]{1,0:T(1,128)S(1)}, f32[1,1024]{1,0:T(1,128)S(1)}, u32[]{:S(2)}, u32[]{:S(2)}) collective-permute-start(f32[1,1024]{1,0:T(1,128)S(1)} %get-tuple-element.29), channel_id=1, source_target_pairs={{0,8},{8,0},{1,9},{9,1},{2,10},{10,2},{3,11},{11,3},{4,12},{12,4},... | collective-permute-start | bytes 12296 | tf_op jit(solution)/shard_map/ppermute | solution.py:440
  68.7 4.7 %collective-permute-start.17 = (bf16[400,1024]{1,0:T(8,128)(2,1)}, bf16[400,1024]{1,0:T(8,128)(2,1)S(1)}, u32[]{:S(2)}, u32[]{:S(2)}) collective-permute-start(bf16[400,1024]{1,0:T(8,128)(2,1)} %get-tuple-element.36), channel_id=1, source_target_pairs={{0,8},{8,0},{1,9},{9,1},{2,10},{10,2},{3,11},{11,3},{4,12},{12,4},... | collective-permute-start | bytes 2457608 | tf_op jit(solution)/shard_map/ppermute | solution.py:467
  69.0 30.9 %all-to-all-start.1 = ((bf16[16,400,128]{2,1,0:T(8,128)(2,1)}), bf16[16,400,128]{2,1,0:T(8,128)(2,1)S(1)}, u32[]{:S(2)}, u32[]{:S(2)}) async-start(bf16[16,400,128]{2,1,0:T(8,128)(2,1)} %get-tuple-element.33), calls=%async_computation.1 | async-start | bytes 3276800 | tf_op jit(solution)/shard_map/all_to_all | solution.py:462
  74.5 8.3 %collective-permute-start.18 = (bf16[784,128]{1,0:T(8,128)(2,1)S(1)}, bf16[784,128]{1,0:T(8,128)(2,1)S(1)}, u32[]{:S(2)}, u32[]{:S(2)}) collective-permute-start(bf16[784,128]{1,0:T(8,128)(2,1)S(1)} %get-tuple-element.39), channel_id=1, source_target_pairs={{0,32},{16,112},{32,64},{48,16},{64,96},{80,48},{96,0},{112,80},{1... | collective-permute-start | bytes 602120 | tf_op jit(solution)/shard_map/ppermute | solution.py:32
  75.0 11.9 %collective-permute-start.19 = (bf16[784,128]{1,0:T(8,128)(2,1)S(1)}, bf16[784,128]{1,0:T(8,128)(2,1)S(1)}, u32[]{:S(2)}, u32[]{:S(2)}) collective-permute-start(bf16[784,128]{1,0:T(8,128)(2,1)S(1)} %get-tuple-element.40), channel_id=1, source_target_pairs={{0,16},{16,32},{32,48},{48,64},{64,80},{80,96},{96,112},{112,0},{1... | collective-permute-start | bytes 602120 | tf_op jit(solution)/shard_map/ppermute | solution.py:32
  75.5 11.5 %collective-permute-start.20 = (bf16[784,128]{1,0:T(8,128)(2,1)S(1)}, bf16[784,128]{1,0:T(8,128)(2,1)S(1)}, u32[]{:S(2)}, u32[]{:S(2)}) collective-permute-start(bf16[784,128]{1,0:T(8,128)(2,1)S(1)} %get-tuple-element.41), channel_id=1, source_target_pairs={{0,112},{16,0},{32,16},{48,32},{64,48},{80,64},{96,80},{112,96},{1... | collective-permute-start | bytes 602120 | tf_op jit(solution)/shard_map/ppermute | solution.py:32
  87.4 8.9 %collective-permute-start.21 = (bf16[400,128]{1,0:T(8,128)(2,1)S(1)}, bf16[400,128]{1,0:T(8,128)(2,1)S(1)}, u32[]{:S(2)}, u32[]{:S(2)}) collective-permute-start(bf16[400,128]{1,0:T(8,128)(2,1)S(1)} %get-tuple-element.44), channel_id=1, source_target_pairs={{0,64},{16,80},{32,96},{48,112},{64,0},{80,16},{96,32},{112,48},{1... | collective-permute-start | bytes 307208 | tf_op jit(solution)/shard_map/ppermute | solution.py:22

commit v18 on v17

--- a/solution.py
+++ b/solution.py
@@ -149,11 +149,12 @@
     ids = labels(n_z, rows)
     found = jnp.zeros((1, size), F32)
     z = lax.axis_index("z")
-    high = jnp.zeros(pieces[0].shape, F32)
+    high = jnp.zeros(pieces[0].shape, BF16)
     for h in range(2):
         for i, q in enumerate(steps):
             piece = pieces[h * n_z // 2 + i]
-            high = jnp.maximum(high, jnp.abs(piece[...].astype(F32)))
+            if h == 0:
+                high = jnp.maximum(high, jnp.abs(piece[...]))
             for k in range(2):
                 to = lax.rem(z + lean(q, z, n_z) + (k + 2) * n_z // 2, n_z)
                 start = (h * n_z + to) * rows
@@ -182,9 +183,12 @@
         found += jnp.sum(jnp.where(hit, tile, 0.0), axis=0, keepdims=True)
     mass = jnp.exp2(scores[...] - col_top)
     col = col_top + jnp.log2(jnp.sum(mass, axis=0, keepdims=True))
-    image_max = jnp.max(jnp.abs(image[...].astype(F32)))
+    wide = jnp.zeros((rows, image.shape[1]), BF16)
+    for r in range(0, size, rows):
+        wide = jnp.maximum(wide, jnp.abs(image[r : r + rows, :]))
+    image_max = jnp.max(wide.astype(F32))
     zero = jnp.zeros((1, LANES), F32)
-    rows_out = jnp.concatenate([*lanes, zero + jnp.max(high), zero], axis=1)
+    rows_out = jnp.concatenate([*lanes, zero + jnp.max(high.astype(F32)), zero], axis=1)
     cols_out = jnp.concatenate([col, zero + image_max, zero + jnp.sum(found)], axis=1)
     first = lax.axis_index("c") == 0
     hold[...] = jnp.where(first, cols_out, rows_out)

time: 102 us -> 102 us (level)
  no operation moved by 1% of the time
where the time goes in v18:
time: 102 us
  starting transfers between devices  50.8 us (50%)
  waiting for transfers between devices  36.1 us (35%)
  Pallas kernels  13.8 us (14%)
    pallas_call x10, Pallas kernels, call(): pl.pallas_call(body, out_shape=outs, in_specs=[pl.BlockSpec(memory_space=...  11.6 us
    ppermute x6, waiting for transfers between devices, turn_z(): return lax.ppermute(x, 'z', pairs if back else [(b, a) for a, b in pairs])  11.3 us
    ppermute x6, starting transfers between devices, turn_both(): return lax.ppermute(x, AXES, pairs)  11.1 us
    ppermute x2, starting transfers between devices, turn(): lax.ppermute(x, axis, [(i, (i + step) % count) for i in range(count)])  9.92 us
    ppermute x4, starting transfers between devices, shards(): pieces = pieces + [lax.ppermute(piece, 'c', SWAP) for piece in pieces]  7.81 us
    ppermute x2, waiting for transfers between devices, turn(): lax.ppermute(x, axis, [(i, (i + step) % count) for i in range(count)])  7.15 us
    all_to_all x1, starting transfers between devices, shards(): image = lax.all_to_all(copies, PLANE, 0, 0).reshape(size, width)  6.9 us
    ppermute x6, starting transfers between devices, turn_z(): return lax.ppermute(x, 'z', pairs if back else [(b, a) for a, b in pairs])  6.21 us
  transfers between devices with their start and end apart: 24, of which 13 were waited for; matrix products, arithmetic and copies ran while one was open for 0% of the time, Pallas kernels for 3%

profile of v18, /device:TPU:1, one launch (start us, length us, event | category | flops | bytes accessed | tf_op | source)
XLA Modules:
  0.0 101.7 jit_solution(16299074898308944098)
XLA Ops:
  0.6 7.8 %collective-permute-start = (bf16[48,1024]{1,0:T(8,128)(2,1)}, bf16[48,1024]{1,0:T(8,128)(2,1)S(1)}, u32[]{:S(2)}, u32[]{:S(2)}) collective-permute-start(bf16[48,1024]{1,0:T(8,128)(2,1)} %near.1), channel_id=1, source_target_pairs={{0,64},{16,80},{32,96},{48,112},{64,0},{80,16},{96,32},{112,48},{1... | collective-permute-start | bytes 294920 | tf_op jit(solution)/shard_map/ppermute | solution.py:22
  8.5 2.2 %copies.1 = bf16[16,48,1024]{2,1,0:T(8,128)(2,1)} custom-call(bf16[48,1024]{1,0:T(8,128)(2,1)} %source.1), custom_call_target="tpu_custom_call" | custom-call | tf_op jit(solution)/shard_map/copies/pallas_call | solution.py:400
  10.7 0.0 copy-start
  10.7 6.9 %all-to-all-start = ((bf16[16,48,1024]{2,1,0:T(8,128)(2,1)}), bf16[16,48,1024]{2,1,0:T(8,128)(2,1)S(1)}, u32[]{:S(2)}, u32[]{:S(2)}) async-start(bf16[16,48,1024]{2,1,0:T(8,128)(2,1)} %copies.1), calls=%async_computation | async-start | bytes 3145728 | tf_op jit(solution)/shard_map/all_to_all | solution.py:408
  17.6 0.0 copy-start.1
  17.7 0.1 collective-permute-start.3
  17.8 3.1 %collective-permute-start.2 = (bf16[96,1024]{1,0:T(8,128)(2,1)S(1)}, bf16[96,1024]{1,0:T(8,128)(2,1)S(1)}, u32[]{:S(2)}, u32[]{:S(2)}) collective-permute-start(bf16[96,1024]{1,0:T(8,128)(2,1)S(1)} %join.1.refs_0_), channel_id=1, source_target_pairs={{16,0},{32,16},{48,32},{64,48},{80,64},{96,80},{112,96},{0,112},{1... | collective-permute-start | bytes 589832 | tf_op jit(solution)/shard_map/ppermute | solution.py:32
  20.9 0.0 collective-permute-start.1
  20.9 1.8 %collective-permute-start.4 = (bf16[96,1024]{1,0:T(8,128)(2,1)S(1)}, bf16[96,1024]{1,0:T(8,128)(2,1)S(1)}, u32[]{:S(2)}, u32[]{:S(2)}) collective-permute-start(bf16[96,1024]{1,0:T(8,128)(2,1)S(1)} %join.1.refs_0_), channel_id=1, source_target_pairs={{0,8},{8,0},{1,9},{9,1},{2,10},{10,2},{3,11},{11,3},{4,12},{12,4},... | collective-permute-start | bytes 589832 | tf_op jit(solution)/shard_map/ppermute | solution.py:418
  22.7 1.2 %collective-permute-done.3.refs_3_ = bf16[96,1024]{1,0:T(8,128)(2,1)S(1)} collective-permute-done((bf16[96,1024]{1,0:T(8,128)(2,1)S(1)}, bf16[96,1024]{1,0:T(8,128)(2,1)S(1)}, u32[]{:S(2)}, u32[]{:S(2)}) %collective-permute-start.3) | collective-permute-done | bytes 196640 | tf_op jit(solution)/shard_map/ppermute | solution.py:32
  23.9 3.8 %collective-permute-start.7 = (bf16[96,1024]{1,0:T(8,128)(2,1)S(1)}, bf16[96,1024]{1,0:T(8,128)(2,1)S(1)}, u32[]{:S(2)}, u32[]{:S(2)}) collective-permute-start(bf16[96,1024]{1,0:T(8,128)(2,1)S(1)} %collective-permute-done.3.refs_3_), channel_id=1, source_target_pairs={{0,8},{8,0},{1,9},{9,1},{2,10},{10,2},{3,11},{11,3},{4,12},{12,4},... | collective-permute-start | bytes 589832 | tf_op jit(solution)/shard_map/ppermute | solution.py:418
  27.7 1.0 %collective-permute-done.2.refs_2_ = bf16[96,1024]{1,0:T(8,128)(2,1)S(1)} collective-permute-done((bf16[96,1024]{1,0:T(8,128)(2,1)S(1)}, bf16[96,1024]{1,0:T(8,128)(2,1)S(1)}, u32[]{:S(2)}, u32[]{:S(2)}) %collective-permute-start.2) | collective-permute-done | bytes 196640 | tf_op jit(solution)/shard_map/ppermute | solution.py:32
  28.7 1.0 collective-permute-start.6
  29.7 1.2 %collective-permute-start.5 = (bf16[96,1024]{1,0:T(8,128)(2,1)S(1)}, bf16[96,1024]{1,0:T(8,128)(2,1)S(1)}, u32[]{:S(2)}, u32[]{:S(2)}) collective-permute-start(bf16[96,1024]{1,0:T(8,128)(2,1)S(1)} %collective-permute-done.1.refs_1_), channel_id=1, source_target_pairs={{0,8},{8,0},{1,9},{9,1},{2,10},{10,2},{3,11},{11,3},{4,12},{12,4},... | collective-permute-start | bytes 589832 | tf_op jit(solution)/shard_map/ppermute | solution.py:418
  30.9 1.4 %collective-permute-start.8 = (s32[384]{0:T(512)S(1)}, s32[384]{0:T(512)S(1)}, u32[]{:S(2)}, u32[]{:S(2)}) collective-permute-start(s32[384]{0:T(512)S(1)} %copy-done.1), channel_id=1, source_target_pairs={{0,128},{128,0},{1,129},{129,1},{2,130},{130,2},{3,131},{131,3},{4... | collective-permute-start | bytes 4616 | tf_op jit(solution)/shard_map/ppermute | solution.py:399
  32.3 3.3 %collective-permute-done.8.refs_10_ = s32[384]{0:T(512)S(1)} collective-permute-done((s32[384]{0:T(512)S(1)}, s32[384]{0:T(512)S(1)}, u32[]{:S(2)}, u32[]{:S(2)}) %collective-permute-start.8) | collective-permute-done | bytes 1568 | tf_op jit(solution)/shard_map/ppermute | solution.py:399
  35.6 0.0 collective-permute-done.6.refs_6_
  35.6 0.0 collective-permute-done.5.refs_5_
  35.6 3.3 %all-to-all-done = bf16[16,48,1024]{2,1,0:T(8,128)(2,1)S(1)} async-done(((bf16[16,48,1024]{2,1,0:T(8,128)(2,1)}), bf16[16,48,1024]{2,1,0:T(8,128)(2,1)S(1)}, u32[]{:S(2)}, u32[]{:S(2)}) %all-to-all-start) | async-done | bytes 1572896 | tf_op jit(solution)/shard_map/all_to_all | solution.py:408
  39.0 2.6 %scores.1 = (f32[1,768]{1,0:T(1,128)S(1)}, f32[768,768]{1,0:T(8,128)S(1)}, bf16[768,1024]{1,0:T(8,128)(2,1)S(1)}, f32[1,1024]{1,0:T(1,128)S(1)}, f32[1,1024]{1,0:T(1,128)S(1)}) custom-call(bf16[96,1024]{1,0:T(8,128)(2,1)S(1)} %join.1.refs_0_, bf16[96,1024]{1,0:T(8,128)(2,1)S(1)} %collective-permute-done.1.refs_1_, ...), custom_call_target="tpu_custom_call" | custom-call | flops 1207959552 | bytes 7092224 | tf_op jit(solution)/shard_map/scores/pallas_call | solution.py:102
  41.5 2.4 %collective-permute-start.9 = (f32[1,1024]{1,0:T(1,128)S(1)}, f32[1,1024]{1,0:T(1,128)S(1)}, u32[]{:S(2)}, u32[]{:S(2)}) collective-permute-start(f32[1,1024]{1,0:T(1,128)S(1)} %get-tuple-element.27), channel_id=1, source_target_pairs={{0,8},{8,0},{1,9},{9,1},{2,10},{10,2},{3,11},{11,3},{4,12},{12,4},... | collective-permute-start | bytes 12296 | tf_op jit(solution)/shard_map/ppermute | solution.py:436
  43.9 0.8 collective-permute-done.9.seen
  44.8 3.9 %collective-permute-start.12 = (f32[1,1792]{1,0:T(1,128)S(1)}, f32[1,1792]{1,0:T(1,128)S(1)}, u32[]{:S(2)}, u32[]{:S(2)}) collective-permute-start(f32[1,1792]{1,0:T(1,128)S(1)} %meet.1.mine), channel_id=1, source_target_pairs={{0,32},{1,33},{2,34},{3,35},{4,36},{5,37},{6,38},{7,39},{8,9},{9,8... | collective-permute-start | bytes 21512 | tf_op jit(solution)/shard_map/ppermute | solution.py:53
  48.7 0.2 collective-permute-start.11
  48.9 1.3 %collective-permute-start.10 = (f32[1,1792]{1,0:T(1,128)S(1)}, f32[1,1792]{1,0:T(1,128)S(1)}, u32[]{:S(2)}, u32[]{:S(2)}) collective-permute-start(f32[1,1792]{1,0:T(1,128)S(1)} %meet.1.mine), channel_id=1, source_target_pairs={{0,16},{1,17},{2,18},{3,19},{4,20},{5,21},{6,22},{7,23},{8,136},{9... | collective-permute-start | bytes 21512 | tf_op jit(solution)/shard_map/ppermute | solution.py:53
  50.2 1.0 %collective-permute-done.11.two = f32[1,1792]{1,0:T(1,128)S(1)} collective-permute-done((f32[1,1792]{1,0:T(1,128)S(1)}, f32[1,1792]{1,0:T(1,128)S(1)}, u32[]{:S(2)}, u32[]{:S(2)}) %collective-permute-start.11) | collective-permute-done | bytes 7200 | tf_op jit(solution)/shard_map/ppermute | solution.py:53
  51.2 1.4 %collective-permute-done.10.one = f32[1,1792]{1,0:T(1,128)S(1)} collective-permute-done((f32[1,1792]{1,0:T(1,128)S(1)}, f32[1,1792]{1,0:T(1,128)S(1)}, u32[]{:S(2)}, u32[]{:S(2)}) %collective-permute-start.10) | collective-permute-done | bytes 7200 | tf_op jit(solution)/shard_map/ppermute | solution.py:53
  52.6 0.3 collective-permute-start.15
  53.0 3.4 %collective-permute-start.14 = (f32[1,1792]{1,0:T(1,128)S(1)}, f32[1,1792]{1,0:T(1,128)S(1)}, u32[]{:S(2)}, u32[]{:S(2)}) collective-permute-start(f32[1,1792]{1,0:T(1,128)S(1)} %round.1.mine), channel_id=1, source_target_pairs={{8,14},{9,15},{10,8},{11,9},{12,10},{13,11},{14,12},{15,13},{24,30... | collective-permute-start | bytes 21512 | tf_op jit(solution)/shard_map/ppermute | solution.py:53
  56.4 1.9 %collective-permute-start.13 = (f32[1,1792]{1,0:T(1,128)S(1)}, f32[1,1792]{1,0:T(1,128)S(1)}, u32[]{:S(2)}, u32[]{:S(2)}) collective-permute-start(f32[1,1792]{1,0:T(1,128)S(1)} %round.1.mine), channel_id=1, source_target_pairs={{8,10},{9,11},{10,12},{11,13},{12,14},{13,15},{14,8},{15,9},{24,26... | collective-permute-start | bytes 21512 | tf_op jit(solution)/shard_map/ppermute | solution.py:53
  58.4 3.6 %collective-permute-done.13.one = f32[1,1792]{1,0:T(1,128)S(1)} collective-permute-done((f32[1,1792]{1,0:T(1,128)S(1)}, f32[1,1792]{1,0:T(1,128)S(1)}, u32[]{:S(2)}, u32[]{:S(2)}) %collective-permute-start.13) | collective-permute-done | bytes 7200 | tf_op jit(solution)/shard_map/ppermute | solution.py:53
  62.0 0.3 collective-permute-start.16
  62.3 1.2 %collective-permute-done.16.refs_1_ = f32[1,1024]{1,0:T(1,128)S(1)} collective-permute-done((f32[1,1024]{1,0:T(1,128)S(1)}, f32[1,1024]{1,0:T(1,128)S(1)}, u32[]{:S(2)}, u32[]{:S(2)}) %collective-permute-start.16) | collective-permute-done | bytes 4128 | tf_op jit(solution)/shard_map/ppermute | solution.py:444
  63.5 5.0 %grads.1 = (f32[8,128]{1,0:T(8,128)S(1)}, bf16[384,1024]{1,0:T(8,128)(2,1)S(1)}, bf16[400,1024]{1,0:T(8,128)(2,1)}, bf16[16,400,128]{2,1,0:T(8,128)(2,1)}) custom-call(f32[1,1792]{1,0:T(1,128)S(1)} %get-tuple-element.28.refs_0_, f32[1,1024]{1,0:T(1,128)S(1)} %collective-permute-done.16.refs_1_, f32[768,768]{1,0:T(8,128)S(1)} %get-tuple-element.30.refs_2_, ...), custom_call_target="tpu_custom_call" | custom-call | flops 2415919104 | bytes 8767488 | tf_op jit(solution)/shard_map/grads/pallas_call | solution.py:102
  68.5 0.2 collective-permute-start.17
  68.7 4.7 %all-to-all-start.1 = ((bf16[16,400,128]{2,1,0:T(8,128)(2,1)}), bf16[16,400,128]{2,1,0:T(8,128)(2,1)S(1)}, u32[]{:S(2)}, u32[]{:S(2)}) async-start(bf16[16,400,128]{2,1,0:T(8,128)(2,1)} %get-tuple-element.33), calls=%async_computation.1 | async-start | bytes 3276800 | tf_op jit(solution)/shard_map/all_to_all | solution.py:466
  73.4 1.1 %send.1 = (f32[96,1024]{1,0:T(8,128)S(1)}, f32[1,128]{1,0:T(1,128)S(1)}, bf16[784,128]{1,0:T(8,128)(2,1)S(1)}, bf16[784,128]{1,0:T(8,128)(2,1)S(1)}, bf16[784,128]{1,0:T(8,128)(2,1)S(1)}) custom-call(bf16[384,1024]{1,0:T(8,128)(2,1)S(1)} %get-tuple-element.35.own, bf16[400,1024]{1,0:T(8,128)(2,1)S(1)} %collective-permute-done.17.seen, ...), custom_call_target="tpu_custom_call" | custom-call | flops 10000000000 | bytes 1 | tf_op jit(solution)/shard_map/send/pallas_call | solution.py:102
  74.5 0.3 collective-permute-start.18
  74.8 0.7 collective-permute-start.19
  75.5 2.0 %collective-permute-start.20 = (bf16[784,128]{1,0:T(8,128)(2,1)S(1)}, bf16[784,128]{1,0:T(8,128)(2,1)S(1)}, u32[]{:S(2)}, u32[]{:S(2)}) collective-permute-start(bf16[784,128]{1,0:T(8,128)(2,1)S(1)} %get-tuple-element.41), channel_id=1, source_target_pairs={{0,112},{16,0},{32,16},{48,32},{64,48},{80,64},{96,80},{112,96},{1... | collective-permute-start | bytes 602120 | tf_op jit(solution)/shard_map/ppermute | solution.py:32
  77.5 5.3 %collective-permute-done.18.refs_0_ = bf16[784,128]{1,0:T(8,128)(2,1)S(1)} collective-permute-done((bf16[784,128]{1,0:T(8,128)(2,1)S(1)}, bf16[784,128]{1,0:T(8,128)(2,1)S(1)}, u32[]{:S(2)}, u32[]{:S(2)}) %collective-permute-start.18) | collective-permute-done | bytes 200736 | tf_op jit(solution)/shard_map/ppermute | solution.py:32
  82.8 3.8 %collective-permute-done.19.refs_1_ = bf16[784,128]{1,0:T(8,128)(2,1)S(1)} collective-permute-done((bf16[784,128]{1,0:T(8,128)(2,1)S(1)}, bf16[784,128]{1,0:T(8,128)(2,1)S(1)}, u32[]{:S(2)}, u32[]{:S(2)}) %collective-permute-start.19) | collective-permute-done | bytes 200736 | tf_op jit(solution)/shard_map/ppermute | solution.py:32
  86.6 0.4 relay.1
  87.0 2.1 %collective-permute-start.21 = (bf16[400,128]{1,0:T(8,128)(2,1)S(1)}, bf16[400,128]{1,0:T(8,128)(2,1)S(1)}, u32[]{:S(2)}, u32[]{:S(2)}) collective-permute-start(bf16[400,128]{1,0:T(8,128)(2,1)S(1)} %get-tuple-element.44), channel_id=1, source_target_pairs={{0,64},{16,80},{32,96},{48,112},{64,0},{80,16},{96,32},{112,48},{1... | collective-permute-start | bytes 307208 | tf_op jit(solution)/shard_map/ppermute | solution.py:22
  89.1 7.2 %collective-permute-done.21.pay = bf16[400,128]{1,0:T(8,128)(2,1)S(1)} collective-permute-done((bf16[400,128]{1,0:T(8,128)(2,1)S(1)}, bf16[400,128]{1,0:T(8,128)(2,1)S(1)}, u32[]{:S(2)}, u32[]{:S(2)}) %collective-permute-start.21) | collective-permute-done | bytes 102432 | tf_op jit(solution)/shard_map/ppermute | solution.py:22
  96.2 0.8 text_sum.1
  97.0 2.9 %all-to-all-done.1.got = bf16[16,400,128]{2,1,0:T(8,128)(2,1)S(1)} async-done(((bf16[16,400,128]{2,1,0:T(8,128)(2,1)}), bf16[16,400,128]{2,1,0:T(8,128)(2,1)S(1)}, u32[]{:S(2)}, u32[]{:S(2)}) %all-to-all-start.1) | async-done | bytes 1638432 | tf_op jit(solution)/shard_map/all_to_all | solution.py:466
  99.9 1.7 %image_sum.1 = (f32[48,1024]{1,0:T(8,128)}, f32[1,1]{1,0:T(1,128)}) custom-call(bf16[16,400,128]{2,1,0:T(8,128)(2,1)S(1)} %all-to-all-done.1.got, f32[8,128]{1,0:T(8,128)S(1)} %get-tuple-element.34.terms, f32[1,128]{1,0:T(1,128)S(1)} %get-tuple-element.45.side), custom_call_target="tpu_custom_call" | custom-call | bytes 1839620 | tf_op jit(solution)/shard_map/image_sum/pallas_call | solution.py:102
  (15 shorter events, 0.1 us)
Async XLA Ops:
  0.6 17.0 %collective-permute-start = (bf16[48,1024]{1,0:T(8,128)(2,1)}, bf16[48,1024]{1,0:T(8,128)(2,1)S(1)}, u32[]{:S(2)}, u32[]{:S(2)}) collective-permute-start(bf16[48,1024]{1,0:T(8,128)(2,1)} %near.1), channel_id=1, source_target_pairs={{0,64},{16,80},{32,96},{48,112},{64,0},{80,16},{96,32},{112,48},{1... | collective-permute-start | bytes 294920 | tf_op jit(solution)/shard_map/ppermute | solution.py:22
  10.7 6.9 %copy-start = (bf16[48,1024]{1,0:T(8,128)(2,1)S(1)}, bf16[48,1024]{1,0:T(8,128)(2,1)}, u32[]{:S(2)}) copy-start(bf16[48,1024]{1,0:T(8,128)(2,1)} %near.1) | copy-start | bytes 294916
  10.7 28.3 %all-to-all-start = ((bf16[16,48,1024]{2,1,0:T(8,128)(2,1)}), bf16[16,48,1024]{2,1,0:T(8,128)(2,1)S(1)}, u32[]{:S(2)}, u32[]{:S(2)}) async-start(bf16[16,48,1024]{2,1,0:T(8,128)(2,1)} %copies.1), calls=%async_computation | async-start | bytes 3145728 | tf_op jit(solution)/shard_map/all_to_all | solution.py:408
  17.6 13.3 %copy-start.1 = (s32[384]{0:T(512)S(1)}, s32[384]{0:T(512)}, u32[]{:S(2)}) copy-start(s32[384]{0:T(512)} %refs_9_.1) | copy-start | bytes 4612
  17.7 6.2 %collective-permute-start.3 = (bf16[96,1024]{1,0:T(8,128)(2,1)S(1)}, bf16[96,1024]{1,0:T(8,128)(2,1)S(1)}, u32[]{:S(2)}, u32[]{:S(2)}) collective-permute-start(bf16[96,1024]{1,0:T(8,128)(2,1)S(1)} %join.1.refs_0_), channel_id=1, source_target_pairs={{32,0},{112,16},{64,32},{16,48},{96,64},{48,80},{0,96},{80,112},{3... | collective-permute-start | bytes 589832 | tf_op jit(solution)/shard_map/ppermute | solution.py:32
  17.8 11.0 %collective-permute-start.2 = (bf16[96,1024]{1,0:T(8,128)(2,1)S(1)}, bf16[96,1024]{1,0:T(8,128)(2,1)S(1)}, u32[]{:S(2)}, u32[]{:S(2)}) collective-permute-start(bf16[96,1024]{1,0:T(8,128)(2,1)S(1)} %join.1.refs_0_), channel_id=1, source_target_pairs={{16,0},{32,16},{48,32},{64,48},{80,64},{96,80},{112,96},{0,112},{1... | collective-permute-start | bytes 589832 | tf_op jit(solution)/shard_map/ppermute | solution.py:32
  20.9 8.9 %collective-permute-start.1 = (bf16[96,1024]{1,0:T(8,128)(2,1)S(1)}, bf16[96,1024]{1,0:T(8,128)(2,1)S(1)}, u32[]{:S(2)}, u32[]{:S(2)}) collective-permute-start(bf16[96,1024]{1,0:T(8,128)(2,1)S(1)} %join.1.refs_0_), channel_id=1, source_target_pairs={{112,0},{0,16},{16,32},{32,48},{48,64},{64,80},{80,96},{96,112},{1... | collective-permute-start | bytes 589832 | tf_op jit(solution)/shard_map/ppermute | solution.py:32
  20.9 14.7 %collective-permute-start.4 = (bf16[96,1024]{1,0:T(8,128)(2,1)S(1)}, bf16[96,1024]{1,0:T(8,128)(2,1)S(1)}, u32[]{:S(2)}, u32[]{:S(2)}) collective-permute-start(bf16[96,1024]{1,0:T(8,128)(2,1)S(1)} %join.1.refs_0_), channel_id=1, source_target_pairs={{0,8},{8,0},{1,9},{9,1},{2,10},{10,2},{3,11},{11,3},{4,12},{12,4},... | collective-permute-start | bytes 589832 | tf_op jit(solution)/shard_map/ppermute | solution.py:418
  23.9 11.7 %collective-permute-start.7 = (bf16[96,1024]{1,0:T(8,128)(2,1)S(1)}, bf16[96,1024]{1,0:T(8,128)(2,1)S(1)}, u32[]{:S(2)}, u32[]{:S(2)}) collective-permute-start(bf16[96,1024]{1,0:T(8,128)(2,1)S(1)} %collective-permute-done.3.refs_3_), channel_id=1, source_target_pairs={{0,8},{8,0},{1,9},{9,1},{2,10},{10,2},{3,11},{11,3},{4,12},{12,4},... | collective-permute-start | bytes 589832 | tf_op jit(solution)/shard_map/ppermute | solution.py:418
  28.7 6.9 %collective-permute-start.6 = (bf16[96,1024]{1,0:T(8,128)(2,1)S(1)}, bf16[96,1024]{1,0:T(8,128)(2,1)S(1)}, u32[]{:S(2)}, u32[]{:S(2)}) collective-permute-start(bf16[96,1024]{1,0:T(8,128)(2,1)S(1)} %collective-permute-done.2.refs_2_), channel_id=1, source_target_pairs={{0,8},{8,0},{1,9},{9,1},{2,10},{10,2},{3,11},{11,3},{4,12},{12,4},... | collective-permute-start | bytes 589832 | tf_op jit(solution)/shard_map/ppermute | solution.py:418
  29.7 5.9 %collective-permute-start.5 = (bf16[96,1024]{1,0:T(8,128)(2,1)S(1)}, bf16[96,1024]{1,0:T(8,128)(2,1)S(1)}, u32[]{:S(2)}, u32[]{:S(2)}) collective-permute-start(bf16[96,1024]{1,0:T(8,128)(2,1)S(1)} %collective-permute-done.1.refs_1_), channel_id=1, source_target_pairs={{0,8},{8,0},{1,9},{9,1},{2,10},{10,2},{3,11},{11,3},{4,12},{12,4},... | collective-permute-start | bytes 589832 | tf_op jit(solution)/shard_map/ppermute | solution.py:418
  30.9 4.7 %collective-permute-start.8 = (s32[384]{0:T(512)S(1)}, s32[384]{0:T(512)S(1)}, u32[]{:S(2)}, u32[]{:S(2)}) collective-permute-start(s32[384]{0:T(512)S(1)} %copy-done.1), channel_id=1, source_target_pairs={{0,128},{128,0},{1,129},{129,1},{2,130},{130,2},{3,131},{131,3},{4... | collective-permute-start | bytes 4616 | tf_op jit(solution)/shard_map/ppermute | solution.py:399
  41.5 3.2 %collective-permute-start.9 = (f32[1,1024]{1,0:T(1,128)S(1)}, f32[1,1024]{1,0:T(1,128)S(1)}, u32[]{:S(2)}, u32[]{:S(2)}) collective-permute-start(f32[1,1024]{1,0:T(1,128)S(1)} %get-tuple-element.27), channel_id=1, source_target_pairs={{0,8},{8,0},{1,9},{9,1},{2,10},{10,2},{3,11},{11,3},{4,12},{12,4},... | collective-permute-start | bytes 12296 | tf_op jit(solution)/shard_map/ppermute | solution.py:436
  44.8 5.4 %collective-permute-start.12 = (f32[1,1792]{1,0:T(1,128)S(1)}, f32[1,1792]{1,0:T(1,128)S(1)}, u32[]{:S(2)}, u32[]{:S(2)}) collective-permute-start(f32[1,1792]{1,0:T(1,128)S(1)} %meet.1.mine), channel_id=1, source_target_pairs={{0,32},{1,33},{2,34},{3,35},{4,36},{5,37},{6,38},{7,39},{8,9},{9,8... | collective-permute-start | bytes 21512 | tf_op jit(solution)/shard_map/ppermute | solution.py:53
  48.7 2.5 %collective-permute-start.11 = (f32[1,1792]{1,0:T(1,128)S(1)}, f32[1,1792]{1,0:T(1,128)S(1)}, u32[]{:S(2)}, u32[]{:S(2)}) collective-permute-start(f32[1,1792]{1,0:T(1,128)S(1)} %meet.1.mine), channel_id=1, source_target_pairs={{0,112},{1,113},{2,114},{3,115},{4,116},{5,117},{6,118},{7,119},{8... | collective-permute-start | bytes 21512 | tf_op jit(solution)/shard_map/ppermute | solution.py:53
  48.9 3.7 %collective-permute-start.10 = (f32[1,1792]{1,0:T(1,128)S(1)}, f32[1,1792]{1,0:T(1,128)S(1)}, u32[]{:S(2)}, u32[]{:S(2)}) collective-permute-start(f32[1,1792]{1,0:T(1,128)S(1)} %meet.1.mine), channel_id=1, source_target_pairs={{0,16},{1,17},{2,18},{3,19},{4,20},{5,21},{6,22},{7,23},{8,136},{9... | collective-permute-start | bytes 21512 | tf_op jit(solution)/shard_map/ppermute | solution.py:53
  52.6 5.7 %collective-permute-start.15 = (f32[1,1792]{1,0:T(1,128)S(1)}, f32[1,1792]{1,0:T(1,128)S(1)}, u32[]{:S(2)}, u32[]{:S(2)}) collective-permute-start(f32[1,1792]{1,0:T(1,128)S(1)} %round.1.mine), channel_id=1, source_target_pairs={{0,64},{1,65},{2,66},{3,67},{4,68},{5,69},{6,70},{7,71},{8,12},{9,... | collective-permute-start | bytes 21512 | tf_op jit(solution)/shard_map/ppermute | solution.py:53
  53.0 5.4 %collective-permute-start.14 = (f32[1,1792]{1,0:T(1,128)S(1)}, f32[1,1792]{1,0:T(1,128)S(1)}, u32[]{:S(2)}, u32[]{:S(2)}) collective-permute-start(f32[1,1792]{1,0:T(1,128)S(1)} %round.1.mine), channel_id=1, source_target_pairs={{8,14},{9,15},{10,8},{11,9},{12,10},{13,11},{14,12},{15,13},{24,30... | collective-permute-start | bytes 21512 | tf_op jit(solution)/shard_map/ppermute | solution.py:53
  56.4 5.6 %collective-permute-start.13 = (f32[1,1792]{1,0:T(1,128)S(1)}, f32[1,1792]{1,0:T(1,128)S(1)}, u32[]{:S(2)}, u32[]{:S(2)}) collective-permute-start(f32[1,1792]{1,0:T(1,128)S(1)} %round.1.mine), channel_id=1, source_target_pairs={{8,10},{9,11},{10,12},{11,13},{12,14},{13,15},{14,8},{15,9},{24,26... | collective-permute-start | bytes 21512 | tf_op jit(solution)/shard_map/ppermute | solution.py:53
  62.0 1.4 %collective-permute-start.16 = (f32[1,1024]{1,0:T(1,128)S(1)}, f32[1,1024]{1,0:T(1,128)S(1)}, u32[]{:S(2)}, u32[]{:S(2)}) collective-permute-start(f32[1,1024]{1,0:T(1,128)S(1)} %get-tuple-element.29), channel_id=1, source_target_pairs={{0,8},{8,0},{1,9},{9,1},{2,10},{10,2},{3,11},{11,3},{4,12},{12,4},... | collective-permute-start | bytes 12296 | tf_op jit(solution)/shard_map/ppermute | solution.py:444
  68.5 4.9 %collective-permute-start.17 = (bf16[400,1024]{1,0:T(8,128)(2,1)}, bf16[400,1024]{1,0:T(8,128)(2,1)S(1)}, u32[]{:S(2)}, u32[]{:S(2)}) collective-permute-start(bf16[400,1024]{1,0:T(8,128)(2,1)} %get-tuple-element.36), channel_id=1, source_target_pairs={{0,8},{8,0},{1,9},{9,1},{2,10},{10,2},{3,11},{11,3},{4,12},{12,4},... | collective-permute-start | bytes 2457608 | tf_op jit(solution)/shard_map/ppermute | solution.py:471
  68.7 31.1 %all-to-all-start.1 = ((bf16[16,400,128]{2,1,0:T(8,128)(2,1)}), bf16[16,400,128]{2,1,0:T(8,128)(2,1)S(1)}, u32[]{:S(2)}, u32[]{:S(2)}) async-start(bf16[16,400,128]{2,1,0:T(8,128)(2,1)} %get-tuple-element.33), calls=%async_computation.1 | async-start | bytes 3276800 | tf_op jit(solution)/shard_map/all_to_all | solution.py:466
  74.5 8.3 %collective-permute-start.18 = (bf16[784,128]{1,0:T(8,128)(2,1)S(1)}, bf16[784,128]{1,0:T(8,128)(2,1)S(1)}, u32[]{:S(2)}, u32[]{:S(2)}) collective-permute-start(bf16[784,128]{1,0:T(8,128)(2,1)S(1)} %get-tuple-element.39), channel_id=1, source_target_pairs={{0,32},{16,112},{32,64},{48,16},{64,96},{80,48},{96,0},{112,80},{1... | collective-permute-start | bytes 602120 | tf_op jit(solution)/shard_map/ppermute | solution.py:32
  74.8 11.8 %collective-permute-start.19 = (bf16[784,128]{1,0:T(8,128)(2,1)S(1)}, bf16[784,128]{1,0:T(8,128)(2,1)S(1)}, u32[]{:S(2)}, u32[]{:S(2)}) collective-permute-start(bf16[784,128]{1,0:T(8,128)(2,1)S(1)} %get-tuple-element.40), channel_id=1, source_target_pairs={{0,16},{16,32},{32,48},{48,64},{64,80},{80,96},{96,112},{112,0},{1... | collective-permute-start | bytes 602120 | tf_op jit(solution)/shard_map/ppermute | solution.py:32
  75.5 11.1 %collective-permute-start.20 = (bf16[784,128]{1,0:T(8,128)(2,1)S(1)}, bf16[784,128]{1,0:T(8,128)(2,1)S(1)}, u32[]{:S(2)}, u32[]{:S(2)}) collective-permute-start(bf16[784,128]{1,0:T(8,128)(2,1)S(1)} %get-tuple-element.41), channel_id=1, source_target_pairs={{0,112},{16,0},{32,16},{48,32},{64,48},{80,64},{96,80},{112,96},{1... | collective-permute-start | bytes 602120 | tf_op jit(solution)/shard_map/ppermute | solution.py:32
  87.0 9.2 %collective-permute-start.21 = (bf16[400,128]{1,0:T(8,128)(2,1)S(1)}, bf16[400,128]{1,0:T(8,128)(2,1)S(1)}, u32[]{:S(2)}, u32[]{:S(2)}) collective-permute-start(bf16[400,128]{1,0:T(8,128)(2,1)S(1)} %get-tuple-element.44), channel_id=1, source_target_pairs={{0,64},{16,80},{32,96},{48,112},{64,0},{80,16},{96,32},{112,48},{1... | collective-permute-start | bytes 307208 | tf_op jit(solution)/shard_map/ppermute | solution.py:22

commit v19 on v17

--- a/solution.py
+++ b/solution.py
@@ -369,16 +369,22 @@
     side[...] = total[...] + tails([pay])
 
 
-def image_sum_body(pairs, got, terms, side, out, loss):
+def image_sum_body(pairs, got, terms, side, out, loss, held, sems):
+    copies = []
     rows, width = out.shape
     unit = terms[1:2, :1]
     unit = jnp.where(unit > 0, unit, 1.0)
     pays = [got.at[p] for p in range(got.shape[0])]
     for k in range(width // LANES):
         at = slice(k * rows, (k + 1) * rows)
-        out[:, k * LANES : (k + 1) * LANES] = unit * sum(decode(p[at, :]) for p in pays)
+        lanes = pl.ds(k * LANES, LANES)
+        held[:, lanes] = unit * sum(decode(p[at, :]) for p in pays)
+        copies.append(pltpu.make_async_copy(held.at[:, lanes], out.at[:, lanes], sems.at[k]))
+        copies[-1].start()
     full = side[...] + tails(pays)
     loss[0, 0] = jnp.max(full) * (math.log(2.0) / (2.0 * pairs))
+    for copy in copies:
+        copy.wait()
 
 
 def shards(image_embed, text_embed, pair_index):
@@ -490,6 +496,8 @@
         (image_got, terms, side),
         "image_sum",
         smem_out=1,
+        hbm_out=(0,),
+        scratch=[pltpu.VMEM((rows, width), F32), pltpu.SemaphoreType.DMA((width // LANES,))],
     )
     return (loss[0, 0], grad_image, grad_text)
 

time: 102 us -> 103 us (level)
  no operation moved by 1% of the time
where the time goes in v19:
time: 103 us; the launch traced here: 102 us
  starting transfers between devices  50.5 us (49%)
  waiting for transfers between devices  36.2 us (35%)
  Pallas kernels  14.5 us (14%)
    pallas_call x10, Pallas kernels, call(): pl.pallas_call(body, out_shape=outs, in_specs=[pl.BlockSpec(memory_space=...  12.3 us
    ppermute x6, waiting for transfers between devices, turn_z(): return lax.ppermute(x, 'z', pairs if back else [(b, a) for a, b in pairs])  11.5 us
    ppermute x6, starting transfers between devices, turn_both(): return lax.ppermute(x, AXES, pairs)  11.3 us
    ppermute x2, starting transfers between devices, turn(): lax.ppermute(x, axis, [(i, (i + step) % count) for i in range(count)])  9.6 us
    ppermute x4, starting transfers between devices, shards(): pieces = pieces + [lax.ppermute(piece, 'c', SWAP) for piece in pieces]  7.81 us
    ppermute x2, waiting for transfers between devices, turn(): lax.ppermute(x, axis, [(i, (i + step) % count) for i in range(count)])  7.16 us
    all_to_all x1, starting transfers between devices, shards(): image = lax.all_to_all(copies, PLANE, 0, 0).reshape(size, width)  6.9 us
    ppermute x6, starting transfers between devices, turn_z(): return lax.ppermute(x, 'z', pairs if back else [(b, a) for a, b in pairs])  6.39 us
  transfers between devices with their start and end apart: 24, of which 13 were waited for; matrix products, arithmetic and copies ran while one was open for 0% of the time, Pallas kernels for 3%

profile of v19, /device:TPU:1, one launch (start us, length us, event | category | flops | bytes accessed | tf_op | source)
XLA Modules:
  0.0 102.2 jit_solution(11879980889228572964)
XLA Ops:
  0.6 7.8 %collective-permute-start = (bf16[48,1024]{1,0:T(8,128)(2,1)}, bf16[48,1024]{1,0:T(8,128)(2,1)S(1)}, u32[]{:S(2)}, u32[]{:S(2)}) collective-permute-start(bf16[48,1024]{1,0:T(8,128)(2,1)} %near.1), channel_id=1, source_target_pairs={{0,64},{16,80},{32,96},{48,112},{64,0},{80,16},{96,32},{112,48},{1... | collective-permute-start | bytes 294920 | tf_op jit(solution)/shard_map/ppermute | solution.py:22
  8.5 2.2 %copies.1 = bf16[16,48,1024]{2,1,0:T(8,128)(2,1)} custom-call(bf16[48,1024]{1,0:T(8,128)(2,1)} %source.1), custom_call_target="tpu_custom_call" | custom-call | tf_op jit(solution)/shard_map/copies/pallas_call | solution.py:402
  10.7 0.0 copy-start
  10.7 6.9 %all-to-all-start = ((bf16[16,48,1024]{2,1,0:T(8,128)(2,1)}), bf16[16,48,1024]{2,1,0:T(8,128)(2,1)S(1)}, u32[]{:S(2)}, u32[]{:S(2)}) async-start(bf16[16,48,1024]{2,1,0:T(8,128)(2,1)} %copies.1), calls=%async_computation | async-start | bytes 3145728 | tf_op jit(solution)/shard_map/all_to_all | solution.py:410
  17.6 0.0 copy-start.1
  17.6 0.0 collective-permute-done.far
  17.7 0.1 collective-permute-start.3
  17.8 3.1 %collective-permute-start.2 = (bf16[96,1024]{1,0:T(8,128)(2,1)S(1)}, bf16[96,1024]{1,0:T(8,128)(2,1)S(1)}, u32[]{:S(2)}, u32[]{:S(2)}) collective-permute-start(bf16[96,1024]{1,0:T(8,128)(2,1)S(1)} %join.1.refs_0_), channel_id=1, source_target_pairs={{16,0},{32,16},{48,32},{64,48},{80,64},{96,80},{112,96},{0,112},{1... | collective-permute-start | bytes 589832 | tf_op jit(solution)/shard_map/ppermute | solution.py:32
  20.9 0.0 collective-permute-start.1
  20.9 1.8 %collective-permute-start.4 = (bf16[96,1024]{1,0:T(8,128)(2,1)S(1)}, bf16[96,1024]{1,0:T(8,128)(2,1)S(1)}, u32[]{:S(2)}, u32[]{:S(2)}) collective-permute-start(bf16[96,1024]{1,0:T(8,128)(2,1)S(1)} %join.1.refs_0_), channel_id=1, source_target_pairs={{0,8},{8,0},{1,9},{9,1},{2,10},{10,2},{3,11},{11,3},{4,12},{12,4},... | collective-permute-start | bytes 589832 | tf_op jit(solution)/shard_map/ppermute | solution.py:420
  22.7 1.2 %collective-permute-done.3.refs_3_ = bf16[96,1024]{1,0:T(8,128)(2,1)S(1)} collective-permute-done((bf16[96,1024]{1,0:T(8,128)(2,1)S(1)}, bf16[96,1024]{1,0:T(8,128)(2,1)S(1)}, u32[]{:S(2)}, u32[]{:S(2)}) %collective-permute-start.3) | collective-permute-done | bytes 196640 | tf_op jit(solution)/shard_map/ppermute | solution.py:32
  23.9 3.8 %collective-permute-start.7 = (bf16[96,1024]{1,0:T(8,128)(2,1)S(1)}, bf16[96,1024]{1,0:T(8,128)(2,1)S(1)}, u32[]{:S(2)}, u32[]{:S(2)}) collective-permute-start(bf16[96,1024]{1,0:T(8,128)(2,1)S(1)} %collective-permute-done.3.refs_3_), channel_id=1, source_target_pairs={{0,8},{8,0},{1,9},{9,1},{2,10},{10,2},{3,11},{11,3},{4,12},{12,4},... | collective-permute-start | bytes 589832 | tf_op jit(solution)/shard_map/ppermute | solution.py:420
  27.7 1.0 %collective-permute-done.2.refs_2_ = bf16[96,1024]{1,0:T(8,128)(2,1)S(1)} collective-permute-done((bf16[96,1024]{1,0:T(8,128)(2,1)S(1)}, bf16[96,1024]{1,0:T(8,128)(2,1)S(1)}, u32[]{:S(2)}, u32[]{:S(2)}) %collective-permute-start.2) | collective-permute-done | bytes 196640 | tf_op jit(solution)/shard_map/ppermute | solution.py:32
  28.7 1.0 collective-permute-start.6
  29.7 0.0 collective-permute-done.1.refs_1_
  29.7 1.2 %collective-permute-start.5 = (bf16[96,1024]{1,0:T(8,128)(2,1)S(1)}, bf16[96,1024]{1,0:T(8,128)(2,1)S(1)}, u32[]{:S(2)}, u32[]{:S(2)}) collective-permute-start(bf16[96,1024]{1,0:T(8,128)(2,1)S(1)} %collective-permute-done.1.refs_1_), channel_id=1, source_target_pairs={{0,8},{8,0},{1,9},{9,1},{2,10},{10,2},{3,11},{11,3},{4,12},{12,4},... | collective-permute-start | bytes 589832 | tf_op jit(solution)/shard_map/ppermute | solution.py:420
  30.9 1.4 %collective-permute-start.8 = (s32[384]{0:T(512)S(1)}, s32[384]{0:T(512)S(1)}, u32[]{:S(2)}, u32[]{:S(2)}) collective-permute-start(s32[384]{0:T(512)S(1)} %copy-done.1), channel_id=1, source_target_pairs={{0,128},{128,0},{1,129},{129,1},{2,130},{130,2},{3,131},{131,3},{4... | collective-permute-start | bytes 4616 | tf_op jit(solution)/shard_map/ppermute | solution.py:401
  32.3 3.3 %collective-permute-done.8.refs_10_ = s32[384]{0:T(512)S(1)} collective-permute-done((s32[384]{0:T(512)S(1)}, s32[384]{0:T(512)S(1)}, u32[]{:S(2)}, u32[]{:S(2)}) %collective-permute-start.8) | collective-permute-done | bytes 1568 | tf_op jit(solution)/shard_map/ppermute | solution.py:401
  35.6 3.3 %all-to-all-done = bf16[16,48,1024]{2,1,0:T(8,128)(2,1)S(1)} async-done(((bf16[16,48,1024]{2,1,0:T(8,128)(2,1)}), bf16[16,48,1024]{2,1,0:T(8,128)(2,1)S(1)}, u32[]{:S(2)}, u32[]{:S(2)}) %all-to-all-start) | async-done | bytes 1572896 | tf_op jit(solution)/shard_map/all_to_all | solution.py:410
  39.0 2.8 %scores.1 = (f32[1,768]{1,0:T(1,128)S(1)}, f32[768,768]{1,0:T(8,128)S(1)}, bf16[768,1024]{1,0:T(8,128)(2,1)S(1)}, f32[1,1024]{1,0:T(1,128)S(1)}, f32[1,1024]{1,0:T(1,128)S(1)}) custom-call(bf16[96,1024]{1,0:T(8,128)(2,1)S(1)} %join.1.refs_0_, bf16[96,1024]{1,0:T(8,128)(2,1)S(1)} %collective-permute-done.1.refs_1_, ...), custom_call_target="tpu_custom_call" | custom-call | flops 1207959552 | bytes 7092224 | tf_op jit(solution)/shard_map/scores/pallas_call | solution.py:102
  41.8 2.4 %collective-permute-start.9 = (f32[1,1024]{1,0:T(1,128)S(1)}, f32[1,1024]{1,0:T(1,128)S(1)}, u32[]{:S(2)}, u32[]{:S(2)}) collective-permute-start(f32[1,1024]{1,0:T(1,128)S(1)} %get-tuple-element.27), channel_id=1, source_target_pairs={{0,8},{8,0},{1,9},{9,1},{2,10},{10,2},{3,11},{11,3},{4,12},{12,4},... | collective-permute-start | bytes 12296 | tf_op jit(solution)/shard_map/ppermute | solution.py:438
  44.1 0.8 collective-permute-done.9.seen
  45.0 3.9 %collective-permute-start.12 = (f32[1,1792]{1,0:T(1,128)S(1)}, f32[1,1792]{1,0:T(1,128)S(1)}, u32[]{:S(2)}, u32[]{:S(2)}) collective-permute-start(f32[1,1792]{1,0:T(1,128)S(1)} %meet.1.mine), channel_id=1, source_target_pairs={{0,32},{1,33},{2,34},{3,35},{4,36},{5,37},{6,38},{7,39},{8,9},{9,8... | collective-permute-start | bytes 21512 | tf_op jit(solution)/shard_map/ppermute | solution.py:53
  48.9 0.2 collective-permute-start.11
  49.1 1.3 %collective-permute-start.10 = (f32[1,1792]{1,0:T(1,128)S(1)}, f32[1,1792]{1,0:T(1,128)S(1)}, u32[]{:S(2)}, u32[]{:S(2)}) collective-permute-start(f32[1,1792]{1,0:T(1,128)S(1)} %meet.1.mine), channel_id=1, source_target_pairs={{0,16},{1,17},{2,18},{3,19},{4,20},{5,21},{6,22},{7,23},{8,136},{9... | collective-permute-start | bytes 21512 | tf_op jit(solution)/shard_map/ppermute | solution.py:53
  50.4 1.0 collective-permute-done.11.two
  51.4 1.4 %collective-permute-done.10.one = f32[1,1792]{1,0:T(1,128)S(1)} collective-permute-done((f32[1,1792]{1,0:T(1,128)S(1)}, f32[1,1792]{1,0:T(1,128)S(1)}, u32[]{:S(2)}, u32[]{:S(2)}) %collective-permute-start.10) | collective-permute-done | bytes 7200 | tf_op jit(solution)/shard_map/ppermute | solution.py:53
  52.9 0.3 collective-permute-start.15
  53.2 3.6 %collective-permute-start.14 = (f32[1,1792]{1,0:T(1,128)S(1)}, f32[1,1792]{1,0:T(1,128)S(1)}, u32[]{:S(2)}, u32[]{:S(2)}) collective-permute-start(f32[1,1792]{1,0:T(1,128)S(1)} %round.1.mine), channel_id=1, source_target_pairs={{8,14},{9,15},{10,8},{11,9},{12,10},{13,11},{14,12},{15,13},{24,30... | collective-permute-start | bytes 21512 | tf_op jit(solution)/shard_map/ppermute | solution.py:53
  56.8 1.9 %collective-permute-start.13 = (f32[1,1792]{1,0:T(1,128)S(1)}, f32[1,1792]{1,0:T(1,128)S(1)}, u32[]{:S(2)}, u32[]{:S(2)}) collective-permute-start(f32[1,1792]{1,0:T(1,128)S(1)} %round.1.mine), channel_id=1, source_target_pairs={{8,10},{9,11},{10,12},{11,13},{12,14},{13,15},{14,8},{15,9},{24,26... | collective-permute-start | bytes 21512 | tf_op jit(solution)/shard_map/ppermute | solution.py:53
  58.8 3.6 %collective-permute-done.13.one = f32[1,1792]{1,0:T(1,128)S(1)} collective-permute-done((f32[1,1792]{1,0:T(1,128)S(1)}, f32[1,1792]{1,0:T(1,128)S(1)}, u32[]{:S(2)}, u32[]{:S(2)}) %collective-permute-start.13) | collective-permute-done | bytes 7200 | tf_op jit(solution)/shard_map/ppermute | solution.py:53
  62.5 0.1 collective-permute-start.16
  62.6 1.2 %collective-permute-done.16.refs_1_ = f32[1,1024]{1,0:T(1,128)S(1)} collective-permute-done((f32[1,1024]{1,0:T(1,128)S(1)}, f32[1,1024]{1,0:T(1,128)S(1)}, u32[]{:S(2)}, u32[]{:S(2)}) %collective-permute-start.16) | collective-permute-done | bytes 4128 | tf_op jit(solution)/shard_map/ppermute | solution.py:446
  63.7 5.0 %grads.1 = (f32[8,128]{1,0:T(8,128)S(1)}, bf16[384,1024]{1,0:T(8,128)(2,1)S(1)}, bf16[400,1024]{1,0:T(8,128)(2,1)}, bf16[16,400,128]{2,1,0:T(8,128)(2,1)}) custom-call(f32[1,1792]{1,0:T(1,128)S(1)} %get-tuple-element.28.refs_0_, f32[1,1024]{1,0:T(1,128)S(1)} %collective-permute-done.16.refs_1_, f32[768,768]{1,0:T(8,128)S(1)} %get-tuple-element.30.refs_2_, ...), custom_call_target="tpu_custom_call" | custom-call | flops 2415919104 | bytes 8767488 | tf_op jit(solution)/shard_map/grads/pallas_call | solution.py:102
  68.7 0.3 collective-permute-start.17
  69.0 4.5 %all-to-all-start.1 = ((bf16[16,400,128]{2,1,0:T(8,128)(2,1)}), bf16[16,400,128]{2,1,0:T(8,128)(2,1)S(1)}, u32[]{:S(2)}, u32[]{:S(2)}) async-start(bf16[16,400,128]{2,1,0:T(8,128)(2,1)} %get-tuple-element.33), calls=%async_computation.1 | async-start | bytes 3276800 | tf_op jit(solution)/shard_map/all_to_all | solution.py:468
  73.5 1.1 %send.1 = (f32[96,1024]{1,0:T(8,128)S(1)}, f32[1,128]{1,0:T(1,128)S(1)}, bf16[784,128]{1,0:T(8,128)(2,1)S(1)}, bf16[784,128]{1,0:T(8,128)(2,1)S(1)}, bf16[784,128]{1,0:T(8,128)(2,1)S(1)}) custom-call(bf16[384,1024]{1,0:T(8,128)(2,1)S(1)} %get-tuple-element.35.own, bf16[400,1024]{1,0:T(8,128)(2,1)S(1)} %collective-permute-done.17.seen, ...), custom_call_target="tpu_custom_call" | custom-call | flops 10000000000 | bytes 1 | tf_op jit(solution)/shard_map/send/pallas_call | solution.py:102
  74.5 0.5 collective-permute-start.18
  75.0 0.5 collective-permute-start.19
  75.5 2.2 %collective-permute-start.20 = (bf16[784,128]{1,0:T(8,128)(2,1)S(1)}, bf16[784,128]{1,0:T(8,128)(2,1)S(1)}, u32[]{:S(2)}, u32[]{:S(2)}) collective-permute-start(bf16[784,128]{1,0:T(8,128)(2,1)S(1)} %get-tuple-element.41), channel_id=1, source_target_pairs={{0,112},{16,0},{32,16},{48,32},{64,48},{80,64},{96,80},{112,96},{1... | collective-permute-start | bytes 602120 | tf_op jit(solution)/shard_map/ppermute | solution.py:32
  77.7 5.2 %collective-permute-done.18.refs_0_ = bf16[784,128]{1,0:T(8,128)(2,1)S(1)} collective-permute-done((bf16[784,128]{1,0:T(8,128)(2,1)S(1)}, bf16[784,128]{1,0:T(8,128)(2,1)S(1)}, u32[]{:S(2)}, u32[]{:S(2)}) %collective-permute-start.18) | collective-permute-done | bytes 200736 | tf_op jit(solution)/shard_map/ppermute | solution.py:32
  82.9 4.1 %collective-permute-done.19.refs_1_ = bf16[784,128]{1,0:T(8,128)(2,1)S(1)} collective-permute-done((bf16[784,128]{1,0:T(8,128)(2,1)S(1)}, bf16[784,128]{1,0:T(8,128)(2,1)S(1)}, u32[]{:S(2)}, u32[]{:S(2)}) %collective-permute-start.19) | collective-permute-done | bytes 200736 | tf_op jit(solution)/shard_map/ppermute | solution.py:32
  87.0 0.4 relay.1
  87.4 1.8 %collective-permute-start.21 = (bf16[400,128]{1,0:T(8,128)(2,1)S(1)}, bf16[400,128]{1,0:T(8,128)(2,1)S(1)}, u32[]{:S(2)}, u32[]{:S(2)}) collective-permute-start(bf16[400,128]{1,0:T(8,128)(2,1)S(1)} %get-tuple-element.44), channel_id=1, source_target_pairs={{0,64},{16,80},{32,96},{48,112},{64,0},{80,16},{96,32},{112,48},{1... | collective-permute-start | bytes 307208 | tf_op jit(solution)/shard_map/ppermute | solution.py:22
  89.2 7.2 %collective-permute-done.21.pay = bf16[400,128]{1,0:T(8,128)(2,1)S(1)} collective-permute-done((bf16[400,128]{1,0:T(8,128)(2,1)S(1)}, bf16[400,128]{1,0:T(8,128)(2,1)S(1)}, u32[]{:S(2)}, u32[]{:S(2)}) %collective-permute-start.21) | collective-permute-done | bytes 102432 | tf_op jit(solution)/shard_map/ppermute | solution.py:22
  96.3 0.8 text_sum.1
  97.1 2.8 %all-to-all-done.1.got = bf16[16,400,128]{2,1,0:T(8,128)(2,1)S(1)} async-done(((bf16[16,400,128]{2,1,0:T(8,128)(2,1)}), bf16[16,400,128]{2,1,0:T(8,128)(2,1)S(1)}, u32[]{:S(2)}, u32[]{:S(2)}) %all-to-all-start.1) | async-done | bytes 1638432 | tf_op jit(solution)/shard_map/all_to_all | solution.py:468
  99.9 2.1 %image_sum.1 = (f32[48,1024]{1,0:T(8,128)}, f32[1,1]{1,0:T(1,128)}) custom-call(bf16[16,400,128]{2,1,0:T(8,128)(2,1)S(1)} %all-to-all-done.1.got, f32[8,128]{1,0:T(8,128)S(1)} %get-tuple-element.34.terms, f32[1,128]{1,0:T(1,128)S(1)} %get-tuple-element.45.side), custom_call_target="tpu_custom_call" | custom-call | bytes 1839620 | tf_op jit(solution)/shard_map/image_sum/pallas_call | solution.py:102
  (15 shorter events, 0.1 us)
Async XLA Ops:
  0.6 17.0 %collective-permute-start = (bf16[48,1024]{1,0:T(8,128)(2,1)}, bf16[48,1024]{1,0:T(8,128)(2,1)S(1)}, u32[]{:S(2)}, u32[]{:S(2)}) collective-permute-start(bf16[48,1024]{1,0:T(8,128)(2,1)} %near.1), channel_id=1, source_target_pairs={{0,64},{16,80},{32,96},{48,112},{64,0},{80,16},{96,32},{112,48},{1... | collective-permute-start | bytes 294920 | tf_op jit(solution)/shard_map/ppermute | solution.py:22
  10.7 6.9 %copy-start = (bf16[48,1024]{1,0:T(8,128)(2,1)S(1)}, bf16[48,1024]{1,0:T(8,128)(2,1)}, u32[]{:S(2)}) copy-start(bf16[48,1024]{1,0:T(8,128)(2,1)} %near.1) | copy-start | bytes 294916
  10.7 28.3 %all-to-all-start = ((bf16[16,48,1024]{2,1,0:T(8,128)(2,1)}), bf16[16,48,1024]{2,1,0:T(8,128)(2,1)S(1)}, u32[]{:S(2)}, u32[]{:S(2)}) async-start(bf16[16,48,1024]{2,1,0:T(8,128)(2,1)} %copies.1), calls=%async_computation | async-start | bytes 3145728 | tf_op jit(solution)/shard_map/all_to_all | solution.py:410
  17.6 13.3 %copy-start.1 = (s32[384]{0:T(512)S(1)}, s32[384]{0:T(512)}, u32[]{:S(2)}) copy-start(s32[384]{0:T(512)} %refs_9_.1) | copy-start | bytes 4612
  17.7 6.2 %collective-permute-start.3 = (bf16[96,1024]{1,0:T(8,128)(2,1)S(1)}, bf16[96,1024]{1,0:T(8,128)(2,1)S(1)}, u32[]{:S(2)}, u32[]{:S(2)}) collective-permute-start(bf16[96,1024]{1,0:T(8,128)(2,1)S(1)} %join.1.refs_0_), channel_id=1, source_target_pairs={{32,0},{112,16},{64,32},{16,48},{96,64},{48,80},{0,96},{80,112},{3... | collective-permute-start | bytes 589832 | tf_op jit(solution)/shard_map/ppermute | solution.py:32
  17.8 11.0 %collective-permute-start.2 = (bf16[96,1024]{1,0:T(8,128)(2,1)S(1)}, bf16[96,1024]{1,0:T(8,128)(2,1)S(1)}, u32[]{:S(2)}, u32[]{:S(2)}) collective-permute-start(bf16[96,1024]{1,0:T(8,128)(2,1)S(1)} %join.1.refs_0_), channel_id=1, source_target_pairs={{16,0},{32,16},{48,32},{64,48},{80,64},{96,80},{112,96},{0,112},{1... | collective-permute-start | bytes 589832 | tf_op jit(solution)/shard_map/ppermute | solution.py:32
  20.9 8.9 %collective-permute-start.1 = (bf16[96,1024]{1,0:T(8,128)(2,1)S(1)}, bf16[96,1024]{1,0:T(8,128)(2,1)S(1)}, u32[]{:S(2)}, u32[]{:S(2)}) collective-permute-start(bf16[96,1024]{1,0:T(8,128)(2,1)S(1)} %join.1.refs_0_), channel_id=1, source_target_pairs={{112,0},{0,16},{16,32},{32,48},{48,64},{64,80},{80,96},{96,112},{1... | collective-permute-start | bytes 589832 | tf_op jit(solution)/shard_map/ppermute | solution.py:32
  20.9 14.7 %collective-permute-start.4 = (bf16[96,1024]{1,0:T(8,128)(2,1)S(1)}, bf16[96,1024]{1,0:T(8,128)(2,1)S(1)}, u32[]{:S(2)}, u32[]{:S(2)}) collective-permute-start(bf16[96,1024]{1,0:T(8,128)(2,1)S(1)} %join.1.refs_0_), channel_id=1, source_target_pairs={{0,8},{8,0},{1,9},{9,1},{2,10},{10,2},{3,11},{11,3},{4,12},{12,4},... | collective-permute-start | bytes 589832 | tf_op jit(solution)/shard_map/ppermute | solution.py:420
  23.9 11.7 %collective-permute-start.7 = (bf16[96,1024]{1,0:T(8,128)(2,1)S(1)}, bf16[96,1024]{1,0:T(8,128)(2,1)S(1)}, u32[]{:S(2)}, u32[]{:S(2)}) collective-permute-start(bf16[96,1024]{1,0:T(8,128)(2,1)S(1)} %collective-permute-done.3.refs_3_), channel_id=1, source_target_pairs={{0,8},{8,0},{1,9},{9,1},{2,10},{10,2},{3,11},{11,3},{4,12},{12,4},... | collective-permute-start | bytes 589832 | tf_op jit(solution)/shard_map/ppermute | solution.py:420
  28.7 6.9 %collective-permute-start.6 = (bf16[96,1024]{1,0:T(8,128)(2,1)S(1)}, bf16[96,1024]{1,0:T(8,128)(2,1)S(1)}, u32[]{:S(2)}, u32[]{:S(2)}) collective-permute-start(bf16[96,1024]{1,0:T(8,128)(2,1)S(1)} %collective-permute-done.2.refs_2_), channel_id=1, source_target_pairs={{0,8},{8,0},{1,9},{9,1},{2,10},{10,2},{3,11},{11,3},{4,12},{12,4},... | collective-permute-start | bytes 589832 | tf_op jit(solution)/shard_map/ppermute | solution.py:420
  29.7 5.9 %collective-permute-start.5 = (bf16[96,1024]{1,0:T(8,128)(2,1)S(1)}, bf16[96,1024]{1,0:T(8,128)(2,1)S(1)}, u32[]{:S(2)}, u32[]{:S(2)}) collective-permute-start(bf16[96,1024]{1,0:T(8,128)(2,1)S(1)} %collective-permute-done.1.refs_1_), channel_id=1, source_target_pairs={{0,8},{8,0},{1,9},{9,1},{2,10},{10,2},{3,11},{11,3},{4,12},{12,4},... | collective-permute-start | bytes 589832 | tf_op jit(solution)/shard_map/ppermute | solution.py:420
  30.9 4.7 %collective-permute-start.8 = (s32[384]{0:T(512)S(1)}, s32[384]{0:T(512)S(1)}, u32[]{:S(2)}, u32[]{:S(2)}) collective-permute-start(s32[384]{0:T(512)S(1)} %copy-done.1), channel_id=1, source_target_pairs={{0,128},{128,0},{1,129},{129,1},{2,130},{130,2},{3,131},{131,3},{4... | collective-permute-start | bytes 4616 | tf_op jit(solution)/shard_map/ppermute | solution.py:401
  41.8 3.2 %collective-permute-start.9 = (f32[1,1024]{1,0:T(1,128)S(1)}, f32[1,1024]{1,0:T(1,128)S(1)}, u32[]{:S(2)}, u32[]{:S(2)}) collective-permute-start(f32[1,1024]{1,0:T(1,128)S(1)} %get-tuple-element.27), channel_id=1, source_target_pairs={{0,8},{8,0},{1,9},{9,1},{2,10},{10,2},{3,11},{11,3},{4,12},{12,4},... | collective-permute-start | bytes 12296 | tf_op jit(solution)/shard_map/ppermute | solution.py:438
  45.0 5.4 %collective-permute-start.12 = (f32[1,1792]{1,0:T(1,128)S(1)}, f32[1,1792]{1,0:T(1,128)S(1)}, u32[]{:S(2)}, u32[]{:S(2)}) collective-permute-start(f32[1,1792]{1,0:T(1,128)S(1)} %meet.1.mine), channel_id=1, source_target_pairs={{0,32},{1,33},{2,34},{3,35},{4,36},{5,37},{6,38},{7,39},{8,9},{9,8... | collective-permute-start | bytes 21512 | tf_op jit(solution)/shard_map/ppermute | solution.py:53
  48.9 2.5 %collective-permute-start.11 = (f32[1,1792]{1,0:T(1,128)S(1)}, f32[1,1792]{1,0:T(1,128)S(1)}, u32[]{:S(2)}, u32[]{:S(2)}) collective-permute-start(f32[1,1792]{1,0:T(1,128)S(1)} %meet.1.mine), channel_id=1, source_target_pairs={{0,112},{1,113},{2,114},{3,115},{4,116},{5,117},{6,118},{7,119},{8... | collective-permute-start | bytes 21512 | tf_op jit(solution)/shard_map/ppermute | solution.py:53
  49.1 3.7 %collective-permute-start.10 = (f32[1,1792]{1,0:T(1,128)S(1)}, f32[1,1792]{1,0:T(1,128)S(1)}, u32[]{:S(2)}, u32[]{:S(2)}) collective-permute-start(f32[1,1792]{1,0:T(1,128)S(1)} %meet.1.mine), channel_id=1, source_target_pairs={{0,16},{1,17},{2,18},{3,19},{4,20},{5,21},{6,22},{7,23},{8,136},{9... | collective-permute-start | bytes 21512 | tf_op jit(solution)/shard_map/ppermute | solution.py:53
  52.9 5.9 %collective-permute-start.15 = (f32[1,1792]{1,0:T(1,128)S(1)}, f32[1,1792]{1,0:T(1,128)S(1)}, u32[]{:S(2)}, u32[]{:S(2)}) collective-permute-start(f32[1,1792]{1,0:T(1,128)S(1)} %round.1.mine), channel_id=1, source_target_pairs={{0,64},{1,65},{2,66},{3,67},{4,68},{5,69},{6,70},{7,71},{8,12},{9,... | collective-permute-start | bytes 21512 | tf_op jit(solution)/shard_map/ppermute | solution.py:53
  53.2 5.6 %collective-permute-start.14 = (f32[1,1792]{1,0:T(1,128)S(1)}, f32[1,1792]{1,0:T(1,128)S(1)}, u32[]{:S(2)}, u32[]{:S(2)}) collective-permute-start(f32[1,1792]{1,0:T(1,128)S(1)} %round.1.mine), channel_id=1, source_target_pairs={{8,14},{9,15},{10,8},{11,9},{12,10},{13,11},{14,12},{15,13},{24,30... | collective-permute-start | bytes 21512 | tf_op jit(solution)/shard_map/ppermute | solution.py:53
  56.8 5.6 %collective-permute-start.13 = (f32[1,1792]{1,0:T(1,128)S(1)}, f32[1,1792]{1,0:T(1,128)S(1)}, u32[]{:S(2)}, u32[]{:S(2)}) collective-permute-start(f32[1,1792]{1,0:T(1,128)S(1)} %round.1.mine), channel_id=1, source_target_pairs={{8,10},{9,11},{10,12},{11,13},{12,14},{13,15},{14,8},{15,9},{24,26... | collective-permute-start | bytes 21512 | tf_op jit(solution)/shard_map/ppermute | solution.py:53
  62.5 1.3 %collective-permute-start.16 = (f32[1,1024]{1,0:T(1,128)S(1)}, f32[1,1024]{1,0:T(1,128)S(1)}, u32[]{:S(2)}, u32[]{:S(2)}) collective-permute-start(f32[1,1024]{1,0:T(1,128)S(1)} %get-tuple-element.29), channel_id=1, source_target_pairs={{0,8},{8,0},{1,9},{9,1},{2,10},{10,2},{3,11},{11,3},{4,12},{12,4},... | collective-permute-start | bytes 12296 | tf_op jit(solution)/shard_map/ppermute | solution.py:446
  68.7 4.7 %collective-permute-start.17 = (bf16[400,1024]{1,0:T(8,128)(2,1)}, bf16[400,1024]{1,0:T(8,128)(2,1)S(1)}, u32[]{:S(2)}, u32[]{:S(2)}) collective-permute-start(bf16[400,1024]{1,0:T(8,128)(2,1)} %get-tuple-element.36), channel_id=1, source_target_pairs={{0,8},{8,0},{1,9},{9,1},{2,10},{10,2},{3,11},{11,3},{4,12},{12,4},... | collective-permute-start | bytes 2457608 | tf_op jit(solution)/shard_map/ppermute | solution.py:473
  69.0 30.9 %all-to-all-start.1 = ((bf16[16,400,128]{2,1,0:T(8,128)(2,1)}), bf16[16,400,128]{2,1,0:T(8,128)(2,1)S(1)}, u32[]{:S(2)}, u32[]{:S(2)}) async-start(bf16[16,400,128]{2,1,0:T(8,128)(2,1)} %get-tuple-element.33), calls=%async_computation.1 | async-start | bytes 3276800 | tf_op jit(solution)/shard_map/all_to_all | solution.py:468
  74.5 8.3 %collective-permute-start.18 = (bf16[784,128]{1,0:T(8,128)(2,1)S(1)}, bf16[784,128]{1,0:T(8,128)(2,1)S(1)}, u32[]{:S(2)}, u32[]{:S(2)}) collective-permute-start(bf16[784,128]{1,0:T(8,128)(2,1)S(1)} %get-tuple-element.39), channel_id=1, source_target_pairs={{0,32},{16,112},{32,64},{48,16},{64,96},{80,48},{96,0},{112,80},{1... | collective-permute-start | bytes 602120 | tf_op jit(solution)/shard_map/ppermute | solution.py:32
  75.0 11.9 %collective-permute-start.19 = (bf16[784,128]{1,0:T(8,128)(2,1)S(1)}, bf16[784,128]{1,0:T(8,128)(2,1)S(1)}, u32[]{:S(2)}, u32[]{:S(2)}) collective-permute-start(bf16[784,128]{1,0:T(8,128)(2,1)S(1)} %get-tuple-element.40), channel_id=1, source_target_pairs={{0,16},{16,32},{32,48},{48,64},{64,80},{80,96},{96,112},{112,0},{1... | collective-permute-start | bytes 602120 | tf_op jit(solution)/shard_map/ppermute | solution.py:32
  75.5 11.5 %collective-permute-start.20 = (bf16[784,128]{1,0:T(8,128)(2,1)S(1)}, bf16[784,128]{1,0:T(8,128)(2,1)S(1)}, u32[]{:S(2)}, u32[]{:S(2)}) collective-permute-start(bf16[784,128]{1,0:T(8,128)(2,1)S(1)} %get-tuple-element.41), channel_id=1, source_target_pairs={{0,112},{16,0},{32,16},{48,32},{64,48},{80,64},{96,80},{112,96},{1... | collective-permute-start | bytes 602120 | tf_op jit(solution)/shard_map/ppermute | solution.py:32
  87.4 8.9 %collective-permute-start.21 = (bf16[400,128]{1,0:T(8,128)(2,1)S(1)}, bf16[400,128]{1,0:T(8,128)(2,1)S(1)}, u32[]{:S(2)}, u32[]{:S(2)}) collective-permute-start(bf16[400,128]{1,0:T(8,128)(2,1)S(1)} %get-tuple-element.44), channel_id=1, source_target_pairs={{0,64},{16,80},{32,96},{48,112},{64,0},{80,16},{96,32},{112,48},{1... | collective-permute-start | bytes 307208 | tf_op jit(solution)/shard_map/ppermute | solution.py:22
